TPU v7x, 32 devices: a whole 2x2x4 slice. The times are simulated.
32 devices in a mesh: seq: 8 (over z, y), head: 4 (over x, core).
Axes of the slice: x: 2, y: 2, z: 4, core: 2. Of those that a mesh axis runs over, the one named last changes fastest.
Arguments:
- x_input: bfloat16 [8192, 8192], P('seq', 'head'), may hold values from -6 to 6
- z_input: bfloat16 [8192, 8192], P('seq', 'head'), may hold values from -6 to 6
- bc_input: bfloat16 [8192, 8, 256], P('seq', 'head'), may hold values from -6 to 6
- conv_weight_x: float32 [4, 8192], P(None, 'head'), may hold values from -3 to 3
- conv_weight_bc: float32 [4, 8, 256], P(None, 'head'), may hold values from -3 to 3
- step_size: float32 [8192, 128], P('seq', 'head'), may hold values from 0 to 1
- log_decay: float32 [8192, 128], P('seq', 'head'), may hold values from -1 to 0
- skip_gain: float32 [128], P('head'), may hold values from 0.5 to 2
- norm_gain: float32 [8192], P('head'), may hold values from 0.1 to 1.9
- out_weight: bfloat16 [8192, 4096], P('head'), may hold values from -0.0625 to 0.0625
Outputs:
- layer_out: bfloat16 [8192, 4096], P(('seq', 'head'))
All inputs are finite; a program needn't handle non-finite values.
Results may differ from a plain program's by a relative error of at most 0.012.
Values may be sent and summed in bfloat16 or wider, within the bound.
No kernel may reach another device: no remote copies, remote signals or barrier semaphores. Data moves between devices by JAX's collectives and lax.ppermute only.
A program may use at most 256 MiB of HBM per device.

v0:
```python
import jax
import jax.numpy as jnp
from jax import lax
from jax.sharding import PartitionSpec as P

P_SIZE = 64
N = 128
KCONV = 4
BLOCK_LEN = 256


EPS = 1e-05


def from_behind(block, axis, distance):
    devices = range(lax.axis_size(axis))
    route = [(i - distance, i) for i in devices if i - distance in devices]
    return lax.ppermute(block, axis, route)


def conv_silu(padded, weight, length):
    summed = jnp.zeros((length,) + padded.shape[1:], jnp.float32)
    for offset in range(weight.shape[0]):
        summed = summed + weight[offset] * padded[offset : offset + length].astype(jnp.float32)
    return jax.nn.silu(summed).astype(jnp.bfloat16)


def local(
    x_input,
    z_input,
    bc_input,
    conv_weight_x,
    conv_weight_bc,
    step_size,
    log_decay,
    skip_gain,
    norm_gain,
    out_weight,
):
    length = x_input.shape[0]
    width = x_input.shape[1]
    groups = bc_input.shape[1]
    per_group = step_size.shape[1] // groups
    lead_rows = KCONV - 1
    highest = lax.Precision.HIGHEST
    prior_x, prior_bc = from_behind(
        (x_input[length - lead_rows :], bc_input[length - lead_rows :]), "seq", 1
    )
    x_conv = conv_silu(jnp.concatenate([prior_x, x_input], 0), conv_weight_x, length)
    bc_conv = conv_silu(jnp.concatenate([prior_bc, bc_input], 0), conv_weight_bc, length)
    blocks = length // BLOCK_LEN
    x_float = x_conv.astype(jnp.float32).reshape(blocks, BLOCK_LEN, groups, per_group, P_SIZE)
    bc_blocks = bc_conv.reshape(blocks, BLOCK_LEN, groups, 2 * N)
    b_half = bc_blocks[..., :N]
    c_half = bc_blocks[..., N:]
    b_mat = b_half.astype(jnp.float32)
    c_mat = c_half.astype(jnp.float32)
    driven = step_size.reshape(blocks, BLOCK_LEN, groups, per_group)[..., None] * x_float
    cumulative = jnp.cumsum(log_decay.reshape(blocks, BLOCK_LEN, groups, per_group), axis=1)
    lower_mask = jnp.tril(jnp.ones((BLOCK_LEN, BLOCK_LEN), bool))[None, :, :, None, None]
    log_gap = cumulative[:, :, None] - cumulative[:, None, :]
    decay_table = jnp.where(lower_mask, jnp.exp(jnp.where(lower_mask, log_gap, 0.0)), 0.0)
    scores = jnp.einsum("ctgn,csgn->ctsg", c_half, b_half, preferred_element_type=jnp.float32)
    within = jnp.einsum(
        "ctsgh,csghp->ctghp", scores[..., None] * decay_table, driven, precision=highest
    )
    last_log = cumulative[:, -1]
    fading = jnp.exp(last_log[:, None] - cumulative)[..., None] * driven
    block_states = jnp.einsum("csgn,csghp->cghnp", b_mat, fading, precision=highest)

    def pass_block(carry_state, pair):
        log_total, fresh = pair
        return (jnp.exp(log_total)[..., None, None] * carry_state + fresh, carry_state)

    empty_state = jnp.zeros((groups, per_group, N, P_SIZE), jnp.float32)
    final_state, entering = lax.scan(pass_block, empty_state, (last_log, block_states))
    offsets = jnp.cumsum(last_log, axis=0) - last_log
    device_log = jnp.sum(last_log, axis=0)

    def relay_turn(turn_index, incoming_state):
        return from_behind(
            jnp.exp(device_log)[..., None, None] * incoming_state + final_state, "seq", 1
        )

    incoming = lax.fori_loop(0, lax.axis_size("seq") - 1, relay_turn, empty_state)
    entering = entering + jnp.exp(offsets)[..., None, None] * incoming[None]
    carried = jnp.exp(cumulative)[..., None] * jnp.einsum(
        "ctgn,cghnp->ctghp", c_mat, entering, precision=highest
    )
    mixed = within + carried + skip_gain.reshape(groups, per_group)[..., None] * x_float
    gated_out = mixed.reshape(length, width) * jax.nn.silu(z_input.astype(jnp.float32))
    grouped = gated_out.reshape(length, groups, width // groups)
    normed = grouped * lax.rsqrt(jnp.mean(grouped * grouped, axis=-1, keepdims=True) + EPS)
    normed = (normed.reshape(length, width) * norm_gain).astype(jnp.bfloat16)
    result = lax.psum_scatter(
        jnp.dot(normed, out_weight, preferred_element_type=jnp.float32),
        "head",
        scatter_dimension=0,
        tiled=True,
    )
    return result.astype(jnp.bfloat16)


def solution(mesh):
    in_specs = (
        P("seq", "head"),
        P("seq", "head"),
        P("seq", "head", None),
        P(None, "head"),
        P(None, "head", None),
        P("seq", "head"),
        P("seq", "head"),
        P("head"),
        P("head"),
        P("head", None),
    )
    out_specs = P(("seq", "head"), None)
    return jax.shard_map(local, mesh=mesh, in_specs=in_specs, out_specs=out_specs, check_vma=False)
```

profile of v0, /device:TPU:0, one launch (start us, length us, event | category | flops | bytes accessed | tf_op | source)
XLA Modules:
  0.0 533.7 jit_solution(650218771404319879)
XLA Ops:
  8.4 5.7 %collective-permute-start.1 = (bf16[3,2048]{0,1:T(8,128)(2,1)}, bf16[3,2048]{0,1:T(8,128)(2,1)}, u32[]{:S(2)}, u32[]{:S(2)}) collective-permute-start(bf16[3,2048]{0,1:T(8,128)(2,1)} %copy.61), channel_id=1, source_target_pairs={{0,4},{4,8},{8,12},{12,16},{16,20},{20,24},{24,28},{1,5},{5,9},{9,... | collective-permute-start | bytes 36872 | tf_op jit(solution)/shard_map/ppermute | solution.py:18
  30.3 6.4 %copy.62 = bf16[1024,2048]{0,1:T(8,128)(2,1)} copy(bf16[1024,2048]{1,0:T(8,128)(2,1)} %param.14) | data formatting | bytes 8388608 | tf_op args[0]
  39.0 6.4 %copy.84 = bf16[1024,2048]{0,1:T(8,128)(2,1)} copy(bf16[1024,2048]{1,0:T(8,128)(2,1)} %param.15) | data formatting | bytes 8388608 | tf_op args[1]
  53.5 17.2 %fusion.33 = f32[1024,2048]{0,1:T(8,128)} fusion(bf16[1024,2048]{0,1:T(8,128)(2,1)} %copy.62, f32[2048]{0:T(1024)S(1)} %bitcast.106, bf16[3,2048]{0,1:T(8,128)(2,1)} %collective-permute-done.1, f32[2048]{0:T(1024)S(1)} %bitcast.107, f32[2048]{0:T(1024)S(1)} %bitcast.105, f32[2048]{0:T(1024)S(1)} %bitcast.104), kind=kLoop, calls=%fused_computation.48 | loop fusion | flops 54525952 | bytes 12627968 | tf_op jit(solution)/shard_map/reshape | solution.py:52
  70.7 10.6 %reshape.90 = f32[4,256,2,16,64]{1,0,4,3,2:T(4,128)} reshape(f32[1024,2048]{0,1:T(8,128)} %fusion.33) | data formatting | bytes 16777216 | tf_op jit(solution)/shard_map/reshape | solution.py:52
  81.3 8.4 %broadcast_multiply_fusion = (f32[4,256,2,16,64]{1,0,4,3,2:T(4,128)S(1)}, f32[4,256,2,16,64]{1,0,4,3,2:T(4,128)}) fusion(f32[4,256,2,16]{1,0,3,2:T(4,128)S(1)} %copy.76, f32[4,256,2,16,64]{1,0,4,3,2:T(4,128)} %reshape.90, f32[4,256,2,16]{1,0,3,2:T(4,128)S(1)} %mul.200), kind=kLoop, calls=%fused_computation.46 | loop fusion | flops 4194304 | bytes 25427968 | tf_op jit(solution)/shard_map/mul | solution.py:68
  89.7 5.7 %fusion.34 = f32[4,2,16,128,64]{3,4,2,1,0:T(8,128)} fusion(f32[4,256,2,16,64]{1,0,4,3,2:T(4,128)S(1)} %get-tuple-element.148, bf16[4,256,2,128]{3,1,0,2:T(8,128)(2,1)S(1)} %get-tuple-element.151), kind=kOutput, calls=%fused_computation.49 | convolution fusion | flops 3221225472 | bytes 13107200 | tf_op jit(solution)/shard_map/csgn,csghp->cghnp/dot_general | solution.py:69
  95.5 26.9 %while.26 = (s32[]{:T(128)}, f32[2,16,128,64]{3,2,1,0:T(8,128)S(1)}, f32[4,2,16,128,64]{4,3,2,1,0:T(8,128)}, f32[4,2,16]{2,1,0:T(2,128)S(1)}, f32[4,2,16,128,64]{3,4,2,1,0:T(8,128)}, /*index=5*/s32[]{:T(128)}, s32[]{:T(128)}) while((s32[]{:T(128)}, f32[2,16,128,64]{3,2,1,0:T(8,128)S(1)}, f32[4,2,16,128,64]{4,3,2,1,0:T(8,128)}, ...), condition=%wide.region_3.4_spmd.clone, body=%wide.region_2.3_spmd.clone.sunk | while | flops 1048579 | bytes 10486752 | solution.py:76
  123.1 168.2 %while.25 = (s32[]{:T(128)}, f32[2,16,128,64]{2,3,1,0:T(8,128)S(1)}, f32[2,16,1,1]{1,0,3,2:T(2,128)S(1)}, f32[2,16,128,64]{2,3,1,0:T(8,128)S(1)}, s32[]{:T(128)}) while((s32[]{:T(128)}, f32[2,16,128,64]{2,3,1,0:T(8,128)S(1)}, f32[2,16,1,1]{1,0,3,2:T(2,128)S(1)}, f32[2,16,128,64]{2,3,1,0:T(8,128)S(1)}, s32[]{:T(128)}) %tuple.60), condition=%wide.region_7.8_spmd, body=%wide.region_6.7_spmd.sunk | while | flops 524290 | bytes 7340261 | solution.py:85
  126.2 21.8 %collective-permute-done = f32[2,16,128,64]{2,3,1,0:T(8,128)S(1)} collective-permute-done((f32[2,16,128,64]{2,3,1,0:T(8,128)S(1)}, f32[2,16,128,64]{2,3,1,0:T(8,128)S(1)}, u32[]{:S(2)}, u32[]{:S(2)}) %collective-permute-start) | collective-permute-done | bytes 1048608 | tf_op jit(solution)/shard_map/while/body/eval_jaxpr/ppermute | solution.py:18
  152.6 20.8 %collective-permute-done = f32[2,16,128,64]{2,3,1,0:T(8,128)S(1)} collective-permute-done((f32[2,16,128,64]{2,3,1,0:T(8,128)S(1)}, f32[2,16,128,64]{2,3,1,0:T(8,128)S(1)}, u32[]{:S(2)}, u32[]{:S(2)}) %collective-permute-start) | collective-permute-done | bytes 1048608 | tf_op jit(solution)/shard_map/while/body/eval_jaxpr/ppermute | solution.py:18
  178.1 19.9 %collective-permute-done = f32[2,16,128,64]{2,3,1,0:T(8,128)S(1)} collective-permute-done((f32[2,16,128,64]{2,3,1,0:T(8,128)S(1)}, f32[2,16,128,64]{2,3,1,0:T(8,128)S(1)}, u32[]{:S(2)}, u32[]{:S(2)}) %collective-permute-start) | collective-permute-done | bytes 1048608 | tf_op jit(solution)/shard_map/while/body/eval_jaxpr/ppermute | solution.py:18
  203.5 19.0 %collective-permute-done = f32[2,16,128,64]{2,3,1,0:T(8,128)S(1)} collective-permute-done((f32[2,16,128,64]{2,3,1,0:T(8,128)S(1)}, f32[2,16,128,64]{2,3,1,0:T(8,128)S(1)}, u32[]{:S(2)}, u32[]{:S(2)}) %collective-permute-start) | collective-permute-done | bytes 1048608 | tf_op jit(solution)/shard_map/while/body/eval_jaxpr/ppermute | solution.py:18
  222.7 5.3 %collective-permute-start = (f32[2,16,128,64]{2,3,1,0:T(8,128)S(1)}, f32[2,16,128,64]{2,3,1,0:T(8,128)S(1)}, u32[]{:S(2)}, u32[]{:S(2)}) collective-permute-start(f32[2,16,128,64]{2,3,1,0:T(8,128)S(1)} %multiply_add_fusion.2), channel_id=1, source_target_pairs={{0,4},{4,8},{8,12},{12,16},{16,20},{20,24},{24,28},{1,5},{5,9},{9,... | collective-permute-start | bytes 3145736 | tf_op jit(solution)/shard_map/while/body/eval_jaxpr/ppermute | solution.py:18
  228.0 18.1 %collective-permute-done = f32[2,16,128,64]{2,3,1,0:T(8,128)S(1)} collective-permute-done((f32[2,16,128,64]{2,3,1,0:T(8,128)S(1)}, f32[2,16,128,64]{2,3,1,0:T(8,128)S(1)}, u32[]{:S(2)}, u32[]{:S(2)}) %collective-permute-start) | collective-permute-done | bytes 1048608 | tf_op jit(solution)/shard_map/while/body/eval_jaxpr/ppermute | solution.py:18
  246.3 5.3 %collective-permute-start = (f32[2,16,128,64]{2,3,1,0:T(8,128)S(1)}, f32[2,16,128,64]{2,3,1,0:T(8,128)S(1)}, u32[]{:S(2)}, u32[]{:S(2)}) collective-permute-start(f32[2,16,128,64]{2,3,1,0:T(8,128)S(1)} %multiply_add_fusion.2), channel_id=1, source_target_pairs={{0,4},{4,8},{8,12},{12,16},{16,20},{20,24},{24,28},{1,5},{5,9},{9,... | collective-permute-start | bytes 3145736 | tf_op jit(solution)/shard_map/while/body/eval_jaxpr/ppermute | solution.py:18
  251.7 17.8 %collective-permute-done = f32[2,16,128,64]{2,3,1,0:T(8,128)S(1)} collective-permute-done((f32[2,16,128,64]{2,3,1,0:T(8,128)S(1)}, f32[2,16,128,64]{2,3,1,0:T(8,128)S(1)}, u32[]{:S(2)}, u32[]{:S(2)}) %collective-permute-start) | collective-permute-done | bytes 1048608 | tf_op jit(solution)/shard_map/while/body/eval_jaxpr/ppermute | solution.py:18
  275.0 16.3 %collective-permute-done = f32[2,16,128,64]{2,3,1,0:T(8,128)S(1)} collective-permute-done((f32[2,16,128,64]{2,3,1,0:T(8,128)S(1)}, f32[2,16,128,64]{2,3,1,0:T(8,128)S(1)}, u32[]{:S(2)}, u32[]{:S(2)}) %collective-permute-start) | collective-permute-done | bytes 1048608 | tf_op jit(solution)/shard_map/while/body/eval_jaxpr/ppermute | solution.py:18
  291.9 9.8 %fusion.22 = f32[4,2,16,64,256]{4,3,2,1,0:T(8,128)S(1)} fusion(f32[4,2,16,128,64]{4,3,2,1,0:T(8,128)} %get-tuple-element.83, f32[2,16,128,64]{3,2,1,0:T(8,128)S(1)} %copy.80, f32[4,2,16]{2,1,0:T(2,128)S(1)} %copy-done.8, bf16[4,256,2,128]{3,1,0,2:T(8,128)(2,1)} %copy-done.1), kind=kOutput, calls=%fused_computation.33 | convolution fusion | flops 3223322624 | bytes 14156288 | tf_op jit(solution)/shard_map/ctgn,cghnp->ctghp/dot_general | solution.py:87
  301.8 42.0 %fusion.18 = f32[4,256,2,16,64]{1,4,3,2,0:T(8,128)} fusion(f32[4,2,16,64,256]{4,3,2,1,0:T(8,128)S(1)} %fusion.22, f32[4,256,2,16,64]{1,0,4,3,2:T(4,128)} %reshape.90, f32[4,256,2,16]{1,3,2,0:T(8,128)S(1)} %bitcast_bitcast_fusion, f32[4,256,256,2]{2,1,3,0:T(8,128)S(1)} %copy-done.2, pred[256,256]{1,0:T(8,128)(4,1)S(1)} %copy-done.4, ...), kind=kOutput, calls=%fused_computation.28 | convolution fusion | flops 6484393984 | bytes 35979392 | tf_op jit(solution)/shard_map/ctsgh,csghp->ctghp/dot_general | solution.py:64
  343.8 13.8 %copy.83 = f32[4,256,2,16,64]{1,0,4,3,2:T(4,128)} copy(f32[4,256,2,16,64]{1,4,3,2,0:T(8,128)} %fusion.18) | data formatting | bytes 16777216 | tf_op jit(solution)/shard_map/add | solution.py:90
  357.6 5.6 %copy.93 = f32[256,8,4,256]{3,1,2,0:T(8,128)S(1)} copy(f32[256,8,4,256]{3,2,1,0:T(4,128)} %bitcast.101) | data formatting | bytes 16777216
  369.1 22.9 %fusion.52 = f32[1024,4096]{1,0:T(8,128)} fusion(bf16[1024,2048]{0,1:T(8,128)(2,1)S(1)} %fusion.16, bf16[2048,4096]{1,0:T(8,128)(2,1)} %param.23), kind=kOutput, calls=%fused_computation.85 | convolution fusion | flops 17179869184 | bytes 37748736 | tf_op jit(solution)/shard_map/dot_general | solution.py:96
  392.1 130.5 %reduce-scatter.2.cloned.1.call-done = f32[256,4096]{1,0:T(8,128)} async-done(((f32[1024,4096]{1,0:T(8,128)}), f32[256,4096]{1,0:T(8,128)}) %reduce-scatter.2.cloned.1.call-update) | async-done | bytes 4194320 | tf_op jit(solution)/shard_map/reduce_scatter | solution.py:95
  (95 shorter events, 89.8 us)
Async XLA Ops:
  6.5 516.1 %reduce-scatter.2.cloned.1.call-start = ((), (), s32[]{:S(2)}) async-start(), calls=%async_computation.1 | async-start | bytes 20971520 | tf_op jit(solution)/shard_map/reduce_scatter | solution.py:95
  8.4 45.1 %collective-permute-start.1 = (bf16[3,2048]{0,1:T(8,128)(2,1)}, bf16[3,2048]{0,1:T(8,128)(2,1)}, u32[]{:S(2)}, u32[]{:S(2)}) collective-permute-start(bf16[3,2048]{0,1:T(8,128)(2,1)} %copy.61), channel_id=1, source_target_pairs={{0,4},{4,8},{8,12},{12,16},{16,20},{20,24},{24,28},{1,5},{5,9},{9,... | collective-permute-start | bytes 36872 | tf_op jit(solution)/shard_map/ppermute | solution.py:18
  16.0 29.4 %collective-permute-start.2 = (bf16[3,2,256]{2,0,1:T(4,128)(2,1)}, bf16[3,2,256]{2,0,1:T(4,128)(2,1)}, u32[]{:S(2)}, u32[]{:S(2)}) collective-permute-start(bf16[3,2,256]{2,0,1:T(4,128)(2,1)} %slice.88), channel_id=1, source_target_pairs={{0,4},{4,8},{8,12},{12,16},{16,20},{20,24},{24,28},{1,5},{5,9},{9,... | collective-permute-start | bytes 9224 | tf_op jit(solution)/shard_map/ppermute | solution.py:18
  47.7 5.8 %copy-start.5 = (f32[1,2048]{1,0:T(1,128)S(1)}, f32[1,2048]{1,0:T(1,128)}, u32[]{:S(2)}) copy-start(f32[1,2048]{1,0:T(1,128)} %get-tuple-element.155) | copy-start | bytes 24580
  47.7 5.8 %copy-start.6 = (f32[1,2048]{1,0:T(1,128)S(1)}, f32[1,2048]{1,0:T(1,128)}, u32[]{:S(2)}) copy-start(f32[1,2048]{1,0:T(1,128)} %get-tuple-element.156) | copy-start | bytes 24580
  47.7 5.8 %copy-start.7 = (f32[1,2048]{1,0:T(1,128)S(1)}, f32[1,2048]{1,0:T(1,128)}, u32[]{:S(2)}) copy-start(f32[1,2048]{1,0:T(1,128)} %get-tuple-element.157) | copy-start | bytes 24580
  48.0 0.8 copy-start.1
  123.1 168.8 %copy-start.8 = (f32[4,2,16]{2,1,0:T(2,128)S(1)}, f32[4,2,16]{2,1,0:T(2,128)}, u32[]{:S(2)}) copy-start(f32[4,2,16]{2,1,0:T(2,128)} %fusion.37) | copy-start | bytes 1540
  123.3 24.7 %collective-permute-start = (f32[2,16,128,64]{2,3,1,0:T(8,128)S(1)}, f32[2,16,128,64]{2,3,1,0:T(8,128)S(1)}, u32[]{:S(2)}, u32[]{:S(2)}) collective-permute-start(f32[2,16,128,64]{2,3,1,0:T(8,128)S(1)} %multiply_add_fusion.2), channel_id=1, source_target_pairs={{0,4},{4,8},{8,12},{12,16},{16,20},{20,24},{24,28},{1,5},{5,9},{9,... | collective-permute-start | bytes 3145736 | tf_op jit(solution)/shard_map/while/body/eval_jaxpr/ppermute | solution.py:18
  148.1 25.3 %collective-permute-start = (f32[2,16,128,64]{2,3,1,0:T(8,128)S(1)}, f32[2,16,128,64]{2,3,1,0:T(8,128)S(1)}, u32[]{:S(2)}, u32[]{:S(2)}) collective-permute-start(f32[2,16,128,64]{2,3,1,0:T(8,128)S(1)} %multiply_add_fusion.2), channel_id=1, source_target_pairs={{0,4},{4,8},{8,12},{12,16},{16,20},{20,24},{24,28},{1,5},{5,9},{9,... | collective-permute-start | bytes 3145736 | tf_op jit(solution)/shard_map/while/body/eval_jaxpr/ppermute | solution.py:18
  173.6 24.4 %collective-permute-start = (f32[2,16,128,64]{2,3,1,0:T(8,128)S(1)}, f32[2,16,128,64]{2,3,1,0:T(8,128)S(1)}, u32[]{:S(2)}, u32[]{:S(2)}) collective-permute-start(f32[2,16,128,64]{2,3,1,0:T(8,128)S(1)} %multiply_add_fusion.2), channel_id=1, source_target_pairs={{0,4},{4,8},{8,12},{12,16},{16,20},{20,24},{24,28},{1,5},{5,9},{9,... | collective-permute-start | bytes 3145736 | tf_op jit(solution)/shard_map/while/body/eval_jaxpr/ppermute | solution.py:18
  198.2 24.3 %collective-permute-start = (f32[2,16,128,64]{2,3,1,0:T(8,128)S(1)}, f32[2,16,128,64]{2,3,1,0:T(8,128)S(1)}, u32[]{:S(2)}, u32[]{:S(2)}) collective-permute-start(f32[2,16,128,64]{2,3,1,0:T(8,128)S(1)} %multiply_add_fusion.2), channel_id=1, source_target_pairs={{0,4},{4,8},{8,12},{12,16},{16,20},{20,24},{24,28},{1,5},{5,9},{9,... | collective-permute-start | bytes 3145736 | tf_op jit(solution)/shard_map/while/body/eval_jaxpr/ppermute | solution.py:18
  222.7 23.4 %collective-permute-start = (f32[2,16,128,64]{2,3,1,0:T(8,128)S(1)}, f32[2,16,128,64]{2,3,1,0:T(8,128)S(1)}, u32[]{:S(2)}, u32[]{:S(2)}) collective-permute-start(f32[2,16,128,64]{2,3,1,0:T(8,128)S(1)} %multiply_add_fusion.2), channel_id=1, source_target_pairs={{0,4},{4,8},{8,12},{12,16},{16,20},{20,24},{24,28},{1,5},{5,9},{9,... | collective-permute-start | bytes 3145736 | tf_op jit(solution)/shard_map/while/body/eval_jaxpr/ppermute | solution.py:18
  246.3 23.1 %collective-permute-start = (f32[2,16,128,64]{2,3,1,0:T(8,128)S(1)}, f32[2,16,128,64]{2,3,1,0:T(8,128)S(1)}, u32[]{:S(2)}, u32[]{:S(2)}) collective-permute-start(f32[2,16,128,64]{2,3,1,0:T(8,128)S(1)} %multiply_add_fusion.2), channel_id=1, source_target_pairs={{0,4},{4,8},{8,12},{12,16},{16,20},{20,24},{24,28},{1,5},{5,9},{9,... | collective-permute-start | bytes 3145736 | tf_op jit(solution)/shard_map/while/body/eval_jaxpr/ppermute | solution.py:18
  269.6 21.7 %collective-permute-start = (f32[2,16,128,64]{2,3,1,0:T(8,128)S(1)}, f32[2,16,128,64]{2,3,1,0:T(8,128)S(1)}, u32[]{:S(2)}, u32[]{:S(2)}) collective-permute-start(f32[2,16,128,64]{2,3,1,0:T(8,128)S(1)} %multiply_add_fusion.2), channel_id=1, source_target_pairs={{0,4},{4,8},{8,12},{12,16},{16,20},{20,24},{24,28},{1,5},{5,9},{9,... | collective-permute-start | bytes 3145736 | tf_op jit(solution)/shard_map/while/body/eval_jaxpr/ppermute | solution.py:18
  291.9 9.8 %copy-start.2 = (f32[4,256,256,2]{2,1,3,0:T(8,128)S(1)}, f32[4,256,256,2]{2,1,3,0:T(8,128)}, u32[]{:S(2)}) copy-start(f32[4,256,256,2]{2,1,3,0:T(8,128)} %copy.69) | copy-start | bytes 6291460
  291.9 9.8 %copy-start.3 = (f32[4,256,2,16]{1,3,2,0:T(8,128)S(1)}, f32[4,256,2,16]{1,3,2,0:T(8,128)}, u32[]{:S(2)}) copy-start(f32[4,256,2,16]{1,3,2,0:T(8,128)} %get-tuple-element.152) | copy-start | bytes 393220
  291.9 9.8 %copy-start.4 = (pred[256,256]{1,0:T(8,128)(4,1)S(1)}, pred[256,256]{1,0:T(8,128)(4,1)}, u32[]{:S(2)}) copy-start(pred[256,256]{1,0:T(8,128)(4,1)} %iota_compare_fusion) | copy-start | bytes 196612
  291.9 9.8 %copy-start.10 = (f32[2,16]{1,0:T(2,128)S(1)}, f32[2,16]{1,0:T(2,128)}, u32[]{:S(2)}) copy-start(f32[2,16]{1,0:T(2,128)} %mul.238) | copy-start | bytes 388
  357.6 5.7 %copy-start = (bf16[1024,2048]{0,1:T(8,128)(2,1)S(1)}, bf16[1024,2048]{0,1:T(8,128)(2,1)}, u32[]{:S(2)}) copy-start(bf16[1024,2048]{0,1:T(8,128)(2,1)} %copy.84) | copy-start | bytes 12582916
  363.2 2.8 copy-start.9
Sparse Core Ops, SparseCore 0:
  392.2 130.3 reduce-scatter.1
where the time goes:
time: 543 us; the launch traced here: 534 us
  waiting for transfers between devices  264 us (49%)
  matrix products  82.2 us (15%)
  local copies, waits for them, and re-layouts  71.3 us (13%)
  other arithmetic  59.5 us (11%)
  starting transfers between devices  42.1 us (8%)
  between operations  14.1 us (3%)
    ppermute x9, waiting for transfers between devices, from_behind(): return lax.ppermute(block, axis, route)  134 us
    reduce_scatter x1, waiting for transfers between devices, local(): lax.psum_scatter(jnp.dot(normed, out_weight, preferred_element_type=jnp.f...  130 us
    ppermute x9, starting transfers between devices, from_behind(): return lax.ppermute(block, axis, route)  42 us
    dot_general x1, matrix products, local(): jnp.einsum('ctsgh,csghp->ctghp', scores[..., None] * decay_table, driven,...  42 us
    dot_general x1, matrix products, local(): jnp.dot(normed, out_weight, preferred_element_type=jnp.float32)  22.9 us
    unnamed x26, local copies, waits for them, and re-layouts  20.7 us
    reshape x1, other arithmetic, local(): x_conv.astype(jnp.float32)  17.2 us
    add x1, local copies, waits for them, and re-layouts, local(): within + carried + skip_gain.reshape(groups, per_group)[..., None] * x_float  13.8 us
  transfers between devices with their start and end apart: 10, of which 8 were waited for; matrix products, arithmetic and copies ran while one was open for 7% of the time, Pallas kernels for 0%

commit v1 on v0

v1 whole, which is shorter than its diff:
```python
import functools

import jax
import jax.numpy as jnp
import numpy as np
from jax import lax
from jax.experimental import pallas as pl
from jax.experimental.pallas import tpu as pltpu
from jax.sharding import PartitionSpec as P

P_SIZE = 64
N = 128
KCONV = 4
EPS = 1e-05
LOG2E = 1.4426950408889634

TOK_A = 256
TOK_B = 128
SLAB = 256
LEAD = 16
B_PARTS = 4
VMEM_LIMIT = 50 * 1024 * 1024
HIGHEST = lax.Precision.HIGHEST
F32 = jnp.float32
BF16 = jnp.bfloat16


def params(limit=VMEM_LIMIT):
    return pltpu.CompilerParams(vmem_limit_bytes=limit)


def dot(a, b, dims=((1,), (0,)), precision=None):
    return lax.dot_general(a, b, (dims, ((), ())), precision=precision, preferred_element_type=F32)


def half_silu(half):
    return half + half * jnp.tanh(half)


def whole(shape):
    return pl.BlockSpec(shape, lambda *_: (0,) * len(shape))


def decay_kernel(ld, ld_t, step, ones, cum, cum_t, f_dev, st, f_blk, e_blk, e_dev, blk_x, dev_total):
    length, heads = ld.shape
    blocks = length // TOK_B
    row = lax.broadcasted_iota(jnp.int32, (TOK_B, TOK_B), 0)
    col = lax.broadcasted_iota(jnp.int32, (TOK_B, TOK_B), 1)
    lower = (row >= col).astype(F32)
    upper = (row <= col).astype(F32)

    def put(ref, rows, value):
        high = value.astype(BF16)
        ref[rows, 0:heads] = high
        ref[rows, heads : 2 * heads] = (value - high.astype(F32)).astype(BF16)

    cums, totals = [], []
    for b in range(blocks):
        rows = slice(b * TOK_B, (b + 1) * TOK_B)
        c = dot(lower, ld[rows, :] * LOG2E, precision=HIGHEST)
        cum[rows, :] = c
        cum_t[:, rows] = dot(ld_t[:, rows] * LOG2E, upper, precision=HIGHEST)
        cums.append(c)
        totals.append(c[TOK_B - 1 : TOK_B, :])
    before = [jnp.zeros_like(totals[0])]
    for b in range(blocks):
        before.append(before[-1] + totals[b])
    total = before[-1]
    dev_total[...] = total
    blk_x[...] = dot(jnp.exp2(jnp.concatenate(totals, 0)), ones[0:heads, :].astype(F32), precision=HIGHEST)
    for b in range(blocks):
        rows = slice(b * TOK_B, (b + 1) * TOK_B)
        s = step[rows, :]
        dev = cums[b] + before[b]
        put(f_dev, rows, jnp.exp2(total - dev) * s)
        put(st, rows, s)
        put(f_blk, rows, jnp.exp2(totals[b] - cums[b]) * s)
        put(e_blk, rows, jnp.exp2(cums[b]))
        put(e_dev, rows, jnp.exp2(dev))


def decays(log_decay, step, ones):
    length, heads = log_decay.shape
    blocks = length // TOK_B
    width = ones.shape[1]
    pair = jax.ShapeDtypeStruct((length, 2 * heads), BF16)
    return pl.pallas_call(
        decay_kernel,
        out_shape=(
            jax.ShapeDtypeStruct((length, heads), F32),
            jax.ShapeDtypeStruct((heads, length), F32),
            pair,
            pair,
            pair,
            pair,
            pair,
            jax.ShapeDtypeStruct((blocks, width), F32),
            jax.ShapeDtypeStruct((1, heads), F32),
        ),
        compiler_params=params(),
        name="decays",
    )(log_decay, log_decay.T, step, ones)


def conv_kernel(odd, x, x_lead, bc, bc_lead, halo, wx, wbc, f_dev, ones, x_out, bc_out, keep, send, buf, xf, state):
    i = pl.program_id(0)
    rows, width = x.shape
    bc_width = bc.shape[1]
    groups = bc_width // (2 * N)
    per = width // groups
    half = width // 2
    part = 64

    @pl.when(i == 0)
    def _():
        buf[0:LEAD, 0:width] = halo[:, 0:width].astype(F32)
        buf[0:LEAD, width:] = halo[:, width:].astype(F32)
        state[...] = jnp.zeros_like(state)

    @pl.when(i > 0)
    def _():
        buf[0:LEAD, 0:width] = x_lead[...].astype(F32)
        buf[0:LEAD, width:] = bc_lead[...].astype(F32)

    def conv(offset, lanes, weights, r):
        total = None
        for k in range(KCONV):
            first = LEAD - (KCONV - 1) + k + r
            term = weights[k : k + 1, :] * buf[first : first + part, pl.ds(offset + lanes, SLAB)]
            total = term if total is None else total + term
        return half_silu(total)

    for c in range(bc_width // SLAB):
        lanes = c * SLAB
        buf[LEAD:, width + lanes : width + lanes + SLAB] = bc[:, lanes : lanes + SLAB].astype(F32)
        w = wbc[:, lanes : lanes + SLAB] * 0.5
        for r in range(0, rows, part):
            bc_out[r : r + part, lanes : lanes + SLAB] = conv(width, lanes, w, r).astype(BF16)

    def slab(c, _):
        lanes = pl.multiple_of(c * SLAB, SLAB)
        ds = pl.ds(lanes, SLAB)
        buf[LEAD:, ds] = x[:, ds].astype(F32)
        w = wx[:, ds] * 0.5
        scale = dot(f_dev[...], ones[:, ds])
        for r in range(0, rows, part):
            value = conv(0, lanes, w, r).astype(BF16)
            x_out[r : r + part, ds] = value
            xf[r : r + part, ds] = (value.astype(F32) * scale[r : r + part]).astype(BF16)
        return 0

    lax.fori_loop(0, width // SLAB, slab, 0)
    for g in range(groups):
        b_mat = bc_out[:, 2 * N * g : 2 * N * g + N]
        lanes = slice(g * per, (g + 1) * per)
        state[:, lanes] += dot(b_mat, xf[:, lanes], ((0,), (0,)))

    @pl.when(i == pl.num_programs(0) - 1)
    def _():
        is_odd = odd[0] == 1
        low, high = state[:, 0:half], state[:, half:]
        keep[...] = jnp.where(is_odd, high, low)
        send[...] = jnp.where(is_odd, low, high).astype(BF16)


def conv_states(odd, x, bc, halo, wx, wbc, f_dev, ones):
    length, width = x.shape
    bc_width = bc.shape[1]
    half = width // 2
    lead = lambda i, _: (jnp.maximum(i * (TOK_A // LEAD) - 1, 0), 0)
    block = lambda i, _: (i, 0)
    return pl.pallas_call(
        conv_kernel,
        grid_spec=pltpu.PrefetchScalarGridSpec(
            num_scalar_prefetch=1,
            grid=(length // TOK_A,),
            in_specs=[
                pl.BlockSpec((TOK_A, width), block),
                pl.BlockSpec((LEAD, width), lead),
                pl.BlockSpec((TOK_A, bc_width), block),
                pl.BlockSpec((LEAD, bc_width), lead),
                whole(halo.shape),
                whole(wx.shape),
                whole(wbc.shape),
                pl.BlockSpec((TOK_A, f_dev.shape[1]), block),
                whole(ones.shape),
            ],
            out_specs=[
                pl.BlockSpec((TOK_A, width), block),
                pl.BlockSpec((TOK_A, bc_width), block),
                whole((N, half)),
                whole((N, half)),
            ],
            scratch_shapes=[
                pltpu.VMEM((LEAD + TOK_A, width + bc_width), F32),
                pltpu.VMEM((TOK_A, width), BF16),
                pltpu.VMEM((N, width), F32),
            ],
        ),
        out_shape=(
            jax.ShapeDtypeStruct((length, width), BF16),
            jax.ShapeDtypeStruct((length, bc_width), BF16),
            jax.ShapeDtypeStruct((N, half), F32),
            jax.ShapeDtypeStruct((N, half), BF16),
        ),
        compiler_params=params(),
        name="conv_states",
    )(odd, x, x, bc, bc, halo, wx, wbc, f_dev, ones)


def scan_kernel(head0, x, bc, z, cum, cum_t, st, f_blk, e_blk, e_dev, blk_x, skip, ones, u_out, v_out, state):
    i = pl.program_id(0)
    rows, width = x.shape
    per_slab = SLAB // P_SIZE

    @pl.when(i == 0)
    def _():
        state[...] = jnp.zeros_like(state)

    row = lax.broadcasted_iota(jnp.int32, (rows, rows), 0)
    col = lax.broadcasted_iota(jnp.int32, (rows, rows), 1)
    b_mat = bc[:, 0:N]
    c_mat = bc[:, N : 2 * N]
    scores = jnp.where(row >= col, dot(c_mat, b_mat, ((1,), (1,))), 0.0)
    lane = lax.broadcasted_iota(jnp.int32, (rows, 2 * P_SIZE), 1)
    first = lane < P_SIZE
    zero = jnp.zeros((rows, 2 * P_SIZE), BF16)
    fade_rows = blk_x[pl.ds(i, 1), :]
    for s in range(width // SLAB):
        lanes = slice(s * SLAB, (s + 1) * SLAB)
        xs = x[:, lanes].astype(F32)
        sel = ones[:, lanes]
        xd = (xs * dot(st[...], sel)).astype(BF16)
        old = state[:, lanes]
        carried = dot(c_mat, old.astype(BF16)) * dot(e_blk[...], sel)
        within = []
        for q in range(per_slab // 2):
            tables = []
            for h in (2 * q, 2 * q + 1):
                head = head0 + s * per_slab + h
                gap = jnp.minimum(cum[:, head : head + 1] - cum_t[head : head + 1, :], 0.0)
                tables.append((scores * jnp.exp2(gap)).astype(BF16))
            xp = xd[:, q * 2 * P_SIZE : (q + 1) * 2 * P_SIZE]
            stacked = jnp.concatenate([jnp.where(first, xp, zero), jnp.where(first, zero, xp)], 0)
            within.append(dot(jnp.concatenate(tables, 1), stacked))
        y = jnp.concatenate(within, 1) + carried + skip[:, lanes] * xs
        gate = half_silu(z[:, lanes].astype(F32) * 0.5)
        u_out[:, lanes] = (y * gate).astype(BF16)
        v_out[:, lanes] = (gate * dot(e_dev[...], sel)).astype(BF16)
        xf = (xs * dot(f_blk[...], sel)).astype(BF16)
        state[:, lanes] = old * fade_rows[:, lanes] + dot(b_mat, xf, ((0,), (0,)))


def scan_part(part, x, bc, z, cum, cum_t, st, f_blk, e_blk, e_dev, blk_x, skip, ones):
    length, full = x.shape
    width = full // B_PARTS
    groups = bc.shape[1] // (2 * N)
    group = part * groups // B_PARTS
    heads = cum.shape[1]
    blocks = length // TOK_B
    out = jax.ShapeDtypeStruct((length, width), BF16)
    cols = lambda i: (i, part)
    narrow = pl.BlockSpec((TOK_B, 2 * heads), lambda i: (i, 0))
    return pl.pallas_call(
        functools.partial(scan_kernel, part * heads // B_PARTS),
        grid=(blocks,),
        in_specs=[
            pl.BlockSpec((TOK_B, width), cols),
            pl.BlockSpec((TOK_B, 2 * N), lambda i: (i, group)),
            pl.BlockSpec((TOK_B, width), cols),
            pl.BlockSpec((TOK_B, heads), lambda i: (i, 0)),
            pl.BlockSpec((heads, TOK_B), lambda i: (0, i)),
            narrow,
            narrow,
            narrow,
            narrow,
            pl.BlockSpec((blocks, width), lambda i: (0, part)),
            pl.BlockSpec((1, width), lambda i: (0, part)),
            pl.BlockSpec((2 * heads, width), lambda i: (0, part)),
        ],
        out_specs=[pl.BlockSpec((TOK_B, width), lambda i: (i, 0))] * 2,
        out_shape=(out, out),
        scratch_shapes=[pltpu.VMEM((N, width), F32)],
        compiler_params=params(),
        cost_estimate=pl.CostEstimate(
            flops=length * width * 4000, bytes_accessed=length * width * 10, transcendentals=length * width * 4
        ),
        name="scan_part",
    )(x, bc, z, cum, cum_t, st, f_blk, e_blk, e_dev, blk_x, skip, ones)


def norm_kernel(info, bc, keep, recv, gain, *refs):
    uv, out = refs[:-1], refs[-1]
    us, vs = uv[:B_PARTS], uv[B_PARTS:]
    width = out.shape[1]
    groups = bc.shape[1] // (2 * N)
    per = width // groups
    half = width // 2
    part = width // B_PARTS
    is_odd = info[1] == 1
    for g in range(groups):
        c_mat = bc[:, 2 * N * g + N : 2 * N * (g + 1)]
        pieces = []
        squares = None
        for p in range(g * per // part, (g + 1) * per // part):
            start = p * part
            side = start // half
            lanes = slice(start - side * half, start - side * half + part)
            mine, other = keep[:, lanes], recv[:, lanes]
            inc = jnp.where(is_odd, other, mine) if side == 0 else jnp.where(is_odd, mine, other)
            gated = us[p][...].astype(F32) + vs[p][...].astype(F32) * dot(c_mat, inc)
            square = jnp.sum(gated * gated, axis=-1, keepdims=True)
            squares = square if squares is None else squares + square
            pieces.append((start, gated))
        scale = lax.rsqrt(squares * (1.0 / per) + EPS)
        for start, gated in pieces:
            out[:, start : start + part] = (gated * scale * gain[:, start : start + part]).astype(BF16)


def norm_rows(info, count, bc, keep, recv, gain, us, vs):
    rows = 128
    steps = count // rows
    width = gain.shape[1]
    take = lambda i, info: (info[0] * steps + i, 0)
    return pl.pallas_call(
        norm_kernel,
        grid_spec=pltpu.PrefetchScalarGridSpec(
            num_scalar_prefetch=1,
            grid=(steps,),
            in_specs=[
                pl.BlockSpec((rows, bc.shape[1]), take),
                whole(keep.shape),
                whole(recv.shape),
                whole(gain.shape),
            ]
            + [pl.BlockSpec((rows, u.shape[1]), take) for u in us + vs],
            out_specs=pl.BlockSpec((rows, width), lambda i, info: (i, 0)),
        ),
        out_shape=jax.ShapeDtypeStruct((count, width), BF16),
        compiler_params=params(),
        cost_estimate=pl.CostEstimate(
            flops=count * width * 256, bytes_accessed=count * width * 6, transcendentals=0
        ),
        name="norm_rows",
    )(info, bc, keep, recv, gain, *us, *vs)


def project_kernel(a0, a1, w0, w1, out):
    out[...] = (dot(a0[...], w0[...]) + dot(a1[...], w1[...])).astype(out.dtype)


def project(a0, a1, w0, w1, first, count, kind):
    rows, depth = a0.shape
    tile = min(512, count)
    base = first // tile
    return pl.pallas_call(
        project_kernel,
        grid=(count // tile,),
        in_specs=[
            whole(a0.shape),
            whole(a1.shape),
            pl.BlockSpec((depth, tile), lambda j: (0, base + j)),
            pl.BlockSpec((depth, tile), lambda j: (0, base + j)),
        ],
        out_specs=pl.BlockSpec((rows, tile), lambda j: (0, j)),
        out_shape=jax.ShapeDtypeStruct((rows, count), kind),
        compiler_params=params(),
        cost_estimate=pl.CostEstimate(
            flops=4 * rows * depth * count, bytes_accessed=4 * depth * count, transcendentals=0
        ),
        name="project",
    )(a0, a1, w0, w1)


def shift(block, distance):
    size = lax.axis_size("seq")
    return lax.ppermute(block, "seq", [(i, i + distance) for i in range(size - distance)])


def swap(block, axis, bit):
    return lax.ppermute(block, axis, [(i, i ^ bit) for i in range(lax.axis_size(axis))])


def after(value, *others):
    return lax.optimization_barrier((value,) + others)[0]


def local(
    x_input,
    z_input,
    bc_input,
    conv_weight_x,
    conv_weight_bc,
    step_size,
    log_decay,
    skip_gain,
    norm_gain,
    out_weight,
):
    length, width = x_input.shape
    heads = step_size.shape[1]
    seq = lax.axis_size("seq")
    ways = lax.axis_size("head")
    me = lax.axis_index("seq")
    mine = lax.axis_index("head")
    half = width // 2
    odd = me % 2
    is_odd = odd == 1

    bc = bc_input.reshape(length, -1)
    halo = shift(jnp.concatenate([x_input[length - LEAD :], bc[length - LEAD :]], 1), 1)
    weight_mate = swap(out_weight, "head", 1)

    ones = jnp.asarray(np.tile(np.repeat(np.eye(heads), P_SIZE, axis=1), (2, 1)), BF16)
    cum, cum_t, f_dev, st, f_blk, e_blk, e_dev, blk_x, dev_total = decays(log_decay, step_size, ones)
    x_conv, bc_conv, keep, send = conv_states(
        odd.reshape(1).astype(jnp.int32),
        x_input,
        bc,
        halo,
        conv_weight_x,
        conv_weight_bc.reshape(KCONV, -1),
        f_dev,
        ones,
    )

    logs = lax.all_gather(dev_total[0], "seq")
    side = jnp.where(is_odd, logs[:, heads // 2 :], logs[:, : heads // 2])
    spread = lambda v: jnp.repeat(jnp.exp2(v), P_SIZE)[None, :]
    pair = me // 2
    even_log = lax.dynamic_index_in_dim(side, 2 * pair, 0, keepdims=False)
    odd_log = lax.dynamic_index_in_dim(side, 2 * pair + 1, 0, keepdims=False)
    index = jnp.arange(seq)[:, None] // 2

    def window(count):
        inside = (index >= pair - count) & (index < pair)
        return spread(jnp.sum(jnp.where(inside, side, 0.0), axis=0))

    skip = jnp.repeat(skip_gain, P_SIZE)[None, :]
    us, vs = [], []

    def scan_next(x):
        k = len(us)
        u, v = scan_part(k, x, bc_conv, z_input, cum, cum_t, st, f_blk, e_blk, e_dev, blk_x, skip, ones)
        us.append(u)
        vs.append(v)

    got = swap(send, "seq", 1)
    scan_next(x_conv)
    received = got.astype(F32)
    first = jnp.where(is_odd, received, keep)
    second = jnp.where(is_odd, keep, received)
    own = spread(odd_log) * first + second
    behind = jnp.zeros_like(own)
    covered = 0
    pairs = seq // 2
    while covered < pairs - 1:
        if covered == 0:
            wave = own
        else:
            wave = own + spread(even_log + odd_log) * behind
        arrived = shift(wave.astype(BF16), 2 * (covered + 1))
        if len(us) < B_PARTS - 1:
            scan_next(after(x_conv, got))
        got = arrived
        behind = behind + window(covered) * arrived.astype(F32)
        covered = 2 * covered + 1
    entering_odd = spread(even_log) * behind + first
    back = swap(jnp.where(is_odd, behind, entering_odd).astype(BF16), "seq", 1)
    while len(us) < B_PARTS:
        scan_next(after(x_conv, got))
    held = jnp.where(is_odd, entering_odd, behind).astype(BF16)

    count = length // ways
    gain = norm_gain[None, :]

    def rows_for(target):
        info = jnp.stack([target, odd]).astype(jnp.int32)
        return norm_rows(info, count, bc_conv, held, back, gain, us, vs)

    far_mate = swap(rows_for(mine ^ 3), "head", 1)
    far = rows_for(mine ^ 2)
    columns = out_weight.shape[1]
    chunk = columns // 4
    arrivals = []
    for c in range(0, columns, chunk):
        sent = project(far, far_mate, out_weight, weight_mate, c, chunk, BF16)
        arrivals.append(swap(sent, "head", 2))
    near_mate = swap(rows_for(mine ^ 1), "head", 1)
    near = rows_for(mine)
    total = project(near, near_mate, out_weight, weight_mate, 0, columns, F32)
    return (total + jnp.concatenate(arrivals, 1).astype(F32)).astype(BF16)


def solution(mesh):
    in_specs = (
        P("seq", "head"),
        P("seq", "head"),
        P("seq", "head", None),
        P(None, "head"),
        P(None, "head", None),
        P("seq", "head"),
        P("seq", "head"),
        P("head"),
        P("head"),
        P("head", None),
    )
    out_specs = P(("seq", "head"), None)
    return jax.shard_map(local, mesh=mesh, in_specs=in_specs, out_specs=out_specs, check_vma=False)
```

time: 543 us -> 184 us (0.34); the launches traced: 534 us -> 182 us
  waiting for transfers between devices: 264 us -> 22.6 us
  Pallas kernels: 0 us -> 103 us
  matrix products: 82.2 us -> 0 us
  other arithmetic: 59.5 us -> 5.07 us
  local copies, waits for them, and re-layouts: 71.3 us -> 19.3 us
  starting transfers between devices: 42.1 us -> 13.3 us
  blocking collectives: 0 us -> 18.6 us
  between operations: 14.1 us -> 0.35 us
    reduce_scatter x1 -> x0, waiting for transfers between devices: 130 us -> none  [local(): lax.psum_scatter(jnp.dot(normed, out_weight, preferred_element_type=jnp.f...]
    ppermute x9 -> x12, waiting for transfers between devices: 134 us -> 22.6 us  [the longest x9 17.3 us: swap(): lax.ppermute(block, axis, [(i, i ^ bit) for i in range(lax.axis_size(axis...]
    pallas_call x0 -> x15, Pallas kernels: none -> 103 us  [the longest x5 36.7 us: project(): pl.pallas_call(project_kernel, grid=(count // tile,), in_specs=[whole(a0....]
    dot_general x5 -> x0, matrix products: 82.2 us -> none  [the longest x1 42 us: local(): jnp.einsum('ctsgh,csghp->ctghp', scores[..., None] * decay_table, driven,...]
    ppermute x9 -> x12, starting transfers between devices: 42 us -> 13.3 us  [the longest x3 7.57 us: shift(): lax.ppermute(block, 'seq', [(i, i + distance) for i in range(size - dista...]
    all_gather x0 -> x1, blocking collectives: none -> 18.6 us  [local(): logs = lax.all_gather(dev_total[0], 'seq')]
    reshape x1 -> x0, other arithmetic: 17.2 us -> none  [local(): x_conv.astype(jnp.float32)]
    add x1 -> x0, local copies, waits for them, and re-layouts: 13.8 us -> none  [local(): within + carried + skip_gain.reshape(groups, per_group)[..., None] * x_float]
  transfers between devices with their start and end apart: 10 -> 12, of which waited for: 8 -> 4; matrix products, arithmetic and copies ran while one was open for 7% -> 4% of each run, Pallas kernels for 0% -> 57%
where the time goes in v1:
time: 184 us; the launch traced here: 182 us
  Pallas kernels  103 us (56%)
  waiting for transfers between devices  22.6 us (12%)
  local copies, waits for them, and re-layouts  19.3 us (10%)
  blocking collectives  18.6 us (10%)
  starting transfers between devices  13.3 us (7%)
  other arithmetic  5.07 us (3%)
    pallas_call x5, Pallas kernels, project(): pl.pallas_call(project_kernel, grid=(count // tile,), in_specs=[whole(a0....  36.7 us
    pallas_call x4, Pallas kernels, scan_part(): pl.pallas_call(functools.partial(scan_kernel, part * heads // B_PARTS), g...  35.1 us
    all_gather x1, blocking collectives, local(): logs = lax.all_gather(dev_total[0], 'seq')  18.6 us
    pallas_call x1, Pallas kernels, conv_states(): pl.pallas_call(conv_kernel, grid_spec=pltpu.PrefetchScalarGridSpec(num_sc...  17.4 us
    ppermute x9, waiting for transfers between devices, swap(): lax.ppermute(block, axis, [(i, i ^ bit) for i in range(lax.axis_size(axis...  17.3 us
    unnamed x57, local copies, waits for them, and re-layouts  16.8 us
    pallas_call x4, Pallas kernels, norm_rows(): pl.pallas_call(norm_kernel, grid_spec=pltpu.PrefetchScalarGridSpec(num_sc...  12.5 us
    ppermute x3, starting transfers between devices, shift(): lax.ppermute(block, 'seq', [(i, i + distance) for i in range(size - dista...  7.57 us
  transfers between devices with their start and end apart: 12, of which 4 were waited for; matrix products, arithmetic and copies ran while one was open for 4% of the time, Pallas kernels for 57%

profile of v1, /device:TPU:0, one launch (start us, length us, event | category | flops | bytes accessed | tf_op | source)
XLA Modules:
  0.0 182.4 jit_solution(16021497454048762463)
XLA Ops:
  2.1 4.5 %collective-permute-start = (bf16[16,2560]{1,0:T(8,128)(2,1)S(1)}, bf16[16,2560]{1,0:T(8,128)(2,1)S(1)}, u32[]{:S(2)}, u32[]{:S(2)}) collective-permute-start(bf16[16,2560]{1,0:T(8,128)(2,1)S(1)} %pad_maximum_fusion), channel_id=1, source_target_pairs={{0,4},{4,8},{8,12},{12,16},{16,20},{20,24},{24,28},{1,5},{5,9},{9,... | collective-permute-start | bytes 245768 | tf_op jit(solution)/shard_map/ppermute | solution.py:377
  14.1 18.6 %all-gather = f32[8,1,32]{2,1,0:T(1,128)S(1)} all-gather(f32[1,1,32]{2,1,0:T(1,128)S(1)} %bitcast.29), channel_id=1, replica_groups=mesh['seq'=8,'head'=4] {'seq'}, dimensions={0}, use_global_device_ids=true | all-gather | bytes 1152 | tf_op jit(solution)/shard_map/all_gather | solution.py:427
  33.5 1.4 copy.16
  35.0 17.4 %conv_states.1 = (bf16[1024,2048]{1,0:T(8,128)(2,1)}, bf16[1024,512]{1,0:T(8,128)(2,1)S(1)}, f32[128,1024]{1,0:T(8,128)S(1)}, bf16[128,1024]{1,0:T(8,128)(2,1)}) custom-call(s32[1]{0:T(128)} %bitcast.1.odd, bf16[1024,2048]{1,0:T(8,128)(2,1)} %x_lead.1, bf16[1024,2048]{1,0:T(8,128)(2,1)} %x_lead.1, bf16[1024,512]{1,0:T(8,128)(2,1)S(1)} %bitcast.21, ...), custom_call_target="tpu_custom_call" | custom-call | tf_op jit(solution)/shard_map/conv_states/pallas_call | solution.py:172
  54.0 6.0 %collective-permute-done.1 = bf16[128,1024]{1,0:T(8,128)(2,1)S(1)} collective-permute-done((bf16[128,1024]{1,0:T(8,128)(2,1)}, bf16[128,1024]{1,0:T(8,128)(2,1)S(1)}, u32[]{:S(2)}, u32[]{:S(2)}) %collective-permute-start.1) | collective-permute-done | bytes 262176 | tf_op jit(solution)/shard_map/ppermute | solution.py:381
  61.8 5.3 %collective-permute-done.2 = bf16[128,1024]{1,0:T(8,128)(2,1)S(1)} collective-permute-done((bf16[128,1024]{1,0:T(8,128)(2,1)S(1)}, bf16[128,1024]{1,0:T(8,128)(2,1)S(1)}, u32[]{:S(2)}, u32[]{:S(2)}) %collective-permute-start.2) | collective-permute-done | bytes 262176 | tf_op jit(solution)/shard_map/ppermute | solution.py:377
  67.2 1.8 collective-permute-start.3
  71.8 8.8 %scan_part.4 = (bf16[1024,512]{1,0:T(8,128)(2,1)S(1)}, bf16[1024,512]{1,0:T(8,128)(2,1)}) custom-call(bf16[1024,2048]{1,0:T(8,128)(2,1)} %get-tuple-element.47.x, bf16[1024,512]{1,0:T(8,128)(2,1)} %copy-done, bf16[1024,2048]{1,0:T(8,128)(2,1)} %z.7, f32[1024,32]{1,0:T(8,128)S(1)} %get-tuple-element.35.cum, f32[32,1024]{1,0:T(8,128)S(1)} %get-tuple-element.36.cum_t, ...), custom_call_target="tpu_custom_call" | custom-call | flops 2097152000 | bytes 5242880 | tf_op jit(solution)/shard_map/scan_part/pallas_call | solution.py:264
  80.6 8.8 %scan_part.5 = (bf16[1024,512]{1,0:T(8,128)(2,1)S(1)}, bf16[1024,512]{1,0:T(8,128)(2,1)}) custom-call(bf16[1024,2048]{1,0:T(8,128)(2,1)} %get-tuple-element.47.x, bf16[1024,512]{1,0:T(8,128)(2,1)} %copy-done, bf16[1024,2048]{1,0:T(8,128)(2,1)} %z.7, f32[1024,32]{1,0:T(8,128)S(1)} %get-tuple-element.35.cum, f32[32,1024]{1,0:T(8,128)S(1)} %get-tuple-element.36.cum_t, ...), custom_call_target="tpu_custom_call" | custom-call | flops 2097152000 | bytes 5242880 | tf_op jit(solution)/shard_map/scan_part/pallas_call | solution.py:264
  91.9 8.7 %scan_part.6 = (bf16[1024,512]{1,0:T(8,128)(2,1)S(1)}, bf16[1024,512]{1,0:T(8,128)(2,1)}) custom-call(bf16[1024,2048]{1,0:T(8,128)(2,1)} %get-tuple-element.47.x, bf16[1024,512]{1,0:T(8,128)(2,1)} %copy-done, bf16[1024,2048]{1,0:T(8,128)(2,1)} %z.7, f32[1024,32]{1,0:T(8,128)S(1)} %get-tuple-element.35.cum, f32[32,1024]{1,0:T(8,128)S(1)} %get-tuple-element.36.cum_t, ...), custom_call_target="tpu_custom_call" | custom-call | flops 2097152000 | bytes 5242880 | tf_op jit(solution)/shard_map/scan_part/pallas_call | solution.py:264
  101.6 8.8 %scan_part.7 = (bf16[1024,512]{1,0:T(8,128)(2,1)S(1)}, bf16[1024,512]{1,0:T(8,128)(2,1)}) custom-call(bf16[1024,2048]{1,0:T(8,128)(2,1)} %get-tuple-element.47.x, bf16[1024,512]{1,0:T(8,128)(2,1)} %copy-done, bf16[1024,2048]{1,0:T(8,128)(2,1)} %z.7, f32[1024,32]{1,0:T(8,128)S(1)} %get-tuple-element.35.cum, f32[32,1024]{1,0:T(8,128)S(1)} %get-tuple-element.36.cum_t, ...), custom_call_target="tpu_custom_call" | custom-call | flops 2097152000 | bytes 5242880 | tf_op jit(solution)/shard_map/scan_part/pallas_call | solution.py:264
  111.4 3.7 %norm_rows.7 = bf16[256,2048]{1,0:T(8,128)(2,1)} custom-call(s32[2]{0:T(128)S(1)} %pad_add_fusion.3.info, bf16[1024,512]{1,0:T(8,128)(2,1)S(1)} %copy-done.1, bf16[128,1024]{1,0:T(8,128)(2,1)S(1)} %get-tuple-element.57.keep, bf16[128,1024]{1,0:T(8,128)(2,1)S(1)} %collective-permute-done.4.recv, f32[1,2048]{1,0:T(1,128)S(1)} %bitcast.24, ...), custom_call_target="tpu_custom_call" | custom-call | flops 134217728 | bytes 3145728 | tf_op jit(solution)/shard_map/norm_rows/pallas_call | solution.py:325
  116.2 2.9 %norm_rows.5 = bf16[256,2048]{1,0:T(8,128)(2,1)S(1)} custom-call(s32[2]{0:T(128)S(1)} %pad_add_fusion.1.info, bf16[1024,512]{1,0:T(8,128)(2,1)S(1)} %copy-done.1, bf16[128,1024]{1,0:T(8,128)(2,1)S(1)} %get-tuple-element.57.keep, bf16[128,1024]{1,0:T(8,128)(2,1)S(1)} %copy-done.18, f32[1,2048]{1,0:T(1,128)S(1)} %bitcast.25, ...), custom_call_target="tpu_custom_call" | custom-call | flops 134217728 | bytes 3145728 | tf_op jit(solution)/shard_map/norm_rows/pallas_call | solution.py:325
  119.8 2.9 %norm_rows.6.a0 = bf16[256,2048]{1,0:T(8,128)(2,1)S(1)} custom-call(s32[2]{0:T(128)S(1)} %pad_add_fusion.2.info, bf16[1024,512]{1,0:T(8,128)(2,1)S(1)} %copy-done.1, bf16[128,1024]{1,0:T(8,128)(2,1)S(1)} %get-tuple-element.57.keep, bf16[128,1024]{1,0:T(8,128)(2,1)S(1)} %copy-done.18, f32[1,2048]{1,0:T(1,128)S(1)} %bitcast.26, ...), custom_call_target="tpu_custom_call" | custom-call | flops 134217728 | bytes 3145728 | tf_op jit(solution)/shard_map/norm_rows/pallas_call | solution.py:325
  122.8 3.0 %norm_rows.4.a0 = bf16[256,2048]{1,0:T(8,128)(2,1)S(1)} custom-call(s32[2]{0:T(128)S(1)} %pad_add_fusion.info, bf16[1024,512]{1,0:T(8,128)(2,1)S(1)} %copy-done.1, bf16[128,1024]{1,0:T(8,128)(2,1)S(1)} %get-tuple-element.57.keep, bf16[128,1024]{1,0:T(8,128)(2,1)S(1)} %copy-done.19, f32[1,2048]{1,0:T(1,128)S(1)} %bitcast.27, ...), custom_call_target="tpu_custom_call" | custom-call | flops 134217728 | bytes 3145728 | tf_op jit(solution)/shard_map/norm_rows/pallas_call | solution.py:325
  125.8 4.8 %project.6 = bf16[256,1024]{1,0:T(8,128)(2,1)S(1)} custom-call(bf16[256,2048]{1,0:T(8,128)(2,1)S(1)} %norm_rows.6.a0, bf16[256,2048]{1,0:T(8,128)(2,1)S(1)} %collective-permute-done.7.a1, bf16[2048,4096]{1,0:T(8,128)(2,1)} %w0.9, bf16[2048,4096]{1,0:T(8,128)(2,1)} %collective-permute-done.6.w1), custom_call_target="tpu_custom_call" | custom-call | flops 2147483648 | bytes 8388608 | tf_op jit(solution)/shard_map/project/pallas_call | solution.py:356
  130.6 1.6 collective-permute-start.8
  132.2 4.8 %project.7 = bf16[256,1024]{1,0:T(8,128)(2,1)S(1)} custom-call(bf16[256,2048]{1,0:T(8,128)(2,1)S(1)} %norm_rows.6.a0, bf16[256,2048]{1,0:T(8,128)(2,1)S(1)} %collective-permute-done.7.a1, bf16[2048,4096]{1,0:T(8,128)(2,1)} %w0.9, bf16[2048,4096]{1,0:T(8,128)(2,1)} %collective-permute-done.6.w1), custom_call_target="tpu_custom_call" | custom-call | flops 2147483648 | bytes 8388608 | tf_op jit(solution)/shard_map/project/pallas_call | solution.py:356
  137.6 4.8 %project.8 = bf16[256,1024]{1,0:T(8,128)(2,1)S(1)} custom-call(bf16[256,2048]{1,0:T(8,128)(2,1)S(1)} %norm_rows.6.a0, bf16[256,2048]{1,0:T(8,128)(2,1)S(1)} %collective-permute-done.7.a1, bf16[2048,4096]{1,0:T(8,128)(2,1)} %w0.9, bf16[2048,4096]{1,0:T(8,128)(2,1)} %collective-permute-done.6.w1), custom_call_target="tpu_custom_call" | custom-call | flops 2147483648 | bytes 8388608 | tf_op jit(solution)/shard_map/project/pallas_call | solution.py:356
  142.4 1.6 collective-permute-start.10
  144.0 4.8 %project.9 = bf16[256,1024]{1,0:T(8,128)(2,1)S(1)} custom-call(bf16[256,2048]{1,0:T(8,128)(2,1)S(1)} %norm_rows.6.a0, bf16[256,2048]{1,0:T(8,128)(2,1)S(1)} %collective-permute-done.7.a1, bf16[2048,4096]{1,0:T(8,128)(2,1)} %w0.9, bf16[2048,4096]{1,0:T(8,128)(2,1)} %collective-permute-done.6.w1), custom_call_target="tpu_custom_call" | custom-call | flops 2147483648 | bytes 8388608 | tf_op jit(solution)/shard_map/project/pallas_call | solution.py:356
  149.4 17.5 %project.5 = f32[256,4096]{1,0:T(8,128)} custom-call(bf16[256,2048]{1,0:T(8,128)(2,1)S(1)} %norm_rows.4.a0, bf16[256,2048]{1,0:T(8,128)(2,1)S(1)} %collective-permute-done.5.a1, bf16[2048,4096]{1,0:T(8,128)(2,1)} %w0.9, bf16[2048,4096]{1,0:T(8,128)(2,1)} %collective-permute-done.6.w1), custom_call_target="tpu_custom_call" | custom-call | flops 8589934592 | bytes 33554432 | tf_op jit(solution)/shard_map/project/pallas_call | solution.py:356
  167.9 10.3 %collective-permute-done.11 = bf16[256,1024]{1,0:T(8,128)(2,1)S(1)} collective-permute-done((bf16[256,1024]{1,0:T(8,128)(2,1)S(1)}, bf16[256,1024]{1,0:T(8,128)(2,1)S(1)}, u32[]{:S(2)}, u32[]{:S(2)}) %collective-permute-start.11) | collective-permute-done | bytes 524320 | tf_op jit(solution)/shard_map/ppermute | solution.py:381
  178.2 4.2 %add_convert_fusion = bf16[256,4096]{1,0:T(8,128)(2,1)} fusion(f32[256,4096]{1,0:T(8,128)} %project.5, bf16[256,1024]{1,0:T(8,128)(2,1)S(1)} %collective-permute-done.11, bf16[256,1024]{1,0:T(8,128)(2,1)S(1)} %collective-permute-done.10, bf16[256,1024]{1,0:T(8,128)(2,1)S(1)} %collective-permute-done.9, bf16[256,1024]{1,0:T(8,128)(2,1)S(1)} %collective-permute-done.8), kind=kLoop, calls=%fused_computation | loop fusion | flops 10485760 | bytes 8388608 | tf_op jit(solution)/shard_map/convert_element_type | solution.py:492
  (101 shorter events, 25.1 us)
Async XLA Ops:
  0.0 35.0 %copy-start.6 = (bf16[64,2048]{1,0:T(8,128)(2,1)S(1)}, bf16[64,2048]{1,0:T(8,128)(2,1)}, u32[]{:S(2)}) copy-start(bf16[64,2048]{1,0:T(8,128)(2,1)} %constant.65.clone.ones) | copy-start | bytes 786436
  0.0 35.0 %copy-start.24 = (f32[4,2048]{1,0:T(4,128)S(1)}, f32[4,2048]{1,0:T(4,128)}, u32[]{:S(2)}) copy-start(f32[4,2048]{1,0:T(4,128)} %wx.1) | copy-start | bytes 98308
  0.0 125.8 %collective-permute-start.6 = (bf16[2048,4096]{1,0:T(8,128)(2,1)}, bf16[2048,4096]{1,0:T(8,128)(2,1)}, u32[]{:S(2)}, u32[]{:S(2)}) collective-permute-start(bf16[2048,4096]{1,0:T(8,128)(2,1)} %w0.9), channel_id=1, source_target_pairs={{0,1},{1,0},{2,3},{3,2},{4,5},{5,4},{6,7},{7,6},{8,9},{9,8},{10,11... | collective-permute-start | bytes 50331656 | tf_op jit(solution)/shard_map/ppermute | solution.py:381
  2.1 32.9 %collective-permute-start = (bf16[16,2560]{1,0:T(8,128)(2,1)S(1)}, bf16[16,2560]{1,0:T(8,128)(2,1)S(1)}, u32[]{:S(2)}, u32[]{:S(2)}) collective-permute-start(bf16[16,2560]{1,0:T(8,128)(2,1)S(1)} %pad_maximum_fusion), channel_id=1, source_target_pairs={{0,4},{4,8},{8,12},{12,16},{16,20},{20,24},{24,28},{1,5},{5,9},{9,... | collective-permute-start | bytes 245768 | tf_op jit(solution)/shard_map/ppermute | solution.py:377
  14.1 66.5 %copy-start.9 = (bf16[1024,64]{1,0:T(8,128)(2,1)}, bf16[1024,64]{1,0:T(8,128)(2,1)S(1)}, u32[]{:S(2)}) copy-start(bf16[1024,64]{1,0:T(8,128)(2,1)S(1)} %get-tuple-element.38.f_blk) | copy-start | bytes 393220
  35.0 18.4 %copy-start.25 = (f32[32]{0:T(128)S(1)}, f32[32]{0:T(128)}, u32[]{:S(2)}) copy-start(f32[32]{0:T(128)} %param.18) | copy-start | bytes 388
  53.4 15.7 %copy-start.7 = (f32[128,1024]{1,0:T(8,128)}, f32[128,1024]{1,0:T(8,128)S(1)}, u32[]{:S(2)}) copy-start(f32[128,1024]{1,0:T(8,128)S(1)} %get-tuple-element.33) | copy-start | bytes 1572868
  53.4 6.6 %collective-permute-start.1 = (bf16[128,1024]{1,0:T(8,128)(2,1)}, bf16[128,1024]{1,0:T(8,128)(2,1)S(1)}, u32[]{:S(2)}, u32[]{:S(2)}) collective-permute-start(bf16[128,1024]{1,0:T(8,128)(2,1)} %get-tuple-element.32), channel_id=1, source_target_pairs={{0,4},{4,0},{8,12},{12,8},{16,20},{20,16},{24,28},{28,24},{1,5},{5... | collective-permute-start | bytes 786440 | tf_op jit(solution)/shard_map/ppermute | solution.py:381
  60.1 7.0 %collective-permute-start.2 = (bf16[128,1024]{1,0:T(8,128)(2,1)S(1)}, bf16[128,1024]{1,0:T(8,128)(2,1)S(1)}, u32[]{:S(2)}, u32[]{:S(2)}) collective-permute-start(bf16[128,1024]{1,0:T(8,128)(2,1)S(1)} %fusion.1), channel_id=1, source_target_pairs={{0,8},{4,12},{8,16},{12,20},{16,24},{20,28},{1,9},{5,13},{9,17},{1... | collective-permute-start | bytes 786440 | tf_op jit(solution)/shard_map/ppermute | solution.py:377
  67.2 23.1 %collective-permute-start.3 = (bf16[128,1024]{1,0:T(8,128)(2,1)S(1)}, bf16[128,1024]{1,0:T(8,128)(2,1)S(1)}, u32[]{:S(2)}, u32[]{:S(2)}) collective-permute-start(bf16[128,1024]{1,0:T(8,128)(2,1)S(1)} %add_convert_fusion.1), channel_id=1, source_target_pairs={{0,16},{4,20},{8,24},{12,28},{1,17},{5,21},{9,25},{13,29},{2,18},{... | collective-permute-start | bytes 786440 | tf_op jit(solution)/shard_map/ppermute | solution.py:377
  71.8 8.8 %copy-start.13 = (bf16[1024,64]{1,0:T(8,128)(2,1)S(1)}, bf16[1024,64]{1,0:T(8,128)(2,1)}, u32[]{:S(2)}) copy-start(bf16[1024,64]{1,0:T(8,128)(2,1)} %copy-done.11) | copy-start | bytes 393220
  71.8 8.8 %copy-start.16 = (bf16[1024,64]{1,0:T(8,128)(2,1)S(1)}, bf16[1024,64]{1,0:T(8,128)(2,1)}, u32[]{:S(2)}) copy-start(bf16[1024,64]{1,0:T(8,128)(2,1)} %copy-done.14) | copy-start | bytes 393220
  80.6 9.8 %copy-start.8 = (f32[128,1024]{1,0:T(8,128)S(1)}, f32[128,1024]{1,0:T(8,128)}, u32[]{:S(2)}) copy-start(f32[128,1024]{1,0:T(8,128)} %copy-done.7) | copy-start | bytes 1572868
  90.6 20.8 %collective-permute-start.4 = (bf16[128,1024]{1,0:T(8,128)(2,1)S(1)}, bf16[128,1024]{1,0:T(8,128)(2,1)S(1)}, u32[]{:S(2)}, u32[]{:S(2)}) collective-permute-start(bf16[128,1024]{1,0:T(8,128)(2,1)S(1)} %get-tuple-element.56), channel_id=1, source_target_pairs={{0,4},{4,0},{8,12},{12,8},{16,20},{20,16},{24,28},{28,24},{1,5},{5... | collective-permute-start | bytes 786440 | tf_op jit(solution)/shard_map/ppermute | solution.py:381
  101.6 9.8 %copy-start.1 = (bf16[1024,512]{1,0:T(8,128)(2,1)S(1)}, bf16[1024,512]{1,0:T(8,128)(2,1)}, u32[]{:S(2)}) copy-start(bf16[1024,512]{1,0:T(8,128)(2,1)} %copy-done) | copy-start | bytes 3145732
  101.6 9.8 %copy-start.23 = (f32[2048]{0:T(1024)S(1)}, f32[2048]{0:T(1024)}, u32[]{:S(2)}) copy-start(f32[2048]{0:T(1024)} %param.19) | copy-start | bytes 24580
  111.4 3.7 %copy-start.17 = (bf16[128,1024]{1,0:T(8,128)(2,1)}, bf16[128,1024]{1,0:T(8,128)(2,1)S(1)}, u32[]{:S(2)}) copy-start(bf16[128,1024]{1,0:T(8,128)(2,1)S(1)} %collective-permute-done.4.recv) | copy-start | bytes 786436
  115.1 10.6 %collective-permute-start.7 = (bf16[256,2048]{1,0:T(8,128)(2,1)}, bf16[256,2048]{1,0:T(8,128)(2,1)S(1)}, u32[]{:S(2)}, u32[]{:S(2)}) collective-permute-start(bf16[256,2048]{1,0:T(8,128)(2,1)} %norm_rows.7), channel_id=1, source_target_pairs={{0,1},{1,0},{2,3},{3,2},{4,5},{5,4},{6,7},{7,6},{8,9},{9,8},{10,11... | collective-permute-start | bytes 3145736 | tf_op jit(solution)/shard_map/ppermute | solution.py:381
  119.1 30.3 %collective-permute-start.5 = (bf16[256,2048]{1,0:T(8,128)(2,1)S(1)}, bf16[256,2048]{1,0:T(8,128)(2,1)S(1)}, u32[]{:S(2)}, u32[]{:S(2)}) collective-permute-start(bf16[256,2048]{1,0:T(8,128)(2,1)S(1)} %norm_rows.5), channel_id=1, source_target_pairs={{0,1},{1,0},{2,3},{3,2},{4,5},{5,4},{6,7},{7,6},{8,9},{9,8},{10,11... | collective-permute-start | bytes 3145736 | tf_op jit(solution)/shard_map/ppermute | solution.py:381
  119.8 3.0 %copy-start.19 = (bf16[128,1024]{1,0:T(8,128)(2,1)S(1)}, bf16[128,1024]{1,0:T(8,128)(2,1)}, u32[]{:S(2)}) copy-start(bf16[128,1024]{1,0:T(8,128)(2,1)} %copy-done.17) | copy-start | bytes 786436
  130.6 36.3 %collective-permute-start.8 = (bf16[256,1024]{1,0:T(8,128)(2,1)S(1)}, bf16[256,1024]{1,0:T(8,128)(2,1)S(1)}, u32[]{:S(2)}, u32[]{:S(2)}) collective-permute-start(bf16[256,1024]{1,0:T(8,128)(2,1)S(1)} %project.6), channel_id=1, source_target_pairs={{0,2},{1,3},{2,0},{3,1},{4,6},{5,7},{6,4},{7,5},{8,10},{9,11},{10,... | collective-permute-start | bytes 1572872 | tf_op jit(solution)/shard_map/ppermute | solution.py:381
  137.0 29.9 %collective-permute-start.9 = (bf16[256,1024]{1,0:T(8,128)(2,1)S(1)}, bf16[256,1024]{1,0:T(8,128)(2,1)S(1)}, u32[]{:S(2)}, u32[]{:S(2)}) collective-permute-start(bf16[256,1024]{1,0:T(8,128)(2,1)S(1)} %project.7), channel_id=1, source_target_pairs={{0,2},{1,3},{2,0},{3,1},{4,6},{5,7},{6,4},{7,5},{8,10},{9,11},{10,... | collective-permute-start | bytes 1572872 | tf_op jit(solution)/shard_map/ppermute | solution.py:381
  142.4 25.5 %collective-permute-start.10 = (bf16[256,1024]{1,0:T(8,128)(2,1)S(1)}, bf16[256,1024]{1,0:T(8,128)(2,1)S(1)}, u32[]{:S(2)}, u32[]{:S(2)}) collective-permute-start(bf16[256,1024]{1,0:T(8,128)(2,1)S(1)} %project.8), channel_id=1, source_target_pairs={{0,2},{1,3},{2,0},{3,1},{4,6},{5,7},{6,4},{7,5},{8,10},{9,11},{10,... | collective-permute-start | bytes 1572872 | tf_op jit(solution)/shard_map/ppermute | solution.py:381
  148.8 29.4 %collective-permute-start.11 = (bf16[256,1024]{1,0:T(8,128)(2,1)S(1)}, bf16[256,1024]{1,0:T(8,128)(2,1)S(1)}, u32[]{:S(2)}, u32[]{:S(2)}) collective-permute-start(bf16[256,1024]{1,0:T(8,128)(2,1)S(1)} %project.9), channel_id=1, source_target_pairs={{0,2},{1,3},{2,0},{3,1},{4,6},{5,7},{6,4},{7,5},{8,10},{9,11},{10,... | collective-permute-start | bytes 1572872 | tf_op jit(solution)/shard_map/ppermute | solution.py:381
  (14 other events, 12.5 us)

commit v2 on v1

v2 whole, which is shorter than its diff:
```python
import functools

import jax
import jax.numpy as jnp
import numpy as np
from jax import lax
from jax.experimental import pallas as pl
from jax.experimental.pallas import tpu as pltpu
from jax.sharding import PartitionSpec as P

P_SIZE = 64
N = 128
KCONV = 4
EPS = 1e-05
LOG2E = 1.4426950408889634

TOK_A = 256
ROWS_A = 32
TOK_B = 128
STEP_B = 512
EXTRA = 16
SLAB = 256
LEAD = 16
B_PARTS = 4
MIB = 1024 * 1024
HIGHEST = lax.Precision.HIGHEST
F32 = jnp.float32
BF16 = jnp.bfloat16


def params(mib):
    return pltpu.CompilerParams(vmem_limit_bytes=mib * MIB)


def dot(a, b, dims=((1,), (0,)), precision=None):
    return lax.dot_general(a, b, (dims, ((), ())), precision=precision, preferred_element_type=F32)


def half_silu(half):
    return half + half * jnp.tanh(half)


def whole(shape):
    return pl.BlockSpec(shape, lambda *_: (0,) * len(shape))


def decay_kernel(ld_t, step_t, ones, cum, cum_s, log_s, f_dev, f_blk, e_blk, rates):
    heads, length = ld_t.shape
    blocks = length // TOK_B
    row = lax.broadcasted_iota(jnp.int32, (TOK_B, TOK_B), 0)
    col = lax.broadcasted_iota(jnp.int32, (TOK_B, TOK_B), 1)
    lower = (row >= col).astype(F32)
    upper = (row <= col).astype(F32)
    eye = (row == col).astype(BF16)

    def put(ref, rows, value):
        high = value.astype(BF16)
        low = (value - high.astype(F32)).astype(BF16)
        ref[rows, :] = dot(eye, jnp.concatenate([high, low], 0), ((1,), (1,))).astype(BF16)

    cums, totals, row_totals = [], [], []
    for b in range(blocks):
        rows = slice(b * TOK_B, (b + 1) * TOK_B)
        logs = ld_t[:, rows] * LOG2E
        c = dot(lower, logs, ((1,), (1,)), HIGHEST)
        cum[rows, :] = c
        row_totals.append(c[TOK_B - 1 : TOK_B, :])
        c = dot(logs, upper, precision=HIGHEST)
        cums.append(c)
        totals.append(c[:, TOK_B - 1 : TOK_B])
    before, row_before = [jnp.zeros_like(totals[0])], [jnp.zeros_like(row_totals[0])]
    for b in range(blocks):
        before.append(before[-1] + totals[b])
        row_before.append(row_before[-1] + row_totals[b])
    total = before[-1]
    logs = jnp.concatenate(row_totals + row_before[:-1] + row_before[-1:] * 8, 0)
    rates[...] = dot(jnp.exp2(logs), ones[0:heads, :].astype(F32), precision=HIGHEST)
    for b in range(blocks):
        rows = slice(b * TOK_B, (b + 1) * TOK_B)
        s = step_t[:, rows]
        log_step = jnp.log2(s)
        log_s[:, rows] = log_step
        cum_s[:, rows] = cums[b] - log_step
        put(f_dev, rows, jnp.exp2(total - (cums[b] + before[b])) * s)
        put(f_blk, rows, jnp.exp2(totals[b] - cums[b]) * s)
        put(e_blk, rows, jnp.exp2(cums[b]))


def decays(log_decay, step, ones):
    length, heads = log_decay.shape
    blocks = length // TOK_B
    width = ones.shape[1]
    wide = jax.ShapeDtypeStruct((heads, length), F32)
    pair = jax.ShapeDtypeStruct((length, 2 * heads), BF16)
    return pl.pallas_call(
        decay_kernel,
        out_shape=(
            jax.ShapeDtypeStruct((length, heads), F32),
            wide,
            wide,
            pair,
            pair,
            pair,
            jax.ShapeDtypeStruct((2 * blocks + 8, width), F32),
        ),
        compiler_params=params(16),
        name="decays",
    )(log_decay.T, step.T, ones)


def put_message(ref, state, decay):
    high = decay.astype(BF16)
    low = (decay - high.astype(F32)).astype(BF16)
    rest = jnp.zeros((EXTRA - 2, state.shape[1]), BF16)
    ref[0:N, :] = state.astype(BF16)
    ref[N:, :] = jnp.concatenate([high, low, rest], 0)


def take_message(ref):
    extra = ref[N:, :].astype(F32)
    return ref[0:N, :].astype(F32), extra[0:1] + extra[1:2]


def conv_kernel(odd, x, x_lead, bc, bc_lead, halo, wx, wbc, f_dev, ones, rates, x_out, bc_out, keep, send, xf, state):
    i = pl.program_id(0)
    rows, width = x.shape
    bc_width = bc.shape[1]
    groups = bc_width // (2 * N)
    per = width // groups
    half = width // 2

    @pl.when(i == 0)
    def _():
        state[...] = jnp.zeros_like(state)

    def conv(src, lead, weights, emit):
        w0, w1, w2, w3 = [w * 0.5 for w in weights]
        back = LEAD - 8
        r1 = pltpu.roll(lead, 1, 0)
        last_x, last_p = lead[back:], (w1 * lead + w0 * r1)[back:]
        for r in range(0, rows, ROWS_A):
            cur = src(r).astype(F32)
            r1 = pltpu.roll(jnp.concatenate([last_x, cur], 0), 1, 0)[8:]
            p = w1 * cur + w0 * r1
            p2 = pltpu.roll(jnp.concatenate([last_p, p], 0), 2, 0)[8:]
            emit(r, half_silu((w3 * cur + w2 * r1) + p2))
            last_x, last_p = cur[ROWS_A - 8 :], p[ROWS_A - 8 :]

    start = i == 0
    for c in range(groups):
        for lanes in range(c * 2 * N, (c + 1) * 2 * N, N):
            ds = slice(lanes, lanes + N)

            def emit_bc(r, value):
                bc_out[r : r + ROWS_A, ds] = value.astype(BF16)

            lead = jnp.where(start, halo[:, width + lanes : width + lanes + N], bc_lead[:, ds]).astype(F32)
            inner = slice(lanes - c * 2 * N, lanes - c * 2 * N + N)
            conv(lambda r: bc[r : r + ROWS_A, ds], lead, [wbc[k, c : c + 1, inner] for k in range(KCONV)], emit_bc)

    def slab(c, _):
        ds = pl.ds(pl.multiple_of(c * SLAB, SLAB), SLAB)
        scale = dot(f_dev[...], ones[:, ds])

        def emit(r, value):
            value = value.astype(BF16)
            x_out[r : r + ROWS_A, ds] = value
            xf[r : r + ROWS_A, ds] = (value.astype(F32) * scale[r : r + ROWS_A]).astype(BF16)

        lead = jnp.where(start, halo[:, ds], x_lead[:, ds]).astype(F32)
        conv(lambda r: x[r : r + ROWS_A, ds], lead, [wx[k : k + 1, ds] for k in range(KCONV)], emit)
        return 0

    lax.fori_loop(0, width // SLAB, slab, 0)
    for g in range(groups):
        b_mat = bc_out[:, 2 * N * g : 2 * N * g + N]
        lanes = slice(g * per, (g + 1) * per)
        state[:, lanes] += dot(b_mat, xf[:, lanes], ((0,), (0,)))

    @pl.when(i == pl.num_programs(0) - 1)
    def _():
        is_odd = odd[0] == 1
        low, high = state[:, 0:half], state[:, half:]
        keep[...] = jnp.where(is_odd, high, low)
        row = rates.shape[0] - 1
        decay = jnp.where(is_odd, rates[row : row + 1, 0:half], rates[row : row + 1, half:])
        put_message(send, jnp.where(is_odd, low, high), decay)


def conv_states(odd, x, bc, halo, wx, wbc, f_dev, ones, rates):
    length, width = x.shape
    bc_width = bc.shape[1]
    half = width // 2
    lead = lambda i, _: (jnp.maximum(i * (TOK_A // LEAD) - 1, 0), 0)
    block = lambda i, _: (i, 0)
    return pl.pallas_call(
        conv_kernel,
        grid_spec=pltpu.PrefetchScalarGridSpec(
            num_scalar_prefetch=1,
            grid=(length // TOK_A,),
            in_specs=[
                pl.BlockSpec((TOK_A, width), block),
                pl.BlockSpec((LEAD, width), lead),
                pl.BlockSpec((TOK_A, bc_width), block),
                pl.BlockSpec((LEAD, bc_width), lead),
                whole(halo.shape),
                whole(wx.shape),
                whole(wbc.shape),
                pl.BlockSpec((TOK_A, f_dev.shape[1]), block),
                whole(ones.shape),
                whole(rates.shape),
            ],
            out_specs=[
                pl.BlockSpec((TOK_A, width), block),
                pl.BlockSpec((TOK_A, bc_width), block),
                whole((N, half)),
                whole((N + EXTRA, half)),
            ],
            scratch_shapes=[
                pltpu.VMEM((TOK_A, width), BF16),
                pltpu.VMEM((N, width), F32),
            ],
        ),
        out_shape=(
            jax.ShapeDtypeStruct((length, width), BF16),
            jax.ShapeDtypeStruct((length, bc_width), BF16),
            jax.ShapeDtypeStruct((N, half), F32),
            jax.ShapeDtypeStruct((N + EXTRA, half), BF16),
        ),
        compiler_params=params(20),
        name="conv_states",
    )(odd, x, x, bc, bc, halo, wx, wbc, f_dev, ones, rates)


def pair_kernel(odd, got, keep, rates, _, msg, own, first, aux):
    half = keep.shape[1]
    is_odd = odd[0] == 1
    arrived, their = take_message(got)
    row = rates.shape[0] - 1
    mine = jnp.where(is_odd, rates[row : row + 1, half:], rates[row : row + 1, 0:half])
    early = jnp.where(is_odd, arrived, keep[...])
    late = jnp.where(is_odd, keep[...], arrived)
    even_decay = jnp.where(is_odd, their, mine)
    odd_decay = jnp.where(is_odd, mine, their)
    state = odd_decay * early + late
    own[...] = state
    first[...] = early
    aux[0:8, :] = jnp.broadcast_to(even_decay, (8, half))
    aux[8:16, :] = jnp.broadcast_to(even_decay * odd_decay, (8, half))
    put_message(msg, state, even_decay * odd_decay)


def wave_kernel(got, own, aux, behind_in, _, msg, behind):
    before, decay = take_message(got)
    if behind_in is not None:
        before_decay = behind_in[N : N + 1, :]
        before = behind_in[0:N, :] + before_decay * before
        decay = before_decay * decay
    pair_decay = aux[8:9, :]
    behind[0:N, :] = before
    behind[N:, :] = jnp.broadcast_to(decay, (8, before.shape[1]))
    put_message(msg, own[...] + pair_decay * before, pair_decay * decay)


def last_kernel(odd, got, behind_in, first, aux, _, back, held):
    is_odd = odd[0] == 1
    before, _unused = take_message(got)
    if behind_in is not None:
        before = behind_in[0:N, :] + behind_in[N : N + 1, :] * before
    entering_odd = aux[0:1, :] * before + first[...]
    back[...] = jnp.where(is_odd, before, entering_odd).astype(BF16)
    held[...] = jnp.where(is_odd, entering_odd, before).astype(BF16)


SCALAR = pl.BlockSpec(memory_space=pltpu.SMEM)
FULL = pl.BlockSpec(memory_space=pltpu.VMEM)
ANY = pl.BlockSpec(memory_space=pl.ANY)


def combine(kernel, operands, specs, outs, name):
    return pl.pallas_call(
        kernel,
        in_specs=specs,
        out_specs=[FULL] * len(outs),
        out_shape=[jax.ShapeDtypeStruct(s, t) for s, t in outs],
        compiler_params=params(12),
        name=name,
    )(*operands)


def scan_kernel(head0, x, bc, z, cum, cum_s, log_s, f_blk, e_blk, rates, skip, ones, _, uv_out, state):
    i = pl.program_id(0)
    rows, width = x.shape
    per_slab = SLAB // P_SIZE
    inner = rows // TOK_B
    blocks = (rates.shape[0] - 8) // 2

    @pl.when(i == 0)
    def _():
        state[...] = jnp.zeros_like(state)

    row = lax.broadcasted_iota(jnp.int32, (TOK_B, TOK_B), 0)
    col = lax.broadcasted_iota(jnp.int32, (TOK_B, TOK_B), 1)
    keep = row >= col
    first = lax.broadcasted_iota(jnp.int32, (TOK_B, 2 * P_SIZE), 1) < P_SIZE
    zero = jnp.zeros((TOK_B, 2 * P_SIZE), BF16)

    def block(b, _):
        at = pl.ds(pl.multiple_of(b * TOK_B, TOK_B), TOK_B)
        b_mat = bc[at, 0:N]
        c_mat = bc[at, N : 2 * N]
        scores = jnp.where(keep, dot(c_mat, b_mat, ((1,), (1,))), 0.0)
        fade_rows = rates[pl.ds(i * inner + b, 1), :]
        lead_rows = rates[pl.ds(blocks + i * inner + b, 1), :]
        for s in range(width // SLAB):
            lanes = slice(s * SLAB, (s + 1) * SLAB)
            xb = x[at, lanes]
            sel = ones[:, lanes]
            old = state[:, lanes]
            rise = dot(e_blk[at, :], sel)
            carried = dot(c_mat, old.astype(BF16)) * rise
            within = []
            for q in range(per_slab // 2):
                tables = []
                for h in (2 * q, 2 * q + 1):
                    head = head0 + s * per_slab + h
                    column = cum[at, head : head + 1]
                    gap = jnp.minimum(column - cum_s[head : head + 1, at], log_s[head : head + 1, at])
                    tables.append((scores * jnp.exp2(gap)).astype(BF16))
                xp = xb[:, q * 2 * P_SIZE : (q + 1) * 2 * P_SIZE]
                stacked = jnp.concatenate([jnp.where(first, xp, zero), jnp.where(first, zero, xp)], 0)
                within.append(dot(jnp.concatenate(tables, 1), stacked))
            xs = xb.astype(F32)
            y = jnp.concatenate(within, 1) + carried + skip[:, lanes] * xs
            gate = half_silu((z[at, lanes] * 0.5).astype(F32))
            uv_out[at, lanes] = (y * gate).astype(BF16)
            uv_out[at, width + s * SLAB : width + (s + 1) * SLAB] = (gate * rise * lead_rows[:, lanes]).astype(BF16)
            xf = (xs * dot(f_blk[at, :], sel)).astype(BF16)
            state[:, lanes] = old * fade_rows[:, lanes] + dot(b_mat, xf, ((0,), (0,)))
        return 0

    lax.fori_loop(0, inner, block, 0)


def scan_part(part, token, x, bc, z, cum, cum_s, log_s, f_blk, e_blk, rates, skip, ones):
    length, full = x.shape
    width = full // B_PARTS
    groups = bc.shape[1] // (2 * N)
    group = part * groups // B_PARTS
    heads = cum.shape[1]
    cols = lambda i: (i, part)
    narrow = pl.BlockSpec((STEP_B, 2 * heads), lambda i: (i, 0))
    across = pl.BlockSpec((heads, STEP_B), lambda i: (0, i))
    return pl.pallas_call(
        functools.partial(scan_kernel, part * heads // B_PARTS),
        grid=(length // STEP_B,),
        in_specs=[
            pl.BlockSpec((STEP_B, width), cols),
            pl.BlockSpec((STEP_B, 2 * N), lambda i: (i, group)),
            pl.BlockSpec((STEP_B, width), cols),
            pl.BlockSpec((STEP_B, heads), lambda i: (i, 0)),
            across,
            across,
            narrow,
            narrow,
            pl.BlockSpec((rates.shape[0], width), lambda i: (0, part)),
            pl.BlockSpec((1, width), lambda i: (0, part)),
            pl.BlockSpec((2 * heads, width), lambda i: (0, part)),
            ANY,
        ],
        out_specs=pl.BlockSpec((STEP_B, 2 * width), lambda i: (i, 0)),
        out_shape=jax.ShapeDtypeStruct((length, 2 * width), BF16),
        scratch_shapes=[pltpu.VMEM((N, width), F32)],
        compiler_params=params(16),
        cost_estimate=pl.CostEstimate(
            flops=length * width * 4000, bytes_accessed=length * width * 10, transcendentals=length * width * 4
        ),
        name="scan_part",
    )(x, bc, z, cum, cum_s, log_s, f_blk, e_blk, rates, skip, ones, token)


def norm_kernel(info, bc, keep, recv, gain, _, *refs):
    uvs, out = refs[:-1], refs[-1]
    width = out.shape[1]
    groups = bc.shape[1] // (2 * N)
    per = width // groups
    half = width // 2
    part = width // B_PARTS
    is_odd = info[1] == 1
    for g in range(groups):
        c_mat = bc[:, 2 * N * g + N : 2 * N * (g + 1)]
        pieces = []
        squares = None
        for p in range(g * per // part, (g + 1) * per // part):
            start = p * part
            side = start // half
            lanes = slice(start - side * half, start - side * half + part)
            mine, other = keep[:, lanes], recv[:, lanes]
            inc = jnp.where(is_odd, other, mine) if side == 0 else jnp.where(is_odd, mine, other)
            gated = uvs[p][:, 0:part].astype(F32) + uvs[p][:, part:].astype(F32) * dot(c_mat, inc)
            square = jnp.sum(gated * gated, axis=-1, keepdims=True)
            squares = square if squares is None else squares + square
            pieces.append((start, gated))
        scale = lax.rsqrt(squares * (1.0 / per) + EPS)
        for start, gated in pieces:
            out[:, start : start + part] = (gated * scale * gain[:, start : start + part]).astype(BF16)


def norm_rows(info, count, token, bc, keep, recv, gain, uvs):
    rows = 128
    steps = count // rows
    width = gain.shape[1]
    take = lambda i, info: (info[0] * steps + i, 0)
    return pl.pallas_call(
        norm_kernel,
        grid_spec=pltpu.PrefetchScalarGridSpec(
            num_scalar_prefetch=1,
            grid=(steps,),
            in_specs=[
                pl.BlockSpec((rows, bc.shape[1]), take),
                whole(keep.shape),
                whole(recv.shape),
                whole(gain.shape),
                ANY,
            ]
            + [pl.BlockSpec((rows, uv.shape[1]), take) for uv in uvs],
            out_specs=pl.BlockSpec((rows, width), lambda i, info: (i, 0)),
        ),
        out_shape=jax.ShapeDtypeStruct((count, width), BF16),
        compiler_params=params(16),
        cost_estimate=pl.CostEstimate(
            flops=count * width * 256, bytes_accessed=count * width * 6, transcendentals=0
        ),
        name="norm_rows",
    )(info, bc, keep, recv, gain, token, *uvs)


def project_kernel(a0, a1, w0, w1, out):
    out[...] = (dot(a0[...], w0[...]) + dot(a1[...], w1[...])).astype(out.dtype)


def project(a0, a1, w0, w1, first, count, kind):
    rows, depth = a0.shape
    tile = min(512, count)
    base = first // tile
    return pl.pallas_call(
        project_kernel,
        grid=(count // tile,),
        in_specs=[
            whole(a0.shape),
            whole(a1.shape),
            pl.BlockSpec((depth, tile), lambda j: (0, base + j)),
            pl.BlockSpec((depth, tile), lambda j: (0, base + j)),
        ],
        out_specs=pl.BlockSpec((rows, tile), lambda j: (0, j)),
        out_shape=jax.ShapeDtypeStruct((rows, count), kind),
        compiler_params=params(24),
        cost_estimate=pl.CostEstimate(
            flops=4 * rows * depth * count, bytes_accessed=4 * depth * count, transcendentals=0
        ),
        name="project",
    )(a0, a1, w0, w1)


def add_kernel(part, arrived, *refs):
    refs[-1][...] = (part[...] + arrived[...].astype(F32)).astype(BF16)


def add_chunk(total, arrived, out, first):
    rows, count = arrived.shape
    tile = min(512, count)
    base = first // tile
    placed = pl.BlockSpec((rows, tile), lambda j: (0, base + j))
    return pl.pallas_call(
        add_kernel,
        grid=(count // tile,),
        in_specs=[placed, pl.BlockSpec((rows, tile), lambda j: (0, j))] + ([] if out is None else [ANY]),
        out_specs=placed,
        out_shape=jax.ShapeDtypeStruct(total.shape, BF16),
        input_output_aliases={} if out is None else {2: 0},
        compiler_params=params(8),
        name="add_chunk",
    )(*((total, arrived) if out is None else (total, arrived, out)))


def shift(block, distance):
    size = lax.axis_size("seq")
    return lax.ppermute(block, "seq", [(i, i + distance) for i in range(size - distance)])


def swap(block, axis, bit):
    return lax.ppermute(block, axis, [(i, i ^ bit) for i in range(lax.axis_size(axis))])


def local(
    x_input,
    z_input,
    bc_input,
    conv_weight_x,
    conv_weight_bc,
    step_size,
    log_decay,
    skip_gain,
    norm_gain,
    out_weight,
):
    length, width = x_input.shape
    heads = step_size.shape[1]
    ways = lax.axis_size("head")
    pairs = lax.axis_size("seq") // 2
    mine = lax.axis_index("head")
    half = width // 2
    odd = (lax.axis_index("seq") & 1).reshape(1).astype(jnp.int32)

    bc = bc_input.reshape(length, -1)
    halo = shift(jnp.concatenate([x_input[length - LEAD :], bc[length - LEAD :]], 1), 1)
    weight_mate = swap(out_weight, "head", 1)

    ones = jnp.asarray(np.tile(np.repeat(np.eye(heads), P_SIZE, axis=1), (2, 1)), BF16)
    cum, cum_s, log_s, f_dev, f_blk, e_blk, rates = decays(log_decay, step_size, ones)
    x_conv, bc_conv, keep, send = conv_states(
        odd, x_input, bc, halo, conv_weight_x, conv_weight_bc, f_dev, ones, rates
    )

    skip = jnp.repeat(skip_gain, P_SIZE)[None, :]
    uvs = []

    def scan_next(token):
        if len(uvs) < B_PARTS:
            uvs.append(
                scan_part(len(uvs), token, x_conv, bc_conv, z_input, cum, cum_s, log_s, f_blk, e_blk, rates, skip, ones)
            )
        return uvs[-1]

    message = ((N + EXTRA, half), BF16)
    full = ((N, half), F32)
    got = swap(send, "seq", 1)
    done = scan_next(send)
    msg, own, first, aux = combine(
        pair_kernel,
        (odd, got, keep, rates, done),
        [SCALAR, FULL, FULL, FULL, ANY],
        [message, full, full, ((16, half), F32)],
        "pair",
    )
    behind = None
    covered = 0
    while True:
        got = shift(msg, 2 * (covered + 1))
        done = scan_next(msg)
        covered = 2 * covered + 1
        if covered >= pairs - 1:
            break
        operands, specs = [got, own, aux], [FULL, FULL, FULL]
        if behind is None:
            kernel = lambda g, o, a, t, m, b: wave_kernel(g, o, a, None, t, m, b)
        else:
            kernel = wave_kernel
            operands.append(behind)
            specs.append(FULL)
        msg, behind = combine(kernel, operands + [done], specs + [ANY], [message, ((N + 8, half), F32)], "wave")
    operands, specs = [odd, got], [SCALAR, FULL]
    if behind is None:
        kernel = lambda o, g, f, a, t, b, h: last_kernel(o, g, None, f, a, t, b, h)
    else:
        kernel = last_kernel
        operands.append(behind)
        specs.append(FULL)
    out = ((N, half), BF16)
    back, held = combine(kernel, operands + [first, aux, done], specs + [FULL, FULL, ANY], [out, out], "last")
    other = swap(back, "seq", 1)
    while len(uvs) < B_PARTS:
        scan_next(back)

    count = length // ways
    gain = norm_gain[None, :]

    def rows_for(target, token):
        info = jnp.concatenate([target.reshape(1).astype(jnp.int32), odd])
        return norm_rows(info, count, token, bc_conv, held, other, gain, uvs)

    far_mate = rows_for(mine ^ 3, held)
    far = rows_for(mine ^ 2, far_mate)
    far_mate = swap(far_mate, "head", 1)
    columns = out_weight.shape[1]
    eighth = columns // 8
    cuts = [0, eighth, 3 * eighth, 5 * eighth, 7 * eighth, columns]
    arrivals = []
    for lo, hi in zip(cuts[:-1], cuts[1:]):
        sent = project(far, far_mate, out_weight, weight_mate, lo, hi - lo, BF16)
        arrivals.append(swap(sent, "head", 2))
    near_mate = rows_for(mine ^ 1, sent)
    near = rows_for(mine, near_mate)
    near_mate = swap(near_mate, "head", 1)
    total = project(near, near_mate, out_weight, weight_mate, 0, columns, F32)
    result = None
    for arrived, lo in zip(arrivals, cuts):
        result = add_chunk(total, arrived, result, lo)
    return result


def solution(mesh):
    in_specs = (
        P("seq", "head"),
        P("seq", "head"),
        P("seq", "head", None),
        P(None, "head"),
        P(None, "head", None),
        P("seq", "head"),
        P("seq", "head"),
        P("head"),
        P("head"),
        P("head", None),
    )
    out_specs = P(("seq", "head"), None)
    return jax.shard_map(local, mesh=mesh, in_specs=in_specs, out_specs=out_specs, check_vma=False)
```

time: 184 us -> 172 us (0.935)
  local copies, waits for them, and re-layouts: 19.3 us -> 52.4 us
  Pallas kernels: 103 us -> 82.6 us
  blocking collectives: 18.6 us -> 0 us
  waiting for transfers between devices: 22.6 us -> 11.3 us
  starting transfers between devices: 13.3 us -> 23.2 us
  other arithmetic: 5.07 us -> 0.23 us
    unnamed x57 -> x132, local copies, waits for them, and re-layouts: 16.8 us -> 50.6 us
    all_gather x1 -> x0, blocking collectives: 18.6 us -> none  [local(): logs = lax.all_gather(dev_total[0], 'seq')]
    pallas_call x4, Pallas kernels: 35.1 us -> 20.9 us  [scan_part(): pl.pallas_call(functools.partial(scan_kernel, part * heads // B_PARTS), g...]
    pallas_call x0 -> x8, Pallas kernels: none -> 8.21 us  [the longest x5 4.39 us: add_chunk(): pl.pallas_call(add_kernel, grid=(count // tile,), in_specs=[placed, pl.Bl...]
    ppermute x9 -> x10, waiting for transfers between devices: 17.3 us -> 10.4 us  [swap(): lax.ppermute(block, axis, [(i, i ^ bit) for i in range(lax.axis_size(axis...]
    pallas_call x1, Pallas kernels: 17.4 us -> 10.7 us  [conv_states(): pl.pallas_call(conv_kernel, grid_spec=pltpu.PrefetchScalarGridSpec(num_sc...]
    ppermute x3, starting transfers between devices: 7.57 us -> 14.2 us  [shift(): lax.ppermute(block, 'seq', [(i, i + distance) for i in range(size - dista...]
    pallas_call x4, Pallas kernels: 12.5 us -> 7.04 us  [norm_rows(): pl.pallas_call(norm_kernel, grid_spec=pltpu.PrefetchScalarGridSpec(num_sc...]
  transfers between devices with their start and end apart: 12 -> 13, of which waited for: 4 -> 3; matrix products, arithmetic and copies ran while one was open for 4% -> 2% of each run, Pallas kernels for 57% -> 45%
where the time goes in v2:
time: 172 us; the launch traced here: 170 us
  Pallas kernels  82.6 us (48%)
  local copies, waits for them, and re-layouts  52.4 us (30%)
  starting transfers between devices  23.2 us (13%)
  waiting for transfers between devices  11.3 us (7%)
    unnamed x132, local copies, waits for them, and re-layouts  50.6 us
    pallas_call x6, Pallas kernels, project(): pl.pallas_call(project_kernel, grid=(count // tile,), in_specs=[whole(a0....  34.2 us
    pallas_call x4, Pallas kernels, scan_part(): pl.pallas_call(functools.partial(scan_kernel, part * heads // B_PARTS), g...  20.9 us
    ppermute x3, starting transfers between devices, shift(): lax.ppermute(block, 'seq', [(i, i + distance) for i in range(size - dista...  14.2 us
    pallas_call x1, Pallas kernels, conv_states(): pl.pallas_call(conv_kernel, grid_spec=pltpu.PrefetchScalarGridSpec(num_sc...  10.7 us
    ppermute x10, waiting for transfers between devices, swap(): lax.ppermute(block, axis, [(i, i ^ bit) for i in range(lax.axis_size(axis...  10.4 us
    ppermute x10, starting transfers between devices, swap(): lax.ppermute(block, axis, [(i, i ^ bit) for i in range(lax.axis_size(axis...  8.99 us
    pallas_call x4, Pallas kernels, norm_rows(): pl.pallas_call(norm_kernel, grid_spec=pltpu.PrefetchScalarGridSpec(num_sc...  7.04 us
  transfers between devices with their start and end apart: 13, of which 3 were waited for; matrix products, arithmetic and copies ran while one was open for 2% of the time, Pallas kernels for 45%

profile of v2, /device:TPU:0, one launch (start us, length us, event | category | flops | bytes accessed | tf_op | source)
XLA Modules:
  0.0 170.2 jit_solution(14303154530095712289)
XLA Ops:
  2.1 4.6 %collective-permute-start = (bf16[16,2560]{1,0:T(8,128)(2,1)S(1)}, bf16[16,2560]{1,0:T(8,128)(2,1)S(1)}, u32[]{:S(2)}, u32[]{:S(2)}) collective-permute-start(bf16[16,2560]{1,0:T(8,128)(2,1)S(1)} %pad_maximum_fusion), channel_id=1, source_target_pairs={{0,4},{4,8},{8,12},{12,16},{16,20},{20,24},{24,28},{1,5},{5,9},{9,... | collective-permute-start | bytes 245768 | tf_op jit(solution)/shard_map/ppermute | solution.py:488
  12.6 2.2 %copy-done.23 = bf16[1024,2048]{1,0:T(8,128)(2,1)S(1)} copy-done((bf16[1024,2048]{1,0:T(8,128)(2,1)S(1)}, bf16[1024,2048]{1,0:T(8,128)(2,1)}, u32[]{:S(2)}) %copy-start.23) | copy-done | bytes 4194328
  16.4 10.7 %conv_states.1 = (bf16[1024,2048]{1,0:T(8,128)(2,1)S(1)}, bf16[1024,512]{1,0:T(8,128)(2,1)S(1)}, f32[128,1024]{1,0:T(8,128)S(1)}, bf16[144,1024]{1,0:T(8,128)(2,1)}) custom-call(s32[1]{0:T(128)} %bitcast.1.odd, bf16[1024,2048]{1,0:T(8,128)(2,1)S(1)} %copy-done.23, bf16[1024,2048]{1,0:T(8,128)(2,1)S(1)} %copy-done.23, bf16[1024,512]{1,0:T(8,128)(2,1)S(1)} %bitcast.12, ...), custom_call_target="tpu_custom_call" | custom-call | tf_op jit(solution)/shard_map/conv_states/pallas_call | solution.py:196
  27.1 2.0 %copy-done.16 = bf16[1024,2048]{1,0:T(8,128)(2,1)} copy-done((bf16[1024,2048]{1,0:T(8,128)(2,1)}, bf16[1024,2048]{1,0:T(8,128)(2,1)S(1)}, u32[]{:S(2)}) %copy-start.16) | copy-done | bytes 4194328
  31.6 2.2 %copy-done.13 = bf16[1024,2048]{1,0:T(8,128)(2,1)S(1)} copy-done((bf16[1024,2048]{1,0:T(8,128)(2,1)S(1)}, bf16[1024,2048]{1,0:T(8,128)(2,1)}, u32[]{:S(2)}) %copy-start.13) | copy-done | bytes 4194328
  33.8 2.2 %copy-done.17 = bf16[1024,2048]{1,0:T(8,128)(2,1)S(1)} copy-done((bf16[1024,2048]{1,0:T(8,128)(2,1)S(1)}, bf16[1024,2048]{1,0:T(8,128)(2,1)}, u32[]{:S(2)}) %copy-start.17) | copy-done | bytes 4194328
  40.8 5.2 %scan_part.4._.refs_0_ = bf16[1024,1024]{1,0:T(8,128)(2,1)S(1)} custom-call(bf16[1024,2048]{1,0:T(8,128)(2,1)S(1)} %copy-done.17, bf16[1024,512]{1,0:T(8,128)(2,1)S(1)} %get-tuple-element.26.bc, bf16[1024,2048]{1,0:T(8,128)(2,1)S(1)} %copy-done.13, f32[1024,32]{1,0:T(8,128)S(1)} %copy-done.26, f32[32,1024]{1,0:T(8,128)S(1)} %get-tuple-element.31.cum_s, ...), custom_call_target="tpu_custom_call" | custom-call | flops 2097152000 | bytes 5242880 | tf_op jit(solution)/shard_map/scan_part/pallas_call | solution.py:354
  48.3 3.5 %collective-permute-start.2 = (bf16[144,1024]{1,0:T(8,128)(2,1)S(1)}, bf16[144,1024]{1,0:T(8,128)(2,1)S(1)}, u32[]{:S(2)}, u32[]{:S(2)}) collective-permute-start(bf16[144,1024]{1,0:T(8,128)(2,1)S(1)} %get-tuple-element.35._), channel_id=1, source_target_pairs={{0,8},{4,12},{8,16},{12,20},{16,24},{20,28},{1,9},{5,13},{9,17},{1... | collective-permute-start | bytes 884744 | tf_op jit(solution)/shard_map/ppermute | solution.py:488
  51.8 5.3 %scan_part.5.t.refs_1_ = bf16[1024,1024]{1,0:T(8,128)(2,1)S(1)} custom-call(bf16[1024,2048]{1,0:T(8,128)(2,1)S(1)} %copy-done.17, bf16[1024,512]{1,0:T(8,128)(2,1)S(1)} %get-tuple-element.26.bc, bf16[1024,2048]{1,0:T(8,128)(2,1)S(1)} %copy-done.14, f32[1024,32]{1,0:T(8,128)S(1)} %copy-done.27, f32[32,1024]{1,0:T(8,128)S(1)} %get-tuple-element.31.cum_s, ...), custom_call_target="tpu_custom_call" | custom-call | flops 2097152000 | bytes 5242880 | tf_op jit(solution)/shard_map/scan_part/pallas_call | solution.py:354
  60.9 6.1 %collective-permute-start.3 = (bf16[144,1024]{1,0:T(8,128)(2,1)}, bf16[144,1024]{1,0:T(8,128)(2,1)}, u32[]{:S(2)}, u32[]{:S(2)}) collective-permute-start(bf16[144,1024]{1,0:T(8,128)(2,1)} %get-tuple-element.38._), channel_id=1, source_target_pairs={{0,16},{4,20},{8,24},{12,28},{1,17},{5,21},{9,25},{13,29},{2,18},{... | collective-permute-start | bytes 884744 | tf_op jit(solution)/shard_map/ppermute | solution.py:488
  67.1 2.2 %copy-done.15 = bf16[1024,2048]{1,0:T(8,128)(2,1)S(1)} copy-done((bf16[1024,2048]{1,0:T(8,128)(2,1)S(1)}, bf16[1024,2048]{1,0:T(8,128)(2,1)}, u32[]{:S(2)}) %copy-start.15) | copy-done | bytes 4194328
  69.3 2.2 %copy-done.18 = bf16[1024,2048]{1,0:T(8,128)(2,1)S(1)} copy-done((bf16[1024,2048]{1,0:T(8,128)(2,1)S(1)}, bf16[1024,2048]{1,0:T(8,128)(2,1)}, u32[]{:S(2)}) %copy-start.18) | copy-done | bytes 4194328
  76.2 5.2 %scan_part.6._.refs_2_ = bf16[1024,1024]{1,0:T(8,128)(2,1)S(1)} custom-call(bf16[1024,2048]{1,0:T(8,128)(2,1)S(1)} %copy-done.18, bf16[1024,512]{1,0:T(8,128)(2,1)S(1)} %get-tuple-element.26.bc, bf16[1024,2048]{1,0:T(8,128)(2,1)S(1)} %copy-done.15, f32[1024,32]{1,0:T(8,128)S(1)} %copy-done.28, f32[32,1024]{1,0:T(8,128)S(1)} %get-tuple-element.31.cum_s, ...), custom_call_target="tpu_custom_call" | custom-call | flops 2097152000 | bytes 5242880 | tf_op jit(solution)/shard_map/scan_part/pallas_call | solution.py:354
  83.8 5.2 %scan_part.7.refs_3_ = bf16[1024,1024]{1,0:T(8,128)(2,1)S(1)} custom-call(bf16[1024,2048]{1,0:T(8,128)(2,1)S(1)} %copy-done.18, bf16[1024,512]{1,0:T(8,128)(2,1)S(1)} %get-tuple-element.26.bc, bf16[1024,2048]{1,0:T(8,128)(2,1)S(1)} %copy-done.15, f32[1024,32]{1,0:T(8,128)S(1)} %copy-done.28, f32[32,1024]{1,0:T(8,128)S(1)} %get-tuple-element.31.cum_s, ...), custom_call_target="tpu_custom_call" | custom-call | flops 2097152000 | bytes 5242880 | tf_op jit(solution)/shard_map/scan_part/pallas_call | solution.py:354
  90.1 2.4 %norm_rows.4._ = bf16[256,2048]{1,0:T(8,128)(2,1)} custom-call(s32[2]{0:T(128)S(1)} %pad_add_fusion.3.info, bf16[1024,512]{1,0:T(8,128)(2,1)S(1)} %get-tuple-element.26.bc, bf16[128,1024]{1,0:T(8,128)(2,1)S(1)} %get-tuple-element.41.keep._, bf16[128,1024]{1,0:T(8,128)(2,1)S(1)} %collective-permute-done.4.recv, f32[1,2048]{1,0:T(1,128)S(1)} %bitcast.16, ...), custom_call_target="tpu_custom_call" | custom-call | flops 134217728 | bytes 3145728 | tf_op jit(solution)/shard_map/norm_rows/pallas_call | solution.py:414
  100.8 5.8 %copy-done = bf16[2048,4096]{1,0:T(8,128)(2,1)S(1)} copy-done((bf16[2048,4096]{1,0:T(8,128)(2,1)S(1)}, bf16[2048,4096]{1,0:T(8,128)(2,1)}, u32[]{:S(2)}) %copy-start) | copy-done | bytes 16777240
  106.6 3.3 %project.6._ = bf16[256,512]{1,0:T(8,128)(2,1)S(1)} custom-call(bf16[256,2048]{1,0:T(8,128)(2,1)S(1)} %norm_rows.5.a0, bf16[256,2048]{1,0:T(8,128)(2,1)} %collective-permute-done.5.a1, bf16[2048,4096]{1,0:T(8,128)(2,1)S(1)} %copy-done, bf16[2048,4096]{1,0:T(8,128)(2,1)} %collective-permute-done.6.w1), custom_call_target="tpu_custom_call" | custom-call | flops 1073741824 | bytes 4194304 | tf_op jit(solution)/shard_map/project/pallas_call | solution.py:446
  109.9 2.3 %copy-done.7 = bf16[1024,1024]{1,0:T(8,128)(2,1)S(1)} copy-done((bf16[1024,1024]{1,0:T(8,128)(2,1)S(1)}, bf16[1024,1024]{1,0:T(8,128)(2,1)}, u32[]{:S(2)}) %copy-start.7) | copy-done | bytes 2097176
  119.5 4.6 %project.8 = bf16[256,1024]{1,0:T(8,128)(2,1)S(1)} custom-call(bf16[256,2048]{1,0:T(8,128)(2,1)S(1)} %norm_rows.5.a0, bf16[256,2048]{1,0:T(8,128)(2,1)} %collective-permute-done.5.a1, bf16[2048,4096]{1,0:T(8,128)(2,1)S(1)} %copy-done.1, bf16[2048,4096]{1,0:T(8,128)(2,1)} %collective-permute-done.6.w1), custom_call_target="tpu_custom_call" | custom-call | flops 2147483648 | bytes 8388608 | tf_op jit(solution)/shard_map/project/pallas_call | solution.py:446
  124.7 4.6 %project.9 = bf16[256,1024]{1,0:T(8,128)(2,1)S(1)} custom-call(bf16[256,2048]{1,0:T(8,128)(2,1)S(1)} %norm_rows.5.a0, bf16[256,2048]{1,0:T(8,128)(2,1)} %collective-permute-done.5.a1, bf16[2048,4096]{1,0:T(8,128)(2,1)S(1)} %copy-done.1, bf16[2048,4096]{1,0:T(8,128)(2,1)} %collective-permute-done.6.w1), custom_call_target="tpu_custom_call" | custom-call | flops 2147483648 | bytes 8388608 | tf_op jit(solution)/shard_map/project/pallas_call | solution.py:446
  130.9 4.7 %project.10 = bf16[256,1024]{1,0:T(8,128)(2,1)S(1)} custom-call(bf16[256,2048]{1,0:T(8,128)(2,1)S(1)} %norm_rows.5.a0, bf16[256,2048]{1,0:T(8,128)(2,1)} %collective-permute-done.5.a1, bf16[2048,4096]{1,0:T(8,128)(2,1)S(1)} %copy-done.1, bf16[2048,4096]{1,0:T(8,128)(2,1)} %collective-permute-done.6.w1), custom_call_target="tpu_custom_call" | custom-call | flops 2147483648 | bytes 8388608 | tf_op jit(solution)/shard_map/project/pallas_call | solution.py:446
  138.1 3.2 %project.11 = bf16[256,512]{1,0:T(8,128)(2,1)S(1)} custom-call(bf16[256,2048]{1,0:T(8,128)(2,1)S(1)} %norm_rows.5.a0, bf16[256,2048]{1,0:T(8,128)(2,1)} %collective-permute-done.5.a1, bf16[2048,4096]{1,0:T(8,128)(2,1)S(1)} %copy-done.1, bf16[2048,4096]{1,0:T(8,128)(2,1)} %collective-permute-done.6.w1), custom_call_target="tpu_custom_call" | custom-call | flops 1073741824 | bytes 4194304 | tf_op jit(solution)/shard_map/project/pallas_call | solution.py:446
  142.6 13.9 %project.7.part = f32[256,4096]{1,0:T(8,128)S(1)} custom-call(bf16[256,2048]{1,0:T(8,128)(2,1)S(1)} %norm_rows.7.a0, bf16[256,2048]{1,0:T(8,128)(2,1)S(1)} %collective-permute-done.7.a1, bf16[2048,4096]{1,0:T(8,128)(2,1)S(1)} %copy-done.1, bf16[2048,4096]{1,0:T(8,128)(2,1)} %collective-permute-done.6.w1), custom_call_target="tpu_custom_call" | custom-call | flops 8589934592 | bytes 33554432 | tf_op jit(solution)/shard_map/project/pallas_call | solution.py:446
  156.4 9.4 %collective-permute-done.12.arrived = bf16[256,512]{1,0:T(8,128)(2,1)S(1)} collective-permute-done((bf16[256,512]{1,0:T(8,128)(2,1)S(1)}, bf16[256,512]{1,0:T(8,128)(2,1)S(1)}, u32[]{:S(2)}, u32[]{:S(2)}) %collective-permute-start.12) | collective-permute-done | bytes 262176 | tf_op jit(solution)/shard_map/ppermute | solution.py:492
  (166 shorter events, 56.9 us)
Async XLA Ops:
  0.0 12.6 %copy-start.63 = (f32[4,2,256]{2,1,0:T(2,128)S(1)}, f32[4,2,256]{2,1,0:T(2,128)}, u32[]{:S(2)}) copy-start(f32[4,2,256]{2,1,0:T(2,128)} %wbc.1) | copy-start | bytes 24580
  0.0 100.8 %collective-permute-start.6 = (bf16[2048,4096]{1,0:T(8,128)(2,1)}, bf16[2048,4096]{1,0:T(8,128)(2,1)}, u32[]{:S(2)}, u32[]{:S(2)}) collective-permute-start(bf16[2048,4096]{1,0:T(8,128)(2,1)} %w0.11), channel_id=1, source_target_pairs={{0,1},{1,0},{2,3},{3,2},{4,5},{5,4},{6,7},{7,6},{8,9},{9,8},{10,11... | collective-permute-start | bytes 50331656 | tf_op jit(solution)/shard_map/ppermute | solution.py:492
  2.1 9.8 %collective-permute-start = (bf16[16,2560]{1,0:T(8,128)(2,1)S(1)}, bf16[16,2560]{1,0:T(8,128)(2,1)S(1)}, u32[]{:S(2)}, u32[]{:S(2)}) collective-permute-start(bf16[16,2560]{1,0:T(8,128)(2,1)S(1)} %pad_maximum_fusion), channel_id=1, source_target_pairs={{0,4},{4,8},{8,12},{12,16},{16,20},{20,24},{24,28},{1,5},{5,9},{9,... | collective-permute-start | bytes 245768 | tf_op jit(solution)/shard_map/ppermute | solution.py:488
  11.9 15.2 %copy-start.29 = (f32[24,2048]{1,0:T(8,128)}, f32[24,2048]{1,0:T(8,128)S(1)}, u32[]{:S(2)}) copy-start(f32[24,2048]{1,0:T(8,128)S(1)} %get-tuple-element.25.rates) | copy-start | bytes 589828
  11.9 15.2 %copy-start.39 = (bf16[1024,64]{1,0:T(8,128)(2,1)}, bf16[1024,64]{1,0:T(8,128)(2,1)S(1)}, u32[]{:S(2)}) copy-start(bf16[1024,64]{1,0:T(8,128)(2,1)S(1)} %get-tuple-element.34.e_blk) | copy-start | bytes 393220
  16.4 15.0 %copy-start.64 = (f32[32]{0:T(128)S(1)}, f32[32]{0:T(128)}, u32[]{:S(2)}) copy-start(f32[32]{0:T(128)} %param.18) | copy-start | bytes 388
  29.9 16.1 %collective-permute-start.1 = (bf16[144,1024]{1,0:T(8,128)(2,1)}, bf16[144,1024]{1,0:T(8,128)(2,1)}, u32[]{:S(2)}, u32[]{:S(2)}) collective-permute-start(bf16[144,1024]{1,0:T(8,128)(2,1)} %get-tuple-element.27._), channel_id=1, source_target_pairs={{0,4},{4,0},{8,12},{12,8},{16,20},{20,16},{24,28},{28,24},{1,5},{5... | collective-permute-start | bytes 884744 | tf_op jit(solution)/shard_map/ppermute | solution.py:492
  40.8 11.1 %copy-start.14 = (bf16[1024,2048]{1,0:T(8,128)(2,1)S(1)}, bf16[1024,2048]{1,0:T(8,128)(2,1)}, u32[]{:S(2)}) copy-start(bf16[1024,2048]{1,0:T(8,128)(2,1)} %z.7) | copy-start | bytes 12582916
  46.0 46.6 %copy-start.2 = (bf16[1024,1024]{1,0:T(8,128)(2,1)}, bf16[1024,1024]{1,0:T(8,128)(2,1)S(1)}, u32[]{:S(2)}) copy-start(bf16[1024,1024]{1,0:T(8,128)(2,1)S(1)} %scan_part.4._.refs_0_) | copy-start | bytes 6291460
  48.3 9.7 %copy-start.55 = (f32[16,1024]{1,0:T(8,128)}, f32[16,1024]{1,0:T(8,128)S(1)}, u32[]{:S(2)}) copy-start(f32[16,1024]{1,0:T(8,128)S(1)} %get-tuple-element.37.a.aux) | copy-start | bytes 196612
  48.3 9.7 %collective-permute-start.2 = (bf16[144,1024]{1,0:T(8,128)(2,1)S(1)}, bf16[144,1024]{1,0:T(8,128)(2,1)S(1)}, u32[]{:S(2)}, u32[]{:S(2)}) collective-permute-start(bf16[144,1024]{1,0:T(8,128)(2,1)S(1)} %get-tuple-element.35._), channel_id=1, source_target_pairs={{0,8},{4,12},{8,16},{12,20},{16,24},{20,28},{1,9},{5,13},{9,17},{1... | collective-permute-start | bytes 884744 | tf_op jit(solution)/shard_map/ppermute | solution.py:488
  60.9 20.6 %collective-permute-start.3 = (bf16[144,1024]{1,0:T(8,128)(2,1)}, bf16[144,1024]{1,0:T(8,128)(2,1)}, u32[]{:S(2)}, u32[]{:S(2)}) collective-permute-start(bf16[144,1024]{1,0:T(8,128)(2,1)} %get-tuple-element.38._), channel_id=1, source_target_pairs={{0,16},{4,20},{8,24},{12,28},{1,17},{5,21},{9,25},{13,29},{2,18},{... | collective-permute-start | bytes 884744 | tf_op jit(solution)/shard_map/ppermute | solution.py:488
  81.5 8.6 %copy-start.9 = (bf16[1024,1024]{1,0:T(8,128)(2,1)}, bf16[1024,1024]{1,0:T(8,128)(2,1)S(1)}, u32[]{:S(2)}) copy-start(bf16[1024,1024]{1,0:T(8,128)(2,1)S(1)} %scan_part.6._.refs_2_) | copy-start | bytes 6291460
  83.1 6.9 %collective-permute-start.4 = (bf16[128,1024]{1,0:T(8,128)(2,1)S(1)}, bf16[128,1024]{1,0:T(8,128)(2,1)S(1)}, u32[]{:S(2)}, u32[]{:S(2)}) collective-permute-start(bf16[128,1024]{1,0:T(8,128)(2,1)S(1)} %get-tuple-element.42._), channel_id=1, source_target_pairs={{0,4},{4,0},{8,12},{12,8},{16,20},{20,16},{24,28},{28,24},{1,5},{5... | collective-permute-start | bytes 786440 | tf_op jit(solution)/shard_map/ppermute | solution.py:492
  92.5 8.3 %collective-permute-start.5 = (bf16[256,2048]{1,0:T(8,128)(2,1)}, bf16[256,2048]{1,0:T(8,128)(2,1)}, u32[]{:S(2)}, u32[]{:S(2)}) collective-permute-start(bf16[256,2048]{1,0:T(8,128)(2,1)} %norm_rows.4._), channel_id=1, source_target_pairs={{0,1},{1,0},{2,3},{3,2},{4,5},{5,4},{6,7},{7,6},{8,9},{9,8},{10,11... | collective-permute-start | bytes 3145736 | tf_op jit(solution)/shard_map/ppermute | solution.py:492
  99.2 10.7 %copy-start.34 = (bf16[128,1024]{1,0:T(8,128)(2,1)S(1)}, bf16[128,1024]{1,0:T(8,128)(2,1)}, u32[]{:S(2)}) copy-start(bf16[128,1024]{1,0:T(8,128)(2,1)} %copy-done.32) | copy-start | bytes 786436
  99.2 10.7 %copy-start.45 = (bf16[128,1024]{1,0:T(8,128)(2,1)S(1)}, bf16[128,1024]{1,0:T(8,128)(2,1)}, u32[]{:S(2)}) copy-start(bf16[128,1024]{1,0:T(8,128)(2,1)} %copy-done.43) | copy-start | bytes 786436
  106.6 13.0 %copy-start.1 = (bf16[2048,4096]{1,0:T(8,128)(2,1)S(1)}, bf16[2048,4096]{1,0:T(8,128)(2,1)}, u32[]{:S(2)}) copy-start(bf16[2048,4096]{1,0:T(8,128)(2,1)} %w0.11) | copy-start | bytes 50331652
  117.4 23.9 %collective-permute-start.7 = (bf16[256,2048]{1,0:T(8,128)(2,1)S(1)}, bf16[256,2048]{1,0:T(8,128)(2,1)S(1)}, u32[]{:S(2)}, u32[]{:S(2)}) collective-permute-start(bf16[256,2048]{1,0:T(8,128)(2,1)S(1)} %norm_rows.6._), channel_id=1, source_target_pairs={{0,1},{1,0},{2,3},{3,2},{4,5},{5,4},{6,7},{7,6},{8,9},{9,8},{10,11... | collective-permute-start | bytes 3145736 | tf_op jit(solution)/shard_map/ppermute | solution.py:492
  118.0 51.5 %collective-permute-start.8 = (bf16[256,512]{1,0:T(8,128)(2,1)S(1)}, bf16[256,512]{1,0:T(8,128)(2,1)S(1)}, u32[]{:S(2)}, u32[]{:S(2)}) collective-permute-start(bf16[256,512]{1,0:T(8,128)(2,1)S(1)} %project.6._), channel_id=1, source_target_pairs={{0,2},{1,3},{2,0},{3,1},{4,6},{5,7},{6,4},{7,5},{8,10},{9,11},{10,... | collective-permute-start | bytes 786440 | tf_op jit(solution)/shard_map/ppermute | solution.py:492
  124.1 44.4 %collective-permute-start.9 = (bf16[256,1024]{1,0:T(8,128)(2,1)S(1)}, bf16[256,1024]{1,0:T(8,128)(2,1)S(1)}, u32[]{:S(2)}, u32[]{:S(2)}) collective-permute-start(bf16[256,1024]{1,0:T(8,128)(2,1)S(1)} %project.8), channel_id=1, source_target_pairs={{0,2},{1,3},{2,0},{3,1},{4,6},{5,7},{6,4},{7,5},{8,10},{9,11},{10,... | collective-permute-start | bytes 1572872 | tf_op jit(solution)/shard_map/ppermute | solution.py:492
  129.3 38.2 %collective-permute-start.10 = (bf16[256,1024]{1,0:T(8,128)(2,1)S(1)}, bf16[256,1024]{1,0:T(8,128)(2,1)S(1)}, u32[]{:S(2)}, u32[]{:S(2)}) collective-permute-start(bf16[256,1024]{1,0:T(8,128)(2,1)S(1)} %project.9), channel_id=1, source_target_pairs={{0,2},{1,3},{2,0},{3,1},{4,6},{5,7},{6,4},{7,5},{8,10},{9,11},{10,... | collective-permute-start | bytes 1572872 | tf_op jit(solution)/shard_map/ppermute | solution.py:492
  135.6 31.0 %collective-permute-start.11 = (bf16[256,1024]{1,0:T(8,128)(2,1)S(1)}, bf16[256,1024]{1,0:T(8,128)(2,1)S(1)}, u32[]{:S(2)}, u32[]{:S(2)}) collective-permute-start(bf16[256,1024]{1,0:T(8,128)(2,1)S(1)} %project.10), channel_id=1, source_target_pairs={{0,2},{1,3},{2,0},{3,1},{4,6},{5,7},{6,4},{7,5},{8,10},{9,11},{10,... | collective-permute-start | bytes 1572872 | tf_op jit(solution)/shard_map/ppermute | solution.py:492
  141.3 24.6 %collective-permute-start.12 = (bf16[256,512]{1,0:T(8,128)(2,1)S(1)}, bf16[256,512]{1,0:T(8,128)(2,1)S(1)}, u32[]{:S(2)}, u32[]{:S(2)}) collective-permute-start(bf16[256,512]{1,0:T(8,128)(2,1)S(1)} %project.11), channel_id=1, source_target_pairs={{0,2},{1,3},{2,0},{3,1},{4,6},{5,7},{6,4},{7,5},{8,10},{9,11},{10,... | collective-permute-start | bytes 786440 | tf_op jit(solution)/shard_map/ppermute | solution.py:492
  (54 other events, 155.4 us)

commit v3 on v2

--- a/solution.py
+++ b/solution.py
@@ -22,14 +22,12 @@
 SLAB = 256
 LEAD = 16
 B_PARTS = 4
-MIB = 1024 * 1024
 HIGHEST = lax.Precision.HIGHEST
 F32 = jnp.float32
 BF16 = jnp.bfloat16
 
 
-def params(mib):
-    return pltpu.CompilerParams(vmem_limit_bytes=mib * MIB)
+PARAMS = pltpu.CompilerParams(vmem_limit_bytes=64 * 1024 * 1024)
 
 
 def dot(a, b, dims=((1,), (0,)), precision=None):
@@ -103,7 +101,7 @@
             pair,
             jax.ShapeDtypeStruct((2 * blocks + 8, width), F32),
         ),
-        compiler_params=params(16),
+        compiler_params=PARAMS,
         name="decays",
     )(log_decay.T, step.T, ones)
 
@@ -227,7 +225,7 @@
             jax.ShapeDtypeStruct((N, half), F32),
             jax.ShapeDtypeStruct((N + EXTRA, half), BF16),
         ),
-        compiler_params=params(20),
+        compiler_params=PARAMS,
         name="conv_states",
     )(odd, x, x, bc, bc, halo, wx, wbc, f_dev, ones, rates)
 
@@ -283,7 +281,7 @@
         in_specs=specs,
         out_specs=[FULL] * len(outs),
         out_shape=[jax.ShapeDtypeStruct(s, t) for s, t in outs],
-        compiler_params=params(12),
+        compiler_params=PARAMS,
         name=name,
     )(*operands)
 
@@ -371,7 +369,7 @@
         out_specs=pl.BlockSpec((STEP_B, 2 * width), lambda i: (i, 0)),
         out_shape=jax.ShapeDtypeStruct((length, 2 * width), BF16),
         scratch_shapes=[pltpu.VMEM((N, width), F32)],
-        compiler_params=params(16),
+        compiler_params=PARAMS,
         cost_estimate=pl.CostEstimate(
             flops=length * width * 4000, bytes_accessed=length * width * 10, transcendentals=length * width * 4
         ),
@@ -427,7 +425,7 @@
             out_specs=pl.BlockSpec((rows, width), lambda i, info: (i, 0)),
         ),
         out_shape=jax.ShapeDtypeStruct((count, width), BF16),
-        compiler_params=params(16),
+        compiler_params=PARAMS,
         cost_estimate=pl.CostEstimate(
             flops=count * width * 256, bytes_accessed=count * width * 6, transcendentals=0
         ),
@@ -435,11 +433,11 @@
     )(info, bc, keep, recv, gain, token, *uvs)
 
 
-def project_kernel(a0, a1, w0, w1, out):
+def project_kernel(a0, a1, w0, w1, _, out):
     out[...] = (dot(a0[...], w0[...]) + dot(a1[...], w1[...])).astype(out.dtype)
 
 
-def project(a0, a1, w0, w1, first, count, kind):
+def project(token, a0, a1, w0, w1, first, count, kind):
     rows, depth = a0.shape
     tile = min(512, count)
     base = first // tile
@@ -451,15 +449,16 @@
             whole(a1.shape),
             pl.BlockSpec((depth, tile), lambda j: (0, base + j)),
             pl.BlockSpec((depth, tile), lambda j: (0, base + j)),
+            ANY,
         ],
         out_specs=pl.BlockSpec((rows, tile), lambda j: (0, j)),
         out_shape=jax.ShapeDtypeStruct((rows, count), kind),
-        compiler_params=params(24),
+        compiler_params=PARAMS,
         cost_estimate=pl.CostEstimate(
             flops=4 * rows * depth * count, bytes_accessed=4 * depth * count, transcendentals=0
         ),
         name="project",
-    )(a0, a1, w0, w1)
+    )(a0, a1, w0, w1, token)
 
 
 def add_kernel(part, arrived, *refs):
@@ -478,7 +477,7 @@
         out_specs=placed,
         out_shape=jax.ShapeDtypeStruct(total.shape, BF16),
         input_output_aliases={} if out is None else {2: 0},
-        compiler_params=params(8),
+        compiler_params=PARAMS,
         name="add_chunk",
     )(*((total, arrived) if out is None else (total, arrived, out)))
 
@@ -586,13 +585,14 @@
     eighth = columns // 8
     cuts = [0, eighth, 3 * eighth, 5 * eighth, 7 * eighth, columns]
     arrivals = []
+    sent = far
     for lo, hi in zip(cuts[:-1], cuts[1:]):
-        sent = project(far, far_mate, out_weight, weight_mate, lo, hi - lo, BF16)
+        sent = project(sent, far, far_mate, out_weight, weight_mate, lo, hi - lo, BF16)
         arrivals.append(swap(sent, "head", 2))
     near_mate = rows_for(mine ^ 1, sent)
     near = rows_for(mine, near_mate)
     near_mate = swap(near_mate, "head", 1)
-    total = project(near, near_mate, out_weight, weight_mate, 0, columns, F32)
+    total = project(near, near, near_mate, out_weight, weight_mate, 0, columns, F32)
     result = None
     for arrived, lo in zip(arrivals, cuts):
         result = add_chunk(total, arrived, result, lo)

time: 172 us -> 178 us (1.035)
  the two profiles are of different devices: /device:TPU:0 before, /device:TPU:24 now
where the time goes in v3:
time: 178 us
  Pallas kernels  127 us (71%)
  waiting for transfers between devices  28.9 us (16%)
  starting transfers between devices  14.2 us (8%)
  local copies, waits for them, and re-layouts  5.41 us (3%)
  other arithmetic  2.52 us (1%)
    pallas_call x6, Pallas kernels, project(): pl.pallas_call(project_kernel, grid=(count // tile,), in_specs=[whole(a0....  46.1 us
    pallas_call x4, Pallas kernels, scan_part(): pl.pallas_call(functools.partial(scan_kernel, part * heads // B_PARTS), g...  30.5 us
    ppermute x10, waiting for transfers between devices, swap(): lax.ppermute(block, axis, [(i, i ^ bit) for i in range(lax.axis_size(axis...  18.8 us
    pallas_call x4, Pallas kernels, norm_rows(): pl.pallas_call(norm_kernel, grid_spec=pltpu.PrefetchScalarGridSpec(num_sc...  16.5 us
    pallas_call x1, Pallas kernels, conv_states(): pl.pallas_call(conv_kernel, grid_spec=pltpu.PrefetchScalarGridSpec(num_sc...  13.1 us
    ppermute x3, waiting for transfers between devices, shift(): lax.ppermute(block, 'seq', [(i, i + distance) for i in range(size - dista...  10.2 us
    pallas_call x5, Pallas kernels, add_chunk(): pl.pallas_call(add_kernel, grid=(count // tile,), in_specs=[placed, pl.Bl...  10 us
    ppermute x10, starting transfers between devices, swap(): lax.ppermute(block, axis, [(i, i ^ bit) for i in range(lax.axis_size(axis...  8.05 us
  transfers between devices with their start and end apart: 13, of which 4 were waited for; matrix products, arithmetic and copies ran while one was open for 4% of the time, Pallas kernels for 52%

profile of v3, /device:TPU:24, one launch (start us, length us, event | category | flops | bytes accessed | tf_op | source)
XLA Modules:
  0.0 177.7 jit_solution(12592305757450669974)
XLA Ops:
  2.2 3.4 %collective-permute-start = (bf16[16,2560]{1,0:T(8,128)(2,1)}, bf16[16,2560]{1,0:T(8,128)(2,1)}, u32[]{:S(2)}, u32[]{:S(2)}) collective-permute-start(bf16[16,2560]{1,0:T(8,128)(2,1)} %pad_maximum_fusion), channel_id=1, source_target_pairs={{0,4},{4,8},{8,12},{12,16},{16,20},{20,24},{24,28},{1,5},{5,9},{9,... | collective-permute-start | bytes 245768 | tf_op jit(solution)/shard_map/ppermute | solution.py:487
  5.7 2.4 %copy.16 = bf16[128,8,2,256]{3,1,2,0:T(8,128)(2,1)} copy(bf16[128,8,2,256]{3,2,1,0:T(2,128)(2,1)} %bitcast.14) | data formatting | bytes 2097152
  8.1 3.6 %decays.1 = (f32[1024,32]{1,0:T(8,128)}, f32[32,1024]{1,0:T(8,128)}, f32[32,1024]{1,0:T(8,128)}, bf16[1024,64]{1,0:T(8,128)(2,1)}, bf16[1024,64]{1,0:T(8,128)(2,...) custom-call(f32[32,1024]{1,0:T(8,128)} %bitcast.15, f32[32,1024]{1,0:T(8,128)} %bitcast.16, ...), custom_call_target="tpu_custom_call" | custom-call | tf_op jit(solution)/shard_map/decays/pallas_call | solution.py:93
  11.7 13.1 %conv_states.1 = (bf16[1024,2048]{1,0:T(8,128)(2,1)}, bf16[1024,512]{1,0:T(8,128)(2,1)}, f32[128,1024]{1,0:T(8,128)}, bf16[144,1024]{1,0:T(8,128)(2,1)}) custom-call(s32[1]{0:T(128)} %bitcast.1.odd, bf16[1024,2048]{1,0:T(8,128)(2,1)} %x_lead.1, bf16[1024,2048]{1,0:T(8,128)(2,1)} %x_lead.1, bf16[1024,512]{1,0:T(8,128)(2,1)} %bitcast.12, ...), custom_call_target="tpu_custom_call" | custom-call | tf_op jit(solution)/shard_map/conv_states/pallas_call | solution.py:194
  26.3 7.6 %scan_part.4._.refs_0_ = bf16[1024,1024]{1,0:T(8,128)(2,1)} custom-call(bf16[1024,2048]{1,0:T(8,128)(2,1)} %get-tuple-element.29.x, bf16[1024,512]{1,0:T(8,128)(2,1)} %get-tuple-element.26.bc, bf16[1024,2048]{1,0:T(8,128)(2,1)} %z.7, f32[1024,32]{1,0:T(8,128)} %get-tuple-element.30.cum, f32[32,1024]{1,0:T(8,128)} %get-tuple-element.31.cum_s, ...), custom_call_target="tpu_custom_call" | custom-call | flops 2097152000 | bytes 5242880 | tf_op jit(solution)/shard_map/scan_part/pallas_call | solution.py:352
  34.4 2.4 %pair.1 = (bf16[144,1024]{1,0:T(8,128)(2,1)}, f32[128,1024]{1,0:T(8,128)}, f32[128,1024]{1,0:T(8,128)}, f32[16,1024]{1,0:T(8,128)}) custom-call(s32[1]{0:T(128)} %bitcast.1.odd, bf16[144,1024]{1,0:T(8,128)(2,1)} %collective-permute-done.1.got, f32[128,1024]{1,0:T(8,128)} %get-tuple-element.28.keep, f32[24,2048]{1,0:T(8,128)} %get-tuple-element.25.rates, ...), custom_call_target="tpu_custom_call" | custom-call | tf_op jit(solution)/shard_map/pair/pallas_call | solution.py:279
  38.1 7.6 %scan_part.5.t.refs_1_ = bf16[1024,1024]{1,0:T(8,128)(2,1)} custom-call(bf16[1024,2048]{1,0:T(8,128)(2,1)} %get-tuple-element.29.x, bf16[1024,512]{1,0:T(8,128)(2,1)} %get-tuple-element.26.bc, bf16[1024,2048]{1,0:T(8,128)(2,1)} %z.7, f32[1024,32]{1,0:T(8,128)} %get-tuple-element.30.cum, f32[32,1024]{1,0:T(8,128)} %get-tuple-element.31.cum_s, ...), custom_call_target="tpu_custom_call" | custom-call | flops 2097152000 | bytes 5242880 | tf_op jit(solution)/shard_map/scan_part/pallas_call | solution.py:352
  51.3 7.6 %scan_part.6._.refs_2_ = bf16[1024,1024]{1,0:T(8,128)(2,1)} custom-call(bf16[1024,2048]{1,0:T(8,128)(2,1)} %get-tuple-element.29.x, bf16[1024,512]{1,0:T(8,128)(2,1)} %get-tuple-element.26.bc, bf16[1024,2048]{1,0:T(8,128)(2,1)} %z.7, f32[1024,32]{1,0:T(8,128)} %get-tuple-element.30.cum, f32[32,1024]{1,0:T(8,128)} %get-tuple-element.31.cum_s, ...), custom_call_target="tpu_custom_call" | custom-call | flops 2097152000 | bytes 5242880 | tf_op jit(solution)/shard_map/scan_part/pallas_call | solution.py:352
  58.9 8.2 %collective-permute-done.3.got = bf16[144,1024]{1,0:T(8,128)(2,1)} collective-permute-done((bf16[144,1024]{1,0:T(8,128)(2,1)}, bf16[144,1024]{1,0:T(8,128)(2,1)}, u32[]{:S(2)}, u32[]{:S(2)}) %collective-permute-start.3) | collective-permute-done | bytes 294944 | tf_op jit(solution)/shard_map/ppermute | solution.py:487
  67.1 2.2 %last.1 = (bf16[128,1024]{1,0:T(8,128)(2,1)}, bf16[128,1024]{1,0:T(8,128)(2,1)}) custom-call(s32[1]{0:T(128)} %bitcast.1.odd, bf16[144,1024]{1,0:T(8,128)(2,1)} %collective-permute-done.3.got, f32[136,1024]{1,0:T(8,128)} %get-tuple-element.39.behind_in, f32[128,1024]{1,0:T(8,128)} %get-tuple-element.40.first, f32[16,1024]{1,0:T(8,128)} %get-tuple-element.37.a.aux, ...), custom_call_target="tpu_custom_call" | custom-call | tf_op jit(solution)/shard_map/last/pallas_call | solution.py:279
  71.8 7.6 %scan_part.7.refs_3_ = bf16[1024,1024]{1,0:T(8,128)(2,1)} custom-call(bf16[1024,2048]{1,0:T(8,128)(2,1)} %get-tuple-element.29.x, bf16[1024,512]{1,0:T(8,128)(2,1)} %get-tuple-element.26.bc, bf16[1024,2048]{1,0:T(8,128)(2,1)} %z.7, f32[1024,32]{1,0:T(8,128)} %get-tuple-element.30.cum, f32[32,1024]{1,0:T(8,128)} %get-tuple-element.31.cum_s, ...), custom_call_target="tpu_custom_call" | custom-call | flops 2097152000 | bytes 5242880 | tf_op jit(solution)/shard_map/scan_part/pallas_call | solution.py:352
  79.5 4.2 %norm_rows.4._ = bf16[256,2048]{1,0:T(8,128)(2,1)} custom-call(s32[2]{0:T(128)} %pad_add_fusion.3.info, bf16[1024,512]{1,0:T(8,128)(2,1)} %get-tuple-element.26.bc, bf16[128,1024]{1,0:T(8,128)(2,1)} %get-tuple-element.41.keep._, bf16[128,1024]{1,0:T(8,128)(2,1)} %collective-permute-done.4.recv, f32[1,2048]{1,0:T(1,128)} %bitcast.17, ...), custom_call_target="tpu_custom_call" | custom-call | flops 134217728 | bytes 3145728 | tf_op jit(solution)/shard_map/norm_rows/pallas_call | solution.py:412
  84.3 4.1 %norm_rows.5.a0._ = bf16[256,2048]{1,0:T(8,128)(2,1)} custom-call(s32[2]{0:T(128)} %get-tuple-element.44.info, bf16[1024,512]{1,0:T(8,128)(2,1)} %get-tuple-element.26.bc, bf16[128,1024]{1,0:T(8,128)(2,1)} %get-tuple-element.41.keep._, bf16[128,1024]{1,0:T(8,128)(2,1)} %collective-permute-done.4.recv, f32[1,2048]{1,0:T(1,128)} %bitcast.18, ...), custom_call_target="tpu_custom_call" | custom-call | flops 134217728 | bytes 3145728 | tf_op jit(solution)/shard_map/norm_rows/pallas_call | solution.py:412
  88.4 4.8 %project.6._ = bf16[256,512]{1,0:T(8,128)(2,1)} custom-call(bf16[256,2048]{1,0:T(8,128)(2,1)} %norm_rows.5.a0._, bf16[256,2048]{1,0:T(8,128)(2,1)} %collective-permute-done.5.a1, bf16[2048,4096]{1,0:T(8,128)(2,1)} %w0.11, bf16[2048,4096]{1,0:T(8,128)(2,1)} %collective-permute-done.6.w1, bf16[256,2048]{1,0:T(8,128)(2,1)} %norm_rows.5.a0._), custom_call_target="tpu_custom_call" | custom-call | flops 1073741824 | bytes 4194304 | tf_op jit(solution)/shard_map/project/pallas_call | solution.py:444
  93.2 6.1 %project.7._ = bf16[256,1024]{1,0:T(8,128)(2,1)} custom-call(bf16[256,2048]{1,0:T(8,128)(2,1)} %norm_rows.5.a0._, bf16[256,2048]{1,0:T(8,128)(2,1)} %collective-permute-done.5.a1, bf16[2048,4096]{1,0:T(8,128)(2,1)} %w0.11, bf16[2048,4096]{1,0:T(8,128)(2,1)} %collective-permute-done.6.w1, bf16[256,512]{1,0:T(8,128)(2,1)} %project.6._), custom_call_target="tpu_custom_call" | custom-call | flops 2147483648 | bytes 8388608 | tf_op jit(solution)/shard_map/project/pallas_call | solution.py:444
  99.3 6.1 %project.8._ = bf16[256,1024]{1,0:T(8,128)(2,1)} custom-call(bf16[256,2048]{1,0:T(8,128)(2,1)} %norm_rows.5.a0._, bf16[256,2048]{1,0:T(8,128)(2,1)} %collective-permute-done.5.a1, bf16[2048,4096]{1,0:T(8,128)(2,1)} %w0.11, bf16[2048,4096]{1,0:T(8,128)(2,1)} %collective-permute-done.6.w1, bf16[256,1024]{1,0:T(8,128)(2,1)} %project.7._), custom_call_target="tpu_custom_call" | custom-call | flops 2147483648 | bytes 8388608 | tf_op jit(solution)/shard_map/project/pallas_call | solution.py:444
  105.4 6.1 %project.9._ = bf16[256,1024]{1,0:T(8,128)(2,1)} custom-call(bf16[256,2048]{1,0:T(8,128)(2,1)} %norm_rows.5.a0._, bf16[256,2048]{1,0:T(8,128)(2,1)} %collective-permute-done.5.a1, bf16[2048,4096]{1,0:T(8,128)(2,1)} %w0.11, bf16[2048,4096]{1,0:T(8,128)(2,1)} %collective-permute-done.6.w1, bf16[256,1024]{1,0:T(8,128)(2,1)} %project.8._), custom_call_target="tpu_custom_call" | custom-call | flops 2147483648 | bytes 8388608 | tf_op jit(solution)/shard_map/project/pallas_call | solution.py:444
  111.6 4.9 %project.10._ = bf16[256,512]{1,0:T(8,128)(2,1)} custom-call(bf16[256,2048]{1,0:T(8,128)(2,1)} %norm_rows.5.a0._, bf16[256,2048]{1,0:T(8,128)(2,1)} %collective-permute-done.5.a1, bf16[2048,4096]{1,0:T(8,128)(2,1)} %w0.11, bf16[2048,4096]{1,0:T(8,128)(2,1)} %collective-permute-done.6.w1, bf16[256,1024]{1,0:T(8,128)(2,1)} %project.9._), custom_call_target="tpu_custom_call" | custom-call | flops 1073741824 | bytes 4194304 | tf_op jit(solution)/shard_map/project/pallas_call | solution.py:444
  116.4 4.1 %norm_rows.6._ = bf16[256,2048]{1,0:T(8,128)(2,1)} custom-call(s32[2]{0:T(128)} %get-tuple-element.43.info, bf16[1024,512]{1,0:T(8,128)(2,1)} %get-tuple-element.26.bc, bf16[128,1024]{1,0:T(8,128)(2,1)} %get-tuple-element.41.keep._, bf16[128,1024]{1,0:T(8,128)(2,1)} %collective-permute-done.4.recv, f32[1,2048]{1,0:T(1,128)} %bitcast.19, ...), custom_call_target="tpu_custom_call" | custom-call | flops 134217728 | bytes 3145728 | tf_op jit(solution)/shard_map/norm_rows/pallas_call | solution.py:412
  125.7 4.1 %norm_rows.7.a0._ = bf16[256,2048]{1,0:T(8,128)(2,1)} custom-call(s32[2]{0:T(128)} %pad_add_fusion.info, bf16[1024,512]{1,0:T(8,128)(2,1)} %get-tuple-element.26.bc, bf16[128,1024]{1,0:T(8,128)(2,1)} %get-tuple-element.41.keep._, bf16[128,1024]{1,0:T(8,128)(2,1)} %collective-permute-done.4.recv, f32[1,2048]{1,0:T(1,128)} %bitcast.20, ...), custom_call_target="tpu_custom_call" | custom-call | flops 134217728 | bytes 3145728 | tf_op jit(solution)/shard_map/norm_rows/pallas_call | solution.py:412
  131.4 18.0 %project.11.part = f32[256,4096]{1,0:T(8,128)} custom-call(bf16[256,2048]{1,0:T(8,128)(2,1)} %norm_rows.7.a0._, bf16[256,2048]{1,0:T(8,128)(2,1)} %collective-permute-done.7.a1, bf16[2048,4096]{1,0:T(8,128)(2,1)} %w0.11, bf16[2048,4096]{1,0:T(8,128)(2,1)} %collective-permute-done.6.w1, bf16[256,2048]{1,0:T(8,128)(2,1)} %norm_rows.7.a0._), custom_call_target="tpu_custom_call" | custom-call | flops 8589934592 | bytes 33554432 | tf_op jit(solution)/shard_map/project/pallas_call | solution.py:444
  151.3 18.3 %collective-permute-done.11.arrived = bf16[256,1024]{1,0:T(8,128)(2,1)} collective-permute-done((bf16[256,1024]{1,0:T(8,128)(2,1)}, bf16[256,1024]{1,0:T(8,128)(2,1)}, u32[]{:S(2)}, u32[]{:S(2)}) %collective-permute-start.11) | collective-permute-done | bytes 524320 | tf_op jit(solution)/shard_map/ppermute | solution.py:491
  171.7 2.1 %add_chunk.7.refs_0_ = bf16[256,4096]{1,0:T(8,128)(2,1)} custom-call(f32[256,4096]{1,0:T(8,128)} %project.11.part, bf16[256,1024]{1,0:T(8,128)(2,1)} %collective-permute-done.10.arrived, bf16[256,4096]{1,0:T(8,128)(2,1)} %add_chunk.6.refs_0_), custom_call_target="tpu_custom_call", output_to_operand_aliasing={{}: (2, {})} | custom-call | tf_op jit(solution)/shard_map/add_chunk/pallas_call | solution.py:473
  173.8 2.1 %add_chunk.8.refs_0_ = bf16[256,4096]{1,0:T(8,128)(2,1)} custom-call(f32[256,4096]{1,0:T(8,128)} %project.11.part, bf16[256,1024]{1,0:T(8,128)(2,1)} %collective-permute-done.9.arrived, bf16[256,4096]{1,0:T(8,128)(2,1)} %add_chunk.7.refs_0_), custom_call_target="tpu_custom_call", output_to_operand_aliasing={{}: (2, {})} | custom-call | tf_op jit(solution)/shard_map/add_chunk/pallas_call | solution.py:473
  (36 shorter events, 26.7 us)
Async XLA Ops:
  0.0 88.4 %collective-permute-start.6 = (bf16[2048,4096]{1,0:T(8,128)(2,1)}, bf16[2048,4096]{1,0:T(8,128)(2,1)}, u32[]{:S(2)}, u32[]{:S(2)}) collective-permute-start(bf16[2048,4096]{1,0:T(8,128)(2,1)} %w0.11), channel_id=1, source_target_pairs={{0,1},{1,0},{2,3},{3,2},{4,5},{5,4},{6,7},{7,6},{8,9},{9,8},{10,11... | collective-permute-start | bytes 50331656 | tf_op jit(solution)/shard_map/ppermute | solution.py:491
  2.2 9.5 %collective-permute-start = (bf16[16,2560]{1,0:T(8,128)(2,1)}, bf16[16,2560]{1,0:T(8,128)(2,1)}, u32[]{:S(2)}, u32[]{:S(2)}) collective-permute-start(bf16[16,2560]{1,0:T(8,128)(2,1)} %pad_maximum_fusion), channel_id=1, source_target_pairs={{0,4},{4,8},{8,12},{12,16},{16,20},{20,24},{24,28},{1,5},{5,9},{9,... | collective-permute-start | bytes 245768 | tf_op jit(solution)/shard_map/ppermute | solution.py:487
  24.8 9.5 %collective-permute-start.1 = (bf16[144,1024]{1,0:T(8,128)(2,1)}, bf16[144,1024]{1,0:T(8,128)(2,1)}, u32[]{:S(2)}, u32[]{:S(2)}) collective-permute-start(bf16[144,1024]{1,0:T(8,128)(2,1)} %get-tuple-element.27._), channel_id=1, source_target_pairs={{0,4},{4,0},{8,12},{12,8},{16,20},{20,16},{24,28},{28,24},{1,5},{5... | collective-permute-start | bytes 884744 | tf_op jit(solution)/shard_map/ppermute | solution.py:491
  36.8 10.9 %collective-permute-start.2 = (bf16[144,1024]{1,0:T(8,128)(2,1)}, bf16[144,1024]{1,0:T(8,128)(2,1)}, u32[]{:S(2)}, u32[]{:S(2)}) collective-permute-start(bf16[144,1024]{1,0:T(8,128)(2,1)} %get-tuple-element.35._), channel_id=1, source_target_pairs={{0,8},{4,12},{8,16},{12,20},{16,24},{20,28},{1,9},{5,13},{9,17},{1... | collective-permute-start | bytes 884744 | tf_op jit(solution)/shard_map/ppermute | solution.py:487
  49.8 17.3 %collective-permute-start.3 = (bf16[144,1024]{1,0:T(8,128)(2,1)}, bf16[144,1024]{1,0:T(8,128)(2,1)}, u32[]{:S(2)}, u32[]{:S(2)}) collective-permute-start(bf16[144,1024]{1,0:T(8,128)(2,1)} %get-tuple-element.38._), channel_id=1, source_target_pairs={{0,16},{4,20},{8,24},{12,28},{1,17},{5,21},{9,25},{13,29},{2,18},{... | collective-permute-start | bytes 884744 | tf_op jit(solution)/shard_map/ppermute | solution.py:487
  69.3 10.1 %collective-permute-start.4 = (bf16[128,1024]{1,0:T(8,128)(2,1)}, bf16[128,1024]{1,0:T(8,128)(2,1)}, u32[]{:S(2)}, u32[]{:S(2)}) collective-permute-start(bf16[128,1024]{1,0:T(8,128)(2,1)} %get-tuple-element.42._), channel_id=1, source_target_pairs={{0,4},{4,0},{8,12},{12,8},{16,20},{20,16},{24,28},{28,24},{1,5},{5... | collective-permute-start | bytes 786440 | tf_op jit(solution)/shard_map/ppermute | solution.py:491
  83.6 4.7 %collective-permute-start.5 = (bf16[256,2048]{1,0:T(8,128)(2,1)}, bf16[256,2048]{1,0:T(8,128)(2,1)}, u32[]{:S(2)}, u32[]{:S(2)}) collective-permute-start(bf16[256,2048]{1,0:T(8,128)(2,1)} %norm_rows.4._), channel_id=1, source_target_pairs={{0,1},{1,0},{2,3},{3,2},{4,5},{5,4},{6,7},{7,6},{8,9},{9,8},{10,11... | collective-permute-start | bytes 3145736 | tf_op jit(solution)/shard_map/ppermute | solution.py:491
  120.6 9.3 %collective-permute-start.7 = (bf16[256,2048]{1,0:T(8,128)(2,1)}, bf16[256,2048]{1,0:T(8,128)(2,1)}, u32[]{:S(2)}, u32[]{:S(2)}) collective-permute-start(bf16[256,2048]{1,0:T(8,128)(2,1)} %norm_rows.6._), channel_id=1, source_target_pairs={{0,1},{1,0},{2,3},{3,2},{4,5},{5,4},{6,7},{7,6},{8,9},{9,8},{10,11... | collective-permute-start | bytes 3145736 | tf_op jit(solution)/shard_map/ppermute | solution.py:491
  121.7 27.7 %collective-permute-start.12 = (bf16[256,512]{1,0:T(8,128)(2,1)}, bf16[256,512]{1,0:T(8,128)(2,1)}, u32[]{:S(2)}, u32[]{:S(2)}) collective-permute-start(bf16[256,512]{1,0:T(8,128)(2,1)} %project.6._), channel_id=1, source_target_pairs={{0,2},{1,3},{2,0},{3,1},{4,6},{5,7},{6,4},{7,5},{8,10},{9,11},{10,... | collective-permute-start | bytes 786440 | tf_op jit(solution)/shard_map/ppermute | solution.py:491
  123.2 52.7 %collective-permute-start.8 = (bf16[256,512]{1,0:T(8,128)(2,1)}, bf16[256,512]{1,0:T(8,128)(2,1)}, u32[]{:S(2)}, u32[]{:S(2)}) collective-permute-start(bf16[256,512]{1,0:T(8,128)(2,1)} %project.10._), channel_id=1, source_target_pairs={{0,2},{1,3},{2,0},{3,1},{4,6},{5,7},{6,4},{7,5},{8,10},{9,11},{10,... | collective-permute-start | bytes 786440 | tf_op jit(solution)/shard_map/ppermute | solution.py:491
  123.7 50.0 %collective-permute-start.9 = (bf16[256,1024]{1,0:T(8,128)(2,1)}, bf16[256,1024]{1,0:T(8,128)(2,1)}, u32[]{:S(2)}, u32[]{:S(2)}) collective-permute-start(bf16[256,1024]{1,0:T(8,128)(2,1)} %project.9._), channel_id=1, source_target_pairs={{0,2},{1,3},{2,0},{3,1},{4,6},{5,7},{6,4},{7,5},{8,10},{9,11},{10,... | collective-permute-start | bytes 1572872 | tf_op jit(solution)/shard_map/ppermute | solution.py:491
  125.2 46.5 %collective-permute-start.10 = (bf16[256,1024]{1,0:T(8,128)(2,1)}, bf16[256,1024]{1,0:T(8,128)(2,1)}, u32[]{:S(2)}, u32[]{:S(2)}) collective-permute-start(bf16[256,1024]{1,0:T(8,128)(2,1)} %project.8._), channel_id=1, source_target_pairs={{0,2},{1,3},{2,0},{3,1},{4,6},{5,7},{6,4},{7,5},{8,10},{9,11},{10,... | collective-permute-start | bytes 1572872 | tf_op jit(solution)/shard_map/ppermute | solution.py:491
  129.9 39.7 %collective-permute-start.11 = (bf16[256,1024]{1,0:T(8,128)(2,1)}, bf16[256,1024]{1,0:T(8,128)(2,1)}, u32[]{:S(2)}, u32[]{:S(2)}) collective-permute-start(bf16[256,1024]{1,0:T(8,128)(2,1)} %project.7._), channel_id=1, source_target_pairs={{0,2},{1,3},{2,0},{3,1},{4,6},{5,7},{6,4},{7,5},{8,10},{9,11},{10,... | collective-permute-start | bytes 1572872 | tf_op jit(solution)/shard_map/ppermute | solution.py:491

commit v4 on v2

v4 whole, which is shorter than its diff:
```python
import functools

import jax
import jax.numpy as jnp
import numpy as np
from jax import lax
from jax.experimental import pallas as pl
from jax.experimental.pallas import tpu as pltpu
from jax.sharding import PartitionSpec as P

P_SIZE = 64
N = 128
KCONV = 4
EPS = 1e-05
LOG2E = 1.4426950408889634

TOK_A = 256
ROWS_A = 32
TOK_B = 128
STEP_B = 256
EXTRA = 16
SLAB = 256
ROWS_C = 128
TILE = 256
SLOTS = 4
LEAD = 16
B_PARTS = 4
HIGHEST = lax.Precision.HIGHEST
F32 = jnp.float32
BF16 = jnp.bfloat16


def params(mib):
    return pltpu.CompilerParams(vmem_limit_bytes=mib * 1024 * 1024)


CHEAP = pl.CostEstimate(flops=1, bytes_accessed=1, transcendentals=0)
SCALAR = pl.BlockSpec(memory_space=pltpu.SMEM)
FULL = pl.BlockSpec(memory_space=pltpu.VMEM)
FAR = pl.BlockSpec(memory_space=pltpu.HBM)
ANY = pl.BlockSpec(memory_space=pl.ANY)


def dot(a, b, dims=((1,), (0,)), precision=None):
    return lax.dot_general(a, b, (dims, ((), ())), precision=precision, preferred_element_type=F32)


def half_silu(half):
    return half + half * jnp.tanh(half)


def whole(shape):
    return pl.BlockSpec(shape, lambda *_: (0,) * len(shape))


def decay_kernel(ld_t, step_t, skip, ones, cum, cum_s, log_s, f_dev, f_blk, e_blk, rates):
    heads, length = ld_t.shape
    blocks = length // TOK_B
    row = lax.broadcasted_iota(jnp.int32, (TOK_B, TOK_B), 0)
    col = lax.broadcasted_iota(jnp.int32, (TOK_B, TOK_B), 1)
    lower = (row >= col).astype(F32)
    upper = (row <= col).astype(F32)
    eye = (row == col).astype(BF16)

    def put(ref, rows, value):
        high = value.astype(BF16)
        low = (value - high.astype(F32)).astype(BF16)
        ref[rows, :] = dot(eye, jnp.concatenate([high, low], 0), ((1,), (1,))).astype(BF16)

    cums, totals, row_totals = [], [], []
    for b in range(blocks):
        rows = slice(b * TOK_B, (b + 1) * TOK_B)
        logs = ld_t[:, rows] * LOG2E
        c = dot(lower, logs, ((1,), (1,)), HIGHEST)
        cum[rows, :] = c
        row_totals.append(c[TOK_B - 1 : TOK_B, :])
        c = dot(logs, upper, precision=HIGHEST)
        cums.append(c)
        totals.append(c[:, TOK_B - 1 : TOK_B])
    before, row_before = [jnp.zeros_like(totals[0])], [jnp.zeros_like(row_totals[0])]
    for b in range(blocks):
        before.append(before[-1] + totals[b])
        row_before.append(row_before[-1] + row_totals[b])
    total = before[-1]
    logs = jnp.concatenate(row_totals + row_before[:-1] + row_before[-1:] * 8, 0)
    values = jnp.concatenate([jnp.exp2(logs), jnp.broadcast_to(skip[...], (8, heads))], 0)
    rates[...] = dot(values, ones[0:heads, :].astype(F32), precision=HIGHEST)
    for b in range(blocks):
        rows = slice(b * TOK_B, (b + 1) * TOK_B)
        s = step_t[:, rows]
        log_step = jnp.log2(s)
        log_s[:, rows] = log_step
        cum_s[:, rows] = cums[b] - log_step
        put(f_dev, rows, jnp.exp2(total - (cums[b] + before[b])) * s)
        put(f_blk, rows, jnp.exp2(totals[b] - cums[b]) * s)
        put(e_blk, rows, jnp.exp2(cums[b]))


def decays(log_decay, step, skip, ones):
    length, heads = log_decay.shape
    blocks = length // TOK_B
    width = ones.shape[1]
    wide = jax.ShapeDtypeStruct((heads, length), F32)
    pair = jax.ShapeDtypeStruct((length, 2 * heads), BF16)
    return pl.pallas_call(
        decay_kernel,
        out_shape=(
            jax.ShapeDtypeStruct((length, heads), F32),
            wide,
            wide,
            pair,
            pair,
            pair,
            jax.ShapeDtypeStruct((2 * blocks + 16, width), F32),
        ),
        compiler_params=params(16),
        name="decays",
    )(log_decay.T, step.T, skip[None, :], ones)


def put_message(ref, state, decay):
    high = decay.astype(BF16)
    low = (decay - high.astype(F32)).astype(BF16)
    rest = jnp.zeros((EXTRA - 2, state.shape[1]), BF16)
    ref[0:N, :] = state.astype(BF16)
    ref[N:, :] = jnp.concatenate([high, low, rest], 0)


def take_message(ref):
    extra = ref[N:, :].astype(F32)
    return ref[0:N, :].astype(F32), extra[0:1] + extra[1:2]


def conv_kernel(info, x_far, bc, halo, wx, wbc, f_dev, ones, rates, x_out, bc_out, keep, send, x, sem, xf, state):
    i = pl.program_id(0)
    rows, width = x_out.shape
    bc_width = bc.shape[1]
    groups = bc_width // (2 * N)
    per = width // groups
    half = width // 2

    def fetch(step):
        piece = pl.ds(pl.multiple_of(step * rows, rows), rows)
        return pltpu.make_async_copy(x_far.at[piece], x.at[piece], sem.at[step])

    @pl.when(i == 0)
    def _():
        for step in range(x.shape[0] // rows):
            fetch(step).start()
        state[...] = jnp.zeros_like(state)

    fetch(i).wait()
    base = pl.multiple_of(i * rows, rows)
    before = pl.ds(pl.multiple_of(jnp.maximum(base - LEAD, 0), LEAD), LEAD)

    def at(r):
        return pl.ds(pl.multiple_of(base + r, ROWS_A), ROWS_A)

    def conv(src, lead, weights, emit):
        w0, w1, w2, w3 = [w * 0.5 for w in weights]
        back = LEAD - 8
        r1 = pltpu.roll(lead, 1, 0)
        last_x, last_p = lead[back:], (w1 * lead + w0 * r1)[back:]
        for r in range(0, rows, ROWS_A):
            cur = src(r).astype(F32)
            r1 = pltpu.roll(jnp.concatenate([last_x, cur], 0), 1, 0)[8:]
            p = w1 * cur + w0 * r1
            p2 = pltpu.roll(jnp.concatenate([last_p, p], 0), 2, 0)[8:]
            emit(r, half_silu((w3 * cur + w2 * r1) + p2))
            last_x, last_p = cur[ROWS_A - 8 :], p[ROWS_A - 8 :]

    start = i == 0
    for c in range(groups):
        for lanes in range(c * 2 * N, (c + 1) * 2 * N, N):
            ds = slice(lanes, lanes + N)

            def emit_bc(r, value):
                bc_out[r : r + ROWS_A, ds] = value.astype(BF16)

            lead = jnp.where(start, halo[:, width + lanes : width + lanes + N], bc[before, ds]).astype(F32)
            inner = slice(lanes - c * 2 * N, lanes - c * 2 * N + N)
            conv(lambda r: bc[at(r), ds], lead, [wbc[k, c : c + 1, inner] for k in range(KCONV)], emit_bc)

    def slab(c, _):
        ds = pl.ds(pl.multiple_of(c * SLAB, SLAB), SLAB)
        scale = dot(f_dev[pl.ds(base, rows), :], ones[:, ds])

        def emit(r, value):
            value = value.astype(BF16)
            x_out[r : r + ROWS_A, ds] = value
            xf[r : r + ROWS_A, ds] = (value.astype(F32) * scale[r : r + ROWS_A]).astype(BF16)

        lead = jnp.where(start, halo[:, ds], x[before, ds]).astype(F32)
        conv(lambda r: x[at(r), ds], lead, [wx[k : k + 1, ds] for k in range(KCONV)], emit)
        return 0

    lax.fori_loop(0, width // SLAB, slab, 0)
    for g in range(groups):
        b_mat = bc_out[:, 2 * N * g : 2 * N * g + N]
        lanes = slice(g * per, (g + 1) * per)
        state[:, lanes] += dot(b_mat, xf[:, lanes], ((0,), (0,)))

    @pl.when(i == pl.num_programs(0) - 1)
    def _():
        is_odd = info[0] == 1
        low, high = state[:, 0:half], state[:, half:]
        keep[...] = jnp.where(is_odd, high, low)
        row = rates.shape[0] - 16
        decay = jnp.where(is_odd, rates[row : row + 1, 0:half], rates[row : row + 1, half:])
        put_message(send, jnp.where(is_odd, low, high), decay)


def conv_states(info, x, bc, halo, wx, wbc, f_dev, ones, rates):
    length, width = x.shape
    bc_width = bc.shape[1]
    half = width // 2
    return pl.pallas_call(
        conv_kernel,
        grid=(length // TOK_A,),
        in_specs=[SCALAR, FAR] + [FULL] * 7,
        out_specs=[
            pl.BlockSpec((TOK_A, width), lambda i: (i, 0)),
            pl.BlockSpec((TOK_A, bc_width), lambda i: (i, 0)),
            whole((N, half)),
            whole((N + EXTRA, half)),
        ],
        scratch_shapes=[
            pltpu.VMEM((length, width), BF16),
            pltpu.SemaphoreType.DMA((length // TOK_A,)),
            pltpu.VMEM((TOK_A, width), BF16),
            pltpu.VMEM((N, width), F32),
        ],
        out_shape=(
            pltpu.HBM((length, width), BF16),
            jax.ShapeDtypeStruct((length, bc_width), BF16),
            jax.ShapeDtypeStruct((N, half), F32),
            jax.ShapeDtypeStruct((N + EXTRA, half), BF16),
        ),
        compiler_params=params(20),
        cost_estimate=CHEAP,
        name="conv_states",
    )(info, x, bc, halo, wx, wbc, f_dev, ones, rates)


def pair_kernel(info, got, keep, rates, _, msg, own, first, aux):
    half = keep.shape[1]
    is_odd = info[0] == 1
    arrived, their = take_message(got)
    row = rates.shape[0] - 16
    mine = jnp.where(is_odd, rates[row : row + 1, half:], rates[row : row + 1, 0:half])
    early = jnp.where(is_odd, arrived, keep[...])
    late = jnp.where(is_odd, keep[...], arrived)
    even_decay = jnp.where(is_odd, their, mine)
    odd_decay = jnp.where(is_odd, mine, their)
    state = odd_decay * early + late
    own[...] = state
    first[...] = early
    aux[0:8, :] = jnp.broadcast_to(even_decay, (8, half))
    aux[8:16, :] = jnp.broadcast_to(even_decay * odd_decay, (8, half))
    put_message(msg, state, even_decay * odd_decay)


def wave_kernel(got, own, aux, behind_in, _, msg, behind):
    before, decay = take_message(got)
    if behind_in is not None:
        before_decay = behind_in[N : N + 1, :]
        before = behind_in[0:N, :] + before_decay * before
        decay = before_decay * decay
    pair_decay = aux[8:9, :]
    behind[0:N, :] = before
    behind[N:, :] = jnp.broadcast_to(decay, (8, before.shape[1]))
    put_message(msg, own[...] + pair_decay * before, pair_decay * decay)


def last_kernel(info, got, behind_in, first, aux, _, back, held):
    is_odd = info[0] == 1
    before, _unused = take_message(got)
    if behind_in is not None:
        before = behind_in[0:N, :] + behind_in[N : N + 1, :] * before
    entering_odd = aux[0:1, :] * before + first[...]
    back[...] = jnp.where(is_odd, before, entering_odd).astype(BF16)
    held[...] = jnp.where(is_odd, entering_odd, before).astype(BF16)


def combine(kernel, operands, specs, outs, name):
    return pl.pallas_call(
        kernel,
        in_specs=specs,
        out_specs=[FULL] * len(outs),
        out_shape=[jax.ShapeDtypeStruct(s, t) for s, t in outs],
        compiler_params=params(16),
        name=name,
    )(*operands)


def scan_kernel(part, x_far, z_far, bc_all, cum, cum_s, log_s, f_blk, e_blk, rates, ones, _, uv_out, x, z, sem, state):
    length, width = x.shape
    per_slab = SLAB // P_SIZE
    head0 = part * width // P_SIZE
    first_lane = part * width
    inner = STEP_B // TOK_B
    blocks = length // TOK_B
    group = first_lane * (bc_all.shape[1] // (2 * N)) // (width * B_PARTS)
    b_lanes = slice(2 * N * group, 2 * N * group + N)
    c_lanes = slice(2 * N * group + N, 2 * N * (group + 1))

    def fetch(step):
        piece = pl.ds(pl.multiple_of(step * STEP_B, STEP_B), STEP_B)
        lanes = pl.ds(first_lane, width)
        return (
            pltpu.make_async_copy(x_far.at[piece, lanes], x.at[piece], sem.at[0, step]),
            pltpu.make_async_copy(z_far.at[piece, lanes], z.at[piece], sem.at[1, step]),
        )

    for step in range(length // STEP_B):
        for copy in fetch(step):
            copy.start()
    state[...] = jnp.zeros_like(state)

    row = lax.broadcasted_iota(jnp.int32, (TOK_B, TOK_B), 0)
    col = lax.broadcasted_iota(jnp.int32, (TOK_B, TOK_B), 1)
    keep = row >= col
    first = lax.broadcasted_iota(jnp.int32, (TOK_B, 2 * P_SIZE), 1) < P_SIZE
    zero = jnp.zeros((TOK_B, 2 * P_SIZE), BF16)

    def block(b, _):
        @pl.when(lax.rem(b, inner) == 0)
        def _():
            for copy in fetch(lax.div(b, inner)):
                copy.wait()

        at = pl.ds(pl.multiple_of(b * TOK_B, TOK_B), TOK_B)
        b_mat = bc_all[at, b_lanes]
        c_mat = bc_all[at, c_lanes]
        scores = jnp.where(keep, dot(c_mat, b_mat, ((1,), (1,))), 0.0)
        wide = pl.ds(first_lane, width)
        fade_rows = rates[pl.ds(b, 1), wide]
        lead_rows = rates[pl.ds(blocks + b, 1), wide]
        skip = rates[2 * blocks + 8 : 2 * blocks + 9, wide]
        for s in range(width // SLAB):
            lanes = slice(s * SLAB, (s + 1) * SLAB)
            xb = x[at, lanes]
            sel = ones[:, first_lane + s * SLAB : first_lane + (s + 1) * SLAB]
            old = state[:, lanes]
            rise = dot(e_blk[at, :], sel)
            carried = dot(c_mat, old.astype(BF16)) * rise
            within = []
            for q in range(per_slab // 2):
                tables = []
                for h in (2 * q, 2 * q + 1):
                    head = head0 + s * per_slab + h
                    column = cum[at, head : head + 1]
                    gap = jnp.minimum(column - cum_s[head : head + 1, at], log_s[head : head + 1, at])
                    tables.append((scores * jnp.exp2(gap)).astype(BF16))
                xp = xb[:, q * 2 * P_SIZE : (q + 1) * 2 * P_SIZE]
                stacked = jnp.concatenate([jnp.where(first, xp, zero), jnp.where(first, zero, xp)], 0)
                within.append(dot(jnp.concatenate(tables, 1), stacked))
            xs = xb.astype(F32)
            y = jnp.concatenate(within, 1) + carried + skip[:, lanes] * xs
            gate = half_silu((z[at, lanes] * 0.5).astype(F32))
            uv_out[at, lanes] = (y * gate).astype(BF16)
            uv_out[at, width + s * SLAB : width + (s + 1) * SLAB] = (gate * rise * lead_rows[:, lanes]).astype(BF16)
            xf = (xs * dot(f_blk[at, :], sel)).astype(BF16)
            state[:, lanes] = old * fade_rows[:, lanes] + dot(b_mat, xf, ((0,), (0,)))
        return 0

    lax.fori_loop(0, blocks, block, 0)


def scan_part(part, token, x, bc, z, cum, cum_s, log_s, f_blk, e_blk, rates, ones):
    length, full = x.shape
    width = full // B_PARTS
    return pl.pallas_call(
        functools.partial(scan_kernel, part),
        in_specs=[FAR, FAR] + [FULL] * 8 + [ANY],
        out_specs=FULL,
        out_shape=jax.ShapeDtypeStruct((length, 2 * width), BF16),
        scratch_shapes=[
            pltpu.VMEM((length, width), BF16),
            pltpu.VMEM((length, width), BF16),
            pltpu.SemaphoreType.DMA((2, length // STEP_B)),
            pltpu.VMEM((N, width), F32),
        ],
        compiler_params=params(16),
        cost_estimate=CHEAP,
        name="scan_part",
    )(x, z, bc, cum, cum_s, log_s, f_blk, e_blk, rates, ones, token)


def norm_kernel(slot, info, bc, keep, recv, gain, _, *refs):
    uvs, out = refs[:-1], refs[-1]
    count, width = out.shape
    groups = bc.shape[1] // (2 * N)
    per = width // groups
    half = width // 2
    part = width // B_PARTS
    is_odd = info[0] == 1
    base = info[slot] * count

    def rows(j, _):
        to = pl.ds(pl.multiple_of(j * ROWS_C, ROWS_C), ROWS_C)
        at = pl.ds(pl.multiple_of(base + j * ROWS_C, ROWS_C), ROWS_C)
        for g in range(groups):
            c_mat = bc[at, 2 * N * g + N : 2 * N * (g + 1)]
            pieces = []
            squares = None
            for p in range(g * per // part, (g + 1) * per // part):
                start = p * part
                side = start // half
                lanes = slice(start - side * half, start - side * half + part)
                mine, other = keep[:, lanes], recv[:, lanes]
                inc = jnp.where(is_odd, other, mine) if side == 0 else jnp.where(is_odd, mine, other)
                gated = uvs[p][at, 0:part].astype(F32) + uvs[p][at, part:].astype(F32) * dot(c_mat, inc)
                square = jnp.sum(gated * gated, axis=-1, keepdims=True)
                squares = square if squares is None else squares + square
                pieces.append((start, gated))
            scale = lax.rsqrt(squares * (1.0 / per) + EPS)
            for start, gated in pieces:
                out[to, start : start + part] = (gated * scale * gain[:, start : start + part]).astype(BF16)
        return 0

    lax.fori_loop(0, count // ROWS_C, rows, 0)


def norm_rows(slot, info, count, token, bc, keep, recv, gain, uvs):
    return pl.pallas_call(
        functools.partial(norm_kernel, slot),
        in_specs=[SCALAR] + [FULL] * 4 + [ANY] + [FULL] * len(uvs),
        out_specs=FULL,
        out_shape=jax.ShapeDtypeStruct((count, gain.shape[1]), BF16),
        compiler_params=params(16),
        cost_estimate=CHEAP,
        name="norm_rows",
    )(info, bc, keep, recv, gain, token, *uvs)


def project_kernel(base, added, a0, a1, w0_far, w1_far, *refs):
    out, w0, w1, sem = refs[-4:]
    j = pl.program_id(0)
    tiles = pl.num_programs(0)

    def fetch(t):
        slot = lax.rem(t, SLOTS)
        lanes = pl.ds(pl.multiple_of((base + t) * TILE, TILE), TILE)
        return (
            pltpu.make_async_copy(w0_far.at[:, lanes], w0.at[slot], sem.at[0, slot]),
            pltpu.make_async_copy(w1_far.at[:, lanes], w1.at[slot], sem.at[1, slot]),
        )

    def start(t):
        @pl.when(t < tiles)
        def _():
            for copy in fetch(t):
                copy.start()

    @pl.when(j == 0)
    def _():
        for t in range(SLOTS - 1):
            start(t)

    start(j + SLOTS - 1)
    for copy in fetch(j):
        copy.wait()
    slot = lax.rem(j, SLOTS)
    total = dot(a0[...], w0[slot]) + dot(a1[...], w1[slot])
    if added:
        total = total + refs[0][...].astype(F32)
    out[...] = total.astype(out.dtype)


def project(a0, a1, w0, w1, first, count, kind, arrived=None, result=None):
    rows, depth = a0.shape
    base = first // TILE
    full = arrived is not None
    operands, specs = [a0, a1, w0, w1], [FULL, FULL, FAR, FAR]
    if full:
        operands.append(arrived)
        specs.append(pl.BlockSpec((rows, TILE), lambda j: (0, j)))
    if result is not None:
        operands.append(result)
        specs.append(ANY)
    return pl.pallas_call(
        functools.partial(project_kernel, base, full),
        grid=(count // TILE,),
        in_specs=specs,
        out_specs=pl.BlockSpec((rows, TILE), lambda j: (0, base + j if full else j)),
        out_shape=jax.ShapeDtypeStruct((rows, w0.shape[1] if full else count), kind),
        scratch_shapes=[
            pltpu.VMEM((SLOTS, depth, TILE), BF16),
            pltpu.VMEM((SLOTS, depth, TILE), BF16),
            pltpu.SemaphoreType.DMA((2, SLOTS)),
        ],
        input_output_aliases={} if result is None else {len(operands) - 1: 0},
        compiler_params=params(20),
        cost_estimate=CHEAP,
        name="project",
    )(*operands)


def add_kernel(part, arrived, _, out):
    out[...] = (part[...] + arrived[...].astype(F32)).astype(BF16)


def add_chunk(part, arrived, result, first):
    rows, count = arrived.shape
    base = first // count
    return pl.pallas_call(
        add_kernel,
        grid=(1,),
        in_specs=[FULL, FULL, ANY],
        out_specs=pl.BlockSpec((rows, count), lambda j: (0, base)),
        out_shape=jax.ShapeDtypeStruct(result.shape, BF16),
        input_output_aliases={2: 0},
        compiler_params=params(8),
        cost_estimate=CHEAP,
        name="add_chunk",
    )(part, arrived, result)


def shift(block, distance):
    size = lax.axis_size("seq")
    return lax.ppermute(block, "seq", [(i, i + distance) for i in range(size - distance)])


def swap(block, axis, bit):
    return lax.ppermute(block, axis, [(i, i ^ bit) for i in range(lax.axis_size(axis))])


def local(
    x_input,
    z_input,
    bc_input,
    conv_weight_x,
    conv_weight_bc,
    step_size,
    log_decay,
    skip_gain,
    norm_gain,
    out_weight,
):
    length, width = x_input.shape
    heads = step_size.shape[1]
    ways = lax.axis_size("head")
    pairs = lax.axis_size("seq") // 2
    mine = lax.axis_index("head")
    half = width // 2
    info = jnp.stack([lax.axis_index("seq") & 1, mine ^ 3, mine ^ 2, mine ^ 1, mine]).astype(jnp.int32)

    x_far, z_far, w_far = [pltpu.with_memory_space_constraint(v, pltpu.HBM) for v in (x_input, z_input, out_weight)]
    bc = bc_input.reshape(length, -1)
    halo = shift(jnp.concatenate([x_input[length - LEAD :], bc[length - LEAD :]], 1), 1)
    weight_mate = swap(out_weight, "head", 1)

    ones = jnp.asarray(np.tile(np.repeat(np.eye(heads), P_SIZE, axis=1), (2, 1)), BF16)
    cum, cum_s, log_s, f_dev, f_blk, e_blk, rates = decays(log_decay, step_size, skip_gain, ones)
    x_conv, bc_conv, keep, send = conv_states(
        info, x_far, bc, halo, conv_weight_x, conv_weight_bc, f_dev, ones, rates
    )

    x_conv = pltpu.with_memory_space_constraint(x_conv, pltpu.HBM)
    uvs = []

    def scan_next(token):
        if len(uvs) < B_PARTS:
            uvs.append(
                scan_part(len(uvs), token, x_conv, bc_conv, z_far, cum, cum_s, log_s, f_blk, e_blk, rates, ones)
            )
        return uvs[-1]

    message = ((N + EXTRA, half), BF16)
    full = ((N, half), F32)
    got = swap(send, "seq", 1)
    done = scan_next(send)
    msg, own, first, aux = combine(
        pair_kernel,
        (info, got, keep, rates, done),
        [SCALAR, FULL, FULL, FULL, ANY],
        [message, full, full, ((16, half), F32)],
        "pair",
    )
    behind = None
    covered = 0
    while True:
        got = shift(msg, 2 * (covered + 1))
        done = scan_next(msg)
        covered = 2 * covered + 1
        if covered >= pairs - 1:
            break
        operands, specs = [got, own, aux], [FULL, FULL, FULL]
        if behind is None:
            kernel = lambda g, o, a, t, m, b: wave_kernel(g, o, a, None, t, m, b)
        else:
            kernel = wave_kernel
            operands.append(behind)
            specs.append(FULL)
        msg, behind = combine(kernel, operands + [done], specs + [ANY], [message, ((N + 8, half), F32)], "wave")
    operands, specs = [info, got], [SCALAR, FULL]
    if behind is None:
        kernel = lambda o, g, f, a, t, b, h: last_kernel(o, g, None, f, a, t, b, h)
    else:
        kernel = last_kernel
        operands.append(behind)
        specs.append(FULL)
    out = ((N, half), BF16)
    back, held = combine(kernel, operands + [first, aux, done], specs + [FULL, FULL, ANY], [out, out], "last")
    other = swap(back, "seq", 1)
    while len(uvs) < B_PARTS:
        scan_next(back)

    count = length // ways
    gain = norm_gain[None, :]

    def rows_for(slot, token):
        return norm_rows(slot, info, count, token, bc_conv, held, other, gain, uvs)

    far_mate = rows_for(1, held)
    far = rows_for(2, far_mate)
    far_mate = swap(far_mate, "head", 1)
    columns = out_weight.shape[1]
    cuts = [columns * c // 16 for c in (0, 3, 6, 9, 12, 14, 16)]
    arrivals = []
    for lo, hi in zip(cuts[:-1], cuts[1:]):
        sent = project(far, far_mate, w_far, weight_mate, lo, hi - lo, BF16)
        arrivals.append(swap(sent, "head", 2))
    near_mate = rows_for(3, far)
    near = rows_for(4, near_mate)
    near_mate = swap(near_mate, "head", 1)
    last = project(near, near_mate, w_far, weight_mate, cuts[-2], columns - cuts[-2], F32)
    result = None
    for arrived, lo, hi in zip(arrivals[:-1], cuts[:-2], cuts[1:-1]):
        result = project(near, near_mate, w_far, weight_mate, lo, hi - lo, BF16, arrived, result)
    return add_chunk(last, arrivals[-1], result, cuts[-2])


def solution(mesh):
    in_specs = (
        P("seq", "head"),
        P("seq", "head"),
        P("seq", "head", None),
        P(None, "head"),
        P(None, "head", None),
        P("seq", "head"),
        P("seq", "head"),
        P("head"),
        P("head"),
        P("head", None),
    )
    out_specs = P(("seq", "head"), None)
    return jax.shard_map(local, mesh=mesh, in_specs=in_specs, out_specs=out_specs, check_vma=False)
```

time: 172 us -> 127 us (0.74)
  the two profiles are of different devices: /device:TPU:0 before, /device:TPU:26 now
where the time goes in v4:
time: 127 us
  Pallas kernels  93.5 us (74%)
  starting transfers between devices  14.6 us (11%)
  waiting for transfers between devices  14.4 us (11%)
  local copies, waits for them, and re-layouts  3.28 us (3%)
    pallas_call x12, Pallas kernels, project(): pl.pallas_call(functools.partial(project_kernel, base, full), grid=(count...  46.8 us
    pallas_call x4, Pallas kernels, scan_part(): pl.pallas_call(functools.partial(scan_kernel, part), in_specs=[FAR, FAR]...  24 us
    pallas_call x1, Pallas kernels, conv_states(): pl.pallas_call(conv_kernel, grid=(length // TOK_A,), in_specs=[SCALAR, FA...  12.8 us
    ppermute x3, waiting for transfers between devices, shift(): lax.ppermute(block, 'seq', [(i, i + distance) for i in range(size - dista...  11.5 us
    ppermute x11, starting transfers between devices, swap(): lax.ppermute(block, axis, [(i, i ^ bit) for i in range(lax.axis_size(axis...  8.43 us
    ppermute x3, starting transfers between devices, shift(): lax.ppermute(block, 'seq', [(i, i + distance) for i in range(size - dista...  6.19 us
    pallas_call x4, Pallas kernels, norm_rows(): pl.pallas_call(functools.partial(norm_kernel, slot), in_specs=[SCALAR] +...  6.1 us
    ppermute x11, waiting for transfers between devices, swap(): lax.ppermute(block, axis, [(i, i ^ bit) for i in range(lax.axis_size(axis...  2.82 us
  transfers between devices with their start and end apart: 14, of which 5 were waited for; matrix products, arithmetic and copies ran while one was open for 3% of the time, Pallas kernels for 73%

profile of v4, /device:TPU:26, one launch (start us, length us, event | category | flops | bytes accessed | tf_op | source)
XLA Modules:
  0.0 126.8 jit_solution(2335427344352818206)
XLA Ops:
  2.5 3.4 %collective-permute-start = (bf16[16,2560]{1,0:T(8,128)(2,1)}, bf16[16,2560]{1,0:T(8,128)(2,1)S(1)}, u32[]{:S(2)}, u32[]{:S(2)}) collective-permute-start(bf16[16,2560]{1,0:T(8,128)(2,1)} %pad_maximum_fusion), channel_id=1, source_target_pairs={{0,4},{4,8},{8,12},{12,16},{16,20},{20,24},{24,28},{1,5},{5,9},{9,... | collective-permute-start | bytes 245768 | tf_op jit(solution)/shard_map/ppermute | solution.py:522
  10.2 12.8 %conv_states.1 = (bf16[1024,2048]{1,0:T(8,128)(2,1)}, bf16[1024,512]{1,0:T(8,128)(2,1)S(1)}, f32[128,1024]{1,0:T(8,128)S(1)}, bf16[144,1024]{1,0:T(8,128)(2,1)S(1)}) custom-call(s32[5]{0:T(128)S(1)} %stack.23.info, bf16[1024,2048]{1,0:T(8,128)(2,1)} %x_far.1, bf16[1024,512]{1,0:T(8,128)(2,1)S(1)} %bitcast.13, ...), custom_call_target="tpu_custom_call" | custom-call | flops 1 | bytes 1 | tf_op jit(solution)/shard_map/conv_states/pallas_call | solution.py:217
  23.7 6.0 %scan_part.4._.refs_0_ = bf16[1024,1024]{1,0:T(8,128)(2,1)S(1)} custom-call(bf16[1024,2048]{1,0:T(8,128)(2,1)} %get-tuple-element.29.x_far, bf16[1024,2048]{1,0:T(8,128)(2,1)} %z_far.7, bf16[1024,512]{1,0:T(8,128)(2,1)S(1)} %get-tuple-element.26.bc_all.bc, f32[1024,32]{1,0:T(8,128)S(1)} %get-tuple-element.30.cum, f32[32,1024]{1,0:T(8,128)S(1)} %get-tuple-element.31.cum_s, ...), custom_call_target="tpu_custom_call" | custom-call | flops 1 | bytes 1 | tf_op jit(solution)/shard_map/scan_part/pallas_call | solution.py:373
  29.7 1.8 %collective-permute-done.1.got = bf16[144,1024]{1,0:T(8,128)(2,1)S(1)} collective-permute-done((bf16[144,1024]{1,0:T(8,128)(2,1)S(1)}, bf16[144,1024]{1,0:T(8,128)(2,1)S(1)}, u32[]{:S(2)}, u32[]{:S(2)}) %collective-permute-start.1) | collective-permute-done | bytes 294944 | tf_op jit(solution)/shard_map/ppermute | solution.py:526
  33.5 6.0 %scan_part.5.t.refs_1_ = bf16[1024,1024]{1,0:T(8,128)(2,1)S(1)} custom-call(bf16[1024,2048]{1,0:T(8,128)(2,1)} %get-tuple-element.29.x_far, bf16[1024,2048]{1,0:T(8,128)(2,1)} %z_far.7, bf16[1024,512]{1,0:T(8,128)(2,1)S(1)} %get-tuple-element.26.bc_all.bc, f32[1024,32]{1,0:T(8,128)S(1)} %get-tuple-element.30.cum, f32[32,1024]{1,0:T(8,128)S(1)} %get-tuple-element.31.cum_s, ...), custom_call_target="tpu_custom_call" | custom-call | flops 1 | bytes 1 | tf_op jit(solution)/shard_map/scan_part/pallas_call | solution.py:373
  39.5 2.1 %collective-permute-done.2.g = bf16[144,1024]{1,0:T(8,128)(2,1)S(1)} collective-permute-done((bf16[144,1024]{1,0:T(8,128)(2,1)S(1)}, bf16[144,1024]{1,0:T(8,128)(2,1)S(1)}, u32[]{:S(2)}, u32[]{:S(2)}) %collective-permute-start.2) | collective-permute-done | bytes 294944 | tf_op jit(solution)/shard_map/ppermute | solution.py:522
  43.3 6.0 %scan_part.6._.refs_2_ = bf16[1024,1024]{1,0:T(8,128)(2,1)S(1)} custom-call(bf16[1024,2048]{1,0:T(8,128)(2,1)} %get-tuple-element.29.x_far, bf16[1024,2048]{1,0:T(8,128)(2,1)} %z_far.7, bf16[1024,512]{1,0:T(8,128)(2,1)S(1)} %get-tuple-element.26.bc_all.bc, f32[1024,32]{1,0:T(8,128)S(1)} %get-tuple-element.30.cum, f32[32,1024]{1,0:T(8,128)S(1)} %get-tuple-element.31.cum_s, ...), custom_call_target="tpu_custom_call" | custom-call | flops 1 | bytes 1 | tf_op jit(solution)/shard_map/scan_part/pallas_call | solution.py:373
  49.3 8.3 %collective-permute-done.3.got = bf16[144,1024]{1,0:T(8,128)(2,1)S(1)} collective-permute-done((bf16[144,1024]{1,0:T(8,128)(2,1)S(1)}, bf16[144,1024]{1,0:T(8,128)(2,1)S(1)}, u32[]{:S(2)}, u32[]{:S(2)}) %collective-permute-start.3) | collective-permute-done | bytes 294944 | tf_op jit(solution)/shard_map/ppermute | solution.py:522
  58.9 6.0 %scan_part.7.refs_3_ = bf16[1024,1024]{1,0:T(8,128)(2,1)S(1)} custom-call(bf16[1024,2048]{1,0:T(8,128)(2,1)} %get-tuple-element.29.x_far, bf16[1024,2048]{1,0:T(8,128)(2,1)} %z_far.7, bf16[1024,512]{1,0:T(8,128)(2,1)S(1)} %get-tuple-element.26.bc_all.bc, f32[1024,32]{1,0:T(8,128)S(1)} %get-tuple-element.30.cum, f32[32,1024]{1,0:T(8,128)S(1)} %get-tuple-element.31.cum_s, ...), custom_call_target="tpu_custom_call" | custom-call | flops 1 | bytes 1 | tf_op jit(solution)/shard_map/scan_part/pallas_call | solution.py:373
  71.1 3.8 %project.18 = bf16[256,768]{1,0:T(8,128)(2,1)S(1)} custom-call(bf16[256,2048]{1,0:T(8,128)(2,1)S(1)} %norm_rows.5._.a0, bf16[256,2048]{1,0:T(8,128)(2,1)S(1)} %collective-permute-done.7.a1, bf16[2048,4096]{1,0:T(8,128)(2,1)} %w0_far.23, bf16[2048,4096]{1,0:T(8,128)(2,1)} %collective-permute-done.6.w1_far), custom_call_target="tpu_custom_call" | custom-call | flops 1 | bytes 1 | tf_op jit(solution)/shard_map/project/pallas_call | solution.py:482
  75.5 3.8 %project.17 = bf16[256,768]{1,0:T(8,128)(2,1)S(1)} custom-call(bf16[256,2048]{1,0:T(8,128)(2,1)S(1)} %norm_rows.5._.a0, bf16[256,2048]{1,0:T(8,128)(2,1)S(1)} %collective-permute-done.7.a1, bf16[2048,4096]{1,0:T(8,128)(2,1)} %w0_far.23, bf16[2048,4096]{1,0:T(8,128)(2,1)} %collective-permute-done.6.w1_far), custom_call_target="tpu_custom_call" | custom-call | flops 1 | bytes 1 | tf_op jit(solution)/shard_map/project/pallas_call | solution.py:482
  79.4 1.6 %collective-permute-start.12 = (bf16[256,768]{1,0:T(8,128)(2,1)S(1)}, bf16[256,768]{1,0:T(8,128)(2,1)S(1)}, u32[]{:S(2)}, u32[]{:S(2)}) collective-permute-start(bf16[256,768]{1,0:T(8,128)(2,1)S(1)} %project.17), channel_id=1, source_target_pairs={{0,2},{1,3},{2,0},{3,1},{4,6},{5,7},{6,4},{7,5},{8,10},{9,11},{10,... | collective-permute-start | bytes 1179656 | tf_op jit(solution)/shard_map/ppermute | solution.py:526
  81.0 3.8 %project.16 = bf16[256,768]{1,0:T(8,128)(2,1)S(1)} custom-call(bf16[256,2048]{1,0:T(8,128)(2,1)S(1)} %norm_rows.5._.a0, bf16[256,2048]{1,0:T(8,128)(2,1)S(1)} %collective-permute-done.7.a1, bf16[2048,4096]{1,0:T(8,128)(2,1)} %w0_far.23, bf16[2048,4096]{1,0:T(8,128)(2,1)} %collective-permute-done.6.w1_far), custom_call_target="tpu_custom_call" | custom-call | flops 1 | bytes 1 | tf_op jit(solution)/shard_map/project/pallas_call | solution.py:482
  85.4 3.8 %project.15 = bf16[256,768]{1,0:T(8,128)(2,1)S(1)} custom-call(bf16[256,2048]{1,0:T(8,128)(2,1)S(1)} %norm_rows.5._.a0, bf16[256,2048]{1,0:T(8,128)(2,1)S(1)} %collective-permute-done.7.a1, bf16[2048,4096]{1,0:T(8,128)(2,1)} %w0_far.23, bf16[2048,4096]{1,0:T(8,128)(2,1)} %collective-permute-done.6.w1_far), custom_call_target="tpu_custom_call" | custom-call | flops 1 | bytes 1 | tf_op jit(solution)/shard_map/project/pallas_call | solution.py:482
  89.2 1.6 %collective-permute-start.10 = (bf16[256,768]{1,0:T(8,128)(2,1)S(1)}, bf16[256,768]{1,0:T(8,128)(2,1)S(1)}, u32[]{:S(2)}, u32[]{:S(2)}) collective-permute-start(bf16[256,768]{1,0:T(8,128)(2,1)S(1)} %project.15), channel_id=1, source_target_pairs={{0,2},{1,3},{2,0},{3,1},{4,6},{5,7},{6,4},{7,5},{8,10},{9,11},{10,... | collective-permute-start | bytes 1179656 | tf_op jit(solution)/shard_map/ppermute | solution.py:526
  90.8 3.1 %project.14 = bf16[256,512]{1,0:T(8,128)(2,1)S(1)} custom-call(bf16[256,2048]{1,0:T(8,128)(2,1)S(1)} %norm_rows.5._.a0, bf16[256,2048]{1,0:T(8,128)(2,1)S(1)} %collective-permute-done.7.a1, bf16[2048,4096]{1,0:T(8,128)(2,1)} %w0_far.23, bf16[2048,4096]{1,0:T(8,128)(2,1)} %collective-permute-done.6.w1_far), custom_call_target="tpu_custom_call" | custom-call | flops 1 | bytes 1 | tf_op jit(solution)/shard_map/project/pallas_call | solution.py:482
  93.9 3.1 %project.13 = bf16[256,512]{1,0:T(8,128)(2,1)S(1)} custom-call(bf16[256,2048]{1,0:T(8,128)(2,1)S(1)} %norm_rows.5._.a0, bf16[256,2048]{1,0:T(8,128)(2,1)S(1)} %collective-permute-done.7.a1, bf16[2048,4096]{1,0:T(8,128)(2,1)} %w0_far.23, bf16[2048,4096]{1,0:T(8,128)(2,1)} %collective-permute-done.6.w1_far), custom_call_target="tpu_custom_call" | custom-call | flops 1 | bytes 1 | tf_op jit(solution)/shard_map/project/pallas_call | solution.py:482
  97.6 1.6 %collective-permute-start.8 = (bf16[256,512]{1,0:T(8,128)(2,1)S(1)}, bf16[256,512]{1,0:T(8,128)(2,1)S(1)}, u32[]{:S(2)}, u32[]{:S(2)}) collective-permute-start(bf16[256,512]{1,0:T(8,128)(2,1)S(1)} %project.13), channel_id=1, source_target_pairs={{0,2},{1,3},{2,0},{3,1},{4,6},{5,7},{6,4},{7,5},{8,10},{9,11},{10,... | collective-permute-start | bytes 786440 | tf_op jit(solution)/shard_map/ppermute | solution.py:526
  100.7 3.1 %project.12.part = f32[256,512]{1,0:T(8,128)S(1)} custom-call(bf16[256,2048]{1,0:T(8,128)(2,1)S(1)} %norm_rows.7.a0, bf16[256,2048]{1,0:T(8,128)(2,1)S(1)} %collective-permute-done.5.a1, bf16[2048,4096]{1,0:T(8,128)(2,1)} %w0_far.23, bf16[2048,4096]{1,0:T(8,128)(2,1)} %collective-permute-done.6.w1_far), custom_call_target="tpu_custom_call" | custom-call | flops 1 | bytes 1 | tf_op jit(solution)/shard_map/project/pallas_call | solution.py:482
  103.8 4.6 %project.19.refs_1_ = bf16[256,4096]{1,0:T(8,128)(2,1)} custom-call(bf16[256,2048]{1,0:T(8,128)(2,1)S(1)} %norm_rows.7.a0, bf16[256,2048]{1,0:T(8,128)(2,1)S(1)} %collective-permute-done.5.a1, bf16[2048,4096]{1,0:T(8,128)(2,1)} %w0_far.23, bf16[2048,4096]{1,0:T(8,128)(2,1)} %collective-permute-done.6.w1_far, bf16[256,768]{1,0:T(8,128)(2,1)S(1)} %collective-permute-done.13.refs_0_), custom_call_target="tpu_custom_call" | custom-call | flops 1 | bytes 1 | tf_op jit(solution)/shard_map/project/pallas_call | solution.py:482
  108.4 4.6 %project.20.refs_1_ = bf16[256,4096]{1,0:T(8,128)(2,1)} custom-call(bf16[256,2048]{1,0:T(8,128)(2,1)S(1)} %norm_rows.7.a0, bf16[256,2048]{1,0:T(8,128)(2,1)S(1)} %collective-permute-done.5.a1, bf16[2048,4096]{1,0:T(8,128)(2,1)} %w0_far.23, bf16[2048,4096]{1,0:T(8,128)(2,1)} %collective-permute-done.6.w1_far, ...), custom_call_target="tpu_custom_call", output_to_operand_aliasing={{}: (5, {})} | custom-call | flops 1 | bytes 1 | tf_op jit(solution)/shard_map/project/pallas_call | solution.py:482
  113.0 4.6 %project.21.refs_1_ = bf16[256,4096]{1,0:T(8,128)(2,1)} custom-call(bf16[256,2048]{1,0:T(8,128)(2,1)S(1)} %norm_rows.7.a0, bf16[256,2048]{1,0:T(8,128)(2,1)S(1)} %collective-permute-done.5.a1, bf16[2048,4096]{1,0:T(8,128)(2,1)} %w0_far.23, bf16[2048,4096]{1,0:T(8,128)(2,1)} %collective-permute-done.6.w1_far, ...), custom_call_target="tpu_custom_call", output_to_operand_aliasing={{}: (5, {})} | custom-call | flops 1 | bytes 1 | tf_op jit(solution)/shard_map/project/pallas_call | solution.py:482
  117.6 4.6 %project.22.refs_1_ = bf16[256,4096]{1,0:T(8,128)(2,1)} custom-call(bf16[256,2048]{1,0:T(8,128)(2,1)S(1)} %norm_rows.7.a0, bf16[256,2048]{1,0:T(8,128)(2,1)S(1)} %collective-permute-done.5.a1, bf16[2048,4096]{1,0:T(8,128)(2,1)} %w0_far.23, bf16[2048,4096]{1,0:T(8,128)(2,1)} %collective-permute-done.6.w1_far, ...), custom_call_target="tpu_custom_call", output_to_operand_aliasing={{}: (5, {})} | custom-call | flops 1 | bytes 1 | tf_op jit(solution)/shard_map/project/pallas_call | solution.py:482
  122.2 3.8 %project.23._ = bf16[256,4096]{1,0:T(8,128)(2,1)} custom-call(bf16[256,2048]{1,0:T(8,128)(2,1)S(1)} %norm_rows.7.a0, bf16[256,2048]{1,0:T(8,128)(2,1)S(1)} %collective-permute-done.5.a1, bf16[2048,4096]{1,0:T(8,128)(2,1)} %w0_far.23, bf16[2048,4096]{1,0:T(8,128)(2,1)} %collective-permute-done.6.w1_far, ...), custom_call_target="tpu_custom_call", output_to_operand_aliasing={{}: (5, {})} | custom-call | flops 1 | bytes 1 | tf_op jit(solution)/shard_map/project/pallas_call | solution.py:482
  (50 shorter events, 22.4 us)
Async XLA Ops:
  0.0 7.4 %copy-start = (bf16[64,2048]{1,0:T(8,128)(2,1)S(1)}, bf16[64,2048]{1,0:T(8,128)(2,1)}, u32[]{:S(2)}) copy-start(bf16[64,2048]{1,0:T(8,128)(2,1)} %constant.17.clone.ones) | copy-start | bytes 786436
  0.0 7.4 %copy-start.6 = (f32[32]{0:T(128)S(1)}, f32[32]{0:T(128)}, u32[]{:S(2)}) copy-start(f32[32]{0:T(128)} %param.18) | copy-start | bytes 388
  0.0 7.4 %copy-start.1 = (f32[1024,32]{0,1:T(8,128)S(1)}, f32[1024,32]{0,1:T(8,128)}, u32[]{:S(2)}) copy-start(f32[1024,32]{0,1:T(8,128)} %param.17) | copy-start | bytes 393220
  0.0 7.4 %copy-start.2 = (f32[1024,32]{0,1:T(8,128)S(1)}, f32[1024,32]{0,1:T(8,128)}, u32[]{:S(2)}) copy-start(f32[1024,32]{0,1:T(8,128)} %param.16) | copy-start | bytes 393220
  0.0 10.2 %copy-start.5 = (f32[4,2,256]{2,1,0:T(2,128)S(1)}, f32[4,2,256]{2,1,0:T(2,128)}, u32[]{:S(2)}) copy-start(f32[4,2,256]{2,1,0:T(2,128)} %wbc.1) | copy-start | bytes 24580
  0.0 10.2 %copy-start.4 = (f32[4,2048]{1,0:T(4,128)S(1)}, f32[4,2048]{1,0:T(4,128)}, u32[]{:S(2)}) copy-start(f32[4,2048]{1,0:T(4,128)} %wx.1) | copy-start | bytes 98308
  0.0 71.1 %collective-permute-start.6 = (bf16[2048,4096]{1,0:T(8,128)(2,1)}, bf16[2048,4096]{1,0:T(8,128)(2,1)}, u32[]{:S(2)}, u32[]{:S(2)}) collective-permute-start(bf16[2048,4096]{1,0:T(8,128)(2,1)} %w0_far.23), channel_id=1, source_target_pairs={{0,1},{1,0},{2,3},{3,2},{4,5},{5,4},{6,7},{7,6},{8,9},{9,8},{10,11... | collective-permute-start | bytes 50331656 | tf_op jit(solution)/shard_map/ppermute | solution.py:526
  2.5 7.7 %collective-permute-start = (bf16[16,2560]{1,0:T(8,128)(2,1)}, bf16[16,2560]{1,0:T(8,128)(2,1)S(1)}, u32[]{:S(2)}, u32[]{:S(2)}) collective-permute-start(bf16[16,2560]{1,0:T(8,128)(2,1)} %pad_maximum_fusion), channel_id=1, source_target_pairs={{0,4},{4,8},{8,12},{12,16},{16,20},{20,24},{24,28},{1,5},{5,9},{9,... | collective-permute-start | bytes 245768 | tf_op jit(solution)/shard_map/ppermute | solution.py:522
  23.0 8.5 %collective-permute-start.1 = (bf16[144,1024]{1,0:T(8,128)(2,1)S(1)}, bf16[144,1024]{1,0:T(8,128)(2,1)S(1)}, u32[]{:S(2)}, u32[]{:S(2)}) collective-permute-start(bf16[144,1024]{1,0:T(8,128)(2,1)S(1)} %get-tuple-element.27._), channel_id=1, source_target_pairs={{0,4},{4,0},{8,12},{12,8},{16,20},{20,16},{24,28},{28,24},{1,5},{5... | collective-permute-start | bytes 884744 | tf_op jit(solution)/shard_map/ppermute | solution.py:526
  32.2 9.4 %collective-permute-start.2 = (bf16[144,1024]{1,0:T(8,128)(2,1)S(1)}, bf16[144,1024]{1,0:T(8,128)(2,1)S(1)}, u32[]{:S(2)}, u32[]{:S(2)}) collective-permute-start(bf16[144,1024]{1,0:T(8,128)(2,1)S(1)} %get-tuple-element.35._), channel_id=1, source_target_pairs={{0,8},{4,12},{8,16},{12,20},{16,24},{20,28},{1,9},{5,13},{9,17},{1... | collective-permute-start | bytes 884744 | tf_op jit(solution)/shard_map/ppermute | solution.py:522
  41.8 15.7 %collective-permute-start.3 = (bf16[144,1024]{1,0:T(8,128)(2,1)S(1)}, bf16[144,1024]{1,0:T(8,128)(2,1)S(1)}, u32[]{:S(2)}, u32[]{:S(2)}) collective-permute-start(bf16[144,1024]{1,0:T(8,128)(2,1)S(1)} %get-tuple-element.38._), channel_id=1, source_target_pairs={{0,16},{4,20},{8,24},{12,28},{1,17},{5,21},{9,25},{13,29},{2,18},{... | collective-permute-start | bytes 884744 | tf_op jit(solution)/shard_map/ppermute | solution.py:522
  58.3 7.6 %copy-start.3 = (f32[2048]{0:T(1024)S(1)}, f32[2048]{0:T(1024)}, u32[]{:S(2)}) copy-start(f32[2048]{0:T(1024)} %param.19) | copy-start | bytes 24580
  58.3 7.6 %collective-permute-start.4 = (bf16[128,1024]{1,0:T(8,128)(2,1)S(1)}, bf16[128,1024]{1,0:T(8,128)(2,1)S(1)}, u32[]{:S(2)}, u32[]{:S(2)}) collective-permute-start(bf16[128,1024]{1,0:T(8,128)(2,1)S(1)} %get-tuple-element.42._), channel_id=1, source_target_pairs={{0,4},{4,0},{8,12},{12,8},{16,20},{20,16},{24,28},{28,24},{1,5},{5... | collective-permute-start | bytes 786440 | tf_op jit(solution)/shard_map/ppermute | solution.py:526
  67.4 3.7 %collective-permute-start.7 = (bf16[256,2048]{1,0:T(8,128)(2,1)S(1)}, bf16[256,2048]{1,0:T(8,128)(2,1)S(1)}, u32[]{:S(2)}, u32[]{:S(2)}) collective-permute-start(bf16[256,2048]{1,0:T(8,128)(2,1)S(1)} %norm_rows.4._), channel_id=1, source_target_pairs={{0,1},{1,0},{2,3},{3,2},{4,5},{5,4},{6,7},{7,6},{8,9},{9,8},{10,11... | collective-permute-start | bytes 3145736 | tf_op jit(solution)/shard_map/ppermute | solution.py:526
  70.6 26.5 %collective-permute-start.5 = (bf16[256,2048]{1,0:T(8,128)(2,1)S(1)}, bf16[256,2048]{1,0:T(8,128)(2,1)S(1)}, u32[]{:S(2)}, u32[]{:S(2)}) collective-permute-start(bf16[256,2048]{1,0:T(8,128)(2,1)S(1)} %norm_rows.6._), channel_id=1, source_target_pairs={{0,1},{1,0},{2,3},{3,2},{4,5},{5,4},{6,7},{7,6},{8,9},{9,8},{10,11... | collective-permute-start | bytes 3145736 | tf_op jit(solution)/shard_map/ppermute | solution.py:526
  75.0 22.6 %collective-permute-start.13 = (bf16[256,768]{1,0:T(8,128)(2,1)S(1)}, bf16[256,768]{1,0:T(8,128)(2,1)S(1)}, u32[]{:S(2)}, u32[]{:S(2)}) collective-permute-start(bf16[256,768]{1,0:T(8,128)(2,1)S(1)} %project.18), channel_id=1, source_target_pairs={{0,2},{1,3},{2,0},{3,1},{4,6},{5,7},{6,4},{7,5},{8,10},{9,11},{10,... | collective-permute-start | bytes 1179656 | tf_op jit(solution)/shard_map/ppermute | solution.py:526
  79.4 29.0 %collective-permute-start.12 = (bf16[256,768]{1,0:T(8,128)(2,1)S(1)}, bf16[256,768]{1,0:T(8,128)(2,1)S(1)}, u32[]{:S(2)}, u32[]{:S(2)}) collective-permute-start(bf16[256,768]{1,0:T(8,128)(2,1)S(1)} %project.17), channel_id=1, source_target_pairs={{0,2},{1,3},{2,0},{3,1},{4,6},{5,7},{6,4},{7,5},{8,10},{9,11},{10,... | collective-permute-start | bytes 1179656 | tf_op jit(solution)/shard_map/ppermute | solution.py:526
  84.8 28.2 %collective-permute-start.11 = (bf16[256,768]{1,0:T(8,128)(2,1)S(1)}, bf16[256,768]{1,0:T(8,128)(2,1)S(1)}, u32[]{:S(2)}, u32[]{:S(2)}) collective-permute-start(bf16[256,768]{1,0:T(8,128)(2,1)S(1)} %project.16), channel_id=1, source_target_pairs={{0,2},{1,3},{2,0},{3,1},{4,6},{5,7},{6,4},{7,5},{8,10},{9,11},{10,... | collective-permute-start | bytes 1179656 | tf_op jit(solution)/shard_map/ppermute | solution.py:526
  89.2 28.4 %collective-permute-start.10 = (bf16[256,768]{1,0:T(8,128)(2,1)S(1)}, bf16[256,768]{1,0:T(8,128)(2,1)S(1)}, u32[]{:S(2)}, u32[]{:S(2)}) collective-permute-start(bf16[256,768]{1,0:T(8,128)(2,1)S(1)} %project.15), channel_id=1, source_target_pairs={{0,2},{1,3},{2,0},{3,1},{4,6},{5,7},{6,4},{7,5},{8,10},{9,11},{10,... | collective-permute-start | bytes 1179656 | tf_op jit(solution)/shard_map/ppermute | solution.py:526
  97.1 25.1 %collective-permute-start.9 = (bf16[256,512]{1,0:T(8,128)(2,1)S(1)}, bf16[256,512]{1,0:T(8,128)(2,1)S(1)}, u32[]{:S(2)}, u32[]{:S(2)}) collective-permute-start(bf16[256,512]{1,0:T(8,128)(2,1)S(1)} %project.14), channel_id=1, source_target_pairs={{0,2},{1,3},{2,0},{3,1},{4,6},{5,7},{6,4},{7,5},{8,10},{9,11},{10,... | collective-permute-start | bytes 786440 | tf_op jit(solution)/shard_map/ppermute | solution.py:526
  97.6 28.4 %collective-permute-start.8 = (bf16[256,512]{1,0:T(8,128)(2,1)S(1)}, bf16[256,512]{1,0:T(8,128)(2,1)S(1)}, u32[]{:S(2)}, u32[]{:S(2)}) collective-permute-start(bf16[256,512]{1,0:T(8,128)(2,1)S(1)} %project.13), channel_id=1, source_target_pairs={{0,2},{1,3},{2,0},{3,1},{4,6},{5,7},{6,4},{7,5},{8,10},{9,11},{10,... | collective-permute-start | bytes 786440 | tf_op jit(solution)/shard_map/ppermute | solution.py:526

commit v5 on v4

--- a/solution.py
+++ b/solution.py
@@ -15,7 +15,7 @@
 LOG2E = 1.4426950408889634
 
 TOK_A = 256
-ROWS_A = 32
+ROWS_A = 64
 TOK_B = 128
 STEP_B = 256
 EXTRA = 16
@@ -145,11 +145,15 @@
 
     @pl.when(i == 0)
     def _():
-        for step in range(x.shape[0] // rows):
-            fetch(step).start()
+        fetch(0).start()
         state[...] = jnp.zeros_like(state)
 
     fetch(i).wait()
+
+    @pl.when(i + 1 < pl.num_programs(0))
+    def _():
+        fetch(i + 1).start()
+
     base = pl.multiple_of(i * rows, rows)
     before = pl.ds(pl.multiple_of(jnp.maximum(base - LEAD, 0), LEAD), LEAD)
 
@@ -182,16 +186,18 @@
             conv(lambda r: bc[at(r), ds], lead, [wbc[k, c : c + 1, inner] for k in range(KCONV)], emit_bc)
 
     def slab(c, _):
-        ds = pl.ds(pl.multiple_of(c * SLAB, SLAB), SLAB)
-        scale = dot(f_dev[pl.ds(base, rows), :], ones[:, ds])
-
-        def emit(r, value):
-            value = value.astype(BF16)
-            x_out[r : r + ROWS_A, ds] = value
-            xf[r : r + ROWS_A, ds] = (value.astype(F32) * scale[r : r + ROWS_A]).astype(BF16)
-
-        lead = jnp.where(start, halo[:, ds], x[before, ds]).astype(F32)
-        conv(lambda r: x[at(r), ds], lead, [wx[k : k + 1, ds] for k in range(KCONV)], emit)
+        first = pl.multiple_of(c * SLAB, SLAB)
+        scale = dot(f_dev[pl.ds(base, rows), :], ones[:, pl.ds(first, SLAB)])
+        for sub in range(0, SLAB, N):
+            ds = pl.ds(pl.multiple_of(first + sub, N), N)
+
+            def emit(r, value):
+                value = value.astype(BF16)
+                x_out[r : r + ROWS_A, ds] = value
+                xf[r : r + ROWS_A, ds] = (value.astype(F32) * scale[r : r + ROWS_A, sub : sub + N]).astype(BF16)
+
+            lead = jnp.where(start, halo[:, ds], x[before, ds]).astype(F32)
+            conv(lambda r: x[at(r), ds], lead, [wx[k : k + 1, ds] for k in range(KCONV)], emit)
         return 0
 
     lax.fori_loop(0, width // SLAB, slab, 0)
@@ -282,13 +288,66 @@
     held[...] = jnp.where(is_odd, entering_odd, before).astype(BF16)
 
 
-def combine(kernel, operands, specs, outs, name):
+def pair_split_kernel(info, got, keep, rates, _, first, aux, *refs):
+    outs, wide = refs[:-1], refs[-1]
+    half = keep.shape[1]
+    pairs = len(outs)
+    piece = half // pairs
+    is_odd = info[0] == 1
+    arrived, their = take_message(got)
+    row = rates.shape[0] - 16
+    mine = jnp.where(is_odd, rates[row : row + 1, half:], rates[row : row + 1, 0:half])
+    early = jnp.where(is_odd, arrived, keep[...])
+    late = jnp.where(is_odd, keep[...], arrived)
+    even_decay = jnp.where(is_odd, their, mine)
+    odd_decay = jnp.where(is_odd, mine, their)
+    first[...] = early
+    aux[...] = jnp.broadcast_to(even_decay, (8, half))
+    put_message(wide, odd_decay * early + late, even_decay * odd_decay)
+    for r in range(pairs):
+        owner = lax.rem(info[5] + r, pairs)
+        outs[r][...] = wide[:, pl.ds(pl.multiple_of(owner * piece, piece), piece)]
+
+
+def owner_kernel(info, *refs):
+    pairs = (len(refs) - 3) // 2
+    ins, outs = refs[:pairs], refs[pairs + 1 : 2 * pairs + 1]
+    states, prefixes = refs[-2:]
+    for r in range(pairs):
+        states[lax.rem(info[5] + pairs - r, pairs)] = ins[r][...]
+    before = jnp.zeros(prefixes.shape[1:], F32)
+    for q in range(pairs):
+        prefixes[q] = before.astype(BF16)
+        if q < pairs - 1:
+            state, decay = take_message(states.at[q])
+            before = decay * before + state
+    for r in range(pairs):
+        outs[r][...] = prefixes[lax.rem(info[5] + r, pairs)]
+
+
+def last_split_kernel(info, first, aux, _, *refs):
+    pairs = len(refs) - 3
+    back, held, wide = refs[-3:]
+    piece = back.shape[1] // pairs
+    for r in range(pairs):
+        owner = lax.rem(info[5] + pairs - r, pairs)
+        wide[:, pl.ds(pl.multiple_of(owner * piece, piece), piece)] = refs[r][...]
+    is_odd = info[0] == 1
+    before = wide[...].astype(F32)
+    entering_odd = aux[0:1, :] * before + first[...]
+    back[...] = jnp.where(is_odd, before, entering_odd).astype(BF16)
+    held[...] = jnp.where(is_odd, entering_odd, before).astype(BF16)
+
+
+def combine(kernel, operands, specs, outs, name, scratch=()):
     return pl.pallas_call(
         kernel,
         in_specs=specs,
         out_specs=[FULL] * len(outs),
         out_shape=[jax.ShapeDtypeStruct(s, t) for s, t in outs],
+        scratch_shapes=list(scratch),
         compiler_params=params(16),
+        cost_estimate=CHEAP,
         name=name,
     )(*operands)
 
@@ -323,12 +382,14 @@
     first = lax.broadcasted_iota(jnp.int32, (TOK_B, 2 * P_SIZE), 1) < P_SIZE
     zero = jnp.zeros((TOK_B, 2 * P_SIZE), BF16)
 
-    def block(b, _):
-        @pl.when(lax.rem(b, inner) == 0)
-        def _():
-            for copy in fetch(lax.div(b, inner)):
-                copy.wait()
-
+    def turn(step, _):
+        for copy in fetch(step):
+            copy.wait()
+        for k in range(inner):
+            block(step * inner + k)
+        return 0
+
+    def block(b):
         at = pl.ds(pl.multiple_of(b * TOK_B, TOK_B), TOK_B)
         b_mat = bc_all[at, b_lanes]
         c_mat = bc_all[at, c_lanes]
@@ -362,9 +423,8 @@
             uv_out[at, width + s * SLAB : width + (s + 1) * SLAB] = (gate * rise * lead_rows[:, lanes]).astype(BF16)
             xf = (xs * dot(f_blk[at, :], sel)).astype(BF16)
             state[:, lanes] = old * fade_rows[:, lanes] + dot(b_mat, xf, ((0,), (0,)))
-        return 0
-
-    lax.fori_loop(0, blocks, block, 0)
+
+    lax.fori_loop(0, length // STEP_B, turn, 0)
 
 
 def scan_part(part, token, x, bc, z, cum, cum_s, log_s, f_blk, e_blk, rates, ones):
@@ -497,6 +557,65 @@
     )(*operands)
 
 
+def project_both_kernel(base, a0_far, a1_far, a0_near, a1_near, w0_far, w1_far, far, near, a0, a1, w0, w1, sem):
+    j = pl.program_id(0)
+    tiles = pl.num_programs(0)
+    rows = far.shape[0]
+
+    def fetch(t):
+        slot = lax.rem(t, SLOTS)
+        lanes = pl.ds(pl.multiple_of((base + t) * TILE, TILE), TILE)
+        return (
+            pltpu.make_async_copy(w0_far.at[:, lanes], w0.at[slot], sem.at[0, slot]),
+            pltpu.make_async_copy(w1_far.at[:, lanes], w1.at[slot], sem.at[1, slot]),
+        )
+
+    def start(t):
+        @pl.when(t < tiles)
+        def _():
+            for copy in fetch(t):
+                copy.start()
+
+    @pl.when(j == 0)
+    def _():
+        for t in range(SLOTS - 1):
+            start(t)
+        a0[0:rows, :] = a0_far[...]
+        a0[rows:, :] = a0_near[...]
+        a1[0:rows, :] = a1_far[...]
+        a1[rows:, :] = a1_near[...]
+
+    start(j + SLOTS - 1)
+    for copy in fetch(j):
+        copy.wait()
+    slot = lax.rem(j, SLOTS)
+    total = dot(a0[...], w0[slot]) + dot(a1[...], w1[slot])
+    far[...] = total[0:rows].astype(BF16)
+    near[...] = total[rows:]
+
+
+def project_both(far, far_mate, near, near_mate, w0, w1, first, count):
+    rows, depth = far.shape
+    placed = pl.BlockSpec((rows, TILE), lambda j: (0, j))
+    return pl.pallas_call(
+        functools.partial(project_both_kernel, first // TILE),
+        grid=(count // TILE,),
+        in_specs=[FULL] * 4 + [FAR] * 2,
+        out_specs=[placed, placed],
+        out_shape=[jax.ShapeDtypeStruct((rows, count), BF16), jax.ShapeDtypeStruct((rows, count), F32)],
+        scratch_shapes=[
+            pltpu.VMEM((2 * rows, depth), BF16),
+            pltpu.VMEM((2 * rows, depth), BF16),
+            pltpu.VMEM((SLOTS, depth, TILE), BF16),
+            pltpu.VMEM((SLOTS, depth, TILE), BF16),
+            pltpu.SemaphoreType.DMA((2, SLOTS)),
+        ],
+        compiler_params=params(24),
+        cost_estimate=CHEAP,
+        name="project_both",
+    )(far, far_mate, near, near_mate, w0, w1)
+
+
 def add_kernel(part, arrived, _, out):
     out[...] = (part[...] + arrived[...].astype(F32)).astype(BF16)
 
@@ -526,51 +645,16 @@
     return lax.ppermute(block, axis, [(i, i ^ bit) for i in range(lax.axis_size(axis))])
 
 
-def local(
-    x_input,
-    z_input,
-    bc_input,
-    conv_weight_x,
-    conv_weight_bc,
-    step_size,
-    log_decay,
-    skip_gain,
-    norm_gain,
-    out_weight,
-):
-    length, width = x_input.shape
-    heads = step_size.shape[1]
-    ways = lax.axis_size("head")
+def rotate(block, turns, sends):
     pairs = lax.axis_size("seq") // 2
-    mine = lax.axis_index("head")
-    half = width // 2
-    info = jnp.stack([lax.axis_index("seq") & 1, mine ^ 3, mine ^ 2, mine ^ 1, mine]).astype(jnp.int32)
-
-    x_far, z_far, w_far = [pltpu.with_memory_space_constraint(v, pltpu.HBM) for v in (x_input, z_input, out_weight)]
-    bc = bc_input.reshape(length, -1)
-    halo = shift(jnp.concatenate([x_input[length - LEAD :], bc[length - LEAD :]], 1), 1)
-    weight_mate = swap(out_weight, "head", 1)
-
-    ones = jnp.asarray(np.tile(np.repeat(np.eye(heads), P_SIZE, axis=1), (2, 1)), BF16)
-    cum, cum_s, log_s, f_dev, f_blk, e_blk, rates = decays(log_decay, step_size, skip_gain, ones)
-    x_conv, bc_conv, keep, send = conv_states(
-        info, x_far, bc, halo, conv_weight_x, conv_weight_bc, f_dev, ones, rates
-    )
-
-    x_conv = pltpu.with_memory_space_constraint(x_conv, pltpu.HBM)
-    uvs = []
-
-    def scan_next(token):
-        if len(uvs) < B_PARTS:
-            uvs.append(
-                scan_part(len(uvs), token, x_conv, bc_conv, z_far, cum, cum_s, log_s, f_blk, e_blk, rates, ones)
-            )
-        return uvs[-1]
-
+    route = [(2 * q + y, 2 * ((q + turns) % pairs) + y) for q in range(pairs) if sends(q) for y in (0, 1)]
+    return lax.ppermute(block, "seq", route)
+
+
+def log_steps(info, got, keep, rates, done, pairs, scan_next):
+    half = keep.shape[1]
     message = ((N + EXTRA, half), BF16)
     full = ((N, half), F32)
-    got = swap(send, "seq", 1)
-    done = scan_next(send)
     msg, own, first, aux = combine(
         pair_kernel,
         (info, got, keep, rates, done),
@@ -603,6 +687,90 @@
         specs.append(FULL)
     out = ((N, half), BF16)
     back, held = combine(kernel, operands + [first, aux, done], specs + [FULL, FULL, ANY], [out, out], "last")
+    return back, held
+
+
+def local(
+    x_input,
+    z_input,
+    bc_input,
+    conv_weight_x,
+    conv_weight_bc,
+    step_size,
+    log_decay,
+    skip_gain,
+    norm_gain,
+    out_weight,
+):
+    length, width = x_input.shape
+    heads = step_size.shape[1]
+    ways = lax.axis_size("head")
+    pairs = lax.axis_size("seq") // 2
+    mine = lax.axis_index("head")
+    half = width // 2
+    seq = lax.axis_index("seq")
+    info = jnp.stack([seq & 1, mine ^ 3, mine ^ 2, mine ^ 1, mine, seq >> 1]).astype(jnp.int32)
+
+    x_far, z_far, w_far = [pltpu.with_memory_space_constraint(v, pltpu.HBM) for v in (x_input, z_input, out_weight)]
+    bc = bc_input.reshape(length, -1)
+    halo = shift(jnp.concatenate([x_input[length - LEAD :], bc[length - LEAD :]], 1), 1)
+    weight_mate = swap(out_weight, "head", 1)
+
+    ones = jnp.asarray(np.tile(np.repeat(np.eye(heads), P_SIZE, axis=1), (2, 1)), BF16)
+    cum, cum_s, log_s, f_dev, f_blk, e_blk, rates = decays(log_decay, step_size, skip_gain, ones)
+    x_conv, bc_conv, keep, send = conv_states(
+        info, x_far, bc, halo, conv_weight_x, conv_weight_bc, f_dev, ones, rates
+    )
+
+    x_conv = pltpu.with_memory_space_constraint(x_conv, pltpu.HBM)
+    uvs = []
+
+    def scan_next(token):
+        if len(uvs) < B_PARTS:
+            uvs.append(
+                scan_part(len(uvs), token, x_conv, bc_conv, z_far, cum, cum_s, log_s, f_blk, e_blk, rates, ones)
+            )
+        return uvs[-1]
+
+    message = ((N + EXTRA, half), BF16)
+    full = ((N, half), F32)
+    got = swap(send, "seq", 1)
+    done = scan_next(send)
+    out = ((N, half), BF16)
+    if pairs > 1 and half % (pairs * N) == 0:
+        piece = half // pairs
+        part = ((N + EXTRA, piece), BF16)
+        first, aux, *parts = combine(
+            pair_split_kernel,
+            (info, got, keep, rates, done),
+            [SCALAR, FULL, FULL, FULL, ANY],
+            [full, ((8, half), F32)] + [part] * pairs,
+            "pair",
+            [pltpu.VMEM(*message)],
+        )
+        parts = list(parts[:1]) + [rotate(parts[r], r, lambda q: q < pairs - 1) for r in range(1, pairs)]
+        done = scan_next(parts[0])
+        parts = combine(
+            owner_kernel,
+            [info] + parts + [done],
+            [SCALAR] + [FULL] * pairs + [ANY],
+            [((N, piece), BF16)] * pairs,
+            "owner",
+            [pltpu.VMEM((pairs, N + EXTRA, piece), BF16), pltpu.VMEM((pairs, N, piece), BF16)],
+        )
+        ready = parts[0]
+        parts = list(parts[:1]) + [rotate(parts[r], r, lambda q: (q + r) % pairs > 0) for r in range(1, pairs)]
+        done = scan_next(ready)
+        back, held = combine(
+            last_split_kernel,
+            [info, first, aux, done] + parts,
+            [SCALAR, FULL, FULL, ANY] + [FULL] * pairs,
+            [out, out],
+            "last",
+            [pltpu.VMEM(*out)],
+        )
+    else:
+        back, held = log_steps(info, got, keep, rates, done, pairs, scan_next)
     other = swap(back, "seq", 1)
     while len(uvs) < B_PARTS:
         scan_next(back)
@@ -617,19 +785,22 @@
     far = rows_for(2, far_mate)
     far_mate = swap(far_mate, "head", 1)
     columns = out_weight.shape[1]
-    cuts = [columns * c // 16 for c in (0, 3, 6, 9, 12, 14, 16)]
-    arrivals = []
-    for lo, hi in zip(cuts[:-1], cuts[1:]):
-        sent = project(far, far_mate, w_far, weight_mate, lo, hi - lo, BF16)
-        arrivals.append(swap(sent, "head", 2))
-    near_mate = rows_for(3, far)
+    quarter = columns // 4
+    weights = (w_far, weight_mate)
+    sent = project(far, far_mate, *weights, 0, quarter, BF16)
+    arrivals = [swap(sent, "head", 2)]
+    near_mate = rows_for(3, sent)
     near = rows_for(4, near_mate)
     near_mate = swap(near_mate, "head", 1)
-    last = project(near, near_mate, w_far, weight_mate, cuts[-2], columns - cuts[-2], F32)
-    result = None
-    for arrived, lo, hi in zip(arrivals[:-1], cuts[:-2], cuts[1:-1]):
-        result = project(near, near_mate, w_far, weight_mate, lo, hi - lo, BF16, arrived, result)
-    return add_chunk(last, arrivals[-1], result, cuts[-2])
+    parts = []
+    for c in range(quarter, columns, quarter):
+        sent, part = project_both(far, far_mate, near, near_mate, *weights, c, quarter)
+        arrivals.append(swap(sent, "head", 2))
+        parts.append(part)
+    result = project(near, near_mate, *weights, 0, quarter, BF16, arrivals[0])
+    for c, part in enumerate(parts, 1):
+        result = add_chunk(part, arrivals[c], result, c * quarter)
+    return result
 
 
 def solution(mesh):

time: 127 us -> 133 us (1.047)
  the two profiles are of different devices: /device:TPU:26 before, /device:TPU:0 now
where the time goes in v5:
time: 133 us; the launch traced here: 132 us
  Pallas kernels  75.9 us (57%)
  starting transfers between devices  33.3 us (25%)
  waiting for transfers between devices  18.7 us (14%)
  local copies, waits for them, and re-layouts  3.15 us (2%)
    ppermute x6, starting transfers between devices, rotate(): return lax.ppermute(block, 'seq', route)  20.7 us
    pallas_call x3, Pallas kernels, project_both(): pl.pallas_call(functools.partial(project_both_kernel, first // TILE), gri...  20.5 us
    pallas_call x4, Pallas kernels, scan_part(): pl.pallas_call(functools.partial(scan_kernel, part), in_specs=[FAR, FAR]...  19 us
    ppermute x9, waiting for transfers between devices, swap(): lax.ppermute(block, axis, [(i, i ^ bit) for i in range(lax.axis_size(axis...  18.7 us
    pallas_call x1, Pallas kernels, conv_states(): pl.pallas_call(conv_kernel, grid=(length // TOK_A,), in_specs=[SCALAR, FA...  13.9 us
    pallas_call x2, Pallas kernels, project(): pl.pallas_call(functools.partial(project_kernel, base, full), grid=(count...  9.94 us
    ppermute x9, starting transfers between devices, swap(): lax.ppermute(block, axis, [(i, i ^ bit) for i in range(lax.axis_size(axis...  7.99 us
    pallas_call x4, Pallas kernels, norm_rows(): pl.pallas_call(functools.partial(norm_kernel, slot), in_specs=[SCALAR] +...  6.07 us
  transfers between devices with their start and end apart: 16, of which 5 were waited for; matrix products, arithmetic and copies ran while one was open for 3% of the time, Pallas kernels for 52%

profile of v5, /device:TPU:0, one launch (start us, length us, event | category | flops | bytes accessed | tf_op | source)
XLA Modules:
  0.0 132.0 jit_solution(12369810303600349020)
XLA Ops:
  2.8 4.6 %collective-permute-start = (bf16[16,2560]{1,0:T(8,128)(2,1)}, bf16[16,2560]{1,0:T(8,128)(2,1)S(1)}, u32[]{:S(2)}, u32[]{:S(2)}) collective-permute-start(bf16[16,2560]{1,0:T(8,128)(2,1)} %pad_maximum_fusion), channel_id=1, source_target_pairs={{0,4},{4,8},{8,12},{12,16},{16,20},{20,24},{24,28},{1,5},{5,9},{9,... | collective-permute-start | bytes 245768 | tf_op jit(solution)/shard_map/ppermute | solution.py:641
  8.9 1.5 %decays.1 = (f32[1024,32]{1,0:T(8,128)S(1)}, f32[32,1024]{1,0:T(8,128)S(1)}, f32[32,1024]{1,0:T(8,128)S(1)}, bf16[1024,64]{1,0:T(8,128)(2,1)S(1)}, bf16[1024,64]...) custom-call(f32[32,1024]{1,0:T(8,128)S(1)} %bitcast.15, f32[32,1024]{1,0:T(8,128)S(1)} %bitcast.16, ...), custom_call_target="tpu_custom_call" | custom-call | tf_op jit(solution)/shard_map/decays/pallas_call | solution.py:105
  10.5 13.9 %conv_states.1 = (bf16[1024,2048]{1,0:T(8,128)(2,1)}, bf16[1024,512]{1,0:T(8,128)(2,1)S(1)}, f32[128,1024]{1,0:T(8,128)S(1)}, bf16[144,1024]{1,0:T(8,128)(2,1)S(1)}) custom-call(s32[6]{0:T(128)S(1)} %stack.27.info, bf16[1024,2048]{1,0:T(8,128)(2,1)} %x_far.1, bf16[1024,512]{1,0:T(8,128)(2,1)S(1)} %bitcast.14, ...), custom_call_target="tpu_custom_call" | custom-call | flops 1 | bytes 1 | tf_op jit(solution)/shard_map/conv_states/pallas_call | solution.py:223
  24.4 1.8 %collective-permute-start.1 = (bf16[144,1024]{1,0:T(8,128)(2,1)S(1)}, bf16[144,1024]{1,0:T(8,128)(2,1)S(1)}, u32[]{:S(2)}, u32[]{:S(2)}) collective-permute-start(bf16[144,1024]{1,0:T(8,128)(2,1)S(1)} %get-tuple-element.37._), channel_id=1, source_target_pairs={{0,4},{4,0},{8,12},{12,8},{16,20},{20,16},{24,28},{28,24},{1,5},{5... | collective-permute-start | bytes 884744 | tf_op jit(solution)/shard_map/ppermute | solution.py:645
  26.2 4.7 %scan_part.4._.refs_0_ = bf16[1024,1024]{1,0:T(8,128)(2,1)S(1)} custom-call(bf16[1024,2048]{1,0:T(8,128)(2,1)} %get-tuple-element.39.x_far, bf16[1024,2048]{1,0:T(8,128)(2,1)} %z_far.7, bf16[1024,512]{1,0:T(8,128)(2,1)S(1)} %get-tuple-element.36.bc_all.bc, f32[1024,32]{1,0:T(8,128)S(1)} %get-tuple-element.40.cum, f32[32,1024]{1,0:T(8,128)S(1)} %get-tuple-element.41.cum_s, ...), custom_call_target="tpu_custom_call" | custom-call | flops 1 | bytes 1 | tf_op jit(solution)/shard_map/scan_part/pallas_call | solution.py:433
  31.0 2.5 %collective-permute-done.1.got = bf16[144,1024]{1,0:T(8,128)(2,1)S(1)} collective-permute-done((bf16[144,1024]{1,0:T(8,128)(2,1)S(1)}, bf16[144,1024]{1,0:T(8,128)(2,1)S(1)}, u32[]{:S(2)}, u32[]{:S(2)}) %collective-permute-start.1) | collective-permute-done | bytes 294944 | tf_op jit(solution)/shard_map/ppermute | solution.py:645
  34.3 4.1 %collective-permute-start.2 = (bf16[144,256]{1,0:T(8,128)(2,1)S(1)}, bf16[144,256]{1,0:T(8,128)(2,1)S(1)}, u32[]{:S(2)}, u32[]{:S(2)}) collective-permute-start(bf16[144,256]{1,0:T(8,128)(2,1)S(1)} %get-tuple-element.48), channel_id=1, source_target_pairs={{0,8},{4,12},{8,16},{12,20},{16,24},{20,28},{1,9},{5,13},{9,17},{1... | collective-permute-start | bytes 221192 | tf_op jit(solution)/shard_map/ppermute | solution.py:651
  38.4 4.5 %collective-permute-start.3 = (bf16[144,256]{1,0:T(8,128)(2,1)S(1)}, bf16[144,256]{1,0:T(8,128)(2,1)S(1)}, u32[]{:S(2)}, u32[]{:S(2)}) collective-permute-start(bf16[144,256]{1,0:T(8,128)(2,1)S(1)} %get-tuple-element.49), channel_id=1, source_target_pairs={{0,16},{4,20},{8,24},{12,28},{16,0},{20,4},{1,17},{5,21},{9,25},{1... | collective-permute-start | bytes 221192 | tf_op jit(solution)/shard_map/ppermute | solution.py:651
  42.9 1.9 %collective-permute-start.4 = (bf16[144,256]{1,0:T(8,128)(2,1)S(1)}, bf16[144,256]{1,0:T(8,128)(2,1)S(1)}, u32[]{:S(2)}, u32[]{:S(2)}) collective-permute-start(bf16[144,256]{1,0:T(8,128)(2,1)S(1)} %get-tuple-element.50), channel_id=1, source_target_pairs={{0,24},{4,28},{8,0},{12,4},{16,8},{20,12},{1,25},{5,29},{9,1},{13,... | collective-permute-start | bytes 221192 | tf_op jit(solution)/shard_map/ppermute | solution.py:651
  44.8 4.8 %scan_part.5.refs_4_.refs_1_ = bf16[1024,1024]{1,0:T(8,128)(2,1)S(1)} custom-call(bf16[1024,2048]{1,0:T(8,128)(2,1)} %get-tuple-element.39.x_far, bf16[1024,2048]{1,0:T(8,128)(2,1)} %z_far.7, bf16[1024,512]{1,0:T(8,128)(2,1)S(1)} %get-tuple-element.36.bc_all.bc, f32[1024,32]{1,0:T(8,128)S(1)} %get-tuple-element.40.cum, ...), custom_call_target="tpu_custom_call" | custom-call | flops 1 | bytes 1 | tf_op jit(solution)/shard_map/scan_part/pallas_call | solution.py:433
  50.3 3.9 %collective-permute-start.5 = (bf16[128,256]{1,0:T(8,128)(2,1)S(1)}, bf16[128,256]{1,0:T(8,128)(2,1)S(1)}, u32[]{:S(2)}, u32[]{:S(2)}) collective-permute-start(bf16[128,256]{1,0:T(8,128)(2,1)S(1)} %get-tuple-element.52), channel_id=1, source_target_pairs={{0,8},{4,12},{8,16},{12,20},{16,24},{20,28},{1,9},{5,13},{9,17},{1... | collective-permute-start | bytes 196616 | tf_op jit(solution)/shard_map/ppermute | solution.py:651
  54.2 1.8 %collective-permute-start.6 = (bf16[128,256]{1,0:T(8,128)(2,1)S(1)}, bf16[128,256]{1,0:T(8,128)(2,1)S(1)}, u32[]{:S(2)}, u32[]{:S(2)}) collective-permute-start(bf16[128,256]{1,0:T(8,128)(2,1)S(1)} %get-tuple-element.53), channel_id=1, source_target_pairs={{0,16},{4,20},{8,24},{12,28},{24,8},{28,12},{1,17},{5,21},{9,25},{... | collective-permute-start | bytes 196616 | tf_op jit(solution)/shard_map/ppermute | solution.py:651
  56.0 4.6 %collective-permute-start.7 = (bf16[128,256]{1,0:T(8,128)(2,1)S(1)}, bf16[128,256]{1,0:T(8,128)(2,1)S(1)}, u32[]{:S(2)}, u32[]{:S(2)}) collective-permute-start(bf16[128,256]{1,0:T(8,128)(2,1)S(1)} %get-tuple-element.54), channel_id=1, source_target_pairs={{0,24},{4,28},{16,8},{20,12},{24,16},{28,20},{1,25},{5,29},{17,9},... | collective-permute-start | bytes 196616 | tf_op jit(solution)/shard_map/ppermute | solution.py:651
  60.6 4.8 %scan_part.6._.refs_2_ = bf16[1024,1024]{1,0:T(8,128)(2,1)S(1)} custom-call(bf16[1024,2048]{1,0:T(8,128)(2,1)} %get-tuple-element.39.x_far, bf16[1024,2048]{1,0:T(8,128)(2,1)} %z_far.7, bf16[1024,512]{1,0:T(8,128)(2,1)S(1)} %get-tuple-element.36.bc_all.bc, f32[1024,32]{1,0:T(8,128)S(1)} %get-tuple-element.40.cum, f32[32,1024]{1,0:T(8,128)S(1)} %get-tuple-element.41.cum_s, ...), custom_call_target="tpu_custom_call" | custom-call | flops 1 | bytes 1 | tf_op jit(solution)/shard_map/scan_part/pallas_call | solution.py:433
  66.9 4.7 %scan_part.7.refs_3_ = bf16[1024,1024]{1,0:T(8,128)(2,1)S(1)} custom-call(bf16[1024,2048]{1,0:T(8,128)(2,1)} %get-tuple-element.39.x_far, bf16[1024,2048]{1,0:T(8,128)(2,1)} %z_far.7, bf16[1024,512]{1,0:T(8,128)(2,1)S(1)} %get-tuple-element.36.bc_all.bc, f32[1024,32]{1,0:T(8,128)S(1)} %get-tuple-element.40.cum, f32[32,1024]{1,0:T(8,128)S(1)} %get-tuple-element.41.cum_s, ...), custom_call_target="tpu_custom_call" | custom-call | flops 1 | bytes 1 | tf_op jit(solution)/shard_map/scan_part/pallas_call | solution.py:433
  76.9 4.6 %project.2._ = bf16[256,1024]{1,0:T(8,128)(2,1)S(1)} custom-call(bf16[256,2048]{1,0:T(8,128)(2,1)S(1)} %norm_rows.5.a0.a0_far, bf16[256,2048]{1,0:T(8,128)(2,1)S(1)} %collective-permute-done.9.a1.a1_far, bf16[2048,4096]{1,0:T(8,128)(2,1)} %w0_far.9, bf16[2048,4096]{1,0:T(8,128)(2,1)} %collective-permute-done.10.w1_far), custom_call_target="tpu_custom_call" | custom-call | flops 1 | bytes 1 | tf_op jit(solution)/shard_map/project/pallas_call | solution.py:542
  81.5 1.5 %norm_rows.6._ = bf16[256,2048]{1,0:T(8,128)(2,1)S(1)} custom-call(s32[6]{0:T(128)S(1)} %stack.27.info, bf16[1024,512]{1,0:T(8,128)(2,1)S(1)} %get-tuple-element.36.bc_all.bc, bf16[128,1024]{1,0:T(8,128)(2,1)S(1)} %get-tuple-element.55.keep._, bf16[128,1024]{1,0:T(8,128)(2,1)S(1)} %collective-permute-done.8.recv, f32[1,2048]{1,0:T(1,128)S(1)} %bitcast.19, ...), custom_call_target="tpu_custom_call" | custom-call | flops 1 | bytes 1 | tf_op jit(solution)/shard_map/norm_rows/pallas_call | solution.py:486
  83.2 1.5 %collective-permute-start.15 = (bf16[256,1024]{1,0:T(8,128)(2,1)S(1)}, bf16[256,1024]{1,0:T(8,128)(2,1)S(1)}, u32[]{:S(2)}, u32[]{:S(2)}) collective-permute-start(bf16[256,1024]{1,0:T(8,128)(2,1)S(1)} %project.2._), channel_id=1, source_target_pairs={{0,2},{1,3},{2,0},{3,1},{4,6},{5,7},{6,4},{7,5},{8,10},{9,11},{10,... | collective-permute-start | bytes 1572872 | tf_op jit(solution)/shard_map/ppermute | solution.py:645
  86.3 6.9 %project_both.5 = (bf16[256,1024]{1,0:T(8,128)(2,1)S(1)}, f32[256,1024]{1,0:T(8,128)S(1)}) custom-call(bf16[256,2048]{1,0:T(8,128)(2,1)S(1)} %norm_rows.5.a0.a0_far, bf16[256,2048]{1,0:T(8,128)(2,1)S(1)} %collective-permute-done.9.a1.a1_far, bf16[256,2048]{1,0:T(8,128)(2,1)S(1)} %norm_rows.7.a0_near.a0, ...), custom_call_target="tpu_custom_call" | custom-call | flops 1 | bytes 1 | tf_op jit(solution)/shard_map/project_both/pallas_call | solution.py:600
  94.2 6.8 %project_both.4 = (bf16[256,1024]{1,0:T(8,128)(2,1)S(1)}, f32[256,1024]{1,0:T(8,128)S(1)}) custom-call(bf16[256,2048]{1,0:T(8,128)(2,1)S(1)} %norm_rows.5.a0.a0_far, bf16[256,2048]{1,0:T(8,128)(2,1)S(1)} %collective-permute-done.9.a1.a1_far, bf16[256,2048]{1,0:T(8,128)(2,1)S(1)} %norm_rows.7.a0_near.a0, ...), custom_call_target="tpu_custom_call" | custom-call | flops 1 | bytes 1 | tf_op jit(solution)/shard_map/project_both/pallas_call | solution.py:600
  102.1 6.8 %project_both.3 = (bf16[256,1024]{1,0:T(8,128)(2,1)S(1)}, f32[256,1024]{1,0:T(8,128)S(1)}) custom-call(bf16[256,2048]{1,0:T(8,128)(2,1)S(1)} %norm_rows.5.a0.a0_far, bf16[256,2048]{1,0:T(8,128)(2,1)S(1)} %collective-permute-done.9.a1.a1_far, bf16[256,2048]{1,0:T(8,128)(2,1)S(1)} %norm_rows.7.a0_near.a0, ...), custom_call_target="tpu_custom_call" | custom-call | flops 1 | bytes 1 | tf_op jit(solution)/shard_map/project_both/pallas_call | solution.py:600
  110.0 5.3 %project.3._ = bf16[256,4096]{1,0:T(8,128)(2,1)} custom-call(bf16[256,2048]{1,0:T(8,128)(2,1)S(1)} %norm_rows.7.a0_near.a0, bf16[256,2048]{1,0:T(8,128)(2,1)S(1)} %collective-permute-done.11.a1_near.a1, bf16[2048,4096]{1,0:T(8,128)(2,1)} %w0_far.9, bf16[2048,4096]{1,0:T(8,128)(2,1)} %collective-permute-done.10.w1_far, ...), custom_call_target="tpu_custom_call" | custom-call | flops 1 | bytes 1 | tf_op jit(solution)/shard_map/project/pallas_call | solution.py:542
  116.2 4.2 %collective-permute-done.13.arrived = bf16[256,1024]{1,0:T(8,128)(2,1)S(1)} collective-permute-done((bf16[256,1024]{1,0:T(8,128)(2,1)S(1)}, bf16[256,1024]{1,0:T(8,128)(2,1)S(1)}, u32[]{:S(2)}, u32[]{:S(2)}) %collective-permute-start.13) | collective-permute-done | bytes 524320 | tf_op jit(solution)/shard_map/ppermute | solution.py:645
  121.3 9.8 %collective-permute-done.12.arrived = bf16[256,1024]{1,0:T(8,128)(2,1)S(1)} collective-permute-done((bf16[256,1024]{1,0:T(8,128)(2,1)S(1)}, bf16[256,1024]{1,0:T(8,128)(2,1)S(1)}, u32[]{:S(2)}, u32[]{:S(2)}) %collective-permute-start.12) | collective-permute-done | bytes 524320 | tf_op jit(solution)/shard_map/ppermute | solution.py:645
  (49 shorter events, 20.1 us)
Async XLA Ops:
  0.0 8.8 %copy-start = (bf16[64,2048]{1,0:T(8,128)(2,1)S(1)}, bf16[64,2048]{1,0:T(8,128)(2,1)}, u32[]{:S(2)}) copy-start(bf16[64,2048]{1,0:T(8,128)(2,1)} %constant.17.clone.ones) | copy-start | bytes 786436
  0.0 8.8 %copy-start.6 = (f32[32]{0:T(128)S(1)}, f32[32]{0:T(128)}, u32[]{:S(2)}) copy-start(f32[32]{0:T(128)} %param.18) | copy-start | bytes 388
  0.0 8.9 %copy-start.1 = (f32[1024,32]{0,1:T(8,128)S(1)}, f32[1024,32]{0,1:T(8,128)}, u32[]{:S(2)}) copy-start(f32[1024,32]{0,1:T(8,128)} %param.17) | copy-start | bytes 393220
  0.0 8.9 %copy-start.2 = (f32[1024,32]{0,1:T(8,128)S(1)}, f32[1024,32]{0,1:T(8,128)}, u32[]{:S(2)}) copy-start(f32[1024,32]{0,1:T(8,128)} %param.16) | copy-start | bytes 393220
  0.0 10.5 %copy-start.5 = (f32[4,2,256]{2,1,0:T(2,128)S(1)}, f32[4,2,256]{2,1,0:T(2,128)}, u32[]{:S(2)}) copy-start(f32[4,2,256]{2,1,0:T(2,128)} %wbc.1) | copy-start | bytes 24580
  0.0 10.5 %copy-start.4 = (f32[4,2048]{1,0:T(4,128)S(1)}, f32[4,2048]{1,0:T(4,128)}, u32[]{:S(2)}) copy-start(f32[4,2048]{1,0:T(4,128)} %wx.1) | copy-start | bytes 98308
  0.0 76.9 %collective-permute-start.10 = (bf16[2048,4096]{1,0:T(8,128)(2,1)}, bf16[2048,4096]{1,0:T(8,128)(2,1)}, u32[]{:S(2)}, u32[]{:S(2)}) collective-permute-start(bf16[2048,4096]{1,0:T(8,128)(2,1)} %w0_far.9), channel_id=1, source_target_pairs={{0,1},{1,0},{2,3},{3,2},{4,5},{5,4},{6,7},{7,6},{8,9},{9,8},{10,11... | collective-permute-start | bytes 50331656 | tf_op jit(solution)/shard_map/ppermute | solution.py:645
  2.8 7.7 %collective-permute-start = (bf16[16,2560]{1,0:T(8,128)(2,1)}, bf16[16,2560]{1,0:T(8,128)(2,1)S(1)}, u32[]{:S(2)}, u32[]{:S(2)}) collective-permute-start(bf16[16,2560]{1,0:T(8,128)(2,1)} %pad_maximum_fusion), channel_id=1, source_target_pairs={{0,4},{4,8},{8,12},{12,16},{16,20},{20,24},{24,28},{1,5},{5,9},{9,... | collective-permute-start | bytes 245768 | tf_op jit(solution)/shard_map/ppermute | solution.py:641
  24.4 9.1 %collective-permute-start.1 = (bf16[144,1024]{1,0:T(8,128)(2,1)S(1)}, bf16[144,1024]{1,0:T(8,128)(2,1)S(1)}, u32[]{:S(2)}, u32[]{:S(2)}) collective-permute-start(bf16[144,1024]{1,0:T(8,128)(2,1)S(1)} %get-tuple-element.37._), channel_id=1, source_target_pairs={{0,4},{4,0},{8,12},{12,8},{16,20},{20,16},{24,28},{28,24},{1,5},{5... | collective-permute-start | bytes 884744 | tf_op jit(solution)/shard_map/ppermute | solution.py:645
  34.3 15.2 %collective-permute-start.2 = (bf16[144,256]{1,0:T(8,128)(2,1)S(1)}, bf16[144,256]{1,0:T(8,128)(2,1)S(1)}, u32[]{:S(2)}, u32[]{:S(2)}) collective-permute-start(bf16[144,256]{1,0:T(8,128)(2,1)S(1)} %get-tuple-element.48), channel_id=1, source_target_pairs={{0,8},{4,12},{8,16},{12,20},{16,24},{20,28},{1,9},{5,13},{9,17},{1... | collective-permute-start | bytes 221192 | tf_op jit(solution)/shard_map/ppermute | solution.py:651
  38.4 11.2 %collective-permute-start.3 = (bf16[144,256]{1,0:T(8,128)(2,1)S(1)}, bf16[144,256]{1,0:T(8,128)(2,1)S(1)}, u32[]{:S(2)}, u32[]{:S(2)}) collective-permute-start(bf16[144,256]{1,0:T(8,128)(2,1)S(1)} %get-tuple-element.49), channel_id=1, source_target_pairs={{0,16},{4,20},{8,24},{12,28},{16,0},{20,4},{1,17},{5,21},{9,25},{1... | collective-permute-start | bytes 221192 | tf_op jit(solution)/shard_map/ppermute | solution.py:651
  42.9 6.7 %collective-permute-start.4 = (bf16[144,256]{1,0:T(8,128)(2,1)S(1)}, bf16[144,256]{1,0:T(8,128)(2,1)S(1)}, u32[]{:S(2)}, u32[]{:S(2)}) collective-permute-start(bf16[144,256]{1,0:T(8,128)(2,1)S(1)} %get-tuple-element.50), channel_id=1, source_target_pairs={{0,24},{4,28},{8,0},{12,4},{16,8},{20,12},{1,25},{5,29},{9,1},{13,... | collective-permute-start | bytes 221192 | tf_op jit(solution)/shard_map/ppermute | solution.py:651
  50.3 15.1 %collective-permute-start.5 = (bf16[128,256]{1,0:T(8,128)(2,1)S(1)}, bf16[128,256]{1,0:T(8,128)(2,1)S(1)}, u32[]{:S(2)}, u32[]{:S(2)}) collective-permute-start(bf16[128,256]{1,0:T(8,128)(2,1)S(1)} %get-tuple-element.52), channel_id=1, source_target_pairs={{0,8},{4,12},{8,16},{12,20},{16,24},{20,28},{1,9},{5,13},{9,17},{1... | collective-permute-start | bytes 196616 | tf_op jit(solution)/shard_map/ppermute | solution.py:651
  54.2 11.2 %collective-permute-start.6 = (bf16[128,256]{1,0:T(8,128)(2,1)S(1)}, bf16[128,256]{1,0:T(8,128)(2,1)S(1)}, u32[]{:S(2)}, u32[]{:S(2)}) collective-permute-start(bf16[128,256]{1,0:T(8,128)(2,1)S(1)} %get-tuple-element.53), channel_id=1, source_target_pairs={{0,16},{4,20},{8,24},{12,28},{24,8},{28,12},{1,17},{5,21},{9,25},{... | collective-permute-start | bytes 196616 | tf_op jit(solution)/shard_map/ppermute | solution.py:651
  56.0 9.4 %collective-permute-start.7 = (bf16[128,256]{1,0:T(8,128)(2,1)S(1)}, bf16[128,256]{1,0:T(8,128)(2,1)S(1)}, u32[]{:S(2)}, u32[]{:S(2)}) collective-permute-start(bf16[128,256]{1,0:T(8,128)(2,1)S(1)} %get-tuple-element.54), channel_id=1, source_target_pairs={{0,24},{4,28},{16,8},{20,12},{24,16},{28,20},{1,25},{5,29},{17,9},... | collective-permute-start | bytes 196616 | tf_op jit(solution)/shard_map/ppermute | solution.py:651
  66.2 6.5 %copy-start.3 = (f32[2048]{0:T(1024)S(1)}, f32[2048]{0:T(1024)}, u32[]{:S(2)}) copy-start(f32[2048]{0:T(1024)} %param.19) | copy-start | bytes 24580
  66.2 6.4 %collective-permute-start.8 = (bf16[128,1024]{1,0:T(8,128)(2,1)S(1)}, bf16[128,1024]{1,0:T(8,128)(2,1)S(1)}, u32[]{:S(2)}, u32[]{:S(2)}) collective-permute-start(bf16[128,1024]{1,0:T(8,128)(2,1)S(1)} %get-tuple-element.56._), channel_id=1, source_target_pairs={{0,4},{4,0},{8,12},{12,8},{16,20},{20,16},{24,28},{28,24},{1,5},{5... | collective-permute-start | bytes 786440 | tf_op jit(solution)/shard_map/ppermute | solution.py:645
  74.2 2.7 %collective-permute-start.9 = (bf16[256,2048]{1,0:T(8,128)(2,1)S(1)}, bf16[256,2048]{1,0:T(8,128)(2,1)S(1)}, u32[]{:S(2)}, u32[]{:S(2)}) collective-permute-start(bf16[256,2048]{1,0:T(8,128)(2,1)S(1)} %norm_rows.4._), channel_id=1, source_target_pairs={{0,1},{1,0},{2,3},{3,2},{4,5},{5,4},{6,7},{7,6},{8,9},{9,8},{10,11... | collective-permute-start | bytes 3145736 | tf_op jit(solution)/shard_map/ppermute | solution.py:645
  83.0 3.2 %collective-permute-start.11 = (bf16[256,2048]{1,0:T(8,128)(2,1)S(1)}, bf16[256,2048]{1,0:T(8,128)(2,1)S(1)}, u32[]{:S(2)}, u32[]{:S(2)}) collective-permute-start(bf16[256,2048]{1,0:T(8,128)(2,1)S(1)} %norm_rows.6._), channel_id=1, source_target_pairs={{0,1},{1,0},{2,3},{3,2},{4,5},{5,4},{6,7},{7,6},{8,9},{9,8},{10,11... | collective-permute-start | bytes 3145736 | tf_op jit(solution)/shard_map/ppermute | solution.py:645
  83.2 26.8 %collective-permute-start.15 = (bf16[256,1024]{1,0:T(8,128)(2,1)S(1)}, bf16[256,1024]{1,0:T(8,128)(2,1)S(1)}, u32[]{:S(2)}, u32[]{:S(2)}) collective-permute-start(bf16[256,1024]{1,0:T(8,128)(2,1)S(1)} %project.2._), channel_id=1, source_target_pairs={{0,2},{1,3},{2,0},{3,1},{4,6},{5,7},{6,4},{7,5},{8,10},{9,11},{10,... | collective-permute-start | bytes 1572872 | tf_op jit(solution)/shard_map/ppermute | solution.py:645
  93.1 22.2 %collective-permute-start.14 = (bf16[256,1024]{1,0:T(8,128)(2,1)S(1)}, bf16[256,1024]{1,0:T(8,128)(2,1)S(1)}, u32[]{:S(2)}, u32[]{:S(2)}) collective-permute-start(bf16[256,1024]{1,0:T(8,128)(2,1)S(1)} %get-tuple-element.62), channel_id=1, source_target_pairs={{0,2},{1,3},{2,0},{3,1},{4,6},{5,7},{6,4},{7,5},{8,10},{9,11},{10,... | collective-permute-start | bytes 1572872 | tf_op jit(solution)/shard_map/ppermute | solution.py:645
  101.0 19.5 %collective-permute-start.13 = (bf16[256,1024]{1,0:T(8,128)(2,1)S(1)}, bf16[256,1024]{1,0:T(8,128)(2,1)S(1)}, u32[]{:S(2)}, u32[]{:S(2)}) collective-permute-start(bf16[256,1024]{1,0:T(8,128)(2,1)S(1)} %get-tuple-element.60), channel_id=1, source_target_pairs={{0,2},{1,3},{2,0},{3,1},{4,6},{5,7},{6,4},{7,5},{8,10},{9,11},{10,... | collective-permute-start | bytes 1572872 | tf_op jit(solution)/shard_map/ppermute | solution.py:645
  109.0 22.2 %collective-permute-start.12 = (bf16[256,1024]{1,0:T(8,128)(2,1)S(1)}, bf16[256,1024]{1,0:T(8,128)(2,1)S(1)}, u32[]{:S(2)}, u32[]{:S(2)}) collective-permute-start(bf16[256,1024]{1,0:T(8,128)(2,1)S(1)} %get-tuple-element.58), channel_id=1, source_target_pairs={{0,2},{1,3},{2,0},{3,1},{4,6},{5,7},{6,4},{7,5},{8,10},{9,11},{10,... | collective-permute-start | bytes 1572872 | tf_op jit(solution)/shard_map/ppermute | solution.py:645

commit v6 on v4

--- a/solution.py
+++ b/solution.py
@@ -131,13 +131,12 @@
     return ref[0:N, :].astype(F32), extra[0:1] + extra[1:2]
 
 
-def conv_kernel(info, x_far, bc, halo, wx, wbc, f_dev, ones, rates, x_out, bc_out, keep, send, x, sem, xf, state):
+def conv_kernel(info, x_far, bc, halo, wx, wbc, f_dev, ones, rates, x_out, bc_out, send, x, sem, xf, state):
     i = pl.program_id(0)
     rows, width = x_out.shape
     bc_width = bc.shape[1]
     groups = bc_width // (2 * N)
     per = width // groups
-    half = width // 2
 
     def fetch(step):
         piece = pl.ds(pl.multiple_of(step * rows, rows), rows)
@@ -145,11 +144,9 @@
 
     @pl.when(i == 0)
     def _():
-        for step in range(x.shape[0] // rows):
-            fetch(step).start()
+        fetch(0).start()
         state[...] = jnp.zeros_like(state)
 
-    fetch(i).wait()
     base = pl.multiple_of(i * rows, rows)
     before = pl.ds(pl.multiple_of(jnp.maximum(base - LEAD, 0), LEAD), LEAD)
 
@@ -170,6 +167,11 @@
             last_x, last_p = cur[ROWS_A - 8 :], p[ROWS_A - 8 :]
 
     start = i == 0
+
+    def halo_of(lanes):
+        value = halo[:, lanes]
+        return jnp.where(info[0] == 0, jnp.zeros_like(value), value)
+
     for c in range(groups):
         for lanes in range(c * 2 * N, (c + 1) * 2 * N, N):
             ds = slice(lanes, lanes + N)
@@ -177,20 +179,27 @@
             def emit_bc(r, value):
                 bc_out[r : r + ROWS_A, ds] = value.astype(BF16)
 
-            lead = jnp.where(start, halo[:, width + lanes : width + lanes + N], bc[before, ds]).astype(F32)
+            lead = jnp.where(start, halo_of(slice(width + lanes, width + lanes + N)), bc[before, ds]).astype(F32)
             inner = slice(lanes - c * 2 * N, lanes - c * 2 * N + N)
             conv(lambda r: bc[at(r), ds], lead, [wbc[k, c : c + 1, inner] for k in range(KCONV)], emit_bc)
 
+    fetch(i).wait()
+
+    @pl.when(i + 1 < pl.num_programs(0))
+    def _():
+        fetch(i + 1).start()
+
     def slab(c, _):
-        ds = pl.ds(pl.multiple_of(c * SLAB, SLAB), SLAB)
-        scale = dot(f_dev[pl.ds(base, rows), :], ones[:, ds])
+        first = pl.multiple_of(c * SLAB, SLAB)
+        scale = dot(f_dev[pl.ds(base, rows), :], ones[:, pl.ds(first, SLAB)])
+        ds = pl.ds(first, SLAB)
 
         def emit(r, value):
             value = value.astype(BF16)
             x_out[r : r + ROWS_A, ds] = value
             xf[r : r + ROWS_A, ds] = (value.astype(F32) * scale[r : r + ROWS_A]).astype(BF16)
 
-        lead = jnp.where(start, halo[:, ds], x[before, ds]).astype(F32)
+        lead = jnp.where(start, halo_of(ds), x[before, ds]).astype(F32)
         conv(lambda r: x[at(r), ds], lead, [wx[k : k + 1, ds] for k in range(KCONV)], emit)
         return 0
 
@@ -202,18 +211,17 @@
 
     @pl.when(i == pl.num_programs(0) - 1)
     def _():
-        is_odd = info[0] == 1
-        low, high = state[:, 0:half], state[:, half:]
-        keep[...] = jnp.where(is_odd, high, low)
         row = rates.shape[0] - 16
-        decay = jnp.where(is_odd, rates[row : row + 1, 0:half], rates[row : row + 1, half:])
-        put_message(send, jnp.where(is_odd, low, high), decay)
-
-
-def conv_states(info, x, bc, halo, wx, wbc, f_dev, ones, rates):
+        piece = send.shape[2]
+        for owner in range(send.shape[0]):
+            lanes = slice(owner * piece, (owner + 1) * piece)
+            put_message(send.at[owner], state[:, lanes], rates[row : row + 1, lanes])
+
+
+def conv_states(owners, info, x, bc, halo, wx, wbc, f_dev, ones, rates):
     length, width = x.shape
     bc_width = bc.shape[1]
-    half = width // 2
+    sent = (owners, N + EXTRA, width // owners)
     return pl.pallas_call(
         conv_kernel,
         grid=(length // TOK_A,),
@@ -221,8 +229,7 @@
         out_specs=[
             pl.BlockSpec((TOK_A, width), lambda i: (i, 0)),
             pl.BlockSpec((TOK_A, bc_width), lambda i: (i, 0)),
-            whole((N, half)),
-            whole((N + EXTRA, half)),
+            whole(sent),
         ],
         scratch_shapes=[
             pltpu.VMEM((length, width), BF16),
@@ -233,8 +240,7 @@
         out_shape=(
             pltpu.HBM((length, width), BF16),
             jax.ShapeDtypeStruct((length, bc_width), BF16),
-            jax.ShapeDtypeStruct((N, half), F32),
-            jax.ShapeDtypeStruct((N + EXTRA, half), BF16),
+            jax.ShapeDtypeStruct(sent, BF16),
         ),
         compiler_params=params(20),
         cost_estimate=CHEAP,
@@ -242,55 +248,25 @@
     )(info, x, bc, halo, wx, wbc, f_dev, ones, rates)
 
 
-def pair_kernel(info, got, keep, rates, _, msg, own, first, aux):
-    half = keep.shape[1]
-    is_odd = info[0] == 1
-    arrived, their = take_message(got)
-    row = rates.shape[0] - 16
-    mine = jnp.where(is_odd, rates[row : row + 1, half:], rates[row : row + 1, 0:half])
-    early = jnp.where(is_odd, arrived, keep[...])
-    late = jnp.where(is_odd, keep[...], arrived)
-    even_decay = jnp.where(is_odd, their, mine)
-    odd_decay = jnp.where(is_odd, mine, their)
-    state = odd_decay * early + late
-    own[...] = state
-    first[...] = early
-    aux[0:8, :] = jnp.broadcast_to(even_decay, (8, half))
-    aux[8:16, :] = jnp.broadcast_to(even_decay * odd_decay, (8, half))
-    put_message(msg, state, even_decay * odd_decay)
-
-
-def wave_kernel(got, own, aux, behind_in, _, msg, behind):
-    before, decay = take_message(got)
-    if behind_in is not None:
-        before_decay = behind_in[N : N + 1, :]
-        before = behind_in[0:N, :] + before_decay * before
-        decay = before_decay * decay
-    pair_decay = aux[8:9, :]
-    behind[0:N, :] = before
-    behind[N:, :] = jnp.broadcast_to(decay, (8, before.shape[1]))
-    put_message(msg, own[...] + pair_decay * before, pair_decay * decay)
-
-
-def last_kernel(info, got, behind_in, first, aux, _, back, held):
-    is_odd = info[0] == 1
-    before, _unused = take_message(got)
-    if behind_in is not None:
-        before = behind_in[0:N, :] + behind_in[N : N + 1, :] * before
-    entering_odd = aux[0:1, :] * before + first[...]
-    back[...] = jnp.where(is_odd, before, entering_odd).astype(BF16)
-    held[...] = jnp.where(is_odd, entering_odd, before).astype(BF16)
-
-
-def combine(kernel, operands, specs, outs, name):
-    return pl.pallas_call(
-        kernel,
-        in_specs=specs,
-        out_specs=[FULL] * len(outs),
-        out_shape=[jax.ShapeDtypeStruct(s, t) for s, t in outs],
+def prefix_kernel(states, _, prefixes):
+    before = jnp.zeros(prefixes.shape[1:], F32)
+    for device in range(states.shape[0]):
+        prefixes[device] = before.astype(BF16)
+        state, decay = take_message(states.at[device])
+        before = decay * before + state
+
+
+def prefix(states, token):
+    devices, rows, piece = states.shape
+    return pl.pallas_call(
+        prefix_kernel,
+        in_specs=[FULL, ANY],
+        out_specs=FULL,
+        out_shape=jax.ShapeDtypeStruct((devices, rows - EXTRA, piece), BF16),
         compiler_params=params(16),
-        name=name,
-    )(*operands)
+        cost_estimate=CHEAP,
+        name="prefix",
+    )(states, token)
 
 
 def scan_kernel(part, x_far, z_far, bc_all, cum, cum_s, log_s, f_blk, e_blk, rates, ones, _, uv_out, x, z, sem, state):
@@ -323,12 +299,14 @@
     first = lax.broadcasted_iota(jnp.int32, (TOK_B, 2 * P_SIZE), 1) < P_SIZE
     zero = jnp.zeros((TOK_B, 2 * P_SIZE), BF16)
 
-    def block(b, _):
-        @pl.when(lax.rem(b, inner) == 0)
-        def _():
-            for copy in fetch(lax.div(b, inner)):
-                copy.wait()
-
+    def turn(step, _):
+        for copy in fetch(step):
+            copy.wait()
+        for k in range(inner):
+            block(step * inner + k)
+        return 0
+
+    def block(b):
         at = pl.ds(pl.multiple_of(b * TOK_B, TOK_B), TOK_B)
         b_mat = bc_all[at, b_lanes]
         c_mat = bc_all[at, c_lanes]
@@ -362,9 +340,8 @@
             uv_out[at, width + s * SLAB : width + (s + 1) * SLAB] = (gate * rise * lead_rows[:, lanes]).astype(BF16)
             xf = (xs * dot(f_blk[at, :], sel)).astype(BF16)
             state[:, lanes] = old * fade_rows[:, lanes] + dot(b_mat, xf, ((0,), (0,)))
-        return 0
-
-    lax.fori_loop(0, blocks, block, 0)
+
+    lax.fori_loop(0, length // STEP_B, turn, 0)
 
 
 def scan_part(part, token, x, bc, z, cum, cum_s, log_s, f_blk, e_blk, rates, ones):
@@ -387,14 +364,13 @@
     )(x, z, bc, cum, cum_s, log_s, f_blk, e_blk, rates, ones, token)
 
 
-def norm_kernel(slot, info, bc, keep, recv, gain, _, *refs):
+def norm_kernel(slot, info, bc, entering, gain, _, *refs):
     uvs, out = refs[:-1], refs[-1]
     count, width = out.shape
     groups = bc.shape[1] // (2 * N)
     per = width // groups
-    half = width // 2
     part = width // B_PARTS
-    is_odd = info[0] == 1
+    piece = entering.shape[2]
     base = info[slot] * count
 
     def rows(j, _):
@@ -406,10 +382,7 @@
             squares = None
             for p in range(g * per // part, (g + 1) * per // part):
                 start = p * part
-                side = start // half
-                lanes = slice(start - side * half, start - side * half + part)
-                mine, other = keep[:, lanes], recv[:, lanes]
-                inc = jnp.where(is_odd, other, mine) if side == 0 else jnp.where(is_odd, mine, other)
+                inc = jnp.concatenate([entering[k] for k in range(start // piece, (start + part) // piece)], 1)
                 gated = uvs[p][at, 0:part].astype(F32) + uvs[p][at, part:].astype(F32) * dot(c_mat, inc)
                 square = jnp.sum(gated * gated, axis=-1, keepdims=True)
                 squares = square if squares is None else squares + square
@@ -422,16 +395,16 @@
     lax.fori_loop(0, count // ROWS_C, rows, 0)
 
 
-def norm_rows(slot, info, count, token, bc, keep, recv, gain, uvs):
+def norm_rows(slot, info, count, token, bc, entering, gain, uvs):
     return pl.pallas_call(
         functools.partial(norm_kernel, slot),
-        in_specs=[SCALAR] + [FULL] * 4 + [ANY] + [FULL] * len(uvs),
+        in_specs=[SCALAR] + [FULL] * 3 + [ANY] + [FULL] * len(uvs),
         out_specs=FULL,
         out_shape=jax.ShapeDtypeStruct((count, gain.shape[1]), BF16),
         compiler_params=params(16),
         cost_estimate=CHEAP,
         name="norm_rows",
-    )(info, bc, keep, recv, gain, token, *uvs)
+    )(info, bc, entering, gain, token, *uvs)
 
 
 def project_kernel(base, added, a0, a1, w0_far, w1_far, *refs):
@@ -497,6 +470,65 @@
     )(*operands)
 
 
+def project_both_kernel(base, a0_far, a1_far, a0_near, a1_near, w0_far, w1_far, far, near, a0, a1, w0, w1, sem):
+    j = pl.program_id(0)
+    tiles = pl.num_programs(0)
+    rows = far.shape[0]
+
+    def fetch(t):
+        slot = lax.rem(t, SLOTS)
+        lanes = pl.ds(pl.multiple_of((base + t) * TILE, TILE), TILE)
+        return (
+            pltpu.make_async_copy(w0_far.at[:, lanes], w0.at[slot], sem.at[0, slot]),
+            pltpu.make_async_copy(w1_far.at[:, lanes], w1.at[slot], sem.at[1, slot]),
+        )
+
+    def start(t):
+        @pl.when(t < tiles)
+        def _():
+            for copy in fetch(t):
+                copy.start()
+
+    @pl.when(j == 0)
+    def _():
+        for t in range(SLOTS - 1):
+            start(t)
+        a0[0:rows, :] = a0_far[...]
+        a0[rows:, :] = a0_near[...]
+        a1[0:rows, :] = a1_far[...]
+        a1[rows:, :] = a1_near[...]
+
+    start(j + SLOTS - 1)
+    for copy in fetch(j):
+        copy.wait()
+    slot = lax.rem(j, SLOTS)
+    total = dot(a0[...], w0[slot]) + dot(a1[...], w1[slot])
+    far[...] = total[0:rows].astype(BF16)
+    near[...] = total[rows:]
+
+
+def project_both(far, far_mate, near, near_mate, w0, w1, first, count):
+    rows, depth = far.shape
+    placed = pl.BlockSpec((rows, TILE), lambda j: (0, j))
+    return pl.pallas_call(
+        functools.partial(project_both_kernel, first // TILE),
+        grid=(count // TILE,),
+        in_specs=[FULL] * 4 + [FAR] * 2,
+        out_specs=[placed, placed],
+        out_shape=[jax.ShapeDtypeStruct((rows, count), BF16), jax.ShapeDtypeStruct((rows, count), F32)],
+        scratch_shapes=[
+            pltpu.VMEM((2 * rows, depth), BF16),
+            pltpu.VMEM((2 * rows, depth), BF16),
+            pltpu.VMEM((SLOTS, depth, TILE), BF16),
+            pltpu.VMEM((SLOTS, depth, TILE), BF16),
+            pltpu.SemaphoreType.DMA((2, SLOTS)),
+        ],
+        compiler_params=params(24),
+        cost_estimate=CHEAP,
+        name="project_both",
+    )(far, far_mate, near, near_mate, w0, w1)
+
+
 def add_kernel(part, arrived, _, out):
     out[...] = (part[...] + arrived[...].astype(F32)).astype(BF16)
 
@@ -517,9 +549,9 @@
     )(part, arrived, result)
 
 
-def shift(block, distance):
-    size = lax.axis_size("seq")
-    return lax.ppermute(block, "seq", [(i, i + distance) for i in range(size - distance)])
+def shift(block, axis):
+    size = lax.axis_size(axis)
+    return lax.ppermute(block, axis, [(i, (i + 1) % size) for i in range(size)])
 
 
 def swap(block, axis, bit):
@@ -541,95 +573,67 @@
     length, width = x_input.shape
     heads = step_size.shape[1]
     ways = lax.axis_size("head")
-    pairs = lax.axis_size("seq") // 2
+    devices = lax.axis_size("seq")
     mine = lax.axis_index("head")
-    half = width // 2
-    info = jnp.stack([lax.axis_index("seq") & 1, mine ^ 3, mine ^ 2, mine ^ 1, mine]).astype(jnp.int32)
+    seq = lax.axis_index("seq")
+    info = jnp.stack([seq, mine ^ 3, mine ^ 2, mine ^ 1, mine]).astype(jnp.int32)
 
     x_far, z_far, w_far = [pltpu.with_memory_space_constraint(v, pltpu.HBM) for v in (x_input, z_input, out_weight)]
     bc = bc_input.reshape(length, -1)
-    halo = shift(jnp.concatenate([x_input[length - LEAD :], bc[length - LEAD :]], 1), 1)
+    halo = shift(jnp.concatenate([x_input[length - LEAD :], bc[length - LEAD :]], 1), "seq")
     weight_mate = swap(out_weight, "head", 1)
 
     ones = jnp.asarray(np.tile(np.repeat(np.eye(heads), P_SIZE, axis=1), (2, 1)), BF16)
     cum, cum_s, log_s, f_dev, f_blk, e_blk, rates = decays(log_decay, step_size, skip_gain, ones)
-    x_conv, bc_conv, keep, send = conv_states(
-        info, x_far, bc, halo, conv_weight_x, conv_weight_bc, f_dev, ones, rates
+    x_conv, bc_conv, send = conv_states(
+        devices, info, x_far, bc, halo, conv_weight_x, conv_weight_bc, f_dev, ones, rates
     )
 
     x_conv = pltpu.with_memory_space_constraint(x_conv, pltpu.HBM)
     uvs = []
 
     def scan_next(token):
-        if len(uvs) < B_PARTS:
-            uvs.append(
-                scan_part(len(uvs), token, x_conv, bc_conv, z_far, cum, cum_s, log_s, f_blk, e_blk, rates, ones)
-            )
+        uvs.append(
+            scan_part(len(uvs), token, x_conv, bc_conv, z_far, cum, cum_s, log_s, f_blk, e_blk, rates, ones)
+        )
         return uvs[-1]
 
-    message = ((N + EXTRA, half), BF16)
-    full = ((N, half), F32)
-    got = swap(send, "seq", 1)
-    done = scan_next(send)
-    msg, own, first, aux = combine(
-        pair_kernel,
-        (info, got, keep, rates, done),
-        [SCALAR, FULL, FULL, FULL, ANY],
-        [message, full, full, ((16, half), F32)],
-        "pair",
-    )
-    behind = None
-    covered = 0
-    while True:
-        got = shift(msg, 2 * (covered + 1))
-        done = scan_next(msg)
-        covered = 2 * covered + 1
-        if covered >= pairs - 1:
-            break
-        operands, specs = [got, own, aux], [FULL, FULL, FULL]
-        if behind is None:
-            kernel = lambda g, o, a, t, m, b: wave_kernel(g, o, a, None, t, m, b)
-        else:
-            kernel = wave_kernel
-            operands.append(behind)
-            specs.append(FULL)
-        msg, behind = combine(kernel, operands + [done], specs + [ANY], [message, ((N + 8, half), F32)], "wave")
-    operands, specs = [info, got], [SCALAR, FULL]
-    if behind is None:
-        kernel = lambda o, g, f, a, t, b, h: last_kernel(o, g, None, f, a, t, b, h)
-    else:
-        kernel = last_kernel
-        operands.append(behind)
-        specs.append(FULL)
-    out = ((N, half), BF16)
-    back, held = combine(kernel, operands + [first, aux, done], specs + [FULL, FULL, ANY], [out, out], "last")
-    other = swap(back, "seq", 1)
+    states = lax.all_to_all(send, "seq", 0, 0)
+    done = send
+    for _ in range(B_PARTS // 2):
+        done = scan_next(done)
+    prefixes = prefix(states, done)
+    entering = lax.all_to_all(prefixes, "seq", 0, 0)
+    done = prefixes
     while len(uvs) < B_PARTS:
-        scan_next(back)
+        done = scan_next(done)
 
     count = length // ways
     gain = norm_gain[None, :]
 
     def rows_for(slot, token):
-        return norm_rows(slot, info, count, token, bc_conv, held, other, gain, uvs)
-
-    far_mate = rows_for(1, held)
+        return norm_rows(slot, info, count, token, bc_conv, entering, gain, uvs)
+
+    far_mate = rows_for(1, done)
     far = rows_for(2, far_mate)
     far_mate = swap(far_mate, "head", 1)
     columns = out_weight.shape[1]
-    cuts = [columns * c // 16 for c in (0, 3, 6, 9, 12, 14, 16)]
-    arrivals = []
-    for lo, hi in zip(cuts[:-1], cuts[1:]):
-        sent = project(far, far_mate, w_far, weight_mate, lo, hi - lo, BF16)
-        arrivals.append(swap(sent, "head", 2))
-    near_mate = rows_for(3, far)
+    quarter = columns // 4
+    weights = (w_far, weight_mate)
+    sent = project(far, far_mate, *weights, 0, quarter, BF16)
+    arrivals = [swap(sent, "head", 2)]
+    near_mate = rows_for(3, sent)
     near = rows_for(4, near_mate)
     near_mate = swap(near_mate, "head", 1)
-    last = project(near, near_mate, w_far, weight_mate, cuts[-2], columns - cuts[-2], F32)
-    result = None
-    for arrived, lo, hi in zip(arrivals[:-1], cuts[:-2], cuts[1:-1]):
-        result = project(near, near_mate, w_far, weight_mate, lo, hi - lo, BF16, arrived, result)
-    return add_chunk(last, arrivals[-1], result, cuts[-2])
+    parts = []
+    for c in range(quarter, columns, quarter):
+        sent, part = project_both(far, far_mate, near, near_mate, *weights, c, quarter)
+        arrivals.append(swap(sent, "head", 2))
+        parts.append(part)
+    result = project(near, near_mate, *weights, 0, quarter, BF16, arrivals[0])
+    for c, part in enumerate(parts, 1):
+        result = add_chunk(part, arrivals[c], result, c * quarter)
+    return result
 
 
 def solution(mesh):

time: 127 us -> 137 us (1.079)
  the two profiles are of different devices: /device:TPU:26 before, /device:TPU:0 now
where the time goes in v6:
time: 137 us; the launch traced here: 136 us
  Pallas kernels  75.8 us (55%)
  local copies, waits for them, and re-layouts  25.6 us (19%)
  starting transfers between devices  17.7 us (13%)
  waiting for transfers between devices  16.7 us (12%)
    unnamed x76, local copies, waits for them, and re-layouts  23.9 us
    pallas_call x3, Pallas kernels, project_both(): pl.pallas_call(functools.partial(project_both_kernel, first // TILE), gri...  20.5 us
    pallas_call x4, Pallas kernels, scan_part(): pl.pallas_call(functools.partial(scan_kernel, part), in_specs=[FAR, FAR]...  19.1 us
    ppermute x7, waiting for transfers between devices, swap(): lax.ppermute(block, axis, [(i, i ^ bit) for i in range(lax.axis_size(axis...  14.4 us
    pallas_call x1, Pallas kernels, conv_states(): pl.pallas_call(conv_kernel, grid=(length // TOK_A,), in_specs=[SCALAR, FA...  12.7 us
    pallas_call x2, Pallas kernels, project(): pl.pallas_call(functools.partial(project_kernel, base, full), grid=(count...  10.3 us
    pallas_call x4, Pallas kernels, norm_rows(): pl.pallas_call(functools.partial(norm_kernel, slot), in_specs=[SCALAR] +...  7.98 us
    all_to_all x1, starting transfers between devices, local(): entering = lax.all_to_all(prefixes, 'seq', 0, 0)  5.44 us
  transfers between devices with their start and end apart: 10, of which 5 were waited for; matrix products, arithmetic and copies ran while one was open for 3% of the time, Pallas kernels for 50%

profile of v6, /device:TPU:0, one launch (start us, length us, event | category | flops | bytes accessed | tf_op | source)
XLA Modules:
  0.0 136.2 jit_solution(11899913306885617108)
XLA Ops:
  2.2 2.7 %collective-permute-start = (bf16[16,2560]{1,0:T(8,128)(2,1)S(1)}, bf16[16,2560]{1,0:T(8,128)(2,1)S(1)}, u32[]{:S(2)}, u32[]{:S(2)}) collective-permute-start(bf16[16,2560]{1,0:T(8,128)(2,1)S(1)} %pad_maximum_fusion), channel_id=1, source_target_pairs={{0,4},{4,8},{8,12},{12,16},{16,20},{20,24},{24,28},{28,0},{1,5},{5... | collective-permute-start | bytes 245768 | tf_op jit(solution)/shard_map/ppermute | solution.py:554
  4.9 2.4 %copy.15 = bf16[128,8,2,256]{3,1,2,0:T(8,128)(2,1)} copy(bf16[128,8,2,256]{3,2,1,0:T(2,128)(2,1)} %bitcast.21) | data formatting | bytes 2097152
  9.0 1.9 %collective-permute-done.halo = bf16[16,2560]{1,0:T(8,128)(2,1)S(1)} collective-permute-done((bf16[16,2560]{1,0:T(8,128)(2,1)S(1)}, bf16[16,2560]{1,0:T(8,128)(2,1)S(1)}, u32[]{:S(2)}, u32[]{:S(2)}) %collective-permute-start) | collective-permute-done | bytes 81952 | tf_op jit(solution)/shard_map/ppermute | solution.py:554
  12.1 12.7 %conv_states.1 = (bf16[1024,2048]{1,0:T(8,128)(2,1)}, bf16[1024,512]{1,0:T(8,128)(2,1)S(1)}, bf16[8,144,256]{2,1,0:T(8,128)(2,1)}) custom-call(s32[5]{0:T(128)S(1)} %stack.23.info, bf16[1024,2048]{1,0:T(8,128)(2,1)} %x_far.1, bf16[1024,512]{1,0:T(8,128)(2,1)S(1)} %bitcast.13, bf16[16,2560]{1,0:T(8,128)(2,1)S(1)} %collective-permute-done.halo, ...), custom_call_target="tpu_custom_call" | custom-call | flops 1 | bytes 1 | tf_op jit(solution)/shard_map/conv_states/pallas_call | solution.py:225
  24.8 4.2 %all-to-all-start = ((bf16[8,144,256]{2,1,0:T(8,128)(2,1)}), bf16[8,144,256]{2,1,0:T(8,128)(2,1)}, u32[]{:S(2)}, u32[]{:S(2)}) async-start(bf16[8,144,256]{2,1,0:T(8,128)(2,1)} %get-tuple-element.24._), calls=%async_computation | async-start | bytes 1179648 | tf_op jit(solution)/shard_map/all_to_all | solution.py:601
  29.0 4.7 %scan_part.4._.refs_0_ = bf16[1024,1024]{1,0:T(8,128)(2,1)S(1)} custom-call(bf16[1024,2048]{1,0:T(8,128)(2,1)} %get-tuple-element.25.x_far, bf16[1024,2048]{1,0:T(8,128)(2,1)} %z_far.7, bf16[1024,512]{1,0:T(8,128)(2,1)S(1)} %get-tuple-element.23.bc_all.bc, f32[1024,32]{1,0:T(8,128)S(1)} %get-tuple-element.26.cum, f32[32,1024]{1,0:T(8,128)S(1)} %get-tuple-element.27.cum_s, ...), custom_call_target="tpu_custom_call" | custom-call | flops 1 | bytes 1 | tf_op jit(solution)/shard_map/scan_part/pallas_call | solution.py:350
  38.6 4.7 %scan_part.5._.refs_1_ = bf16[1024,1024]{1,0:T(8,128)(2,1)S(1)} custom-call(bf16[1024,2048]{1,0:T(8,128)(2,1)} %get-tuple-element.25.x_far, bf16[1024,2048]{1,0:T(8,128)(2,1)} %z_far.7, bf16[1024,512]{1,0:T(8,128)(2,1)S(1)} %get-tuple-element.23.bc_all.bc, f32[1024,32]{1,0:T(8,128)S(1)} %copy-done.11, f32[32,1024]{1,0:T(8,128)S(1)} %get-tuple-element.27.cum_s, ...), custom_call_target="tpu_custom_call" | custom-call | flops 1 | bytes 1 | tf_op jit(solution)/shard_map/scan_part/pallas_call | solution.py:350
  47.1 5.4 %all-to-all-start.1 = ((bf16[8,128,256]{2,1,0:T(8,128)(2,1)}), bf16[8,128,256]{2,1,0:T(8,128)(2,1)}, u32[]{:S(2)}, u32[]{:S(2)}) async-start(bf16[8,128,256]{2,1,0:T(8,128)(2,1)} %copy-done.16), calls=%async_computation.1 | async-start | bytes 1048576 | tf_op jit(solution)/shard_map/all_to_all | solution.py:606
  58.4 4.8 %scan_part.6._.refs_2_ = bf16[1024,1024]{1,0:T(8,128)(2,1)S(1)} custom-call(bf16[1024,2048]{1,0:T(8,128)(2,1)} %get-tuple-element.25.x_far, bf16[1024,2048]{1,0:T(8,128)(2,1)} %z_far.7, bf16[1024,512]{1,0:T(8,128)(2,1)S(1)} %get-tuple-element.23.bc_all.bc, f32[1024,32]{1,0:T(8,128)S(1)} %copy-done.12, f32[32,1024]{1,0:T(8,128)S(1)} %get-tuple-element.27.cum_s, ...), custom_call_target="tpu_custom_call" | custom-call | flops 1 | bytes 1 | tf_op jit(solution)/shard_map/scan_part/pallas_call | solution.py:350
  63.3 4.8 %scan_part.7._.refs_3_ = bf16[1024,1024]{1,0:T(8,128)(2,1)S(1)} custom-call(bf16[1024,2048]{1,0:T(8,128)(2,1)} %get-tuple-element.25.x_far, bf16[1024,2048]{1,0:T(8,128)(2,1)} %z_far.7, bf16[1024,512]{1,0:T(8,128)(2,1)S(1)} %get-tuple-element.23.bc_all.bc, f32[1024,32]{1,0:T(8,128)S(1)} %copy-done.12, f32[32,1024]{1,0:T(8,128)S(1)} %get-tuple-element.27.cum_s, ...), custom_call_target="tpu_custom_call" | custom-call | flops 1 | bytes 1 | tf_op jit(solution)/shard_map/scan_part/pallas_call | solution.py:350
  70.7 1.6 %copy-done.1 = bf16[1024,1024]{1,0:T(8,128)(2,1)S(1)} copy-done((bf16[1024,1024]{1,0:T(8,128)(2,1)S(1)}, bf16[1024,1024]{1,0:T(8,128)(2,1)}, u32[]{:S(2)}) %copy-start.1) | copy-done | bytes 2097176
  72.3 1.6 %copy-done.4 = bf16[1024,1024]{1,0:T(8,128)(2,1)S(1)} copy-done((bf16[1024,1024]{1,0:T(8,128)(2,1)S(1)}, bf16[1024,1024]{1,0:T(8,128)(2,1)}, u32[]{:S(2)}) %copy-start.4) | copy-done | bytes 2097176
  73.9 1.6 %copy-done.7 = bf16[1024,1024]{1,0:T(8,128)(2,1)S(1)} copy-done((bf16[1024,1024]{1,0:T(8,128)(2,1)S(1)}, bf16[1024,1024]{1,0:T(8,128)(2,1)}, u32[]{:S(2)}) %copy-start.7) | copy-done | bytes 2097176
  75.5 2.0 %norm_rows.4._ = bf16[256,2048]{1,0:T(8,128)(2,1)S(1)} custom-call(s32[5]{0:T(128)S(1)} %stack.23.info, bf16[1024,512]{1,0:T(8,128)(2,1)S(1)} %get-tuple-element.23.bc_all.bc, bf16[8,128,256]{2,1,0:T(8,128)(2,1)} %all-to-all-done.1.entering, f32[1,2048]{1,0:T(1,128)S(1)} %bitcast.16, bf16[1024,1024]{1,0:T(8,128)(2,1)S(1)} %copy-done.7, ...), custom_call_target="tpu_custom_call" | custom-call | flops 1 | bytes 1 | tf_op jit(solution)/shard_map/norm_rows/pallas_call | solution.py:399
  77.6 2.0 %norm_rows.5.a0.a0_far = bf16[256,2048]{1,0:T(8,128)(2,1)S(1)} custom-call(s32[5]{0:T(128)S(1)} %stack.23.info, bf16[1024,512]{1,0:T(8,128)(2,1)S(1)} %get-tuple-element.23.bc_all.bc, bf16[8,128,256]{2,1,0:T(8,128)(2,1)} %all-to-all-done.1.entering, f32[1,2048]{1,0:T(1,128)S(1)} %bitcast.17, bf16[256,2048]{1,0:T(8,128)(2,1)S(1)} %norm_rows.4._, ...), custom_call_target="tpu_custom_call" | custom-call | flops 1 | bytes 1 | tf_op jit(solution)/shard_map/norm_rows/pallas_call | solution.py:399
  80.2 4.9 %project.2._ = bf16[256,1024]{1,0:T(8,128)(2,1)S(1)} custom-call(bf16[256,2048]{1,0:T(8,128)(2,1)S(1)} %norm_rows.5.a0.a0_far, bf16[256,2048]{1,0:T(8,128)(2,1)S(1)} %collective-permute-done.1.a1.a1_far, bf16[2048,4096]{1,0:T(8,128)(2,1)} %w0_far.9, bf16[2048,4096]{1,0:T(8,128)(2,1)} %collective-permute-done.2.w1_far), custom_call_target="tpu_custom_call" | custom-call | flops 1 | bytes 1 | tf_op jit(solution)/shard_map/project/pallas_call | solution.py:455
  85.2 2.0 %norm_rows.6._ = bf16[256,2048]{1,0:T(8,128)(2,1)S(1)} custom-call(s32[5]{0:T(128)S(1)} %stack.23.info, bf16[1024,512]{1,0:T(8,128)(2,1)S(1)} %get-tuple-element.23.bc_all.bc, bf16[8,128,256]{2,1,0:T(8,128)(2,1)} %all-to-all-done.1.entering, f32[1,2048]{1,0:T(1,128)S(1)} %bitcast.18, bf16[256,1024]{1,0:T(8,128)(2,1)S(1)} %project.2._, ...), custom_call_target="tpu_custom_call" | custom-call | flops 1 | bytes 1 | tf_op jit(solution)/shard_map/norm_rows/pallas_call | solution.py:399
  89.1 2.0 %norm_rows.7.a0_near.a0 = bf16[256,2048]{1,0:T(8,128)(2,1)S(1)} custom-call(s32[5]{0:T(128)S(1)} %stack.23.info, bf16[1024,512]{1,0:T(8,128)(2,1)S(1)} %get-tuple-element.23.bc_all.bc, bf16[8,128,256]{2,1,0:T(8,128)(2,1)} %all-to-all-done.1.entering, f32[1,2048]{1,0:T(1,128)S(1)} %bitcast.19, bf16[256,2048]{1,0:T(8,128)(2,1)S(1)} %norm_rows.6._, ...), custom_call_target="tpu_custom_call" | custom-call | flops 1 | bytes 1 | tf_op jit(solution)/shard_map/norm_rows/pallas_call | solution.py:399
  91.1 6.9 %project_both.5 = (bf16[256,1024]{1,0:T(8,128)(2,1)S(1)}, f32[256,1024]{1,0:T(8,128)S(1)}) custom-call(bf16[256,2048]{1,0:T(8,128)(2,1)S(1)} %norm_rows.5.a0.a0_far, bf16[256,2048]{1,0:T(8,128)(2,1)S(1)} %collective-permute-done.1.a1.a1_far, bf16[256,2048]{1,0:T(8,128)(2,1)S(1)} %norm_rows.7.a0_near.a0, ...), custom_call_target="tpu_custom_call" | custom-call | flops 1 | bytes 1 | tf_op jit(solution)/shard_map/project_both/pallas_call | solution.py:513
  98.6 6.8 %project_both.4 = (bf16[256,1024]{1,0:T(8,128)(2,1)S(1)}, f32[256,1024]{1,0:T(8,128)S(1)}) custom-call(bf16[256,2048]{1,0:T(8,128)(2,1)S(1)} %norm_rows.5.a0.a0_far, bf16[256,2048]{1,0:T(8,128)(2,1)S(1)} %collective-permute-done.1.a1.a1_far, bf16[256,2048]{1,0:T(8,128)(2,1)S(1)} %norm_rows.7.a0_near.a0, ...), custom_call_target="tpu_custom_call" | custom-call | flops 1 | bytes 1 | tf_op jit(solution)/shard_map/project_both/pallas_call | solution.py:513
  107.0 6.8 %project_both.3 = (bf16[256,1024]{1,0:T(8,128)(2,1)S(1)}, f32[256,1024]{1,0:T(8,128)S(1)}) custom-call(bf16[256,2048]{1,0:T(8,128)(2,1)S(1)} %norm_rows.5.a0.a0_far, bf16[256,2048]{1,0:T(8,128)(2,1)S(1)} %collective-permute-done.1.a1.a1_far, bf16[256,2048]{1,0:T(8,128)(2,1)S(1)} %norm_rows.7.a0_near.a0, ...), custom_call_target="tpu_custom_call" | custom-call | flops 1 | bytes 1 | tf_op jit(solution)/shard_map/project_both/pallas_call | solution.py:513
  114.4 5.3 %project.3._ = bf16[256,4096]{1,0:T(8,128)(2,1)} custom-call(bf16[256,2048]{1,0:T(8,128)(2,1)S(1)} %norm_rows.7.a0_near.a0, bf16[256,2048]{1,0:T(8,128)(2,1)S(1)} %collective-permute-done.3.a1_near.a1, bf16[2048,4096]{1,0:T(8,128)(2,1)} %w0_far.9, bf16[2048,4096]{1,0:T(8,128)(2,1)} %collective-permute-done.2.w1_far, ...), custom_call_target="tpu_custom_call" | custom-call | flops 1 | bytes 1 | tf_op jit(solution)/shard_map/project/pallas_call | solution.py:455
  120.6 4.2 %collective-permute-done.5.arrived = bf16[256,1024]{1,0:T(8,128)(2,1)S(1)} collective-permute-done((bf16[256,1024]{1,0:T(8,128)(2,1)S(1)}, bf16[256,1024]{1,0:T(8,128)(2,1)S(1)}, u32[]{:S(2)}, u32[]{:S(2)}) %collective-permute-start.5) | collective-permute-done | bytes 524320 | tf_op jit(solution)/shard_map/ppermute | solution.py:558
  125.7 9.6 %collective-permute-done.4.arrived = bf16[256,1024]{1,0:T(8,128)(2,1)S(1)} collective-permute-done((bf16[256,1024]{1,0:T(8,128)(2,1)S(1)}, bf16[256,1024]{1,0:T(8,128)(2,1)S(1)}, u32[]{:S(2)}, u32[]{:S(2)}) %collective-permute-start.4) | collective-permute-done | bytes 524320 | tf_op jit(solution)/shard_map/ppermute | solution.py:558
  (95 shorter events, 30.1 us)
Async XLA Ops:
  0.0 7.3 %copy-start.9 = (bf16[64,2048]{1,0:T(8,128)(2,1)S(1)}, bf16[64,2048]{1,0:T(8,128)(2,1)}, u32[]{:S(2)}) copy-start(bf16[64,2048]{1,0:T(8,128)(2,1)} %constant.17.clone.ones) | copy-start | bytes 786436
  0.0 7.3 %copy-start.36 = (f32[32]{0:T(128)S(1)}, f32[32]{0:T(128)}, u32[]{:S(2)}) copy-start(f32[32]{0:T(128)} %param.18) | copy-start | bytes 388
  0.0 7.3 %copy-start.31 = (f32[1024,32]{0,1:T(8,128)S(1)}, f32[1024,32]{0,1:T(8,128)}, u32[]{:S(2)}) copy-start(f32[1024,32]{0,1:T(8,128)} %param.17) | copy-start | bytes 393220
  0.0 7.3 %copy-start.32 = (f32[1024,32]{0,1:T(8,128)S(1)}, f32[1024,32]{0,1:T(8,128)}, u32[]{:S(2)}) copy-start(f32[1024,32]{0,1:T(8,128)} %param.16) | copy-start | bytes 393220
  0.0 10.9 %copy-start.35 = (f32[4,2,256]{2,1,0:T(2,128)S(1)}, f32[4,2,256]{2,1,0:T(2,128)}, u32[]{:S(2)}) copy-start(f32[4,2,256]{2,1,0:T(2,128)} %wbc.1) | copy-start | bytes 24580
  0.0 10.9 %copy-start.34 = (f32[4,2048]{1,0:T(4,128)S(1)}, f32[4,2048]{1,0:T(4,128)}, u32[]{:S(2)}) copy-start(f32[4,2048]{1,0:T(4,128)} %wx.1) | copy-start | bytes 98308
  0.0 80.2 %collective-permute-start.2 = (bf16[2048,4096]{1,0:T(8,128)(2,1)}, bf16[2048,4096]{1,0:T(8,128)(2,1)}, u32[]{:S(2)}, u32[]{:S(2)}) collective-permute-start(bf16[2048,4096]{1,0:T(8,128)(2,1)} %w0_far.9), channel_id=1, source_target_pairs={{0,1},{1,0},{2,3},{3,2},{4,5},{5,4},{6,7},{7,6},{8,9},{9,8},{10,11... | collective-permute-start | bytes 50331656 | tf_op jit(solution)/shard_map/ppermute | solution.py:558
  2.2 8.7 %collective-permute-start = (bf16[16,2560]{1,0:T(8,128)(2,1)S(1)}, bf16[16,2560]{1,0:T(8,128)(2,1)S(1)}, u32[]{:S(2)}, u32[]{:S(2)}) collective-permute-start(bf16[16,2560]{1,0:T(8,128)(2,1)S(1)} %pad_maximum_fusion), channel_id=1, source_target_pairs={{0,4},{4,8},{8,12},{12,16},{16,20},{20,24},{24,28},{28,0},{1,5},{5... | collective-permute-start | bytes 245768 | tf_op jit(solution)/shard_map/ppermute | solution.py:554
  8.9 20.1 %copy-start.10 = (f32[1024,32]{1,0:T(8,128)}, f32[1024,32]{1,0:T(8,128)S(1)}, u32[]{:S(2)}) copy-start(f32[1024,32]{1,0:T(8,128)S(1)} %get-tuple-element.26.cum) | copy-start | bytes 393220
  8.9 20.1 %copy-start.13 = (f32[32,2048]{1,0:T(8,128)}, f32[32,2048]{1,0:T(8,128)S(1)}, u32[]{:S(2)}) copy-start(f32[32,2048]{1,0:T(8,128)S(1)} %get-tuple-element.22.rates) | copy-start | bytes 786436
  8.9 20.1 %copy-start.18 = (bf16[1024,64]{1,0:T(8,128)(2,1)}, bf16[1024,64]{1,0:T(8,128)(2,1)S(1)}, u32[]{:S(2)}) copy-start(bf16[1024,64]{1,0:T(8,128)(2,1)S(1)} %get-tuple-element.29.f_blk) | copy-start | bytes 393220
  8.9 20.1 %copy-start.22 = (bf16[1024,64]{1,0:T(8,128)(2,1)}, bf16[1024,64]{1,0:T(8,128)(2,1)S(1)}, u32[]{:S(2)}) copy-start(bf16[1024,64]{1,0:T(8,128)(2,1)S(1)} %get-tuple-element.30.e_blk) | copy-start | bytes 393220
  8.9 20.1 %copy-start.27 = (f32[32,1024]{1,0:T(8,128)}, f32[32,1024]{1,0:T(8,128)S(1)}, u32[]{:S(2)}) copy-start(f32[32,1024]{1,0:T(8,128)S(1)} %get-tuple-element.28.log_s) | copy-start | bytes 393220
  24.8 20.3 %all-to-all-start = ((bf16[8,144,256]{2,1,0:T(8,128)(2,1)}), bf16[8,144,256]{2,1,0:T(8,128)(2,1)}, u32[]{:S(2)}, u32[]{:S(2)}) async-start(bf16[8,144,256]{2,1,0:T(8,128)(2,1)} %get-tuple-element.24._), calls=%async_computation | async-start | bytes 1179648 | tf_op jit(solution)/shard_map/all_to_all | solution.py:601
  47.1 23.6 %all-to-all-start.1 = ((bf16[8,128,256]{2,1,0:T(8,128)(2,1)}), bf16[8,128,256]{2,1,0:T(8,128)(2,1)}, u32[]{:S(2)}, u32[]{:S(2)}) async-start(bf16[8,128,256]{2,1,0:T(8,128)(2,1)} %copy-done.16), calls=%async_computation.1 | async-start | bytes 1048576 | tf_op jit(solution)/shard_map/all_to_all | solution.py:606
  63.3 7.4 %copy-start.33 = (f32[2048]{0:T(1024)S(1)}, f32[2048]{0:T(1024)}, u32[]{:S(2)}) copy-start(f32[2048]{0:T(1024)} %param.19) | copy-start | bytes 24580
  77.5 2.7 %collective-permute-start.1 = (bf16[256,2048]{1,0:T(8,128)(2,1)S(1)}, bf16[256,2048]{1,0:T(8,128)(2,1)S(1)}, u32[]{:S(2)}, u32[]{:S(2)}) collective-permute-start(bf16[256,2048]{1,0:T(8,128)(2,1)S(1)} %norm_rows.4._), channel_id=1, source_target_pairs={{0,1},{1,0},{2,3},{3,2},{4,5},{5,4},{6,7},{7,6},{8,9},{9,8},{10,11... | collective-permute-start | bytes 3145736 | tf_op jit(solution)/shard_map/ppermute | solution.py:558
  79.6 5.6 %copy-start.2 = (bf16[1024,1024]{1,0:T(8,128)(2,1)S(1)}, bf16[1024,1024]{1,0:T(8,128)(2,1)}, u32[]{:S(2)}) copy-start(bf16[1024,1024]{1,0:T(8,128)(2,1)} %copy-done) | copy-start | bytes 6291460
  79.6 5.6 %copy-start.5 = (bf16[1024,1024]{1,0:T(8,128)(2,1)S(1)}, bf16[1024,1024]{1,0:T(8,128)(2,1)}, u32[]{:S(2)}) copy-start(bf16[1024,1024]{1,0:T(8,128)(2,1)} %copy-done.3) | copy-start | bytes 6291460
  87.2 3.9 %collective-permute-start.3 = (bf16[256,2048]{1,0:T(8,128)(2,1)S(1)}, bf16[256,2048]{1,0:T(8,128)(2,1)S(1)}, u32[]{:S(2)}, u32[]{:S(2)}) collective-permute-start(bf16[256,2048]{1,0:T(8,128)(2,1)S(1)} %norm_rows.6._), channel_id=1, source_target_pairs={{0,1},{1,0},{2,3},{3,2},{4,5},{5,4},{6,7},{7,6},{8,9},{9,8},{10,11... | collective-permute-start | bytes 3145736 | tf_op jit(solution)/shard_map/ppermute | solution.py:558
  87.6 26.8 %collective-permute-start.7 = (bf16[256,1024]{1,0:T(8,128)(2,1)S(1)}, bf16[256,1024]{1,0:T(8,128)(2,1)S(1)}, u32[]{:S(2)}, u32[]{:S(2)}) collective-permute-start(bf16[256,1024]{1,0:T(8,128)(2,1)S(1)} %project.2._), channel_id=1, source_target_pairs={{0,2},{1,3},{2,0},{3,1},{4,6},{5,7},{6,4},{7,5},{8,10},{9,11},{10,... | collective-permute-start | bytes 1572872 | tf_op jit(solution)/shard_map/ppermute | solution.py:558
  98.0 21.8 %collective-permute-start.6 = (bf16[256,1024]{1,0:T(8,128)(2,1)S(1)}, bf16[256,1024]{1,0:T(8,128)(2,1)S(1)}, u32[]{:S(2)}, u32[]{:S(2)}) collective-permute-start(bf16[256,1024]{1,0:T(8,128)(2,1)S(1)} %get-tuple-element.36), channel_id=1, source_target_pairs={{0,2},{1,3},{2,0},{3,1},{4,6},{5,7},{6,4},{7,5},{8,10},{9,11},{10,... | collective-permute-start | bytes 1572872 | tf_op jit(solution)/shard_map/ppermute | solution.py:558
  105.4 19.4 %collective-permute-start.5 = (bf16[256,1024]{1,0:T(8,128)(2,1)S(1)}, bf16[256,1024]{1,0:T(8,128)(2,1)S(1)}, u32[]{:S(2)}, u32[]{:S(2)}) collective-permute-start(bf16[256,1024]{1,0:T(8,128)(2,1)S(1)} %get-tuple-element.34), channel_id=1, source_target_pairs={{0,2},{1,3},{2,0},{3,1},{4,6},{5,7},{6,4},{7,5},{8,10},{9,11},{10,... | collective-permute-start | bytes 1572872 | tf_op jit(solution)/shard_map/ppermute | solution.py:558
  113.8 21.5 %collective-permute-start.4 = (bf16[256,1024]{1,0:T(8,128)(2,1)S(1)}, bf16[256,1024]{1,0:T(8,128)(2,1)S(1)}, u32[]{:S(2)}, u32[]{:S(2)}) collective-permute-start(bf16[256,1024]{1,0:T(8,128)(2,1)S(1)} %get-tuple-element.32), channel_id=1, source_target_pairs={{0,2},{1,3},{2,0},{3,1},{4,6},{5,7},{6,4},{7,5},{8,10},{9,11},{10,... | collective-permute-start | bytes 1572872 | tf_op jit(solution)/shard_map/ppermute | solution.py:558
  (23 other events, 41.5 us)

commit v7 on v6

--- a/solution.py
+++ b/solution.py
@@ -21,10 +21,11 @@
 EXTRA = 16
 SLAB = 256
 ROWS_C = 128
+HALF_C = 512
 TILE = 256
 SLOTS = 4
 LEAD = 16
-B_PARTS = 4
+B_PARTS = 2
 HIGHEST = lax.Precision.HIGHEST
 F32 = jnp.float32
 BF16 = jnp.bfloat16
@@ -47,6 +48,10 @@
 
 def half_silu(half):
     return half + half * jnp.tanh(half)
+
+
+def far(*arrays):
+    return [pltpu.with_memory_space_constraint(a, pltpu.HBM) for a in arrays]
 
 
 def whole(shape):
@@ -100,18 +105,18 @@
     length, heads = log_decay.shape
     blocks = length // TOK_B
     width = ones.shape[1]
-    wide = jax.ShapeDtypeStruct((heads, length), F32)
-    pair = jax.ShapeDtypeStruct((length, 2 * heads), BF16)
+    wide = pltpu.HBM((heads, length), F32)
+    pair = pltpu.HBM((length, 2 * heads), BF16)
     return pl.pallas_call(
         decay_kernel,
         out_shape=(
-            jax.ShapeDtypeStruct((length, heads), F32),
+            pltpu.HBM((length, heads), F32),
             wide,
             wide,
             pair,
             pair,
             pair,
-            jax.ShapeDtypeStruct((2 * blocks + 16, width), F32),
+            pltpu.HBM((2 * blocks + 16, width), F32),
         ),
         compiler_params=params(16),
         name="decays",
@@ -239,8 +244,8 @@
         ],
         out_shape=(
             pltpu.HBM((length, width), BF16),
-            jax.ShapeDtypeStruct((length, bc_width), BF16),
-            jax.ShapeDtypeStruct(sent, BF16),
+            pltpu.HBM((length, bc_width), BF16),
+            pltpu.HBM(sent, BF16),
         ),
         compiler_params=params(20),
         cost_estimate=CHEAP,
@@ -262,36 +267,51 @@
         prefix_kernel,
         in_specs=[FULL, ANY],
         out_specs=FULL,
-        out_shape=jax.ShapeDtypeStruct((devices, rows - EXTRA, piece), BF16),
+        out_shape=pltpu.HBM((devices, rows - EXTRA, piece), BF16),
         compiler_params=params(16),
         cost_estimate=CHEAP,
         name="prefix",
     )(states, token)
 
 
-def scan_kernel(part, x_far, z_far, bc_all, cum, cum_s, log_s, f_blk, e_blk, rates, ones, _, uv_out, x, z, sem, state):
+def scan_kernel(part, *refs):
+    sources, uv_far = refs[:10], refs[11]
+    bc, cum, cum_s, log_s, f_blk, e_blk, rates, ones, x, z, uv, state, small_sem, sem, out_sem = refs[12:]
     length, width = x.shape
     per_slab = SLAB // P_SIZE
     head0 = part * width // P_SIZE
-    first_lane = part * width
     inner = STEP_B // TOK_B
     blocks = length // TOK_B
-    group = first_lane * (bc_all.shape[1] // (2 * N)) // (width * B_PARTS)
-    b_lanes = slice(2 * N * group, 2 * N * group + N)
-    c_lanes = slice(2 * N * group + N, 2 * N * (group + 1))
+    wide = pl.ds(part * width, width)
+    x_far, z_far, bc_far = sources[:3]
+    group = part * (bc_far.shape[1] // (2 * N)) // B_PARTS
+    halves = (bc_far.at[:, pl.ds(2 * N * group, 2 * N)],) + sources[3:8]
+    halves += (sources[8].at[:, wide], sources[9].at[:, wide])
+    small = [
+        pltpu.make_async_copy(source, target, small_sem.at[k])
+        for k, (source, target) in enumerate(zip(halves, (bc, cum, cum_s, log_s, f_blk, e_blk, rates, ones)))
+    ]
+
+    def rows_of(step):
+        return pl.ds(pl.multiple_of(step * STEP_B, STEP_B), STEP_B)
 
     def fetch(step):
-        piece = pl.ds(pl.multiple_of(step * STEP_B, STEP_B), STEP_B)
-        lanes = pl.ds(first_lane, width)
         return (
-            pltpu.make_async_copy(x_far.at[piece, lanes], x.at[piece], sem.at[0, step]),
-            pltpu.make_async_copy(z_far.at[piece, lanes], z.at[piece], sem.at[1, step]),
+            pltpu.make_async_copy(x_far.at[rows_of(step), wide], x.at[rows_of(step)], sem.at[0, step]),
+            pltpu.make_async_copy(z_far.at[rows_of(step), wide], z.at[rows_of(step)], sem.at[1, step]),
         )
 
+    def store(step):
+        return pltpu.make_async_copy(uv.at[rows_of(step)], uv_far.at[rows_of(step)], out_sem.at[step])
+
+    for copy in small:
+        copy.start()
     for step in range(length // STEP_B):
         for copy in fetch(step):
             copy.start()
     state[...] = jnp.zeros_like(state)
+    for copy in small:
+        copy.wait()
 
     row = lax.broadcasted_iota(jnp.int32, (TOK_B, TOK_B), 0)
     col = lax.broadcasted_iota(jnp.int32, (TOK_B, TOK_B), 1)
@@ -304,21 +324,21 @@
             copy.wait()
         for k in range(inner):
             block(step * inner + k)
+        store(step).start()
         return 0
 
     def block(b):
         at = pl.ds(pl.multiple_of(b * TOK_B, TOK_B), TOK_B)
-        b_mat = bc_all[at, b_lanes]
-        c_mat = bc_all[at, c_lanes]
+        b_mat = bc[at, 0:N]
+        c_mat = bc[at, N : 2 * N]
         scores = jnp.where(keep, dot(c_mat, b_mat, ((1,), (1,))), 0.0)
-        wide = pl.ds(first_lane, width)
-        fade_rows = rates[pl.ds(b, 1), wide]
-        lead_rows = rates[pl.ds(blocks + b, 1), wide]
-        skip = rates[2 * blocks + 8 : 2 * blocks + 9, wide]
+        fade_rows = rates[pl.ds(b, 1), :]
+        lead_rows = rates[pl.ds(blocks + b, 1), :]
+        skip = rates[2 * blocks + 8 : 2 * blocks + 9, :]
         for s in range(width // SLAB):
             lanes = slice(s * SLAB, (s + 1) * SLAB)
             xb = x[at, lanes]
-            sel = ones[:, first_lane + s * SLAB : first_lane + (s + 1) * SLAB]
+            sel = ones[:, lanes]
             old = state[:, lanes]
             rise = dot(e_blk[at, :], sel)
             carried = dot(c_mat, old.astype(BF16)) * rise
@@ -336,36 +356,48 @@
             xs = xb.astype(F32)
             y = jnp.concatenate(within, 1) + carried + skip[:, lanes] * xs
             gate = half_silu((z[at, lanes] * 0.5).astype(F32))
-            uv_out[at, lanes] = (y * gate).astype(BF16)
-            uv_out[at, width + s * SLAB : width + (s + 1) * SLAB] = (gate * rise * lead_rows[:, lanes]).astype(BF16)
+            uv[at, lanes] = (y * gate).astype(BF16)
+            uv[at, width + s * SLAB : width + (s + 1) * SLAB] = (gate * rise * lead_rows[:, lanes]).astype(BF16)
             xf = (xs * dot(f_blk[at, :], sel)).astype(BF16)
             state[:, lanes] = old * fade_rows[:, lanes] + dot(b_mat, xf, ((0,), (0,)))
 
     lax.fori_loop(0, length // STEP_B, turn, 0)
-
-
-def scan_part(part, token, x, bc, z, cum, cum_s, log_s, f_blk, e_blk, rates, ones):
+    for step in range(length // STEP_B):
+        store(step).wait()
+
+
+def scan_part(part, token, x, z, bc, cum, cum_s, log_s, f_blk, e_blk, rates, ones):
     length, full = x.shape
     width = full // B_PARTS
+    steps = length // STEP_B
+    same = [pltpu.VMEM(a.shape, a.dtype) for a in (cum, cum_s, log_s, f_blk, e_blk)]
     return pl.pallas_call(
         functools.partial(scan_kernel, part),
-        in_specs=[FAR, FAR] + [FULL] * 8 + [ANY],
-        out_specs=FULL,
-        out_shape=jax.ShapeDtypeStruct((length, 2 * width), BF16),
-        scratch_shapes=[
+        in_specs=[FAR] * 10 + [ANY],
+        out_specs=FAR,
+        out_shape=pltpu.HBM((length, 2 * width), BF16),
+        scratch_shapes=[pltpu.VMEM((length, 2 * N), BF16)]
+        + same
+        + [
+            pltpu.VMEM((rates.shape[0], width), F32),
+            pltpu.VMEM((ones.shape[0], width), BF16),
             pltpu.VMEM((length, width), BF16),
             pltpu.VMEM((length, width), BF16),
-            pltpu.SemaphoreType.DMA((2, length // STEP_B)),
+            pltpu.VMEM((length, 2 * width), BF16),
             pltpu.VMEM((N, width), F32),
+            pltpu.SemaphoreType.DMA((8,)),
+            pltpu.SemaphoreType.DMA((2, steps)),
+            pltpu.SemaphoreType.DMA((steps,)),
         ],
-        compiler_params=params(16),
+        compiler_params=params(24),
         cost_estimate=CHEAP,
         name="scan_part",
     )(x, z, bc, cum, cum_s, log_s, f_blk, e_blk, rates, ones, token)
 
 
-def norm_kernel(slot, info, bc, entering, gain, _, *refs):
-    uvs, out = refs[:-1], refs[-1]
+def norm_kernel(slot, info, bc_far, entering, gain, _, *refs):
+    uvs_far, out = refs[:B_PARTS], refs[B_PARTS]
+    bc, uvs, sem = refs[B_PARTS + 1], refs[B_PARTS + 2 : -1], refs[-1]
     count, width = out.shape
     groups = bc.shape[1] // (2 * N)
     per = width // groups
@@ -373,23 +405,36 @@
     piece = entering.shape[2]
     base = info[slot] * count
 
-    def rows(j, _):
+    def fetch(j):
         to = pl.ds(pl.multiple_of(j * ROWS_C, ROWS_C), ROWS_C)
         at = pl.ds(pl.multiple_of(base + j * ROWS_C, ROWS_C), ROWS_C)
+        pairs = zip((bc_far,) + uvs_far, (bc,) + uvs)
+        return [pltpu.make_async_copy(a.at[at], b.at[to], sem.at[k, j]) for k, (a, b) in enumerate(pairs)]
+
+    for j in range(count // ROWS_C):
+        for copy in fetch(j):
+            copy.start()
+
+    def rows(j, _):
+        for copy in fetch(j):
+            copy.wait()
+        to = pl.ds(pl.multiple_of(j * ROWS_C, ROWS_C), ROWS_C)
         for g in range(groups):
-            c_mat = bc[at, 2 * N * g + N : 2 * N * (g + 1)]
+            c_mat = bc[to, 2 * N * g + N : 2 * N * (g + 1)]
             pieces = []
             squares = None
-            for p in range(g * per // part, (g + 1) * per // part):
-                start = p * part
-                inc = jnp.concatenate([entering[k] for k in range(start // piece, (start + part) // piece)], 1)
-                gated = uvs[p][at, 0:part].astype(F32) + uvs[p][at, part:].astype(F32) * dot(c_mat, inc)
+            for start in range(g * per, (g + 1) * per, HALF_C):
+                p, lane = start // part, start % part
+                inc = jnp.concatenate([entering[k] for k in range(start // piece, (start + HALF_C) // piece)], 1)
+                u = uvs[p][to, lane : lane + HALF_C].astype(F32)
+                v = uvs[p][to, part + lane : part + lane + HALF_C].astype(F32)
+                gated = u + v * dot(c_mat, inc)
                 square = jnp.sum(gated * gated, axis=-1, keepdims=True)
                 squares = square if squares is None else squares + square
                 pieces.append((start, gated))
             scale = lax.rsqrt(squares * (1.0 / per) + EPS)
             for start, gated in pieces:
-                out[to, start : start + part] = (gated * scale * gain[:, start : start + part]).astype(BF16)
+                out[to, start : start + HALF_C] = (gated * scale * gain[:, start : start + HALF_C]).astype(BF16)
         return 0
 
     lax.fori_loop(0, count // ROWS_C, rows, 0)
@@ -398,9 +443,11 @@
 def norm_rows(slot, info, count, token, bc, entering, gain, uvs):
     return pl.pallas_call(
         functools.partial(norm_kernel, slot),
-        in_specs=[SCALAR] + [FULL] * 3 + [ANY] + [FULL] * len(uvs),
+        in_specs=[SCALAR, FAR, FULL, FULL, ANY] + [FAR] * len(uvs),
         out_specs=FULL,
         out_shape=jax.ShapeDtypeStruct((count, gain.shape[1]), BF16),
+        scratch_shapes=[pltpu.VMEM((count, a.shape[1]), BF16) for a in [bc] + uvs]
+        + [pltpu.SemaphoreType.DMA((1 + len(uvs), count // ROWS_C))],
         compiler_params=params(16),
         cost_estimate=CHEAP,
         name="norm_rows",
@@ -578,24 +625,24 @@
     seq = lax.axis_index("seq")
     info = jnp.stack([seq, mine ^ 3, mine ^ 2, mine ^ 1, mine]).astype(jnp.int32)
 
-    x_far, z_far, w_far = [pltpu.with_memory_space_constraint(v, pltpu.HBM) for v in (x_input, z_input, out_weight)]
+    x_far, z_far, w_far = far(x_input, z_input, out_weight)
     bc = bc_input.reshape(length, -1)
     halo = shift(jnp.concatenate([x_input[length - LEAD :], bc[length - LEAD :]], 1), "seq")
     weight_mate = swap(out_weight, "head", 1)
 
     ones = jnp.asarray(np.tile(np.repeat(np.eye(heads), P_SIZE, axis=1), (2, 1)), BF16)
     cum, cum_s, log_s, f_dev, f_blk, e_blk, rates = decays(log_decay, step_size, skip_gain, ones)
+    f_dev, rates = far(f_dev, rates)
     x_conv, bc_conv, send = conv_states(
         devices, info, x_far, bc, halo, conv_weight_x, conv_weight_bc, f_dev, ones, rates
     )
 
-    x_conv = pltpu.with_memory_space_constraint(x_conv, pltpu.HBM)
+    x_conv, bc_conv = far(x_conv, bc_conv)
+    small = far(cum, cum_s, log_s, f_blk, e_blk)
     uvs = []
 
     def scan_next(token):
-        uvs.append(
-            scan_part(len(uvs), token, x_conv, bc_conv, z_far, cum, cum_s, log_s, f_blk, e_blk, rates, ones)
-        )
+        uvs.extend(far(scan_part(len(uvs), token, x_conv, z_far, bc_conv, *small, rates, far(ones)[0])))
         return uvs[-1]
 
     states = lax.all_to_all(send, "seq", 0, 0)
@@ -615,19 +662,19 @@
         return norm_rows(slot, info, count, token, bc_conv, entering, gain, uvs)
 
     far_mate = rows_for(1, done)
-    far = rows_for(2, far_mate)
+    ahead = rows_for(2, far_mate)
     far_mate = swap(far_mate, "head", 1)
     columns = out_weight.shape[1]
     quarter = columns // 4
     weights = (w_far, weight_mate)
-    sent = project(far, far_mate, *weights, 0, quarter, BF16)
+    sent = project(ahead, far_mate, *weights, 0, quarter, BF16)
     arrivals = [swap(sent, "head", 2)]
     near_mate = rows_for(3, sent)
     near = rows_for(4, near_mate)
     near_mate = swap(near_mate, "head", 1)
     parts = []
     for c in range(quarter, columns, quarter):
-        sent, part = project_both(far, far_mate, near, near_mate, *weights, c, quarter)
+        sent, part = project_both(ahead, far_mate, near, near_mate, *weights, c, quarter)
         arrivals.append(swap(sent, "head", 2))
         parts.append(part)
     result = project(near, near_mate, *weights, 0, quarter, BF16, arrivals[0])

time: 137 us -> 131 us (0.956)
  local copies, waits for them, and re-layouts: 25.6 us -> 11.1 us
  waiting for transfers between devices: 16.7 us -> 22.2 us
  Pallas kernels: 75.8 us -> 80.5 us
    unnamed x76 -> x22, local copies, waits for them, and re-layouts: 23.9 us -> 9.43 us
    all_to_all x1, waiting for transfers between devices: 0.46 us -> 5.45 us  [local(): states = lax.all_to_all(send, 'seq', 0, 0)]
    pallas_call x9 -> x7, Pallas kernels: 28.6 us -> 33.1 us  [the longest x2 19.4 us: scan_part(): pl.pallas_call(functools.partial(scan_kernel, part), in_specs=[FAR] * 10...]
    all_to_all x1, waiting for transfers between devices: 0.01 us -> 3.88 us  [local(): entering = lax.all_to_all(prefixes, 'seq', 0, 0)]
    ppermute x1, waiting for transfers between devices: 1.89 us -> 0.01 us  [shift(): return lax.ppermute(block, axis, [(i, (i + 1) % size) for i in range(size)])]
    all_to_all x1, starting transfers between devices: 5.44 us -> 3.67 us  [local(): entering = lax.all_to_all(prefixes, 'seq', 0, 0)]
    ppermute x7, waiting for transfers between devices: 14.4 us -> 12.9 us  [swap(): lax.ppermute(block, axis, [(i, i ^ bit) for i in range(lax.axis_size(axis...]
  transfers between devices with their start and end apart: 10 -> 10, of which waited for: 5 -> 4; matrix products, arithmetic and copies ran while one was open for 3% -> 2% of each run, Pallas kernels for 50% -> 55%
where the time goes in v7:
time: 131 us
  Pallas kernels  80.5 us (61%)
  waiting for transfers between devices  22.2 us (17%)
  starting transfers between devices  16.5 us (13%)
  local copies, waits for them, and re-layouts  11.1 us (8%)
    pallas_call x3, Pallas kernels, project_both(): pl.pallas_call(functools.partial(project_both_kernel, first // TILE), gri...  20.5 us
    pallas_call x2, Pallas kernels, scan_part(): pl.pallas_call(functools.partial(scan_kernel, part), in_specs=[FAR] * 10...  19.4 us
    pallas_call x1, Pallas kernels, conv_states(): pl.pallas_call(conv_kernel, grid=(length // TOK_A,), in_specs=[SCALAR, FA...  13.4 us
    ppermute x7, waiting for transfers between devices, swap(): lax.ppermute(block, axis, [(i, i ^ bit) for i in range(lax.axis_size(axis...  12.9 us
    pallas_call x4, Pallas kernels, norm_rows(): pl.pallas_call(functools.partial(norm_kernel, slot), in_specs=[SCALAR, FA...  11.3 us
    pallas_call x2, Pallas kernels, project(): pl.pallas_call(functools.partial(project_kernel, base, full), grid=(count...  9.96 us
    unnamed x22, local copies, waits for them, and re-layouts  9.43 us
    all_to_all x1, waiting for transfers between devices, local(): states = lax.all_to_all(send, 'seq', 0, 0)  5.45 us
  transfers between devices with their start and end apart: 10, of which 4 were waited for; matrix products, arithmetic and copies ran while one was open for 2% of the time, Pallas kernels for 55%

profile of v7, /device:TPU:0, one launch (start us, length us, event | category | flops | bytes accessed | tf_op | source)
XLA Modules:
  0.0 130.5 jit_solution(9477599717849739070)
XLA Ops:
  2.1 2.6 %collective-permute-start = (bf16[16,2560]{1,0:T(8,128)(2,1)S(1)}, bf16[16,2560]{1,0:T(8,128)(2,1)S(1)}, u32[]{:S(2)}, u32[]{:S(2)}) collective-permute-start(bf16[16,2560]{1,0:T(8,128)(2,1)S(1)} %pad_maximum_fusion), channel_id=1, source_target_pairs={{0,4},{4,8},{8,12},{12,16},{16,20},{20,24},{24,28},{28,0},{1,5},{5... | collective-permute-start | bytes 245768 | tf_op jit(solution)/shard_map/ppermute | solution.py:601
  4.6 1.4 %copy.15 = bf16[128,8,2,256]{3,1,2,0:T(8,128)(2,1)S(1)} copy(bf16[128,8,2,256]{3,2,1,0:T(2,128)(2,1)} %bitcast.21) | data formatting | bytes 2097152
  9.5 2.5 %decays.1 = (f32[1024,32]{1,0:T(8,128)}, f32[32,1024]{1,0:T(8,128)}, f32[32,1024]{1,0:T(8,128)}, bf16[1024,64]{1,0:T(8,128)(2,1)}, bf16[1024,64]{1,0:T(8,128)(2,...) custom-call(f32[32,1024]{1,0:T(8,128)S(1)} %bitcast.14, f32[32,1024]{1,0:T(8,128)S(1)} %bitcast.15, ...), custom_call_target="tpu_custom_call" | custom-call | tf_op jit(solution)/shard_map/decays/pallas_call | solution.py:110
  14.5 13.4 %conv_states.1 = (bf16[1024,2048]{1,0:T(8,128)(2,1)}, bf16[1024,512]{1,0:T(8,128)(2,1)}, bf16[8,144,256]{2,1,0:T(8,128)(2,1)}) custom-call(s32[5]{0:T(128)S(1)} %stack.23.info, bf16[1024,2048]{1,0:T(8,128)(2,1)} %x_far.1, bf16[1024,512]{1,0:T(8,128)(2,1)S(1)} %bitcast.13, bf16[16,2560]{1,0:T(8,128)(2,1)S(1)} %collective-permute-done.halo, ...), custom_call_target="tpu_custom_call" | custom-call | flops 1 | bytes 1 | tf_op jit(solution)/shard_map/conv_states/pallas_call | solution.py:230
  27.8 4.9 %all-to-all-start = ((bf16[8,144,256]{2,1,0:T(8,128)(2,1)}), bf16[8,144,256]{2,1,0:T(8,128)(2,1)S(1)}, u32[]{:S(2)}, u32[]{:S(2)}) async-start(bf16[8,144,256]{2,1,0:T(8,128)(2,1)} %get-tuple-element.24.refs_10_), calls=%async_computation | async-start | bytes 1179648 | tf_op jit(solution)/shard_map/all_to_all | solution.py:648
  32.8 1.1 copy-done.3
  33.9 9.7 %scan_part.2._.refs_0_ = bf16[1024,2048]{1,0:T(8,128)(2,1)} custom-call(bf16[1024,2048]{1,0:T(8,128)(2,1)} %get-tuple-element.25.refs_0_, bf16[1024,2048]{1,0:T(8,128)(2,1)} %refs_1_.3, bf16[1024,512]{1,0:T(8,128)(2,1)} %get-tuple-element.23.refs_2_.bc_far, f32[1024,32]{1,0:T(8,128)} %get-tuple-element.26.refs_3_, f32[32,1024]{1,0:T(8,128)} %get-tuple-element.27.refs_4_, ...), custom_call_target="tpu_custom_call" | custom-call | flops 1 | bytes 1 | tf_op jit(solution)/shard_map/scan_part/pallas_call | solution.py:374
  43.6 5.5 %all-to-all-done.states = bf16[8,144,256]{2,1,0:T(8,128)(2,1)S(1)} async-done(((bf16[8,144,256]{2,1,0:T(8,128)(2,1)}), bf16[8,144,256]{2,1,0:T(8,128)(2,1)S(1)}, u32[]{:S(2)}, u32[]{:S(2)}) %all-to-all-start) | async-done | bytes 589856 | tf_op jit(solution)/shard_map/all_to_all | solution.py:648
  49.9 3.7 %all-to-all-start.1 = ((bf16[8,128,256]{2,1,0:T(8,128)(2,1)}), bf16[8,128,256]{2,1,0:T(8,128)(2,1)S(1)}, u32[]{:S(2)}, u32[]{:S(2)}) async-start(bf16[8,128,256]{2,1,0:T(8,128)(2,1)} %prefix.1.refs_10_), calls=%async_computation.1 | async-start | bytes 1048576 | tf_op jit(solution)/shard_map/all_to_all | solution.py:653
  54.7 9.7 %scan_part.3._.refs_1_ = bf16[1024,2048]{1,0:T(8,128)(2,1)} custom-call(bf16[1024,2048]{1,0:T(8,128)(2,1)} %get-tuple-element.25.refs_0_, bf16[1024,2048]{1,0:T(8,128)(2,1)} %refs_1_.3, bf16[1024,512]{1,0:T(8,128)(2,1)} %get-tuple-element.23.refs_2_.bc_far, f32[1024,32]{1,0:T(8,128)} %get-tuple-element.26.refs_3_, f32[32,1024]{1,0:T(8,128)} %get-tuple-element.27.refs_4_, ...), custom_call_target="tpu_custom_call" | custom-call | flops 1 | bytes 1 | tf_op jit(solution)/shard_map/scan_part/pallas_call | solution.py:374
  64.4 3.9 %all-to-all-done.1.entering = bf16[8,128,256]{2,1,0:T(8,128)(2,1)S(1)} async-done(((bf16[8,128,256]{2,1,0:T(8,128)(2,1)}), bf16[8,128,256]{2,1,0:T(8,128)(2,1)S(1)}, u32[]{:S(2)}, u32[]{:S(2)}) %all-to-all-start.1) | async-done | bytes 524320 | tf_op jit(solution)/shard_map/all_to_all | solution.py:653
  68.2 2.8 %norm_rows.4._ = bf16[256,2048]{1,0:T(8,128)(2,1)S(1)} custom-call(s32[5]{0:T(128)S(1)} %stack.23.info, bf16[1024,512]{1,0:T(8,128)(2,1)} %get-tuple-element.23.refs_2_.bc_far, bf16[8,128,256]{2,1,0:T(8,128)(2,1)S(1)} %all-to-all-done.1.entering, f32[1,2048]{1,0:T(1,128)S(1)} %bitcast.16, bf16[1024,2048]{1,0:T(8,128)(2,1)} %scan_part.3._.refs_1_, ...), custom_call_target="tpu_custom_call" | custom-call | flops 1 | bytes 1 | tf_op jit(solution)/shard_map/norm_rows/pallas_call | solution.py:444
  71.1 2.8 %norm_rows.5.a0.a0_far = bf16[256,2048]{1,0:T(8,128)(2,1)S(1)} custom-call(s32[5]{0:T(128)S(1)} %stack.23.info, bf16[1024,512]{1,0:T(8,128)(2,1)} %get-tuple-element.23.refs_2_.bc_far, bf16[8,128,256]{2,1,0:T(8,128)(2,1)S(1)} %all-to-all-done.1.entering, f32[1,2048]{1,0:T(1,128)S(1)} %bitcast.17, bf16[256,2048]{1,0:T(8,128)(2,1)S(1)} %norm_rows.4._, ...), custom_call_target="tpu_custom_call" | custom-call | flops 1 | bytes 1 | tf_op jit(solution)/shard_map/norm_rows/pallas_call | solution.py:444
  74.0 4.6 %project.2._ = bf16[256,1024]{1,0:T(8,128)(2,1)S(1)} custom-call(bf16[256,2048]{1,0:T(8,128)(2,1)S(1)} %norm_rows.5.a0.a0_far, bf16[256,2048]{1,0:T(8,128)(2,1)S(1)} %collective-permute-done.1.a1.a1_far, bf16[2048,4096]{1,0:T(8,128)(2,1)} %w0_far.9, bf16[2048,4096]{1,0:T(8,128)(2,1)} %collective-permute-done.2.w1_far), custom_call_target="tpu_custom_call" | custom-call | flops 1 | bytes 1 | tf_op jit(solution)/shard_map/project/pallas_call | solution.py:502
  78.6 2.8 %norm_rows.6._ = bf16[256,2048]{1,0:T(8,128)(2,1)S(1)} custom-call(s32[5]{0:T(128)S(1)} %stack.23.info, bf16[1024,512]{1,0:T(8,128)(2,1)} %get-tuple-element.23.refs_2_.bc_far, bf16[8,128,256]{2,1,0:T(8,128)(2,1)S(1)} %all-to-all-done.1.entering, f32[1,2048]{1,0:T(1,128)S(1)} %bitcast.18, bf16[256,1024]{1,0:T(8,128)(2,1)S(1)} %project.2._, ...), custom_call_target="tpu_custom_call" | custom-call | flops 1 | bytes 1 | tf_op jit(solution)/shard_map/norm_rows/pallas_call | solution.py:444
  82.0 1.5 %collective-permute-start.7 = (bf16[256,1024]{1,0:T(8,128)(2,1)S(1)}, bf16[256,1024]{1,0:T(8,128)(2,1)S(1)}, u32[]{:S(2)}, u32[]{:S(2)}) collective-permute-start(bf16[256,1024]{1,0:T(8,128)(2,1)S(1)} %project.2._), channel_id=1, source_target_pairs={{0,2},{1,3},{2,0},{3,1},{4,6},{5,7},{6,4},{7,5},{8,10},{9,11},{10,... | collective-permute-start | bytes 1572872 | tf_op jit(solution)/shard_map/ppermute | solution.py:605
  83.5 2.8 %norm_rows.7.a0_near.a0 = bf16[256,2048]{1,0:T(8,128)(2,1)S(1)} custom-call(s32[5]{0:T(128)S(1)} %stack.23.info, bf16[1024,512]{1,0:T(8,128)(2,1)} %get-tuple-element.23.refs_2_.bc_far, bf16[8,128,256]{2,1,0:T(8,128)(2,1)S(1)} %all-to-all-done.1.entering, f32[1,2048]{1,0:T(1,128)S(1)} %bitcast.19, bf16[256,2048]{1,0:T(8,128)(2,1)S(1)} %norm_rows.6._, ...), custom_call_target="tpu_custom_call" | custom-call | flops 1 | bytes 1 | tf_op jit(solution)/shard_map/norm_rows/pallas_call | solution.py:444
  86.3 6.9 %project_both.5 = (bf16[256,1024]{1,0:T(8,128)(2,1)S(1)}, f32[256,1024]{1,0:T(8,128)S(1)}) custom-call(bf16[256,2048]{1,0:T(8,128)(2,1)S(1)} %norm_rows.5.a0.a0_far, bf16[256,2048]{1,0:T(8,128)(2,1)S(1)} %collective-permute-done.1.a1.a1_far, bf16[256,2048]{1,0:T(8,128)(2,1)S(1)} %norm_rows.7.a0_near.a0, ...), custom_call_target="tpu_custom_call" | custom-call | flops 1 | bytes 1 | tf_op jit(solution)/shard_map/project_both/pallas_call | solution.py:560
  93.8 6.8 %project_both.4 = (bf16[256,1024]{1,0:T(8,128)(2,1)S(1)}, f32[256,1024]{1,0:T(8,128)S(1)}) custom-call(bf16[256,2048]{1,0:T(8,128)(2,1)S(1)} %norm_rows.5.a0.a0_far, bf16[256,2048]{1,0:T(8,128)(2,1)S(1)} %collective-permute-done.1.a1.a1_far, bf16[256,2048]{1,0:T(8,128)(2,1)S(1)} %norm_rows.7.a0_near.a0, ...), custom_call_target="tpu_custom_call" | custom-call | flops 1 | bytes 1 | tf_op jit(solution)/shard_map/project_both/pallas_call | solution.py:560
  100.6 1.6 %collective-permute-start.5 = (bf16[256,1024]{1,0:T(8,128)(2,1)S(1)}, bf16[256,1024]{1,0:T(8,128)(2,1)S(1)}, u32[]{:S(2)}, u32[]{:S(2)}) collective-permute-start(bf16[256,1024]{1,0:T(8,128)(2,1)S(1)} %get-tuple-element.34), channel_id=1, source_target_pairs={{0,2},{1,3},{2,0},{3,1},{4,6},{5,7},{6,4},{7,5},{8,10},{9,11},{10,... | collective-permute-start | bytes 1572872 | tf_op jit(solution)/shard_map/ppermute | solution.py:605
  102.2 6.8 %project_both.3 = (bf16[256,1024]{1,0:T(8,128)(2,1)S(1)}, f32[256,1024]{1,0:T(8,128)S(1)}) custom-call(bf16[256,2048]{1,0:T(8,128)(2,1)S(1)} %norm_rows.5.a0.a0_far, bf16[256,2048]{1,0:T(8,128)(2,1)S(1)} %collective-permute-done.1.a1.a1_far, bf16[256,2048]{1,0:T(8,128)(2,1)S(1)} %norm_rows.7.a0_near.a0, ...), custom_call_target="tpu_custom_call" | custom-call | flops 1 | bytes 1 | tf_op jit(solution)/shard_map/project_both/pallas_call | solution.py:560
  109.6 5.3 %project.3._ = bf16[256,4096]{1,0:T(8,128)(2,1)} custom-call(bf16[256,2048]{1,0:T(8,128)(2,1)S(1)} %norm_rows.7.a0_near.a0, bf16[256,2048]{1,0:T(8,128)(2,1)S(1)} %collective-permute-done.3.a1_near.a1, bf16[2048,4096]{1,0:T(8,128)(2,1)} %w0_far.9, bf16[2048,4096]{1,0:T(8,128)(2,1)} %collective-permute-done.2.w1_far, ...), custom_call_target="tpu_custom_call" | custom-call | flops 1 | bytes 1 | tf_op jit(solution)/shard_map/project/pallas_call | solution.py:502
  115.9 3.4 %collective-permute-done.5.arrived = bf16[256,1024]{1,0:T(8,128)(2,1)S(1)} collective-permute-done((bf16[256,1024]{1,0:T(8,128)(2,1)S(1)}, bf16[256,1024]{1,0:T(8,128)(2,1)S(1)}, u32[]{:S(2)}, u32[]{:S(2)}) %collective-permute-start.5) | collective-permute-done | bytes 524320 | tf_op jit(solution)/shard_map/ppermute | solution.py:605
  120.2 9.4 %collective-permute-done.4.arrived = bf16[256,1024]{1,0:T(8,128)(2,1)S(1)} collective-permute-done((bf16[256,1024]{1,0:T(8,128)(2,1)S(1)}, bf16[256,1024]{1,0:T(8,128)(2,1)S(1)}, u32[]{:S(2)}, u32[]{:S(2)}) %collective-permute-start.4) | collective-permute-done | bytes 524320 | tf_op jit(solution)/shard_map/ppermute | solution.py:605
  (39 shorter events, 14.4 us)
Async XLA Ops:
  0.0 74.0 %collective-permute-start.2 = (bf16[2048,4096]{1,0:T(8,128)(2,1)}, bf16[2048,4096]{1,0:T(8,128)(2,1)}, u32[]{:S(2)}, u32[]{:S(2)}) collective-permute-start(bf16[2048,4096]{1,0:T(8,128)(2,1)} %w0_far.9), channel_id=1, source_target_pairs={{0,1},{1,0},{2,3},{3,2},{4,5},{5,4},{6,7},{7,6},{8,9},{9,8},{10,11... | collective-permute-start | bytes 50331656 | tf_op jit(solution)/shard_map/ppermute | solution.py:605
  2.1 10.0 %collective-permute-start = (bf16[16,2560]{1,0:T(8,128)(2,1)S(1)}, bf16[16,2560]{1,0:T(8,128)(2,1)S(1)}, u32[]{:S(2)}, u32[]{:S(2)}) collective-permute-start(bf16[16,2560]{1,0:T(8,128)(2,1)S(1)} %pad_maximum_fusion), channel_id=1, source_target_pairs={{0,4},{4,8},{8,12},{12,16},{16,20},{20,24},{24,28},{28,0},{1,5},{5... | collective-permute-start | bytes 245768 | tf_op jit(solution)/shard_map/ppermute | solution.py:601
  6.1 1.0 copy-start.1
  7.0 0.9 copy-start.4
  7.9 0.9 copy-start.5
  8.8 0.7 copy-start.9
  12.1 1.0 copy-start.2
  13.0 0.8 copy-start.7
  13.8 0.7 copy-start.8
  27.8 21.2 %all-to-all-start = ((bf16[8,144,256]{2,1,0:T(8,128)(2,1)}), bf16[8,144,256]{2,1,0:T(8,128)(2,1)S(1)}, u32[]{:S(2)}, u32[]{:S(2)}) async-start(bf16[8,144,256]{2,1,0:T(8,128)(2,1)} %get-tuple-element.24.refs_10_), calls=%async_computation | async-start | bytes 1179648 | tf_op jit(solution)/shard_map/all_to_all | solution.py:648
  32.8 1.1 copy-start.3
  49.9 18.3 %all-to-all-start.1 = ((bf16[8,128,256]{2,1,0:T(8,128)(2,1)}), bf16[8,128,256]{2,1,0:T(8,128)(2,1)S(1)}, u32[]{:S(2)}, u32[]{:S(2)}) async-start(bf16[8,128,256]{2,1,0:T(8,128)(2,1)} %prefix.1.refs_10_), calls=%async_computation.1 | async-start | bytes 1048576 | tf_op jit(solution)/shard_map/all_to_all | solution.py:653
  53.6 1.1 copy-start
  54.7 13.6 %copy-start.6 = (f32[2048]{0:T(1024)S(1)}, f32[2048]{0:T(1024)}, u32[]{:S(2)}) copy-start(f32[2048]{0:T(1024)} %param.19) | copy-start | bytes 24580
  71.1 2.9 %collective-permute-start.1 = (bf16[256,2048]{1,0:T(8,128)(2,1)S(1)}, bf16[256,2048]{1,0:T(8,128)(2,1)S(1)}, u32[]{:S(2)}, u32[]{:S(2)}) collective-permute-start(bf16[256,2048]{1,0:T(8,128)(2,1)S(1)} %norm_rows.4._), channel_id=1, source_target_pairs={{0,1},{1,0},{2,3},{3,2},{4,5},{5,4},{6,7},{7,6},{8,9},{9,8},{10,11... | collective-permute-start | bytes 3145736 | tf_op jit(solution)/shard_map/ppermute | solution.py:605
  81.4 4.9 %collective-permute-start.3 = (bf16[256,2048]{1,0:T(8,128)(2,1)S(1)}, bf16[256,2048]{1,0:T(8,128)(2,1)S(1)}, u32[]{:S(2)}, u32[]{:S(2)}) collective-permute-start(bf16[256,2048]{1,0:T(8,128)(2,1)S(1)} %norm_rows.6._), channel_id=1, source_target_pairs={{0,1},{1,0},{2,3},{3,2},{4,5},{5,4},{6,7},{7,6},{8,9},{9,8},{10,11... | collective-permute-start | bytes 3145736 | tf_op jit(solution)/shard_map/ppermute | solution.py:605
  82.0 27.6 %collective-permute-start.7 = (bf16[256,1024]{1,0:T(8,128)(2,1)S(1)}, bf16[256,1024]{1,0:T(8,128)(2,1)S(1)}, u32[]{:S(2)}, u32[]{:S(2)}) collective-permute-start(bf16[256,1024]{1,0:T(8,128)(2,1)S(1)} %project.2._), channel_id=1, source_target_pairs={{0,2},{1,3},{2,0},{3,1},{4,6},{5,7},{6,4},{7,5},{8,10},{9,11},{10,... | collective-permute-start | bytes 1572872 | tf_op jit(solution)/shard_map/ppermute | solution.py:605
  93.2 21.8 %collective-permute-start.6 = (bf16[256,1024]{1,0:T(8,128)(2,1)S(1)}, bf16[256,1024]{1,0:T(8,128)(2,1)S(1)}, u32[]{:S(2)}, u32[]{:S(2)}) collective-permute-start(bf16[256,1024]{1,0:T(8,128)(2,1)S(1)} %get-tuple-element.36), channel_id=1, source_target_pairs={{0,2},{1,3},{2,0},{3,1},{4,6},{5,7},{6,4},{7,5},{8,10},{9,11},{10,... | collective-permute-start | bytes 1572872 | tf_op jit(solution)/shard_map/ppermute | solution.py:605
  100.6 18.7 %collective-permute-start.5 = (bf16[256,1024]{1,0:T(8,128)(2,1)S(1)}, bf16[256,1024]{1,0:T(8,128)(2,1)S(1)}, u32[]{:S(2)}, u32[]{:S(2)}) collective-permute-start(bf16[256,1024]{1,0:T(8,128)(2,1)S(1)} %get-tuple-element.34), channel_id=1, source_target_pairs={{0,2},{1,3},{2,0},{3,1},{4,6},{5,7},{6,4},{7,5},{8,10},{9,11},{10,... | collective-permute-start | bytes 1572872 | tf_op jit(solution)/shard_map/ppermute | solution.py:605
  109.0 20.6 %collective-permute-start.4 = (bf16[256,1024]{1,0:T(8,128)(2,1)S(1)}, bf16[256,1024]{1,0:T(8,128)(2,1)S(1)}, u32[]{:S(2)}, u32[]{:S(2)}) collective-permute-start(bf16[256,1024]{1,0:T(8,128)(2,1)S(1)} %get-tuple-element.32), channel_id=1, source_target_pairs={{0,2},{1,3},{2,0},{3,1},{4,6},{5,7},{6,4},{7,5},{8,10},{9,11},{10,... | collective-permute-start | bytes 1572872 | tf_op jit(solution)/shard_map/ppermute | solution.py:605

commit v8 on v5

--- a/solution.py
+++ b/solution.py
@@ -15,7 +15,7 @@
 LOG2E = 1.4426950408889634
 
 TOK_A = 256
-ROWS_A = 64
+ROWS_A = 32
 TOK_B = 128
 STEP_B = 256
 EXTRA = 16
@@ -45,8 +45,12 @@
     return lax.dot_general(a, b, (dims, ((), ())), precision=precision, preferred_element_type=F32)
 
 
-def half_silu(half):
-    return half + half * jnp.tanh(half)
+def silu(v):
+    return v * pl.reciprocal(1.0 + jnp.exp2(v * -LOG2E), approx=True)
+
+
+def far(*arrays):
+    return [pltpu.with_memory_space_constraint(a, pltpu.HBM) for a in arrays]
 
 
 def whole(shape):
@@ -118,6 +122,33 @@
     )(log_decay.T, step.T, skip[None, :], ones)
 
 
+def tail_kernel(x, bc, out):
+    width, bc_width = x.shape[1], bc.shape[2]
+    out[:, 0:width] = x[...]
+    for g in range(bc.shape[1]):
+        out[:, width + g * bc_width : width + (g + 1) * bc_width] = bc[:, g, :]
+
+
+def tail_rows(x, bc):
+    length, width = x.shape
+    groups, bc_width = bc.shape[1:]
+    at = length // LEAD - 1
+    shape = (LEAD, width + groups * bc_width)
+    return pl.pallas_call(
+        tail_kernel,
+        grid=(1,),
+        in_specs=[
+            pl.BlockSpec((LEAD, width), lambda i: (at, 0)),
+            pl.BlockSpec((LEAD, groups, bc_width), lambda i: (at, 0, 0)),
+        ],
+        out_specs=whole(shape),
+        out_shape=jax.ShapeDtypeStruct(shape, BF16),
+        compiler_params=params(8),
+        cost_estimate=CHEAP,
+        name="tail_rows",
+    )(x, bc)
+
+
 def put_message(ref, state, decay):
     high = decay.astype(BF16)
     low = (decay - high.astype(F32)).astype(BF16)
@@ -148,12 +179,6 @@
         fetch(0).start()
         state[...] = jnp.zeros_like(state)
 
-    fetch(i).wait()
-
-    @pl.when(i + 1 < pl.num_programs(0))
-    def _():
-        fetch(i + 1).start()
-
     base = pl.multiple_of(i * rows, rows)
     before = pl.ds(pl.multiple_of(jnp.maximum(base - LEAD, 0), LEAD), LEAD)
 
@@ -161,7 +186,7 @@
         return pl.ds(pl.multiple_of(base + r, ROWS_A), ROWS_A)
 
     def conv(src, lead, weights, emit):
-        w0, w1, w2, w3 = [w * 0.5 for w in weights]
+        w0, w1, w2, w3 = weights
         back = LEAD - 8
         r1 = pltpu.roll(lead, 1, 0)
         last_x, last_p = lead[back:], (w1 * lead + w0 * r1)[back:]
@@ -170,10 +195,15 @@
             r1 = pltpu.roll(jnp.concatenate([last_x, cur], 0), 1, 0)[8:]
             p = w1 * cur + w0 * r1
             p2 = pltpu.roll(jnp.concatenate([last_p, p], 0), 2, 0)[8:]
-            emit(r, half_silu((w3 * cur + w2 * r1) + p2))
+            emit(r, silu((w3 * cur + w2 * r1) + p2))
             last_x, last_p = cur[ROWS_A - 8 :], p[ROWS_A - 8 :]
 
     start = i == 0
+
+    def halo_of(lanes):
+        value = halo[:, lanes]
+        return jnp.where(info[6] == 0, jnp.zeros_like(value), value)
+
     for c in range(groups):
         for lanes in range(c * 2 * N, (c + 1) * 2 * N, N):
             ds = slice(lanes, lanes + N)
@@ -181,23 +211,28 @@
             def emit_bc(r, value):
                 bc_out[r : r + ROWS_A, ds] = value.astype(BF16)
 
-            lead = jnp.where(start, halo[:, width + lanes : width + lanes + N], bc[before, ds]).astype(F32)
+            lead = jnp.where(start, halo_of(slice(width + lanes, width + lanes + N)), bc[before, ds]).astype(F32)
             inner = slice(lanes - c * 2 * N, lanes - c * 2 * N + N)
             conv(lambda r: bc[at(r), ds], lead, [wbc[k, c : c + 1, inner] for k in range(KCONV)], emit_bc)
+
+    fetch(i).wait()
+
+    @pl.when(i + 1 < pl.num_programs(0))
+    def _():
+        fetch(i + 1).start()
 
     def slab(c, _):
         first = pl.multiple_of(c * SLAB, SLAB)
         scale = dot(f_dev[pl.ds(base, rows), :], ones[:, pl.ds(first, SLAB)])
-        for sub in range(0, SLAB, N):
-            ds = pl.ds(pl.multiple_of(first + sub, N), N)
-
-            def emit(r, value):
-                value = value.astype(BF16)
-                x_out[r : r + ROWS_A, ds] = value
-                xf[r : r + ROWS_A, ds] = (value.astype(F32) * scale[r : r + ROWS_A, sub : sub + N]).astype(BF16)
-
-            lead = jnp.where(start, halo[:, ds], x[before, ds]).astype(F32)
-            conv(lambda r: x[at(r), ds], lead, [wx[k : k + 1, ds] for k in range(KCONV)], emit)
+        ds = pl.ds(first, SLAB)
+
+        def emit(r, value):
+            value = value.astype(BF16)
+            x_out[r : r + ROWS_A, ds] = value
+            xf[r : r + ROWS_A, ds] = (value.astype(F32) * scale[r : r + ROWS_A]).astype(BF16)
+
+        lead = jnp.where(start, halo_of(ds), x[before, ds]).astype(F32)
+        conv(lambda r: x[at(r), ds], lead, [wx[k : k + 1, ds] for k in range(KCONV)], emit)
         return 0
 
     lax.fori_loop(0, width // SLAB, slab, 0)
@@ -418,7 +453,7 @@
                 within.append(dot(jnp.concatenate(tables, 1), stacked))
             xs = xb.astype(F32)
             y = jnp.concatenate(within, 1) + carried + skip[:, lanes] * xs
-            gate = half_silu((z[at, lanes] * 0.5).astype(F32))
+            gate = silu(z[at, lanes].astype(F32))
             uv_out[at, lanes] = (y * gate).astype(BF16)
             uv_out[at, width + s * SLAB : width + (s + 1) * SLAB] = (gate * rise * lead_rows[:, lanes]).astype(BF16)
             xf = (xs * dot(f_blk[at, :], sel)).astype(BF16)
@@ -447,7 +482,7 @@
     )(x, z, bc, cum, cum_s, log_s, f_blk, e_blk, rates, ones, token)
 
 
-def norm_kernel(slot, info, bc, keep, recv, gain, _, *refs):
+def norm_kernel(slots, info, bc, keep, recv, gain, _, *refs):
     uvs, out = refs[:-1], refs[-1]
     count, width = out.shape
     groups = bc.shape[1] // (2 * N)
@@ -455,10 +490,10 @@
     half = width // 2
     part = width // B_PARTS
     is_odd = info[0] == 1
-    base = info[slot] * count
-
-    def rows(j, _):
-        to = pl.ds(pl.multiple_of(j * ROWS_C, ROWS_C), ROWS_C)
+    count = count // len(slots)
+
+    def rows(j, first, base):
+        to = pl.ds(pl.multiple_of(first + j * ROWS_C, ROWS_C), ROWS_C)
         at = pl.ds(pl.multiple_of(base + j * ROWS_C, ROWS_C), ROWS_C)
         for g in range(groups):
             c_mat = bc[at, 2 * N * g + N : 2 * N * (g + 1)]
@@ -477,24 +512,29 @@
             scale = lax.rsqrt(squares * (1.0 / per) + EPS)
             for start, gated in pieces:
                 out[to, start : start + part] = (gated * scale * gain[:, start : start + part]).astype(BF16)
-        return 0
-
-    lax.fori_loop(0, count // ROWS_C, rows, 0)
-
-
-def norm_rows(slot, info, count, token, bc, keep, recv, gain, uvs):
+
+    for k, slot in enumerate(slots):
+
+        def step(j, _):
+            rows(j, k * count, info[slot] * count)
+            return 0
+
+        lax.fori_loop(0, count // ROWS_C, step, 0)
+
+
+def norm_rows(slots, info, count, token, bc, keep, recv, gain, uvs):
     return pl.pallas_call(
-        functools.partial(norm_kernel, slot),
+        functools.partial(norm_kernel, slots),
         in_specs=[SCALAR] + [FULL] * 4 + [ANY] + [FULL] * len(uvs),
         out_specs=FULL,
-        out_shape=jax.ShapeDtypeStruct((count, gain.shape[1]), BF16),
+        out_shape=jax.ShapeDtypeStruct((len(slots) * count, gain.shape[1]), BF16),
         compiler_params=params(16),
         cost_estimate=CHEAP,
         name="norm_rows",
     )(info, bc, keep, recv, gain, token, *uvs)
 
 
-def project_kernel(base, added, a0, a1, w0_far, w1_far, *refs):
+def project_kernel(base, mine, added, a0, a1, w0_far, w1_far, *refs):
     out, w0, w1, sem = refs[-4:]
     j = pl.program_id(0)
     tiles = pl.num_programs(0)
@@ -522,14 +562,14 @@
     for copy in fetch(j):
         copy.wait()
     slot = lax.rem(j, SLOTS)
-    total = dot(a0[...], w0[slot]) + dot(a1[...], w1[slot])
+    total = dot(a0[mine, :], w0[slot]) + dot(a1[mine, :], w1[slot])
     if added:
         total = total + refs[0][...].astype(F32)
     out[...] = total.astype(out.dtype)
 
 
-def project(a0, a1, w0, w1, first, count, kind, arrived=None, result=None):
-    rows, depth = a0.shape
+def project(half, a0, a1, w0, w1, first, count, kind, arrived=None, result=None):
+    rows, depth = a0.shape[0] // 2, a0.shape[1]
     base = first // TILE
     full = arrived is not None
     operands, specs = [a0, a1, w0, w1], [FULL, FULL, FAR, FAR]
@@ -540,7 +580,7 @@
         operands.append(result)
         specs.append(ANY)
     return pl.pallas_call(
-        functools.partial(project_kernel, base, full),
+        functools.partial(project_kernel, base, slice(half * rows, (half + 1) * rows), full),
         grid=(count // TILE,),
         in_specs=specs,
         out_specs=pl.BlockSpec((rows, TILE), lambda j: (0, base + j if full else j)),
@@ -557,7 +597,7 @@
     )(*operands)
 
 
-def project_both_kernel(base, a0_far, a1_far, a0_near, a1_near, w0_far, w1_far, far, near, a0, a1, w0, w1, sem):
+def project_both_kernel(base, a0, a1, w0_far, w1_far, far, near, w0, w1, sem):
     j = pl.program_id(0)
     tiles = pl.num_programs(0)
     rows = far.shape[0]
@@ -580,10 +620,6 @@
     def _():
         for t in range(SLOTS - 1):
             start(t)
-        a0[0:rows, :] = a0_far[...]
-        a0[rows:, :] = a0_near[...]
-        a1[0:rows, :] = a1_far[...]
-        a1[rows:, :] = a1_near[...]
 
     start(j + SLOTS - 1)
     for copy in fetch(j):
@@ -594,18 +630,16 @@
     near[...] = total[rows:]
 
 
-def project_both(far, far_mate, near, near_mate, w0, w1, first, count):
-    rows, depth = far.shape
+def project_both(a0, a1, w0, w1, first, count):
+    rows, depth = a0.shape[0] // 2, a0.shape[1]
     placed = pl.BlockSpec((rows, TILE), lambda j: (0, j))
     return pl.pallas_call(
         functools.partial(project_both_kernel, first // TILE),
         grid=(count // TILE,),
-        in_specs=[FULL] * 4 + [FAR] * 2,
+        in_specs=[FULL] * 2 + [FAR] * 2,
         out_specs=[placed, placed],
         out_shape=[jax.ShapeDtypeStruct((rows, count), BF16), jax.ShapeDtypeStruct((rows, count), F32)],
         scratch_shapes=[
-            pltpu.VMEM((2 * rows, depth), BF16),
-            pltpu.VMEM((2 * rows, depth), BF16),
             pltpu.VMEM((SLOTS, depth, TILE), BF16),
             pltpu.VMEM((SLOTS, depth, TILE), BF16),
             pltpu.SemaphoreType.DMA((2, SLOTS)),
@@ -613,7 +647,7 @@
         compiler_params=params(24),
         cost_estimate=CHEAP,
         name="project_both",
-    )(far, far_mate, near, near_mate, w0, w1)
+    )(a0, a1, w0, w1)
 
 
 def add_kernel(part, arrived, _, out):
@@ -645,10 +679,9 @@
     return lax.ppermute(block, axis, [(i, i ^ bit) for i in range(lax.axis_size(axis))])
 
 
-def rotate(block, turns, sends):
-    pairs = lax.axis_size("seq") // 2
-    route = [(2 * q + y, 2 * ((q + turns) % pairs) + y) for q in range(pairs) if sends(q) for y in (0, 1)]
-    return lax.ppermute(block, "seq", route)
+def rotate(block, distance):
+    size = lax.axis_size("seq")
+    return lax.ppermute(block, "seq", [(i, (i + distance) % size) for i in range(size)])
 
 
 def log_steps(info, got, keep, rates, done, pairs, scan_next):
@@ -709,11 +742,12 @@
     mine = lax.axis_index("head")
     half = width // 2
     seq = lax.axis_index("seq")
-    info = jnp.stack([seq & 1, mine ^ 3, mine ^ 2, mine ^ 1, mine, seq >> 1]).astype(jnp.int32)
-
-    x_far, z_far, w_far = [pltpu.with_memory_space_constraint(v, pltpu.HBM) for v in (x_input, z_input, out_weight)]
+    info = jnp.stack([seq & 1, mine ^ 3, mine ^ 2, mine ^ 1, mine, seq >> 1, seq]).astype(jnp.int32)
+
+    x_far, z_far, w_far = far(x_input, z_input, out_weight)
+    (bc_far,) = far(bc_input)
+    halo = rotate(tail_rows(x_far, bc_far), 1)
     bc = bc_input.reshape(length, -1)
-    halo = shift(jnp.concatenate([x_input[length - LEAD :], bc[length - LEAD :]], 1), 1)
     weight_mate = swap(out_weight, "head", 1)
 
     ones = jnp.asarray(np.tile(np.repeat(np.eye(heads), P_SIZE, axis=1), (2, 1)), BF16)
@@ -722,7 +756,7 @@
         info, x_far, bc, halo, conv_weight_x, conv_weight_bc, f_dev, ones, rates
     )
 
-    x_conv = pltpu.with_memory_space_constraint(x_conv, pltpu.HBM)
+    (x_conv,) = far(x_conv)
     uvs = []
 
     def scan_next(token):
@@ -748,7 +782,7 @@
             "pair",
             [pltpu.VMEM(*message)],
         )
-        parts = list(parts[:1]) + [rotate(parts[r], r, lambda q: q < pairs - 1) for r in range(1, pairs)]
+        parts = list(parts[:1]) + [rotate(parts[r], 2 * r) for r in range(1, pairs)]
         done = scan_next(parts[0])
         parts = combine(
             owner_kernel,
@@ -759,7 +793,7 @@
             [pltpu.VMEM((pairs, N + EXTRA, piece), BF16), pltpu.VMEM((pairs, N, piece), BF16)],
         )
         ready = parts[0]
-        parts = list(parts[:1]) + [rotate(parts[r], r, lambda q: (q + r) % pairs > 0) for r in range(1, pairs)]
+        parts = list(parts[:1]) + [rotate(parts[r], 2 * r) for r in range(1, pairs)]
         done = scan_next(ready)
         back, held = combine(
             last_split_kernel,
@@ -778,26 +812,22 @@
     count = length // ways
     gain = norm_gain[None, :]
 
-    def rows_for(slot, token):
-        return norm_rows(slot, info, count, token, bc_conv, held, other, gain, uvs)
-
-    far_mate = rows_for(1, held)
-    far = rows_for(2, far_mate)
-    far_mate = swap(far_mate, "head", 1)
+    def rows_for(token, *slots):
+        return norm_rows(slots, info, count, token, bc_conv, held, other, gain, uvs)
+
+    mates = rows_for(held, 1, 3)
+    owns = rows_for(mates, 2, 4)
+    operands = (owns, swap(mates, "head", 1), w_far, weight_mate)
     columns = out_weight.shape[1]
     quarter = columns // 4
-    weights = (w_far, weight_mate)
-    sent = project(far, far_mate, *weights, 0, quarter, BF16)
+    sent = project(0, *operands, 0, quarter, BF16)
     arrivals = [swap(sent, "head", 2)]
-    near_mate = rows_for(3, sent)
-    near = rows_for(4, near_mate)
-    near_mate = swap(near_mate, "head", 1)
     parts = []
     for c in range(quarter, columns, quarter):
-        sent, part = project_both(far, far_mate, near, near_mate, *weights, c, quarter)
+        sent, part = project_both(*operands, c, quarter)
         arrivals.append(swap(sent, "head", 2))
         parts.append(part)
-    result = project(near, near_mate, *weights, 0, quarter, BF16, arrivals[0])
+    result = project(1, *operands, 0, quarter, BF16, arrivals[0])
     for c, part in enumerate(parts, 1):
         result = add_chunk(part, arrivals[c], result, c * quarter)
     return result

time: 133 us -> 121 us (0.910)
  starting transfers between devices: 33.3 us -> 16.8 us
  waiting for transfers between devices: 18.7 us -> 27 us
  local copies, waits for them, and re-layouts: 3.15 us -> 0.35 us
    ppermute x7, starting transfers between devices: 25.3 us -> 11.5 us  [rotate(): lax.ppermute(block, 'seq', [(i, (i + distance) % size) for i in range(siz...]
    ppermute x7, waiting for transfers between devices: 0.02 us -> 4.4 us  [rotate(): lax.ppermute(block, 'seq', [(i, (i + distance) % size) for i in range(siz...]
    ppermute x9 -> x8, waiting for transfers between devices: 18.7 us -> 22.6 us  [swap(): lax.ppermute(block, axis, [(i, i ^ bit) for i in range(lax.axis_size(axis...]
    ppermute x9 -> x8, starting transfers between devices: 7.99 us -> 5.26 us  [swap(): lax.ppermute(block, axis, [(i, i ^ bit) for i in range(lax.axis_size(axis...]
    slice x2 -> x0, local copies, waits for them, and re-layouts: 1.58 us -> none  [the longest x1 0.85 us: local(): x_input[length - LEAD:]]
    pallas_call x6 -> x5, Pallas kernels: 16 us -> 16.5 us  [the longest x2 9.94 us: project(): pl.pallas_call(functools.partial(project_kernel, base, slice(half * rows,...]
  transfers between devices with their start and end apart: 16 -> 15, of which waited for: 5 -> 6; matrix products, arithmetic and copies ran while one was open for 3% -> 0% of each run, Pallas kernels for 52% -> 59%
where the time goes in v8:
time: 121 us; the launch traced here: 120 us
  Pallas kernels  75.9 us (63%)
  waiting for transfers between devices  27 us (22%)
  starting transfers between devices  16.8 us (14%)
    ppermute x8, waiting for transfers between devices, swap(): lax.ppermute(block, axis, [(i, i ^ bit) for i in range(lax.axis_size(axis...  22.6 us
    pallas_call x3, Pallas kernels, project_both(): pl.pallas_call(functools.partial(project_both_kernel, first // TILE), gri...  20.5 us
    pallas_call x4, Pallas kernels, scan_part(): pl.pallas_call(functools.partial(scan_kernel, part), in_specs=[FAR, FAR]...  19.2 us
    pallas_call x1, Pallas kernels, conv_states(): pl.pallas_call(conv_kernel, grid=(length // TOK_A,), in_specs=[SCALAR, FA...  13.3 us
    ppermute x7, starting transfers between devices, rotate(): lax.ppermute(block, 'seq', [(i, (i + distance) % size) for i in range(siz...  11.5 us
    pallas_call x2, Pallas kernels, project(): pl.pallas_call(functools.partial(project_kernel, base, slice(half * rows,...  9.94 us
    ppermute x8, starting transfers between devices, swap(): lax.ppermute(block, axis, [(i, i ^ bit) for i in range(lax.axis_size(axis...  5.26 us
    pallas_call x2, Pallas kernels, norm_rows(): pl.pallas_call(functools.partial(norm_kernel, slots), in_specs=[SCALAR] +...  5.05 us
  transfers between devices with their start and end apart: 15, of which 6 were waited for; matrix products, arithmetic and copies ran while one was open for 0% of the time, Pallas kernels for 59%

profile of v8, /device:TPU:0, one launch (start us, length us, event | category | flops | bytes accessed | tf_op | source)
XLA Modules:
  0.0 120.4 jit_solution(15800755877747746202)
XLA Ops:
  0.5 1.5 %tail_rows.1 = bf16[16,2560]{1,0:T(8,128)(2,1)} custom-call(bf16[1024,2048]{1,0:T(8,128)(2,1)} %x_far.1, bf16[1024,2,256]{2,1,0:T(2,128)(2,1)} %bc.1), custom_call_target="tpu_custom_call" | custom-call | flops 1 | bytes 1 | tf_op jit(solution)/shard_map/tail_rows/pallas_call | solution.py:137
  2.0 2.7 %collective-permute-start = (bf16[16,2560]{1,0:T(8,128)(2,1)}, bf16[16,2560]{1,0:T(8,128)(2,1)S(1)}, u32[]{:S(2)}, u32[]{:S(2)}) collective-permute-start(bf16[16,2560]{1,0:T(8,128)(2,1)} %tail_rows.1), channel_id=1, source_target_pairs={{0,4},{4,8},{8,12},{12,16},{16,20},{20,24},{24,28},{28,0},{1,5},{5... | collective-permute-start | bytes 245768 | tf_op jit(solution)/shard_map/ppermute | solution.py:684
  4.9 1.5 %decays.1 = (f32[1024,32]{1,0:T(8,128)S(1)}, f32[32,1024]{1,0:T(8,128)S(1)}, f32[32,1024]{1,0:T(8,128)S(1)}, bf16[1024,64]{1,0:T(8,128)(2,1)S(1)}, bf16[1024,64]...) custom-call(f32[32,1024]{1,0:T(8,128)S(1)} %bitcast.14, f32[32,1024]{1,0:T(8,128)S(1)} %bitcast.15, ...), custom_call_target="tpu_custom_call" | custom-call | tf_op jit(solution)/shard_map/decays/pallas_call | solution.py:109
  6.6 4.4 %collective-permute-done.halo = bf16[16,2560]{1,0:T(8,128)(2,1)S(1)} collective-permute-done((bf16[16,2560]{1,0:T(8,128)(2,1)}, bf16[16,2560]{1,0:T(8,128)(2,1)S(1)}, u32[]{:S(2)}, u32[]{:S(2)}) %collective-permute-start) | collective-permute-done | bytes 81952 | tf_op jit(solution)/shard_map/ppermute | solution.py:684
  11.0 13.3 %conv_states.1 = (bf16[1024,2048]{1,0:T(8,128)(2,1)}, bf16[1024,512]{1,0:T(8,128)(2,1)S(1)}, f32[128,1024]{1,0:T(8,128)S(1)}, bf16[144,1024]{1,0:T(8,128)(2,1)S(1)}) custom-call(s32[7]{0:T(128)S(1)} %stack.31.info, bf16[1024,2048]{1,0:T(8,128)(2,1)} %x_far.1, bf16[1024,512]{1,0:T(8,128)(2,1)S(1)} %bitcast.13, ...), custom_call_target="tpu_custom_call" | custom-call | flops 1 | bytes 1 | tf_op jit(solution)/shard_map/conv_states/pallas_call | solution.py:258
  24.3 4.8 %scan_part.4._.refs_0_ = bf16[1024,1024]{1,0:T(8,128)(2,1)S(1)} custom-call(bf16[1024,2048]{1,0:T(8,128)(2,1)} %get-tuple-element.39.x_far, bf16[1024,2048]{1,0:T(8,128)(2,1)} %z_far.7, bf16[1024,512]{1,0:T(8,128)(2,1)S(1)} %get-tuple-element.36.bc_all.bc, f32[1024,32]{1,0:T(8,128)S(1)} %get-tuple-element.40.cum, f32[32,1024]{1,0:T(8,128)S(1)} %get-tuple-element.41.cum_s, ...), custom_call_target="tpu_custom_call" | custom-call | flops 1 | bytes 1 | tf_op jit(solution)/shard_map/scan_part/pallas_call | solution.py:468
  29.1 3.9 %collective-permute-done.1.got = bf16[144,1024]{1,0:T(8,128)(2,1)S(1)} collective-permute-done((bf16[144,1024]{1,0:T(8,128)(2,1)S(1)}, bf16[144,1024]{1,0:T(8,128)(2,1)S(1)}, u32[]{:S(2)}, u32[]{:S(2)}) %collective-permute-start.1) | collective-permute-done | bytes 294944 | tf_op jit(solution)/shard_map/ppermute | solution.py:679
  34.0 2.1 %collective-permute-start.3 = (bf16[144,256]{1,0:T(8,128)(2,1)S(1)}, bf16[144,256]{1,0:T(8,128)(2,1)S(1)}, u32[]{:S(2)}, u32[]{:S(2)}) collective-permute-start(bf16[144,256]{1,0:T(8,128)(2,1)S(1)} %get-tuple-element.49), channel_id=1, source_target_pairs={{0,16},{4,20},{8,24},{12,28},{16,0},{20,4},{24,8},{28,12},{1,17},{... | collective-permute-start | bytes 221192 | tf_op jit(solution)/shard_map/ppermute | solution.py:684
  36.1 1.7 %collective-permute-start.4 = (bf16[144,256]{1,0:T(8,128)(2,1)S(1)}, bf16[144,256]{1,0:T(8,128)(2,1)S(1)}, u32[]{:S(2)}, u32[]{:S(2)}) collective-permute-start(bf16[144,256]{1,0:T(8,128)(2,1)S(1)} %get-tuple-element.50), channel_id=1, source_target_pairs={{0,24},{4,28},{8,0},{12,4},{16,8},{20,12},{24,16},{28,20},{1,25},{... | collective-permute-start | bytes 221192 | tf_op jit(solution)/shard_map/ppermute | solution.py:684
  37.8 4.8 %scan_part.5.refs_4_.refs_1_ = bf16[1024,1024]{1,0:T(8,128)(2,1)S(1)} custom-call(bf16[1024,2048]{1,0:T(8,128)(2,1)} %get-tuple-element.39.x_far, bf16[1024,2048]{1,0:T(8,128)(2,1)} %z_far.7, bf16[1024,512]{1,0:T(8,128)(2,1)S(1)} %get-tuple-element.36.bc_all.bc, f32[1024,32]{1,0:T(8,128)S(1)} %get-tuple-element.40.cum, ...), custom_call_target="tpu_custom_call" | custom-call | flops 1 | bytes 1 | tf_op jit(solution)/shard_map/scan_part/pallas_call | solution.py:468
  44.1 1.7 %collective-permute-start.6 = (bf16[128,256]{1,0:T(8,128)(2,1)S(1)}, bf16[128,256]{1,0:T(8,128)(2,1)S(1)}, u32[]{:S(2)}, u32[]{:S(2)}) collective-permute-start(bf16[128,256]{1,0:T(8,128)(2,1)S(1)} %get-tuple-element.53), channel_id=1, source_target_pairs={{0,16},{4,20},{8,24},{12,28},{16,0},{20,4},{24,8},{28,12},{1,17},{... | collective-permute-start | bytes 196616 | tf_op jit(solution)/shard_map/ppermute | solution.py:684
  45.7 2.6 %collective-permute-start.7 = (bf16[128,256]{1,0:T(8,128)(2,1)S(1)}, bf16[128,256]{1,0:T(8,128)(2,1)S(1)}, u32[]{:S(2)}, u32[]{:S(2)}) collective-permute-start(bf16[128,256]{1,0:T(8,128)(2,1)S(1)} %get-tuple-element.54), channel_id=1, source_target_pairs={{0,24},{4,28},{8,0},{12,4},{16,8},{20,12},{24,16},{28,20},{1,25},{... | collective-permute-start | bytes 196616 | tf_op jit(solution)/shard_map/ppermute | solution.py:684
  48.3 4.8 %scan_part.6._.refs_2_ = bf16[1024,1024]{1,0:T(8,128)(2,1)S(1)} custom-call(bf16[1024,2048]{1,0:T(8,128)(2,1)} %get-tuple-element.39.x_far, bf16[1024,2048]{1,0:T(8,128)(2,1)} %z_far.7, bf16[1024,512]{1,0:T(8,128)(2,1)S(1)} %get-tuple-element.36.bc_all.bc, f32[1024,32]{1,0:T(8,128)S(1)} %get-tuple-element.40.cum, f32[32,1024]{1,0:T(8,128)S(1)} %get-tuple-element.41.cum_s, ...), custom_call_target="tpu_custom_call" | custom-call | flops 1 | bytes 1 | tf_op jit(solution)/shard_map/scan_part/pallas_call | solution.py:468
  54.3 4.8 %scan_part.7.refs_3_ = bf16[1024,1024]{1,0:T(8,128)(2,1)S(1)} custom-call(bf16[1024,2048]{1,0:T(8,128)(2,1)} %get-tuple-element.39.x_far, bf16[1024,2048]{1,0:T(8,128)(2,1)} %z_far.7, bf16[1024,512]{1,0:T(8,128)(2,1)S(1)} %get-tuple-element.36.bc_all.bc, f32[1024,32]{1,0:T(8,128)S(1)} %get-tuple-element.40.cum, f32[32,1024]{1,0:T(8,128)S(1)} %get-tuple-element.41.cum_s, ...), custom_call_target="tpu_custom_call" | custom-call | flops 1 | bytes 1 | tf_op jit(solution)/shard_map/scan_part/pallas_call | solution.py:468
  60.4 2.5 %norm_rows.2._ = bf16[512,2048]{1,0:T(8,128)(2,1)S(1)} custom-call(s32[7]{0:T(128)S(1)} %stack.31.info, bf16[1024,512]{1,0:T(8,128)(2,1)S(1)} %get-tuple-element.36.bc_all.bc, bf16[128,1024]{1,0:T(8,128)(2,1)S(1)} %get-tuple-element.55.keep._, bf16[128,1024]{1,0:T(8,128)(2,1)S(1)} %collective-permute-done.8.recv, f32[1,2048]{1,0:T(1,128)S(1)} %bitcast.16, ...), custom_call_target="tpu_custom_call" | custom-call | flops 1 | bytes 1 | tf_op jit(solution)/shard_map/norm_rows/pallas_call | solution.py:526
  63.0 2.5 %norm_rows.3.a0 = bf16[512,2048]{1,0:T(8,128)(2,1)S(1)} custom-call(s32[7]{0:T(128)S(1)} %stack.31.info, bf16[1024,512]{1,0:T(8,128)(2,1)S(1)} %get-tuple-element.36.bc_all.bc, bf16[128,1024]{1,0:T(8,128)(2,1)S(1)} %get-tuple-element.55.keep._, bf16[128,1024]{1,0:T(8,128)(2,1)S(1)} %collective-permute-done.8.recv, f32[1,2048]{1,0:T(1,128)S(1)} %bitcast.17, ...), custom_call_target="tpu_custom_call" | custom-call | flops 1 | bytes 1 | tf_op jit(solution)/shard_map/norm_rows/pallas_call | solution.py:526
  65.5 1.6 %collective-permute-done.9.a1 = bf16[512,2048]{1,0:T(8,128)(2,1)S(1)} collective-permute-done((bf16[512,2048]{1,0:T(8,128)(2,1)S(1)}, bf16[512,2048]{1,0:T(8,128)(2,1)S(1)}, u32[]{:S(2)}, u32[]{:S(2)}) %collective-permute-start.9) | collective-permute-done | bytes 2097184 | tf_op jit(solution)/shard_map/ppermute | solution.py:679
  67.1 4.6 %project.2 = bf16[256,1024]{1,0:T(8,128)(2,1)S(1)} custom-call(bf16[512,2048]{1,0:T(8,128)(2,1)S(1)} %norm_rows.3.a0, bf16[512,2048]{1,0:T(8,128)(2,1)S(1)} %collective-permute-done.9.a1, bf16[2048,4096]{1,0:T(8,128)(2,1)} %w0_far.9, bf16[2048,4096]{1,0:T(8,128)(2,1)} %collective-permute-done.10.w1_far), custom_call_target="tpu_custom_call" | custom-call | flops 1 | bytes 1 | tf_op jit(solution)/shard_map/project/pallas_call | solution.py:582
  73.2 6.8 %project_both.5 = (bf16[256,1024]{1,0:T(8,128)(2,1)S(1)}, f32[256,1024]{1,0:T(8,128)S(1)}) custom-call(bf16[512,2048]{1,0:T(8,128)(2,1)S(1)} %norm_rows.3.a0, bf16[512,2048]{1,0:T(8,128)(2,1)S(1)} %collective-permute-done.9.a1, bf16[2048,4096]{1,0:T(8,128)(2,1)} %w0_far.9, bf16[2048,4096]{1,0:T(8,128)(2,1)} %collective-permute-done.10.w1_far), custom_call_target="tpu_custom_call" | custom-call | flops 1 | bytes 1 | tf_op jit(solution)/shard_map/project_both/pallas_call | solution.py:636
  80.7 6.8 %project_both.4 = (bf16[256,1024]{1,0:T(8,128)(2,1)S(1)}, f32[256,1024]{1,0:T(8,128)S(1)}) custom-call(bf16[512,2048]{1,0:T(8,128)(2,1)S(1)} %norm_rows.3.a0, bf16[512,2048]{1,0:T(8,128)(2,1)S(1)} %collective-permute-done.9.a1, bf16[2048,4096]{1,0:T(8,128)(2,1)} %w0_far.9, bf16[2048,4096]{1,0:T(8,128)(2,1)} %collective-permute-done.10.w1_far), custom_call_target="tpu_custom_call" | custom-call | flops 1 | bytes 1 | tf_op jit(solution)/shard_map/project_both/pallas_call | solution.py:636
  89.1 6.8 %project_both.3 = (bf16[256,1024]{1,0:T(8,128)(2,1)S(1)}, f32[256,1024]{1,0:T(8,128)S(1)}) custom-call(bf16[512,2048]{1,0:T(8,128)(2,1)S(1)} %norm_rows.3.a0, bf16[512,2048]{1,0:T(8,128)(2,1)S(1)} %collective-permute-done.9.a1, bf16[2048,4096]{1,0:T(8,128)(2,1)} %w0_far.9, bf16[2048,4096]{1,0:T(8,128)(2,1)} %collective-permute-done.10.w1_far), custom_call_target="tpu_custom_call" | custom-call | flops 1 | bytes 1 | tf_op jit(solution)/shard_map/project_both/pallas_call | solution.py:636
  96.6 5.3 %project.3._ = bf16[256,4096]{1,0:T(8,128)(2,1)} custom-call(bf16[512,2048]{1,0:T(8,128)(2,1)S(1)} %norm_rows.3.a0, bf16[512,2048]{1,0:T(8,128)(2,1)S(1)} %collective-permute-done.9.a1, bf16[2048,4096]{1,0:T(8,128)(2,1)} %w0_far.9, bf16[2048,4096]{1,0:T(8,128)(2,1)} %collective-permute-done.10.w1_far, bf16[256,1024]{1,0:T(8,128)(2,1)S(1)} %collective-permute-done.14.refs_0_), custom_call_target="tpu_custom_call" | custom-call | flops 1 | bytes 1 | tf_op jit(solution)/shard_map/project/pallas_call | solution.py:582
  102.8 6.2 %collective-permute-done.12.arrived = bf16[256,1024]{1,0:T(8,128)(2,1)S(1)} collective-permute-done((bf16[256,1024]{1,0:T(8,128)(2,1)S(1)}, bf16[256,1024]{1,0:T(8,128)(2,1)S(1)}, u32[]{:S(2)}, u32[]{:S(2)}) %collective-permute-start.12) | collective-permute-done | bytes 524320 | tf_op jit(solution)/shard_map/ppermute | solution.py:679
  109.9 9.5 %collective-permute-done.11.arrived = bf16[256,1024]{1,0:T(8,128)(2,1)S(1)} collective-permute-done((bf16[256,1024]{1,0:T(8,128)(2,1)S(1)}, bf16[256,1024]{1,0:T(8,128)(2,1)S(1)}, u32[]{:S(2)}, u32[]{:S(2)}) %collective-permute-start.11) | collective-permute-done | bytes 524320 | tf_op jit(solution)/shard_map/ppermute | solution.py:679
  (44 shorter events, 12.7 us)
Async XLA Ops:
  0.0 4.7 %copy-start.7 = (bf16[1024,2,256]{2,1,0:T(2,128)(2,1)S(1)}, bf16[1024,2,256]{2,1,0:T(2,128)(2,1)}, u32[]{:S(2)}) copy-start(bf16[1024,2,256]{2,1,0:T(2,128)(2,1)} %bc.1) | copy-start | bytes 3145732
  0.0 67.1 %collective-permute-start.10 = (bf16[2048,4096]{1,0:T(8,128)(2,1)}, bf16[2048,4096]{1,0:T(8,128)(2,1)}, u32[]{:S(2)}, u32[]{:S(2)}) collective-permute-start(bf16[2048,4096]{1,0:T(8,128)(2,1)} %w0_far.9), channel_id=1, source_target_pairs={{0,1},{1,0},{2,3},{3,2},{4,5},{5,4},{6,7},{7,6},{8,9},{9,8},{10,11... | collective-permute-start | bytes 50331656 | tf_op jit(solution)/shard_map/ppermute | solution.py:679
  2.0 2.9 %copy-start = (bf16[64,2048]{1,0:T(8,128)(2,1)S(1)}, bf16[64,2048]{1,0:T(8,128)(2,1)}, u32[]{:S(2)}) copy-start(bf16[64,2048]{1,0:T(8,128)(2,1)} %constant.17.clone.ones) | copy-start | bytes 786436
  2.0 2.9 %copy-start.1 = (f32[1024,32]{0,1:T(8,128)S(1)}, f32[1024,32]{0,1:T(8,128)}, u32[]{:S(2)}) copy-start(f32[1024,32]{0,1:T(8,128)} %param.17) | copy-start | bytes 393220
  2.0 2.9 %copy-start.2 = (f32[1024,32]{0,1:T(8,128)S(1)}, f32[1024,32]{0,1:T(8,128)}, u32[]{:S(2)}) copy-start(f32[1024,32]{0,1:T(8,128)} %param.16) | copy-start | bytes 393220
  2.0 3.0 %copy-start.6 = (f32[32]{0:T(128)S(1)}, f32[32]{0:T(128)}, u32[]{:S(2)}) copy-start(f32[32]{0:T(128)} %param.18) | copy-start | bytes 388
  2.0 9.0 %copy-start.3 = (f32[4,2048]{1,0:T(4,128)S(1)}, f32[4,2048]{1,0:T(4,128)}, u32[]{:S(2)}) copy-start(f32[4,2048]{1,0:T(4,128)} %wx.1) | copy-start | bytes 98308
  2.0 9.0 %copy-start.5 = (f32[4,2,256]{2,1,0:T(2,128)S(1)}, f32[4,2,256]{2,1,0:T(2,128)}, u32[]{:S(2)}) copy-start(f32[4,2,256]{2,1,0:T(2,128)} %wbc.1) | copy-start | bytes 24580
  2.0 8.9 %collective-permute-start = (bf16[16,2560]{1,0:T(8,128)(2,1)}, bf16[16,2560]{1,0:T(8,128)(2,1)S(1)}, u32[]{:S(2)}, u32[]{:S(2)}) collective-permute-start(bf16[16,2560]{1,0:T(8,128)(2,1)} %tail_rows.1), channel_id=1, source_target_pairs={{0,4},{4,8},{8,12},{12,16},{16,20},{20,24},{24,28},{28,0},{1,5},{5... | collective-permute-start | bytes 245768 | tf_op jit(solution)/shard_map/ppermute | solution.py:684
  24.2 8.8 %collective-permute-start.1 = (bf16[144,1024]{1,0:T(8,128)(2,1)S(1)}, bf16[144,1024]{1,0:T(8,128)(2,1)S(1)}, u32[]{:S(2)}, u32[]{:S(2)}) collective-permute-start(bf16[144,1024]{1,0:T(8,128)(2,1)S(1)} %get-tuple-element.37._), channel_id=1, source_target_pairs={{0,4},{4,0},{8,12},{12,8},{16,20},{20,16},{24,28},{28,24},{1,5},{5... | collective-permute-start | bytes 884744 | tf_op jit(solution)/shard_map/ppermute | solution.py:679
  33.9 8.7 %collective-permute-start.2 = (bf16[144,256]{1,0:T(8,128)(2,1)S(1)}, bf16[144,256]{1,0:T(8,128)(2,1)S(1)}, u32[]{:S(2)}, u32[]{:S(2)}) collective-permute-start(bf16[144,256]{1,0:T(8,128)(2,1)S(1)} %get-tuple-element.48), channel_id=1, source_target_pairs={{0,8},{4,12},{8,16},{12,20},{16,24},{20,28},{24,0},{28,4},{1,9},{5... | collective-permute-start | bytes 221192 | tf_op jit(solution)/shard_map/ppermute | solution.py:684
  34.0 8.6 %collective-permute-start.3 = (bf16[144,256]{1,0:T(8,128)(2,1)S(1)}, bf16[144,256]{1,0:T(8,128)(2,1)S(1)}, u32[]{:S(2)}, u32[]{:S(2)}) collective-permute-start(bf16[144,256]{1,0:T(8,128)(2,1)S(1)} %get-tuple-element.49), channel_id=1, source_target_pairs={{0,16},{4,20},{8,24},{12,28},{16,0},{20,4},{24,8},{28,12},{1,17},{... | collective-permute-start | bytes 221192 | tf_op jit(solution)/shard_map/ppermute | solution.py:684
  36.1 6.6 %collective-permute-start.4 = (bf16[144,256]{1,0:T(8,128)(2,1)S(1)}, bf16[144,256]{1,0:T(8,128)(2,1)S(1)}, u32[]{:S(2)}, u32[]{:S(2)}) collective-permute-start(bf16[144,256]{1,0:T(8,128)(2,1)S(1)} %get-tuple-element.50), channel_id=1, source_target_pairs={{0,24},{4,28},{8,0},{12,4},{16,8},{20,12},{24,16},{28,20},{1,25},{... | collective-permute-start | bytes 221192 | tf_op jit(solution)/shard_map/ppermute | solution.py:684
  43.3 9.8 %collective-permute-start.5 = (bf16[128,256]{1,0:T(8,128)(2,1)S(1)}, bf16[128,256]{1,0:T(8,128)(2,1)S(1)}, u32[]{:S(2)}, u32[]{:S(2)}) collective-permute-start(bf16[128,256]{1,0:T(8,128)(2,1)S(1)} %get-tuple-element.52), channel_id=1, source_target_pairs={{0,8},{4,12},{8,16},{12,20},{16,24},{20,28},{24,0},{28,4},{1,9},{5... | collective-permute-start | bytes 196616 | tf_op jit(solution)/shard_map/ppermute | solution.py:684
  44.1 9.0 %collective-permute-start.6 = (bf16[128,256]{1,0:T(8,128)(2,1)S(1)}, bf16[128,256]{1,0:T(8,128)(2,1)S(1)}, u32[]{:S(2)}, u32[]{:S(2)}) collective-permute-start(bf16[128,256]{1,0:T(8,128)(2,1)S(1)} %get-tuple-element.53), channel_id=1, source_target_pairs={{0,16},{4,20},{8,24},{12,28},{16,0},{20,4},{24,8},{28,12},{1,17},{... | collective-permute-start | bytes 196616 | tf_op jit(solution)/shard_map/ppermute | solution.py:684
  45.7 7.4 %collective-permute-start.7 = (bf16[128,256]{1,0:T(8,128)(2,1)S(1)}, bf16[128,256]{1,0:T(8,128)(2,1)S(1)}, u32[]{:S(2)}, u32[]{:S(2)}) collective-permute-start(bf16[128,256]{1,0:T(8,128)(2,1)S(1)} %get-tuple-element.54), channel_id=1, source_target_pairs={{0,24},{4,28},{8,0},{12,4},{16,8},{20,12},{24,16},{28,20},{1,25},{... | collective-permute-start | bytes 196616 | tf_op jit(solution)/shard_map/ppermute | solution.py:684
  53.9 6.5 %copy-start.4 = (f32[2048]{0:T(1024)S(1)}, f32[2048]{0:T(1024)}, u32[]{:S(2)}) copy-start(f32[2048]{0:T(1024)} %param.19) | copy-start | bytes 24580
  53.9 6.4 %collective-permute-start.8 = (bf16[128,1024]{1,0:T(8,128)(2,1)S(1)}, bf16[128,1024]{1,0:T(8,128)(2,1)S(1)}, u32[]{:S(2)}, u32[]{:S(2)}) collective-permute-start(bf16[128,1024]{1,0:T(8,128)(2,1)S(1)} %get-tuple-element.56._), channel_id=1, source_target_pairs={{0,4},{4,0},{8,12},{12,8},{16,20},{20,16},{24,28},{28,24},{1,5},{5... | collective-permute-start | bytes 786440 | tf_op jit(solution)/shard_map/ppermute | solution.py:679
  62.9 4.2 %collective-permute-start.9 = (bf16[512,2048]{1,0:T(8,128)(2,1)S(1)}, bf16[512,2048]{1,0:T(8,128)(2,1)S(1)}, u32[]{:S(2)}, u32[]{:S(2)}) collective-permute-start(bf16[512,2048]{1,0:T(8,128)(2,1)S(1)} %norm_rows.2._), channel_id=1, source_target_pairs={{0,1},{1,0},{2,3},{3,2},{4,5},{5,4},{6,7},{7,6},{8,9},{9,8},{10,11... | collective-permute-start | bytes 6291464 | tf_op jit(solution)/shard_map/ppermute | solution.py:679
  71.7 24.8 %collective-permute-start.14 = (bf16[256,1024]{1,0:T(8,128)(2,1)S(1)}, bf16[256,1024]{1,0:T(8,128)(2,1)S(1)}, u32[]{:S(2)}, u32[]{:S(2)}) collective-permute-start(bf16[256,1024]{1,0:T(8,128)(2,1)S(1)} %project.2), channel_id=1, source_target_pairs={{0,2},{1,3},{2,0},{3,1},{4,6},{5,7},{6,4},{7,5},{8,10},{9,11},{10,... | collective-permute-start | bytes 1572872 | tf_op jit(solution)/shard_map/ppermute | solution.py:679
  80.1 21.8 %collective-permute-start.13 = (bf16[256,1024]{1,0:T(8,128)(2,1)S(1)}, bf16[256,1024]{1,0:T(8,128)(2,1)S(1)}, u32[]{:S(2)}, u32[]{:S(2)}) collective-permute-start(bf16[256,1024]{1,0:T(8,128)(2,1)S(1)} %get-tuple-element.62), channel_id=1, source_target_pairs={{0,2},{1,3},{2,0},{3,1},{4,6},{5,7},{6,4},{7,5},{8,10},{9,11},{10,... | collective-permute-start | bytes 1572872 | tf_op jit(solution)/shard_map/ppermute | solution.py:679
  87.6 21.5 %collective-permute-start.12 = (bf16[256,1024]{1,0:T(8,128)(2,1)S(1)}, bf16[256,1024]{1,0:T(8,128)(2,1)S(1)}, u32[]{:S(2)}, u32[]{:S(2)}) collective-permute-start(bf16[256,1024]{1,0:T(8,128)(2,1)S(1)} %get-tuple-element.60), channel_id=1, source_target_pairs={{0,2},{1,3},{2,0},{3,1},{4,6},{5,7},{6,4},{7,5},{8,10},{9,11},{10,... | collective-permute-start | bytes 1572872 | tf_op jit(solution)/shard_map/ppermute | solution.py:679
  95.9 23.6 %collective-permute-start.11 = (bf16[256,1024]{1,0:T(8,128)(2,1)S(1)}, bf16[256,1024]{1,0:T(8,128)(2,1)S(1)}, u32[]{:S(2)}, u32[]{:S(2)}) collective-permute-start(bf16[256,1024]{1,0:T(8,128)(2,1)S(1)} %get-tuple-element.58), channel_id=1, source_target_pairs={{0,2},{1,3},{2,0},{3,1},{4,6},{5,7},{6,4},{7,5},{8,10},{9,11},{10,... | collective-permute-start | bytes 1572872 | tf_op jit(solution)/shard_map/ppermute | solution.py:679

commit v9 on v8

v9 whole, which is shorter than its diff:
```python
import functools

import jax
import jax.numpy as jnp
import numpy as np
from jax import lax
from jax.experimental import pallas as pl
from jax.experimental.pallas import tpu as pltpu
from jax.sharding import PartitionSpec as P

P_SIZE = 64
N = 128
KCONV = 4
EPS = 1e-05
LOG2E = 1.4426950408889634

TOK_A = 256
ROWS_A = 32
TOK_B = 128
STEP_B = 256
EXTRA = 16
SLAB = 256
ROWS_C = 128
TILE = 256
SLOTS = 4
LEAD = 16
B_PARTS = 2
HIGHEST = lax.Precision.HIGHEST
F32 = jnp.float32
BF16 = jnp.bfloat16


def params(mib):
    return pltpu.CompilerParams(vmem_limit_bytes=mib * 1024 * 1024)


CHEAP = pl.CostEstimate(flops=1, bytes_accessed=1, transcendentals=0)
SCALAR = pl.BlockSpec(memory_space=pltpu.SMEM)
FULL = pl.BlockSpec(memory_space=pltpu.VMEM)
FAR = pl.BlockSpec(memory_space=pltpu.HBM)
ANY = pl.BlockSpec(memory_space=pl.ANY)

ODD, ROWS, PAIR, SEQ, GROUP = 0, 1, 5, 6, 7


def dot(a, b, dims=((1,), (0,)), precision=None):
    return lax.dot_general(a, b, (dims, ((), ())), precision=precision, preferred_element_type=F32)


def half_silu(half):
    return half + half * jnp.tanh(half)


def far(*arrays):
    return [pltpu.with_memory_space_constraint(a, pltpu.HBM) for a in arrays]


def whole(shape):
    return pl.BlockSpec(shape, lambda *_: (0,) * len(shape))


def decay_kernel(ld_t, step_t, skip, ones, cum, cum_s, log_s, f_dev, f_blk, e_blk, rates, by_row):
    heads, length = ld_t.shape
    blocks = length // TOK_B
    row = lax.broadcasted_iota(jnp.int32, (TOK_B, TOK_B), 0)
    col = lax.broadcasted_iota(jnp.int32, (TOK_B, TOK_B), 1)
    lower = (row >= col).astype(F32)
    upper = (row <= col).astype(F32)
    eye = (row == col).astype(BF16)

    def put(ref, rows, value):
        high = value.astype(BF16)
        low = (value - high.astype(F32)).astype(BF16)
        ref[rows, :] = dot(eye, jnp.concatenate([high, low], 0), ((1,), (1,))).astype(BF16)

    cums, totals, row_totals = [], [], []
    for b in range(blocks):
        rows = slice(b * TOK_B, (b + 1) * TOK_B)
        logs = ld_t[:, rows] * LOG2E
        c = dot(lower, logs, ((1,), (1,)), HIGHEST)
        for g in range(cum.shape[0]):
            cum[g, rows, :] = c[:, g * cum.shape[2] : (g + 1) * cum.shape[2]]
        row_totals.append(c[TOK_B - 1 : TOK_B, :])
        c = dot(logs, upper, precision=HIGHEST)
        cums.append(c)
        totals.append(c[:, TOK_B - 1 : TOK_B])
    before, row_before = [jnp.zeros_like(totals[0])], [jnp.zeros_like(row_totals[0])]
    for b in range(blocks):
        before.append(before[-1] + totals[b])
        row_before.append(row_before[-1] + row_totals[b])
    total = before[-1]
    logs = jnp.concatenate(row_totals + row_before[:-1] + row_before[-1:] * 8, 0)
    values = jnp.concatenate([jnp.exp2(logs), jnp.broadcast_to(skip[...], (8, heads))], 0)
    spread = dot(values, ones[0:heads, :].astype(F32), precision=HIGHEST)
    rates[...] = spread
    for b in range(2 * blocks):
        by_row[b] = spread[b : b + 1, :]
    by_row[2 * blocks] = spread[2 * blocks + 8 : 2 * blocks + 9, :]
    for b in range(blocks):
        rows = slice(b * TOK_B, (b + 1) * TOK_B)
        s = step_t[:, rows]
        log_step = jnp.log2(s)
        shifted = cums[b] - log_step
        for g in range(cum.shape[0]):
            own = slice(g * cum.shape[2], (g + 1) * cum.shape[2])
            log_s[g, :, rows] = log_step[own, :]
            cum_s[g, :, rows] = shifted[own, :]
        put(f_dev, rows, jnp.exp2(total - (cums[b] + before[b])) * s)
        put(f_blk, rows, jnp.exp2(totals[b] - cums[b]) * s)
        put(e_blk, rows, jnp.exp2(cums[b]))


def decays(groups, log_decay, step, skip, ones):
    length, heads = log_decay.shape
    blocks = length // TOK_B
    width = ones.shape[1]
    wide = jax.ShapeDtypeStruct((groups, heads // groups, length), F32)
    pair = jax.ShapeDtypeStruct((length, 2 * heads), BF16)
    return pl.pallas_call(
        decay_kernel,
        out_shape=(
            jax.ShapeDtypeStruct((groups, length, heads // groups), F32),
            wide,
            wide,
            pair,
            pair,
            pair,
            jax.ShapeDtypeStruct((2 * blocks + 16, width), F32),
            jax.ShapeDtypeStruct((2 * blocks + 1, 1, width), F32),
        ),
        compiler_params=params(16),
        name="decays",
    )(log_decay.T, step.T, skip[None, :], ones)


def tail_kernel(x, bc, out):
    width, bc_width = x.shape[1], bc.shape[2]
    out[:, 0:width] = x[...]
    for g in range(bc.shape[1]):
        out[:, width + g * bc_width : width + (g + 1) * bc_width] = bc[:, g, :]


def tail_rows(x, bc):
    length, width = x.shape
    groups, bc_width = bc.shape[1:]
    at = length // LEAD - 1
    shape = (LEAD, width + groups * bc_width)
    return pl.pallas_call(
        tail_kernel,
        grid=(1,),
        in_specs=[
            pl.BlockSpec((LEAD, width), lambda i: (at, 0)),
            pl.BlockSpec((LEAD, groups, bc_width), lambda i: (at, 0, 0)),
        ],
        out_specs=whole(shape),
        out_shape=jax.ShapeDtypeStruct(shape, BF16),
        compiler_params=params(8),
        cost_estimate=CHEAP,
        name="tail_rows",
    )(x, bc)


def put_message(ref, state, decay):
    high = decay.astype(BF16)
    low = (decay - high.astype(F32)).astype(BF16)
    rest = jnp.zeros((EXTRA - 2, state.shape[1]), BF16)
    ref[0:N, :] = state.astype(BF16)
    ref[N:, :] = jnp.concatenate([high, low, rest], 0)


def take_message(ref):
    extra = ref[N:, :].astype(F32)
    return ref[0:N, :].astype(F32), extra[0:1] + extra[1:2]


def conv_kernel(
    order, info, x, x_lead, bc, bc_lead, halo, bc_halo, wx, wbc, f_dev, ones, rates, x_out, bc_out, final, xf, state
):
    i = pl.program_id(0)
    rows, width = x.shape
    group = info[GROUP + order]

    @pl.when(i == 0)
    def _():
        state[...] = jnp.zeros_like(state)

    def conv(src, first, behind, weights, emit):
        at_start = jnp.where(info[SEQ] == 0, jnp.zeros_like(first), first)
        lead = jnp.where(i == 0, at_start, behind).astype(F32)
        w0, w1, w2, w3 = [w * 0.5 for w in weights]
        back = LEAD - 8
        r1 = pltpu.roll(lead, 1, 0)
        last_x, last_p = lead[back:], (w1 * lead + w0 * r1)[back:]
        for r in range(0, rows, ROWS_A):
            cur = src(r).astype(F32)
            r1 = pltpu.roll(jnp.concatenate([last_x, cur], 0), 1, 0)[8:]
            p = w1 * cur + w0 * r1
            p2 = pltpu.roll(jnp.concatenate([last_p, p], 0), 2, 0)[8:]
            emit(r, half_silu((w3 * cur + w2 * r1) + p2))
            last_x, last_p = cur[ROWS_A - 8 :], p[ROWS_A - 8 :]

    for lanes in range(0, 2 * N, N):
        ds = slice(lanes, lanes + N)

        def emit_bc(r, value):
            bc_out[r : r + ROWS_A, ds] = value.astype(BF16)

        weights = [jnp.where(group == 0, wbc[k, 0:1, ds], wbc[k, 1:2, ds]) for k in range(KCONV)]
        conv(lambda r: bc[r : r + ROWS_A, ds], bc_halo[:, ds], bc_lead[:, ds], weights, emit_bc)

    def slab(c, _):
        ds = pl.ds(pl.multiple_of(c * SLAB, SLAB), SLAB)
        scale = dot(f_dev[...], ones[:, ds])

        def emit(r, value):
            x_out[r : r + ROWS_A, ds] = value.astype(BF16)
            xf[r : r + ROWS_A, ds] = (value * scale[r : r + ROWS_A]).astype(BF16)

        weights = [wx[k : k + 1, ds] for k in range(KCONV)]
        conv(lambda r: x[r : r + ROWS_A, ds], halo[:, ds], x_lead[:, ds], weights, emit)
        return 0

    lax.fori_loop(0, width // SLAB, slab, 0)
    state[...] += dot(bc_out[:, 0:N], xf[...], ((0,), (0,)))

    @pl.when(i == pl.num_programs(0) - 1)
    def _():
        if order == 0:
            row = rates.shape[0] - 16
            put_message(final, state[...], rates[row : row + 1, :])
        else:
            final[...] = state[...]


def conv_states(order, info, x, bc, halo, wx, wbc, f_dev, ones, rates):
    length, full = x.shape
    width = full // 2
    lead = lambda i, info: (jnp.maximum(i * (TOK_A // LEAD) - 1, 0), info[GROUP + order])
    block = lambda i, info: (i, info[GROUP + order])
    column = lambda i, info: (0, info[GROUP + order])
    rows = lambda i, info: (i, 0)
    final = ((N + EXTRA, width), BF16) if order == 0 else ((N, width), F32)
    return pl.pallas_call(
        functools.partial(conv_kernel, order),
        grid_spec=pltpu.PrefetchScalarGridSpec(
            num_scalar_prefetch=1,
            grid=(length // TOK_A,),
            in_specs=[
                pl.BlockSpec((TOK_A, width), block),
                pl.BlockSpec((LEAD, width), lead),
                pl.BlockSpec((TOK_A, 2 * N), block),
                pl.BlockSpec((LEAD, 2 * N), lead),
                pl.BlockSpec((LEAD, width), column),
                pl.BlockSpec((LEAD, 2 * N), lambda i, info: (0, full // (2 * N) + info[GROUP + order])),
                pl.BlockSpec((KCONV, width), column),
                whole(wbc.shape),
                pl.BlockSpec((TOK_A, f_dev.shape[1]), rows),
                pl.BlockSpec((ones.shape[0], width), column),
                pl.BlockSpec((rates.shape[0], width), column),
            ],
            out_specs=[
                pl.BlockSpec((TOK_A, width), rows),
                pl.BlockSpec((TOK_A, 2 * N), rows),
                whole(final[0]),
            ],
            scratch_shapes=[pltpu.VMEM((TOK_A, width), BF16), pltpu.VMEM((N, width), F32)],
        ),
        out_shape=(
            pltpu.HBM((length, width), BF16),
            jax.ShapeDtypeStruct((length, 2 * N), BF16),
            jax.ShapeDtypeStruct(*final),
        ),
        compiler_params=params(16),
        cost_estimate=CHEAP,
        name="conv_states",
    )(info, x, x, bc, bc, halo, halo, wx, wbc, f_dev, ones, rates)


def pair_kernel(info, got, keep, rates, _, msg, own, first, aux):
    half = keep.shape[1]
    is_odd = info[ODD] == 1
    arrived, their = take_message(got)
    row = rates.shape[0] - 16
    mine = rates[row : row + 1, pl.ds(pl.multiple_of(info[GROUP + 1] * half, half), half)]
    early = jnp.where(is_odd, arrived, keep[...])
    late = jnp.where(is_odd, keep[...], arrived)
    even_decay = jnp.where(is_odd, their, mine)
    odd_decay = jnp.where(is_odd, mine, their)
    state = odd_decay * early + late
    own[...] = state
    first[...] = early
    aux[0:8, :] = jnp.broadcast_to(even_decay, (8, half))
    aux[8:16, :] = jnp.broadcast_to(even_decay * odd_decay, (8, half))
    put_message(msg, state, even_decay * odd_decay)


def wave_kernel(got, own, aux, behind_in, _, msg, behind):
    before, decay = take_message(got)
    if behind_in is not None:
        before_decay = behind_in[N : N + 1, :]
        before = behind_in[0:N, :] + before_decay * before
        decay = before_decay * decay
    pair_decay = aux[8:9, :]
    behind[0:N, :] = before
    behind[N:, :] = jnp.broadcast_to(decay, (8, before.shape[1]))
    put_message(msg, own[...] + pair_decay * before, pair_decay * decay)


def last_kernel(info, got, behind_in, first, aux, _, back, held):
    is_odd = info[ODD] == 1
    before, _unused = take_message(got)
    if behind_in is not None:
        before = behind_in[0:N, :] + behind_in[N : N + 1, :] * before
    entering_odd = aux[0:1, :] * before + first[...]
    back[...] = jnp.where(is_odd, before, entering_odd).astype(BF16)
    held[...] = jnp.where(is_odd, entering_odd, before).astype(BF16)


def pair_split_kernel(info, got, keep, rates, _, first, aux, *refs):
    outs, wide = refs[:-1], refs[-1]
    half = keep.shape[1]
    pairs = len(outs)
    piece = half // pairs
    is_odd = info[ODD] == 1
    arrived, their = take_message(got)
    row = rates.shape[0] - 16
    mine = rates[row : row + 1, pl.ds(pl.multiple_of(info[GROUP + 1] * half, half), half)]
    early = jnp.where(is_odd, arrived, keep[...])
    late = jnp.where(is_odd, keep[...], arrived)
    even_decay = jnp.where(is_odd, their, mine)
    odd_decay = jnp.where(is_odd, mine, their)
    first[...] = early
    aux[...] = jnp.broadcast_to(even_decay, (8, half))
    put_message(wide, odd_decay * early + late, even_decay * odd_decay)
    for r in range(pairs):
        owner = lax.rem(info[PAIR] + r, pairs)
        outs[r][...] = wide[:, pl.ds(pl.multiple_of(owner * piece, piece), piece)]


def owner_kernel(info, *refs):
    pairs = (len(refs) - 3) // 2
    ins, outs = refs[:pairs], refs[pairs + 1 : 2 * pairs + 1]
    states, prefixes = refs[-2:]
    for r in range(pairs):
        states[lax.rem(info[PAIR] + pairs - r, pairs)] = ins[r][...]
    before = jnp.zeros(prefixes.shape[1:], F32)
    for q in range(pairs):
        prefixes[q] = before.astype(BF16)
        if q < pairs - 1:
            state, decay = take_message(states.at[q])
            before = decay * before + state
    for r in range(pairs):
        outs[r][...] = prefixes[lax.rem(info[PAIR] + r, pairs)]


def last_split_kernel(info, first, aux, _, *refs):
    pairs = len(refs) - 3
    back, held, wide = refs[-3:]
    piece = back.shape[1] // pairs
    for r in range(pairs):
        owner = lax.rem(info[PAIR] + pairs - r, pairs)
        wide[:, pl.ds(pl.multiple_of(owner * piece, piece), piece)] = refs[r][...]
    is_odd = info[ODD] == 1
    before = wide[...].astype(F32)
    entering_odd = aux[0:1, :] * before + first[...]
    back[...] = jnp.where(is_odd, before, entering_odd).astype(BF16)
    held[...] = jnp.where(is_odd, entering_odd, before).astype(BF16)


def combine(kernel, operands, specs, outs, name, scratch=()):
    return pl.pallas_call(
        kernel,
        in_specs=specs,
        out_specs=[FULL] * len(outs),
        out_shape=[jax.ShapeDtypeStruct(s, t) for s, t in outs],
        scratch_shapes=list(scratch),
        compiler_params=params(16),
        cost_estimate=CHEAP,
        name=name,
    )(*operands)


def scan_kernel(order, part, info, x_far, z_far, bc, cum, cum_s, log_s, f_blk, e_blk, by_row, ones, _, uv_out, x, z, sem, state):
    length, width = x.shape
    per_slab = SLAB // P_SIZE
    inner = STEP_B // TOK_B
    blocks = length // TOK_B
    group = info[GROUP + order]
    first_head = part * width // P_SIZE
    first_lane = group * x_far.shape[1] + part * width

    def fetch(step):
        piece = pl.ds(pl.multiple_of(step * STEP_B, STEP_B), STEP_B)
        return (
            pltpu.make_async_copy(x_far.at[piece, pl.ds(part * width, width)], x.at[piece], sem.at[0, step]),
            pltpu.make_async_copy(
                z_far.at[piece, pl.ds(pl.multiple_of(first_lane, width), width)], z.at[piece], sem.at[1, step]
            ),
        )

    for step in range(length // STEP_B):
        for copy in fetch(step):
            copy.start()
    state[...] = jnp.zeros_like(state)

    row = lax.broadcasted_iota(jnp.int32, (TOK_B, TOK_B), 0)
    col = lax.broadcasted_iota(jnp.int32, (TOK_B, TOK_B), 1)
    keep = row >= col
    first = lax.broadcasted_iota(jnp.int32, (TOK_B, 2 * P_SIZE), 1) < P_SIZE
    zero = jnp.zeros((TOK_B, 2 * P_SIZE), BF16)

    def turn(step, _):
        for copy in fetch(step):
            copy.wait()
        for k in range(inner):
            block(step * inner + k)
        return 0

    def block(b):
        at = pl.ds(pl.multiple_of(b * TOK_B, TOK_B), TOK_B)
        b_mat = bc[at, 0:N]
        c_mat = bc[at, N : 2 * N]
        scores = jnp.where(keep, dot(c_mat, b_mat, ((1,), (1,))), 0.0)
        for s in range(width // SLAB):
            lanes = slice(s * SLAB, (s + 1) * SLAB)
            xb = x[at, lanes]
            wide = pl.ds(pl.multiple_of(first_lane + s * SLAB, SLAB), SLAB)
            sel = ones[:, wide]
            fade_row = by_row[b, :, wide]
            lead_row = by_row[blocks + b, :, wide]
            skip = by_row[2 * blocks, :, wide]
            old = state[:, lanes]
            rise = dot(e_blk[at, :], sel)
            carried = dot(c_mat, old.astype(BF16)) * rise
            within = []
            for q in range(per_slab // 2):
                tables = []
                for h in (2 * q, 2 * q + 1):
                    head = first_head + s * per_slab + h
                    column = cum[group, at, head : head + 1]
                    own = slice(head, head + 1)
                    gap = jnp.minimum(column - cum_s[group, own, at], log_s[group, own, at])
                    tables.append((scores * jnp.exp2(gap)).astype(BF16))
                xp = xb[:, q * 2 * P_SIZE : (q + 1) * 2 * P_SIZE]
                stacked = jnp.concatenate([jnp.where(first, xp, zero), jnp.where(first, zero, xp)], 0)
                within.append(dot(jnp.concatenate(tables, 1), stacked))
            xs = xb.astype(F32)
            y = jnp.concatenate(within, 1) + carried + skip * xs
            gate = half_silu(z[at, lanes].astype(F32) * 0.5)
            uv_out[at, lanes] = (y * gate).astype(BF16)
            uv_out[at, width + s * SLAB : width + (s + 1) * SLAB] = (gate * rise * lead_row).astype(BF16)
            xf = (xs * dot(f_blk[at, :], sel)).astype(BF16)
            state[:, lanes] = old * fade_row + dot(b_mat, xf, ((0,), (0,)))

    lax.fori_loop(0, length // STEP_B, turn, 0)


def scan_part(order, part, info, token, x, z, bc, cum, cum_s, log_s, f_blk, e_blk, by_row, ones):
    length, full = x.shape
    width = full // B_PARTS
    return pl.pallas_call(
        functools.partial(scan_kernel, order, part),
        in_specs=[SCALAR, FAR, FAR] + [FULL] * 8 + [ANY],
        out_specs=FULL,
        out_shape=jax.ShapeDtypeStruct((length, 2 * width), BF16),
        scratch_shapes=[
            pltpu.VMEM((length, width), BF16),
            pltpu.VMEM((length, width), BF16),
            pltpu.SemaphoreType.DMA((2, length // STEP_B)),
            pltpu.VMEM((N, width), F32),
        ],
        compiler_params=params(16),
        cost_estimate=CHEAP,
        name="scan_part",
    )(info, x, z, bc, cum, cum_s, log_s, f_blk, e_blk, by_row, ones, token)


def norm_kernel(row, ahead, info, bc0, bc1, state0, state1, gain, *refs):
    uvs, out = refs[:-1][-2 * B_PARTS :], refs[-1]
    skipped = out.shape[0] - ROWS_C * (out.shape[0] // ROWS_C // (2 if ahead else 1))
    count = out.shape[0] - skipped
    per = state0.shape[1]
    part = per // B_PARTS
    if ahead:
        out[0:skipped, :] = refs[0][...]

    def step(j, _):
        to = pl.ds(pl.multiple_of(skipped + j * ROWS_C, ROWS_C), ROWS_C)
        at = pl.ds(pl.multiple_of(info[ROWS + row] * count + j * ROWS_C, ROWS_C), ROWS_C)
        for order, (bc, state) in enumerate(((bc0, state0), (bc1, state1))):
            c_mat = bc[at, N : 2 * N]
            pieces = []
            squares = None
            for p in range(B_PARTS):
                uv = uvs[order * B_PARTS + p]
                inc = state[:, p * part : (p + 1) * part]
                gated = uv[at, 0:part].astype(F32) + uv[at, part:].astype(F32) * dot(c_mat, inc)
                square = jnp.sum(gated * gated, axis=-1, keepdims=True)
                squares = square if squares is None else squares + square
                pieces.append(gated)
            scale = lax.rsqrt(squares * (1.0 / per) + EPS)
            for p, gated in enumerate(pieces):
                lanes = pl.ds(pl.multiple_of(info[GROUP + order] * per + p * part, part), part)
                out[to, lanes] = (gated * scale * gain[:, lanes]).astype(BF16)
        return 0

    lax.fori_loop(0, count // ROWS_C, step, 0)


def norm_rows(row, info, count, tokens, bcs, states, gain, uvs, ahead=None):
    first = [] if ahead is None else [ahead]
    rows = count if ahead is None else 2 * count
    return pl.pallas_call(
        functools.partial(norm_kernel, row, ahead is not None),
        in_specs=[SCALAR] + [FULL] * (5 + len(first)) + [ANY] * len(tokens) + [FULL] * len(uvs),
        out_specs=FULL,
        out_shape=jax.ShapeDtypeStruct((rows, gain.shape[1]), BF16),
        compiler_params=params(16),
        cost_estimate=CHEAP,
        name="norm_rows",
    )(info, *bcs, *states, gain, *first, *tokens, *uvs)


def stream(base, w0_far, w1_far, w0, w1, sem):
    j = pl.program_id(0)
    tiles = pl.num_programs(0)

    def fetch(t):
        slot = lax.rem(t, SLOTS)
        lanes = pl.ds(pl.multiple_of((base + t) * TILE, TILE), TILE)
        return (
            pltpu.make_async_copy(w0_far.at[:, lanes], w0.at[slot], sem.at[0, slot]),
            pltpu.make_async_copy(w1_far.at[:, lanes], w1.at[slot], sem.at[1, slot]),
        )

    def start(t):
        @pl.when(t < tiles)
        def _():
            for copy in fetch(t):
                copy.start()

    @pl.when(j == 0)
    def _():
        for t in range(SLOTS - 1):
            start(t)

    start(j + SLOTS - 1)
    for copy in fetch(j):
        copy.wait()
    return lax.rem(j, SLOTS)


def buffers(depth):
    return [
        pltpu.VMEM((SLOTS, depth, TILE), BF16),
        pltpu.VMEM((SLOTS, depth, TILE), BF16),
        pltpu.SemaphoreType.DMA((2, SLOTS)),
    ]


def ahead_kernel(base, own, mate, w0_far, w1_far, out, w0, w1, sem):
    slot = stream(base, w0_far, w1_far, w0, w1, sem)
    out[...] = (dot(own[...], w0[slot]) + dot(mate[...], w1[slot])).astype(BF16)


def project_ahead(own, mate, w0, w1, first, count):
    rows, depth = own.shape
    return pl.pallas_call(
        functools.partial(ahead_kernel, first // TILE),
        grid=(count // TILE,),
        in_specs=[FULL, FULL, FAR, FAR],
        out_specs=pl.BlockSpec((rows, TILE), lambda j: (0, j)),
        out_shape=jax.ShapeDtypeStruct((rows, count), BF16),
        scratch_shapes=buffers(depth),
        compiler_params=params(20),
        cost_estimate=CHEAP,
        name="project_ahead",
    )(own, mate, w0, w1)


def both_kernel(base, owns, mate0, mate1, w0_far, w1_far, far, near, mates, w0, w1, sem):
    rows = far.shape[0]

    @pl.when(pl.program_id(0) == 0)
    def _():
        mates[0:rows, :] = mate0[...]
        mates[rows:, :] = mate1[...]

    slot = stream(base, w0_far, w1_far, w0, w1, sem)
    total = dot(owns[...], w0[slot]) + dot(mates[...], w1[slot])
    far[...] = total[0:rows].astype(BF16)
    near[...] = total[rows:]


def project_both(owns, mate0, mate1, w0, w1, first, count):
    rows, depth = mate0.shape
    placed = pl.BlockSpec((rows, TILE), lambda j: (0, j))
    return pl.pallas_call(
        functools.partial(both_kernel, first // TILE),
        grid=(count // TILE,),
        in_specs=[FULL] * 3 + [FAR] * 2,
        out_specs=[placed, placed],
        out_shape=[jax.ShapeDtypeStruct((rows, count), BF16), jax.ShapeDtypeStruct((rows, count), F32)],
        scratch_shapes=[pltpu.VMEM((2 * rows, depth), BF16)] + buffers(depth),
        compiler_params=params(24),
        cost_estimate=CHEAP,
        name="project_both",
    )(owns, mate0, mate1, w0, w1)


def near_kernel(split, owns, mate, w0_far, w1_far, arrived0, arrived1, out, w0, w1, sem):
    slot = stream(0, w0_far, w1_far, w0, w1, sem)
    rows = mate.shape[0]
    total = dot(owns[rows:, :], w0[slot]) + dot(mate[...], w1[slot])
    arrived = jnp.where(pl.program_id(0) < split, arrived0[...], arrived1[...])
    out[...] = (total + arrived.astype(F32)).astype(BF16)


def project_near(owns, mate, w0, w1, arrived0, arrived1):
    rows, depth = mate.shape
    split = arrived0.shape[1] // TILE
    tiles = split + arrived1.shape[1] // TILE
    return pl.pallas_call(
        functools.partial(near_kernel, split),
        grid=(tiles,),
        in_specs=[FULL, FULL, FAR, FAR]
        + [
            pl.BlockSpec((rows, TILE), lambda j: (0, jnp.minimum(j, split - 1))),
            pl.BlockSpec((rows, TILE), lambda j: (0, jnp.maximum(j - split, 0))),
        ],
        out_specs=pl.BlockSpec((rows, TILE), lambda j: (0, j)),
        out_shape=jax.ShapeDtypeStruct((rows, w0.shape[1]), BF16),
        scratch_shapes=buffers(depth),
        compiler_params=params(20),
        cost_estimate=CHEAP,
        name="project_near",
    )(owns, mate, w0, w1, arrived0, arrived1)


def add_kernel(part, arrived, _, out):
    out[...] = (part[...] + arrived[...].astype(F32)).astype(BF16)


def add_chunk(part, arrived, result, first):
    rows, count = arrived.shape
    base = first // TILE
    return pl.pallas_call(
        add_kernel,
        grid=(count // TILE,),
        in_specs=[pl.BlockSpec((rows, TILE), lambda j: (0, j))] * 2 + [ANY],
        out_specs=pl.BlockSpec((rows, TILE), lambda j: (0, base + j)),
        out_shape=jax.ShapeDtypeStruct(result.shape, BF16),
        input_output_aliases={2: 0},
        compiler_params=params(8),
        cost_estimate=CHEAP,
        name="add_chunk",
    )(part, arrived, result)


def shift(block, distance):
    size = lax.axis_size("seq")
    return lax.ppermute(block, "seq", [(i, i + distance) for i in range(size - distance)])


def swap(block, axis, bit):
    return lax.ppermute(block, axis, [(i, i ^ bit) for i in range(lax.axis_size(axis))])


def rotate(block, distance):
    size = lax.axis_size("seq")
    return lax.ppermute(block, "seq", [(i, (i + distance) % size) for i in range(size)])


def log_steps(info, got, keep, rates, done, pairs, scan_next):
    half = keep.shape[1]
    message = ((N + EXTRA, half), BF16)
    full = ((N, half), F32)
    msg, own, first, aux = combine(
        pair_kernel,
        (info, got, keep, rates, done),
        [SCALAR, FULL, FULL, FULL, ANY],
        [message, full, full, ((16, half), F32)],
        "pair",
    )
    behind = None
    covered = 0
    while True:
        got = shift(msg, 2 * (covered + 1))
        done = scan_next(msg)
        covered = 2 * covered + 1
        if covered >= pairs - 1:
            break
        operands, specs = [got, own, aux], [FULL, FULL, FULL]
        if behind is None:
            kernel = lambda g, o, a, t, m, b: wave_kernel(g, o, a, None, t, m, b)
        else:
            kernel = wave_kernel
            operands.append(behind)
            specs.append(FULL)
        msg, behind = combine(kernel, operands + [done], specs + [ANY], [message, ((N + 8, half), F32)], "wave")
    operands, specs = [info, got], [SCALAR, FULL]
    if behind is None:
        kernel = lambda o, g, f, a, t, b, h: last_kernel(o, g, None, f, a, t, b, h)
    else:
        kernel = last_kernel
        operands.append(behind)
        specs.append(FULL)
    out = ((N, half), BF16)
    back, held = combine(kernel, operands + [first, aux, done], specs + [FULL, FULL, ANY], [out, out], "last")
    return back, held


def local(
    x_input,
    z_input,
    bc_input,
    conv_weight_x,
    conv_weight_bc,
    step_size,
    log_decay,
    skip_gain,
    norm_gain,
    out_weight,
):
    length, width = x_input.shape
    heads = step_size.shape[1]
    ways = lax.axis_size("head")
    pairs = lax.axis_size("seq") // 2
    mine = lax.axis_index("head")
    half = width // 2
    seq = lax.axis_index("seq")
    info = jnp.stack([seq & 1, mine ^ 3, mine ^ 2, mine ^ 1, mine, seq >> 1, seq, 1 - (seq & 1), seq & 1]).astype(jnp.int32)

    x_far, z_far, w_far = far(x_input, z_input, out_weight)
    (bc_far,) = far(bc_input)
    halo = rotate(tail_rows(x_far, bc_far), 1)
    bc = bc_input.reshape(length, -1)
    weight_mate = swap(out_weight, "head", 1)

    ones = jnp.asarray(np.tile(np.repeat(np.eye(heads), P_SIZE, axis=1), (2, 1)), BF16)
    cum, cum_s, log_s, f_dev, f_blk, e_blk, rates, by_row = decays(2, log_decay, step_size, skip_gain, ones)
    shared = (info, x_far, bc, halo, conv_weight_x, conv_weight_bc, f_dev, ones, rates)
    x0, bc0, send = conv_states(0, *shared)
    got = swap(send, "seq", 1)
    x1, bc1, keep = conv_states(1, *shared)

    uvs = []
    groups = [(x, z_far, y, cum, cum_s, log_s, f_blk, e_blk, by_row, ones) for x, y in zip(far(x0, x1), (bc0, bc1))]

    def scan_next(token):
        if len(uvs) < 2 * B_PARTS:
            order, part = divmod(len(uvs), B_PARTS)
            uvs.append(scan_part(order, part, info, token, *groups[order]))
        return uvs[-1]

    full = ((N, half), F32)
    message = ((N + EXTRA, half), BF16)
    done = keep
    out = ((N, half), BF16)
    if pairs > 1 and half % (pairs * N) == 0:
        piece = half // pairs
        part = ((N + EXTRA, piece), BF16)
        first, aux, *parts = combine(
            pair_split_kernel,
            (info, got, keep, rates, done),
            [SCALAR, FULL, FULL, FULL, ANY],
            [full, ((8, half), F32)] + [part] * pairs,
            "pair",
            [pltpu.VMEM(*message)],
        )
        parts = list(parts[:1]) + [rotate(parts[r], 2 * r) for r in range(1, pairs)]
        done = scan_next(scan_next(parts[0]))
        parts = combine(
            owner_kernel,
            [info] + parts + [done],
            [SCALAR] + [FULL] * pairs + [ANY],
            [((N, piece), BF16)] * pairs,
            "owner",
            [pltpu.VMEM((pairs, N + EXTRA, piece), BF16), pltpu.VMEM((pairs, N, piece), BF16)],
        )
        ready = parts[0]
        parts = list(parts[:1]) + [rotate(parts[r], 2 * r) for r in range(1, pairs)]
        done = scan_next(ready)
        back, held = combine(
            last_split_kernel,
            [info, first, aux, done] + parts,
            [SCALAR, FULL, FULL, ANY] + [FULL] * pairs,
            [out, out],
            "last",
            [pltpu.VMEM(*out)],
        )
    else:
        back, held = log_steps(info, got, keep, rates, done, pairs, scan_next)
    other = swap(back, "seq", 1)
    while len(uvs) < 2 * B_PARTS:
        scan_next(back)

    count = length // ways
    gain = norm_gain[None, :]

    def rows_for(row, *tokens, ahead=None):
        return norm_rows(row, info, count, tokens, (bc0, bc1), (other, held), gain, uvs, ahead)

    weights = (w_far, weight_mate)
    cuts = [out_weight.shape[1] * c // 16 for c in (0, 2, 6, 10, 14, 16)]
    far_mate = rows_for(0)
    far_own = rows_for(1, far_mate)
    far_mate = swap(far_mate, "head", 1)
    arrivals = []
    for lo, hi in zip(cuts[0:2], cuts[1:3]):
        sent = project_ahead(far_own, far_mate, *weights, lo, hi - lo)
        arrivals.append(swap(sent, "head", 2))
    near_mate = rows_for(2, sent)
    owns = rows_for(3, near_mate, arrivals[0], ahead=far_own)
    near_mate = swap(near_mate, "head", 1)
    parts = []
    for lo, hi in zip(cuts[2:-1], cuts[3:]):
        sent, part = project_both(owns, far_mate, near_mate, *weights, lo, hi - lo)
        arrivals.append(swap(sent, "head", 2))
        parts.append(part)
    result = project_near(owns, near_mate, *weights, *arrivals[:2])
    for part, arrived, lo in zip(parts, arrivals[2:], cuts[2:]):
        result = add_chunk(part, arrived, result, lo)
    return result


def solution(mesh):
    in_specs = (
        P("seq", "head"),
        P("seq", "head"),
        P("seq", "head", None),
        P(None, "head"),
        P(None, "head", None),
        P("seq", "head"),
        P("seq", "head"),
        P("head"),
        P("head"),
        P("head", None),
    )
    out_specs = P(("seq", "head"), None)
    return jax.shard_map(local, mesh=mesh, in_specs=in_specs, out_specs=out_specs, check_vma=False)
```

time: 121 us -> 127 us (1.050)
  waiting for transfers between devices: 27 us -> 16.6 us
  Pallas kernels: 75.9 us -> 85.3 us
  local copies, waits for them, and re-layouts: 0.35 us -> 5.23 us
  starting transfers between devices: 16.8 us -> 19.3 us
    pallas_call x16 -> x20, Pallas kernels: 72.1 us -> 81.5 us  [the longest x4 21.6 us: scan_part(): pl.pallas_call(functools.partial(scan_kernel, order, part), in_specs=[SCA...]
    ppermute x8 -> x10, waiting for transfers between devices: 22.6 us -> 14.6 us  [swap(): lax.ppermute(block, axis, [(i, i ^ bit) for i in range(lax.axis_size(axis...]
    unnamed x17 -> x23, local copies, waits for them, and re-layouts: 0.26 us -> 5.14 us
    ppermute x8 -> x10, starting transfers between devices: 5.26 us -> 7.83 us  [swap(): lax.ppermute(block, axis, [(i, i ^ bit) for i in range(lax.axis_size(axis...]
    ppermute x7, waiting for transfers between devices: 4.4 us -> 2.02 us  [rotate(): lax.ppermute(block, 'seq', [(i, (i + distance) % size) for i in range(siz...]
  transfers between devices with their start and end apart: 15 -> 17, of which waited for: 6 -> 6; matrix products, arithmetic and copies ran while one was open for 0% -> 0% of each run, Pallas kernels for 59% -> 62%
where the time goes in v9:
time: 127 us
  Pallas kernels  85.3 us (67%)
  starting transfers between devices  19.3 us (15%)
  waiting for transfers between devices  16.6 us (13%)
  local copies, waits for them, and re-layouts  5.23 us (4%)
    pallas_call x4, Pallas kernels, scan_part(): pl.pallas_call(functools.partial(scan_kernel, order, part), in_specs=[SCA...  21.6 us
    pallas_call x3, Pallas kernels, project_both(): pl.pallas_call(functools.partial(both_kernel, first // TILE), grid=(count...  17.9 us
    pallas_call x2, Pallas kernels, conv_states(): pl.pallas_call(functools.partial(conv_kernel, order), grid_spec=pltpu.Pre...  15.9 us
    ppermute x10, waiting for transfers between devices, swap(): lax.ppermute(block, axis, [(i, i ^ bit) for i in range(lax.axis_size(axis...  14.6 us
    ppermute x7, starting transfers between devices, rotate(): lax.ppermute(block, 'seq', [(i, (i + distance) % size) for i in range(siz...  11.5 us
    ppermute x10, starting transfers between devices, swap(): lax.ppermute(block, axis, [(i, i ^ bit) for i in range(lax.axis_size(axis...  7.83 us
    pallas_call x2, Pallas kernels, project_ahead(): pl.pallas_call(functools.partial(ahead_kernel, first // TILE), grid=(coun...  7.68 us
    pallas_call x1, Pallas kernels, project_near(): pl.pallas_call(functools.partial(near_kernel, split), grid=(tiles,), in_s...  6.94 us
  transfers between devices with their start and end apart: 17, of which 6 were waited for; matrix products, arithmetic and copies ran while one was open for 0% of the time, Pallas kernels for 62%

profile of v9, /device:TPU:0, one launch (start us, length us, event | category | flops | bytes accessed | tf_op | source)
XLA Modules:
  0.0 126.7 jit_solution(13701987728446347914)
XLA Ops:
  2.0 2.6 %collective-permute-start = (bf16[16,2560]{1,0:T(8,128)(2,1)}, bf16[16,2560]{1,0:T(8,128)(2,1)}, u32[]{:S(2)}, u32[]{:S(2)}) collective-permute-start(bf16[16,2560]{1,0:T(8,128)(2,1)} %tail_rows.1), channel_id=1, source_target_pairs={{0,4},{4,8},{8,12},{12,16},{16,20},{20,24},{24,28},{28,0},{1,5},{5... | collective-permute-start | bytes 245768 | tf_op jit(solution)/shard_map/ppermute | solution.py:671
  9.0 2.0 %collective-permute-done.halo.bc_halo = bf16[16,2560]{1,0:T(8,128)(2,1)} collective-permute-done((bf16[16,2560]{1,0:T(8,128)(2,1)}, bf16[16,2560]{1,0:T(8,128)(2,1)}, u32[]{:S(2)}, u32[]{:S(2)}) %collective-permute-start) | collective-permute-done | bytes 81952 | tf_op jit(solution)/shard_map/ppermute | solution.py:671
  13.4 8.0 %conv_states.2 = (bf16[1024,1024]{1,0:T(8,128)(2,1)}, bf16[1024,256]{1,0:T(8,128)(2,1)S(1)}, bf16[144,1024]{1,0:T(8,128)(2,1)S(1)}) custom-call(s32[9]{0:T(128)S(1)} %stack.36.info, bf16[1024,2048]{1,0:T(8,128)(2,1)} %x_lead.3, bf16[1024,2048]{1,0:T(8,128)(2,1)} %x_lead.3, bf16[1024,512]{1,0:T(8,128)(2,1)S(1)} %bitcast.14, bf16[1024,512]{1,0:T(8,128)(2,1)S(1)} %bitcast.15, ...), custom_call_target="tpu_custom_call" | custom-call | flops 1 | bytes 1 | tf_op jit(solution)/shard_map/conv_states/pallas_call | solution.py:243
  21.3 7.9 %conv_states.3 = (bf16[1024,1024]{1,0:T(8,128)(2,1)}, bf16[1024,256]{1,0:T(8,128)(2,1)S(1)}, f32[128,1024]{1,0:T(8,128)S(1)}) custom-call(s32[9]{0:T(128)S(1)} %stack.36.info, bf16[1024,2048]{1,0:T(8,128)(2,1)} %x_lead.3, bf16[1024,2048]{1,0:T(8,128)(2,1)} %x_lead.3, bf16[1024,512]{1,0:T(8,128)(2,1)S(1)} %bitcast.16, bf16[1024,512]{1,0:T(8,128)(2,1)S(1)} %bitcast.17, ...), custom_call_target="tpu_custom_call" | custom-call | flops 1 | bytes 1 | tf_op jit(solution)/shard_map/conv_states/pallas_call | solution.py:243
  31.3 2.2 %collective-permute-start.3 = (bf16[144,256]{1,0:T(8,128)(2,1)S(1)}, bf16[144,256]{1,0:T(8,128)(2,1)S(1)}, u32[]{:S(2)}, u32[]{:S(2)}) collective-permute-start(bf16[144,256]{1,0:T(8,128)(2,1)S(1)} %get-tuple-element.54), channel_id=1, source_target_pairs={{0,16},{4,20},{8,24},{12,28},{16,0},{20,4},{24,8},{28,12},{1,17},{... | collective-permute-start | bytes 221192 | tf_op jit(solution)/shard_map/ppermute | solution.py:671
  33.5 1.7 %collective-permute-start.4 = (bf16[144,256]{1,0:T(8,128)(2,1)S(1)}, bf16[144,256]{1,0:T(8,128)(2,1)S(1)}, u32[]{:S(2)}, u32[]{:S(2)}) collective-permute-start(bf16[144,256]{1,0:T(8,128)(2,1)S(1)} %get-tuple-element.55), channel_id=1, source_target_pairs={{0,24},{4,28},{8,0},{12,4},{16,8},{20,12},{24,16},{28,20},{1,25},{... | collective-permute-start | bytes 221192 | tf_op jit(solution)/shard_map/ppermute | solution.py:671
  35.2 5.4 %scan_part.4._.refs_0_.refs_1_.refs_3_ = bf16[1024,1024]{1,0:T(8,128)(2,1)S(1)} custom-call(s32[9]{0:T(128)S(1)} %stack.36.info, bf16[1024,1024]{1,0:T(8,128)(2,1)} %get-tuple-element.56.x_far, bf16[1024,2048]{1,0:T(8,128)(2,1)} %z_far.7, bf16[1024,256]{1,0:T(8,128)(2,1)S(1)} %get-tuple-element.39.bc.bc0, f32[2,1024,16]{2,1,0:T(8,128)S(1)} %get-tuple-element.46.cum, ...), custom_call_target="tpu_custom_call" | custom-call | flops 1 | bytes 1 | tf_op jit(solution)/shard_map/scan_part/pallas_call | solution.py:461
  40.6 5.4 %scan_part.5.refs_4_.refs_1_.refs_2_ = bf16[1024,1024]{1,0:T(8,128)(2,1)S(1)} custom-call(s32[9]{0:T(128)S(1)} %stack.36.info, bf16[1024,1024]{1,0:T(8,128)(2,1)} %get-tuple-element.56.x_far, bf16[1024,2048]{1,0:T(8,128)(2,1)} %z_far.7, bf16[1024,256]{1,0:T(8,128)(2,1)S(1)} %get-tuple-element.39.bc.bc0, f32[2,1024,16]{2,1,0:T(8,128)S(1)} %get-tuple-element.46.cum, ...), custom_call_target="tpu_custom_call" | custom-call | flops 1 | bytes 1 | tf_op jit(solution)/shard_map/scan_part/pallas_call | solution.py:461
  48.5 2.8 %collective-permute-start.7 = (bf16[128,256]{1,0:T(8,128)(2,1)S(1)}, bf16[128,256]{1,0:T(8,128)(2,1)S(1)}, u32[]{:S(2)}, u32[]{:S(2)}) collective-permute-start(bf16[128,256]{1,0:T(8,128)(2,1)S(1)} %get-tuple-element.60), channel_id=1, source_target_pairs={{0,24},{4,28},{8,0},{12,4},{16,8},{20,12},{24,16},{28,20},{1,25},{... | collective-permute-start | bytes 196616 | tf_op jit(solution)/shard_map/ppermute | solution.py:671
  51.3 5.4 %scan_part.6._.refs_2_.refs_3_.refs_5_ = bf16[1024,1024]{1,0:T(8,128)(2,1)S(1)} custom-call(s32[9]{0:T(128)S(1)} %stack.36.info, bf16[1024,1024]{1,0:T(8,128)(2,1)} %get-tuple-element.45.x_far, bf16[1024,2048]{1,0:T(8,128)(2,1)} %z_far.7, bf16[1024,256]{1,0:T(8,128)(2,1)S(1)} %get-tuple-element.40.bc.bc1, f32[2,1024,16]{2,1,0:T(8,128)S(1)} %get-tuple-element.46.cum, ...), custom_call_target="tpu_custom_call" | custom-call | flops 1 | bytes 1 | tf_op jit(solution)/shard_map/scan_part/pallas_call | solution.py:461
  58.9 5.4 %scan_part.7.refs_3_.refs_4_.refs_6_ = bf16[1024,1024]{1,0:T(8,128)(2,1)S(1)} custom-call(s32[9]{0:T(128)S(1)} %stack.36.info, bf16[1024,1024]{1,0:T(8,128)(2,1)} %get-tuple-element.45.x_far, bf16[1024,2048]{1,0:T(8,128)(2,1)} %z_far.7, bf16[1024,256]{1,0:T(8,128)(2,1)S(1)} %get-tuple-element.40.bc.bc1, f32[2,1024,16]{2,1,0:T(8,128)S(1)} %get-tuple-element.46.cum, ...), custom_call_target="tpu_custom_call" | custom-call | flops 1 | bytes 1 | tf_op jit(solution)/shard_map/scan_part/pallas_call | solution.py:461
  68.5 4.6 %project_ahead.2.refs_0_ = bf16[256,1024]{1,0:T(8,128)(2,1)S(1)} custom-call(bf16[256,2048]{1,0:T(8,128)(2,1)S(1)} %norm_rows.5.own.refs_0_, bf16[256,2048]{1,0:T(8,128)(2,1)S(1)} %collective-permute-done.9.mate.mate0, bf16[2048,4096]{1,0:T(8,128)(2,1)} %w0_far.11, bf16[2048,4096]{1,0:T(8,128)(2,1)} %collective-permute-done.10.w1_far), custom_call_target="tpu_custom_call" | custom-call | flops 1 | bytes 1 | tf_op jit(solution)/shard_map/project_ahead/pallas_call | solution.py:568
  74.9 3.1 %project_ahead.3 = bf16[256,512]{1,0:T(8,128)(2,1)S(1)} custom-call(bf16[256,2048]{1,0:T(8,128)(2,1)S(1)} %norm_rows.5.own.refs_0_, bf16[256,2048]{1,0:T(8,128)(2,1)S(1)} %collective-permute-done.9.mate.mate0, bf16[2048,4096]{1,0:T(8,128)(2,1)} %w0_far.11, bf16[2048,4096]{1,0:T(8,128)(2,1)} %collective-permute-done.10.w1_far), custom_call_target="tpu_custom_call" | custom-call | flops 1 | bytes 1 | tf_op jit(solution)/shard_map/project_ahead/pallas_call | solution.py:568
  78.0 1.6 %collective-permute-start.11 = (bf16[256,512]{1,0:T(8,128)(2,1)S(1)}, bf16[256,512]{1,0:T(8,128)(2,1)S(1)}, u32[]{:S(2)}, u32[]{:S(2)}) collective-permute-start(bf16[256,512]{1,0:T(8,128)(2,1)S(1)} %project_ahead.3), channel_id=1, source_target_pairs={{0,2},{1,3},{2,0},{3,1},{4,6},{5,7},{6,4},{7,5},{8,10},{9,11},{10,... | collective-permute-start | bytes 786440 | tf_op jit(solution)/shard_map/ppermute | solution.py:666
  80.1 7.1 %collective-permute-done.11.refs_2_.arrived0 = bf16[256,512]{1,0:T(8,128)(2,1)S(1)} collective-permute-done((bf16[256,512]{1,0:T(8,128)(2,1)S(1)}, bf16[256,512]{1,0:T(8,128)(2,1)S(1)}, u32[]{:S(2)}, u32[]{:S(2)}) %collective-permute-start.11) | collective-permute-done | bytes 262176 | tf_op jit(solution)/shard_map/ppermute | solution.py:666
  87.2 1.6 %norm_rows.7.owns = bf16[512,2048]{1,0:T(8,128)(2,1)S(1)} custom-call(s32[9]{0:T(128)S(1)} %stack.36.info, bf16[1024,256]{1,0:T(8,128)(2,1)S(1)} %get-tuple-element.39.bc.bc0, bf16[1024,256]{1,0:T(8,128)(2,1)S(1)} %get-tuple-element.40.bc.bc1, bf16[128,1024]{1,0:T(8,128)(2,1)S(1)} %collective-permute-done.8.state0, ...), custom_call_target="tpu_custom_call" | custom-call | flops 1 | bytes 1 | tf_op jit(solution)/shard_map/norm_rows/pallas_call | solution.py:513
  88.7 6.9 %project_both.5 = (bf16[256,1024]{1,0:T(8,128)(2,1)S(1)}, f32[256,1024]{1,0:T(8,128)S(1)}) custom-call(bf16[512,2048]{1,0:T(8,128)(2,1)S(1)} %norm_rows.7.owns, bf16[256,2048]{1,0:T(8,128)(2,1)S(1)} %collective-permute-done.9.mate.mate0, bf16[256,2048]{1,0:T(8,128)(2,1)S(1)} %collective-permute-done.12.mate1.mate, bf16[2048,4096]{1,0:T(8,128)(2,1)} %w0_far.11, ...), custom_call_target="tpu_custom_call" | custom-call | flops 1 | bytes 1 | tf_op jit(solution)/shard_map/project_both/pallas_call | solution.py:598
  95.6 1.6 %collective-permute-start.15 = (bf16[256,1024]{1,0:T(8,128)(2,1)S(1)}, bf16[256,1024]{1,0:T(8,128)(2,1)S(1)}, u32[]{:S(2)}, u32[]{:S(2)}) collective-permute-start(bf16[256,1024]{1,0:T(8,128)(2,1)S(1)} %get-tuple-element.68), channel_id=1, source_target_pairs={{0,2},{1,3},{2,0},{3,1},{4,6},{5,7},{6,4},{7,5},{8,10},{9,11},{10,... | collective-permute-start | bytes 1572872 | tf_op jit(solution)/shard_map/ppermute | solution.py:666
  97.2 6.8 %project_both.4 = (bf16[256,1024]{1,0:T(8,128)(2,1)S(1)}, f32[256,1024]{1,0:T(8,128)S(1)}) custom-call(bf16[512,2048]{1,0:T(8,128)(2,1)S(1)} %norm_rows.7.owns, bf16[256,2048]{1,0:T(8,128)(2,1)S(1)} %collective-permute-done.9.mate.mate0, bf16[256,2048]{1,0:T(8,128)(2,1)S(1)} %collective-permute-done.12.mate1.mate, bf16[2048,4096]{1,0:T(8,128)(2,1)} %w0_far.11, ...), custom_call_target="tpu_custom_call" | custom-call | flops 1 | bytes 1 | tf_op jit(solution)/shard_map/project_both/pallas_call | solution.py:598
  104.6 4.2 %project_both.3 = (bf16[256,512]{1,0:T(8,128)(2,1)S(1)}, f32[256,512]{1,0:T(8,128)S(1)}) custom-call(bf16[512,2048]{1,0:T(8,128)(2,1)S(1)} %norm_rows.7.owns, bf16[256,2048]{1,0:T(8,128)(2,1)S(1)} %collective-permute-done.9.mate.mate0, bf16[256,2048]{1,0:T(8,128)(2,1)S(1)} %collective-permute-done.12.mate1.mate, bf16[2048,4096]{1,0:T(8,128)(2,1)} %w0_far.11, ...), custom_call_target="tpu_custom_call" | custom-call | flops 1 | bytes 1 | tf_op jit(solution)/shard_map/project_both/pallas_call | solution.py:598
  108.8 1.6 %collective-permute-start.13 = (bf16[256,512]{1,0:T(8,128)(2,1)S(1)}, bf16[256,512]{1,0:T(8,128)(2,1)S(1)}, u32[]{:S(2)}, u32[]{:S(2)}) collective-permute-start(bf16[256,512]{1,0:T(8,128)(2,1)S(1)} %get-tuple-element.64), channel_id=1, source_target_pairs={{0,2},{1,3},{2,0},{3,1},{4,6},{5,7},{6,4},{7,5},{8,10},{9,11},{10,... | collective-permute-start | bytes 786440 | tf_op jit(solution)/shard_map/ppermute | solution.py:666
  110.4 6.9 %project_near.1._ = bf16[256,4096]{1,0:T(8,128)(2,1)} custom-call(bf16[512,2048]{1,0:T(8,128)(2,1)S(1)} %norm_rows.7.owns, bf16[256,2048]{1,0:T(8,128)(2,1)S(1)} %collective-permute-done.12.mate1.mate, bf16[2048,4096]{1,0:T(8,128)(2,1)} %w0_far.11, bf16[2048,4096]{1,0:T(8,128)(2,1)} %collective-permute-done.10.w1_far, ...), custom_call_target="tpu_custom_call" | custom-call | flops 1 | bytes 1 | tf_op jit(solution)/shard_map/project_near/pallas_call | solution.py:623
  118.9 2.9 %collective-permute-done.14.arrived = bf16[256,1024]{1,0:T(8,128)(2,1)S(1)} collective-permute-done((bf16[256,1024]{1,0:T(8,128)(2,1)S(1)}, bf16[256,1024]{1,0:T(8,128)(2,1)S(1)}, u32[]{:S(2)}, u32[]{:S(2)}) %collective-permute-start.14) | collective-permute-done | bytes 524320 | tf_op jit(solution)/shard_map/ppermute | solution.py:666
  123.3 2.6 %collective-permute-done.13.arrived = bf16[256,512]{1,0:T(8,128)(2,1)S(1)} collective-permute-done((bf16[256,512]{1,0:T(8,128)(2,1)S(1)}, bf16[256,512]{1,0:T(8,128)(2,1)S(1)}, u32[]{:S(2)}, u32[]{:S(2)}) %collective-permute-start.13) | collective-permute-done | bytes 262176 | tf_op jit(solution)/shard_map/ppermute | solution.py:666
  (58 shorter events, 26.2 us)
Async XLA Ops:
  0.0 4.6 %copy-start.10 = (bf16[1024,2,256]{2,1,0:T(2,128)(2,1)S(1)}, bf16[1024,2,256]{2,1,0:T(2,128)(2,1)}, u32[]{:S(2)}) copy-start(bf16[1024,2,256]{2,1,0:T(2,128)(2,1)} %bc.1) | copy-start | bytes 3145732
  0.0 68.5 %collective-permute-start.10 = (bf16[2048,4096]{1,0:T(8,128)(2,1)}, bf16[2048,4096]{1,0:T(8,128)(2,1)}, u32[]{:S(2)}, u32[]{:S(2)}) collective-permute-start(bf16[2048,4096]{1,0:T(8,128)(2,1)} %w0_far.11), channel_id=1, source_target_pairs={{0,1},{1,0},{2,3},{3,2},{4,5},{5,4},{6,7},{7,6},{8,9},{9,8},{10,11... | collective-permute-start | bytes 50331656 | tf_op jit(solution)/shard_map/ppermute | solution.py:666
  2.0 2.8 %copy-start = (bf16[64,2048]{1,0:T(8,128)(2,1)S(1)}, bf16[64,2048]{1,0:T(8,128)(2,1)}, u32[]{:S(2)}) copy-start(bf16[64,2048]{1,0:T(8,128)(2,1)} %constant.17.clone.ones) | copy-start | bytes 786436
  2.0 2.9 %copy-start.9 = (f32[32]{0:T(128)S(1)}, f32[32]{0:T(128)}, u32[]{:S(2)}) copy-start(f32[32]{0:T(128)} %param.18) | copy-start | bytes 388
  2.0 9.0 %collective-permute-start = (bf16[16,2560]{1,0:T(8,128)(2,1)}, bf16[16,2560]{1,0:T(8,128)(2,1)}, u32[]{:S(2)}, u32[]{:S(2)}) collective-permute-start(bf16[16,2560]{1,0:T(8,128)(2,1)} %tail_rows.1), channel_id=1, source_target_pairs={{0,4},{4,8},{8,12},{12,16},{16,20},{20,24},{24,28},{28,0},{1,5},{5... | collective-permute-start | bytes 245768 | tf_op jit(solution)/shard_map/ppermute | solution.py:671
  4.8 0.9 copy-start.5
  11.0 1.0 copy-start.2
  13.4 8.0 %copy-start.3 = (bf16[1024,64]{1,0:T(8,128)(2,1)S(1)}, bf16[1024,64]{1,0:T(8,128)(2,1)}, u32[]{:S(2)}) copy-start(bf16[1024,64]{1,0:T(8,128)(2,1)} %copy-done.1) | copy-start | bytes 393220
  21.3 8.8 %collective-permute-start.1 = (bf16[144,1024]{1,0:T(8,128)(2,1)S(1)}, bf16[144,1024]{1,0:T(8,128)(2,1)S(1)}, u32[]{:S(2)}, u32[]{:S(2)}) collective-permute-start(bf16[144,1024]{1,0:T(8,128)(2,1)S(1)} %get-tuple-element.41), channel_id=1, source_target_pairs={{0,4},{4,0},{8,12},{12,8},{16,20},{20,16},{24,28},{28,24},{1,5},{5... | collective-permute-start | bytes 884744 | tf_op jit(solution)/shard_map/ppermute | solution.py:666
  31.0 15.1 %collective-permute-start.2 = (bf16[144,256]{1,0:T(8,128)(2,1)S(1)}, bf16[144,256]{1,0:T(8,128)(2,1)S(1)}, u32[]{:S(2)}, u32[]{:S(2)}) collective-permute-start(bf16[144,256]{1,0:T(8,128)(2,1)S(1)} %get-tuple-element.53), channel_id=1, source_target_pairs={{0,8},{4,12},{8,16},{12,20},{16,24},{20,28},{24,0},{28,4},{1,9},{5... | collective-permute-start | bytes 221192 | tf_op jit(solution)/shard_map/ppermute | solution.py:671
  31.3 14.8 %collective-permute-start.3 = (bf16[144,256]{1,0:T(8,128)(2,1)S(1)}, bf16[144,256]{1,0:T(8,128)(2,1)S(1)}, u32[]{:S(2)}, u32[]{:S(2)}) collective-permute-start(bf16[144,256]{1,0:T(8,128)(2,1)S(1)} %get-tuple-element.54), channel_id=1, source_target_pairs={{0,16},{4,20},{8,24},{12,28},{16,0},{20,4},{24,8},{28,12},{1,17},{... | collective-permute-start | bytes 221192 | tf_op jit(solution)/shard_map/ppermute | solution.py:671
  33.5 12.6 %collective-permute-start.4 = (bf16[144,256]{1,0:T(8,128)(2,1)S(1)}, bf16[144,256]{1,0:T(8,128)(2,1)S(1)}, u32[]{:S(2)}, u32[]{:S(2)}) collective-permute-start(bf16[144,256]{1,0:T(8,128)(2,1)S(1)} %get-tuple-element.55), channel_id=1, source_target_pairs={{0,24},{4,28},{8,0},{12,4},{16,8},{20,12},{24,16},{28,20},{1,25},{... | collective-permute-start | bytes 221192 | tf_op jit(solution)/shard_map/ppermute | solution.py:671
  46.7 10.0 %collective-permute-start.5 = (bf16[128,256]{1,0:T(8,128)(2,1)S(1)}, bf16[128,256]{1,0:T(8,128)(2,1)S(1)}, u32[]{:S(2)}, u32[]{:S(2)}) collective-permute-start(bf16[128,256]{1,0:T(8,128)(2,1)S(1)} %get-tuple-element.58), channel_id=1, source_target_pairs={{0,8},{4,12},{8,16},{12,20},{16,24},{20,28},{24,0},{28,4},{1,9},{5... | collective-permute-start | bytes 196616 | tf_op jit(solution)/shard_map/ppermute | solution.py:671
  47.1 9.7 %collective-permute-start.6 = (bf16[128,256]{1,0:T(8,128)(2,1)S(1)}, bf16[128,256]{1,0:T(8,128)(2,1)S(1)}, u32[]{:S(2)}, u32[]{:S(2)}) collective-permute-start(bf16[128,256]{1,0:T(8,128)(2,1)S(1)} %get-tuple-element.59), channel_id=1, source_target_pairs={{0,16},{4,20},{8,24},{12,28},{16,0},{20,4},{24,8},{28,12},{1,17},{... | collective-permute-start | bytes 196616 | tf_op jit(solution)/shard_map/ppermute | solution.py:671
  48.5 8.3 %collective-permute-start.7 = (bf16[128,256]{1,0:T(8,128)(2,1)S(1)}, bf16[128,256]{1,0:T(8,128)(2,1)S(1)}, u32[]{:S(2)}, u32[]{:S(2)}) collective-permute-start(bf16[128,256]{1,0:T(8,128)(2,1)S(1)} %get-tuple-element.60), channel_id=1, source_target_pairs={{0,24},{4,28},{8,0},{12,4},{16,8},{20,12},{24,16},{28,20},{1,25},{... | collective-permute-start | bytes 196616 | tf_op jit(solution)/shard_map/ppermute | solution.py:671
  57.6 6.7 %copy-start.7 = (f32[2048]{0:T(1024)S(1)}, f32[2048]{0:T(1024)}, u32[]{:S(2)}) copy-start(f32[2048]{0:T(1024)} %param.19) | copy-start | bytes 24580
  57.6 6.7 %collective-permute-start.8 = (bf16[128,1024]{1,0:T(8,128)(2,1)S(1)}, bf16[128,1024]{1,0:T(8,128)(2,1)S(1)}, u32[]{:S(2)}, u32[]{:S(2)}) collective-permute-start(bf16[128,1024]{1,0:T(8,128)(2,1)S(1)} %get-tuple-element.61._), channel_id=1, source_target_pairs={{0,4},{4,0},{8,12},{12,8},{16,20},{20,16},{24,28},{28,24},{1,5},{5... | collective-permute-start | bytes 786440 | tf_op jit(solution)/shard_map/ppermute | solution.py:666
  65.8 2.7 %collective-permute-start.9 = (bf16[256,2048]{1,0:T(8,128)(2,1)S(1)}, bf16[256,2048]{1,0:T(8,128)(2,1)S(1)}, u32[]{:S(2)}, u32[]{:S(2)}) collective-permute-start(bf16[256,2048]{1,0:T(8,128)(2,1)S(1)} %norm_rows.4.refs_0_), channel_id=1, source_target_pairs={{0,1},{1,0},{2,3},{3,2},{4,5},{5,4},{6,7},{7,6},{8,9},{9,8},{10,11... | collective-permute-start | bytes 3145736 | tf_op jit(solution)/shard_map/ppermute | solution.py:666
  74.7 14.1 %collective-permute-start.12 = (bf16[256,2048]{1,0:T(8,128)(2,1)S(1)}, bf16[256,2048]{1,0:T(8,128)(2,1)S(1)}, u32[]{:S(2)}, u32[]{:S(2)}) collective-permute-start(bf16[256,2048]{1,0:T(8,128)(2,1)S(1)} %norm_rows.6.refs_1_), channel_id=1, source_target_pairs={{0,1},{1,0},{2,3},{3,2},{4,5},{5,4},{6,7},{7,6},{8,9},{9,8},{10,11... | collective-permute-start | bytes 3145736 | tf_op jit(solution)/shard_map/ppermute | solution.py:666
  78.0 9.2 %collective-permute-start.11 = (bf16[256,512]{1,0:T(8,128)(2,1)S(1)}, bf16[256,512]{1,0:T(8,128)(2,1)S(1)}, u32[]{:S(2)}, u32[]{:S(2)}) collective-permute-start(bf16[256,512]{1,0:T(8,128)(2,1)S(1)} %project_ahead.3), channel_id=1, source_target_pairs={{0,2},{1,3},{2,0},{3,1},{4,6},{5,7},{6,4},{7,5},{8,10},{9,11},{10,... | collective-permute-start | bytes 786440 | tf_op jit(solution)/shard_map/ppermute | solution.py:666
  79.5 30.8 %collective-permute-start.16 = (bf16[256,1024]{1,0:T(8,128)(2,1)S(1)}, bf16[256,1024]{1,0:T(8,128)(2,1)S(1)}, u32[]{:S(2)}, u32[]{:S(2)}) collective-permute-start(bf16[256,1024]{1,0:T(8,128)(2,1)S(1)} %project_ahead.2.refs_0_), channel_id=1, source_target_pairs={{0,2},{1,3},{2,0},{3,1},{4,6},{5,7},{6,4},{7,5},{8,10},{9,11},{10,... | collective-permute-start | bytes 1572872 | tf_op jit(solution)/shard_map/ppermute | solution.py:666
  95.6 21.7 %collective-permute-start.15 = (bf16[256,1024]{1,0:T(8,128)(2,1)S(1)}, bf16[256,1024]{1,0:T(8,128)(2,1)S(1)}, u32[]{:S(2)}, u32[]{:S(2)}) collective-permute-start(bf16[256,1024]{1,0:T(8,128)(2,1)S(1)} %get-tuple-element.68), channel_id=1, source_target_pairs={{0,2},{1,3},{2,0},{3,1},{4,6},{5,7},{6,4},{7,5},{8,10},{9,11},{10,... | collective-permute-start | bytes 1572872 | tf_op jit(solution)/shard_map/ppermute | solution.py:666
  104.0 17.8 %collective-permute-start.14 = (bf16[256,1024]{1,0:T(8,128)(2,1)S(1)}, bf16[256,1024]{1,0:T(8,128)(2,1)S(1)}, u32[]{:S(2)}, u32[]{:S(2)}) collective-permute-start(bf16[256,1024]{1,0:T(8,128)(2,1)S(1)} %get-tuple-element.66), channel_id=1, source_target_pairs={{0,2},{1,3},{2,0},{3,1},{4,6},{5,7},{6,4},{7,5},{8,10},{9,11},{10,... | collective-permute-start | bytes 1572872 | tf_op jit(solution)/shard_map/ppermute | solution.py:666
  108.8 17.1 %collective-permute-start.13 = (bf16[256,512]{1,0:T(8,128)(2,1)S(1)}, bf16[256,512]{1,0:T(8,128)(2,1)S(1)}, u32[]{:S(2)}, u32[]{:S(2)}) collective-permute-start(bf16[256,512]{1,0:T(8,128)(2,1)S(1)} %get-tuple-element.64), channel_id=1, source_target_pairs={{0,2},{1,3},{2,0},{3,1},{4,6},{5,7},{6,4},{7,5},{8,10},{9,11},{10,... | collective-permute-start | bytes 786440 | tf_op jit(solution)/shard_map/ppermute | solution.py:666
  (4 other events, 3.1 us)

commit v10 on v9

--- a/solution.py
+++ b/solution.py
@@ -2,7 +2,6 @@
 
 import jax
 import jax.numpy as jnp
-import numpy as np
 from jax import lax
 from jax.experimental import pallas as pl
 from jax.experimental.pallas import tpu as pltpu
@@ -59,27 +58,40 @@
     return pl.BlockSpec(shape, lambda *_: (0,) * len(shape))
 
 
-def decay_kernel(ld_t, step_t, skip, ones, cum, cum_s, log_s, f_dev, f_blk, e_blk, rates, by_row):
+def decay_kernel(info, ld_t, step_t, skip, cum, cum_s, log_s, f_dev, f_blk, e_blk, rates, by_row, ones):
     heads, length = ld_t.shape
     blocks = length // TOK_B
+    per = heads // 2
+    width = rates.shape[2]
+    swapped = info[GROUP] == 1
     row = lax.broadcasted_iota(jnp.int32, (TOK_B, TOK_B), 0)
     col = lax.broadcasted_iota(jnp.int32, (TOK_B, TOK_B), 1)
     lower = (row >= col).astype(F32)
     upper = (row <= col).astype(F32)
     eye = (row == col).astype(BF16)
 
+    def ordered(value):
+        return jnp.where(swapped, jnp.concatenate([value[per:], value[:per]], 0), value)
+
     def put(ref, rows, value):
         high = value.astype(BF16)
         low = (value - high.astype(F32)).astype(BF16)
-        ref[rows, :] = dot(eye, jnp.concatenate([high, low], 0), ((1,), (1,))).astype(BF16)
-
+        for g in range(2):
+            own = slice(g * per, (g + 1) * per)
+            both = jnp.concatenate([high[own], low[own]], 0)
+            ref[g, rows, :] = dot(eye, both, ((1,), (1,))).astype(BF16)
+
+    member = lax.broadcasted_iota(jnp.int32, (per, width), 0) == lax.broadcasted_iota(jnp.int32, (per, width), 1) // P_SIZE
+    member = member.astype(F32)
+    ones[0:per, :] = member.astype(BF16)
+    ones[per:, :] = member.astype(BF16)
     cums, totals, row_totals = [], [], []
     for b in range(blocks):
         rows = slice(b * TOK_B, (b + 1) * TOK_B)
-        logs = ld_t[:, rows] * LOG2E
+        logs = ordered(ld_t[:, rows]) * LOG2E
         c = dot(lower, logs, ((1,), (1,)), HIGHEST)
-        for g in range(cum.shape[0]):
-            cum[g, rows, :] = c[:, g * cum.shape[2] : (g + 1) * cum.shape[2]]
+        for g in range(2):
+            cum[g, rows, :] = c[:, g * per : (g + 1) * per]
         row_totals.append(c[TOK_B - 1 : TOK_B, :])
         c = dot(logs, upper, precision=HIGHEST)
         cums.append(c)
@@ -90,19 +102,22 @@
         row_before.append(row_before[-1] + row_totals[b])
     total = before[-1]
     logs = jnp.concatenate(row_totals + row_before[:-1] + row_before[-1:] * 8, 0)
-    values = jnp.concatenate([jnp.exp2(logs), jnp.broadcast_to(skip[...], (8, heads))], 0)
-    spread = dot(values, ones[0:heads, :].astype(F32), precision=HIGHEST)
-    rates[...] = spread
-    for b in range(2 * blocks):
-        by_row[b] = spread[b : b + 1, :]
-    by_row[2 * blocks] = spread[2 * blocks + 8 : 2 * blocks + 9, :]
+    gains = jnp.broadcast_to(skip[...], (8, heads))
+    gains = jnp.where(swapped, jnp.concatenate([gains[:, per:], gains[:, :per]], 1), gains)
+    values = jnp.concatenate([jnp.exp2(logs), gains], 0)
+    for g in range(2):
+        spread = dot(values[:, g * per : (g + 1) * per], member, precision=HIGHEST)
+        rates[g] = spread
+        for b in range(2 * blocks):
+            by_row[g, b] = spread[b : b + 1, :]
+        by_row[g, 2 * blocks] = spread[2 * blocks + 8 : 2 * blocks + 9, :]
     for b in range(blocks):
         rows = slice(b * TOK_B, (b + 1) * TOK_B)
-        s = step_t[:, rows]
+        s = ordered(step_t[:, rows])
         log_step = jnp.log2(s)
         shifted = cums[b] - log_step
-        for g in range(cum.shape[0]):
-            own = slice(g * cum.shape[2], (g + 1) * cum.shape[2])
+        for g in range(2):
+            own = slice(g * per, (g + 1) * per)
             log_s[g, :, rows] = log_step[own, :]
             cum_s[g, :, rows] = shifted[own, :]
         put(f_dev, rows, jnp.exp2(total - (cums[b] + before[b])) * s)
@@ -110,27 +125,32 @@
         put(e_blk, rows, jnp.exp2(cums[b]))
 
 
-def decays(groups, log_decay, step, skip, ones):
+def decays(info, log_decay, step, skip, width):
     length, heads = log_decay.shape
     blocks = length // TOK_B
-    width = ones.shape[1]
-    wide = jax.ShapeDtypeStruct((groups, heads // groups, length), F32)
-    pair = jax.ShapeDtypeStruct((length, 2 * heads), BF16)
+    per = heads // 2
+    across = jax.ShapeDtypeStruct((2, per, length), F32)
+    pair = jax.ShapeDtypeStruct((2, length, 2 * per), BF16)
+    shapes = (
+        jax.ShapeDtypeStruct((2, length, per), F32),
+        across,
+        across,
+        pair,
+        pair,
+        pair,
+        jax.ShapeDtypeStruct((2, 2 * blocks + 16, width), F32),
+        jax.ShapeDtypeStruct((2, 2 * blocks + 1, 1, width), F32),
+        jax.ShapeDtypeStruct((2 * per, width), BF16),
+    )
     return pl.pallas_call(
         decay_kernel,
-        out_shape=(
-            jax.ShapeDtypeStruct((groups, length, heads // groups), F32),
-            wide,
-            wide,
-            pair,
-            pair,
-            pair,
-            jax.ShapeDtypeStruct((2 * blocks + 16, width), F32),
-            jax.ShapeDtypeStruct((2 * blocks + 1, 1, width), F32),
-        ),
+        in_specs=[SCALAR] + [FULL] * 3,
+        out_specs=[FULL] * len(shapes),
+        out_shape=shapes,
         compiler_params=params(16),
+        cost_estimate=CHEAP,
         name="decays",
-    )(log_decay.T, step.T, skip[None, :], ones)
+    )(info, *far(log_decay.T, step.T, skip[None, :]))
 
 
 def tail_kernel(x, bc, out):
@@ -174,7 +194,7 @@
 
 
 def conv_kernel(
-    order, info, x, x_lead, bc, bc_lead, halo, bc_halo, wx, wbc, f_dev, ones, rates, x_out, bc_out, final, xf, state
+    order, info, x, x_lead, bc, bc_lead, halo, bc_halo, wx, wbc, f_dev, ones, rates, x_out, bc_out, final, xf, state, down
 ):
     i = pl.program_id(0)
     rows, width = x.shape
@@ -183,51 +203,55 @@
     @pl.when(i == 0)
     def _():
         state[...] = jnp.zeros_like(state)
+        row = lax.broadcasted_iota(jnp.int32, down.shape, 0)
+        col = lax.broadcasted_iota(jnp.int32, down.shape, 1)
+        down[...] = (row == col + 1).astype(BF16)
 
     def conv(src, first, behind, weights, emit):
         at_start = jnp.where(info[SEQ] == 0, jnp.zeros_like(first), first)
         lead = jnp.where(i == 0, at_start, behind).astype(F32)
         w0, w1, w2, w3 = [w * 0.5 for w in weights]
         back = LEAD - 8
-        r1 = pltpu.roll(lead, 1, 0)
-        last_x, last_p = lead[back:], (w1 * lead + w0 * r1)[back:]
+        lead_r1 = pltpu.roll(lead, 1, 0)
+        last_p = (w1 * lead + w0 * lead_r1)[back:]
+        moved = dot(down[...], src)
+        top = lax.broadcasted_iota(jnp.int32, (8, lead.shape[1]), 0) == 0
+        head = jnp.where(top, jnp.broadcast_to(lead[LEAD - 1 :], top.shape), moved[0:8])
         for r in range(0, rows, ROWS_A):
-            cur = src(r).astype(F32)
-            r1 = pltpu.roll(jnp.concatenate([last_x, cur], 0), 1, 0)[8:]
+            cur = src[r : r + ROWS_A].astype(F32)
+            r1 = moved[r : r + ROWS_A] if r else jnp.concatenate([head, moved[8:ROWS_A]], 0)
             p = w1 * cur + w0 * r1
             p2 = pltpu.roll(jnp.concatenate([last_p, p], 0), 2, 0)[8:]
             emit(r, half_silu((w3 * cur + w2 * r1) + p2))
-            last_x, last_p = cur[ROWS_A - 8 :], p[ROWS_A - 8 :]
-
-    for lanes in range(0, 2 * N, N):
-        ds = slice(lanes, lanes + N)
+            last_p = p[ROWS_A - 8 :]
+
+    for lanes in range(0, 2 * N, SLAB):
+        ds = slice(lanes, lanes + SLAB)
 
         def emit_bc(r, value):
             bc_out[r : r + ROWS_A, ds] = value.astype(BF16)
 
         weights = [jnp.where(group == 0, wbc[k, 0:1, ds], wbc[k, 1:2, ds]) for k in range(KCONV)]
-        conv(lambda r: bc[r : r + ROWS_A, ds], bc_halo[:, ds], bc_lead[:, ds], weights, emit_bc)
-
-    def slab(c, _):
-        ds = pl.ds(pl.multiple_of(c * SLAB, SLAB), SLAB)
-        scale = dot(f_dev[...], ones[:, ds])
+        conv(bc[:, ds], bc_halo[:, ds], bc_lead[:, ds], weights, emit_bc)
+
+    for lanes in range(0, width, SLAB):
+        ds = slice(lanes, lanes + SLAB)
+        scale = dot(f_dev[0], ones[:, ds])
 
         def emit(r, value):
             x_out[r : r + ROWS_A, ds] = value.astype(BF16)
             xf[r : r + ROWS_A, ds] = (value * scale[r : r + ROWS_A]).astype(BF16)
 
         weights = [wx[k : k + 1, ds] for k in range(KCONV)]
-        conv(lambda r: x[r : r + ROWS_A, ds], halo[:, ds], x_lead[:, ds], weights, emit)
-        return 0
-
-    lax.fori_loop(0, width // SLAB, slab, 0)
+        conv(x[:, ds], halo[:, ds], x_lead[:, ds], weights, emit)
+
     state[...] += dot(bc_out[:, 0:N], xf[...], ((0,), (0,)))
 
     @pl.when(i == pl.num_programs(0) - 1)
     def _():
         if order == 0:
-            row = rates.shape[0] - 16
-            put_message(final, state[...], rates[row : row + 1, :])
+            row = rates.shape[1] - 16
+            put_message(final, state[...], rates[0, row : row + 1, :])
         else:
             final[...] = state[...]
 
@@ -254,16 +278,20 @@
                 pl.BlockSpec((LEAD, 2 * N), lambda i, info: (0, full // (2 * N) + info[GROUP + order])),
                 pl.BlockSpec((KCONV, width), column),
                 whole(wbc.shape),
-                pl.BlockSpec((TOK_A, f_dev.shape[1]), rows),
-                pl.BlockSpec((ones.shape[0], width), column),
-                pl.BlockSpec((rates.shape[0], width), column),
+                pl.BlockSpec((1, TOK_A, f_dev.shape[2]), lambda i, info: (order, i, 0)),
+                whole(ones.shape),
+                pl.BlockSpec((1,) + rates.shape[1:], lambda i, info: (order, 0, 0)),
             ],
             out_specs=[
                 pl.BlockSpec((TOK_A, width), rows),
                 pl.BlockSpec((TOK_A, 2 * N), rows),
                 whole(final[0]),
             ],
-            scratch_shapes=[pltpu.VMEM((TOK_A, width), BF16), pltpu.VMEM((N, width), F32)],
+            scratch_shapes=[
+                pltpu.VMEM((TOK_A, width), BF16),
+                pltpu.VMEM((N, width), F32),
+                pltpu.VMEM((TOK_A, TOK_A), BF16),
+            ],
         ),
         out_shape=(
             pltpu.HBM((length, width), BF16),
@@ -280,8 +308,8 @@
     half = keep.shape[1]
     is_odd = info[ODD] == 1
     arrived, their = take_message(got)
-    row = rates.shape[0] - 16
-    mine = rates[row : row + 1, pl.ds(pl.multiple_of(info[GROUP + 1] * half, half), half)]
+    row = rates.shape[1] - 16
+    mine = rates[1, row : row + 1, :]
     early = jnp.where(is_odd, arrived, keep[...])
     late = jnp.where(is_odd, keep[...], arrived)
     even_decay = jnp.where(is_odd, their, mine)
@@ -323,8 +351,8 @@
     piece = half // pairs
     is_odd = info[ODD] == 1
     arrived, their = take_message(got)
-    row = rates.shape[0] - 16
-    mine = rates[row : row + 1, pl.ds(pl.multiple_of(info[GROUP + 1] * half, half), half)]
+    row = rates.shape[1] - 16
+    mine = rates[1, row : row + 1, :]
     early = jnp.where(is_odd, arrived, keep[...])
     late = jnp.where(is_odd, keep[...], arrived)
     even_decay = jnp.where(is_odd, their, mine)
@@ -385,9 +413,8 @@
     per_slab = SLAB // P_SIZE
     inner = STEP_B // TOK_B
     blocks = length // TOK_B
-    group = info[GROUP + order]
     first_head = part * width // P_SIZE
-    first_lane = group * x_far.shape[1] + part * width
+    first_lane = info[GROUP + order] * x_far.shape[1] + part * width
 
     def fetch(step):
         piece = pl.ds(pl.multiple_of(step * STEP_B, STEP_B), STEP_B)
@@ -420,26 +447,27 @@
         at = pl.ds(pl.multiple_of(b * TOK_B, TOK_B), TOK_B)
         b_mat = bc[at, 0:N]
         c_mat = bc[at, N : 2 * N]
+        b_across = b_mat.T
         scores = jnp.where(keep, dot(c_mat, b_mat, ((1,), (1,))), 0.0)
         for s in range(width // SLAB):
             lanes = slice(s * SLAB, (s + 1) * SLAB)
             xb = x[at, lanes]
-            wide = pl.ds(pl.multiple_of(first_lane + s * SLAB, SLAB), SLAB)
+            wide = slice(part * width + s * SLAB, part * width + (s + 1) * SLAB)
             sel = ones[:, wide]
-            fade_row = by_row[b, :, wide]
-            lead_row = by_row[blocks + b, :, wide]
-            skip = by_row[2 * blocks, :, wide]
+            fade_row = by_row[order, b, :, wide]
+            lead_row = by_row[order, blocks + b, :, wide]
+            skip = by_row[order, 2 * blocks, :, wide]
             old = state[:, lanes]
-            rise = dot(e_blk[at, :], sel)
+            rise = dot(e_blk[order, at, :], sel)
             carried = dot(c_mat, old.astype(BF16)) * rise
             within = []
             for q in range(per_slab // 2):
                 tables = []
                 for h in (2 * q, 2 * q + 1):
                     head = first_head + s * per_slab + h
-                    column = cum[group, at, head : head + 1]
+                    column = cum[order, at, head : head + 1]
                     own = slice(head, head + 1)
-                    gap = jnp.minimum(column - cum_s[group, own, at], log_s[group, own, at])
+                    gap = jnp.minimum(column - cum_s[order, own, at], log_s[order, own, at])
                     tables.append((scores * jnp.exp2(gap)).astype(BF16))
                 xp = xb[:, q * 2 * P_SIZE : (q + 1) * 2 * P_SIZE]
                 stacked = jnp.concatenate([jnp.where(first, xp, zero), jnp.where(first, zero, xp)], 0)
@@ -449,8 +477,8 @@
             gate = half_silu(z[at, lanes].astype(F32) * 0.5)
             uv_out[at, lanes] = (y * gate).astype(BF16)
             uv_out[at, width + s * SLAB : width + (s + 1) * SLAB] = (gate * rise * lead_row).astype(BF16)
-            xf = (xs * dot(f_blk[at, :], sel)).astype(BF16)
-            state[:, lanes] = old * fade_row + dot(b_mat, xf, ((0,), (0,)))
+            xf = (xs * dot(f_blk[order, at, :], sel)).astype(BF16)
+            state[:, lanes] = old * fade_row + dot(b_across, xf)
 
     lax.fori_loop(0, length // STEP_B, turn, 0)
 
@@ -475,18 +503,15 @@
     )(info, x, z, bc, cum, cum_s, log_s, f_blk, e_blk, by_row, ones, token)
 
 
-def norm_kernel(row, ahead, info, bc0, bc1, state0, state1, gain, *refs):
-    uvs, out = refs[:-1][-2 * B_PARTS :], refs[-1]
-    skipped = out.shape[0] - ROWS_C * (out.shape[0] // ROWS_C // (2 if ahead else 1))
-    count = out.shape[0] - skipped
+def norm_kernel(places, info, bc0, bc1, state0, state1, gain, _, *refs):
+    uvs, out = refs[:-1], refs[-1]
+    count = out.shape[0] // len(places)
     per = state0.shape[1]
     part = per // B_PARTS
-    if ahead:
-        out[0:skipped, :] = refs[0][...]
-
-    def step(j, _):
-        to = pl.ds(pl.multiple_of(skipped + j * ROWS_C, ROWS_C), ROWS_C)
-        at = pl.ds(pl.multiple_of(info[ROWS + row] * count + j * ROWS_C, ROWS_C), ROWS_C)
+
+    def rows(first, base):
+        to = pl.ds(pl.multiple_of(first, ROWS_C), ROWS_C)
+        at = pl.ds(pl.multiple_of(base, ROWS_C), ROWS_C)
         for order, (bc, state) in enumerate(((bc0, state0), (bc1, state1))):
             c_mat = bc[at, N : 2 * N]
             pieces = []
@@ -502,23 +527,26 @@
             for p, gated in enumerate(pieces):
                 lanes = pl.ds(pl.multiple_of(info[GROUP + order] * per + p * part, part), part)
                 out[to, lanes] = (gated * scale * gain[:, lanes]).astype(BF16)
-        return 0
-
-    lax.fori_loop(0, count // ROWS_C, step, 0)
-
-
-def norm_rows(row, info, count, tokens, bcs, states, gain, uvs, ahead=None):
-    first = [] if ahead is None else [ahead]
-    rows = count if ahead is None else 2 * count
+
+    for k, place in enumerate(places):
+
+        def step(j, _):
+            rows(k * count + j * ROWS_C, info[ROWS + place] * count + j * ROWS_C)
+            return 0
+
+        lax.fori_loop(0, count // ROWS_C, step, 0)
+
+
+def norm_rows(places, info, count, token, bcs, states, gain, uvs):
     return pl.pallas_call(
-        functools.partial(norm_kernel, row, ahead is not None),
-        in_specs=[SCALAR] + [FULL] * (5 + len(first)) + [ANY] * len(tokens) + [FULL] * len(uvs),
+        functools.partial(norm_kernel, places),
+        in_specs=[SCALAR] + [FULL] * 5 + [ANY] + [FULL] * len(uvs),
         out_specs=FULL,
-        out_shape=jax.ShapeDtypeStruct((rows, gain.shape[1]), BF16),
+        out_shape=jax.ShapeDtypeStruct((len(places) * count, gain.shape[1]), BF16),
         compiler_params=params(16),
         cost_estimate=CHEAP,
         name="norm_rows",
-    )(info, *bcs, *states, gain, *first, *tokens, *uvs)
+    )(info, *bcs, *states, gain, token, *uvs)
 
 
 def stream(base, w0_far, w1_far, w0, w1, sem):
@@ -558,13 +586,14 @@
     ]
 
 
-def ahead_kernel(base, own, mate, w0_far, w1_far, out, w0, w1, sem):
+def ahead_kernel(base, owns, mates, w0_far, w1_far, out, w0, w1, sem):
     slot = stream(base, w0_far, w1_far, w0, w1, sem)
-    out[...] = (dot(own[...], w0[slot]) + dot(mate[...], w1[slot])).astype(BF16)
-
-
-def project_ahead(own, mate, w0, w1, first, count):
-    rows, depth = own.shape
+    rows = out.shape[0]
+    out[...] = (dot(owns[0:rows, :], w0[slot]) + dot(mates[0:rows, :], w1[slot])).astype(BF16)
+
+
+def project_ahead(owns, mates, w0, w1, first, count):
+    rows, depth = owns.shape[0] // 2, owns.shape[1]
     return pl.pallas_call(
         functools.partial(ahead_kernel, first // TILE),
         grid=(count // TILE,),
@@ -575,86 +604,89 @@
         compiler_params=params(20),
         cost_estimate=CHEAP,
         name="project_ahead",
-    )(own, mate, w0, w1)
-
-
-def both_kernel(base, owns, mate0, mate1, w0_far, w1_far, far, near, mates, w0, w1, sem):
-    rows = far.shape[0]
-
-    @pl.when(pl.program_id(0) == 0)
-    def _():
-        mates[0:rows, :] = mate0[...]
-        mates[rows:, :] = mate1[...]
-
+    )(owns, mates, w0, w1)
+
+
+def both_kernel(base, cut, owns, mates, w0_far, w1_far, *refs):
+    fars, near, w0, w1, sem = refs[:-4], *refs[-4:]
+    rows = near.shape[0]
     slot = stream(base, w0_far, w1_far, w0, w1, sem)
     total = dot(owns[...], w0[slot]) + dot(mates[...], w1[slot])
-    far[...] = total[0:rows].astype(BF16)
     near[...] = total[rows:]
-
-
-def project_both(owns, mate0, mate1, w0, w1, first, count):
-    rows, depth = mate0.shape
+    for k, far_out in enumerate(fars):
+
+        @pl.when(pl.program_id(0) // cut == k)
+        def _():
+            far_out[...] = total[0:rows].astype(BF16)
+
+
+def project_both(owns, mates, w0, w1, first, count, chunk):
+    rows, depth = owns.shape[0] // 2, owns.shape[1]
+    cut = chunk // TILE
+    chunks = count // chunk
+
+    def placed(k):
+        return pl.BlockSpec((rows, TILE), lambda j: (0, jnp.clip(j - k * cut, 0, cut - 1)))
+
+    *fars, near = pl.pallas_call(
+        functools.partial(both_kernel, first // TILE, cut),
+        grid=(count // TILE,),
+        in_specs=[FULL] * 2 + [FAR] * 2,
+        out_specs=[placed(k) for k in range(chunks)] + [pl.BlockSpec((rows, TILE), lambda j: (0, j))],
+        out_shape=[jax.ShapeDtypeStruct((rows, chunk), BF16)] * chunks + [jax.ShapeDtypeStruct((rows, count), F32)],
+        scratch_shapes=buffers(depth),
+        compiler_params=params(24),
+        cost_estimate=CHEAP,
+        name="project_both",
+    )(owns, mates, w0, w1)
+    return fars, near
+
+
+def near_kernel(owns, mates, w0_far, w1_far, arrived, out, w0, w1, sem):
+    slot = stream(0, w0_far, w1_far, w0, w1, sem)
+    rows = out.shape[0]
+    total = dot(owns[rows:, :], w0[slot]) + dot(mates[rows:, :], w1[slot])
+    out[...] = (total + arrived[...].astype(F32)).astype(BF16)
+
+
+def project_near(owns, mates, w0, w1, arrived):
+    rows, depth = owns.shape[0] // 2, owns.shape[1]
     placed = pl.BlockSpec((rows, TILE), lambda j: (0, j))
     return pl.pallas_call(
-        functools.partial(both_kernel, first // TILE),
-        grid=(count // TILE,),
-        in_specs=[FULL] * 3 + [FAR] * 2,
-        out_specs=[placed, placed],
-        out_shape=[jax.ShapeDtypeStruct((rows, count), BF16), jax.ShapeDtypeStruct((rows, count), F32)],
-        scratch_shapes=[pltpu.VMEM((2 * rows, depth), BF16)] + buffers(depth),
-        compiler_params=params(24),
-        cost_estimate=CHEAP,
-        name="project_both",
-    )(owns, mate0, mate1, w0, w1)
-
-
-def near_kernel(split, owns, mate, w0_far, w1_far, arrived0, arrived1, out, w0, w1, sem):
-    slot = stream(0, w0_far, w1_far, w0, w1, sem)
-    rows = mate.shape[0]
-    total = dot(owns[rows:, :], w0[slot]) + dot(mate[...], w1[slot])
-    arrived = jnp.where(pl.program_id(0) < split, arrived0[...], arrived1[...])
-    out[...] = (total + arrived.astype(F32)).astype(BF16)
-
-
-def project_near(owns, mate, w0, w1, arrived0, arrived1):
-    rows, depth = mate.shape
-    split = arrived0.shape[1] // TILE
-    tiles = split + arrived1.shape[1] // TILE
-    return pl.pallas_call(
-        functools.partial(near_kernel, split),
-        grid=(tiles,),
-        in_specs=[FULL, FULL, FAR, FAR]
-        + [
-            pl.BlockSpec((rows, TILE), lambda j: (0, jnp.minimum(j, split - 1))),
-            pl.BlockSpec((rows, TILE), lambda j: (0, jnp.maximum(j - split, 0))),
-        ],
-        out_specs=pl.BlockSpec((rows, TILE), lambda j: (0, j)),
+        near_kernel,
+        grid=(arrived.shape[1] // TILE,),
+        in_specs=[FULL, FULL, FAR, FAR, placed],
+        out_specs=placed,
         out_shape=jax.ShapeDtypeStruct((rows, w0.shape[1]), BF16),
         scratch_shapes=buffers(depth),
         compiler_params=params(20),
         cost_estimate=CHEAP,
         name="project_near",
-    )(owns, mate, w0, w1, arrived0, arrived1)
-
-
-def add_kernel(part, arrived, _, out):
-    out[...] = (part[...] + arrived[...].astype(F32)).astype(BF16)
-
-
-def add_chunk(part, arrived, result, first):
-    rows, count = arrived.shape
-    base = first // TILE
+    )(owns, mates, w0, w1, arrived)
+
+
+def add_kernel(near, *refs):
+    arrived, out = refs[:-2], refs[-1]
+    chunk = arrived[0].shape[1]
+    for k, part in enumerate(arrived):
+        lanes = slice(k * chunk, (k + 1) * chunk)
+        out[:, lanes] = (near[:, lanes] + part[...].astype(F32)).astype(BF16)
+
+
+def add_chunks(near, first, arrived, result, at):
+    rows, chunk = arrived[0].shape
+    count = chunk * len(arrived)
     return pl.pallas_call(
         add_kernel,
-        grid=(count // TILE,),
-        in_specs=[pl.BlockSpec((rows, TILE), lambda j: (0, j))] * 2 + [ANY],
-        out_specs=pl.BlockSpec((rows, TILE), lambda j: (0, base + j)),
+        grid=(1,),
+        in_specs=[pl.BlockSpec((rows, count), lambda j: (0, first // count))] + [FULL] * len(arrived) + [ANY],
+        out_specs=pl.BlockSpec((rows, count), lambda j: (0, at // count)),
         out_shape=jax.ShapeDtypeStruct(result.shape, BF16),
-        input_output_aliases={2: 0},
+        input_output_aliases={1 + len(arrived): 0},
         compiler_params=params(8),
         cost_estimate=CHEAP,
-        name="add_chunk",
-    )(part, arrived, result)
+        name="add_chunks",
+    )(near, *arrived, result)
 
 
 def shift(block, distance):
@@ -737,9 +769,9 @@
     bc = bc_input.reshape(length, -1)
     weight_mate = swap(out_weight, "head", 1)
 
-    ones = jnp.asarray(np.tile(np.repeat(np.eye(heads), P_SIZE, axis=1), (2, 1)), BF16)
-    cum, cum_s, log_s, f_dev, f_blk, e_blk, rates, by_row = decays(2, log_decay, step_size, skip_gain, ones)
-    shared = (info, x_far, bc, halo, conv_weight_x, conv_weight_bc, f_dev, ones, rates)
+    cum, cum_s, log_s, f_dev, f_blk, e_blk, rates, by_row, ones = decays(info, log_decay, step_size, skip_gain, half)
+    taps = far(conv_weight_x, conv_weight_bc)
+    shared = (info, x_far, bc, halo, *taps, f_dev, ones, rates)
     x0, bc0, send = conv_states(0, *shared)
     got = swap(send, "seq", 1)
     x1, bc1, keep = conv_states(1, *shared)
@@ -798,29 +830,25 @@
     count = length // ways
     gain = norm_gain[None, :]
 
-    def rows_for(row, *tokens, ahead=None):
-        return norm_rows(row, info, count, tokens, (bc0, bc1), (other, held), gain, uvs, ahead)
-
-    weights = (w_far, weight_mate)
-    cuts = [out_weight.shape[1] * c // 16 for c in (0, 2, 6, 10, 14, 16)]
-    far_mate = rows_for(0)
-    far_own = rows_for(1, far_mate)
-    far_mate = swap(far_mate, "head", 1)
-    arrivals = []
-    for lo, hi in zip(cuts[0:2], cuts[1:3]):
-        sent = project_ahead(far_own, far_mate, *weights, lo, hi - lo)
-        arrivals.append(swap(sent, "head", 2))
-    near_mate = rows_for(2, sent)
-    owns = rows_for(3, near_mate, arrivals[0], ahead=far_own)
-    near_mate = swap(near_mate, "head", 1)
-    parts = []
-    for lo, hi in zip(cuts[2:-1], cuts[3:]):
-        sent, part = project_both(owns, far_mate, near_mate, *weights, lo, hi - lo)
-        arrivals.append(swap(sent, "head", 2))
-        parts.append(part)
-    result = project_near(owns, near_mate, *weights, *arrivals[:2])
-    for part, arrived, lo in zip(parts, arrivals[2:], cuts[2:]):
-        result = add_chunk(part, arrived, result, lo)
+    def rows_for(token, *places):
+        return norm_rows(places, info, count, token, (bc0, bc1), (other, held), gain, uvs)
+
+    mates = rows_for(held, 0, 2)
+    owns = rows_for(mates, 1, 3)
+    operands = (owns, swap(mates, "head", 1), w_far, weight_mate)
+    columns = out_weight.shape[1]
+    chunk = columns // 8
+    first = swap(project_ahead(*operands, 0, chunk), "head", 2)
+    calls = []
+    for lo, hi in ((1, 2), (2, 4), (4, 6), (6, 8)):
+        sent, near = project_both(*operands, lo * chunk, (hi - lo) * chunk, chunk)
+        calls.append((near, lo, [swap(part, "head", 2) for part in sent]))
+    result = project_near(*operands, first)
+    for near, lo, arrived in calls[:-1]:
+        result = add_chunks(near, 0, arrived, result, lo * chunk)
+    near, lo, arrived = calls[-1]
+    for k, part in enumerate(arrived):
+        result = add_chunks(near, k * chunk, [part], result, (lo + k) * chunk)
     return result
 
 

time: 127 us -> 120 us (0.945)
  local copies, waits for them, and re-layouts: 5.23 us -> 0.33 us
  Pallas kernels: 85.3 us -> 82.6 us
  starting transfers between devices: 19.3 us -> 20.8 us
    unnamed x23 -> x5, local copies, waits for them, and re-layouts: 5.14 us -> 0.24 us
    pallas_call x2 -> x1, Pallas kernels: 7.68 us -> 3.09 us  [project_ahead(): pl.pallas_call(functools.partial(ahead_kernel, first // TILE), grid=(coun...]
    pallas_call x12 -> x13, Pallas kernels: 36.3 us -> 40.7 us  [the longest x4 25.2 us: project_both(): pl.pallas_call(functools.partial(both_kernel, first // TILE, cut), grid=(...]
    pallas_call x2, Pallas kernels: 15.9 us -> 13.9 us  [conv_states(): pl.pallas_call(functools.partial(conv_kernel, order), grid_spec=pltpu.Pre...]
    ppermute x10 -> x12, waiting for transfers between devices: 14.6 us -> 12.7 us  [swap(): lax.ppermute(block, axis, [(i, i ^ bit) for i in range(lax.axis_size(axis...]
    ppermute x10 -> x12, starting transfers between devices: 7.83 us -> 9.3 us  [swap(): lax.ppermute(block, axis, [(i, i ^ bit) for i in range(lax.axis_size(axis...]
  transfers between devices with their start and end apart: 17 -> 19, of which waited for: 6 -> 7; matrix products, arithmetic and copies ran while one was open for 0% -> 0% of each run, Pallas kernels for 62% -> 66%
where the time goes in v10:
time: 120 us
  Pallas kernels  82.6 us (69%)
  starting transfers between devices  20.8 us (17%)
  waiting for transfers between devices  15.7 us (13%)
    pallas_call x4, Pallas kernels, project_both(): pl.pallas_call(functools.partial(both_kernel, first // TILE, cut), grid=(...  25.2 us
    pallas_call x4, Pallas kernels, scan_part(): pl.pallas_call(functools.partial(scan_kernel, order, part), in_specs=[SCA...  21.8 us
    pallas_call x2, Pallas kernels, conv_states(): pl.pallas_call(functools.partial(conv_kernel, order), grid_spec=pltpu.Pre...  13.9 us
    ppermute x12, waiting for transfers between devices, swap(): lax.ppermute(block, axis, [(i, i ^ bit) for i in range(lax.axis_size(axis...  12.7 us
    ppermute x7, starting transfers between devices, rotate(): lax.ppermute(block, 'seq', [(i, (i + distance) % size) for i in range(siz...  11.5 us
    ppermute x12, starting transfers between devices, swap(): lax.ppermute(block, axis, [(i, i ^ bit) for i in range(lax.axis_size(axis...  9.3 us
    pallas_call x2, Pallas kernels, norm_rows(): pl.pallas_call(functools.partial(norm_kernel, places), in_specs=[SCALAR]...  5.02 us
    pallas_call x5, Pallas kernels, add_chunks(): pl.pallas_call(add_kernel, grid=(1,), in_specs=[pl.BlockSpec((rows, count...  4.01 us
  transfers between devices with their start and end apart: 19, of which 7 were waited for; matrix products, arithmetic and copies ran while one was open for 0% of the time, Pallas kernels for 66%

profile of v10, /device:TPU:0, one launch (start us, length us, event | category | flops | bytes accessed | tf_op | source)
XLA Modules:
  0.0 119.8 jit_solution(10390681690310488809)
XLA Ops:
  1.3 2.7 %collective-permute-start = (bf16[16,2560]{1,0:T(8,128)(2,1)S(1)}, bf16[16,2560]{1,0:T(8,128)(2,1)S(1)}, u32[]{:S(2)}, u32[]{:S(2)}) collective-permute-start(bf16[16,2560]{1,0:T(8,128)(2,1)S(1)} %tail_rows.1), channel_id=1, source_target_pairs={{0,4},{4,8},{8,12},{12,16},{16,20},{20,24},{24,28},{28,0},{1,5},{5... | collective-permute-start | bytes 245768 | tf_op jit(solution)/shard_map/ppermute | solution.py:703
  4.1 2.7 %decays.1 = (f32[2,1024,16]{2,1,0:T(8,128)S(1)}, f32[2,16,1024]{2,1,0:T(8,128)S(1)}, f32[2,16,1024]{2,1,0:T(8,128)S(1)}, bf16[2,1024,32]{2,1,0:T(8,128)(2,1)S(1)...) custom-call(s32[9]{0:T(128)S(1)} %stack.36.info, ...), custom_call_target="tpu_custom_call" | custom-call | flops 1 | bytes 1 | tf_op jit(solution)/shard_map/decays/pallas_call | solution.py:145
  7.0 3.0 %collective-permute-done.halo.bc_halo = bf16[16,2560]{1,0:T(8,128)(2,1)S(1)} collective-permute-done((bf16[16,2560]{1,0:T(8,128)(2,1)S(1)}, bf16[16,2560]{1,0:T(8,128)(2,1)S(1)}, u32[]{:S(2)}, u32[]{:S(2)}) %collective-permute-start) | collective-permute-done | bytes 81952 | tf_op jit(solution)/shard_map/ppermute | solution.py:703
  10.1 7.0 %conv_states.2 = (bf16[1024,1024]{1,0:T(8,128)(2,1)}, bf16[1024,256]{1,0:T(8,128)(2,1)S(1)}, bf16[144,1024]{1,0:T(8,128)(2,1)S(1)}) custom-call(s32[9]{0:T(128)S(1)} %stack.36.info, bf16[1024,2048]{1,0:T(8,128)(2,1)} %x_lead.3, bf16[1024,2048]{1,0:T(8,128)(2,1)} %x_lead.3, bf16[1024,512]{1,0:T(8,128)(2,1)S(1)} %bitcast.14, bf16[1024,512]{1,0:T(8,128)(2,1)S(1)} %bitcast.15, ...), custom_call_target="tpu_custom_call" | custom-call | flops 1 | bytes 1 | tf_op jit(solution)/shard_map/conv_states/pallas_call | solution.py:267
  17.0 6.9 %conv_states.3 = (bf16[1024,1024]{1,0:T(8,128)(2,1)}, bf16[1024,256]{1,0:T(8,128)(2,1)S(1)}, f32[128,1024]{1,0:T(8,128)S(1)}) custom-call(s32[9]{0:T(128)S(1)} %stack.36.info, bf16[1024,2048]{1,0:T(8,128)(2,1)} %x_lead.3, bf16[1024,2048]{1,0:T(8,128)(2,1)} %x_lead.3, bf16[1024,512]{1,0:T(8,128)(2,1)S(1)} %bitcast.16, bf16[1024,512]{1,0:T(8,128)(2,1)S(1)} %bitcast.17, ...), custom_call_target="tpu_custom_call" | custom-call | flops 1 | bytes 1 | tf_op jit(solution)/shard_map/conv_states/pallas_call | solution.py:267
  24.0 1.8 %collective-permute-done.1.got = bf16[144,1024]{1,0:T(8,128)(2,1)S(1)} collective-permute-done((bf16[144,1024]{1,0:T(8,128)(2,1)S(1)}, bf16[144,1024]{1,0:T(8,128)(2,1)S(1)}, u32[]{:S(2)}, u32[]{:S(2)}) %collective-permute-start.1) | collective-permute-done | bytes 294944 | tf_op jit(solution)/shard_map/ppermute | solution.py:698
  26.7 2.0 %collective-permute-start.3 = (bf16[144,256]{1,0:T(8,128)(2,1)S(1)}, bf16[144,256]{1,0:T(8,128)(2,1)S(1)}, u32[]{:S(2)}, u32[]{:S(2)}) collective-permute-start(bf16[144,256]{1,0:T(8,128)(2,1)S(1)} %get-tuple-element.61), channel_id=1, source_target_pairs={{0,16},{4,20},{8,24},{12,28},{16,0},{20,4},{24,8},{28,12},{1,17},{... | collective-permute-start | bytes 221192 | tf_op jit(solution)/shard_map/ppermute | solution.py:703
  28.8 1.8 %collective-permute-start.4 = (bf16[144,256]{1,0:T(8,128)(2,1)S(1)}, bf16[144,256]{1,0:T(8,128)(2,1)S(1)}, u32[]{:S(2)}, u32[]{:S(2)}) collective-permute-start(bf16[144,256]{1,0:T(8,128)(2,1)S(1)} %get-tuple-element.62), channel_id=1, source_target_pairs={{0,24},{4,28},{8,0},{12,4},{16,8},{20,12},{24,16},{28,20},{1,25},{... | collective-permute-start | bytes 221192 | tf_op jit(solution)/shard_map/ppermute | solution.py:703
  30.5 5.4 %scan_part.4._.refs_0_ = bf16[1024,1024]{1,0:T(8,128)(2,1)S(1)} custom-call(s32[9]{0:T(128)S(1)} %stack.36.info, bf16[1024,1024]{1,0:T(8,128)(2,1)} %get-tuple-element.63.x_far, bf16[1024,2048]{1,0:T(8,128)(2,1)} %z_far.7, bf16[1024,256]{1,0:T(8,128)(2,1)S(1)} %get-tuple-element.46.bc.bc0, f32[2,1024,16]{2,1,0:T(8,128)S(1)} %get-tuple-element.53.cum, ...), custom_call_target="tpu_custom_call" | custom-call | flops 1 | bytes 1 | tf_op jit(solution)/shard_map/scan_part/pallas_call | solution.py:489
  36.0 5.4 %scan_part.5.refs_4_.refs_1_ = bf16[1024,1024]{1,0:T(8,128)(2,1)S(1)} custom-call(s32[9]{0:T(128)S(1)} %stack.36.info, bf16[1024,1024]{1,0:T(8,128)(2,1)} %get-tuple-element.63.x_far, bf16[1024,2048]{1,0:T(8,128)(2,1)} %z_far.7, bf16[1024,256]{1,0:T(8,128)(2,1)S(1)} %get-tuple-element.46.bc.bc0, f32[2,1024,16]{2,1,0:T(8,128)S(1)} %get-tuple-element.53.cum, ...), custom_call_target="tpu_custom_call" | custom-call | flops 1 | bytes 1 | tf_op jit(solution)/shard_map/scan_part/pallas_call | solution.py:489
  44.2 2.8 %collective-permute-start.7 = (bf16[128,256]{1,0:T(8,128)(2,1)S(1)}, bf16[128,256]{1,0:T(8,128)(2,1)S(1)}, u32[]{:S(2)}, u32[]{:S(2)}) collective-permute-start(bf16[128,256]{1,0:T(8,128)(2,1)S(1)} %get-tuple-element.67), channel_id=1, source_target_pairs={{0,24},{4,28},{8,0},{12,4},{16,8},{20,12},{24,16},{28,20},{1,25},{... | collective-permute-start | bytes 196616 | tf_op jit(solution)/shard_map/ppermute | solution.py:703
  47.1 5.4 %scan_part.6._.refs_2_ = bf16[1024,1024]{1,0:T(8,128)(2,1)S(1)} custom-call(s32[9]{0:T(128)S(1)} %stack.36.info, bf16[1024,1024]{1,0:T(8,128)(2,1)} %get-tuple-element.52.x_far, bf16[1024,2048]{1,0:T(8,128)(2,1)} %z_far.7, bf16[1024,256]{1,0:T(8,128)(2,1)S(1)} %get-tuple-element.47.bc.bc1, f32[2,1024,16]{2,1,0:T(8,128)S(1)} %get-tuple-element.53.cum, ...), custom_call_target="tpu_custom_call" | custom-call | flops 1 | bytes 1 | tf_op jit(solution)/shard_map/scan_part/pallas_call | solution.py:489
  53.7 5.4 %scan_part.7.refs_3_ = bf16[1024,1024]{1,0:T(8,128)(2,1)S(1)} custom-call(s32[9]{0:T(128)S(1)} %stack.36.info, bf16[1024,1024]{1,0:T(8,128)(2,1)} %get-tuple-element.52.x_far, bf16[1024,2048]{1,0:T(8,128)(2,1)} %z_far.7, bf16[1024,256]{1,0:T(8,128)(2,1)S(1)} %get-tuple-element.47.bc.bc1, f32[2,1024,16]{2,1,0:T(8,128)S(1)} %get-tuple-element.53.cum, ...), custom_call_target="tpu_custom_call" | custom-call | flops 1 | bytes 1 | tf_op jit(solution)/shard_map/scan_part/pallas_call | solution.py:489
  59.8 2.5 %norm_rows.2._ = bf16[512,2048]{1,0:T(8,128)(2,1)S(1)} custom-call(s32[9]{0:T(128)S(1)} %stack.36.info, bf16[1024,256]{1,0:T(8,128)(2,1)S(1)} %get-tuple-element.46.bc.bc0, bf16[1024,256]{1,0:T(8,128)(2,1)S(1)} %get-tuple-element.47.bc.bc1, bf16[128,1024]{1,0:T(8,128)(2,1)S(1)} %collective-permute-done.8.state0, ...), custom_call_target="tpu_custom_call" | custom-call | flops 1 | bytes 1 | tf_op jit(solution)/shard_map/norm_rows/pallas_call | solution.py:541
  62.4 2.5 %norm_rows.3.owns = bf16[512,2048]{1,0:T(8,128)(2,1)S(1)} custom-call(s32[9]{0:T(128)S(1)} %stack.36.info, bf16[1024,256]{1,0:T(8,128)(2,1)S(1)} %get-tuple-element.46.bc.bc0, bf16[1024,256]{1,0:T(8,128)(2,1)S(1)} %get-tuple-element.47.bc.bc1, bf16[128,1024]{1,0:T(8,128)(2,1)S(1)} %collective-permute-done.8.state0, ...), custom_call_target="tpu_custom_call" | custom-call | flops 1 | bytes 1 | tf_op jit(solution)/shard_map/norm_rows/pallas_call | solution.py:541
  64.9 1.6 %collective-permute-done.9.mates = bf16[512,2048]{1,0:T(8,128)(2,1)S(1)} collective-permute-done((bf16[512,2048]{1,0:T(8,128)(2,1)S(1)}, bf16[512,2048]{1,0:T(8,128)(2,1)S(1)}, u32[]{:S(2)}, u32[]{:S(2)}) %collective-permute-start.9) | collective-permute-done | bytes 2097184 | tf_op jit(solution)/shard_map/ppermute | solution.py:698
  66.6 3.1 %project_ahead.1 = bf16[256,512]{1,0:T(8,128)(2,1)S(1)} custom-call(bf16[512,2048]{1,0:T(8,128)(2,1)S(1)} %norm_rows.3.owns, bf16[512,2048]{1,0:T(8,128)(2,1)S(1)} %collective-permute-done.9.mates, bf16[2048,4096]{1,0:T(8,128)(2,1)} %w0_far.11, bf16[2048,4096]{1,0:T(8,128)(2,1)} %collective-permute-done.10.w1_far), custom_call_target="tpu_custom_call" | custom-call | flops 1 | bytes 1 | tf_op jit(solution)/shard_map/project_ahead/pallas_call | solution.py:597
  71.1 4.3 %project_both.7 = (bf16[256,512]{1,0:T(8,128)(2,1)S(1)}, f32[256,512]{1,0:T(8,128)S(1)}) custom-call(bf16[512,2048]{1,0:T(8,128)(2,1)S(1)} %norm_rows.3.owns, bf16[512,2048]{1,0:T(8,128)(2,1)S(1)} %collective-permute-done.9.mates, bf16[2048,4096]{1,0:T(8,128)(2,1)} %w0_far.11, bf16[2048,4096]{1,0:T(8,128)(2,1)} %collective-permute-done.10.w1_far), custom_call_target="tpu_custom_call" | custom-call | flops 1 | bytes 1 | tf_op jit(solution)/shard_map/project_both/pallas_call | solution.py:631
  76.1 7.0 %project_both.6 = (bf16[256,512]{1,0:T(8,128)(2,1)S(1)}, bf16[256,512]{1,0:T(8,128)(2,1)S(1)}, f32[256,1024]{1,0:T(8,128)S(1)}) custom-call(bf16[512,2048]{1,0:T(8,128)(2,1)S(1)} %norm_rows.3.owns, bf16[512,2048]{1,0:T(8,128)(2,1)S(1)} %collective-permute-done.9.mates, bf16[2048,4096]{1,0:T(8,128)(2,1)} %w0_far.11, ...), custom_call_target="tpu_custom_call" | custom-call | flops 1 | bytes 1 | tf_op jit(solution)/shard_map/project_both/pallas_call | solution.py:631
  85.2 7.0 %project_both.5 = (bf16[256,512]{1,0:T(8,128)(2,1)S(1)}, bf16[256,512]{1,0:T(8,128)(2,1)S(1)}, f32[256,1024]{1,0:T(8,128)S(1)}) custom-call(bf16[512,2048]{1,0:T(8,128)(2,1)S(1)} %norm_rows.3.owns, bf16[512,2048]{1,0:T(8,128)(2,1)S(1)} %collective-permute-done.9.mates, bf16[2048,4096]{1,0:T(8,128)(2,1)} %w0_far.11, ...), custom_call_target="tpu_custom_call" | custom-call | flops 1 | bytes 1 | tf_op jit(solution)/shard_map/project_both/pallas_call | solution.py:631
  93.6 7.0 %project_both.4 = (bf16[256,512]{1,0:T(8,128)(2,1)S(1)}, bf16[256,512]{1,0:T(8,128)(2,1)S(1)}, f32[256,1024]{1,0:T(8,128)S(1)}) custom-call(bf16[512,2048]{1,0:T(8,128)(2,1)S(1)} %norm_rows.3.owns, bf16[512,2048]{1,0:T(8,128)(2,1)S(1)} %collective-permute-done.9.mates, bf16[2048,4096]{1,0:T(8,128)(2,1)} %w0_far.11, ...), custom_call_target="tpu_custom_call" | custom-call | flops 1 | bytes 1 | tf_op jit(solution)/shard_map/project_both/pallas_call | solution.py:631
  103.4 3.8 %project_near.1.refs_1_ = bf16[256,4096]{1,0:T(8,128)(2,1)} custom-call(bf16[512,2048]{1,0:T(8,128)(2,1)S(1)} %norm_rows.3.owns, bf16[512,2048]{1,0:T(8,128)(2,1)S(1)} %collective-permute-done.9.mates, bf16[2048,4096]{1,0:T(8,128)(2,1)} %w0_far.11, bf16[2048,4096]{1,0:T(8,128)(2,1)} %collective-permute-done.10.w1_far, ...), custom_call_target="tpu_custom_call" | custom-call | flops 1 | bytes 1 | tf_op jit(solution)/shard_map/project_near/pallas_call | solution.py:655
  110.8 4.7 %collective-permute-done.12.refs_0_ = bf16[256,512]{1,0:T(8,128)(2,1)S(1)} collective-permute-done((bf16[256,512]{1,0:T(8,128)(2,1)S(1)}, bf16[256,512]{1,0:T(8,128)(2,1)S(1)}, u32[]{:S(2)}, u32[]{:S(2)}) %collective-permute-start.12) | collective-permute-done | bytes 262176 | tf_op jit(solution)/shard_map/ppermute | solution.py:698
  116.3 2.7 %collective-permute-done.11.refs_0_ = bf16[256,512]{1,0:T(8,128)(2,1)S(1)} collective-permute-done((bf16[256,512]{1,0:T(8,128)(2,1)S(1)}, bf16[256,512]{1,0:T(8,128)(2,1)S(1)}, u32[]{:S(2)}, u32[]{:S(2)}) %collective-permute-start.11) | collective-permute-done | bytes 262176 | tf_op jit(solution)/shard_map/ppermute | solution.py:698
  (44 shorter events, 20.9 us)
Async XLA Ops:
  0.0 6.8 %copy-start.1 = (bf16[1024,2,256]{2,1,0:T(2,128)(2,1)S(1)}, bf16[1024,2,256]{2,1,0:T(2,128)(2,1)}, u32[]{:S(2)}) copy-start(bf16[1024,2,256]{2,1,0:T(2,128)(2,1)} %bc.1) | copy-start | bytes 3145732
  0.0 66.6 %collective-permute-start.10 = (bf16[2048,4096]{1,0:T(8,128)(2,1)}, bf16[2048,4096]{1,0:T(8,128)(2,1)}, u32[]{:S(2)}, u32[]{:S(2)}) collective-permute-start(bf16[2048,4096]{1,0:T(8,128)(2,1)} %w0_far.11), channel_id=1, source_target_pairs={{0,1},{1,0},{2,3},{3,2},{4,5},{5,4},{6,7},{7,6},{8,9},{9,8},{10,11... | collective-permute-start | bytes 50331656 | tf_op jit(solution)/shard_map/ppermute | solution.py:698
  1.3 8.7 %collective-permute-start = (bf16[16,2560]{1,0:T(8,128)(2,1)S(1)}, bf16[16,2560]{1,0:T(8,128)(2,1)S(1)}, u32[]{:S(2)}, u32[]{:S(2)}) collective-permute-start(bf16[16,2560]{1,0:T(8,128)(2,1)S(1)} %tail_rows.1), channel_id=1, source_target_pairs={{0,4},{4,8},{8,12},{12,16},{16,20},{20,24},{24,28},{28,0},{1,5},{5... | collective-permute-start | bytes 245768 | tf_op jit(solution)/shard_map/ppermute | solution.py:703
  17.0 8.8 %collective-permute-start.1 = (bf16[144,1024]{1,0:T(8,128)(2,1)S(1)}, bf16[144,1024]{1,0:T(8,128)(2,1)S(1)}, u32[]{:S(2)}, u32[]{:S(2)}) collective-permute-start(bf16[144,1024]{1,0:T(8,128)(2,1)S(1)} %get-tuple-element.48), channel_id=1, source_target_pairs={{0,4},{4,0},{8,12},{12,8},{16,20},{20,16},{24,28},{28,24},{1,5},{5... | collective-permute-start | bytes 884744 | tf_op jit(solution)/shard_map/ppermute | solution.py:698
  26.6 14.8 %collective-permute-start.2 = (bf16[144,256]{1,0:T(8,128)(2,1)S(1)}, bf16[144,256]{1,0:T(8,128)(2,1)S(1)}, u32[]{:S(2)}, u32[]{:S(2)}) collective-permute-start(bf16[144,256]{1,0:T(8,128)(2,1)S(1)} %get-tuple-element.60), channel_id=1, source_target_pairs={{0,8},{4,12},{8,16},{12,20},{16,24},{20,28},{24,0},{28,4},{1,9},{5... | collective-permute-start | bytes 221192 | tf_op jit(solution)/shard_map/ppermute | solution.py:703
  26.7 14.7 %collective-permute-start.3 = (bf16[144,256]{1,0:T(8,128)(2,1)S(1)}, bf16[144,256]{1,0:T(8,128)(2,1)S(1)}, u32[]{:S(2)}, u32[]{:S(2)}) collective-permute-start(bf16[144,256]{1,0:T(8,128)(2,1)S(1)} %get-tuple-element.61), channel_id=1, source_target_pairs={{0,16},{4,20},{8,24},{12,28},{16,0},{20,4},{24,8},{28,12},{1,17},{... | collective-permute-start | bytes 221192 | tf_op jit(solution)/shard_map/ppermute | solution.py:703
  28.8 12.7 %collective-permute-start.4 = (bf16[144,256]{1,0:T(8,128)(2,1)S(1)}, bf16[144,256]{1,0:T(8,128)(2,1)S(1)}, u32[]{:S(2)}, u32[]{:S(2)}) collective-permute-start(bf16[144,256]{1,0:T(8,128)(2,1)S(1)} %get-tuple-element.62), channel_id=1, source_target_pairs={{0,24},{4,28},{8,0},{12,4},{16,8},{20,12},{24,16},{28,20},{1,25},{... | collective-permute-start | bytes 221192 | tf_op jit(solution)/shard_map/ppermute | solution.py:703
  42.1 10.5 %collective-permute-start.5 = (bf16[128,256]{1,0:T(8,128)(2,1)S(1)}, bf16[128,256]{1,0:T(8,128)(2,1)S(1)}, u32[]{:S(2)}, u32[]{:S(2)}) collective-permute-start(bf16[128,256]{1,0:T(8,128)(2,1)S(1)} %get-tuple-element.65), channel_id=1, source_target_pairs={{0,8},{4,12},{8,16},{12,20},{16,24},{20,28},{24,0},{28,4},{1,9},{5... | collective-permute-start | bytes 196616 | tf_op jit(solution)/shard_map/ppermute | solution.py:703
  42.7 9.8 %collective-permute-start.6 = (bf16[128,256]{1,0:T(8,128)(2,1)S(1)}, bf16[128,256]{1,0:T(8,128)(2,1)S(1)}, u32[]{:S(2)}, u32[]{:S(2)}) collective-permute-start(bf16[128,256]{1,0:T(8,128)(2,1)S(1)} %get-tuple-element.66), channel_id=1, source_target_pairs={{0,16},{4,20},{8,24},{12,28},{16,0},{20,4},{24,8},{28,12},{1,17},{... | collective-permute-start | bytes 196616 | tf_op jit(solution)/shard_map/ppermute | solution.py:703
  44.2 8.3 %collective-permute-start.7 = (bf16[128,256]{1,0:T(8,128)(2,1)S(1)}, bf16[128,256]{1,0:T(8,128)(2,1)S(1)}, u32[]{:S(2)}, u32[]{:S(2)}) collective-permute-start(bf16[128,256]{1,0:T(8,128)(2,1)S(1)} %get-tuple-element.67), channel_id=1, source_target_pairs={{0,24},{4,28},{8,0},{12,4},{16,8},{20,12},{24,16},{28,20},{1,25},{... | collective-permute-start | bytes 196616 | tf_op jit(solution)/shard_map/ppermute | solution.py:703
  53.4 6.5 %copy-start = (f32[2048]{0:T(1024)S(1)}, f32[2048]{0:T(1024)}, u32[]{:S(2)}) copy-start(f32[2048]{0:T(1024)} %param.18) | copy-start | bytes 24580
  53.4 6.4 %collective-permute-start.8 = (bf16[128,1024]{1,0:T(8,128)(2,1)S(1)}, bf16[128,1024]{1,0:T(8,128)(2,1)S(1)}, u32[]{:S(2)}, u32[]{:S(2)}) collective-permute-start(bf16[128,1024]{1,0:T(8,128)(2,1)S(1)} %get-tuple-element.68._), channel_id=1, source_target_pairs={{0,4},{4,0},{8,12},{12,8},{16,20},{20,16},{24,28},{28,24},{1,5},{5... | collective-permute-start | bytes 786440 | tf_op jit(solution)/shard_map/ppermute | solution.py:698
  62.3 4.2 %collective-permute-start.9 = (bf16[512,2048]{1,0:T(8,128)(2,1)S(1)}, bf16[512,2048]{1,0:T(8,128)(2,1)S(1)}, u32[]{:S(2)}, u32[]{:S(2)}) collective-permute-start(bf16[512,2048]{1,0:T(8,128)(2,1)S(1)} %norm_rows.2._), channel_id=1, source_target_pairs={{0,1},{1,0},{2,3},{3,2},{4,5},{5,4},{6,7},{7,6},{8,9},{9,8},{10,11... | collective-permute-start | bytes 6291464 | tf_op jit(solution)/shard_map/ppermute | solution.py:698
  69.7 31.0 %collective-permute-start.18 = (bf16[256,512]{1,0:T(8,128)(2,1)S(1)}, bf16[256,512]{1,0:T(8,128)(2,1)S(1)}, u32[]{:S(2)}, u32[]{:S(2)}) collective-permute-start(bf16[256,512]{1,0:T(8,128)(2,1)S(1)} %project_ahead.1), channel_id=1, source_target_pairs={{0,2},{1,3},{2,0},{3,1},{4,6},{5,7},{6,4},{7,5},{8,10},{9,11},{10,... | collective-permute-start | bytes 786440 | tf_op jit(solution)/shard_map/ppermute | solution.py:698
  75.4 25.9 %collective-permute-start.17 = (bf16[256,512]{1,0:T(8,128)(2,1)S(1)}, bf16[256,512]{1,0:T(8,128)(2,1)S(1)}, u32[]{:S(2)}, u32[]{:S(2)}) collective-permute-start(bf16[256,512]{1,0:T(8,128)(2,1)S(1)} %get-tuple-element.80), channel_id=1, source_target_pairs={{0,2},{1,3},{2,0},{3,1},{4,6},{5,7},{6,4},{7,5},{8,10},{9,11},{10,... | collective-permute-start | bytes 786440 | tf_op jit(solution)/shard_map/ppermute | solution.py:698
  83.1 19.7 %collective-permute-start.15 = (bf16[256,512]{1,0:T(8,128)(2,1)S(1)}, bf16[256,512]{1,0:T(8,128)(2,1)S(1)}, u32[]{:S(2)}, u32[]{:S(2)}) collective-permute-start(bf16[256,512]{1,0:T(8,128)(2,1)S(1)} %get-tuple-element.77), channel_id=1, source_target_pairs={{0,2},{1,3},{2,0},{3,1},{4,6},{5,7},{6,4},{7,5},{8,10},{9,11},{10,... | collective-permute-start | bytes 786440 | tf_op jit(solution)/shard_map/ppermute | solution.py:698
  84.6 23.4 %collective-permute-start.16 = (bf16[256,512]{1,0:T(8,128)(2,1)S(1)}, bf16[256,512]{1,0:T(8,128)(2,1)S(1)}, u32[]{:S(2)}, u32[]{:S(2)}) collective-permute-start(bf16[256,512]{1,0:T(8,128)(2,1)S(1)} %get-tuple-element.78), channel_id=1, source_target_pairs={{0,2},{1,3},{2,0},{3,1},{4,6},{5,7},{6,4},{7,5},{8,10},{9,11},{10,... | collective-permute-start | bytes 786440 | tf_op jit(solution)/shard_map/ppermute | solution.py:698
  92.2 16.6 %collective-permute-start.13 = (bf16[256,512]{1,0:T(8,128)(2,1)S(1)}, bf16[256,512]{1,0:T(8,128)(2,1)S(1)}, u32[]{:S(2)}, u32[]{:S(2)}) collective-permute-start(bf16[256,512]{1,0:T(8,128)(2,1)S(1)} %get-tuple-element.74), channel_id=1, source_target_pairs={{0,2},{1,3},{2,0},{3,1},{4,6},{5,7},{6,4},{7,5},{8,10},{9,11},{10,... | collective-permute-start | bytes 786440 | tf_op jit(solution)/shard_map/ppermute | solution.py:698
  100.6 9.3 %collective-permute-start.14 = (bf16[256,512]{1,0:T(8,128)(2,1)S(1)}, bf16[256,512]{1,0:T(8,128)(2,1)S(1)}, u32[]{:S(2)}, u32[]{:S(2)}) collective-permute-start(bf16[256,512]{1,0:T(8,128)(2,1)S(1)} %get-tuple-element.75), channel_id=1, source_target_pairs={{0,2},{1,3},{2,0},{3,1},{4,6},{5,7},{6,4},{7,5},{8,10},{9,11},{10,... | collective-permute-start | bytes 786440 | tf_op jit(solution)/shard_map/ppermute | solution.py:698
  101.3 14.2 %collective-permute-start.12 = (bf16[256,512]{1,0:T(8,128)(2,1)S(1)}, bf16[256,512]{1,0:T(8,128)(2,1)S(1)}, u32[]{:S(2)}, u32[]{:S(2)}) collective-permute-start(bf16[256,512]{1,0:T(8,128)(2,1)S(1)} %get-tuple-element.72), channel_id=1, source_target_pairs={{0,2},{1,3},{2,0},{3,1},{4,6},{5,7},{6,4},{7,5},{8,10},{9,11},{10,... | collective-permute-start | bytes 786440 | tf_op jit(solution)/shard_map/ppermute | solution.py:698
  102.7 16.3 %collective-permute-start.11 = (bf16[256,512]{1,0:T(8,128)(2,1)S(1)}, bf16[256,512]{1,0:T(8,128)(2,1)S(1)}, u32[]{:S(2)}, u32[]{:S(2)}) collective-permute-start(bf16[256,512]{1,0:T(8,128)(2,1)S(1)} %get-tuple-element.71), channel_id=1, source_target_pairs={{0,2},{1,3},{2,0},{3,1},{4,6},{5,7},{6,4},{7,5},{8,10},{9,11},{10,... | collective-permute-start | bytes 786440 | tf_op jit(solution)/shard_map/ppermute | solution.py:698

commit v11 on v10

--- a/solution.py
+++ b/solution.py
@@ -58,7 +58,7 @@
     return pl.BlockSpec(shape, lambda *_: (0,) * len(shape))
 
 
-def decay_kernel(info, ld_t, step_t, skip, cum, cum_s, log_s, f_dev, f_blk, e_blk, rates, by_row, ones):
+def decay_kernel(info, ld_t, step_t, skip, cum, cum_s, log_s, f_dev, f_blk, e_blk, rates, ones):
     heads, length = ld_t.shape
     blocks = length // TOK_B
     per = heads // 2
@@ -106,11 +106,7 @@
     gains = jnp.where(swapped, jnp.concatenate([gains[:, per:], gains[:, :per]], 1), gains)
     values = jnp.concatenate([jnp.exp2(logs), gains], 0)
     for g in range(2):
-        spread = dot(values[:, g * per : (g + 1) * per], member, precision=HIGHEST)
-        rates[g] = spread
-        for b in range(2 * blocks):
-            by_row[g, b] = spread[b : b + 1, :]
-        by_row[g, 2 * blocks] = spread[2 * blocks + 8 : 2 * blocks + 9, :]
+        rates[g] = dot(values[:, g * per : (g + 1) * per], member, precision=HIGHEST)
     for b in range(blocks):
         rows = slice(b * TOK_B, (b + 1) * TOK_B)
         s = ordered(step_t[:, rows])
@@ -139,7 +135,6 @@
         pair,
         pair,
         jax.ShapeDtypeStruct((2, 2 * blocks + 16, width), F32),
-        jax.ShapeDtypeStruct((2, 2 * blocks + 1, 1, width), F32),
         jax.ShapeDtypeStruct((2 * per, width), BF16),
     )
     return pl.pallas_call(
@@ -205,25 +200,25 @@
         state[...] = jnp.zeros_like(state)
         row = lax.broadcasted_iota(jnp.int32, down.shape, 0)
         col = lax.broadcasted_iota(jnp.int32, down.shape, 1)
-        down[...] = (row == col + 1).astype(BF16)
+        down[...] = (lax.rem(row, rows) == col + 1 + row // rows).astype(BF16)
 
     def conv(src, first, behind, weights, emit):
         at_start = jnp.where(info[SEQ] == 0, jnp.zeros_like(first), first)
         lead = jnp.where(i == 0, at_start, behind).astype(F32)
         w0, w1, w2, w3 = [w * 0.5 for w in weights]
-        back = LEAD - 8
-        lead_r1 = pltpu.roll(lead, 1, 0)
-        last_p = (w1 * lead + w0 * lead_r1)[back:]
         moved = dot(down[...], src)
-        top = lax.broadcasted_iota(jnp.int32, (8, lead.shape[1]), 0) == 0
-        head = jnp.where(top, jnp.broadcast_to(lead[LEAD - 1 :], top.shape), moved[0:8])
+        around = jnp.concatenate([lead[LEAD - 8 :], src[0:8].astype(F32)], 0)
         for r in range(0, rows, ROWS_A):
-            cur = src[r : r + ROWS_A].astype(F32)
-            r1 = moved[r : r + ROWS_A] if r else jnp.concatenate([head, moved[8:ROWS_A]], 0)
-            p = w1 * cur + w0 * r1
-            p2 = pltpu.roll(jnp.concatenate([last_p, p], 0), 2, 0)[8:]
-            emit(r, half_silu((w3 * cur + w2 * r1) + p2))
-            last_p = p[ROWS_A - 8 :]
+            total = w3 * src[r : r + ROWS_A].astype(F32)
+            for k, weight in ((1, w2), (2, w1), (3, w0)):
+                first = (k - 1) * rows + r
+                if r:
+                    shifted = moved[first : first + ROWS_A]
+                else:
+                    top = pltpu.roll(around, k, 0)[8:]
+                    shifted = jnp.concatenate([top, moved[first + 8 : first + ROWS_A]], 0)
+                total = total + weight * shifted
+            emit(r, half_silu(total))
 
     for lanes in range(0, 2 * N, SLAB):
         ds = slice(lanes, lanes + SLAB)
@@ -290,7 +285,7 @@
             scratch_shapes=[
                 pltpu.VMEM((TOK_A, width), BF16),
                 pltpu.VMEM((N, width), F32),
-                pltpu.VMEM((TOK_A, TOK_A), BF16),
+                pltpu.VMEM((3 * TOK_A, TOK_A), BF16),
             ],
         ),
         out_shape=(
@@ -408,7 +403,7 @@
     )(*operands)
 
 
-def scan_kernel(order, part, info, x_far, z_far, bc, cum, cum_s, log_s, f_blk, e_blk, by_row, ones, _, uv_out, x, z, sem, state):
+def scan_kernel(order, part, info, x_far, z_far, bc, cum, cum_s, log_s, f_blk, e_blk, rates, ones, _, uv_out, x, z, sem, state):
     length, width = x.shape
     per_slab = SLAB // P_SIZE
     inner = STEP_B // TOK_B
@@ -454,9 +449,9 @@
             xb = x[at, lanes]
             wide = slice(part * width + s * SLAB, part * width + (s + 1) * SLAB)
             sel = ones[:, wide]
-            fade_row = by_row[order, b, :, wide]
-            lead_row = by_row[order, blocks + b, :, wide]
-            skip = by_row[order, 2 * blocks, :, wide]
+            fade_row = rates[order, pl.ds(b, 1), wide]
+            lead_row = rates[order, pl.ds(blocks + b, 1), wide]
+            skip = rates[order, 2 * blocks + 8 : 2 * blocks + 9, wide]
             old = state[:, lanes]
             rise = dot(e_blk[order, at, :], sel)
             carried = dot(c_mat, old.astype(BF16)) * rise
@@ -483,7 +478,7 @@
     lax.fori_loop(0, length // STEP_B, turn, 0)
 
 
-def scan_part(order, part, info, token, x, z, bc, cum, cum_s, log_s, f_blk, e_blk, by_row, ones):
+def scan_part(order, part, info, token, x, z, bc, cum, cum_s, log_s, f_blk, e_blk, rates, ones):
     length, full = x.shape
     width = full // B_PARTS
     return pl.pallas_call(
@@ -500,7 +495,7 @@
         compiler_params=params(16),
         cost_estimate=CHEAP,
         name="scan_part",
-    )(info, x, z, bc, cum, cum_s, log_s, f_blk, e_blk, by_row, ones, token)
+    )(info, x, z, bc, cum, cum_s, log_s, f_blk, e_blk, rates, ones, token)
 
 
 def norm_kernel(places, info, bc0, bc1, state0, state1, gain, _, *refs):
@@ -769,7 +764,7 @@
     bc = bc_input.reshape(length, -1)
     weight_mate = swap(out_weight, "head", 1)
 
-    cum, cum_s, log_s, f_dev, f_blk, e_blk, rates, by_row, ones = decays(info, log_decay, step_size, skip_gain, half)
+    cum, cum_s, log_s, f_dev, f_blk, e_blk, rates, ones = decays(info, log_decay, step_size, skip_gain, half)
     taps = far(conv_weight_x, conv_weight_bc)
     shared = (info, x_far, bc, halo, *taps, f_dev, ones, rates)
     x0, bc0, send = conv_states(0, *shared)
@@ -777,7 +772,7 @@
     x1, bc1, keep = conv_states(1, *shared)
 
     uvs = []
-    groups = [(x, z_far, y, cum, cum_s, log_s, f_blk, e_blk, by_row, ones) for x, y in zip(far(x0, x1), (bc0, bc1))]
+    groups = [(x, z_far, y, cum, cum_s, log_s, f_blk, e_blk, rates, ones) for x, y in zip(far(x0, x1), (bc0, bc1))]
 
     def scan_next(token):
         if len(uvs) < 2 * B_PARTS:

time: 120 us -> 120 us (level)
  no operation moved by 1% of the time
where the time goes in v11:
time: 120 us
  Pallas kernels  83.3 us (69%)
  starting transfers between devices  21 us (18%)
  waiting for transfers between devices  15.3 us (13%)
    pallas_call x4, Pallas kernels, project_both(): pl.pallas_call(functools.partial(both_kernel, first // TILE, cut), grid=(...  25.2 us
    pallas_call x4, Pallas kernels, scan_part(): pl.pallas_call(functools.partial(scan_kernel, order, part), in_specs=[SCA...  21.9 us
    pallas_call x2, Pallas kernels, conv_states(): pl.pallas_call(functools.partial(conv_kernel, order), grid_spec=pltpu.Pre...  14.4 us
    ppermute x12, waiting for transfers between devices, swap(): lax.ppermute(block, axis, [(i, i ^ bit) for i in range(lax.axis_size(axis...  12.2 us
    ppermute x7, starting transfers between devices, rotate(): lax.ppermute(block, 'seq', [(i, (i + distance) % size) for i in range(siz...  11.5 us
    ppermute x12, starting transfers between devices, swap(): lax.ppermute(block, axis, [(i, i ^ bit) for i in range(lax.axis_size(axis...  9.5 us
    pallas_call x2, Pallas kernels, norm_rows(): pl.pallas_call(functools.partial(norm_kernel, places), in_specs=[SCALAR]...  4.99 us
    pallas_call x5, Pallas kernels, add_chunks(): pl.pallas_call(add_kernel, grid=(1,), in_specs=[pl.BlockSpec((rows, count...  4.01 us
  transfers between devices with their start and end apart: 19, of which 7 were waited for; matrix products, arithmetic and copies ran while one was open for 0% of the time, Pallas kernels for 66%

profile of v11, /device:TPU:0, one launch (start us, length us, event | category | flops | bytes accessed | tf_op | source)
XLA Modules:
  0.0 120.1 jit_solution(5523447744517261873)
XLA Ops:
  1.3 2.7 %collective-permute-start = (bf16[16,2560]{1,0:T(8,128)(2,1)S(1)}, bf16[16,2560]{1,0:T(8,128)(2,1)S(1)}, u32[]{:S(2)}, u32[]{:S(2)}) collective-permute-start(bf16[16,2560]{1,0:T(8,128)(2,1)S(1)} %tail_rows.1), channel_id=1, source_target_pairs={{0,4},{4,8},{8,12},{12,16},{16,20},{20,24},{24,28},{28,0},{1,5},{5... | collective-permute-start | bytes 245768 | tf_op jit(solution)/shard_map/ppermute | solution.py:698
  4.1 2.7 %decays.1 = (f32[2,1024,16]{2,1,0:T(8,128)S(1)}, f32[2,16,1024]{2,1,0:T(8,128)S(1)}, f32[2,16,1024]{2,1,0:T(8,128)S(1)}, bf16[2,1024,32]{2,1,0:T(8,128)(2,1)S(1)...) custom-call(s32[9]{0:T(128)S(1)} %stack.36.info, ...), custom_call_target="tpu_custom_call" | custom-call | flops 1 | bytes 1 | tf_op jit(solution)/shard_map/decays/pallas_call | solution.py:140
  7.0 3.0 %collective-permute-done.halo.bc_halo = bf16[16,2560]{1,0:T(8,128)(2,1)S(1)} collective-permute-done((bf16[16,2560]{1,0:T(8,128)(2,1)S(1)}, bf16[16,2560]{1,0:T(8,128)(2,1)S(1)}, u32[]{:S(2)}, u32[]{:S(2)}) %collective-permute-start) | collective-permute-done | bytes 81952 | tf_op jit(solution)/shard_map/ppermute | solution.py:698
  10.1 7.2 %conv_states.2 = (bf16[1024,1024]{1,0:T(8,128)(2,1)}, bf16[1024,256]{1,0:T(8,128)(2,1)S(1)}, bf16[144,1024]{1,0:T(8,128)(2,1)S(1)}) custom-call(s32[9]{0:T(128)S(1)} %stack.36.info, bf16[1024,2048]{1,0:T(8,128)(2,1)} %x_lead.3, bf16[1024,2048]{1,0:T(8,128)(2,1)} %x_lead.3, bf16[1024,512]{1,0:T(8,128)(2,1)S(1)} %bitcast.14, bf16[1024,512]{1,0:T(8,128)(2,1)S(1)} %bitcast.15, ...), custom_call_target="tpu_custom_call" | custom-call | flops 1 | bytes 1 | tf_op jit(solution)/shard_map/conv_states/pallas_call | solution.py:262
  17.3 7.2 %conv_states.3 = (bf16[1024,1024]{1,0:T(8,128)(2,1)}, bf16[1024,256]{1,0:T(8,128)(2,1)S(1)}, f32[128,1024]{1,0:T(8,128)S(1)}) custom-call(s32[9]{0:T(128)S(1)} %stack.36.info, bf16[1024,2048]{1,0:T(8,128)(2,1)} %x_lead.3, bf16[1024,2048]{1,0:T(8,128)(2,1)} %x_lead.3, bf16[1024,512]{1,0:T(8,128)(2,1)S(1)} %bitcast.16, bf16[1024,512]{1,0:T(8,128)(2,1)S(1)} %bitcast.17, ...), custom_call_target="tpu_custom_call" | custom-call | flops 1 | bytes 1 | tf_op jit(solution)/shard_map/conv_states/pallas_call | solution.py:262
  24.5 1.6 %collective-permute-done.1.got = bf16[144,1024]{1,0:T(8,128)(2,1)S(1)} collective-permute-done((bf16[144,1024]{1,0:T(8,128)(2,1)S(1)}, bf16[144,1024]{1,0:T(8,128)(2,1)S(1)}, u32[]{:S(2)}, u32[]{:S(2)}) %collective-permute-start.1) | collective-permute-done | bytes 294944 | tf_op jit(solution)/shard_map/ppermute | solution.py:693
  27.0 2.1 %collective-permute-start.3 = (bf16[144,256]{1,0:T(8,128)(2,1)S(1)}, bf16[144,256]{1,0:T(8,128)(2,1)S(1)}, u32[]{:S(2)}, u32[]{:S(2)}) collective-permute-start(bf16[144,256]{1,0:T(8,128)(2,1)S(1)} %get-tuple-element.59), channel_id=1, source_target_pairs={{0,16},{4,20},{8,24},{12,28},{16,0},{20,4},{24,8},{28,12},{1,17},{... | collective-permute-start | bytes 221192 | tf_op jit(solution)/shard_map/ppermute | solution.py:698
  29.0 1.8 %collective-permute-start.4 = (bf16[144,256]{1,0:T(8,128)(2,1)S(1)}, bf16[144,256]{1,0:T(8,128)(2,1)S(1)}, u32[]{:S(2)}, u32[]{:S(2)}) collective-permute-start(bf16[144,256]{1,0:T(8,128)(2,1)S(1)} %get-tuple-element.60), channel_id=1, source_target_pairs={{0,24},{4,28},{8,0},{12,4},{16,8},{20,12},{24,16},{28,20},{1,25},{... | collective-permute-start | bytes 221192 | tf_op jit(solution)/shard_map/ppermute | solution.py:698
  30.8 5.5 %scan_part.4._.refs_0_ = bf16[1024,1024]{1,0:T(8,128)(2,1)S(1)} custom-call(s32[9]{0:T(128)S(1)} %stack.36.info, bf16[1024,1024]{1,0:T(8,128)(2,1)} %get-tuple-element.61.x_far, bf16[1024,2048]{1,0:T(8,128)(2,1)} %z_far.7, bf16[1024,256]{1,0:T(8,128)(2,1)S(1)} %get-tuple-element.45.bc.bc0, f32[2,1024,16]{2,1,0:T(8,128)S(1)} %get-tuple-element.52.cum, ...), custom_call_target="tpu_custom_call" | custom-call | flops 1 | bytes 1 | tf_op jit(solution)/shard_map/scan_part/pallas_call | solution.py:484
  36.3 5.5 %scan_part.5.refs_4_.refs_1_ = bf16[1024,1024]{1,0:T(8,128)(2,1)S(1)} custom-call(s32[9]{0:T(128)S(1)} %stack.36.info, bf16[1024,1024]{1,0:T(8,128)(2,1)} %get-tuple-element.61.x_far, bf16[1024,2048]{1,0:T(8,128)(2,1)} %z_far.7, bf16[1024,256]{1,0:T(8,128)(2,1)S(1)} %get-tuple-element.45.bc.bc0, f32[2,1024,16]{2,1,0:T(8,128)S(1)} %get-tuple-element.52.cum, ...), custom_call_target="tpu_custom_call" | custom-call | flops 1 | bytes 1 | tf_op jit(solution)/shard_map/scan_part/pallas_call | solution.py:484
  44.6 2.8 %collective-permute-start.7 = (bf16[128,256]{1,0:T(8,128)(2,1)S(1)}, bf16[128,256]{1,0:T(8,128)(2,1)S(1)}, u32[]{:S(2)}, u32[]{:S(2)}) collective-permute-start(bf16[128,256]{1,0:T(8,128)(2,1)S(1)} %get-tuple-element.65), channel_id=1, source_target_pairs={{0,24},{4,28},{8,0},{12,4},{16,8},{20,12},{24,16},{28,20},{1,25},{... | collective-permute-start | bytes 196616 | tf_op jit(solution)/shard_map/ppermute | solution.py:698
  47.4 5.5 %scan_part.6._.refs_2_ = bf16[1024,1024]{1,0:T(8,128)(2,1)S(1)} custom-call(s32[9]{0:T(128)S(1)} %stack.36.info, bf16[1024,1024]{1,0:T(8,128)(2,1)} %get-tuple-element.51.x_far, bf16[1024,2048]{1,0:T(8,128)(2,1)} %z_far.7, bf16[1024,256]{1,0:T(8,128)(2,1)S(1)} %get-tuple-element.46.bc.bc1, f32[2,1024,16]{2,1,0:T(8,128)S(1)} %get-tuple-element.52.cum, ...), custom_call_target="tpu_custom_call" | custom-call | flops 1 | bytes 1 | tf_op jit(solution)/shard_map/scan_part/pallas_call | solution.py:484
  54.3 5.5 %scan_part.7.refs_3_ = bf16[1024,1024]{1,0:T(8,128)(2,1)S(1)} custom-call(s32[9]{0:T(128)S(1)} %stack.36.info, bf16[1024,1024]{1,0:T(8,128)(2,1)} %get-tuple-element.51.x_far, bf16[1024,2048]{1,0:T(8,128)(2,1)} %z_far.7, bf16[1024,256]{1,0:T(8,128)(2,1)S(1)} %get-tuple-element.46.bc.bc1, f32[2,1024,16]{2,1,0:T(8,128)S(1)} %get-tuple-element.52.cum, ...), custom_call_target="tpu_custom_call" | custom-call | flops 1 | bytes 1 | tf_op jit(solution)/shard_map/scan_part/pallas_call | solution.py:484
  60.2 2.5 %norm_rows.2._ = bf16[512,2048]{1,0:T(8,128)(2,1)S(1)} custom-call(s32[9]{0:T(128)S(1)} %stack.36.info, bf16[1024,256]{1,0:T(8,128)(2,1)S(1)} %get-tuple-element.45.bc.bc0, bf16[1024,256]{1,0:T(8,128)(2,1)S(1)} %get-tuple-element.46.bc.bc1, bf16[128,1024]{1,0:T(8,128)(2,1)S(1)} %collective-permute-done.8.state0, ...), custom_call_target="tpu_custom_call" | custom-call | flops 1 | bytes 1 | tf_op jit(solution)/shard_map/norm_rows/pallas_call | solution.py:536
  62.8 2.5 %norm_rows.3.owns = bf16[512,2048]{1,0:T(8,128)(2,1)S(1)} custom-call(s32[9]{0:T(128)S(1)} %stack.36.info, bf16[1024,256]{1,0:T(8,128)(2,1)S(1)} %get-tuple-element.45.bc.bc0, bf16[1024,256]{1,0:T(8,128)(2,1)S(1)} %get-tuple-element.46.bc.bc1, bf16[128,1024]{1,0:T(8,128)(2,1)S(1)} %collective-permute-done.8.state0, ...), custom_call_target="tpu_custom_call" | custom-call | flops 1 | bytes 1 | tf_op jit(solution)/shard_map/norm_rows/pallas_call | solution.py:536
  65.3 1.6 %collective-permute-done.9.mates = bf16[512,2048]{1,0:T(8,128)(2,1)S(1)} collective-permute-done((bf16[512,2048]{1,0:T(8,128)(2,1)S(1)}, bf16[512,2048]{1,0:T(8,128)(2,1)S(1)}, u32[]{:S(2)}, u32[]{:S(2)}) %collective-permute-start.9) | collective-permute-done | bytes 2097184 | tf_op jit(solution)/shard_map/ppermute | solution.py:693
  66.9 3.1 %project_ahead.1 = bf16[256,512]{1,0:T(8,128)(2,1)S(1)} custom-call(bf16[512,2048]{1,0:T(8,128)(2,1)S(1)} %norm_rows.3.owns, bf16[512,2048]{1,0:T(8,128)(2,1)S(1)} %collective-permute-done.9.mates, bf16[2048,4096]{1,0:T(8,128)(2,1)} %w0_far.11, bf16[2048,4096]{1,0:T(8,128)(2,1)} %collective-permute-done.10.w1_far), custom_call_target="tpu_custom_call" | custom-call | flops 1 | bytes 1 | tf_op jit(solution)/shard_map/project_ahead/pallas_call | solution.py:592
  71.5 4.2 %project_both.7 = (bf16[256,512]{1,0:T(8,128)(2,1)S(1)}, f32[256,512]{1,0:T(8,128)S(1)}) custom-call(bf16[512,2048]{1,0:T(8,128)(2,1)S(1)} %norm_rows.3.owns, bf16[512,2048]{1,0:T(8,128)(2,1)S(1)} %collective-permute-done.9.mates, bf16[2048,4096]{1,0:T(8,128)(2,1)} %w0_far.11, bf16[2048,4096]{1,0:T(8,128)(2,1)} %collective-permute-done.10.w1_far), custom_call_target="tpu_custom_call" | custom-call | flops 1 | bytes 1 | tf_op jit(solution)/shard_map/project_both/pallas_call | solution.py:626
  76.5 7.0 %project_both.6 = (bf16[256,512]{1,0:T(8,128)(2,1)S(1)}, bf16[256,512]{1,0:T(8,128)(2,1)S(1)}, f32[256,1024]{1,0:T(8,128)S(1)}) custom-call(bf16[512,2048]{1,0:T(8,128)(2,1)S(1)} %norm_rows.3.owns, bf16[512,2048]{1,0:T(8,128)(2,1)S(1)} %collective-permute-done.9.mates, bf16[2048,4096]{1,0:T(8,128)(2,1)} %w0_far.11, ...), custom_call_target="tpu_custom_call" | custom-call | flops 1 | bytes 1 | tf_op jit(solution)/shard_map/project_both/pallas_call | solution.py:626
  85.5 7.0 %project_both.5 = (bf16[256,512]{1,0:T(8,128)(2,1)S(1)}, bf16[256,512]{1,0:T(8,128)(2,1)S(1)}, f32[256,1024]{1,0:T(8,128)S(1)}) custom-call(bf16[512,2048]{1,0:T(8,128)(2,1)S(1)} %norm_rows.3.owns, bf16[512,2048]{1,0:T(8,128)(2,1)S(1)} %collective-permute-done.9.mates, bf16[2048,4096]{1,0:T(8,128)(2,1)} %w0_far.11, ...), custom_call_target="tpu_custom_call" | custom-call | flops 1 | bytes 1 | tf_op jit(solution)/shard_map/project_both/pallas_call | solution.py:626
  94.0 7.0 %project_both.4 = (bf16[256,512]{1,0:T(8,128)(2,1)S(1)}, bf16[256,512]{1,0:T(8,128)(2,1)S(1)}, f32[256,1024]{1,0:T(8,128)S(1)}) custom-call(bf16[512,2048]{1,0:T(8,128)(2,1)S(1)} %norm_rows.3.owns, bf16[512,2048]{1,0:T(8,128)(2,1)S(1)} %collective-permute-done.9.mates, bf16[2048,4096]{1,0:T(8,128)(2,1)} %w0_far.11, ...), custom_call_target="tpu_custom_call" | custom-call | flops 1 | bytes 1 | tf_op jit(solution)/shard_map/project_both/pallas_call | solution.py:626
  103.7 3.8 %project_near.1.refs_1_ = bf16[256,4096]{1,0:T(8,128)(2,1)} custom-call(bf16[512,2048]{1,0:T(8,128)(2,1)S(1)} %norm_rows.3.owns, bf16[512,2048]{1,0:T(8,128)(2,1)S(1)} %collective-permute-done.9.mates, bf16[2048,4096]{1,0:T(8,128)(2,1)} %w0_far.11, bf16[2048,4096]{1,0:T(8,128)(2,1)} %collective-permute-done.10.w1_far, ...), custom_call_target="tpu_custom_call" | custom-call | flops 1 | bytes 1 | tf_op jit(solution)/shard_map/project_near/pallas_call | solution.py:650
  111.2 4.7 %collective-permute-done.12.refs_0_ = bf16[256,512]{1,0:T(8,128)(2,1)S(1)} collective-permute-done((bf16[256,512]{1,0:T(8,128)(2,1)S(1)}, bf16[256,512]{1,0:T(8,128)(2,1)S(1)}, u32[]{:S(2)}, u32[]{:S(2)}) %collective-permute-start.12) | collective-permute-done | bytes 262176 | tf_op jit(solution)/shard_map/ppermute | solution.py:693
  116.7 2.7 %collective-permute-done.11.refs_0_ = bf16[256,512]{1,0:T(8,128)(2,1)S(1)} collective-permute-done((bf16[256,512]{1,0:T(8,128)(2,1)S(1)}, bf16[256,512]{1,0:T(8,128)(2,1)S(1)}, u32[]{:S(2)}, u32[]{:S(2)}) %collective-permute-start.11) | collective-permute-done | bytes 262176 | tf_op jit(solution)/shard_map/ppermute | solution.py:693
  (44 shorter events, 20.8 us)
Async XLA Ops:
  0.0 6.8 %copy-start.1 = (bf16[1024,2,256]{2,1,0:T(2,128)(2,1)S(1)}, bf16[1024,2,256]{2,1,0:T(2,128)(2,1)}, u32[]{:S(2)}) copy-start(bf16[1024,2,256]{2,1,0:T(2,128)(2,1)} %bc.1) | copy-start | bytes 3145732
  0.0 66.9 %collective-permute-start.10 = (bf16[2048,4096]{1,0:T(8,128)(2,1)}, bf16[2048,4096]{1,0:T(8,128)(2,1)}, u32[]{:S(2)}, u32[]{:S(2)}) collective-permute-start(bf16[2048,4096]{1,0:T(8,128)(2,1)} %w0_far.11), channel_id=1, source_target_pairs={{0,1},{1,0},{2,3},{3,2},{4,5},{5,4},{6,7},{7,6},{8,9},{9,8},{10,11... | collective-permute-start | bytes 50331656 | tf_op jit(solution)/shard_map/ppermute | solution.py:693
  1.3 8.7 %collective-permute-start = (bf16[16,2560]{1,0:T(8,128)(2,1)S(1)}, bf16[16,2560]{1,0:T(8,128)(2,1)S(1)}, u32[]{:S(2)}, u32[]{:S(2)}) collective-permute-start(bf16[16,2560]{1,0:T(8,128)(2,1)S(1)} %tail_rows.1), channel_id=1, source_target_pairs={{0,4},{4,8},{8,12},{12,16},{16,20},{20,24},{24,28},{28,0},{1,5},{5... | collective-permute-start | bytes 245768 | tf_op jit(solution)/shard_map/ppermute | solution.py:698
  17.3 8.7 %collective-permute-start.1 = (bf16[144,1024]{1,0:T(8,128)(2,1)S(1)}, bf16[144,1024]{1,0:T(8,128)(2,1)S(1)}, u32[]{:S(2)}, u32[]{:S(2)}) collective-permute-start(bf16[144,1024]{1,0:T(8,128)(2,1)S(1)} %get-tuple-element.47), channel_id=1, source_target_pairs={{0,4},{4,0},{8,12},{12,8},{16,20},{20,16},{24,28},{28,24},{1,5},{5... | collective-permute-start | bytes 884744 | tf_op jit(solution)/shard_map/ppermute | solution.py:693
  26.9 14.9 %collective-permute-start.2 = (bf16[144,256]{1,0:T(8,128)(2,1)S(1)}, bf16[144,256]{1,0:T(8,128)(2,1)S(1)}, u32[]{:S(2)}, u32[]{:S(2)}) collective-permute-start(bf16[144,256]{1,0:T(8,128)(2,1)S(1)} %get-tuple-element.58), channel_id=1, source_target_pairs={{0,8},{4,12},{8,16},{12,20},{16,24},{20,28},{24,0},{28,4},{1,9},{5... | collective-permute-start | bytes 221192 | tf_op jit(solution)/shard_map/ppermute | solution.py:698
  27.0 14.8 %collective-permute-start.3 = (bf16[144,256]{1,0:T(8,128)(2,1)S(1)}, bf16[144,256]{1,0:T(8,128)(2,1)S(1)}, u32[]{:S(2)}, u32[]{:S(2)}) collective-permute-start(bf16[144,256]{1,0:T(8,128)(2,1)S(1)} %get-tuple-element.59), channel_id=1, source_target_pairs={{0,16},{4,20},{8,24},{12,28},{16,0},{20,4},{24,8},{28,12},{1,17},{... | collective-permute-start | bytes 221192 | tf_op jit(solution)/shard_map/ppermute | solution.py:698
  29.0 12.8 %collective-permute-start.4 = (bf16[144,256]{1,0:T(8,128)(2,1)S(1)}, bf16[144,256]{1,0:T(8,128)(2,1)S(1)}, u32[]{:S(2)}, u32[]{:S(2)}) collective-permute-start(bf16[144,256]{1,0:T(8,128)(2,1)S(1)} %get-tuple-element.60), channel_id=1, source_target_pairs={{0,24},{4,28},{8,0},{12,4},{16,8},{20,12},{24,16},{28,20},{1,25},{... | collective-permute-start | bytes 221192 | tf_op jit(solution)/shard_map/ppermute | solution.py:698
  42.4 10.5 %collective-permute-start.5 = (bf16[128,256]{1,0:T(8,128)(2,1)S(1)}, bf16[128,256]{1,0:T(8,128)(2,1)S(1)}, u32[]{:S(2)}, u32[]{:S(2)}) collective-permute-start(bf16[128,256]{1,0:T(8,128)(2,1)S(1)} %get-tuple-element.63), channel_id=1, source_target_pairs={{0,8},{4,12},{8,16},{12,20},{16,24},{20,28},{24,0},{28,4},{1,9},{5... | collective-permute-start | bytes 196616 | tf_op jit(solution)/shard_map/ppermute | solution.py:698
  43.0 9.9 %collective-permute-start.6 = (bf16[128,256]{1,0:T(8,128)(2,1)S(1)}, bf16[128,256]{1,0:T(8,128)(2,1)S(1)}, u32[]{:S(2)}, u32[]{:S(2)}) collective-permute-start(bf16[128,256]{1,0:T(8,128)(2,1)S(1)} %get-tuple-element.64), channel_id=1, source_target_pairs={{0,16},{4,20},{8,24},{12,28},{16,0},{20,4},{24,8},{28,12},{1,17},{... | collective-permute-start | bytes 196616 | tf_op jit(solution)/shard_map/ppermute | solution.py:698
  44.6 8.4 %collective-permute-start.7 = (bf16[128,256]{1,0:T(8,128)(2,1)S(1)}, bf16[128,256]{1,0:T(8,128)(2,1)S(1)}, u32[]{:S(2)}, u32[]{:S(2)}) collective-permute-start(bf16[128,256]{1,0:T(8,128)(2,1)S(1)} %get-tuple-element.65), channel_id=1, source_target_pairs={{0,24},{4,28},{8,0},{12,4},{16,8},{20,12},{24,16},{28,20},{1,25},{... | collective-permute-start | bytes 196616 | tf_op jit(solution)/shard_map/ppermute | solution.py:698
  53.8 6.5 %copy-start = (f32[2048]{0:T(1024)S(1)}, f32[2048]{0:T(1024)}, u32[]{:S(2)}) copy-start(f32[2048]{0:T(1024)} %param.18) | copy-start | bytes 24580
  53.8 6.4 %collective-permute-start.8 = (bf16[128,1024]{1,0:T(8,128)(2,1)S(1)}, bf16[128,1024]{1,0:T(8,128)(2,1)S(1)}, u32[]{:S(2)}, u32[]{:S(2)}) collective-permute-start(bf16[128,1024]{1,0:T(8,128)(2,1)S(1)} %get-tuple-element.66._), channel_id=1, source_target_pairs={{0,4},{4,0},{8,12},{12,8},{16,20},{20,16},{24,28},{28,24},{1,5},{5... | collective-permute-start | bytes 786440 | tf_op jit(solution)/shard_map/ppermute | solution.py:693
  62.7 4.2 %collective-permute-start.9 = (bf16[512,2048]{1,0:T(8,128)(2,1)S(1)}, bf16[512,2048]{1,0:T(8,128)(2,1)S(1)}, u32[]{:S(2)}, u32[]{:S(2)}) collective-permute-start(bf16[512,2048]{1,0:T(8,128)(2,1)S(1)} %norm_rows.2._), channel_id=1, source_target_pairs={{0,1},{1,0},{2,3},{3,2},{4,5},{5,4},{6,7},{7,6},{8,9},{9,8},{10,11... | collective-permute-start | bytes 6291464 | tf_op jit(solution)/shard_map/ppermute | solution.py:693
  70.0 31.0 %collective-permute-start.18 = (bf16[256,512]{1,0:T(8,128)(2,1)S(1)}, bf16[256,512]{1,0:T(8,128)(2,1)S(1)}, u32[]{:S(2)}, u32[]{:S(2)}) collective-permute-start(bf16[256,512]{1,0:T(8,128)(2,1)S(1)} %project_ahead.1), channel_id=1, source_target_pairs={{0,2},{1,3},{2,0},{3,1},{4,6},{5,7},{6,4},{7,5},{8,10},{9,11},{10,... | collective-permute-start | bytes 786440 | tf_op jit(solution)/shard_map/ppermute | solution.py:693
  75.8 25.9 %collective-permute-start.17 = (bf16[256,512]{1,0:T(8,128)(2,1)S(1)}, bf16[256,512]{1,0:T(8,128)(2,1)S(1)}, u32[]{:S(2)}, u32[]{:S(2)}) collective-permute-start(bf16[256,512]{1,0:T(8,128)(2,1)S(1)} %get-tuple-element.78), channel_id=1, source_target_pairs={{0,2},{1,3},{2,0},{3,1},{4,6},{5,7},{6,4},{7,5},{8,10},{9,11},{10,... | collective-permute-start | bytes 786440 | tf_op jit(solution)/shard_map/ppermute | solution.py:693
  83.4 19.7 %collective-permute-start.15 = (bf16[256,512]{1,0:T(8,128)(2,1)S(1)}, bf16[256,512]{1,0:T(8,128)(2,1)S(1)}, u32[]{:S(2)}, u32[]{:S(2)}) collective-permute-start(bf16[256,512]{1,0:T(8,128)(2,1)S(1)} %get-tuple-element.75), channel_id=1, source_target_pairs={{0,2},{1,3},{2,0},{3,1},{4,6},{5,7},{6,4},{7,5},{8,10},{9,11},{10,... | collective-permute-start | bytes 786440 | tf_op jit(solution)/shard_map/ppermute | solution.py:693
  84.9 23.4 %collective-permute-start.16 = (bf16[256,512]{1,0:T(8,128)(2,1)S(1)}, bf16[256,512]{1,0:T(8,128)(2,1)S(1)}, u32[]{:S(2)}, u32[]{:S(2)}) collective-permute-start(bf16[256,512]{1,0:T(8,128)(2,1)S(1)} %get-tuple-element.76), channel_id=1, source_target_pairs={{0,2},{1,3},{2,0},{3,1},{4,6},{5,7},{6,4},{7,5},{8,10},{9,11},{10,... | collective-permute-start | bytes 786440 | tf_op jit(solution)/shard_map/ppermute | solution.py:693
  92.5 16.6 %collective-permute-start.13 = (bf16[256,512]{1,0:T(8,128)(2,1)S(1)}, bf16[256,512]{1,0:T(8,128)(2,1)S(1)}, u32[]{:S(2)}, u32[]{:S(2)}) collective-permute-start(bf16[256,512]{1,0:T(8,128)(2,1)S(1)} %get-tuple-element.72), channel_id=1, source_target_pairs={{0,2},{1,3},{2,0},{3,1},{4,6},{5,7},{6,4},{7,5},{8,10},{9,11},{10,... | collective-permute-start | bytes 786440 | tf_op jit(solution)/shard_map/ppermute | solution.py:693
  101.0 9.3 %collective-permute-start.14 = (bf16[256,512]{1,0:T(8,128)(2,1)S(1)}, bf16[256,512]{1,0:T(8,128)(2,1)S(1)}, u32[]{:S(2)}, u32[]{:S(2)}) collective-permute-start(bf16[256,512]{1,0:T(8,128)(2,1)S(1)} %get-tuple-element.73), channel_id=1, source_target_pairs={{0,2},{1,3},{2,0},{3,1},{4,6},{5,7},{6,4},{7,5},{8,10},{9,11},{10,... | collective-permute-start | bytes 786440 | tf_op jit(solution)/shard_map/ppermute | solution.py:693
  101.7 14.2 %collective-permute-start.12 = (bf16[256,512]{1,0:T(8,128)(2,1)S(1)}, bf16[256,512]{1,0:T(8,128)(2,1)S(1)}, u32[]{:S(2)}, u32[]{:S(2)}) collective-permute-start(bf16[256,512]{1,0:T(8,128)(2,1)S(1)} %get-tuple-element.70), channel_id=1, source_target_pairs={{0,2},{1,3},{2,0},{3,1},{4,6},{5,7},{6,4},{7,5},{8,10},{9,11},{10,... | collective-permute-start | bytes 786440 | tf_op jit(solution)/shard_map/ppermute | solution.py:693
  103.1 16.3 %collective-permute-start.11 = (bf16[256,512]{1,0:T(8,128)(2,1)S(1)}, bf16[256,512]{1,0:T(8,128)(2,1)S(1)}, u32[]{:S(2)}, u32[]{:S(2)}) collective-permute-start(bf16[256,512]{1,0:T(8,128)(2,1)S(1)} %get-tuple-element.69), channel_id=1, source_target_pairs={{0,2},{1,3},{2,0},{3,1},{4,6},{5,7},{6,4},{7,5},{8,10},{9,11},{10,... | collective-permute-start | bytes 786440 | tf_op jit(solution)/shard_map/ppermute | solution.py:693

commit v12 on v10

--- a/solution.py
+++ b/solution.py
@@ -58,11 +58,13 @@
     return pl.BlockSpec(shape, lambda *_: (0,) * len(shape))
 
 
-def decay_kernel(info, ld_t, step_t, skip, cum, cum_s, log_s, f_dev, f_blk, e_blk, rates, by_row, ones):
+def decay_kernel(info, ld_t, step_t, skip, *refs):
+    cum, cum_s, log_s, f_dev, f_blk, e_blk, rates = [refs[2 * k : 2 * k + 2] for k in range(7)]
+    ones = refs[14]
     heads, length = ld_t.shape
     blocks = length // TOK_B
     per = heads // 2
-    width = rates.shape[2]
+    width = ones.shape[1]
     swapped = info[GROUP] == 1
     row = lax.broadcasted_iota(jnp.int32, (TOK_B, TOK_B), 0)
     col = lax.broadcasted_iota(jnp.int32, (TOK_B, TOK_B), 1)
@@ -79,7 +81,7 @@
         for g in range(2):
             own = slice(g * per, (g + 1) * per)
             both = jnp.concatenate([high[own], low[own]], 0)
-            ref[g, rows, :] = dot(eye, both, ((1,), (1,))).astype(BF16)
+            ref[g][rows, :] = dot(eye, both, ((1,), (1,))).astype(BF16)
 
     member = lax.broadcasted_iota(jnp.int32, (per, width), 0) == lax.broadcasted_iota(jnp.int32, (per, width), 1) // P_SIZE
     member = member.astype(F32)
@@ -91,7 +93,7 @@
         logs = ordered(ld_t[:, rows]) * LOG2E
         c = dot(lower, logs, ((1,), (1,)), HIGHEST)
         for g in range(2):
-            cum[g, rows, :] = c[:, g * per : (g + 1) * per]
+            cum[g][rows, :] = c[:, g * per : (g + 1) * per]
         row_totals.append(c[TOK_B - 1 : TOK_B, :])
         c = dot(logs, upper, precision=HIGHEST)
         cums.append(c)
@@ -106,11 +108,7 @@
     gains = jnp.where(swapped, jnp.concatenate([gains[:, per:], gains[:, :per]], 1), gains)
     values = jnp.concatenate([jnp.exp2(logs), gains], 0)
     for g in range(2):
-        spread = dot(values[:, g * per : (g + 1) * per], member, precision=HIGHEST)
-        rates[g] = spread
-        for b in range(2 * blocks):
-            by_row[g, b] = spread[b : b + 1, :]
-        by_row[g, 2 * blocks] = spread[2 * blocks + 8 : 2 * blocks + 9, :]
+        rates[g][...] = dot(values[:, g * per : (g + 1) * per], member, precision=HIGHEST)
     for b in range(blocks):
         rows = slice(b * TOK_B, (b + 1) * TOK_B)
         s = ordered(step_t[:, rows])
@@ -118,8 +116,8 @@
         shifted = cums[b] - log_step
         for g in range(2):
             own = slice(g * per, (g + 1) * per)
-            log_s[g, :, rows] = log_step[own, :]
-            cum_s[g, :, rows] = shifted[own, :]
+            log_s[g][:, rows] = log_step[own, :]
+            cum_s[g][:, rows] = shifted[own, :]
         put(f_dev, rows, jnp.exp2(total - (cums[b] + before[b])) * s)
         put(f_blk, rows, jnp.exp2(totals[b] - cums[b]) * s)
         put(e_blk, rows, jnp.exp2(cums[b]))
@@ -129,20 +127,13 @@
     length, heads = log_decay.shape
     blocks = length // TOK_B
     per = heads // 2
-    across = jax.ShapeDtypeStruct((2, per, length), F32)
-    pair = jax.ShapeDtypeStruct((2, length, 2 * per), BF16)
-    shapes = (
-        jax.ShapeDtypeStruct((2, length, per), F32),
-        across,
-        across,
-        pair,
-        pair,
-        pair,
-        jax.ShapeDtypeStruct((2, 2 * blocks + 16, width), F32),
-        jax.ShapeDtypeStruct((2, 2 * blocks + 1, 1, width), F32),
-        jax.ShapeDtypeStruct((2 * per, width), BF16),
-    )
-    return pl.pallas_call(
+    across = jax.ShapeDtypeStruct((per, length), F32)
+    pair = jax.ShapeDtypeStruct((length, 2 * per), BF16)
+    column = jax.ShapeDtypeStruct((length, per), F32)
+    rates = jax.ShapeDtypeStruct((2 * blocks + 16, width), F32)
+    shapes = [shape for shape in (column, across, across, pair, pair, pair, rates) for _ in range(2)]
+    shapes.append(jax.ShapeDtypeStruct((2 * per, width), BF16))
+    *refs, ones = pl.pallas_call(
         decay_kernel,
         in_specs=[SCALAR] + [FULL] * 3,
         out_specs=[FULL] * len(shapes),
@@ -151,6 +142,7 @@
         cost_estimate=CHEAP,
         name="decays",
     )(info, *far(log_decay.T, step.T, skip[None, :]))
+    return [tuple(refs[2 * k : 2 * k + 2]) for k in range(7)], ones
 
 
 def tail_kernel(x, bc, out):
@@ -236,7 +228,7 @@
 
     for lanes in range(0, width, SLAB):
         ds = slice(lanes, lanes + SLAB)
-        scale = dot(f_dev[0], ones[:, ds])
+        scale = dot(f_dev[...], ones[:, ds])
 
         def emit(r, value):
             x_out[r : r + ROWS_A, ds] = value.astype(BF16)
@@ -250,8 +242,8 @@
     @pl.when(i == pl.num_programs(0) - 1)
     def _():
         if order == 0:
-            row = rates.shape[1] - 16
-            put_message(final, state[...], rates[0, row : row + 1, :])
+            row = rates.shape[0] - 16
+            put_message(final, state[...], rates[row : row + 1, :])
         else:
             final[...] = state[...]
 
@@ -278,9 +270,9 @@
                 pl.BlockSpec((LEAD, 2 * N), lambda i, info: (0, full // (2 * N) + info[GROUP + order])),
                 pl.BlockSpec((KCONV, width), column),
                 whole(wbc.shape),
-                pl.BlockSpec((1, TOK_A, f_dev.shape[2]), lambda i, info: (order, i, 0)),
+                pl.BlockSpec((TOK_A, f_dev.shape[1]), rows),
                 whole(ones.shape),
-                pl.BlockSpec((1,) + rates.shape[1:], lambda i, info: (order, 0, 0)),
+                whole(rates.shape),
             ],
             out_specs=[
                 pl.BlockSpec((TOK_A, width), rows),
@@ -308,8 +300,8 @@
     half = keep.shape[1]
     is_odd = info[ODD] == 1
     arrived, their = take_message(got)
-    row = rates.shape[1] - 16
-    mine = rates[1, row : row + 1, :]
+    row = rates.shape[0] - 16
+    mine = rates[row : row + 1, :]
     early = jnp.where(is_odd, arrived, keep[...])
     late = jnp.where(is_odd, keep[...], arrived)
     even_decay = jnp.where(is_odd, their, mine)
@@ -351,8 +343,8 @@
     piece = half // pairs
     is_odd = info[ODD] == 1
     arrived, their = take_message(got)
-    row = rates.shape[1] - 16
-    mine = rates[1, row : row + 1, :]
+    row = rates.shape[0] - 16
+    mine = rates[row : row + 1, :]
     early = jnp.where(is_odd, arrived, keep[...])
     late = jnp.where(is_odd, keep[...], arrived)
     even_decay = jnp.where(is_odd, their, mine)
@@ -408,7 +400,7 @@
     )(*operands)
 
 
-def scan_kernel(order, part, info, x_far, z_far, bc, cum, cum_s, log_s, f_blk, e_blk, by_row, ones, _, uv_out, x, z, sem, state):
+def scan_kernel(order, part, info, x_far, z_far, bc, cum, cum_s, log_s, f_blk, e_blk, rates, ones, _, uv_out, x, z, sem, state):
     length, width = x.shape
     per_slab = SLAB // P_SIZE
     inner = STEP_B // TOK_B
@@ -454,36 +446,36 @@
             xb = x[at, lanes]
             wide = slice(part * width + s * SLAB, part * width + (s + 1) * SLAB)
             sel = ones[:, wide]
-            fade_row = by_row[order, b, :, wide]
-            lead_row = by_row[order, blocks + b, :, wide]
-            skip = by_row[order, 2 * blocks, :, wide]
+            fade_row = rates[pl.ds(b, 1), wide]
+            lead_row = rates[pl.ds(blocks + b, 1), wide]
+            skip = rates[2 * blocks + 8 : 2 * blocks + 9, wide]
             old = state[:, lanes]
-            rise = dot(e_blk[order, at, :], sel)
+            rise = dot(e_blk[at, :], sel)
             carried = dot(c_mat, old.astype(BF16)) * rise
             within = []
             for q in range(per_slab // 2):
                 tables = []
                 for h in (2 * q, 2 * q + 1):
                     head = first_head + s * per_slab + h
-                    column = cum[order, at, head : head + 1]
+                    column = cum[at, head : head + 1]
                     own = slice(head, head + 1)
-                    gap = jnp.minimum(column - cum_s[order, own, at], log_s[order, own, at])
+                    gap = jnp.minimum(column - cum_s[own, at], log_s[own, at])
                     tables.append((scores * jnp.exp2(gap)).astype(BF16))
                 xp = xb[:, q * 2 * P_SIZE : (q + 1) * 2 * P_SIZE]
                 stacked = jnp.concatenate([jnp.where(first, xp, zero), jnp.where(first, zero, xp)], 0)
                 within.append(dot(jnp.concatenate(tables, 1), stacked))
             xs = xb.astype(F32)
             y = jnp.concatenate(within, 1) + carried + skip * xs
-            gate = half_silu(z[at, lanes].astype(F32) * 0.5)
+            gate = half_silu((z[at, lanes] * 0.5).astype(F32))
             uv_out[at, lanes] = (y * gate).astype(BF16)
             uv_out[at, width + s * SLAB : width + (s + 1) * SLAB] = (gate * rise * lead_row).astype(BF16)
-            xf = (xs * dot(f_blk[order, at, :], sel)).astype(BF16)
+            xf = (xs * dot(f_blk[at, :], sel)).astype(BF16)
             state[:, lanes] = old * fade_row + dot(b_across, xf)
 
     lax.fori_loop(0, length // STEP_B, turn, 0)
 
 
-def scan_part(order, part, info, token, x, z, bc, cum, cum_s, log_s, f_blk, e_blk, by_row, ones):
+def scan_part(order, part, info, token, x, z, bc, cum, cum_s, log_s, f_blk, e_blk, rates, ones):
     length, full = x.shape
     width = full // B_PARTS
     return pl.pallas_call(
@@ -500,11 +492,18 @@
         compiler_params=params(16),
         cost_estimate=CHEAP,
         name="scan_part",
-    )(info, x, z, bc, cum, cum_s, log_s, f_blk, e_blk, by_row, ones, token)
-
-
-def norm_kernel(places, info, bc0, bc1, state0, state1, gain, _, *refs):
-    uvs, out = refs[:-1], refs[-1]
+    )(info, x, z, bc, cum, cum_s, log_s, f_blk, e_blk, rates, ones, token)
+
+
+def norm_kernel(places, fetched, info, bc0, bc1, state0, state1, gain, _, *refs):
+    uvs, refs = refs[: 2 * B_PARTS], refs[2 * B_PARTS :]
+    weights, out, tiles, sem = refs[:fetched], refs[fetched], refs[fetched + 1 : 2 * fetched + 1], refs[-1]
+    copies = [
+        pltpu.make_async_copy(weight.at[:, pl.ds(0, tile.shape[1])], tile, sem.at[k])
+        for k, (weight, tile) in enumerate(zip(weights, tiles))
+    ]
+    for copy in copies:
+        copy.start()
     count = out.shape[0] // len(places)
     per = state0.shape[1]
     part = per // B_PARTS
@@ -535,18 +534,22 @@
             return 0
 
         lax.fori_loop(0, count // ROWS_C, step, 0)
-
-
-def norm_rows(places, info, count, token, bcs, states, gain, uvs):
+    for copy in copies:
+        copy.wait()
+
+
+def norm_rows(places, info, count, token, bcs, states, gain, uvs, weights=(), columns=0):
+    tile = jax.ShapeDtypeStruct((gain.shape[1], columns), BF16)
     return pl.pallas_call(
-        functools.partial(norm_kernel, places),
-        in_specs=[SCALAR] + [FULL] * 5 + [ANY] + [FULL] * len(uvs),
-        out_specs=FULL,
-        out_shape=jax.ShapeDtypeStruct((len(places) * count, gain.shape[1]), BF16),
+        functools.partial(norm_kernel, places, len(weights)),
+        in_specs=[SCALAR] + [FULL] * 5 + [ANY] + [FULL] * len(uvs) + [FAR] * len(weights),
+        out_specs=[FULL] * (1 + len(weights)),
+        out_shape=[jax.ShapeDtypeStruct((len(places) * count, gain.shape[1]), BF16)] + [tile] * len(weights),
+        scratch_shapes=[pltpu.SemaphoreType.DMA((2,))],
         compiler_params=params(16),
         cost_estimate=CHEAP,
         name="norm_rows",
-    )(info, *bcs, *states, gain, token, *uvs)
+    )(info, *bcs, *states, gain, token, *uvs, *weights)
 
 
 def stream(base, w0_far, w1_far, w0, w1, sem):
@@ -586,22 +589,18 @@
     ]
 
 
-def ahead_kernel(base, owns, mates, w0_far, w1_far, out, w0, w1, sem):
-    slot = stream(base, w0_far, w1_far, w0, w1, sem)
+def ahead_kernel(owns, mates, w0, w1, out):
     rows = out.shape[0]
-    out[...] = (dot(owns[0:rows, :], w0[slot]) + dot(mates[0:rows, :], w1[slot])).astype(BF16)
-
-
-def project_ahead(owns, mates, w0, w1, first, count):
-    rows, depth = owns.shape[0] // 2, owns.shape[1]
+    out[...] = (dot(owns[0:rows, :], w0[...]) + dot(mates[0:rows, :], w1[...])).astype(BF16)
+
+
+def project_ahead(owns, mates, w0, w1):
     return pl.pallas_call(
-        functools.partial(ahead_kernel, first // TILE),
-        grid=(count // TILE,),
-        in_specs=[FULL, FULL, FAR, FAR],
-        out_specs=pl.BlockSpec((rows, TILE), lambda j: (0, j)),
-        out_shape=jax.ShapeDtypeStruct((rows, count), BF16),
-        scratch_shapes=buffers(depth),
-        compiler_params=params(20),
+        ahead_kernel,
+        in_specs=[FULL] * 4,
+        out_specs=FULL,
+        out_shape=jax.ShapeDtypeStruct((owns.shape[0] // 2, w0.shape[1]), BF16),
+        compiler_params=params(16),
         cost_estimate=CHEAP,
         name="project_ahead",
     )(owns, mates, w0, w1)
@@ -703,13 +702,13 @@
     return lax.ppermute(block, "seq", [(i, (i + distance) % size) for i in range(size)])
 
 
-def log_steps(info, got, keep, rates, done, pairs, scan_next):
+def log_steps(info, got, keep, rates_kept, done, pairs, scan_next):
     half = keep.shape[1]
     message = ((N + EXTRA, half), BF16)
     full = ((N, half), F32)
     msg, own, first, aux = combine(
         pair_kernel,
-        (info, got, keep, rates, done),
+        (info, got, keep, rates_kept, done),
         [SCALAR, FULL, FULL, FULL, ANY],
         [message, full, full, ((16, half), F32)],
         "pair",
@@ -767,17 +766,19 @@
     (bc_far,) = far(bc_input)
     halo = rotate(tail_rows(x_far, bc_far), 1)
     bc = bc_input.reshape(length, -1)
-    weight_mate = swap(out_weight, "head", 1)
-
-    cum, cum_s, log_s, f_dev, f_blk, e_blk, rates, by_row, ones = decays(info, log_decay, step_size, skip_gain, half)
+    (weight_mate,) = far(swap(out_weight, "head", 1))
+
+    (cum, cum_s, log_s, f_dev, f_blk, e_blk, rates), ones = decays(info, log_decay, step_size, skip_gain, half)
     taps = far(conv_weight_x, conv_weight_bc)
-    shared = (info, x_far, bc, halo, *taps, f_dev, ones, rates)
-    x0, bc0, send = conv_states(0, *shared)
+    shared = (info, x_far, bc, halo, *taps)
+    x0, bc0, send = conv_states(0, *shared, f_dev[0], ones, rates[0])
     got = swap(send, "seq", 1)
-    x1, bc1, keep = conv_states(1, *shared)
+    x1, bc1, keep = conv_states(1, *shared, f_dev[1], ones, rates[1])
+    rates_kept = rates[1]
 
     uvs = []
-    groups = [(x, z_far, y, cum, cum_s, log_s, f_blk, e_blk, by_row, ones) for x, y in zip(far(x0, x1), (bc0, bc1))]
+    xs, bcs = far(x0, x1), (bc0, bc1)
+    groups = [(x, z_far, *rest, ones) for x, *rest in zip(xs, bcs, cum, cum_s, log_s, f_blk, e_blk, rates)]
 
     def scan_next(token):
         if len(uvs) < 2 * B_PARTS:
@@ -794,7 +795,7 @@
         part = ((N + EXTRA, piece), BF16)
         first, aux, *parts = combine(
             pair_split_kernel,
-            (info, got, keep, rates, done),
+            (info, got, keep, rates_kept, done),
             [SCALAR, FULL, FULL, FULL, ANY],
             [full, ((8, half), F32)] + [part] * pairs,
             "pair",
@@ -822,7 +823,7 @@
             [pltpu.VMEM(*out)],
         )
     else:
-        back, held = log_steps(info, got, keep, rates, done, pairs, scan_next)
+        back, held = log_steps(info, got, keep, rates_kept, done, pairs, scan_next)
     other = swap(back, "seq", 1)
     while len(uvs) < 2 * B_PARTS:
         scan_next(back)
@@ -830,15 +831,14 @@
     count = length // ways
     gain = norm_gain[None, :]
 
-    def rows_for(token, *places):
-        return norm_rows(places, info, count, token, (bc0, bc1), (other, held), gain, uvs)
-
-    mates = rows_for(held, 0, 2)
-    owns = rows_for(mates, 1, 3)
-    operands = (owns, swap(mates, "head", 1), w_far, weight_mate)
     columns = out_weight.shape[1]
     chunk = columns // 8
-    first = swap(project_ahead(*operands, 0, chunk), "head", 2)
+    weights = (w_far, weight_mate)
+    shared = ((bc0, bc1), (other, held), gain, uvs)
+    (mates,) = norm_rows((0, 2), info, count, held, *shared)
+    owns, w0, w1 = norm_rows((1, 3), info, count, mates, *shared, weights, chunk)
+    operands = (owns, swap(mates, "head", 1), *weights)
+    first = swap(project_ahead(*operands[:2], w0, w1), "head", 2)
     calls = []
     for lo, hi in ((1, 2), (2, 4), (4, 6), (6, 8)):
         sent, near = project_both(*operands, lo * chunk, (hi - lo) * chunk, chunk)

time: 120 us -> 118 us (0.983)
  Pallas kernels: 82.6 us -> 81.2 us
    pallas_call x3, Pallas kernels: 8.11 us -> 6.58 us  [the longest x2 5.34 us: norm_rows(): pl.pallas_call(functools.partial(norm_kernel, places, len(weights)), in_s...]
  transfers between devices with their start and end apart: 19 -> 19, of which waited for: 7 -> 7; matrix products, arithmetic and copies ran while one was open for 0% -> 0% of each run, Pallas kernels for 66% -> 67%
where the time goes in v12:
time: 118 us
  Pallas kernels  81.2 us (69%)
  starting transfers between devices  20.8 us (18%)
  waiting for transfers between devices  15.3 us (13%)
    pallas_call x4, Pallas kernels, project_both(): pl.pallas_call(functools.partial(both_kernel, first // TILE, cut), grid=(...  25.5 us
    pallas_call x4, Pallas kernels, scan_part(): pl.pallas_call(functools.partial(scan_kernel, order, part), in_specs=[SCA...  21.5 us
    pallas_call x2, Pallas kernels, conv_states(): pl.pallas_call(functools.partial(conv_kernel, order), grid_spec=pltpu.Pre...  13.9 us
    ppermute x12, waiting for transfers between devices, swap(): lax.ppermute(block, axis, [(i, i ^ bit) for i in range(lax.axis_size(axis...  12.3 us
    ppermute x7, starting transfers between devices, rotate(): lax.ppermute(block, 'seq', [(i, (i + distance) % size) for i in range(siz...  11.5 us
    ppermute x12, starting transfers between devices, swap(): lax.ppermute(block, axis, [(i, i ^ bit) for i in range(lax.axis_size(axis...  9.3 us
    pallas_call x2, Pallas kernels, norm_rows(): pl.pallas_call(functools.partial(norm_kernel, places, len(weights)), in_s...  5.34 us
    pallas_call x5, Pallas kernels, add_chunks(): pl.pallas_call(add_kernel, grid=(1,), in_specs=[pl.BlockSpec((rows, count...  4.01 us
  transfers between devices with their start and end apart: 19, of which 7 were waited for; matrix products, arithmetic and copies ran while one was open for 0% of the time, Pallas kernels for 67%

profile of v12, /device:TPU:0, one launch (start us, length us, event | category | flops | bytes accessed | tf_op | source)
XLA Modules:
  0.0 117.9 jit_solution(13156942326230924237)
XLA Ops:
  1.3 2.7 %collective-permute-start = (bf16[16,2560]{1,0:T(8,128)(2,1)S(1)}, bf16[16,2560]{1,0:T(8,128)(2,1)S(1)}, u32[]{:S(2)}, u32[]{:S(2)}) collective-permute-start(bf16[16,2560]{1,0:T(8,128)(2,1)S(1)} %tail_rows.1), channel_id=1, source_target_pairs={{0,4},{4,8},{8,12},{12,16},{16,20},{20,24},{24,28},{28,0},{1,5},{5... | collective-permute-start | bytes 245768 | tf_op jit(solution)/shard_map/ppermute | solution.py:702
  4.1 2.7 %decays.1 = (f32[1024,16]{1,0:T(8,128)S(1)}, f32[1024,16]{1,0:T(8,128)S(1)}, f32[16,1024]{1,0:T(8,128)S(1)}, f32[16,1024]{1,0:T(8,128)S(1)}, f32[16,1024]{1,0:T(...) custom-call(s32[9]{0:T(128)S(1)} %stack.36.info, ...), custom_call_target="tpu_custom_call" | custom-call | flops 1 | bytes 1 | tf_op jit(solution)/shard_map/decays/pallas_call | solution.py:136
  7.1 3.0 %collective-permute-done.halo.bc_halo = bf16[16,2560]{1,0:T(8,128)(2,1)S(1)} collective-permute-done((bf16[16,2560]{1,0:T(8,128)(2,1)S(1)}, bf16[16,2560]{1,0:T(8,128)(2,1)S(1)}, u32[]{:S(2)}, u32[]{:S(2)}) %collective-permute-start) | collective-permute-done | bytes 81952 | tf_op jit(solution)/shard_map/ppermute | solution.py:702
  10.1 6.9 %conv_states.2 = (bf16[1024,1024]{1,0:T(8,128)(2,1)}, bf16[1024,256]{1,0:T(8,128)(2,1)S(1)}, bf16[144,1024]{1,0:T(8,128)(2,1)S(1)}) custom-call(s32[9]{0:T(128)S(1)} %stack.36.info, bf16[1024,2048]{1,0:T(8,128)(2,1)} %x_lead.3, bf16[1024,2048]{1,0:T(8,128)(2,1)} %x_lead.3, bf16[1024,512]{1,0:T(8,128)(2,1)S(1)} %bitcast.14, bf16[1024,512]{1,0:T(8,128)(2,1)S(1)} %bitcast.15, ...), custom_call_target="tpu_custom_call" | custom-call | flops 1 | bytes 1 | tf_op jit(solution)/shard_map/conv_states/pallas_call | solution.py:259
  17.0 6.9 %conv_states.3 = (bf16[1024,1024]{1,0:T(8,128)(2,1)}, bf16[1024,256]{1,0:T(8,128)(2,1)S(1)}, f32[128,1024]{1,0:T(8,128)S(1)}) custom-call(s32[9]{0:T(128)S(1)} %stack.36.info, bf16[1024,2048]{1,0:T(8,128)(2,1)} %x_lead.3, bf16[1024,2048]{1,0:T(8,128)(2,1)} %x_lead.3, bf16[1024,512]{1,0:T(8,128)(2,1)S(1)} %bitcast.16, bf16[1024,512]{1,0:T(8,128)(2,1)S(1)} %bitcast.17, ...), custom_call_target="tpu_custom_call" | custom-call | flops 1 | bytes 1 | tf_op jit(solution)/shard_map/conv_states/pallas_call | solution.py:259
  23.9 1.8 %collective-permute-done.1.got = bf16[144,1024]{1,0:T(8,128)(2,1)S(1)} collective-permute-done((bf16[144,1024]{1,0:T(8,128)(2,1)S(1)}, bf16[144,1024]{1,0:T(8,128)(2,1)S(1)}, u32[]{:S(2)}, u32[]{:S(2)}) %collective-permute-start.1) | collective-permute-done | bytes 294944 | tf_op jit(solution)/shard_map/ppermute | solution.py:697
  26.7 2.0 %collective-permute-start.3 = (bf16[144,256]{1,0:T(8,128)(2,1)S(1)}, bf16[144,256]{1,0:T(8,128)(2,1)S(1)}, u32[]{:S(2)}, u32[]{:S(2)}) collective-permute-start(bf16[144,256]{1,0:T(8,128)(2,1)S(1)} %get-tuple-element.71), channel_id=1, source_target_pairs={{0,16},{4,20},{8,24},{12,28},{16,0},{20,4},{24,8},{28,12},{1,17},{... | collective-permute-start | bytes 221192 | tf_op jit(solution)/shard_map/ppermute | solution.py:702
  28.7 1.8 %collective-permute-start.4 = (bf16[144,256]{1,0:T(8,128)(2,1)S(1)}, bf16[144,256]{1,0:T(8,128)(2,1)S(1)}, u32[]{:S(2)}, u32[]{:S(2)}) collective-permute-start(bf16[144,256]{1,0:T(8,128)(2,1)S(1)} %get-tuple-element.72), channel_id=1, source_target_pairs={{0,24},{4,28},{8,0},{12,4},{16,8},{20,12},{24,16},{28,20},{1,25},{... | collective-permute-start | bytes 221192 | tf_op jit(solution)/shard_map/ppermute | solution.py:702
  30.5 5.4 %scan_part.4._.refs_0_ = bf16[1024,1024]{1,0:T(8,128)(2,1)S(1)} custom-call(s32[9]{0:T(128)S(1)} %stack.36.info, bf16[1024,1024]{1,0:T(8,128)(2,1)} %get-tuple-element.73.x_far, bf16[1024,2048]{1,0:T(8,128)(2,1)} %z_far.7, bf16[1024,256]{1,0:T(8,128)(2,1)S(1)} %get-tuple-element.55.bc.bc0, f32[1024,16]{1,0:T(8,128)S(1)} %get-tuple-element.74.cum, ...), custom_call_target="tpu_custom_call" | custom-call | flops 1 | bytes 1 | tf_op jit(solution)/shard_map/scan_part/pallas_call | solution.py:481
  35.9 5.4 %scan_part.5.refs_4_.refs_1_ = bf16[1024,1024]{1,0:T(8,128)(2,1)S(1)} custom-call(s32[9]{0:T(128)S(1)} %stack.36.info, bf16[1024,1024]{1,0:T(8,128)(2,1)} %get-tuple-element.73.x_far, bf16[1024,2048]{1,0:T(8,128)(2,1)} %z_far.7, bf16[1024,256]{1,0:T(8,128)(2,1)S(1)} %get-tuple-element.55.bc.bc0, f32[1024,16]{1,0:T(8,128)S(1)} %get-tuple-element.74.cum, ...), custom_call_target="tpu_custom_call" | custom-call | flops 1 | bytes 1 | tf_op jit(solution)/shard_map/scan_part/pallas_call | solution.py:481
  42.6 1.5 %collective-permute-start.6 = (bf16[128,256]{1,0:T(8,128)(2,1)S(1)}, bf16[128,256]{1,0:T(8,128)(2,1)S(1)}, u32[]{:S(2)}, u32[]{:S(2)}) collective-permute-start(bf16[128,256]{1,0:T(8,128)(2,1)S(1)} %get-tuple-element.81), channel_id=1, source_target_pairs={{0,16},{4,20},{8,24},{12,28},{16,0},{20,4},{24,8},{28,12},{1,17},{... | collective-permute-start | bytes 196616 | tf_op jit(solution)/shard_map/ppermute | solution.py:702
  44.1 2.8 %collective-permute-start.7 = (bf16[128,256]{1,0:T(8,128)(2,1)S(1)}, bf16[128,256]{1,0:T(8,128)(2,1)S(1)}, u32[]{:S(2)}, u32[]{:S(2)}) collective-permute-start(bf16[128,256]{1,0:T(8,128)(2,1)S(1)} %get-tuple-element.82), channel_id=1, source_target_pairs={{0,24},{4,28},{8,0},{12,4},{16,8},{20,12},{24,16},{28,20},{1,25},{... | collective-permute-start | bytes 196616 | tf_op jit(solution)/shard_map/ppermute | solution.py:702
  47.0 5.4 %scan_part.6._.refs_2_ = bf16[1024,1024]{1,0:T(8,128)(2,1)S(1)} custom-call(s32[9]{0:T(128)S(1)} %stack.36.info, bf16[1024,1024]{1,0:T(8,128)(2,1)} %get-tuple-element.63.x_far, bf16[1024,2048]{1,0:T(8,128)(2,1)} %z_far.7, bf16[1024,256]{1,0:T(8,128)(2,1)S(1)} %get-tuple-element.58.bc.bc1, f32[1024,16]{1,0:T(8,128)S(1)} %get-tuple-element.64.cum, ...), custom_call_target="tpu_custom_call" | custom-call | flops 1 | bytes 1 | tf_op jit(solution)/shard_map/scan_part/pallas_call | solution.py:481
  53.6 5.4 %scan_part.7.refs_3_ = bf16[1024,1024]{1,0:T(8,128)(2,1)S(1)} custom-call(s32[9]{0:T(128)S(1)} %stack.36.info, bf16[1024,1024]{1,0:T(8,128)(2,1)} %get-tuple-element.63.x_far, bf16[1024,2048]{1,0:T(8,128)(2,1)} %z_far.7, bf16[1024,256]{1,0:T(8,128)(2,1)S(1)} %get-tuple-element.58.bc.bc1, f32[1024,16]{1,0:T(8,128)S(1)} %get-tuple-element.64.cum, ...), custom_call_target="tpu_custom_call" | custom-call | flops 1 | bytes 1 | tf_op jit(solution)/shard_map/scan_part/pallas_call | solution.py:481
  59.7 2.5 %norm_rows.2._ = bf16[512,2048]{1,0:T(8,128)(2,1)S(1)} custom-call(s32[9]{0:T(128)S(1)} %stack.36.info, bf16[1024,256]{1,0:T(8,128)(2,1)S(1)} %get-tuple-element.55.bc.bc0, bf16[1024,256]{1,0:T(8,128)(2,1)S(1)} %get-tuple-element.58.bc.bc1, bf16[128,1024]{1,0:T(8,128)(2,1)S(1)} %collective-permute-done.8.state0, ...), custom_call_target="tpu_custom_call" | custom-call | flops 1 | bytes 1 | tf_op jit(solution)/shard_map/norm_rows/pallas_call | solution.py:543
  62.3 2.8 %norm_rows.3 = (bf16[512,2048]{1,0:T(8,128)(2,1)S(1)}, bf16[2048,512]{1,0:T(8,128)(2,1)S(1)}, bf16[2048,512]{1,0:T(8,128)(2,1)S(1)}) custom-call(s32[9]{0:T(128)S(1)} %stack.36.info, bf16[1024,256]{1,0:T(8,128)(2,1)S(1)} %get-tuple-element.55.bc.bc0, bf16[1024,256]{1,0:T(8,128)(2,1)S(1)} %get-tuple-element.58.bc.bc1, ...), custom_call_target="tpu_custom_call" | custom-call | flops 1 | bytes 1 | tf_op jit(solution)/shard_map/norm_rows/pallas_call | solution.py:543
  67.7 1.5 %collective-permute-start.18 = (bf16[256,512]{1,0:T(8,128)(2,1)S(1)}, bf16[256,512]{1,0:T(8,128)(2,1)S(1)}, u32[]{:S(2)}, u32[]{:S(2)}) collective-permute-start(bf16[256,512]{1,0:T(8,128)(2,1)S(1)} %project_ahead.1), channel_id=1, source_target_pairs={{0,2},{1,3},{2,0},{3,1},{4,6},{5,7},{6,4},{7,5},{8,10},{9,11},{10,... | collective-permute-start | bytes 786440 | tf_op jit(solution)/shard_map/ppermute | solution.py:697
  69.2 4.3 %project_both.7 = (bf16[256,512]{1,0:T(8,128)(2,1)S(1)}, f32[256,512]{1,0:T(8,128)S(1)}) custom-call(bf16[512,2048]{1,0:T(8,128)(2,1)S(1)} %get-tuple-element.85.owns, bf16[512,2048]{1,0:T(8,128)(2,1)S(1)} %collective-permute-done.10.mates, bf16[2048,4096]{1,0:T(8,128)(2,1)} %w0_far.9, bf16[2048,4096]{1,0:T(8,128)(2,1)} %collective-permute-done.9.refs_5_.w1_far), custom_call_target="tpu_custom_call" | custom-call | flops 1 | bytes 1 | tf_op jit(solution)/shard_map/project_both/pallas_call | solution.py:630
  74.1 7.1 %project_both.6 = (bf16[256,512]{1,0:T(8,128)(2,1)S(1)}, bf16[256,512]{1,0:T(8,128)(2,1)S(1)}, f32[256,1024]{1,0:T(8,128)S(1)}) custom-call(bf16[512,2048]{1,0:T(8,128)(2,1)S(1)} %get-tuple-element.85.owns, bf16[512,2048]{1,0:T(8,128)(2,1)S(1)} %collective-permute-done.10.mates, bf16[2048,4096]{1,0:T(8,128)(2,1)} %w0_far.9, ...), custom_call_target="tpu_custom_call" | custom-call | flops 1 | bytes 1 | tf_op jit(solution)/shard_map/project_both/pallas_call | solution.py:630
  83.3 7.1 %project_both.5 = (bf16[256,512]{1,0:T(8,128)(2,1)S(1)}, bf16[256,512]{1,0:T(8,128)(2,1)S(1)}, f32[256,1024]{1,0:T(8,128)S(1)}) custom-call(bf16[512,2048]{1,0:T(8,128)(2,1)S(1)} %get-tuple-element.85.owns, bf16[512,2048]{1,0:T(8,128)(2,1)S(1)} %collective-permute-done.10.mates, bf16[2048,4096]{1,0:T(8,128)(2,1)} %w0_far.9, ...), custom_call_target="tpu_custom_call" | custom-call | flops 1 | bytes 1 | tf_op jit(solution)/shard_map/project_both/pallas_call | solution.py:630
  91.9 7.1 %project_both.4 = (bf16[256,512]{1,0:T(8,128)(2,1)S(1)}, bf16[256,512]{1,0:T(8,128)(2,1)S(1)}, f32[256,1024]{1,0:T(8,128)S(1)}) custom-call(bf16[512,2048]{1,0:T(8,128)(2,1)S(1)} %get-tuple-element.85.owns, bf16[512,2048]{1,0:T(8,128)(2,1)S(1)} %collective-permute-done.10.mates, bf16[2048,4096]{1,0:T(8,128)(2,1)} %w0_far.9, ...), custom_call_target="tpu_custom_call" | custom-call | flops 1 | bytes 1 | tf_op jit(solution)/shard_map/project_both/pallas_call | solution.py:630
  101.7 3.8 %project_near.1.refs_1_ = bf16[256,4096]{1,0:T(8,128)(2,1)} custom-call(bf16[512,2048]{1,0:T(8,128)(2,1)S(1)} %get-tuple-element.85.owns, bf16[512,2048]{1,0:T(8,128)(2,1)S(1)} %collective-permute-done.10.mates, bf16[2048,4096]{1,0:T(8,128)(2,1)} %w0_far.9, bf16[2048,4096]{1,0:T(8,128)(2,1)} %collective-permute-done.9.refs_5_.w1_far, ...), custom_call_target="tpu_custom_call" | custom-call | flops 1 | bytes 1 | tf_op jit(solution)/shard_map/project_near/pallas_call | solution.py:654
  109.1 4.7 %collective-permute-done.12.refs_0_ = bf16[256,512]{1,0:T(8,128)(2,1)S(1)} collective-permute-done((bf16[256,512]{1,0:T(8,128)(2,1)S(1)}, bf16[256,512]{1,0:T(8,128)(2,1)S(1)}, u32[]{:S(2)}, u32[]{:S(2)}) %collective-permute-start.12) | collective-permute-done | bytes 262176 | tf_op jit(solution)/shard_map/ppermute | solution.py:697
  114.6 2.6 %collective-permute-done.11.refs_0_ = bf16[256,512]{1,0:T(8,128)(2,1)S(1)} collective-permute-done((bf16[256,512]{1,0:T(8,128)(2,1)S(1)}, bf16[256,512]{1,0:T(8,128)(2,1)S(1)}, u32[]{:S(2)}, u32[]{:S(2)}) %collective-permute-start.11) | collective-permute-done | bytes 262176 | tf_op jit(solution)/shard_map/ppermute | solution.py:697
  (44 shorter events, 20.4 us)
Async XLA Ops:
  0.0 6.8 %copy-start.1 = (bf16[1024,2,256]{2,1,0:T(2,128)(2,1)S(1)}, bf16[1024,2,256]{2,1,0:T(2,128)(2,1)}, u32[]{:S(2)}) copy-start(bf16[1024,2,256]{2,1,0:T(2,128)(2,1)} %bc.1) | copy-start | bytes 3145732
  0.0 62.3 %collective-permute-start.9 = (bf16[2048,4096]{1,0:T(8,128)(2,1)}, bf16[2048,4096]{1,0:T(8,128)(2,1)}, u32[]{:S(2)}, u32[]{:S(2)}) collective-permute-start(bf16[2048,4096]{1,0:T(8,128)(2,1)} %w0_far.9), channel_id=1, source_target_pairs={{0,1},{1,0},{2,3},{3,2},{4,5},{5,4},{6,7},{7,6},{8,9},{9,8},{10,11... | collective-permute-start | bytes 50331656 | tf_op jit(solution)/shard_map/ppermute | solution.py:697
  1.3 8.7 %collective-permute-start = (bf16[16,2560]{1,0:T(8,128)(2,1)S(1)}, bf16[16,2560]{1,0:T(8,128)(2,1)S(1)}, u32[]{:S(2)}, u32[]{:S(2)}) collective-permute-start(bf16[16,2560]{1,0:T(8,128)(2,1)S(1)} %tail_rows.1), channel_id=1, source_target_pairs={{0,4},{4,8},{8,12},{12,16},{16,20},{20,24},{24,28},{28,0},{1,5},{5... | collective-permute-start | bytes 245768 | tf_op jit(solution)/shard_map/ppermute | solution.py:702
  17.0 8.8 %collective-permute-start.1 = (bf16[144,1024]{1,0:T(8,128)(2,1)S(1)}, bf16[144,1024]{1,0:T(8,128)(2,1)S(1)}, u32[]{:S(2)}, u32[]{:S(2)}) collective-permute-start(bf16[144,1024]{1,0:T(8,128)(2,1)S(1)} %get-tuple-element.59), channel_id=1, source_target_pairs={{0,4},{4,0},{8,12},{12,8},{16,20},{20,16},{24,28},{28,24},{1,5},{5... | collective-permute-start | bytes 884744 | tf_op jit(solution)/shard_map/ppermute | solution.py:697
  26.6 14.7 %collective-permute-start.2 = (bf16[144,256]{1,0:T(8,128)(2,1)S(1)}, bf16[144,256]{1,0:T(8,128)(2,1)S(1)}, u32[]{:S(2)}, u32[]{:S(2)}) collective-permute-start(bf16[144,256]{1,0:T(8,128)(2,1)S(1)} %get-tuple-element.70), channel_id=1, source_target_pairs={{0,8},{4,12},{8,16},{12,20},{16,24},{20,28},{24,0},{28,4},{1,9},{5... | collective-permute-start | bytes 221192 | tf_op jit(solution)/shard_map/ppermute | solution.py:702
  26.7 14.6 %collective-permute-start.3 = (bf16[144,256]{1,0:T(8,128)(2,1)S(1)}, bf16[144,256]{1,0:T(8,128)(2,1)S(1)}, u32[]{:S(2)}, u32[]{:S(2)}) collective-permute-start(bf16[144,256]{1,0:T(8,128)(2,1)S(1)} %get-tuple-element.71), channel_id=1, source_target_pairs={{0,16},{4,20},{8,24},{12,28},{16,0},{20,4},{24,8},{28,12},{1,17},{... | collective-permute-start | bytes 221192 | tf_op jit(solution)/shard_map/ppermute | solution.py:702
  28.7 12.6 %collective-permute-start.4 = (bf16[144,256]{1,0:T(8,128)(2,1)S(1)}, bf16[144,256]{1,0:T(8,128)(2,1)S(1)}, u32[]{:S(2)}, u32[]{:S(2)}) collective-permute-start(bf16[144,256]{1,0:T(8,128)(2,1)S(1)} %get-tuple-element.72), channel_id=1, source_target_pairs={{0,24},{4,28},{8,0},{12,4},{16,8},{20,12},{24,16},{28,20},{1,25},{... | collective-permute-start | bytes 221192 | tf_op jit(solution)/shard_map/ppermute | solution.py:702
  42.0 10.4 %collective-permute-start.5 = (bf16[128,256]{1,0:T(8,128)(2,1)S(1)}, bf16[128,256]{1,0:T(8,128)(2,1)S(1)}, u32[]{:S(2)}, u32[]{:S(2)}) collective-permute-start(bf16[128,256]{1,0:T(8,128)(2,1)S(1)} %get-tuple-element.80), channel_id=1, source_target_pairs={{0,8},{4,12},{8,16},{12,20},{16,24},{20,28},{24,0},{28,4},{1,9},{5... | collective-permute-start | bytes 196616 | tf_op jit(solution)/shard_map/ppermute | solution.py:702
  42.6 9.8 %collective-permute-start.6 = (bf16[128,256]{1,0:T(8,128)(2,1)S(1)}, bf16[128,256]{1,0:T(8,128)(2,1)S(1)}, u32[]{:S(2)}, u32[]{:S(2)}) collective-permute-start(bf16[128,256]{1,0:T(8,128)(2,1)S(1)} %get-tuple-element.81), channel_id=1, source_target_pairs={{0,16},{4,20},{8,24},{12,28},{16,0},{20,4},{24,8},{28,12},{1,17},{... | collective-permute-start | bytes 196616 | tf_op jit(solution)/shard_map/ppermute | solution.py:702
  44.1 8.3 %collective-permute-start.7 = (bf16[128,256]{1,0:T(8,128)(2,1)S(1)}, bf16[128,256]{1,0:T(8,128)(2,1)S(1)}, u32[]{:S(2)}, u32[]{:S(2)}) collective-permute-start(bf16[128,256]{1,0:T(8,128)(2,1)S(1)} %get-tuple-element.82), channel_id=1, source_target_pairs={{0,24},{4,28},{8,0},{12,4},{16,8},{20,12},{24,16},{28,20},{1,25},{... | collective-permute-start | bytes 196616 | tf_op jit(solution)/shard_map/ppermute | solution.py:702
  53.2 6.5 %copy-start = (f32[2048]{0:T(1024)S(1)}, f32[2048]{0:T(1024)}, u32[]{:S(2)}) copy-start(f32[2048]{0:T(1024)} %param.18) | copy-start | bytes 24580
  53.2 6.4 %collective-permute-start.8 = (bf16[128,1024]{1,0:T(8,128)(2,1)S(1)}, bf16[128,1024]{1,0:T(8,128)(2,1)S(1)}, u32[]{:S(2)}, u32[]{:S(2)}) collective-permute-start(bf16[128,1024]{1,0:T(8,128)(2,1)S(1)} %get-tuple-element.83._), channel_id=1, source_target_pairs={{0,4},{4,0},{8,12},{12,8},{16,20},{20,16},{24,28},{28,24},{1,5},{5... | collective-permute-start | bytes 786440 | tf_op jit(solution)/shard_map/ppermute | solution.py:697
  62.2 4.2 %collective-permute-start.10 = (bf16[512,2048]{1,0:T(8,128)(2,1)S(1)}, bf16[512,2048]{1,0:T(8,128)(2,1)S(1)}, u32[]{:S(2)}, u32[]{:S(2)}) collective-permute-start(bf16[512,2048]{1,0:T(8,128)(2,1)S(1)} %norm_rows.2._), channel_id=1, source_target_pairs={{0,1},{1,0},{2,3},{3,2},{4,5},{5,4},{6,7},{7,6},{8,9},{9,8},{10,11... | collective-permute-start | bytes 6291464 | tf_op jit(solution)/shard_map/ppermute | solution.py:697
  67.7 31.3 %collective-permute-start.18 = (bf16[256,512]{1,0:T(8,128)(2,1)S(1)}, bf16[256,512]{1,0:T(8,128)(2,1)S(1)}, u32[]{:S(2)}, u32[]{:S(2)}) collective-permute-start(bf16[256,512]{1,0:T(8,128)(2,1)S(1)} %project_ahead.1), channel_id=1, source_target_pairs={{0,2},{1,3},{2,0},{3,1},{4,6},{5,7},{6,4},{7,5},{8,10},{9,11},{10,... | collective-permute-start | bytes 786440 | tf_op jit(solution)/shard_map/ppermute | solution.py:697
  73.4 26.2 %collective-permute-start.17 = (bf16[256,512]{1,0:T(8,128)(2,1)S(1)}, bf16[256,512]{1,0:T(8,128)(2,1)S(1)}, u32[]{:S(2)}, u32[]{:S(2)}) collective-permute-start(bf16[256,512]{1,0:T(8,128)(2,1)S(1)} %get-tuple-element.96), channel_id=1, source_target_pairs={{0,2},{1,3},{2,0},{3,1},{4,6},{5,7},{6,4},{7,5},{8,10},{9,11},{10,... | collective-permute-start | bytes 786440 | tf_op jit(solution)/shard_map/ppermute | solution.py:697
  81.2 19.8 %collective-permute-start.15 = (bf16[256,512]{1,0:T(8,128)(2,1)S(1)}, bf16[256,512]{1,0:T(8,128)(2,1)S(1)}, u32[]{:S(2)}, u32[]{:S(2)}) collective-permute-start(bf16[256,512]{1,0:T(8,128)(2,1)S(1)} %get-tuple-element.93), channel_id=1, source_target_pairs={{0,2},{1,3},{2,0},{3,1},{4,6},{5,7},{6,4},{7,5},{8,10},{9,11},{10,... | collective-permute-start | bytes 786440 | tf_op jit(solution)/shard_map/ppermute | solution.py:697
  82.7 23.6 %collective-permute-start.16 = (bf16[256,512]{1,0:T(8,128)(2,1)S(1)}, bf16[256,512]{1,0:T(8,128)(2,1)S(1)}, u32[]{:S(2)}, u32[]{:S(2)}) collective-permute-start(bf16[256,512]{1,0:T(8,128)(2,1)S(1)} %get-tuple-element.94), channel_id=1, source_target_pairs={{0,2},{1,3},{2,0},{3,1},{4,6},{5,7},{6,4},{7,5},{8,10},{9,11},{10,... | collective-permute-start | bytes 786440 | tf_op jit(solution)/shard_map/ppermute | solution.py:697
  90.4 16.8 %collective-permute-start.13 = (bf16[256,512]{1,0:T(8,128)(2,1)S(1)}, bf16[256,512]{1,0:T(8,128)(2,1)S(1)}, u32[]{:S(2)}, u32[]{:S(2)}) collective-permute-start(bf16[256,512]{1,0:T(8,128)(2,1)S(1)} %get-tuple-element.90), channel_id=1, source_target_pairs={{0,2},{1,3},{2,0},{3,1},{4,6},{5,7},{6,4},{7,5},{8,10},{9,11},{10,... | collective-permute-start | bytes 786440 | tf_op jit(solution)/shard_map/ppermute | solution.py:697
  98.9 9.3 %collective-permute-start.14 = (bf16[256,512]{1,0:T(8,128)(2,1)S(1)}, bf16[256,512]{1,0:T(8,128)(2,1)S(1)}, u32[]{:S(2)}, u32[]{:S(2)}) collective-permute-start(bf16[256,512]{1,0:T(8,128)(2,1)S(1)} %get-tuple-element.91), channel_id=1, source_target_pairs={{0,2},{1,3},{2,0},{3,1},{4,6},{5,7},{6,4},{7,5},{8,10},{9,11},{10,... | collective-permute-start | bytes 786440 | tf_op jit(solution)/shard_map/ppermute | solution.py:697
  99.6 14.2 %collective-permute-start.12 = (bf16[256,512]{1,0:T(8,128)(2,1)S(1)}, bf16[256,512]{1,0:T(8,128)(2,1)S(1)}, u32[]{:S(2)}, u32[]{:S(2)}) collective-permute-start(bf16[256,512]{1,0:T(8,128)(2,1)S(1)} %get-tuple-element.88), channel_id=1, source_target_pairs={{0,2},{1,3},{2,0},{3,1},{4,6},{5,7},{6,4},{7,5},{8,10},{9,11},{10,... | collective-permute-start | bytes 786440 | tf_op jit(solution)/shard_map/ppermute | solution.py:697
  101.0 16.2 %collective-permute-start.11 = (bf16[256,512]{1,0:T(8,128)(2,1)S(1)}, bf16[256,512]{1,0:T(8,128)(2,1)S(1)}, u32[]{:S(2)}, u32[]{:S(2)}) collective-permute-start(bf16[256,512]{1,0:T(8,128)(2,1)S(1)} %get-tuple-element.87), channel_id=1, source_target_pairs={{0,2},{1,3},{2,0},{3,1},{4,6},{5,7},{6,4},{7,5},{8,10},{9,11},{10,... | collective-permute-start | bytes 786440 | tf_op jit(solution)/shard_map/ppermute | solution.py:697

commit v13 on v12

--- a/solution.py
+++ b/solution.py
@@ -58,9 +58,11 @@
     return pl.BlockSpec(shape, lambda *_: (0,) * len(shape))
 
 
-def decay_kernel(info, ld_t, step_t, skip, *refs):
+def decay_kernel(info, ld_t, step_t, skip, x_far, *refs):
     cum, cum_s, log_s, f_dev, f_blk, e_blk, rates = [refs[2 * k : 2 * k + 2] for k in range(7)]
-    ones = refs[14]
+    ones, x, sem = refs[14:]
+    copy = pltpu.make_async_copy(x_far, x, sem)
+    copy.start()
     heads, length = ld_t.shape
     blocks = length // TOK_B
     per = heads // 2
@@ -121,9 +123,10 @@
         put(f_dev, rows, jnp.exp2(total - (cums[b] + before[b])) * s)
         put(f_blk, rows, jnp.exp2(totals[b] - cums[b]) * s)
         put(e_blk, rows, jnp.exp2(cums[b]))
-
-
-def decays(info, log_decay, step, skip, width):
+    copy.wait()
+
+
+def decays(info, log_decay, step, skip, x, width):
     length, heads = log_decay.shape
     blocks = length // TOK_B
     per = heads // 2
@@ -132,17 +135,18 @@
     column = jax.ShapeDtypeStruct((length, per), F32)
     rates = jax.ShapeDtypeStruct((2 * blocks + 16, width), F32)
     shapes = [shape for shape in (column, across, across, pair, pair, pair, rates) for _ in range(2)]
-    shapes.append(jax.ShapeDtypeStruct((2 * per, width), BF16))
-    *refs, ones = pl.pallas_call(
+    shapes += [jax.ShapeDtypeStruct((2 * per, width), BF16), pltpu.VMEM(x.shape, BF16)]
+    *refs, ones, x_near = pl.pallas_call(
         decay_kernel,
-        in_specs=[SCALAR] + [FULL] * 3,
+        in_specs=[SCALAR] + [FULL] * 3 + [FAR],
         out_specs=[FULL] * len(shapes),
         out_shape=shapes,
+        scratch_shapes=[pltpu.SemaphoreType.DMA],
         compiler_params=params(16),
         cost_estimate=CHEAP,
         name="decays",
-    )(info, *far(log_decay.T, step.T, skip[None, :]))
-    return [tuple(refs[2 * k : 2 * k + 2]) for k in range(7)], ones
+    )(info, *far(log_decay.T, step.T, skip[None, :], x))
+    return [tuple(refs[2 * k : 2 * k + 2]) for k in range(7)], ones, x_near
 
 
 def tail_kernel(x, bc, out):
@@ -185,21 +189,24 @@
     return ref[0:N, :].astype(F32), extra[0:1] + extra[1:2]
 
 
-def conv_kernel(
-    order, info, x, x_lead, bc, bc_lead, halo, bc_halo, wx, wbc, f_dev, ones, rates, x_out, bc_out, final, xf, state, down
-):
-    i = pl.program_id(0)
-    rows, width = x.shape
+def conv_kernel(order, info, x, bc, halo, wx, wbc, f_dev, ones, rates, *refs):
+    z_far, refs = (None, refs) if order == 0 else (refs[0], refs[1:])
+    x_out, bc_out, final = refs[:3]
+    xf, state, down = refs[-3:]
+    length, width = x_out.shape
+    rows = TOK_A
     group = info[GROUP + order]
-
-    @pl.when(i == 0)
-    def _():
-        state[...] = jnp.zeros_like(state)
-        row = lax.broadcasted_iota(jnp.int32, down.shape, 0)
-        col = lax.broadcasted_iota(jnp.int32, down.shape, 1)
-        down[...] = (row == col + 1).astype(BF16)
-
-    def conv(src, first, behind, weights, emit):
+    first_lane = pl.multiple_of(group * width, width)
+    first_bc = pl.multiple_of(group * 2 * N, 2 * N)
+    if z_far is not None:
+        fetch = pltpu.make_async_copy(z_far, refs[3], refs[4])
+        fetch.start()
+    state[...] = jnp.zeros_like(state)
+    row = lax.broadcasted_iota(jnp.int32, down.shape, 0)
+    col = lax.broadcasted_iota(jnp.int32, down.shape, 1)
+    down[...] = (row == col + 1).astype(BF16)
+
+    def conv(i, src, first, behind, weights, emit):
         at_start = jnp.where(info[SEQ] == 0, jnp.zeros_like(first), first)
         lead = jnp.where(i == 0, at_start, behind).astype(F32)
         w0, w1, w2, w3 = [w * 0.5 for w in weights]
@@ -217,83 +224,74 @@
             emit(r, half_silu((w3 * cur + w2 * r1) + p2))
             last_p = p[ROWS_A - 8 :]
 
-    for lanes in range(0, 2 * N, SLAB):
-        ds = slice(lanes, lanes + SLAB)
-
-        def emit_bc(r, value):
-            bc_out[r : r + ROWS_A, ds] = value.astype(BF16)
-
-        weights = [jnp.where(group == 0, wbc[k, 0:1, ds], wbc[k, 1:2, ds]) for k in range(KCONV)]
-        conv(bc[:, ds], bc_halo[:, ds], bc_lead[:, ds], weights, emit_bc)
-
-    for lanes in range(0, width, SLAB):
-        ds = slice(lanes, lanes + SLAB)
-        scale = dot(f_dev[...], ones[:, ds])
-
-        def emit(r, value):
-            x_out[r : r + ROWS_A, ds] = value.astype(BF16)
-            xf[r : r + ROWS_A, ds] = (value * scale[r : r + ROWS_A]).astype(BF16)
-
-        weights = [wx[k : k + 1, ds] for k in range(KCONV)]
-        conv(x[:, ds], halo[:, ds], x_lead[:, ds], weights, emit)
-
-    state[...] += dot(bc_out[:, 0:N], xf[...], ((0,), (0,)))
-
-    @pl.when(i == pl.num_programs(0) - 1)
-    def _():
-        if order == 0:
-            row = rates.shape[0] - 16
-            put_message(final, state[...], rates[row : row + 1, :])
-        else:
-            final[...] = state[...]
-
-
-def conv_states(order, info, x, bc, halo, wx, wbc, f_dev, ones, rates):
+    def step(i, _):
+        at = pl.ds(pl.multiple_of(i * rows, rows), rows)
+        behind = pl.ds(pl.multiple_of(jnp.maximum(i * rows - LEAD, 0), LEAD), LEAD)
+
+        def out(r):
+            return pl.ds(pl.multiple_of(i * rows + r, ROWS_A), ROWS_A)
+
+        for lanes in range(0, 2 * N, SLAB):
+            ds = slice(lanes, lanes + SLAB)
+            src = pl.ds(pl.multiple_of(first_bc + lanes, SLAB), SLAB)
+            halo_src = pl.ds(pl.multiple_of(x.shape[1] + first_bc + lanes, SLAB), SLAB)
+
+            def emit_bc(r, value):
+                bc_out[out(r), ds] = value.astype(BF16)
+
+            weights = [jnp.where(group == 0, wbc[k, 0:1, ds], wbc[k, 1:2, ds]) for k in range(KCONV)]
+            conv(i, bc[at, src], halo[:, halo_src], bc[behind, src], weights, emit_bc)
+
+        for lanes in range(0, width, SLAB):
+            ds = slice(lanes, lanes + SLAB)
+            src = pl.ds(pl.multiple_of(first_lane + lanes, SLAB), SLAB)
+            scale = dot(f_dev[at, :], ones[:, ds])
+
+            def emit(r, value):
+                x_out[out(r), ds] = value.astype(BF16)
+                xf[r : r + ROWS_A, ds] = (value * scale[r : r + ROWS_A]).astype(BF16)
+
+            weights = [wx[k : k + 1, ds] for k in range(KCONV)]
+            conv(i, x[at, src], halo[:, src], x[behind, src], weights, emit)
+
+        state[...] += dot(bc_out[at, 0:N], xf[...], ((0,), (0,)))
+        return 0
+
+    lax.fori_loop(0, length // rows, step, 0)
+    if order == 0:
+        row = rates.shape[0] - 16
+        put_message(final, state[...], rates[row : row + 1, :])
+    else:
+        final[...] = state[...]
+        fetch.wait()
+
+
+def conv_states(order, info, x, bc, halo, wx, wbc, f_dev, ones, rates, z=None):
     length, full = x.shape
     width = full // 2
-    lead = lambda i, info: (jnp.maximum(i * (TOK_A // LEAD) - 1, 0), info[GROUP + order])
-    block = lambda i, info: (i, info[GROUP + order])
     column = lambda i, info: (0, info[GROUP + order])
-    rows = lambda i, info: (i, 0)
     final = ((N + EXTRA, width), BF16) if order == 0 else ((N, width), F32)
+    more = [] if z is None else [z]
     return pl.pallas_call(
         functools.partial(conv_kernel, order),
         grid_spec=pltpu.PrefetchScalarGridSpec(
             num_scalar_prefetch=1,
-            grid=(length // TOK_A,),
-            in_specs=[
-                pl.BlockSpec((TOK_A, width), block),
-                pl.BlockSpec((LEAD, width), lead),
-                pl.BlockSpec((TOK_A, 2 * N), block),
-                pl.BlockSpec((LEAD, 2 * N), lead),
-                pl.BlockSpec((LEAD, width), column),
-                pl.BlockSpec((LEAD, 2 * N), lambda i, info: (0, full // (2 * N) + info[GROUP + order])),
-                pl.BlockSpec((KCONV, width), column),
-                whole(wbc.shape),
-                pl.BlockSpec((TOK_A, f_dev.shape[1]), rows),
-                whole(ones.shape),
-                whole(rates.shape),
-            ],
-            out_specs=[
-                pl.BlockSpec((TOK_A, width), rows),
-                pl.BlockSpec((TOK_A, 2 * N), rows),
-                whole(final[0]),
-            ],
-            scratch_shapes=[
-                pltpu.VMEM((TOK_A, width), BF16),
-                pltpu.VMEM((N, width), F32),
-                pltpu.VMEM((TOK_A, TOK_A), BF16),
-            ],
+            grid=(1,),
+            in_specs=[FULL] * 3 + [pl.BlockSpec((KCONV, width), column)] + [FULL] * 4 + [FAR] * len(more),
+            out_specs=[FULL] * (3 + len(more)),
+            scratch_shapes=[pltpu.SemaphoreType.DMA] * len(more)
+            + [pltpu.VMEM((TOK_A, width), BF16), pltpu.VMEM((N, width), F32), pltpu.VMEM((TOK_A, TOK_A), BF16)],
         ),
-        out_shape=(
-            pltpu.HBM((length, width), BF16),
-            jax.ShapeDtypeStruct((length, 2 * N), BF16),
+        out_shape=[
+            pltpu.VMEM((length, width), BF16),
+            pltpu.VMEM((length, 2 * N), BF16),
             jax.ShapeDtypeStruct(*final),
-        ),
+        ]
+        + [pltpu.VMEM(a.shape, BF16) for a in more],
         compiler_params=params(16),
         cost_estimate=CHEAP,
         name="conv_states",
-    )(info, x, x, bc, bc, halo, halo, wx, wbc, f_dev, ones, rates)
+    )(info, x, bc, halo, wx, wbc, f_dev, ones, rates, *more)
 
 
 def pair_kernel(info, got, keep, rates, _, msg, own, first, aux):
@@ -400,26 +398,14 @@
     )(*operands)
 
 
-def scan_kernel(order, part, info, x_far, z_far, bc, cum, cum_s, log_s, f_blk, e_blk, rates, ones, _, uv_out, x, z, sem, state):
-    length, width = x.shape
+def scan_kernel(order, part, info, x, z, bc, cum, cum_s, log_s, f_blk, e_blk, rates, ones, _, uv_out, state):
+    length = x.shape[0]
+    width = state.shape[1]
     per_slab = SLAB // P_SIZE
     inner = STEP_B // TOK_B
     blocks = length // TOK_B
     first_head = part * width // P_SIZE
-    first_lane = info[GROUP + order] * x_far.shape[1] + part * width
-
-    def fetch(step):
-        piece = pl.ds(pl.multiple_of(step * STEP_B, STEP_B), STEP_B)
-        return (
-            pltpu.make_async_copy(x_far.at[piece, pl.ds(part * width, width)], x.at[piece], sem.at[0, step]),
-            pltpu.make_async_copy(
-                z_far.at[piece, pl.ds(pl.multiple_of(first_lane, width), width)], z.at[piece], sem.at[1, step]
-            ),
-        )
-
-    for step in range(length // STEP_B):
-        for copy in fetch(step):
-            copy.start()
+    first_lane = info[GROUP + order] * x.shape[1] + part * width
     state[...] = jnp.zeros_like(state)
 
     row = lax.broadcasted_iota(jnp.int32, (TOK_B, TOK_B), 0)
@@ -429,8 +415,6 @@
     zero = jnp.zeros((TOK_B, 2 * P_SIZE), BF16)
 
     def turn(step, _):
-        for copy in fetch(step):
-            copy.wait()
         for k in range(inner):
             block(step * inner + k)
         return 0
@@ -443,7 +427,7 @@
         scores = jnp.where(keep, dot(c_mat, b_mat, ((1,), (1,))), 0.0)
         for s in range(width // SLAB):
             lanes = slice(s * SLAB, (s + 1) * SLAB)
-            xb = x[at, lanes]
+            xb = x[at, part * width + s * SLAB : part * width + (s + 1) * SLAB]
             wide = slice(part * width + s * SLAB, part * width + (s + 1) * SLAB)
             sel = ones[:, wide]
             fade_row = rates[pl.ds(b, 1), wide]
@@ -466,7 +450,7 @@
                 within.append(dot(jnp.concatenate(tables, 1), stacked))
             xs = xb.astype(F32)
             y = jnp.concatenate(within, 1) + carried + skip * xs
-            gate = half_silu((z[at, lanes] * 0.5).astype(F32))
+            gate = half_silu((z[at, pl.ds(pl.multiple_of(first_lane + s * SLAB, SLAB), SLAB)] * 0.5).astype(F32))
             uv_out[at, lanes] = (y * gate).astype(BF16)
             uv_out[at, width + s * SLAB : width + (s + 1) * SLAB] = (gate * rise * lead_row).astype(BF16)
             xf = (xs * dot(f_blk[at, :], sel)).astype(BF16)
@@ -480,16 +464,11 @@
     width = full // B_PARTS
     return pl.pallas_call(
         functools.partial(scan_kernel, order, part),
-        in_specs=[SCALAR, FAR, FAR] + [FULL] * 8 + [ANY],
+        in_specs=[SCALAR] + [FULL] * 10 + [ANY],
         out_specs=FULL,
-        out_shape=jax.ShapeDtypeStruct((length, 2 * width), BF16),
-        scratch_shapes=[
-            pltpu.VMEM((length, width), BF16),
-            pltpu.VMEM((length, width), BF16),
-            pltpu.SemaphoreType.DMA((2, length // STEP_B)),
-            pltpu.VMEM((N, width), F32),
-        ],
-        compiler_params=params(16),
+        out_shape=pltpu.VMEM((length, 2 * width), BF16),
+        scratch_shapes=[pltpu.VMEM((N, width), F32)],
+        compiler_params=params(12),
         cost_estimate=CHEAP,
         name="scan_part",
     )(info, x, z, bc, cum, cum_s, log_s, f_blk, e_blk, rates, ones, token)
@@ -768,17 +747,18 @@
     bc = bc_input.reshape(length, -1)
     (weight_mate,) = far(swap(out_weight, "head", 1))
 
-    (cum, cum_s, log_s, f_dev, f_blk, e_blk, rates), ones = decays(info, log_decay, step_size, skip_gain, half)
+    (cum, cum_s, log_s, f_dev, f_blk, e_blk, rates), ones, x_near = decays(
+        info, log_decay, step_size, skip_gain, x_input, half
+    )
     taps = far(conv_weight_x, conv_weight_bc)
-    shared = (info, x_far, bc, halo, *taps)
+    shared = (info, x_near, bc, halo, *taps)
     x0, bc0, send = conv_states(0, *shared, f_dev[0], ones, rates[0])
     got = swap(send, "seq", 1)
-    x1, bc1, keep = conv_states(1, *shared, f_dev[1], ones, rates[1])
+    x1, bc1, keep, z_near = conv_states(1, *shared, f_dev[1], ones, rates[1], z_far)
     rates_kept = rates[1]
 
     uvs = []
-    xs, bcs = far(x0, x1), (bc0, bc1)
-    groups = [(x, z_far, *rest, ones) for x, *rest in zip(xs, bcs, cum, cum_s, log_s, f_blk, e_blk, rates)]
+    groups = [(x, z_near, *rest, ones) for x, *rest in zip((x0, x1), (bc0, bc1), cum, cum_s, log_s, f_blk, e_blk, rates)]
 
     def scan_next(token):
         if len(uvs) < 2 * B_PARTS:

time: 118 us -> 114 us (0.966)
  Pallas kernels: 81.2 us -> 76 us
  starting transfers between devices: 20.8 us -> 22 us
    pallas_call x4, Pallas kernels: 21.5 us -> 17.5 us  [scan_part(): pl.pallas_call(functools.partial(scan_kernel, order, part), in_specs=[SCA...]
    pallas_call x2, Pallas kernels: 13.9 us -> 10.8 us  [conv_states(): pl.pallas_call(functools.partial(conv_kernel, order), grid_spec=pltpu.Pre...]
    pallas_call x1, Pallas kernels: 2.72 us -> 4.6 us  [decays(): pl.pallas_call(decay_kernel, in_specs=[SCALAR] + [FULL] * 3 + [FAR], out_...]
    ppermute x7, waiting for transfers between devices: 3.02 us -> 1.22 us  [rotate(): lax.ppermute(block, 'seq', [(i, (i + distance) % size) for i in range(siz...]
    ppermute x12, waiting for transfers between devices: 12.3 us -> 13.7 us  [swap(): lax.ppermute(block, axis, [(i, i ^ bit) for i in range(lax.axis_size(axis...]
    ppermute x12, starting transfers between devices: 9.3 us -> 10.6 us  [swap(): lax.ppermute(block, axis, [(i, i ^ bit) for i in range(lax.axis_size(axis...]
  transfers between devices with their start and end apart: 19 -> 19, of which waited for: 7 -> 7; matrix products, arithmetic and copies ran while one was open for 0% -> 0% of each run, Pallas kernels for 67% -> 65%
where the time goes in v13:
time: 114 us
  Pallas kernels  76 us (67%)
  starting transfers between devices  22 us (19%)
  waiting for transfers between devices  14.9 us (13%)
    pallas_call x4, Pallas kernels, project_both(): pl.pallas_call(functools.partial(both_kernel, first // TILE, cut), grid=(...  25.5 us
    pallas_call x4, Pallas kernels, scan_part(): pl.pallas_call(functools.partial(scan_kernel, order, part), in_specs=[SCA...  17.5 us
    ppermute x12, waiting for transfers between devices, swap(): lax.ppermute(block, axis, [(i, i ^ bit) for i in range(lax.axis_size(axis...  13.7 us
    ppermute x7, starting transfers between devices, rotate(): lax.ppermute(block, 'seq', [(i, (i + distance) % size) for i in range(siz...  11.4 us
    pallas_call x2, Pallas kernels, conv_states(): pl.pallas_call(functools.partial(conv_kernel, order), grid_spec=pltpu.Pre...  10.8 us
    ppermute x12, starting transfers between devices, swap(): lax.ppermute(block, axis, [(i, i ^ bit) for i in range(lax.axis_size(axis...  10.6 us
    pallas_call x2, Pallas kernels, norm_rows(): pl.pallas_call(functools.partial(norm_kernel, places, len(weights)), in_s...  5.32 us
    pallas_call x1, Pallas kernels, decays(): pl.pallas_call(decay_kernel, in_specs=[SCALAR] + [FULL] * 3 + [FAR], out_...  4.6 us
  transfers between devices with their start and end apart: 19, of which 7 were waited for; matrix products, arithmetic and copies ran while one was open for 0% of the time, Pallas kernels for 65%

profile of v13, /device:TPU:0, one launch (start us, length us, event | category | flops | bytes accessed | tf_op | source)
XLA Modules:
  0.0 113.5 jit_solution(5223698469576914258)
XLA Ops:
  1.3 2.6 %collective-permute-start = (bf16[16,2560]{1,0:T(8,128)(2,1)S(1)}, bf16[16,2560]{1,0:T(8,128)(2,1)S(1)}, u32[]{:S(2)}, u32[]{:S(2)}) collective-permute-start(bf16[16,2560]{1,0:T(8,128)(2,1)S(1)} %tail_rows.1), channel_id=1, source_target_pairs={{0,4},{4,8},{8,12},{12,16},{16,20},{20,24},{24,28},{28,0},{1,5},{5... | collective-permute-start | bytes 245768 | tf_op jit(solution)/shard_map/ppermute | solution.py:681
  4.0 4.6 %decays.1 = (f32[1024,16]{1,0:T(8,128)S(1)}, f32[1024,16]{1,0:T(8,128)S(1)}, f32[16,1024]{1,0:T(8,128)S(1)}, f32[16,1024]{1,0:T(8,128)S(1)}, f32[16,1024]{1,0:T(...) custom-call(s32[9]{0:T(128)S(1)} %stack.36.info, ...), custom_call_target="tpu_custom_call" | custom-call | flops 1 | bytes 1 | tf_op jit(solution)/shard_map/decays/pallas_call | solution.py:139
  10.1 5.4 %conv_states.2 = (bf16[1024,1024]{1,0:T(8,128)(2,1)S(1)}, bf16[1024,256]{1,0:T(8,128)(2,1)S(1)}, bf16[144,1024]{1,0:T(8,128)(2,1)S(1)}) custom-call(s32[9]{0:T(128)S(1)} %stack.36.info, bf16[1024,2048]{1,0:T(8,128)(2,1)S(1)} %get-tuple-element.54.x, bf16[1024,512]{1,0:T(8,128)(2,1)S(1)} %bitcast.14, bf16[16,2560]{1,0:T(8,128)(2,1)S(1)} %collective-permute-done.halo, ...), custom_call_target="tpu_custom_call" | custom-call | flops 1 | bytes 1 | tf_op jit(solution)/shard_map/conv_states/pallas_call | solution.py:275
  15.9 5.4 %conv_states.3 = (bf16[1024,1024]{1,0:T(8,128)(2,1)S(1)}, bf16[1024,256]{1,0:T(8,128)(2,1)S(1)}, f32[128,1024]{1,0:T(8,128)S(1)}, bf16[1024,2048]{1,0:T(8,128)(2,1)S(1)}) custom-call(s32[9]{0:T(128)S(1)} %stack.36.info, bf16[1024,2048]{1,0:T(8,128)(2,1)S(1)} %get-tuple-element.54.x, bf16[1024,512]{1,0:T(8,128)(2,1)S(1)} %bitcast.15, ...), custom_call_target="tpu_custom_call" | custom-call | flops 1 | bytes 1 | tf_op jit(solution)/shard_map/conv_states/pallas_call | solution.py:275
  21.3 3.1 %collective-permute-done.1.got = bf16[144,1024]{1,0:T(8,128)(2,1)S(1)} collective-permute-done((bf16[144,1024]{1,0:T(8,128)(2,1)S(1)}, bf16[144,1024]{1,0:T(8,128)(2,1)S(1)}, u32[]{:S(2)}, u32[]{:S(2)}) %collective-permute-start.1) | collective-permute-done | bytes 294944 | tf_op jit(solution)/shard_map/ppermute | solution.py:676
  26.0 2.6 %collective-permute-start.3 = (bf16[144,256]{1,0:T(8,128)(2,1)S(1)}, bf16[144,256]{1,0:T(8,128)(2,1)S(1)}, u32[]{:S(2)}, u32[]{:S(2)}) collective-permute-start(bf16[144,256]{1,0:T(8,128)(2,1)S(1)} %get-tuple-element.75), channel_id=1, source_target_pairs={{0,16},{4,20},{8,24},{12,28},{16,0},{20,4},{24,8},{28,12},{1,17},{... | collective-permute-start | bytes 221192 | tf_op jit(solution)/shard_map/ppermute | solution.py:681
  28.6 1.3 %collective-permute-start.4 = (bf16[144,256]{1,0:T(8,128)(2,1)S(1)}, bf16[144,256]{1,0:T(8,128)(2,1)S(1)}, u32[]{:S(2)}, u32[]{:S(2)}) collective-permute-start(bf16[144,256]{1,0:T(8,128)(2,1)S(1)} %get-tuple-element.76), channel_id=1, source_target_pairs={{0,24},{4,28},{8,0},{12,4},{16,8},{20,12},{24,16},{28,20},{1,25},{... | collective-permute-start | bytes 221192 | tf_op jit(solution)/shard_map/ppermute | solution.py:681
  29.9 4.4 %scan_part.4._.refs_0_ = bf16[1024,1024]{1,0:T(8,128)(2,1)S(1)} custom-call(s32[9]{0:T(128)S(1)} %stack.36.info, bf16[1024,1024]{1,0:T(8,128)(2,1)S(1)} %get-tuple-element.77.x, bf16[1024,2048]{1,0:T(8,128)(2,1)S(1)} %get-tuple-element.67.z, bf16[1024,256]{1,0:T(8,128)(2,1)S(1)} %get-tuple-element.58.bc.bc0, f32[1024,16]{1,0:T(8,128)S(1)} %get-tuple-element.78.cum, ...), custom_call_target="tpu_custom_call" | custom-call | flops 1 | bytes 1 | tf_op jit(solution)/shard_map/scan_part/pallas_call | solution.py:465
  34.3 4.4 %scan_part.5.refs_4_.refs_1_ = bf16[1024,1024]{1,0:T(8,128)(2,1)S(1)} custom-call(s32[9]{0:T(128)S(1)} %stack.36.info, bf16[1024,1024]{1,0:T(8,128)(2,1)S(1)} %get-tuple-element.77.x, bf16[1024,2048]{1,0:T(8,128)(2,1)S(1)} %get-tuple-element.67.z, bf16[1024,256]{1,0:T(8,128)(2,1)S(1)} %get-tuple-element.58.bc.bc0, f32[1024,16]{1,0:T(8,128)S(1)} %get-tuple-element.78.cum, ...), custom_call_target="tpu_custom_call" | custom-call | flops 1 | bytes 1 | tf_op jit(solution)/shard_map/scan_part/pallas_call | solution.py:465
  40.7 2.8 %collective-permute-start.7 = (bf16[128,256]{1,0:T(8,128)(2,1)S(1)}, bf16[128,256]{1,0:T(8,128)(2,1)S(1)}, u32[]{:S(2)}, u32[]{:S(2)}) collective-permute-start(bf16[128,256]{1,0:T(8,128)(2,1)S(1)} %get-tuple-element.86), channel_id=1, source_target_pairs={{0,24},{4,28},{8,0},{12,4},{16,8},{20,12},{24,16},{28,20},{1,25},{... | collective-permute-start | bytes 196616 | tf_op jit(solution)/shard_map/ppermute | solution.py:681
  43.6 4.4 %scan_part.6._.refs_2_ = bf16[1024,1024]{1,0:T(8,128)(2,1)S(1)} custom-call(s32[9]{0:T(128)S(1)} %stack.36.info, bf16[1024,1024]{1,0:T(8,128)(2,1)S(1)} %get-tuple-element.66.x, bf16[1024,2048]{1,0:T(8,128)(2,1)S(1)} %get-tuple-element.67.z, bf16[1024,256]{1,0:T(8,128)(2,1)S(1)} %get-tuple-element.61.bc.bc1, f32[1024,16]{1,0:T(8,128)S(1)} %get-tuple-element.68.cum, ...), custom_call_target="tpu_custom_call" | custom-call | flops 1 | bytes 1 | tf_op jit(solution)/shard_map/scan_part/pallas_call | solution.py:465
  50.1 4.4 %scan_part.7.refs_3_ = bf16[1024,1024]{1,0:T(8,128)(2,1)S(1)} custom-call(s32[9]{0:T(128)S(1)} %stack.36.info, bf16[1024,1024]{1,0:T(8,128)(2,1)S(1)} %get-tuple-element.66.x, bf16[1024,2048]{1,0:T(8,128)(2,1)S(1)} %get-tuple-element.67.z, bf16[1024,256]{1,0:T(8,128)(2,1)S(1)} %get-tuple-element.61.bc.bc1, f32[1024,16]{1,0:T(8,128)S(1)} %get-tuple-element.68.cum, ...), custom_call_target="tpu_custom_call" | custom-call | flops 1 | bytes 1 | tf_op jit(solution)/shard_map/scan_part/pallas_call | solution.py:465
  55.3 2.5 %norm_rows.2._ = bf16[512,2048]{1,0:T(8,128)(2,1)S(1)} custom-call(s32[9]{0:T(128)S(1)} %stack.36.info, bf16[1024,256]{1,0:T(8,128)(2,1)S(1)} %get-tuple-element.58.bc.bc0, bf16[1024,256]{1,0:T(8,128)(2,1)S(1)} %get-tuple-element.61.bc.bc1, bf16[128,1024]{1,0:T(8,128)(2,1)S(1)} %collective-permute-done.8.state0, ...), custom_call_target="tpu_custom_call" | custom-call | flops 1 | bytes 1 | tf_op jit(solution)/shard_map/norm_rows/pallas_call | solution.py:522
  57.9 2.8 %norm_rows.3 = (bf16[512,2048]{1,0:T(8,128)(2,1)S(1)}, bf16[2048,512]{1,0:T(8,128)(2,1)S(1)}, bf16[2048,512]{1,0:T(8,128)(2,1)S(1)}) custom-call(s32[9]{0:T(128)S(1)} %stack.36.info, bf16[1024,256]{1,0:T(8,128)(2,1)S(1)} %get-tuple-element.58.bc.bc0, bf16[1024,256]{1,0:T(8,128)(2,1)S(1)} %get-tuple-element.61.bc.bc1, ...), custom_call_target="tpu_custom_call" | custom-call | flops 1 | bytes 1 | tf_op jit(solution)/shard_map/norm_rows/pallas_call | solution.py:522
  63.3 1.4 %collective-permute-start.18 = (bf16[256,512]{1,0:T(8,128)(2,1)S(1)}, bf16[256,512]{1,0:T(8,128)(2,1)S(1)}, u32[]{:S(2)}, u32[]{:S(2)}) collective-permute-start(bf16[256,512]{1,0:T(8,128)(2,1)S(1)} %project_ahead.1), channel_id=1, source_target_pairs={{0,2},{1,3},{2,0},{3,1},{4,6},{5,7},{6,4},{7,5},{8,10},{9,11},{10,... | collective-permute-start | bytes 786440 | tf_op jit(solution)/shard_map/ppermute | solution.py:676
  64.7 4.3 %project_both.7 = (bf16[256,512]{1,0:T(8,128)(2,1)S(1)}, f32[256,512]{1,0:T(8,128)S(1)}) custom-call(bf16[512,2048]{1,0:T(8,128)(2,1)S(1)} %get-tuple-element.89.owns, bf16[512,2048]{1,0:T(8,128)(2,1)S(1)} %collective-permute-done.10.mates, bf16[2048,4096]{1,0:T(8,128)(2,1)} %w0_far.9, bf16[2048,4096]{1,0:T(8,128)(2,1)} %collective-permute-done.9.refs_5_.w1_far), custom_call_target="tpu_custom_call" | custom-call | flops 1 | bytes 1 | tf_op jit(solution)/shard_map/project_both/pallas_call | solution.py:609
  69.7 7.1 %project_both.6 = (bf16[256,512]{1,0:T(8,128)(2,1)S(1)}, bf16[256,512]{1,0:T(8,128)(2,1)S(1)}, f32[256,1024]{1,0:T(8,128)S(1)}) custom-call(bf16[512,2048]{1,0:T(8,128)(2,1)S(1)} %get-tuple-element.89.owns, bf16[512,2048]{1,0:T(8,128)(2,1)S(1)} %collective-permute-done.10.mates, bf16[2048,4096]{1,0:T(8,128)(2,1)} %w0_far.9, ...), custom_call_target="tpu_custom_call" | custom-call | flops 1 | bytes 1 | tf_op jit(solution)/shard_map/project_both/pallas_call | solution.py:609
  76.8 1.4 %collective-permute-start.15 = (bf16[256,512]{1,0:T(8,128)(2,1)S(1)}, bf16[256,512]{1,0:T(8,128)(2,1)S(1)}, u32[]{:S(2)}, u32[]{:S(2)}) collective-permute-start(bf16[256,512]{1,0:T(8,128)(2,1)S(1)} %get-tuple-element.97), channel_id=1, source_target_pairs={{0,2},{1,3},{2,0},{3,1},{4,6},{5,7},{6,4},{7,5},{8,10},{9,11},{10,... | collective-permute-start | bytes 786440 | tf_op jit(solution)/shard_map/ppermute | solution.py:676
  78.9 7.1 %project_both.5 = (bf16[256,512]{1,0:T(8,128)(2,1)S(1)}, bf16[256,512]{1,0:T(8,128)(2,1)S(1)}, f32[256,1024]{1,0:T(8,128)S(1)}) custom-call(bf16[512,2048]{1,0:T(8,128)(2,1)S(1)} %get-tuple-element.89.owns, bf16[512,2048]{1,0:T(8,128)(2,1)S(1)} %collective-permute-done.10.mates, bf16[2048,4096]{1,0:T(8,128)(2,1)} %w0_far.9, ...), custom_call_target="tpu_custom_call" | custom-call | flops 1 | bytes 1 | tf_op jit(solution)/shard_map/project_both/pallas_call | solution.py:609
  86.0 1.4 %collective-permute-start.13 = (bf16[256,512]{1,0:T(8,128)(2,1)S(1)}, bf16[256,512]{1,0:T(8,128)(2,1)S(1)}, u32[]{:S(2)}, u32[]{:S(2)}) collective-permute-start(bf16[256,512]{1,0:T(8,128)(2,1)S(1)} %get-tuple-element.94), channel_id=1, source_target_pairs={{0,2},{1,3},{2,0},{3,1},{4,6},{5,7},{6,4},{7,5},{8,10},{9,11},{10,... | collective-permute-start | bytes 786440 | tf_op jit(solution)/shard_map/ppermute | solution.py:676
  87.4 7.1 %project_both.4 = (bf16[256,512]{1,0:T(8,128)(2,1)S(1)}, bf16[256,512]{1,0:T(8,128)(2,1)S(1)}, f32[256,1024]{1,0:T(8,128)S(1)}) custom-call(bf16[512,2048]{1,0:T(8,128)(2,1)S(1)} %get-tuple-element.89.owns, bf16[512,2048]{1,0:T(8,128)(2,1)S(1)} %collective-permute-done.10.mates, bf16[2048,4096]{1,0:T(8,128)(2,1)} %w0_far.9, ...), custom_call_target="tpu_custom_call" | custom-call | flops 1 | bytes 1 | tf_op jit(solution)/shard_map/project_both/pallas_call | solution.py:609
  97.3 3.8 %project_near.1.refs_1_ = bf16[256,4096]{1,0:T(8,128)(2,1)} custom-call(bf16[512,2048]{1,0:T(8,128)(2,1)S(1)} %get-tuple-element.89.owns, bf16[512,2048]{1,0:T(8,128)(2,1)S(1)} %collective-permute-done.10.mates, bf16[2048,4096]{1,0:T(8,128)(2,1)} %w0_far.9, bf16[2048,4096]{1,0:T(8,128)(2,1)} %collective-permute-done.9.refs_5_.w1_far, ...), custom_call_target="tpu_custom_call" | custom-call | flops 1 | bytes 1 | tf_op jit(solution)/shard_map/project_near/pallas_call | solution.py:633
  104.7 4.7 %collective-permute-done.12.refs_0_ = bf16[256,512]{1,0:T(8,128)(2,1)S(1)} collective-permute-done((bf16[256,512]{1,0:T(8,128)(2,1)S(1)}, bf16[256,512]{1,0:T(8,128)(2,1)S(1)}, u32[]{:S(2)}, u32[]{:S(2)}) %collective-permute-start.12) | collective-permute-done | bytes 262176 | tf_op jit(solution)/shard_map/ppermute | solution.py:676
  110.2 2.6 %collective-permute-done.11.refs_0_ = bf16[256,512]{1,0:T(8,128)(2,1)S(1)} collective-permute-done((bf16[256,512]{1,0:T(8,128)(2,1)S(1)}, bf16[256,512]{1,0:T(8,128)(2,1)S(1)}, u32[]{:S(2)}, u32[]{:S(2)}) %collective-permute-start.11) | collective-permute-done | bytes 262176 | tf_op jit(solution)/shard_map/ppermute | solution.py:676
  (44 shorter events, 21.7 us)
Async XLA Ops:
  0.0 57.9 %collective-permute-start.9 = (bf16[2048,4096]{1,0:T(8,128)(2,1)}, bf16[2048,4096]{1,0:T(8,128)(2,1)}, u32[]{:S(2)}, u32[]{:S(2)}) collective-permute-start(bf16[2048,4096]{1,0:T(8,128)(2,1)} %w0_far.9), channel_id=1, source_target_pairs={{0,1},{1,0},{2,3},{3,2},{4,5},{5,4},{6,7},{7,6},{8,9},{9,8},{10,11... | collective-permute-start | bytes 50331656 | tf_op jit(solution)/shard_map/ppermute | solution.py:676
  1.3 8.7 %collective-permute-start = (bf16[16,2560]{1,0:T(8,128)(2,1)S(1)}, bf16[16,2560]{1,0:T(8,128)(2,1)S(1)}, u32[]{:S(2)}, u32[]{:S(2)}) collective-permute-start(bf16[16,2560]{1,0:T(8,128)(2,1)S(1)} %tail_rows.1), channel_id=1, source_target_pairs={{0,4},{4,8},{8,12},{12,16},{16,20},{20,24},{24,28},{28,0},{1,5},{5... | collective-permute-start | bytes 245768 | tf_op jit(solution)/shard_map/ppermute | solution.py:681
  4.0 4.6 %copy-start.1 = (bf16[1024,2,256]{2,1,0:T(2,128)(2,1)S(1)}, bf16[1024,2,256]{2,1,0:T(2,128)(2,1)}, u32[]{:S(2)}) copy-start(bf16[1024,2,256]{2,1,0:T(2,128)(2,1)} %bc.1) | copy-start | bytes 3145732
  15.5 8.9 %collective-permute-start.1 = (bf16[144,1024]{1,0:T(8,128)(2,1)S(1)}, bf16[144,1024]{1,0:T(8,128)(2,1)S(1)}, u32[]{:S(2)}, u32[]{:S(2)}) collective-permute-start(bf16[144,1024]{1,0:T(8,128)(2,1)S(1)} %get-tuple-element.62), channel_id=1, source_target_pairs={{0,4},{4,0},{8,12},{12,8},{16,20},{20,16},{24,28},{28,24},{1,5},{5... | collective-permute-start | bytes 884744 | tf_op jit(solution)/shard_map/ppermute | solution.py:676
  25.2 13.5 %collective-permute-start.2 = (bf16[144,256]{1,0:T(8,128)(2,1)S(1)}, bf16[144,256]{1,0:T(8,128)(2,1)S(1)}, u32[]{:S(2)}, u32[]{:S(2)}) collective-permute-start(bf16[144,256]{1,0:T(8,128)(2,1)S(1)} %get-tuple-element.74), channel_id=1, source_target_pairs={{0,8},{4,12},{8,16},{12,20},{16,24},{20,28},{24,0},{28,4},{1,9},{5... | collective-permute-start | bytes 221192 | tf_op jit(solution)/shard_map/ppermute | solution.py:681
  26.0 12.7 %collective-permute-start.3 = (bf16[144,256]{1,0:T(8,128)(2,1)S(1)}, bf16[144,256]{1,0:T(8,128)(2,1)S(1)}, u32[]{:S(2)}, u32[]{:S(2)}) collective-permute-start(bf16[144,256]{1,0:T(8,128)(2,1)S(1)} %get-tuple-element.75), channel_id=1, source_target_pairs={{0,16},{4,20},{8,24},{12,28},{16,0},{20,4},{24,8},{28,12},{1,17},{... | collective-permute-start | bytes 221192 | tf_op jit(solution)/shard_map/ppermute | solution.py:681
  28.6 10.2 %collective-permute-start.4 = (bf16[144,256]{1,0:T(8,128)(2,1)S(1)}, bf16[144,256]{1,0:T(8,128)(2,1)S(1)}, u32[]{:S(2)}, u32[]{:S(2)}) collective-permute-start(bf16[144,256]{1,0:T(8,128)(2,1)S(1)} %get-tuple-element.76), channel_id=1, source_target_pairs={{0,24},{4,28},{8,0},{12,4},{16,8},{20,12},{24,16},{28,20},{1,25},{... | collective-permute-start | bytes 221192 | tf_op jit(solution)/shard_map/ppermute | solution.py:681
  39.4 8.6 %collective-permute-start.5 = (bf16[128,256]{1,0:T(8,128)(2,1)S(1)}, bf16[128,256]{1,0:T(8,128)(2,1)S(1)}, u32[]{:S(2)}, u32[]{:S(2)}) collective-permute-start(bf16[128,256]{1,0:T(8,128)(2,1)S(1)} %get-tuple-element.84), channel_id=1, source_target_pairs={{0,8},{4,12},{8,16},{12,20},{16,24},{20,28},{24,0},{28,4},{1,9},{5... | collective-permute-start | bytes 196616 | tf_op jit(solution)/shard_map/ppermute | solution.py:681
  40.1 7.9 %collective-permute-start.6 = (bf16[128,256]{1,0:T(8,128)(2,1)S(1)}, bf16[128,256]{1,0:T(8,128)(2,1)S(1)}, u32[]{:S(2)}, u32[]{:S(2)}) collective-permute-start(bf16[128,256]{1,0:T(8,128)(2,1)S(1)} %get-tuple-element.85), channel_id=1, source_target_pairs={{0,16},{4,20},{8,24},{12,28},{16,0},{20,4},{24,8},{28,12},{1,17},{... | collective-permute-start | bytes 196616 | tf_op jit(solution)/shard_map/ppermute | solution.py:681
  40.7 7.3 %collective-permute-start.7 = (bf16[128,256]{1,0:T(8,128)(2,1)S(1)}, bf16[128,256]{1,0:T(8,128)(2,1)S(1)}, u32[]{:S(2)}, u32[]{:S(2)}) collective-permute-start(bf16[128,256]{1,0:T(8,128)(2,1)S(1)} %get-tuple-element.86), channel_id=1, source_target_pairs={{0,24},{4,28},{8,0},{12,4},{16,8},{20,12},{24,16},{28,20},{1,25},{... | collective-permute-start | bytes 196616 | tf_op jit(solution)/shard_map/ppermute | solution.py:681
  48.8 6.5 %copy-start = (f32[2048]{0:T(1024)S(1)}, f32[2048]{0:T(1024)}, u32[]{:S(2)}) copy-start(f32[2048]{0:T(1024)} %param.18) | copy-start | bytes 24580
  48.9 6.4 %collective-permute-start.8 = (bf16[128,1024]{1,0:T(8,128)(2,1)S(1)}, bf16[128,1024]{1,0:T(8,128)(2,1)S(1)}, u32[]{:S(2)}, u32[]{:S(2)}) collective-permute-start(bf16[128,1024]{1,0:T(8,128)(2,1)S(1)} %get-tuple-element.87._), channel_id=1, source_target_pairs={{0,4},{4,0},{8,12},{12,8},{16,20},{20,16},{24,28},{28,24},{1,5},{5... | collective-permute-start | bytes 786440 | tf_op jit(solution)/shard_map/ppermute | solution.py:676
  57.8 4.2 %collective-permute-start.10 = (bf16[512,2048]{1,0:T(8,128)(2,1)S(1)}, bf16[512,2048]{1,0:T(8,128)(2,1)S(1)}, u32[]{:S(2)}, u32[]{:S(2)}) collective-permute-start(bf16[512,2048]{1,0:T(8,128)(2,1)S(1)} %norm_rows.2._), channel_id=1, source_target_pairs={{0,1},{1,0},{2,3},{3,2},{4,5},{5,4},{6,7},{7,6},{8,9},{9,8},{10,11... | collective-permute-start | bytes 6291464 | tf_op jit(solution)/shard_map/ppermute | solution.py:676
  63.3 31.2 %collective-permute-start.18 = (bf16[256,512]{1,0:T(8,128)(2,1)S(1)}, bf16[256,512]{1,0:T(8,128)(2,1)S(1)}, u32[]{:S(2)}, u32[]{:S(2)}) collective-permute-start(bf16[256,512]{1,0:T(8,128)(2,1)S(1)} %project_ahead.1), channel_id=1, source_target_pairs={{0,2},{1,3},{2,0},{3,1},{4,6},{5,7},{6,4},{7,5},{8,10},{9,11},{10,... | collective-permute-start | bytes 786440 | tf_op jit(solution)/shard_map/ppermute | solution.py:676
  69.0 26.2 %collective-permute-start.17 = (bf16[256,512]{1,0:T(8,128)(2,1)S(1)}, bf16[256,512]{1,0:T(8,128)(2,1)S(1)}, u32[]{:S(2)}, u32[]{:S(2)}) collective-permute-start(bf16[256,512]{1,0:T(8,128)(2,1)S(1)} %get-tuple-element.100), channel_id=1, source_target_pairs={{0,2},{1,3},{2,0},{3,1},{4,6},{5,7},{6,4},{7,5},{8,10},{9,11},{10,... | collective-permute-start | bytes 786440 | tf_op jit(solution)/shard_map/ppermute | solution.py:676
  76.8 19.8 %collective-permute-start.15 = (bf16[256,512]{1,0:T(8,128)(2,1)S(1)}, bf16[256,512]{1,0:T(8,128)(2,1)S(1)}, u32[]{:S(2)}, u32[]{:S(2)}) collective-permute-start(bf16[256,512]{1,0:T(8,128)(2,1)S(1)} %get-tuple-element.97), channel_id=1, source_target_pairs={{0,2},{1,3},{2,0},{3,1},{4,6},{5,7},{6,4},{7,5},{8,10},{9,11},{10,... | collective-permute-start | bytes 786440 | tf_op jit(solution)/shard_map/ppermute | solution.py:676
  78.2 23.6 %collective-permute-start.16 = (bf16[256,512]{1,0:T(8,128)(2,1)S(1)}, bf16[256,512]{1,0:T(8,128)(2,1)S(1)}, u32[]{:S(2)}, u32[]{:S(2)}) collective-permute-start(bf16[256,512]{1,0:T(8,128)(2,1)S(1)} %get-tuple-element.98), channel_id=1, source_target_pairs={{0,2},{1,3},{2,0},{3,1},{4,6},{5,7},{6,4},{7,5},{8,10},{9,11},{10,... | collective-permute-start | bytes 786440 | tf_op jit(solution)/shard_map/ppermute | solution.py:676
  86.0 16.8 %collective-permute-start.13 = (bf16[256,512]{1,0:T(8,128)(2,1)S(1)}, bf16[256,512]{1,0:T(8,128)(2,1)S(1)}, u32[]{:S(2)}, u32[]{:S(2)}) collective-permute-start(bf16[256,512]{1,0:T(8,128)(2,1)S(1)} %get-tuple-element.94), channel_id=1, source_target_pairs={{0,2},{1,3},{2,0},{3,1},{4,6},{5,7},{6,4},{7,5},{8,10},{9,11},{10,... | collective-permute-start | bytes 786440 | tf_op jit(solution)/shard_map/ppermute | solution.py:676
  94.5 9.3 %collective-permute-start.14 = (bf16[256,512]{1,0:T(8,128)(2,1)S(1)}, bf16[256,512]{1,0:T(8,128)(2,1)S(1)}, u32[]{:S(2)}, u32[]{:S(2)}) collective-permute-start(bf16[256,512]{1,0:T(8,128)(2,1)S(1)} %get-tuple-element.95), channel_id=1, source_target_pairs={{0,2},{1,3},{2,0},{3,1},{4,6},{5,7},{6,4},{7,5},{8,10},{9,11},{10,... | collective-permute-start | bytes 786440 | tf_op jit(solution)/shard_map/ppermute | solution.py:676
  95.2 14.2 %collective-permute-start.12 = (bf16[256,512]{1,0:T(8,128)(2,1)S(1)}, bf16[256,512]{1,0:T(8,128)(2,1)S(1)}, u32[]{:S(2)}, u32[]{:S(2)}) collective-permute-start(bf16[256,512]{1,0:T(8,128)(2,1)S(1)} %get-tuple-element.92), channel_id=1, source_target_pairs={{0,2},{1,3},{2,0},{3,1},{4,6},{5,7},{6,4},{7,5},{8,10},{9,11},{10,... | collective-permute-start | bytes 786440 | tf_op jit(solution)/shard_map/ppermute | solution.py:676
  96.6 16.2 %collective-permute-start.11 = (bf16[256,512]{1,0:T(8,128)(2,1)S(1)}, bf16[256,512]{1,0:T(8,128)(2,1)S(1)}, u32[]{:S(2)}, u32[]{:S(2)}) collective-permute-start(bf16[256,512]{1,0:T(8,128)(2,1)S(1)} %get-tuple-element.91), channel_id=1, source_target_pairs={{0,2},{1,3},{2,0},{3,1},{4,6},{5,7},{6,4},{7,5},{8,10},{9,11},{10,... | collective-permute-start | bytes 786440 | tf_op jit(solution)/shard_map/ppermute | solution.py:676

commit v14 on v13

--- a/solution.py
+++ b/solution.py
@@ -58,11 +58,20 @@
     return pl.BlockSpec(shape, lambda *_: (0,) * len(shape))
 
 
+def group_copies(x_far, x, group, sems):
+    length, width = x.shape
+    rows = length // 4
+    lanes = pl.ds(pl.multiple_of(group * width, width), width)
+    pieces = [pl.ds(k * rows, rows) for k in range(4)]
+    return [pltpu.make_async_copy(x_far.at[at, lanes], x.at[at], sems.at[k]) for k, at in enumerate(pieces)]
+
+
 def decay_kernel(info, ld_t, step_t, skip, x_far, *refs):
     cum, cum_s, log_s, f_dev, f_blk, e_blk, rates = [refs[2 * k : 2 * k + 2] for k in range(7)]
-    ones, x, sem = refs[14:]
-    copy = pltpu.make_async_copy(x_far, x, sem)
-    copy.start()
+    ones, wide_ones, x, sem = refs[14:]
+    copies = group_copies(x_far, x, info[GROUP], sem)
+    for copy in copies:
+        copy.start()
     heads, length = ld_t.shape
     blocks = length // TOK_B
     per = heads // 2
@@ -89,13 +98,21 @@
     member = member.astype(F32)
     ones[0:per, :] = member.astype(BF16)
     ones[per:, :] = member.astype(BF16)
+    shape = (per, per * TOK_B)
+    spread = lax.broadcasted_iota(jnp.int32, shape, 0) == lax.broadcasted_iota(jnp.int32, shape, 1) // TOK_B
+    for k in range(3):
+        wide_ones[k * per : (k + 1) * per, :] = spread.astype(F32).astype(BF16)
     cums, totals, row_totals = [], [], []
     for b in range(blocks):
         rows = slice(b * TOK_B, (b + 1) * TOK_B)
         logs = ordered(ld_t[:, rows]) * LOG2E
         c = dot(lower, logs, ((1,), (1,)), HIGHEST)
         for g in range(2):
-            cum[g][rows, :] = c[:, g * per : (g + 1) * per]
+            rest = c[:, g * per : (g + 1) * per]
+            for k in range(3):
+                kept = rest.astype(BF16)
+                cum[g][rows, k * per : (k + 1) * per] = kept
+                rest = rest - kept.astype(F32)
         row_totals.append(c[TOK_B - 1 : TOK_B, :])
         c = dot(logs, upper, precision=HIGHEST)
         cums.append(c)
@@ -123,7 +140,8 @@
         put(f_dev, rows, jnp.exp2(total - (cums[b] + before[b])) * s)
         put(f_blk, rows, jnp.exp2(totals[b] - cums[b]) * s)
         put(e_blk, rows, jnp.exp2(cums[b]))
-    copy.wait()
+    for copy in copies:
+        copy.wait()
 
 
 def decays(info, log_decay, step, skip, x, width):
@@ -132,21 +150,25 @@
     per = heads // 2
     across = jax.ShapeDtypeStruct((per, length), F32)
     pair = jax.ShapeDtypeStruct((length, 2 * per), BF16)
-    column = jax.ShapeDtypeStruct((length, per), F32)
+    column = jax.ShapeDtypeStruct((length, 3 * per), BF16)
     rates = jax.ShapeDtypeStruct((2 * blocks + 16, width), F32)
     shapes = [shape for shape in (column, across, across, pair, pair, pair, rates) for _ in range(2)]
-    shapes += [jax.ShapeDtypeStruct((2 * per, width), BF16), pltpu.VMEM(x.shape, BF16)]
-    *refs, ones, x_near = pl.pallas_call(
+    shapes += [
+        jax.ShapeDtypeStruct((2 * per, width), BF16),
+        jax.ShapeDtypeStruct((3 * per, per * TOK_B), BF16),
+        pltpu.VMEM((length, width), BF16),
+    ]
+    *refs, ones, wide_ones, x_near = pl.pallas_call(
         decay_kernel,
         in_specs=[SCALAR] + [FULL] * 3 + [FAR],
         out_specs=[FULL] * len(shapes),
         out_shape=shapes,
-        scratch_shapes=[pltpu.SemaphoreType.DMA],
+        scratch_shapes=[pltpu.SemaphoreType.DMA((4,))],
         compiler_params=params(16),
         cost_estimate=CHEAP,
         name="decays",
     )(info, *far(log_decay.T, step.T, skip[None, :], x))
-    return [tuple(refs[2 * k : 2 * k + 2]) for k in range(7)], ones, x_near
+    return [tuple(refs[2 * k : 2 * k + 2]) for k in range(7)], ones, wide_ones, x_near
 
 
 def tail_kernel(x, bc, out):
@@ -190,17 +212,23 @@
 
 
 def conv_kernel(order, info, x, bc, halo, wx, wbc, f_dev, ones, rates, *refs):
-    z_far, refs = (None, refs) if order == 0 else (refs[0], refs[1:])
+    next_far, refs = refs[0], refs[1:]
     x_out, bc_out, final = refs[:3]
     xf, state, down = refs[-3:]
     length, width = x_out.shape
     rows = TOK_A
     group = info[GROUP + order]
     first_lane = pl.multiple_of(group * width, width)
+    taken, sem = refs[3:5]
     first_bc = pl.multiple_of(group * 2 * N, 2 * N)
-    if z_far is not None:
-        fetch = pltpu.make_async_copy(z_far, refs[3], refs[4])
-        fetch.start()
+    if order == 0:
+        copies = group_copies(next_far, taken, info[GROUP + 1], sem)
+    else:
+        part = length // 4
+        pieces = [pl.ds(k * part, part) for k in range(4)]
+        copies = [pltpu.make_async_copy(next_far.at[at], taken.at[at], sem.at[k]) for k, at in enumerate(pieces)]
+    for copy in copies:
+        copy.start()
     state[...] = jnp.zeros_like(state)
     row = lax.broadcasted_iota(jnp.int32, down.shape, 0)
     col = lax.broadcasted_iota(jnp.int32, down.shape, 1)
@@ -234,7 +262,7 @@
         for lanes in range(0, 2 * N, SLAB):
             ds = slice(lanes, lanes + SLAB)
             src = pl.ds(pl.multiple_of(first_bc + lanes, SLAB), SLAB)
-            halo_src = pl.ds(pl.multiple_of(x.shape[1] + first_bc + lanes, SLAB), SLAB)
+            halo_src = pl.ds(pl.multiple_of(2 * width + first_bc + lanes, SLAB), SLAB)
 
             def emit_bc(r, value):
                 bc_out[out(r), ds] = value.astype(BF16)
@@ -252,7 +280,7 @@
                 xf[r : r + ROWS_A, ds] = (value * scale[r : r + ROWS_A]).astype(BF16)
 
             weights = [wx[k : k + 1, ds] for k in range(KCONV)]
-            conv(i, x[at, src], halo[:, src], x[behind, src], weights, emit)
+            conv(i, x[at, ds], halo[:, src], x[behind, ds], weights, emit)
 
         state[...] += dot(bc_out[at, 0:N], xf[...], ((0,), (0,)))
         return 0
@@ -263,35 +291,39 @@
         put_message(final, state[...], rates[row : row + 1, :])
     else:
         final[...] = state[...]
-        fetch.wait()
-
-
-def conv_states(order, info, x, bc, halo, wx, wbc, f_dev, ones, rates, z=None):
-    length, full = x.shape
-    width = full // 2
+    for copy in copies:
+        copy.wait()
+
+
+def conv_states(order, info, x, bc, halo, wx, wbc, f_dev, ones, rates, ahead):
+    length, width = x.shape
     column = lambda i, info: (0, info[GROUP + order])
     final = ((N + EXTRA, width), BF16) if order == 0 else ((N, width), F32)
-    more = [] if z is None else [z]
+    taken = (length, width) if order == 0 else ahead.shape
     return pl.pallas_call(
         functools.partial(conv_kernel, order),
         grid_spec=pltpu.PrefetchScalarGridSpec(
             num_scalar_prefetch=1,
             grid=(1,),
-            in_specs=[FULL] * 3 + [pl.BlockSpec((KCONV, width), column)] + [FULL] * 4 + [FAR] * len(more),
-            out_specs=[FULL] * (3 + len(more)),
-            scratch_shapes=[pltpu.SemaphoreType.DMA] * len(more)
-            + [pltpu.VMEM((TOK_A, width), BF16), pltpu.VMEM((N, width), F32), pltpu.VMEM((TOK_A, TOK_A), BF16)],
+            in_specs=[FULL] * 3 + [pl.BlockSpec((KCONV, width), column)] + [FULL] * 4 + [FAR],
+            out_specs=[FULL] * 4,
+            scratch_shapes=[
+                pltpu.SemaphoreType.DMA((4,)),
+                pltpu.VMEM((TOK_A, width), BF16),
+                pltpu.VMEM((N, width), F32),
+                pltpu.VMEM((TOK_A, TOK_A), BF16),
+            ],
         ),
         out_shape=[
             pltpu.VMEM((length, width), BF16),
             pltpu.VMEM((length, 2 * N), BF16),
             jax.ShapeDtypeStruct(*final),
-        ]
-        + [pltpu.VMEM(a.shape, BF16) for a in more],
+            pltpu.VMEM(taken, BF16),
+        ],
         compiler_params=params(16),
         cost_estimate=CHEAP,
         name="conv_states",
-    )(info, x, bc, halo, wx, wbc, f_dev, ones, rates, *more)
+    )(info, x, bc, halo, wx, wbc, f_dev, ones, rates, ahead)
 
 
 def pair_kernel(info, got, keep, rates, _, msg, own, first, aux):
@@ -398,7 +430,7 @@
     )(*operands)
 
 
-def scan_kernel(order, part, info, x, z, bc, cum, cum_s, log_s, f_blk, e_blk, rates, ones, _, uv_out, state):
+def scan_kernel(order, part, info, x, z, bc, cum, cum_s, log_s, f_blk, e_blk, rates, ones, wide_ones, _, uv_out, state):
     length = x.shape[0]
     width = state.shape[1]
     per_slab = SLAB // P_SIZE
@@ -436,12 +468,14 @@
             old = state[:, lanes]
             rise = dot(e_blk[at, :], sel)
             carried = dot(c_mat, old.astype(BF16)) * rise
+            first_column = (first_head + s * per_slab) * TOK_B
+            columns = dot(cum[at, :], wide_ones[:, first_column : first_column + per_slab * TOK_B])
             within = []
             for q in range(per_slab // 2):
                 tables = []
                 for h in (2 * q, 2 * q + 1):
                     head = first_head + s * per_slab + h
-                    column = cum[at, head : head + 1]
+                    column = columns[:, h * TOK_B : (h + 1) * TOK_B]
                     own = slice(head, head + 1)
                     gap = jnp.minimum(column - cum_s[own, at], log_s[own, at])
                     tables.append((scores * jnp.exp2(gap)).astype(BF16))
@@ -459,35 +493,35 @@
     lax.fori_loop(0, length // STEP_B, turn, 0)
 
 
-def scan_part(order, part, info, token, x, z, bc, cum, cum_s, log_s, f_blk, e_blk, rates, ones):
+def scan_part(order, part, info, token, x, z, bc, cum, cum_s, log_s, f_blk, e_blk, rates, ones, wide_ones):
     length, full = x.shape
     width = full // B_PARTS
     return pl.pallas_call(
         functools.partial(scan_kernel, order, part),
-        in_specs=[SCALAR] + [FULL] * 10 + [ANY],
+        in_specs=[SCALAR] + [FULL] * 11 + [ANY],
         out_specs=FULL,
         out_shape=pltpu.VMEM((length, 2 * width), BF16),
         scratch_shapes=[pltpu.VMEM((N, width), F32)],
         compiler_params=params(12),
         cost_estimate=CHEAP,
         name="scan_part",
-    )(info, x, z, bc, cum, cum_s, log_s, f_blk, e_blk, rates, ones, token)
+    )(info, x, z, bc, cum, cum_s, log_s, f_blk, e_blk, rates, ones, wide_ones, token)
 
 
 def norm_kernel(places, fetched, info, bc0, bc1, state0, state1, gain, _, *refs):
     uvs, refs = refs[: 2 * B_PARTS], refs[2 * B_PARTS :]
-    weights, out, tiles, sem = refs[:fetched], refs[fetched], refs[fetched + 1 : 2 * fetched + 1], refs[-1]
+    weights, outs, tiles, sem = refs[:fetched], refs[fetched : -1 - fetched], refs[len(refs) - 1 - fetched : -1], refs[-1]
     copies = [
         pltpu.make_async_copy(weight.at[:, pl.ds(0, tile.shape[1])], tile, sem.at[k])
         for k, (weight, tile) in enumerate(zip(weights, tiles))
     ]
     for copy in copies:
         copy.start()
-    count = out.shape[0] // len(places)
+    count = outs[0].shape[0] * len(outs) // len(places)
     per = state0.shape[1]
     part = per // B_PARTS
 
-    def rows(first, base):
+    def rows(out, first, base):
         to = pl.ds(pl.multiple_of(first, ROWS_C), ROWS_C)
         at = pl.ds(pl.multiple_of(base, ROWS_C), ROWS_C)
         for order, (bc, state) in enumerate(((bc0, state0), (bc1, state1))):
@@ -509,7 +543,8 @@
     for k, place in enumerate(places):
 
         def step(j, _):
-            rows(k * count + j * ROWS_C, info[ROWS + place] * count + j * ROWS_C)
+            out, first = (outs[k], 0) if len(outs) > 1 else (outs[0], k * count)
+            rows(out, first + j * ROWS_C, info[ROWS + place] * count + j * ROWS_C)
             return 0
 
         lax.fori_loop(0, count // ROWS_C, step, 0)
@@ -517,13 +552,15 @@
         copy.wait()
 
 
-def norm_rows(places, info, count, token, bcs, states, gain, uvs, weights=(), columns=0):
+def norm_rows(places, apart, info, count, token, bcs, states, gain, uvs, weights=(), columns=0):
     tile = jax.ShapeDtypeStruct((gain.shape[1], columns), BF16)
+    arrays = len(places) if apart else 1
+    rows = jax.ShapeDtypeStruct((len(places) * count // arrays, gain.shape[1]), BF16)
     return pl.pallas_call(
         functools.partial(norm_kernel, places, len(weights)),
         in_specs=[SCALAR] + [FULL] * 5 + [ANY] + [FULL] * len(uvs) + [FAR] * len(weights),
-        out_specs=[FULL] * (1 + len(weights)),
-        out_shape=[jax.ShapeDtypeStruct((len(places) * count, gain.shape[1]), BF16)] + [tile] * len(weights),
+        out_specs=[FULL] * (arrays + len(weights)),
+        out_shape=[rows] * arrays + [tile] * len(weights),
         scratch_shapes=[pltpu.SemaphoreType.DMA((2,))],
         compiler_params=params(16),
         cost_estimate=CHEAP,
@@ -568,12 +605,11 @@
     ]
 
 
-def ahead_kernel(owns, mates, w0, w1, out):
-    rows = out.shape[0]
-    out[...] = (dot(owns[0:rows, :], w0[...]) + dot(mates[0:rows, :], w1[...])).astype(BF16)
-
-
-def project_ahead(owns, mates, w0, w1):
+def ahead_kernel(owns, mate, w0, w1, out):
+    out[...] = (dot(owns[0 : out.shape[0], :], w0[...]) + dot(mate[...], w1[...])).astype(BF16)
+
+
+def project_ahead(owns, mate, w0, w1):
     return pl.pallas_call(
         ahead_kernel,
         in_specs=[FULL] * 4,
@@ -582,7 +618,26 @@
         compiler_params=params(16),
         cost_estimate=CHEAP,
         name="project_ahead",
-    )(owns, mates, w0, w1)
+    )(owns, mate, w0, w1)
+
+
+def join_kernel(first, second, _, out):
+    rows = first.shape[0]
+    out[0:rows, :] = first[...]
+    out[rows:, :] = second[...]
+
+
+def join(first, second, token):
+    rows, depth = first.shape
+    return pl.pallas_call(
+        join_kernel,
+        in_specs=[FULL, FULL, ANY],
+        out_specs=FULL,
+        out_shape=jax.ShapeDtypeStruct((2 * rows, depth), BF16),
+        compiler_params=params(8),
+        cost_estimate=CHEAP,
+        name="join",
+    )(first, second, token)
 
 
 def both_kernel(base, cut, owns, mates, w0_far, w1_far, *refs):
@@ -747,18 +802,18 @@
     bc = bc_input.reshape(length, -1)
     (weight_mate,) = far(swap(out_weight, "head", 1))
 
-    (cum, cum_s, log_s, f_dev, f_blk, e_blk, rates), ones, x_near = decays(
+    (cum, cum_s, log_s, f_dev, f_blk, e_blk, rates), ones, wide_ones, x_sent = decays(
         info, log_decay, step_size, skip_gain, x_input, half
     )
     taps = far(conv_weight_x, conv_weight_bc)
-    shared = (info, x_near, bc, halo, *taps)
-    x0, bc0, send = conv_states(0, *shared, f_dev[0], ones, rates[0])
+    shared = (bc, halo, *taps)
+    x0, bc0, send, x_kept = conv_states(0, info, x_sent, *shared, f_dev[0], ones, rates[0], x_far)
     got = swap(send, "seq", 1)
-    x1, bc1, keep, z_near = conv_states(1, *shared, f_dev[1], ones, rates[1], z_far)
+    x1, bc1, keep, z_near = conv_states(1, info, x_kept, *shared, f_dev[1], ones, rates[1], z_far)
     rates_kept = rates[1]
 
     uvs = []
-    groups = [(x, z_near, *rest, ones) for x, *rest in zip((x0, x1), (bc0, bc1), cum, cum_s, log_s, f_blk, e_blk, rates)]
+    groups = [(x, z_near, *rest, ones, wide_ones) for x, *rest in zip((x0, x1), (bc0, bc1), cum, cum_s, log_s, f_blk, e_blk, rates)]
 
     def scan_next(token):
         if len(uvs) < 2 * B_PARTS:
@@ -768,7 +823,7 @@
 
     full = ((N, half), F32)
     message = ((N + EXTRA, half), BF16)
-    done = keep
+    done = scan_next(keep)
     out = ((N, half), BF16)
     if pairs > 1 and half % (pairs * N) == 0:
         piece = half // pairs
@@ -782,7 +837,7 @@
             [pltpu.VMEM(*message)],
         )
         parts = list(parts[:1]) + [rotate(parts[r], 2 * r) for r in range(1, pairs)]
-        done = scan_next(scan_next(parts[0]))
+        done = scan_next(parts[0])
         parts = combine(
             owner_kernel,
             [info] + parts + [done],
@@ -815,10 +870,12 @@
     chunk = columns // 8
     weights = (w_far, weight_mate)
     shared = ((bc0, bc1), (other, held), gain, uvs)
-    (mates,) = norm_rows((0, 2), info, count, held, *shared)
-    owns, w0, w1 = norm_rows((1, 3), info, count, mates, *shared, weights, chunk)
-    operands = (owns, swap(mates, "head", 1), *weights)
-    first = swap(project_ahead(*operands[:2], w0, w1), "head", 2)
+    far_mate, near_mate = norm_rows((0, 2), True, info, count, held, *shared)
+    owns, w0, w1 = norm_rows((1, 3), False, info, count, far_mate, *shared, weights, chunk)
+    far_mate = swap(far_mate, "head", 1)
+    sent = project_ahead(owns, far_mate, w0, w1)
+    first = swap(sent, "head", 2)
+    operands = (owns, join(far_mate, swap(near_mate, "head", 1), sent), *weights)
     calls = []
     for lo, hi in ((1, 2), (2, 4), (4, 6), (6, 8)):
         sent, near = project_both(*operands, lo * chunk, (hi - lo) * chunk, chunk)

time: 114 us -> 115 us (level)
  Pallas kernels: 76 us -> 81 us
  waiting for transfers between devices: 14.9 us -> 9.99 us
    ppermute x12 -> x13, waiting for transfers between devices: 13.7 us -> 8.48 us  [swap(): lax.ppermute(block, axis, [(i, i ^ bit) for i in range(lax.axis_size(axis...]
    pallas_call x4, Pallas kernels: 17.5 us -> 22.6 us  [scan_part(): pl.pallas_call(functools.partial(scan_kernel, order, part), in_specs=[SCA...]
    ppermute x12 -> x13, starting transfers between devices: 10.6 us -> 11 us  [swap(): lax.ppermute(block, axis, [(i, i ^ bit) for i in range(lax.axis_size(axis...]
  transfers between devices with their start and end apart: 19 -> 20, of which waited for: 7 -> 4; matrix products, arithmetic and copies ran while one was open for 0% -> 0% of each run, Pallas kernels for 65% -> 70%
where the time goes in v14:
time: 115 us
  Pallas kernels  81 us (70%)
  starting transfers between devices  23.1 us (20%)
  waiting for transfers between devices  9.99 us (9%)
    pallas_call x4, Pallas kernels, project_both(): pl.pallas_call(functools.partial(both_kernel, first // TILE, cut), grid=(...  25.4 us
    pallas_call x4, Pallas kernels, scan_part(): pl.pallas_call(functools.partial(scan_kernel, order, part), in_specs=[SCA...  22.6 us
    ppermute x7, starting transfers between devices, rotate(): lax.ppermute(block, 'seq', [(i, (i + distance) % size) for i in range(siz...  12 us
    ppermute x13, starting transfers between devices, swap(): lax.ppermute(block, axis, [(i, i ^ bit) for i in range(lax.axis_size(axis...  11 us
    pallas_call x2, Pallas kernels, conv_states(): pl.pallas_call(functools.partial(conv_kernel, order), grid_spec=pltpu.Pre...  10.9 us
    ppermute x13, waiting for transfers between devices, swap(): lax.ppermute(block, axis, [(i, i ^ bit) for i in range(lax.axis_size(axis...  8.48 us
    pallas_call x2, Pallas kernels, norm_rows(): pl.pallas_call(functools.partial(norm_kernel, places, len(weights)), in_s...  5.32 us
    pallas_call x1, Pallas kernels, decays(): pl.pallas_call(decay_kernel, in_specs=[SCALAR] + [FULL] * 3 + [FAR], out_...  4.32 us
  transfers between devices with their start and end apart: 20, of which 4 were waited for; matrix products, arithmetic and copies ran while one was open for 0% of the time, Pallas kernels for 70%

profile of v14, /device:TPU:0, one launch (start us, length us, event | category | flops | bytes accessed | tf_op | source)
XLA Modules:
  0.0 114.6 jit_solution(12962308617492770468)
XLA Ops:
  1.3 2.6 %collective-permute-start = (bf16[16,2560]{1,0:T(8,128)(2,1)S(1)}, bf16[16,2560]{1,0:T(8,128)(2,1)S(1)}, u32[]{:S(2)}, u32[]{:S(2)}) collective-permute-start(bf16[16,2560]{1,0:T(8,128)(2,1)S(1)} %tail_rows.1), channel_id=1, source_target_pairs={{0,4},{4,8},{8,12},{12,16},{16,20},{20,24},{24,28},{28,0},{1,5},{5... | collective-permute-start | bytes 245768 | tf_op jit(solution)/shard_map/ppermute | solution.py:736
  4.0 4.3 %decays.1 = (bf16[1024,48]{1,0:T(8,128)(2,1)S(1)}, bf16[1024,48]{1,0:T(8,128)(2,1)S(1)}, f32[16,1024]{1,0:T(8,128)S(1)}, f32[16,1024]{1,0:T(8,128)S(1)}, f32[16,...) custom-call(s32[9]{0:T(128)S(1)} %stack.36.info, ...), custom_call_target="tpu_custom_call" | custom-call | flops 1 | bytes 1 | tf_op jit(solution)/shard_map/decays/pallas_call | solution.py:161
  10.1 5.5 %conv_states.2 = (bf16[1024,1024]{1,0:T(8,128)(2,1)S(1)}, bf16[1024,256]{1,0:T(8,128)(2,1)S(1)}, bf16[144,1024]{1,0:T(8,128)(2,1)S(1)}, bf16[1024,1024]{1,0:T(8,128)(2,1)S(1)}) custom-call(s32[9]{0:T(128)S(1)} %stack.36.info, bf16[1024,1024]{1,0:T(8,128)(2,1)S(1)} %get-tuple-element.58.x, bf16[1024,512]{1,0:T(8,128)(2,1)S(1)} %bitcast.14, ...), custom_call_target="tpu_custom_call" | custom-call | flops 1 | bytes 1 | tf_op jit(solution)/shard_map/conv_states/pallas_call | solution.py:303
  15.6 5.5 %conv_states.3 = (bf16[1024,1024]{1,0:T(8,128)(2,1)S(1)}, bf16[1024,256]{1,0:T(8,128)(2,1)S(1)}, f32[128,1024]{1,0:T(8,128)S(1)}, bf16[1024,2048]{1,0:T(8,128)(2,1)S(1)}) custom-call(s32[9]{0:T(128)S(1)} %stack.36.info, bf16[1024,1024]{1,0:T(8,128)(2,1)S(1)} %get-tuple-element.63.x, bf16[1024,512]{1,0:T(8,128)(2,1)S(1)} %bitcast.15, ...), custom_call_target="tpu_custom_call" | custom-call | flops 1 | bytes 1 | tf_op jit(solution)/shard_map/conv_states/pallas_call | solution.py:303
  21.1 5.7 %scan_part.4._.refs_0_ = bf16[1024,1024]{1,0:T(8,128)(2,1)S(1)} custom-call(s32[9]{0:T(128)S(1)} %stack.36.info, bf16[1024,1024]{1,0:T(8,128)(2,1)S(1)} %get-tuple-element.69.x, bf16[1024,2048]{1,0:T(8,128)(2,1)S(1)} %get-tuple-element.70.z, bf16[1024,256]{1,0:T(8,128)(2,1)S(1)} %get-tuple-element.62.bc.bc0, bf16[1024,48]{1,0:T(8,128)(2,1)S(1)} %get-tuple-element.71.cum, ...), custom_call_target="tpu_custom_call" | custom-call | flops 1 | bytes 1 | tf_op jit(solution)/shard_map/scan_part/pallas_call | solution.py:499
  27.7 1.6 %collective-permute-start.2 = (bf16[144,256]{1,0:T(8,128)(2,1)S(1)}, bf16[144,256]{1,0:T(8,128)(2,1)S(1)}, u32[]{:S(2)}, u32[]{:S(2)}) collective-permute-start(bf16[144,256]{1,0:T(8,128)(2,1)S(1)} %get-tuple-element.86), channel_id=1, source_target_pairs={{0,8},{4,12},{8,16},{12,20},{16,24},{20,28},{24,0},{28,4},{1,9},{5... | collective-permute-start | bytes 221192 | tf_op jit(solution)/shard_map/ppermute | solution.py:736
  30.6 2.7 %collective-permute-start.4 = (bf16[144,256]{1,0:T(8,128)(2,1)S(1)}, bf16[144,256]{1,0:T(8,128)(2,1)S(1)}, u32[]{:S(2)}, u32[]{:S(2)}) collective-permute-start(bf16[144,256]{1,0:T(8,128)(2,1)S(1)} %get-tuple-element.88), channel_id=1, source_target_pairs={{0,24},{4,28},{8,0},{12,4},{16,8},{20,12},{24,16},{28,20},{1,25},{... | collective-permute-start | bytes 221192 | tf_op jit(solution)/shard_map/ppermute | solution.py:736
  33.3 5.6 %scan_part.5.refs_4_.refs_1_ = bf16[1024,1024]{1,0:T(8,128)(2,1)S(1)} custom-call(s32[9]{0:T(128)S(1)} %stack.36.info, bf16[1024,1024]{1,0:T(8,128)(2,1)S(1)} %get-tuple-element.69.x, bf16[1024,2048]{1,0:T(8,128)(2,1)S(1)} %get-tuple-element.70.z, bf16[1024,256]{1,0:T(8,128)(2,1)S(1)} %get-tuple-element.62.bc.bc0, ...), custom_call_target="tpu_custom_call" | custom-call | flops 1 | bytes 1 | tf_op jit(solution)/shard_map/scan_part/pallas_call | solution.py:499
  39.7 1.9 %collective-permute-start.6 = (bf16[128,256]{1,0:T(8,128)(2,1)S(1)}, bf16[128,256]{1,0:T(8,128)(2,1)S(1)}, u32[]{:S(2)}, u32[]{:S(2)}) collective-permute-start(bf16[128,256]{1,0:T(8,128)(2,1)S(1)} %get-tuple-element.91), channel_id=1, source_target_pairs={{0,16},{4,20},{8,24},{12,28},{16,0},{20,4},{24,8},{28,12},{1,17},{... | collective-permute-start | bytes 196616 | tf_op jit(solution)/shard_map/ppermute | solution.py:736
  41.5 1.9 %collective-permute-start.7 = (bf16[128,256]{1,0:T(8,128)(2,1)S(1)}, bf16[128,256]{1,0:T(8,128)(2,1)S(1)}, u32[]{:S(2)}, u32[]{:S(2)}) collective-permute-start(bf16[128,256]{1,0:T(8,128)(2,1)S(1)} %get-tuple-element.92), channel_id=1, source_target_pairs={{0,24},{4,28},{8,0},{12,4},{16,8},{20,12},{24,16},{28,20},{1,25},{... | collective-permute-start | bytes 196616 | tf_op jit(solution)/shard_map/ppermute | solution.py:736
  43.5 5.7 %scan_part.6._.refs_2_ = bf16[1024,1024]{1,0:T(8,128)(2,1)S(1)} custom-call(s32[9]{0:T(128)S(1)} %stack.36.info, bf16[1024,1024]{1,0:T(8,128)(2,1)S(1)} %get-tuple-element.79.x, bf16[1024,2048]{1,0:T(8,128)(2,1)S(1)} %get-tuple-element.70.z, bf16[1024,256]{1,0:T(8,128)(2,1)S(1)} %get-tuple-element.66.bc.bc1, bf16[1024,48]{1,0:T(8,128)(2,1)S(1)} %get-tuple-element.80.cum, ...), custom_call_target="tpu_custom_call" | custom-call | flops 1 | bytes 1 | tf_op jit(solution)/shard_map/scan_part/pallas_call | solution.py:499
  51.4 5.7 %scan_part.7.refs_3_ = bf16[1024,1024]{1,0:T(8,128)(2,1)S(1)} custom-call(s32[9]{0:T(128)S(1)} %stack.36.info, bf16[1024,1024]{1,0:T(8,128)(2,1)S(1)} %get-tuple-element.79.x, bf16[1024,2048]{1,0:T(8,128)(2,1)S(1)} %get-tuple-element.70.z, bf16[1024,256]{1,0:T(8,128)(2,1)S(1)} %get-tuple-element.66.bc.bc1, bf16[1024,48]{1,0:T(8,128)(2,1)S(1)} %get-tuple-element.80.cum, ...), custom_call_target="tpu_custom_call" | custom-call | flops 1 | bytes 1 | tf_op jit(solution)/shard_map/scan_part/pallas_call | solution.py:499
  57.1 2.5 %norm_rows.2 = (bf16[256,2048]{1,0:T(8,128)(2,1)S(1)}, bf16[256,2048]{1,0:T(8,128)(2,1)S(1)}) custom-call(s32[9]{0:T(128)S(1)} %stack.36.info, bf16[1024,256]{1,0:T(8,128)(2,1)S(1)} %get-tuple-element.62.bc.bc0, bf16[1024,256]{1,0:T(8,128)(2,1)S(1)} %get-tuple-element.66.bc.bc1, bf16[128,1024]{1,0:T(8,128)(2,1)S(1)} %collective-permute-done.8.state0, ...), custom_call_target="tpu_custom_call" | custom-call | flops 1 | bytes 1 | tf_op jit(solution)/shard_map/norm_rows/pallas_call | solution.py:559
  60.3 2.8 %norm_rows.3 = (bf16[512,2048]{1,0:T(8,128)(2,1)S(1)}, bf16[2048,512]{1,0:T(8,128)(2,1)S(1)}, bf16[2048,512]{1,0:T(8,128)(2,1)S(1)}) custom-call(s32[9]{0:T(128)S(1)} %stack.36.info, bf16[1024,256]{1,0:T(8,128)(2,1)S(1)} %get-tuple-element.62.bc.bc0, bf16[1024,256]{1,0:T(8,128)(2,1)S(1)} %get-tuple-element.66.bc.bc1, ...), custom_call_target="tpu_custom_call" | custom-call | flops 1 | bytes 1 | tf_op jit(solution)/shard_map/norm_rows/pallas_call | solution.py:559
  64.3 1.6 %collective-permute-start.19 = (bf16[256,512]{1,0:T(8,128)(2,1)S(1)}, bf16[256,512]{1,0:T(8,128)(2,1)S(1)}, u32[]{:S(2)}, u32[]{:S(2)}) collective-permute-start(bf16[256,512]{1,0:T(8,128)(2,1)S(1)} %project_ahead.1._), channel_id=1, source_target_pairs={{0,2},{1,3},{2,0},{3,1},{4,6},{5,7},{6,4},{7,5},{8,10},{9,11},{10,... | collective-permute-start | bytes 786440 | tf_op jit(solution)/shard_map/ppermute | solution.py:731
  66.0 4.3 %project_both.7 = (bf16[256,512]{1,0:T(8,128)(2,1)S(1)}, f32[256,512]{1,0:T(8,128)S(1)}) custom-call(bf16[512,2048]{1,0:T(8,128)(2,1)S(1)} %get-tuple-element.96.owns, bf16[512,2048]{1,0:T(8,128)(2,1)S(1)} %join.1.mates, bf16[2048,4096]{1,0:T(8,128)(2,1)} %w0_far.9, bf16[2048,4096]{1,0:T(8,128)(2,1)} %collective-permute-done.9.refs_5_.w1_far), custom_call_target="tpu_custom_call" | custom-call | flops 1 | bytes 1 | tf_op jit(solution)/shard_map/project_both/pallas_call | solution.py:664
  71.0 7.0 %project_both.6 = (bf16[256,512]{1,0:T(8,128)(2,1)S(1)}, bf16[256,512]{1,0:T(8,128)(2,1)S(1)}, f32[256,1024]{1,0:T(8,128)S(1)}) custom-call(bf16[512,2048]{1,0:T(8,128)(2,1)S(1)} %get-tuple-element.96.owns, bf16[512,2048]{1,0:T(8,128)(2,1)S(1)} %join.1.mates, bf16[2048,4096]{1,0:T(8,128)(2,1)} %w0_far.9, bf16[2048,4096]{1,0:T(8,128)(2,1)} %collective-permute-done.9.refs_5_.w1_far), custom_call_target="tpu_custom_call" | custom-call | flops 1 | bytes 1 | tf_op jit(solution)/shard_map/project_both/pallas_call | solution.py:664
  78.0 1.6 %collective-permute-start.16 = (bf16[256,512]{1,0:T(8,128)(2,1)S(1)}, bf16[256,512]{1,0:T(8,128)(2,1)S(1)}, u32[]{:S(2)}, u32[]{:S(2)}) collective-permute-start(bf16[256,512]{1,0:T(8,128)(2,1)S(1)} %get-tuple-element.107), channel_id=1, source_target_pairs={{0,2},{1,3},{2,0},{3,1},{4,6},{5,7},{6,4},{7,5},{8,10},{9,11},{10,... | collective-permute-start | bytes 786440 | tf_op jit(solution)/shard_map/ppermute | solution.py:731
  80.1 7.0 %project_both.5 = (bf16[256,512]{1,0:T(8,128)(2,1)S(1)}, bf16[256,512]{1,0:T(8,128)(2,1)S(1)}, f32[256,1024]{1,0:T(8,128)S(1)}) custom-call(bf16[512,2048]{1,0:T(8,128)(2,1)S(1)} %get-tuple-element.96.owns, bf16[512,2048]{1,0:T(8,128)(2,1)S(1)} %join.1.mates, bf16[2048,4096]{1,0:T(8,128)(2,1)} %w0_far.9, bf16[2048,4096]{1,0:T(8,128)(2,1)} %collective-permute-done.9.refs_5_.w1_far), custom_call_target="tpu_custom_call" | custom-call | flops 1 | bytes 1 | tf_op jit(solution)/shard_map/project_both/pallas_call | solution.py:664
  87.1 1.6 %collective-permute-start.14 = (bf16[256,512]{1,0:T(8,128)(2,1)S(1)}, bf16[256,512]{1,0:T(8,128)(2,1)S(1)}, u32[]{:S(2)}, u32[]{:S(2)}) collective-permute-start(bf16[256,512]{1,0:T(8,128)(2,1)S(1)} %get-tuple-element.104), channel_id=1, source_target_pairs={{0,2},{1,3},{2,0},{3,1},{4,6},{5,7},{6,4},{7,5},{8,10},{9,11},{10,... | collective-permute-start | bytes 786440 | tf_op jit(solution)/shard_map/ppermute | solution.py:731
  88.7 7.0 %project_both.4 = (bf16[256,512]{1,0:T(8,128)(2,1)S(1)}, bf16[256,512]{1,0:T(8,128)(2,1)S(1)}, f32[256,1024]{1,0:T(8,128)S(1)}) custom-call(bf16[512,2048]{1,0:T(8,128)(2,1)S(1)} %get-tuple-element.96.owns, bf16[512,2048]{1,0:T(8,128)(2,1)S(1)} %join.1.mates, bf16[2048,4096]{1,0:T(8,128)(2,1)} %w0_far.9, bf16[2048,4096]{1,0:T(8,128)(2,1)} %collective-permute-done.9.refs_5_.w1_far), custom_call_target="tpu_custom_call" | custom-call | flops 1 | bytes 1 | tf_op jit(solution)/shard_map/project_both/pallas_call | solution.py:664
  98.3 3.8 %project_near.1.refs_1_ = bf16[256,4096]{1,0:T(8,128)(2,1)} custom-call(bf16[512,2048]{1,0:T(8,128)(2,1)S(1)} %get-tuple-element.96.owns, bf16[512,2048]{1,0:T(8,128)(2,1)S(1)} %join.1.mates, bf16[2048,4096]{1,0:T(8,128)(2,1)} %w0_far.9, bf16[2048,4096]{1,0:T(8,128)(2,1)} %collective-permute-done.9.refs_5_.w1_far, ...), custom_call_target="tpu_custom_call" | custom-call | flops 1 | bytes 1 | tf_op jit(solution)/shard_map/project_near/pallas_call | solution.py:688
  105.9 4.7 %collective-permute-done.13.refs_0_ = bf16[256,512]{1,0:T(8,128)(2,1)S(1)} collective-permute-done((bf16[256,512]{1,0:T(8,128)(2,1)S(1)}, bf16[256,512]{1,0:T(8,128)(2,1)S(1)}, u32[]{:S(2)}, u32[]{:S(2)}) %collective-permute-start.13) | collective-permute-done | bytes 262176 | tf_op jit(solution)/shard_map/ppermute | solution.py:731
  111.4 2.5 %collective-permute-done.12.refs_0_ = bf16[256,512]{1,0:T(8,128)(2,1)S(1)} collective-permute-done((bf16[256,512]{1,0:T(8,128)(2,1)S(1)}, bf16[256,512]{1,0:T(8,128)(2,1)S(1)}, u32[]{:S(2)}, u32[]{:S(2)}) %collective-permute-start.12) | collective-permute-done | bytes 262176 | tf_op jit(solution)/shard_map/ppermute | solution.py:731
  (47 shorter events, 19.4 us)
Async XLA Ops:
  0.0 60.3 %collective-permute-start.9 = (bf16[2048,4096]{1,0:T(8,128)(2,1)}, bf16[2048,4096]{1,0:T(8,128)(2,1)}, u32[]{:S(2)}, u32[]{:S(2)}) collective-permute-start(bf16[2048,4096]{1,0:T(8,128)(2,1)} %w0_far.9), channel_id=1, source_target_pairs={{0,1},{1,0},{2,3},{3,2},{4,5},{5,4},{6,7},{7,6},{8,9},{9,8},{10,11... | collective-permute-start | bytes 50331656 | tf_op jit(solution)/shard_map/ppermute | solution.py:731
  1.3 8.7 %collective-permute-start = (bf16[16,2560]{1,0:T(8,128)(2,1)S(1)}, bf16[16,2560]{1,0:T(8,128)(2,1)S(1)}, u32[]{:S(2)}, u32[]{:S(2)}) collective-permute-start(bf16[16,2560]{1,0:T(8,128)(2,1)S(1)} %tail_rows.1), channel_id=1, source_target_pairs={{0,4},{4,8},{8,12},{12,16},{16,20},{20,24},{24,28},{28,0},{1,5},{5... | collective-permute-start | bytes 245768 | tf_op jit(solution)/shard_map/ppermute | solution.py:736
  4.0 4.3 %copy-start.1 = (bf16[1024,2,256]{2,1,0:T(2,128)(2,1)S(1)}, bf16[1024,2,256]{2,1,0:T(2,128)(2,1)}, u32[]{:S(2)}) copy-start(bf16[1024,2,256]{2,1,0:T(2,128)(2,1)} %bc.1) | copy-start | bytes 3145732
  15.5 11.3 %collective-permute-start.1 = (bf16[144,1024]{1,0:T(8,128)(2,1)S(1)}, bf16[144,1024]{1,0:T(8,128)(2,1)S(1)}, u32[]{:S(2)}, u32[]{:S(2)}) collective-permute-start(bf16[144,1024]{1,0:T(8,128)(2,1)S(1)} %get-tuple-element.67), channel_id=1, source_target_pairs={{0,4},{4,0},{8,12},{12,8},{16,20},{20,16},{24,28},{28,24},{1,5},{5... | collective-permute-start | bytes 884744 | tf_op jit(solution)/shard_map/ppermute | solution.py:731
  27.7 11.2 %collective-permute-start.2 = (bf16[144,256]{1,0:T(8,128)(2,1)S(1)}, bf16[144,256]{1,0:T(8,128)(2,1)S(1)}, u32[]{:S(2)}, u32[]{:S(2)}) collective-permute-start(bf16[144,256]{1,0:T(8,128)(2,1)S(1)} %get-tuple-element.86), channel_id=1, source_target_pairs={{0,8},{4,12},{8,16},{12,20},{16,24},{20,28},{24,0},{28,4},{1,9},{5... | collective-permute-start | bytes 221192 | tf_op jit(solution)/shard_map/ppermute | solution.py:736
  29.3 9.6 %collective-permute-start.3 = (bf16[144,256]{1,0:T(8,128)(2,1)S(1)}, bf16[144,256]{1,0:T(8,128)(2,1)S(1)}, u32[]{:S(2)}, u32[]{:S(2)}) collective-permute-start(bf16[144,256]{1,0:T(8,128)(2,1)S(1)} %get-tuple-element.87), channel_id=1, source_target_pairs={{0,16},{4,20},{8,24},{12,28},{16,0},{20,4},{24,8},{28,12},{1,17},{... | collective-permute-start | bytes 221192 | tf_op jit(solution)/shard_map/ppermute | solution.py:736
  30.6 8.4 %collective-permute-start.4 = (bf16[144,256]{1,0:T(8,128)(2,1)S(1)}, bf16[144,256]{1,0:T(8,128)(2,1)S(1)}, u32[]{:S(2)}, u32[]{:S(2)}) collective-permute-start(bf16[144,256]{1,0:T(8,128)(2,1)S(1)} %get-tuple-element.88), channel_id=1, source_target_pairs={{0,24},{4,28},{8,0},{12,4},{16,8},{20,12},{24,16},{28,20},{1,25},{... | collective-permute-start | bytes 221192 | tf_op jit(solution)/shard_map/ppermute | solution.py:736
  39.6 9.6 %collective-permute-start.5 = (bf16[128,256]{1,0:T(8,128)(2,1)S(1)}, bf16[128,256]{1,0:T(8,128)(2,1)S(1)}, u32[]{:S(2)}, u32[]{:S(2)}) collective-permute-start(bf16[128,256]{1,0:T(8,128)(2,1)S(1)} %get-tuple-element.90), channel_id=1, source_target_pairs={{0,8},{4,12},{8,16},{12,20},{16,24},{20,28},{24,0},{28,4},{1,9},{5... | collective-permute-start | bytes 196616 | tf_op jit(solution)/shard_map/ppermute | solution.py:736
  39.7 9.5 %collective-permute-start.6 = (bf16[128,256]{1,0:T(8,128)(2,1)S(1)}, bf16[128,256]{1,0:T(8,128)(2,1)S(1)}, u32[]{:S(2)}, u32[]{:S(2)}) collective-permute-start(bf16[128,256]{1,0:T(8,128)(2,1)S(1)} %get-tuple-element.91), channel_id=1, source_target_pairs={{0,16},{4,20},{8,24},{12,28},{16,0},{20,4},{24,8},{28,12},{1,17},{... | collective-permute-start | bytes 196616 | tf_op jit(solution)/shard_map/ppermute | solution.py:736
  41.5 7.6 %collective-permute-start.7 = (bf16[128,256]{1,0:T(8,128)(2,1)S(1)}, bf16[128,256]{1,0:T(8,128)(2,1)S(1)}, u32[]{:S(2)}, u32[]{:S(2)}) collective-permute-start(bf16[128,256]{1,0:T(8,128)(2,1)S(1)} %get-tuple-element.92), channel_id=1, source_target_pairs={{0,24},{4,28},{8,0},{12,4},{16,8},{20,12},{24,16},{28,20},{1,25},{... | collective-permute-start | bytes 196616 | tf_op jit(solution)/shard_map/ppermute | solution.py:736
  50.0 7.2 %copy-start = (f32[2048]{0:T(1024)S(1)}, f32[2048]{0:T(1024)}, u32[]{:S(2)}) copy-start(f32[2048]{0:T(1024)} %param.18) | copy-start | bytes 24580
  50.0 7.2 %collective-permute-start.8 = (bf16[128,1024]{1,0:T(8,128)(2,1)S(1)}, bf16[128,1024]{1,0:T(8,128)(2,1)S(1)}, u32[]{:S(2)}, u32[]{:S(2)}) collective-permute-start(bf16[128,1024]{1,0:T(8,128)(2,1)S(1)} %get-tuple-element.93._), channel_id=1, source_target_pairs={{0,4},{4,0},{8,12},{12,8},{16,20},{20,16},{24,28},{28,24},{1,5},{5... | collective-permute-start | bytes 786440 | tf_op jit(solution)/shard_map/ppermute | solution.py:731
  59.7 3.4 %collective-permute-start.10 = (bf16[256,2048]{1,0:T(8,128)(2,1)S(1)}, bf16[256,2048]{1,0:T(8,128)(2,1)S(1)}, u32[]{:S(2)}, u32[]{:S(2)}) collective-permute-start(bf16[256,2048]{1,0:T(8,128)(2,1)S(1)} %get-tuple-element.95._), channel_id=1, source_target_pairs={{0,1},{1,0},{2,3},{3,2},{4,5},{5,4},{6,7},{7,6},{8,9},{9,8},{10,11... | collective-permute-start | bytes 3145736 | tf_op jit(solution)/shard_map/ppermute | solution.py:731
  59.8 6.1 %collective-permute-start.11 = (bf16[256,2048]{1,0:T(8,128)(2,1)S(1)}, bf16[256,2048]{1,0:T(8,128)(2,1)S(1)}, u32[]{:S(2)}, u32[]{:S(2)}) collective-permute-start(bf16[256,2048]{1,0:T(8,128)(2,1)S(1)} %get-tuple-element.97), channel_id=1, source_target_pairs={{0,1},{1,0},{2,3},{3,2},{4,5},{5,4},{6,7},{7,6},{8,9},{9,8},{10,11... | collective-permute-start | bytes 3145736 | tf_op jit(solution)/shard_map/ppermute | solution.py:731
  64.3 31.3 %collective-permute-start.19 = (bf16[256,512]{1,0:T(8,128)(2,1)S(1)}, bf16[256,512]{1,0:T(8,128)(2,1)S(1)}, u32[]{:S(2)}, u32[]{:S(2)}) collective-permute-start(bf16[256,512]{1,0:T(8,128)(2,1)S(1)} %project_ahead.1._), channel_id=1, source_target_pairs={{0,2},{1,3},{2,0},{3,1},{4,6},{5,7},{6,4},{7,5},{8,10},{9,11},{10,... | collective-permute-start | bytes 786440 | tf_op jit(solution)/shard_map/ppermute | solution.py:731
  70.3 25.9 %collective-permute-start.18 = (bf16[256,512]{1,0:T(8,128)(2,1)S(1)}, bf16[256,512]{1,0:T(8,128)(2,1)S(1)}, u32[]{:S(2)}, u32[]{:S(2)}) collective-permute-start(bf16[256,512]{1,0:T(8,128)(2,1)S(1)} %get-tuple-element.110), channel_id=1, source_target_pairs={{0,2},{1,3},{2,0},{3,1},{4,6},{5,7},{6,4},{7,5},{8,10},{9,11},{10,... | collective-permute-start | bytes 786440 | tf_op jit(solution)/shard_map/ppermute | solution.py:731
  78.0 19.8 %collective-permute-start.16 = (bf16[256,512]{1,0:T(8,128)(2,1)S(1)}, bf16[256,512]{1,0:T(8,128)(2,1)S(1)}, u32[]{:S(2)}, u32[]{:S(2)}) collective-permute-start(bf16[256,512]{1,0:T(8,128)(2,1)S(1)} %get-tuple-element.107), channel_id=1, source_target_pairs={{0,2},{1,3},{2,0},{3,1},{4,6},{5,7},{6,4},{7,5},{8,10},{9,11},{10,... | collective-permute-start | bytes 786440 | tf_op jit(solution)/shard_map/ppermute | solution.py:731
  79.5 23.4 %collective-permute-start.17 = (bf16[256,512]{1,0:T(8,128)(2,1)S(1)}, bf16[256,512]{1,0:T(8,128)(2,1)S(1)}, u32[]{:S(2)}, u32[]{:S(2)}) collective-permute-start(bf16[256,512]{1,0:T(8,128)(2,1)S(1)} %get-tuple-element.108), channel_id=1, source_target_pairs={{0,2},{1,3},{2,0},{3,1},{4,6},{5,7},{6,4},{7,5},{8,10},{9,11},{10,... | collective-permute-start | bytes 786440 | tf_op jit(solution)/shard_map/ppermute | solution.py:731
  87.1 16.7 %collective-permute-start.14 = (bf16[256,512]{1,0:T(8,128)(2,1)S(1)}, bf16[256,512]{1,0:T(8,128)(2,1)S(1)}, u32[]{:S(2)}, u32[]{:S(2)}) collective-permute-start(bf16[256,512]{1,0:T(8,128)(2,1)S(1)} %get-tuple-element.104), channel_id=1, source_target_pairs={{0,2},{1,3},{2,0},{3,1},{4,6},{5,7},{6,4},{7,5},{8,10},{9,11},{10,... | collective-permute-start | bytes 786440 | tf_op jit(solution)/shard_map/ppermute | solution.py:731
  95.7 9.3 %collective-permute-start.15 = (bf16[256,512]{1,0:T(8,128)(2,1)S(1)}, bf16[256,512]{1,0:T(8,128)(2,1)S(1)}, u32[]{:S(2)}, u32[]{:S(2)}) collective-permute-start(bf16[256,512]{1,0:T(8,128)(2,1)S(1)} %get-tuple-element.105), channel_id=1, source_target_pairs={{0,2},{1,3},{2,0},{3,1},{4,6},{5,7},{6,4},{7,5},{8,10},{9,11},{10,... | collective-permute-start | bytes 786440 | tf_op jit(solution)/shard_map/ppermute | solution.py:731
  96.3 14.3 %collective-permute-start.13 = (bf16[256,512]{1,0:T(8,128)(2,1)S(1)}, bf16[256,512]{1,0:T(8,128)(2,1)S(1)}, u32[]{:S(2)}, u32[]{:S(2)}) collective-permute-start(bf16[256,512]{1,0:T(8,128)(2,1)S(1)} %get-tuple-element.102), channel_id=1, source_target_pairs={{0,2},{1,3},{2,0},{3,1},{4,6},{5,7},{6,4},{7,5},{8,10},{9,11},{10,... | collective-permute-start | bytes 786440 | tf_op jit(solution)/shard_map/ppermute | solution.py:731
  97.8 16.1 %collective-permute-start.12 = (bf16[256,512]{1,0:T(8,128)(2,1)S(1)}, bf16[256,512]{1,0:T(8,128)(2,1)S(1)}, u32[]{:S(2)}, u32[]{:S(2)}) collective-permute-start(bf16[256,512]{1,0:T(8,128)(2,1)S(1)} %get-tuple-element.101), channel_id=1, source_target_pairs={{0,2},{1,3},{2,0},{3,1},{4,6},{5,7},{6,4},{7,5},{8,10},{9,11},{10,... | collective-permute-start | bytes 786440 | tf_op jit(solution)/shard_map/ppermute | solution.py:731

commit v15 on v14

--- a/solution.py
+++ b/solution.py
@@ -67,8 +67,8 @@
 
 
 def decay_kernel(info, ld_t, step_t, skip, x_far, *refs):
-    cum, cum_s, log_s, f_dev, f_blk, e_blk, rates = [refs[2 * k : 2 * k + 2] for k in range(7)]
-    ones, wide_ones, x, sem = refs[14:]
+    cum, cum_s, log_s, f_dev, f_blk, rates = [refs[2 * k : 2 * k + 2] for k in range(6)]
+    ones, x, sem = refs[12:]
     copies = group_copies(x_far, x, info[GROUP], sem)
     for copy in copies:
         copy.start()
@@ -94,25 +94,18 @@
             both = jnp.concatenate([high[own], low[own]], 0)
             ref[g][rows, :] = dot(eye, both, ((1,), (1,))).astype(BF16)
 
-    member = lax.broadcasted_iota(jnp.int32, (per, width), 0) == lax.broadcasted_iota(jnp.int32, (per, width), 1) // P_SIZE
-    member = member.astype(F32)
+    first = lax.broadcasted_iota(jnp.int32, (per, width), 0) * P_SIZE
+    lane = lax.broadcasted_iota(jnp.int32, (per, width), 1)
+    member = ((lane >= first) & (lane < first + P_SIZE)).astype(F32)
     ones[0:per, :] = member.astype(BF16)
     ones[per:, :] = member.astype(BF16)
-    shape = (per, per * TOK_B)
-    spread = lax.broadcasted_iota(jnp.int32, shape, 0) == lax.broadcasted_iota(jnp.int32, shape, 1) // TOK_B
-    for k in range(3):
-        wide_ones[k * per : (k + 1) * per, :] = spread.astype(F32).astype(BF16)
     cums, totals, row_totals = [], [], []
     for b in range(blocks):
         rows = slice(b * TOK_B, (b + 1) * TOK_B)
         logs = ordered(ld_t[:, rows]) * LOG2E
         c = dot(lower, logs, ((1,), (1,)), HIGHEST)
         for g in range(2):
-            rest = c[:, g * per : (g + 1) * per]
-            for k in range(3):
-                kept = rest.astype(BF16)
-                cum[g][rows, k * per : (k + 1) * per] = kept
-                rest = rest - kept.astype(F32)
+            cum[g][rows, :] = c[:, g * per : (g + 1) * per]
         row_totals.append(c[TOK_B - 1 : TOK_B, :])
         c = dot(logs, upper, precision=HIGHEST)
         cums.append(c)
@@ -133,13 +126,13 @@
         s = ordered(step_t[:, rows])
         log_step = jnp.log2(s)
         shifted = cums[b] - log_step
+        fade = jnp.exp2(totals[b] - cums[b]) * s
         for g in range(2):
             own = slice(g * per, (g + 1) * per)
             log_s[g][:, rows] = log_step[own, :]
             cum_s[g][:, rows] = shifted[own, :]
+            f_blk[g][:, rows] = fade[own, :]
         put(f_dev, rows, jnp.exp2(total - (cums[b] + before[b])) * s)
-        put(f_blk, rows, jnp.exp2(totals[b] - cums[b]) * s)
-        put(e_blk, rows, jnp.exp2(cums[b]))
     for copy in copies:
         copy.wait()
 
@@ -150,15 +143,14 @@
     per = heads // 2
     across = jax.ShapeDtypeStruct((per, length), F32)
     pair = jax.ShapeDtypeStruct((length, 2 * per), BF16)
-    column = jax.ShapeDtypeStruct((length, 3 * per), BF16)
+    column = jax.ShapeDtypeStruct((length, per), F32)
     rates = jax.ShapeDtypeStruct((2 * blocks + 16, width), F32)
-    shapes = [shape for shape in (column, across, across, pair, pair, pair, rates) for _ in range(2)]
+    shapes = [shape for shape in (column, across, across, pair, across, rates) for _ in range(2)]
     shapes += [
         jax.ShapeDtypeStruct((2 * per, width), BF16),
-        jax.ShapeDtypeStruct((3 * per, per * TOK_B), BF16),
         pltpu.VMEM((length, width), BF16),
     ]
-    *refs, ones, wide_ones, x_near = pl.pallas_call(
+    *refs, ones, x_near = pl.pallas_call(
         decay_kernel,
         in_specs=[SCALAR] + [FULL] * 3 + [FAR],
         out_specs=[FULL] * len(shapes),
@@ -168,7 +160,7 @@
         cost_estimate=CHEAP,
         name="decays",
     )(info, *far(log_decay.T, step.T, skip[None, :], x))
-    return [tuple(refs[2 * k : 2 * k + 2]) for k in range(7)], ones, wide_ones, x_near
+    return [tuple(refs[2 * k : 2 * k + 2]) for k in range(6)], ones, x_near
 
 
 def tail_kernel(x, bc, out):
@@ -234,14 +226,13 @@
     col = lax.broadcasted_iota(jnp.int32, down.shape, 1)
     down[...] = (row == col + 1).astype(BF16)
 
-    def conv(i, src, first, behind, weights, emit):
+    def conv(i, src, moved, first, behind, weights, emit):
         at_start = jnp.where(info[SEQ] == 0, jnp.zeros_like(first), first)
         lead = jnp.where(i == 0, at_start, behind).astype(F32)
         w0, w1, w2, w3 = [w * 0.5 for w in weights]
         back = LEAD - 8
         lead_r1 = pltpu.roll(lead, 1, 0)
         last_p = (w1 * lead + w0 * lead_r1)[back:]
-        moved = dot(down[...], src)
         top = lax.broadcasted_iota(jnp.int32, (8, lead.shape[1]), 0) == 0
         head = jnp.where(top, jnp.broadcast_to(lead[LEAD - 1 :], top.shape), moved[0:8])
         for r in range(0, rows, ROWS_A):
@@ -268,19 +259,21 @@
                 bc_out[out(r), ds] = value.astype(BF16)
 
             weights = [jnp.where(group == 0, wbc[k, 0:1, ds], wbc[k, 1:2, ds]) for k in range(KCONV)]
-            conv(i, bc[at, src], halo[:, halo_src], bc[behind, src], weights, emit_bc)
-
+            conv(i, bc[at, src], dot(down[...], bc[at, src]), halo[:, halo_src], bc[behind, src], weights, emit_bc)
+
+        all_moved = dot(down[...], x[at, :])
+        all_scale = dot(f_dev[at, :], ones[...])
         for lanes in range(0, width, SLAB):
             ds = slice(lanes, lanes + SLAB)
             src = pl.ds(pl.multiple_of(first_lane + lanes, SLAB), SLAB)
-            scale = dot(f_dev[at, :], ones[:, ds])
+            scale = all_scale[:, ds]
 
             def emit(r, value):
                 x_out[out(r), ds] = value.astype(BF16)
                 xf[r : r + ROWS_A, ds] = (value * scale[r : r + ROWS_A]).astype(BF16)
 
             weights = [wx[k : k + 1, ds] for k in range(KCONV)]
-            conv(i, x[at, ds], halo[:, src], x[behind, ds], weights, emit)
+            conv(i, x[at, ds], all_moved[:, ds], halo[:, src], x[behind, ds], weights, emit)
 
         state[...] += dot(bc_out[at, 0:N], xf[...], ((0,), (0,)))
         return 0
@@ -430,7 +423,7 @@
     )(*operands)
 
 
-def scan_kernel(order, part, info, x, z, bc, cum, cum_s, log_s, f_blk, e_blk, rates, ones, wide_ones, _, uv_out, state):
+def scan_kernel(order, part, info, x, z, bc, cum, cum_s, log_s, f_blk, rates, _, uv_out, state):
     length = x.shape[0]
     width = state.shape[1]
     per_slab = SLAB // P_SIZE
@@ -461,51 +454,53 @@
             lanes = slice(s * SLAB, (s + 1) * SLAB)
             xb = x[at, part * width + s * SLAB : part * width + (s + 1) * SLAB]
             wide = slice(part * width + s * SLAB, part * width + (s + 1) * SLAB)
-            sel = ones[:, wide]
             fade_row = rates[pl.ds(b, 1), wide]
             lead_row = rates[pl.ds(blocks + b, 1), wide]
             skip = rates[2 * blocks + 8 : 2 * blocks + 9, wide]
             old = state[:, lanes]
-            rise = dot(e_blk[at, :], sel)
-            carried = dot(c_mat, old.astype(BF16)) * rise
-            first_column = (first_head + s * per_slab) * TOK_B
-            columns = dot(cum[at, :], wide_ones[:, first_column : first_column + per_slab * TOK_B])
-            within = []
+            carried = dot(c_mat, old.astype(BF16))
+            within, grown, rises = [], [], []
             for q in range(per_slab // 2):
-                tables = []
+                tables, fades, columns = [], [], []
                 for h in (2 * q, 2 * q + 1):
                     head = first_head + s * per_slab + h
-                    column = columns[:, h * TOK_B : (h + 1) * TOK_B]
                     own = slice(head, head + 1)
+                    column = jnp.broadcast_to(cum[at, own], (TOK_B, TOK_B))
                     gap = jnp.minimum(column - cum_s[own, at], log_s[own, at])
                     tables.append((scores * jnp.exp2(gap)).astype(BF16))
+                    fades.append(b_across * f_blk[own, at].astype(BF16))
+                    columns.append(column)
                 xp = xb[:, q * 2 * P_SIZE : (q + 1) * 2 * P_SIZE]
                 stacked = jnp.concatenate([jnp.where(first, xp, zero), jnp.where(first, zero, xp)], 0)
-                within.append(dot(jnp.concatenate(tables, 1), stacked))
+                both = jnp.concatenate([jnp.concatenate(tables, 1), jnp.concatenate(fades, 1)], 0)
+                product = dot(both, stacked)
+                within.append(product[0:TOK_B])
+                grown.append(product[TOK_B:])
+                rises.append(jnp.exp2(jnp.where(first, columns[0], columns[1])))
+            rise = jnp.concatenate(rises, 1)
             xs = xb.astype(F32)
-            y = jnp.concatenate(within, 1) + carried + skip * xs
+            y = jnp.concatenate(within, 1) + carried * rise + skip * xs
             gate = half_silu((z[at, pl.ds(pl.multiple_of(first_lane + s * SLAB, SLAB), SLAB)] * 0.5).astype(F32))
             uv_out[at, lanes] = (y * gate).astype(BF16)
             uv_out[at, width + s * SLAB : width + (s + 1) * SLAB] = (gate * rise * lead_row).astype(BF16)
-            xf = (xs * dot(f_blk[at, :], sel)).astype(BF16)
-            state[:, lanes] = old * fade_row + dot(b_across, xf)
+            state[:, lanes] = old * fade_row + jnp.concatenate(grown, 1)
 
     lax.fori_loop(0, length // STEP_B, turn, 0)
 
 
-def scan_part(order, part, info, token, x, z, bc, cum, cum_s, log_s, f_blk, e_blk, rates, ones, wide_ones):
+def scan_part(order, part, info, token, x, z, bc, cum, cum_s, log_s, f_blk, rates):
     length, full = x.shape
     width = full // B_PARTS
     return pl.pallas_call(
         functools.partial(scan_kernel, order, part),
-        in_specs=[SCALAR] + [FULL] * 11 + [ANY],
+        in_specs=[SCALAR] + [FULL] * 8 + [ANY],
         out_specs=FULL,
         out_shape=pltpu.VMEM((length, 2 * width), BF16),
         scratch_shapes=[pltpu.VMEM((N, width), F32)],
         compiler_params=params(12),
         cost_estimate=CHEAP,
         name="scan_part",
-    )(info, x, z, bc, cum, cum_s, log_s, f_blk, e_blk, rates, ones, wide_ones, token)
+    )(info, x, z, bc, cum, cum_s, log_s, f_blk, rates, token)
 
 
 def norm_kernel(places, fetched, info, bc0, bc1, state0, state1, gain, _, *refs):
@@ -802,7 +797,7 @@
     bc = bc_input.reshape(length, -1)
     (weight_mate,) = far(swap(out_weight, "head", 1))
 
-    (cum, cum_s, log_s, f_dev, f_blk, e_blk, rates), ones, wide_ones, x_sent = decays(
+    (cum, cum_s, log_s, f_dev, f_blk, rates), ones, x_sent = decays(
         info, log_decay, step_size, skip_gain, x_input, half
     )
     taps = far(conv_weight_x, conv_weight_bc)
@@ -813,7 +808,7 @@
     rates_kept = rates[1]
 
     uvs = []
-    groups = [(x, z_near, *rest, ones, wide_ones) for x, *rest in zip((x0, x1), (bc0, bc1), cum, cum_s, log_s, f_blk, e_blk, rates)]
+    groups = list(zip((x0, x1), (z_near, z_near), (bc0, bc1), cum, cum_s, log_s, f_blk, rates))
 
     def scan_next(token):
         if len(uvs) < 2 * B_PARTS:

time: 115 us -> 112 us (0.974)
  Pallas kernels: 81 us -> 74 us
  waiting for transfers between devices: 9.99 us -> 14 us
    pallas_call x4, Pallas kernels: 22.6 us -> 15.8 us  [scan_part(): pl.pallas_call(functools.partial(scan_kernel, order, part), in_specs=[SCA...]
    ppermute x13, waiting for transfers between devices: 8.48 us -> 11.5 us  [swap(): lax.ppermute(block, axis, [(i, i ^ bit) for i in range(lax.axis_size(axis...]
  transfers between devices with their start and end apart: 20 -> 20, of which waited for: 4 -> 8; matrix products, arithmetic and copies ran while one was open for 0% -> 0% of each run, Pallas kernels for 70% -> 66%
where the time goes in v15:
time: 112 us; the launch traced here: 111 us
  Pallas kernels  74 us (66%)
  starting transfers between devices  22.5 us (20%)
  waiting for transfers between devices  14 us (12%)
    pallas_call x4, Pallas kernels, project_both(): pl.pallas_call(functools.partial(both_kernel, first // TILE, cut), grid=(...  25.4 us
    pallas_call x4, Pallas kernels, scan_part(): pl.pallas_call(functools.partial(scan_kernel, order, part), in_specs=[SCA...  15.8 us
    ppermute x7, starting transfers between devices, rotate(): lax.ppermute(block, 'seq', [(i, (i + distance) % size) for i in range(siz...  12.2 us
    ppermute x13, waiting for transfers between devices, swap(): lax.ppermute(block, axis, [(i, i ^ bit) for i in range(lax.axis_size(axis...  11.5 us
    pallas_call x2, Pallas kernels, conv_states(): pl.pallas_call(functools.partial(conv_kernel, order), grid_spec=pltpu.Pre...  11.3 us
    ppermute x13, starting transfers between devices, swap(): lax.ppermute(block, axis, [(i, i ^ bit) for i in range(lax.axis_size(axis...  10.4 us
    pallas_call x2, Pallas kernels, norm_rows(): pl.pallas_call(functools.partial(norm_kernel, places, len(weights)), in_s...  5.32 us
    pallas_call x5, Pallas kernels, add_chunks(): pl.pallas_call(add_kernel, grid=(1,), in_specs=[pl.BlockSpec((rows, count...  4.01 us
  transfers between devices with their start and end apart: 20, of which 8 were waited for; matrix products, arithmetic and copies ran while one was open for 0% of the time, Pallas kernels for 66%

profile of v15, /device:TPU:0, one launch (start us, length us, event | category | flops | bytes accessed | tf_op | source)
XLA Modules:
  0.0 111.1 jit_solution(4991840971013327860)
XLA Ops:
  1.3 2.6 %collective-permute-start = (bf16[16,2560]{1,0:T(8,128)(2,1)S(1)}, bf16[16,2560]{1,0:T(8,128)(2,1)S(1)}, u32[]{:S(2)}, u32[]{:S(2)}) collective-permute-start(bf16[16,2560]{1,0:T(8,128)(2,1)S(1)} %tail_rows.1), channel_id=1, source_target_pairs={{0,4},{4,8},{8,12},{12,16},{16,20},{20,24},{24,28},{28,0},{1,5},{5... | collective-permute-start | bytes 245768 | tf_op jit(solution)/shard_map/ppermute | solution.py:731
  4.0 3.9 %decays.1 = (f32[1024,16]{1,0:T(8,128)S(1)}, f32[1024,16]{1,0:T(8,128)S(1)}, f32[16,1024]{1,0:T(8,128)S(1)}, f32[16,1024]{1,0:T(8,128)S(1)}, f32[16,1024]{1,0:T(...) custom-call(s32[9]{0:T(128)S(1)} %stack.36.info, ...), custom_call_target="tpu_custom_call" | custom-call | flops 1 | bytes 1 | tf_op jit(solution)/shard_map/decays/pallas_call | solution.py:153
  8.2 1.9 %collective-permute-done.halo = bf16[16,2560]{1,0:T(8,128)(2,1)S(1)} collective-permute-done((bf16[16,2560]{1,0:T(8,128)(2,1)S(1)}, bf16[16,2560]{1,0:T(8,128)(2,1)S(1)}, u32[]{:S(2)}, u32[]{:S(2)}) %collective-permute-start) | collective-permute-done | bytes 81952 | tf_op jit(solution)/shard_map/ppermute | solution.py:731
  10.1 5.6 %conv_states.2 = (bf16[1024,1024]{1,0:T(8,128)(2,1)S(1)}, bf16[1024,256]{1,0:T(8,128)(2,1)S(1)}, bf16[144,1024]{1,0:T(8,128)(2,1)S(1)}, bf16[1024,1024]{1,0:T(8,128)(2,1)S(1)}) custom-call(s32[9]{0:T(128)S(1)} %stack.36.info, bf16[1024,1024]{1,0:T(8,128)(2,1)S(1)} %get-tuple-element.55.x, bf16[1024,512]{1,0:T(8,128)(2,1)S(1)} %bitcast.14, ...), custom_call_target="tpu_custom_call" | custom-call | flops 1 | bytes 1 | tf_op jit(solution)/shard_map/conv_states/pallas_call | solution.py:296
  15.8 5.6 %conv_states.3 = (bf16[1024,1024]{1,0:T(8,128)(2,1)S(1)}, bf16[1024,256]{1,0:T(8,128)(2,1)S(1)}, f32[128,1024]{1,0:T(8,128)S(1)}, bf16[1024,2048]{1,0:T(8,128)(2,1)S(1)}) custom-call(s32[9]{0:T(128)S(1)} %stack.36.info, bf16[1024,1024]{1,0:T(8,128)(2,1)S(1)} %get-tuple-element.60.x, bf16[1024,512]{1,0:T(8,128)(2,1)S(1)} %bitcast.15, ...), custom_call_target="tpu_custom_call" | custom-call | flops 1 | bytes 1 | tf_op jit(solution)/shard_map/conv_states/pallas_call | solution.py:296
  21.4 3.9 %scan_part.4._.refs_0_ = bf16[1024,1024]{1,0:T(8,128)(2,1)S(1)} custom-call(s32[9]{0:T(128)S(1)} %stack.36.info, bf16[1024,1024]{1,0:T(8,128)(2,1)S(1)} %get-tuple-element.66.x, bf16[1024,2048]{1,0:T(8,128)(2,1)S(1)} %get-tuple-element.67.z, bf16[1024,256]{1,0:T(8,128)(2,1)S(1)} %get-tuple-element.59.bc.bc0, f32[1024,16]{1,0:T(8,128)S(1)} %get-tuple-element.68.cum, ...), custom_call_target="tpu_custom_call" | custom-call | flops 1 | bytes 1 | tf_op jit(solution)/shard_map/scan_part/pallas_call | solution.py:494
  27.5 1.6 %collective-permute-start.3 = (bf16[144,256]{1,0:T(8,128)(2,1)S(1)}, bf16[144,256]{1,0:T(8,128)(2,1)S(1)}, u32[]{:S(2)}, u32[]{:S(2)}) collective-permute-start(bf16[144,256]{1,0:T(8,128)(2,1)S(1)} %get-tuple-element.81), channel_id=1, source_target_pairs={{0,16},{4,20},{8,24},{12,28},{16,0},{20,4},{24,8},{28,12},{1,17},{... | collective-permute-start | bytes 221192 | tf_op jit(solution)/shard_map/ppermute | solution.py:731
  29.1 2.3 %collective-permute-start.4 = (bf16[144,256]{1,0:T(8,128)(2,1)S(1)}, bf16[144,256]{1,0:T(8,128)(2,1)S(1)}, u32[]{:S(2)}, u32[]{:S(2)}) collective-permute-start(bf16[144,256]{1,0:T(8,128)(2,1)S(1)} %get-tuple-element.82), channel_id=1, source_target_pairs={{0,24},{4,28},{8,0},{12,4},{16,8},{20,12},{24,16},{28,20},{1,25},{... | collective-permute-start | bytes 221192 | tf_op jit(solution)/shard_map/ppermute | solution.py:731
  31.4 3.9 %scan_part.5.refs_4_.refs_1_ = bf16[1024,1024]{1,0:T(8,128)(2,1)S(1)} custom-call(s32[9]{0:T(128)S(1)} %stack.36.info, bf16[1024,1024]{1,0:T(8,128)(2,1)S(1)} %get-tuple-element.66.x, bf16[1024,2048]{1,0:T(8,128)(2,1)S(1)} %get-tuple-element.67.z, bf16[1024,256]{1,0:T(8,128)(2,1)S(1)} %get-tuple-element.59.bc.bc0, f32[1024,16]{1,0:T(8,128)S(1)} %get-tuple-element.68.cum, ...), custom_call_target="tpu_custom_call" | custom-call | flops 1 | bytes 1 | tf_op jit(solution)/shard_map/scan_part/pallas_call | solution.py:494
  36.3 1.9 %collective-permute-start.5 = (bf16[128,256]{1,0:T(8,128)(2,1)S(1)}, bf16[128,256]{1,0:T(8,128)(2,1)S(1)}, u32[]{:S(2)}, u32[]{:S(2)}) collective-permute-start(bf16[128,256]{1,0:T(8,128)(2,1)S(1)} %get-tuple-element.84), channel_id=1, source_target_pairs={{0,8},{4,12},{8,16},{12,20},{16,24},{20,28},{24,0},{28,4},{1,9},{5... | collective-permute-start | bytes 196616 | tf_op jit(solution)/shard_map/ppermute | solution.py:731
  40.6 3.9 %scan_part.6._.refs_2_ = bf16[1024,1024]{1,0:T(8,128)(2,1)S(1)} custom-call(s32[9]{0:T(128)S(1)} %stack.36.info, bf16[1024,1024]{1,0:T(8,128)(2,1)S(1)} %get-tuple-element.74.x, bf16[1024,2048]{1,0:T(8,128)(2,1)S(1)} %get-tuple-element.67.z, bf16[1024,256]{1,0:T(8,128)(2,1)S(1)} %get-tuple-element.63.bc.bc1, f32[1024,16]{1,0:T(8,128)S(1)} %get-tuple-element.75.cum, ...), custom_call_target="tpu_custom_call" | custom-call | flops 1 | bytes 1 | tf_op jit(solution)/shard_map/scan_part/pallas_call | solution.py:494
  46.7 3.9 %scan_part.7.refs_3_ = bf16[1024,1024]{1,0:T(8,128)(2,1)S(1)} custom-call(s32[9]{0:T(128)S(1)} %stack.36.info, bf16[1024,1024]{1,0:T(8,128)(2,1)S(1)} %get-tuple-element.74.x, bf16[1024,2048]{1,0:T(8,128)(2,1)S(1)} %get-tuple-element.67.z, bf16[1024,256]{1,0:T(8,128)(2,1)S(1)} %get-tuple-element.63.bc.bc1, f32[1024,16]{1,0:T(8,128)S(1)} %get-tuple-element.75.cum, ...), custom_call_target="tpu_custom_call" | custom-call | flops 1 | bytes 1 | tf_op jit(solution)/shard_map/scan_part/pallas_call | solution.py:494
  50.6 3.1 %collective-permute-done.8.state0 = bf16[128,1024]{1,0:T(8,128)(2,1)S(1)} collective-permute-done((bf16[128,1024]{1,0:T(8,128)(2,1)S(1)}, bf16[128,1024]{1,0:T(8,128)(2,1)S(1)}, u32[]{:S(2)}, u32[]{:S(2)}) %collective-permute-start.8) | collective-permute-done | bytes 262176 | tf_op jit(solution)/shard_map/ppermute | solution.py:726
  53.7 2.5 %norm_rows.2 = (bf16[256,2048]{1,0:T(8,128)(2,1)S(1)}, bf16[256,2048]{1,0:T(8,128)(2,1)S(1)}) custom-call(s32[9]{0:T(128)S(1)} %stack.36.info, bf16[1024,256]{1,0:T(8,128)(2,1)S(1)} %get-tuple-element.59.bc.bc0, bf16[1024,256]{1,0:T(8,128)(2,1)S(1)} %get-tuple-element.63.bc.bc1, bf16[128,1024]{1,0:T(8,128)(2,1)S(1)} %collective-permute-done.8.state0, ...), custom_call_target="tpu_custom_call" | custom-call | flops 1 | bytes 1 | tf_op jit(solution)/shard_map/norm_rows/pallas_call | solution.py:554
  56.8 2.8 %norm_rows.3 = (bf16[512,2048]{1,0:T(8,128)(2,1)S(1)}, bf16[2048,512]{1,0:T(8,128)(2,1)S(1)}, bf16[2048,512]{1,0:T(8,128)(2,1)S(1)}) custom-call(s32[9]{0:T(128)S(1)} %stack.36.info, bf16[1024,256]{1,0:T(8,128)(2,1)S(1)} %get-tuple-element.59.bc.bc0, bf16[1024,256]{1,0:T(8,128)(2,1)S(1)} %get-tuple-element.63.bc.bc1, ...), custom_call_target="tpu_custom_call" | custom-call | flops 1 | bytes 1 | tf_op jit(solution)/shard_map/norm_rows/pallas_call | solution.py:554
  61.6 4.3 %project_both.7 = (bf16[256,512]{1,0:T(8,128)(2,1)S(1)}, f32[256,512]{1,0:T(8,128)S(1)}) custom-call(bf16[512,2048]{1,0:T(8,128)(2,1)S(1)} %get-tuple-element.90.owns, bf16[512,2048]{1,0:T(8,128)(2,1)S(1)} %join.1.mates, bf16[2048,4096]{1,0:T(8,128)(2,1)} %w0_far.9, bf16[2048,4096]{1,0:T(8,128)(2,1)} %collective-permute-done.9.refs_5_.w1_far), custom_call_target="tpu_custom_call" | custom-call | flops 1 | bytes 1 | tf_op jit(solution)/shard_map/project_both/pallas_call | solution.py:659
  65.9 1.6 %collective-permute-start.18 = (bf16[256,512]{1,0:T(8,128)(2,1)S(1)}, bf16[256,512]{1,0:T(8,128)(2,1)S(1)}, u32[]{:S(2)}, u32[]{:S(2)}) collective-permute-start(bf16[256,512]{1,0:T(8,128)(2,1)S(1)} %get-tuple-element.104), channel_id=1, source_target_pairs={{0,2},{1,3},{2,0},{3,1},{4,6},{5,7},{6,4},{7,5},{8,10},{9,11},{10,... | collective-permute-start | bytes 786440 | tf_op jit(solution)/shard_map/ppermute | solution.py:726
  67.5 7.0 %project_both.6 = (bf16[256,512]{1,0:T(8,128)(2,1)S(1)}, bf16[256,512]{1,0:T(8,128)(2,1)S(1)}, f32[256,1024]{1,0:T(8,128)S(1)}) custom-call(bf16[512,2048]{1,0:T(8,128)(2,1)S(1)} %get-tuple-element.90.owns, bf16[512,2048]{1,0:T(8,128)(2,1)S(1)} %join.1.mates, bf16[2048,4096]{1,0:T(8,128)(2,1)} %w0_far.9, bf16[2048,4096]{1,0:T(8,128)(2,1)} %collective-permute-done.9.refs_5_.w1_far), custom_call_target="tpu_custom_call" | custom-call | flops 1 | bytes 1 | tf_op jit(solution)/shard_map/project_both/pallas_call | solution.py:659
  76.6 7.0 %project_both.5 = (bf16[256,512]{1,0:T(8,128)(2,1)S(1)}, bf16[256,512]{1,0:T(8,128)(2,1)S(1)}, f32[256,1024]{1,0:T(8,128)S(1)}) custom-call(bf16[512,2048]{1,0:T(8,128)(2,1)S(1)} %get-tuple-element.90.owns, bf16[512,2048]{1,0:T(8,128)(2,1)S(1)} %join.1.mates, bf16[2048,4096]{1,0:T(8,128)(2,1)} %w0_far.9, bf16[2048,4096]{1,0:T(8,128)(2,1)} %collective-permute-done.9.refs_5_.w1_far), custom_call_target="tpu_custom_call" | custom-call | flops 1 | bytes 1 | tf_op jit(solution)/shard_map/project_both/pallas_call | solution.py:659
  84.2 7.0 %project_both.4 = (bf16[256,512]{1,0:T(8,128)(2,1)S(1)}, bf16[256,512]{1,0:T(8,128)(2,1)S(1)}, f32[256,1024]{1,0:T(8,128)S(1)}) custom-call(bf16[512,2048]{1,0:T(8,128)(2,1)S(1)} %get-tuple-element.90.owns, bf16[512,2048]{1,0:T(8,128)(2,1)S(1)} %join.1.mates, bf16[2048,4096]{1,0:T(8,128)(2,1)} %w0_far.9, bf16[2048,4096]{1,0:T(8,128)(2,1)} %collective-permute-done.9.refs_5_.w1_far), custom_call_target="tpu_custom_call" | custom-call | flops 1 | bytes 1 | tf_op jit(solution)/shard_map/project_both/pallas_call | solution.py:659
  91.3 1.6 %collective-permute-start.15 = (bf16[256,512]{1,0:T(8,128)(2,1)S(1)}, bf16[256,512]{1,0:T(8,128)(2,1)S(1)}, u32[]{:S(2)}, u32[]{:S(2)}) collective-permute-start(bf16[256,512]{1,0:T(8,128)(2,1)S(1)} %get-tuple-element.99), channel_id=1, source_target_pairs={{0,2},{1,3},{2,0},{3,1},{4,6},{5,7},{6,4},{7,5},{8,10},{9,11},{10,... | collective-permute-start | bytes 786440 | tf_op jit(solution)/shard_map/ppermute | solution.py:726
  94.9 3.8 %project_near.1.refs_1_ = bf16[256,4096]{1,0:T(8,128)(2,1)} custom-call(bf16[512,2048]{1,0:T(8,128)(2,1)S(1)} %get-tuple-element.90.owns, bf16[512,2048]{1,0:T(8,128)(2,1)S(1)} %join.1.mates, bf16[2048,4096]{1,0:T(8,128)(2,1)} %w0_far.9, bf16[2048,4096]{1,0:T(8,128)(2,1)} %collective-permute-done.9.refs_5_.w1_far, ...), custom_call_target="tpu_custom_call" | custom-call | flops 1 | bytes 1 | tf_op jit(solution)/shard_map/project_near/pallas_call | solution.py:683
  101.4 4.7 %collective-permute-done.13.refs_0_ = bf16[256,512]{1,0:T(8,128)(2,1)S(1)} collective-permute-done((bf16[256,512]{1,0:T(8,128)(2,1)S(1)}, bf16[256,512]{1,0:T(8,128)(2,1)S(1)}, u32[]{:S(2)}, u32[]{:S(2)}) %collective-permute-start.13) | collective-permute-done | bytes 262176 | tf_op jit(solution)/shard_map/ppermute | solution.py:726
  106.9 3.5 %collective-permute-done.12.refs_0_ = bf16[256,512]{1,0:T(8,128)(2,1)S(1)} collective-permute-done((bf16[256,512]{1,0:T(8,128)(2,1)S(1)}, bf16[256,512]{1,0:T(8,128)(2,1)S(1)}, u32[]{:S(2)}, u32[]{:S(2)}) %collective-permute-start.12) | collective-permute-done | bytes 262176 | tf_op jit(solution)/shard_map/ppermute | solution.py:726
  (47 shorter events, 20.7 us)
Async XLA Ops:
  0.0 56.8 %collective-permute-start.9 = (bf16[2048,4096]{1,0:T(8,128)(2,1)}, bf16[2048,4096]{1,0:T(8,128)(2,1)}, u32[]{:S(2)}, u32[]{:S(2)}) collective-permute-start(bf16[2048,4096]{1,0:T(8,128)(2,1)} %w0_far.9), channel_id=1, source_target_pairs={{0,1},{1,0},{2,3},{3,2},{4,5},{5,4},{6,7},{7,6},{8,9},{9,8},{10,11... | collective-permute-start | bytes 50331656 | tf_op jit(solution)/shard_map/ppermute | solution.py:726
  1.3 8.7 %collective-permute-start = (bf16[16,2560]{1,0:T(8,128)(2,1)S(1)}, bf16[16,2560]{1,0:T(8,128)(2,1)S(1)}, u32[]{:S(2)}, u32[]{:S(2)}) collective-permute-start(bf16[16,2560]{1,0:T(8,128)(2,1)S(1)} %tail_rows.1), channel_id=1, source_target_pairs={{0,4},{4,8},{8,12},{12,16},{16,20},{20,24},{24,28},{28,0},{1,5},{5... | collective-permute-start | bytes 245768 | tf_op jit(solution)/shard_map/ppermute | solution.py:731
  4.0 3.9 %copy-start.1 = (bf16[1024,2,256]{2,1,0:T(2,128)(2,1)S(1)}, bf16[1024,2,256]{2,1,0:T(2,128)(2,1)}, u32[]{:S(2)}) copy-start(bf16[1024,2,256]{2,1,0:T(2,128)(2,1)} %bc.1) | copy-start | bytes 3145732
  15.7 9.7 %collective-permute-start.1 = (bf16[144,1024]{1,0:T(8,128)(2,1)S(1)}, bf16[144,1024]{1,0:T(8,128)(2,1)S(1)}, u32[]{:S(2)}, u32[]{:S(2)}) collective-permute-start(bf16[144,1024]{1,0:T(8,128)(2,1)S(1)} %get-tuple-element.64), channel_id=1, source_target_pairs={{0,4},{4,0},{8,12},{12,8},{16,20},{20,16},{24,28},{28,24},{1,5},{5... | collective-permute-start | bytes 884744 | tf_op jit(solution)/shard_map/ppermute | solution.py:726
  26.2 9.1 %collective-permute-start.2 = (bf16[144,256]{1,0:T(8,128)(2,1)S(1)}, bf16[144,256]{1,0:T(8,128)(2,1)S(1)}, u32[]{:S(2)}, u32[]{:S(2)}) collective-permute-start(bf16[144,256]{1,0:T(8,128)(2,1)S(1)} %get-tuple-element.80), channel_id=1, source_target_pairs={{0,8},{4,12},{8,16},{12,20},{16,24},{20,28},{24,0},{28,4},{1,9},{5... | collective-permute-start | bytes 221192 | tf_op jit(solution)/shard_map/ppermute | solution.py:731
  27.5 8.1 %collective-permute-start.3 = (bf16[144,256]{1,0:T(8,128)(2,1)S(1)}, bf16[144,256]{1,0:T(8,128)(2,1)S(1)}, u32[]{:S(2)}, u32[]{:S(2)}) collective-permute-start(bf16[144,256]{1,0:T(8,128)(2,1)S(1)} %get-tuple-element.81), channel_id=1, source_target_pairs={{0,16},{4,20},{8,24},{12,28},{16,0},{20,4},{24,8},{28,12},{1,17},{... | collective-permute-start | bytes 221192 | tf_op jit(solution)/shard_map/ppermute | solution.py:731
  29.1 6.5 %collective-permute-start.4 = (bf16[144,256]{1,0:T(8,128)(2,1)S(1)}, bf16[144,256]{1,0:T(8,128)(2,1)S(1)}, u32[]{:S(2)}, u32[]{:S(2)}) collective-permute-start(bf16[144,256]{1,0:T(8,128)(2,1)S(1)} %get-tuple-element.82), channel_id=1, source_target_pairs={{0,24},{4,28},{8,0},{12,4},{16,8},{20,12},{24,16},{28,20},{1,25},{... | collective-permute-start | bytes 221192 | tf_op jit(solution)/shard_map/ppermute | solution.py:731
  36.3 8.3 %collective-permute-start.5 = (bf16[128,256]{1,0:T(8,128)(2,1)S(1)}, bf16[128,256]{1,0:T(8,128)(2,1)S(1)}, u32[]{:S(2)}, u32[]{:S(2)}) collective-permute-start(bf16[128,256]{1,0:T(8,128)(2,1)S(1)} %get-tuple-element.84), channel_id=1, source_target_pairs={{0,8},{4,12},{8,16},{12,20},{16,24},{20,28},{24,0},{28,4},{1,9},{5... | collective-permute-start | bytes 196616 | tf_op jit(solution)/shard_map/ppermute | solution.py:731
  38.2 6.5 %collective-permute-start.6 = (bf16[128,256]{1,0:T(8,128)(2,1)S(1)}, bf16[128,256]{1,0:T(8,128)(2,1)S(1)}, u32[]{:S(2)}, u32[]{:S(2)}) collective-permute-start(bf16[128,256]{1,0:T(8,128)(2,1)S(1)} %get-tuple-element.85), channel_id=1, source_target_pairs={{0,16},{4,20},{8,24},{12,28},{16,0},{20,4},{24,8},{28,12},{1,17},{... | collective-permute-start | bytes 196616 | tf_op jit(solution)/shard_map/ppermute | solution.py:731
  39.8 5.2 %collective-permute-start.7 = (bf16[128,256]{1,0:T(8,128)(2,1)S(1)}, bf16[128,256]{1,0:T(8,128)(2,1)S(1)}, u32[]{:S(2)}, u32[]{:S(2)}) collective-permute-start(bf16[128,256]{1,0:T(8,128)(2,1)S(1)} %get-tuple-element.86), channel_id=1, source_target_pairs={{0,24},{4,28},{8,0},{12,4},{16,8},{20,12},{24,16},{28,20},{1,25},{... | collective-permute-start | bytes 196616 | tf_op jit(solution)/shard_map/ppermute | solution.py:731
  45.8 7.9 %copy-start = (f32[2048]{0:T(1024)S(1)}, f32[2048]{0:T(1024)}, u32[]{:S(2)}) copy-start(f32[2048]{0:T(1024)} %param.18) | copy-start | bytes 24580
  45.8 7.9 %collective-permute-start.8 = (bf16[128,1024]{1,0:T(8,128)(2,1)S(1)}, bf16[128,1024]{1,0:T(8,128)(2,1)S(1)}, u32[]{:S(2)}, u32[]{:S(2)}) collective-permute-start(bf16[128,1024]{1,0:T(8,128)(2,1)S(1)} %get-tuple-element.87._), channel_id=1, source_target_pairs={{0,4},{4,0},{8,12},{12,8},{16,20},{20,16},{24,28},{28,24},{1,5},{5... | collective-permute-start | bytes 786440 | tf_op jit(solution)/shard_map/ppermute | solution.py:726
  56.2 3.4 %collective-permute-start.10 = (bf16[256,2048]{1,0:T(8,128)(2,1)S(1)}, bf16[256,2048]{1,0:T(8,128)(2,1)S(1)}, u32[]{:S(2)}, u32[]{:S(2)}) collective-permute-start(bf16[256,2048]{1,0:T(8,128)(2,1)S(1)} %get-tuple-element.89._), channel_id=1, source_target_pairs={{0,1},{1,0},{2,3},{3,2},{4,5},{5,4},{6,7},{7,6},{8,9},{9,8},{10,11... | collective-permute-start | bytes 3145736 | tf_op jit(solution)/shard_map/ppermute | solution.py:726
  56.3 5.2 %collective-permute-start.11 = (bf16[256,2048]{1,0:T(8,128)(2,1)S(1)}, bf16[256,2048]{1,0:T(8,128)(2,1)S(1)}, u32[]{:S(2)}, u32[]{:S(2)}) collective-permute-start(bf16[256,2048]{1,0:T(8,128)(2,1)S(1)} %get-tuple-element.91), channel_id=1, source_target_pairs={{0,1},{1,0},{2,3},{3,2},{4,5},{5,4},{6,7},{7,6},{8,9},{9,8},{10,11... | collective-permute-start | bytes 3145736 | tf_op jit(solution)/shard_map/ppermute | solution.py:726
  60.9 30.4 %collective-permute-start.19 = (bf16[256,512]{1,0:T(8,128)(2,1)S(1)}, bf16[256,512]{1,0:T(8,128)(2,1)S(1)}, u32[]{:S(2)}, u32[]{:S(2)}) collective-permute-start(bf16[256,512]{1,0:T(8,128)(2,1)S(1)} %project_ahead.1._), channel_id=1, source_target_pairs={{0,2},{1,3},{2,0},{3,1},{4,6},{5,7},{6,4},{7,5},{8,10},{9,11},{10,... | collective-permute-start | bytes 786440 | tf_op jit(solution)/shard_map/ppermute | solution.py:726
  65.9 26.9 %collective-permute-start.18 = (bf16[256,512]{1,0:T(8,128)(2,1)S(1)}, bf16[256,512]{1,0:T(8,128)(2,1)S(1)}, u32[]{:S(2)}, u32[]{:S(2)}) collective-permute-start(bf16[256,512]{1,0:T(8,128)(2,1)S(1)} %get-tuple-element.104), channel_id=1, source_target_pairs={{0,2},{1,3},{2,0},{3,1},{4,6},{5,7},{6,4},{7,5},{8,10},{9,11},{10,... | collective-permute-start | bytes 786440 | tf_op jit(solution)/shard_map/ppermute | solution.py:726
  74.5 18.9 %collective-permute-start.16 = (bf16[256,512]{1,0:T(8,128)(2,1)S(1)}, bf16[256,512]{1,0:T(8,128)(2,1)S(1)}, u32[]{:S(2)}, u32[]{:S(2)}) collective-permute-start(bf16[256,512]{1,0:T(8,128)(2,1)S(1)} %get-tuple-element.101), channel_id=1, source_target_pairs={{0,2},{1,3},{2,0},{3,1},{4,6},{5,7},{6,4},{7,5},{8,10},{9,11},{10,... | collective-permute-start | bytes 786440 | tf_op jit(solution)/shard_map/ppermute | solution.py:726
  75.1 24.3 %collective-permute-start.17 = (bf16[256,512]{1,0:T(8,128)(2,1)S(1)}, bf16[256,512]{1,0:T(8,128)(2,1)S(1)}, u32[]{:S(2)}, u32[]{:S(2)}) collective-permute-start(bf16[256,512]{1,0:T(8,128)(2,1)S(1)} %get-tuple-element.102), channel_id=1, source_target_pairs={{0,2},{1,3},{2,0},{3,1},{4,6},{5,7},{6,4},{7,5},{8,10},{9,11},{10,... | collective-permute-start | bytes 786440 | tf_op jit(solution)/shard_map/ppermute | solution.py:726
  83.6 16.7 %collective-permute-start.14 = (bf16[256,512]{1,0:T(8,128)(2,1)S(1)}, bf16[256,512]{1,0:T(8,128)(2,1)S(1)}, u32[]{:S(2)}, u32[]{:S(2)}) collective-permute-start(bf16[256,512]{1,0:T(8,128)(2,1)S(1)} %get-tuple-element.98), channel_id=1, source_target_pairs={{0,2},{1,3},{2,0},{3,1},{4,6},{5,7},{6,4},{7,5},{8,10},{9,11},{10,... | collective-permute-start | bytes 786440 | tf_op jit(solution)/shard_map/ppermute | solution.py:726
  91.3 9.3 %collective-permute-start.15 = (bf16[256,512]{1,0:T(8,128)(2,1)S(1)}, bf16[256,512]{1,0:T(8,128)(2,1)S(1)}, u32[]{:S(2)}, u32[]{:S(2)}) collective-permute-start(bf16[256,512]{1,0:T(8,128)(2,1)S(1)} %get-tuple-element.99), channel_id=1, source_target_pairs={{0,2},{1,3},{2,0},{3,1},{4,6},{5,7},{6,4},{7,5},{8,10},{9,11},{10,... | collective-permute-start | bytes 786440 | tf_op jit(solution)/shard_map/ppermute | solution.py:726
  92.8 13.4 %collective-permute-start.13 = (bf16[256,512]{1,0:T(8,128)(2,1)S(1)}, bf16[256,512]{1,0:T(8,128)(2,1)S(1)}, u32[]{:S(2)}, u32[]{:S(2)}) collective-permute-start(bf16[256,512]{1,0:T(8,128)(2,1)S(1)} %get-tuple-element.96), channel_id=1, source_target_pairs={{0,2},{1,3},{2,0},{3,1},{4,6},{5,7},{6,4},{7,5},{8,10},{9,11},{10,... | collective-permute-start | bytes 786440 | tf_op jit(solution)/shard_map/ppermute | solution.py:726
  93.4 17.0 %collective-permute-start.12 = (bf16[256,512]{1,0:T(8,128)(2,1)S(1)}, bf16[256,512]{1,0:T(8,128)(2,1)S(1)}, u32[]{:S(2)}, u32[]{:S(2)}) collective-permute-start(bf16[256,512]{1,0:T(8,128)(2,1)S(1)} %get-tuple-element.95), channel_id=1, source_target_pairs={{0,2},{1,3},{2,0},{3,1},{4,6},{5,7},{6,4},{7,5},{8,10},{9,11},{10,... | collective-permute-start | bytes 786440 | tf_op jit(solution)/shard_map/ppermute | solution.py:726

commit v16 on v15

--- a/solution.py
+++ b/solution.py
@@ -261,19 +261,17 @@
             weights = [jnp.where(group == 0, wbc[k, 0:1, ds], wbc[k, 1:2, ds]) for k in range(KCONV)]
             conv(i, bc[at, src], dot(down[...], bc[at, src]), halo[:, halo_src], bc[behind, src], weights, emit_bc)
 
-        all_moved = dot(down[...], x[at, :])
-        all_scale = dot(f_dev[at, :], ones[...])
         for lanes in range(0, width, SLAB):
             ds = slice(lanes, lanes + SLAB)
             src = pl.ds(pl.multiple_of(first_lane + lanes, SLAB), SLAB)
-            scale = all_scale[:, ds]
+            scale = dot(f_dev[at, :], ones[:, ds])
 
             def emit(r, value):
                 x_out[out(r), ds] = value.astype(BF16)
                 xf[r : r + ROWS_A, ds] = (value * scale[r : r + ROWS_A]).astype(BF16)
 
             weights = [wx[k : k + 1, ds] for k in range(KCONV)]
-            conv(i, x[at, ds], all_moved[:, ds], halo[:, src], x[behind, ds], weights, emit)
+            conv(i, x[at, ds], dot(down[...], x[at, ds]), halo[:, src], x[behind, ds], weights, emit)
 
         state[...] += dot(bc_out[at, 0:N], xf[...], ((0,), (0,)))
         return 0
@@ -503,8 +501,10 @@
     )(info, x, z, bc, cum, cum_s, log_s, f_blk, rates, token)
 
 
-def norm_kernel(places, fetched, info, bc0, bc1, state0, state1, gain, _, *refs):
-    uvs, refs = refs[: 2 * B_PARTS], refs[2 * B_PARTS :]
+def norm_kernel(order, places, skip, fetched, info, bc, state, gain, _, *refs):
+    uvs, refs = refs[:B_PARTS], refs[B_PARTS:]
+    if order == 0:
+        kept, refs = refs[0], refs[1:]
     weights, outs, tiles, sem = refs[:fetched], refs[fetched : -1 - fetched], refs[len(refs) - 1 - fetched : -1], refs[-1]
     copies = [
         pltpu.make_async_copy(weight.at[:, pl.ds(0, tile.shape[1])], tile, sem.at[k])
@@ -513,33 +513,40 @@
     for copy in copies:
         copy.start()
     count = outs[0].shape[0] * len(outs) // len(places)
-    per = state0.shape[1]
+    per = state.shape[1]
     part = per // B_PARTS
 
-    def rows(out, first, base):
+    def lanes(group, p=0, size=per):
+        return pl.ds(pl.multiple_of(info[GROUP + group] * per + p * part, part), size)
+
+    def rows(out, first, base, source):
         to = pl.ds(pl.multiple_of(first, ROWS_C), ROWS_C)
         at = pl.ds(pl.multiple_of(base, ROWS_C), ROWS_C)
-        for order, (bc, state) in enumerate(((bc0, state0), (bc1, state1))):
-            c_mat = bc[at, N : 2 * N]
-            pieces = []
-            squares = None
-            for p in range(B_PARTS):
-                uv = uvs[order * B_PARTS + p]
-                inc = state[:, p * part : (p + 1) * part]
-                gated = uv[at, 0:part].astype(F32) + uv[at, part:].astype(F32) * dot(c_mat, inc)
-                square = jnp.sum(gated * gated, axis=-1, keepdims=True)
-                squares = square if squares is None else squares + square
-                pieces.append(gated)
-            scale = lax.rsqrt(squares * (1.0 / per) + EPS)
-            for p, gated in enumerate(pieces):
-                lanes = pl.ds(pl.multiple_of(info[GROUP + order] * per + p * part, part), part)
-                out[to, lanes] = (gated * scale * gain[:, lanes]).astype(BF16)
+        c_mat = bc[at, N : 2 * N]
+        pieces = []
+        squares = None
+        for p, uv in enumerate(uvs):
+            inc = state[:, p * part : (p + 1) * part]
+            gated = uv[at, 0:part].astype(F32) + uv[at, part:].astype(F32) * dot(c_mat, inc)
+            square = jnp.sum(gated * gated, axis=-1, keepdims=True)
+            squares = square if squares is None else squares + square
+            pieces.append(gated)
+        scale = lax.rsqrt(squares * (1.0 / per) + EPS)
+        for p, gated in enumerate(pieces):
+            value = (gated * scale * gain[:, lanes(order, p, part)]).astype(BF16)
+            if order == 0:
+                out[to, lanes(0, p, part)] = value
+            else:
+                out[to, p * part : (p + 1) * part] = value
+        if order == 0:
+            out[to, lanes(1)] = kept[pl.ds(pl.multiple_of(source, ROWS_C), ROWS_C), :]
 
     for k, place in enumerate(places):
 
         def step(j, _):
             out, first = (outs[k], 0) if len(outs) > 1 else (outs[0], k * count)
-            rows(out, first + j * ROWS_C, info[ROWS + place] * count + j * ROWS_C)
+            source = skip + k * count + j * ROWS_C
+            rows(out, first + j * ROWS_C, info[ROWS + place] * count + j * ROWS_C, source)
             return 0
 
         lax.fori_loop(0, count // ROWS_C, step, 0)
@@ -547,20 +554,22 @@
         copy.wait()
 
 
-def norm_rows(places, apart, info, count, token, bcs, states, gain, uvs, weights=(), columns=0):
+def norm_rows(order, places, info, count, token, bc, state, gain, uvs, kept=None, skip=0, apart=False, weights=(), columns=0):
+    width = state.shape[1] if order else gain.shape[1]
     tile = jax.ShapeDtypeStruct((gain.shape[1], columns), BF16)
     arrays = len(places) if apart else 1
-    rows = jax.ShapeDtypeStruct((len(places) * count // arrays, gain.shape[1]), BF16)
+    rows = jax.ShapeDtypeStruct((len(places) * count // arrays, width), BF16)
+    joined = [] if kept is None else [kept]
     return pl.pallas_call(
-        functools.partial(norm_kernel, places, len(weights)),
-        in_specs=[SCALAR] + [FULL] * 5 + [ANY] + [FULL] * len(uvs) + [FAR] * len(weights),
+        functools.partial(norm_kernel, order, places, skip, len(weights)),
+        in_specs=[SCALAR] + [FULL] * 3 + [ANY] + [FULL] * (len(uvs) + len(joined)) + [FAR] * len(weights),
         out_specs=[FULL] * (arrays + len(weights)),
         out_shape=[rows] * arrays + [tile] * len(weights),
         scratch_shapes=[pltpu.SemaphoreType.DMA((2,))],
         compiler_params=params(16),
         cost_estimate=CHEAP,
         name="norm_rows",
-    )(info, *bcs, *states, gain, token, *uvs, *weights)
+    )(info, bc, state, gain, token, *uvs, *joined, *weights)
 
 
 def stream(base, w0_far, w1_far, w0, w1, sem):
@@ -795,7 +804,6 @@
     (bc_far,) = far(bc_input)
     halo = rotate(tail_rows(x_far, bc_far), 1)
     bc = bc_input.reshape(length, -1)
-    (weight_mate,) = far(swap(out_weight, "head", 1))
 
     (cum, cum_s, log_s, f_dev, f_blk, rates), ones, x_sent = decays(
         info, log_decay, step_size, skip_gain, x_input, half
@@ -804,6 +812,7 @@
     shared = (bc, halo, *taps)
     x0, bc0, send, x_kept = conv_states(0, info, x_sent, *shared, f_dev[0], ones, rates[0], x_far)
     got = swap(send, "seq", 1)
+    (weight_mate,) = far(swap(lax.optimization_barrier((out_weight, send))[0], "head", 1))
     x1, bc1, keep, z_near = conv_states(1, info, x_kept, *shared, f_dev[1], ones, rates[1], z_far)
     rates_kept = rates[1]
 
@@ -864,9 +873,10 @@
     columns = out_weight.shape[1]
     chunk = columns // 8
     weights = (w_far, weight_mate)
-    shared = ((bc0, bc1), (other, held), gain, uvs)
-    far_mate, near_mate = norm_rows((0, 2), True, info, count, held, *shared)
-    owns, w0, w1 = norm_rows((1, 3), False, info, count, far_mate, *shared, weights, chunk)
+    (kept,) = norm_rows(1, (0, 2, 1, 3), info, count, held, bc1, held, gain, uvs[B_PARTS:])
+    shared = (bc0, other, gain, uvs[:B_PARTS], kept)
+    far_mate, near_mate = norm_rows(0, (0, 2), info, count, kept, *shared, apart=True)
+    owns, w0, w1 = norm_rows(0, (1, 3), info, count, far_mate, *shared, 2 * count, False, weights, chunk)
     far_mate = swap(far_mate, "head", 1)
     sent = project_ahead(owns, far_mate, w0, w1)
     first = swap(sent, "head", 2)

time: 112 us -> 116 us (1.036)
  local copies, waits for them, and re-layouts: 0.33 us -> 6.07 us
  waiting for transfers between devices: 14 us -> 10.7 us
  Pallas kernels: 74 us -> 75.3 us
    unnamed x5 -> x7, local copies, waits for them, and re-layouts: 0.24 us -> 5.99 us
    ppermute x13, waiting for transfers between devices: 11.5 us -> 8.57 us  [swap(): lax.ppermute(block, axis, [(i, i ^ bit) for i in range(lax.axis_size(axis...]
    pallas_call x2 -> x3, Pallas kernels: 5.32 us -> 8.24 us  [norm_rows(): pl.pallas_call(functools.partial(norm_kernel, order, places, skip, len(we...]
  transfers between devices with their start and end apart: 20 -> 20, of which waited for: 8 -> 7; matrix products, arithmetic and copies ran while one was open for 0% -> 0% of each run, Pallas kernels for 66% -> 59%
where the time goes in v16:
time: 116 us
  Pallas kernels  75.3 us (65%)
  starting transfers between devices  23.5 us (20%)
  waiting for transfers between devices  10.7 us (9%)
  local copies, waits for them, and re-layouts  6.07 us (5%)
    pallas_call x4, Pallas kernels, project_both(): pl.pallas_call(functools.partial(both_kernel, first // TILE, cut), grid=(...  25.2 us
    pallas_call x4, Pallas kernels, scan_part(): pl.pallas_call(functools.partial(scan_kernel, order, part), in_specs=[SCA...  14.8 us
    ppermute x7, starting transfers between devices, rotate(): lax.ppermute(block, 'seq', [(i, (i + distance) % size) for i in range(siz...  13.1 us
    pallas_call x2, Pallas kernels, conv_states(): pl.pallas_call(functools.partial(conv_kernel, order), grid_spec=pltpu.Pre...  10.7 us
    ppermute x13, starting transfers between devices, swap(): lax.ppermute(block, axis, [(i, i ^ bit) for i in range(lax.axis_size(axis...  10.4 us
    ppermute x13, waiting for transfers between devices, swap(): lax.ppermute(block, axis, [(i, i ^ bit) for i in range(lax.axis_size(axis...  8.57 us
    pallas_call x3, Pallas kernels, norm_rows(): pl.pallas_call(functools.partial(norm_kernel, order, places, skip, len(we...  8.24 us
    unnamed x7, local copies, waits for them, and re-layouts  5.99 us
  transfers between devices with their start and end apart: 20, of which 7 were waited for; matrix products, arithmetic and copies ran while one was open for 0% of the time, Pallas kernels for 59%

profile of v16, /device:TPU:0, one launch (start us, length us, event | category | flops | bytes accessed | tf_op | source)
XLA Modules:
  0.0 115.9 jit_solution(2706651211476147230)
XLA Ops:
  0.9 3.0 %collective-permute-start = (bf16[16,2560]{1,0:T(8,128)(2,1)S(1)}, bf16[16,2560]{1,0:T(8,128)(2,1)S(1)}, u32[]{:S(2)}, u32[]{:S(2)}) collective-permute-start(bf16[16,2560]{1,0:T(8,128)(2,1)S(1)} %tail_rows.1), channel_id=1, source_target_pairs={{0,4},{4,8},{8,12},{12,16},{16,20},{20,24},{24,28},{28,0},{1,5},{5... | collective-permute-start | bytes 245768 | tf_op jit(solution)/shard_map/ppermute | solution.py:740
  4.0 3.9 %decays.1 = (f32[1024,16]{1,0:T(8,128)S(1)}, f32[1024,16]{1,0:T(8,128)S(1)}, f32[16,1024]{1,0:T(8,128)S(1)}, f32[16,1024]{1,0:T(8,128)S(1)}, f32[16,1024]{1,0:T(...) custom-call(s32[9]{0:T(128)S(1)} %stack.36.info, ...), custom_call_target="tpu_custom_call" | custom-call | flops 1 | bytes 1 | tf_op jit(solution)/shard_map/decays/pallas_call | solution.py:153
  9.4 5.4 %conv_states.2 = (bf16[1024,1024]{1,0:T(8,128)(2,1)S(1)}, bf16[1024,256]{1,0:T(8,128)(2,1)S(1)}, bf16[144,1024]{1,0:T(8,128)(2,1)S(1)}, bf16[1024,1024]{1,0:T(8,128)(2,1)S(1)}) custom-call(s32[9]{0:T(128)S(1)} %stack.36.info, bf16[1024,1024]{1,0:T(8,128)(2,1)S(1)} %get-tuple-element.56.x, bf16[1024,512]{1,0:T(8,128)(2,1)S(1)} %bitcast.14, ...), custom_call_target="tpu_custom_call" | custom-call | flops 1 | bytes 1 | tf_op jit(solution)/shard_map/conv_states/pallas_call | solution.py:294
  15.2 5.4 %conv_states.3 = (bf16[1024,1024]{1,0:T(8,128)(2,1)S(1)}, bf16[1024,256]{1,0:T(8,128)(2,1)S(1)}, f32[128,1024]{1,0:T(8,128)S(1)}, bf16[1024,2048]{1,0:T(8,128)(2,1)S(1)}) custom-call(s32[9]{0:T(128)S(1)} %stack.36.info, bf16[1024,1024]{1,0:T(8,128)(2,1)S(1)} %get-tuple-element.62.x, bf16[1024,512]{1,0:T(8,128)(2,1)S(1)} %bitcast.15, ...), custom_call_target="tpu_custom_call" | custom-call | flops 1 | bytes 1 | tf_op jit(solution)/shard_map/conv_states/pallas_call | solution.py:294
  20.6 3.7 %scan_part.4._.refs_0_ = bf16[1024,1024]{1,0:T(8,128)(2,1)S(1)} custom-call(s32[9]{0:T(128)S(1)} %stack.36.info, bf16[1024,1024]{1,0:T(8,128)(2,1)S(1)} %get-tuple-element.66.x, bf16[1024,2048]{1,0:T(8,128)(2,1)S(1)} %get-tuple-element.67.z, bf16[1024,256]{1,0:T(8,128)(2,1)S(1)} %get-tuple-element.60.bc, f32[1024,16]{1,0:T(8,128)S(1)} %get-tuple-element.68.cum, ...), custom_call_target="tpu_custom_call" | custom-call | flops 1 | bytes 1 | tf_op jit(solution)/shard_map/scan_part/pallas_call | solution.py:492
  25.2 1.6 %collective-permute-start.2 = (bf16[144,256]{1,0:T(8,128)(2,1)S(1)}, bf16[144,256]{1,0:T(8,128)(2,1)S(1)}, u32[]{:S(2)}, u32[]{:S(2)}) collective-permute-start(bf16[144,256]{1,0:T(8,128)(2,1)S(1)} %get-tuple-element.81), channel_id=1, source_target_pairs={{0,8},{4,12},{8,16},{12,20},{16,24},{20,28},{24,0},{28,4},{1,9},{5... | collective-permute-start | bytes 221192 | tf_op jit(solution)/shard_map/ppermute | solution.py:740
  28.2 2.6 %collective-permute-start.4 = (bf16[144,256]{1,0:T(8,128)(2,1)S(1)}, bf16[144,256]{1,0:T(8,128)(2,1)S(1)}, u32[]{:S(2)}, u32[]{:S(2)}) collective-permute-start(bf16[144,256]{1,0:T(8,128)(2,1)S(1)} %get-tuple-element.83), channel_id=1, source_target_pairs={{0,24},{4,28},{8,0},{12,4},{16,8},{20,12},{24,16},{28,20},{1,25},{... | collective-permute-start | bytes 221192 | tf_op jit(solution)/shard_map/ppermute | solution.py:740
  30.8 3.7 %scan_part.5.refs_4_.refs_1_ = bf16[1024,1024]{1,0:T(8,128)(2,1)S(1)} custom-call(s32[9]{0:T(128)S(1)} %stack.36.info, bf16[1024,1024]{1,0:T(8,128)(2,1)S(1)} %get-tuple-element.66.x, bf16[1024,2048]{1,0:T(8,128)(2,1)S(1)} %get-tuple-element.67.z, bf16[1024,256]{1,0:T(8,128)(2,1)S(1)} %get-tuple-element.60.bc, f32[1024,16]{1,0:T(8,128)S(1)} %get-tuple-element.68.cum, ...), custom_call_target="tpu_custom_call" | custom-call | flops 1 | bytes 1 | tf_op jit(solution)/shard_map/scan_part/pallas_call | solution.py:492
  35.3 2.1 %collective-permute-start.5 = (bf16[128,256]{1,0:T(8,128)(2,1)S(1)}, bf16[128,256]{1,0:T(8,128)(2,1)S(1)}, u32[]{:S(2)}, u32[]{:S(2)}) collective-permute-start(bf16[128,256]{1,0:T(8,128)(2,1)S(1)} %get-tuple-element.85), channel_id=1, source_target_pairs={{0,8},{4,12},{8,16},{12,20},{16,24},{20,28},{24,0},{28,4},{1,9},{5... | collective-permute-start | bytes 196616 | tf_op jit(solution)/shard_map/ppermute | solution.py:740
  37.4 1.7 %collective-permute-start.6 = (bf16[128,256]{1,0:T(8,128)(2,1)S(1)}, bf16[128,256]{1,0:T(8,128)(2,1)S(1)}, u32[]{:S(2)}, u32[]{:S(2)}) collective-permute-start(bf16[128,256]{1,0:T(8,128)(2,1)S(1)} %get-tuple-element.86), channel_id=1, source_target_pairs={{0,16},{4,20},{8,24},{12,28},{16,0},{20,4},{24,8},{28,12},{1,17},{... | collective-permute-start | bytes 196616 | tf_op jit(solution)/shard_map/ppermute | solution.py:740
  39.8 3.7 %scan_part.6._.refs_0_ = bf16[1024,1024]{1,0:T(8,128)(2,1)S(1)} custom-call(s32[9]{0:T(128)S(1)} %stack.36.info, bf16[1024,1024]{1,0:T(8,128)(2,1)S(1)} %get-tuple-element.74.x, bf16[1024,2048]{1,0:T(8,128)(2,1)S(1)} %get-tuple-element.67.z, bf16[1024,256]{1,0:T(8,128)(2,1)S(1)} %get-tuple-element.75.bc, f32[1024,16]{1,0:T(8,128)S(1)} %get-tuple-element.76.cum, ...), custom_call_target="tpu_custom_call" | custom-call | flops 1 | bytes 1 | tf_op jit(solution)/shard_map/scan_part/pallas_call | solution.py:492
  46.1 3.7 %scan_part.7.refs_1_ = bf16[1024,1024]{1,0:T(8,128)(2,1)S(1)} custom-call(s32[9]{0:T(128)S(1)} %stack.36.info, bf16[1024,1024]{1,0:T(8,128)(2,1)S(1)} %get-tuple-element.74.x, bf16[1024,2048]{1,0:T(8,128)(2,1)S(1)} %get-tuple-element.67.z, bf16[1024,256]{1,0:T(8,128)(2,1)S(1)} %get-tuple-element.75.bc, f32[1024,16]{1,0:T(8,128)S(1)} %get-tuple-element.76.cum, ...), custom_call_target="tpu_custom_call" | custom-call | flops 1 | bytes 1 | tf_op jit(solution)/shard_map/scan_part/pallas_call | solution.py:492
  49.8 3.4 %norm_rows.3._.refs_2_ = bf16[1024,1024]{1,0:T(8,128)(2,1)S(1)} custom-call(s32[9]{0:T(128)S(1)} %stack.36.info, bf16[1024,256]{1,0:T(8,128)(2,1)S(1)} %get-tuple-element.75.bc, bf16[128,1024]{1,0:T(8,128)(2,1)S(1)} %get-tuple-element.89.state._, f32[1,2048]{1,0:T(1,128)S(1)} %bitcast.16, bf16[128,1024]{1,0:T(8,128)(2,1)S(1)} %get-tuple-element.89.state._, ...), custom_call_target="tpu_custom_call" | custom-call | flops 1 | bytes 1 | tf_op jit(solution)/shard_map/norm_rows/pallas_call | solution.py:563
  53.2 2.1 %norm_rows.4 = (bf16[256,2048]{1,0:T(8,128)(2,1)S(1)}, bf16[256,2048]{1,0:T(8,128)(2,1)S(1)}) custom-call(s32[9]{0:T(128)S(1)} %stack.36.info, bf16[1024,256]{1,0:T(8,128)(2,1)S(1)} %get-tuple-element.60.bc, bf16[128,1024]{1,0:T(8,128)(2,1)S(1)} %collective-permute-done.8.state, f32[1,2048]{1,0:T(1,128)S(1)} %bitcast.17, ...), custom_call_target="tpu_custom_call" | custom-call | flops 1 | bytes 1 | tf_op jit(solution)/shard_map/norm_rows/pallas_call | solution.py:563
  55.9 5.8 %copy-done.1 = bf16[2048,4096]{1,0:T(8,128)(2,1)} copy-done((bf16[2048,4096]{1,0:T(8,128)(2,1)}, bf16[2048,4096]{1,0:T(8,128)(2,1)S(1)}, u32[]{:S(2)}) %copy-start.1) | copy-done | bytes 16777240
  61.6 2.8 %norm_rows.5 = (bf16[512,2048]{1,0:T(8,128)(2,1)S(1)}, bf16[2048,512]{1,0:T(8,128)(2,1)S(1)}, bf16[2048,512]{1,0:T(8,128)(2,1)S(1)}) custom-call(s32[9]{0:T(128)S(1)} %stack.36.info, bf16[1024,256]{1,0:T(8,128)(2,1)S(1)} %get-tuple-element.60.bc, bf16[128,1024]{1,0:T(8,128)(2,1)S(1)} %collective-permute-done.8.state, f32[1,2048]{1,0:T(1,128)S(1)} %bitcast.18, ...), custom_call_target="tpu_custom_call" | custom-call | flops 1 | bytes 1 | tf_op jit(solution)/shard_map/norm_rows/pallas_call | solution.py:563
  67.4 4.3 %project_both.7 = (bf16[256,512]{1,0:T(8,128)(2,1)S(1)}, f32[256,512]{1,0:T(8,128)S(1)}) custom-call(bf16[512,2048]{1,0:T(8,128)(2,1)S(1)} %get-tuple-element.92.owns, bf16[512,2048]{1,0:T(8,128)(2,1)S(1)} %join.1.mates, bf16[2048,4096]{1,0:T(8,128)(2,1)} %w0_far.9, bf16[2048,4096]{1,0:T(8,128)(2,1)} %copy-done.1), custom_call_target="tpu_custom_call" | custom-call | flops 1 | bytes 1 | tf_op jit(solution)/shard_map/project_both/pallas_call | solution.py:668
  72.3 7.0 %project_both.6 = (bf16[256,512]{1,0:T(8,128)(2,1)S(1)}, bf16[256,512]{1,0:T(8,128)(2,1)S(1)}, f32[256,1024]{1,0:T(8,128)S(1)}) custom-call(bf16[512,2048]{1,0:T(8,128)(2,1)S(1)} %get-tuple-element.92.owns, bf16[512,2048]{1,0:T(8,128)(2,1)S(1)} %join.1.mates, bf16[2048,4096]{1,0:T(8,128)(2,1)} %w0_far.9, bf16[2048,4096]{1,0:T(8,128)(2,1)} %copy-done.1), custom_call_target="tpu_custom_call" | custom-call | flops 1 | bytes 1 | tf_op jit(solution)/shard_map/project_both/pallas_call | solution.py:668
  81.4 7.0 %project_both.5 = (bf16[256,512]{1,0:T(8,128)(2,1)S(1)}, bf16[256,512]{1,0:T(8,128)(2,1)S(1)}, f32[256,1024]{1,0:T(8,128)S(1)}) custom-call(bf16[512,2048]{1,0:T(8,128)(2,1)S(1)} %get-tuple-element.92.owns, bf16[512,2048]{1,0:T(8,128)(2,1)S(1)} %join.1.mates, bf16[2048,4096]{1,0:T(8,128)(2,1)} %w0_far.9, bf16[2048,4096]{1,0:T(8,128)(2,1)} %copy-done.1), custom_call_target="tpu_custom_call" | custom-call | flops 1 | bytes 1 | tf_op jit(solution)/shard_map/project_both/pallas_call | solution.py:668
  88.4 1.6 %collective-permute-start.14 = (bf16[256,512]{1,0:T(8,128)(2,1)S(1)}, bf16[256,512]{1,0:T(8,128)(2,1)S(1)}, u32[]{:S(2)}, u32[]{:S(2)}) collective-permute-start(bf16[256,512]{1,0:T(8,128)(2,1)S(1)} %get-tuple-element.100), channel_id=1, source_target_pairs={{0,2},{1,3},{2,0},{3,1},{4,6},{5,7},{6,4},{7,5},{8,10},{9,11},{10,... | collective-permute-start | bytes 786440 | tf_op jit(solution)/shard_map/ppermute | solution.py:735
  90.0 7.0 %project_both.4 = (bf16[256,512]{1,0:T(8,128)(2,1)S(1)}, bf16[256,512]{1,0:T(8,128)(2,1)S(1)}, f32[256,1024]{1,0:T(8,128)S(1)}) custom-call(bf16[512,2048]{1,0:T(8,128)(2,1)S(1)} %get-tuple-element.92.owns, bf16[512,2048]{1,0:T(8,128)(2,1)S(1)} %join.1.mates, bf16[2048,4096]{1,0:T(8,128)(2,1)} %w0_far.9, bf16[2048,4096]{1,0:T(8,128)(2,1)} %copy-done.1), custom_call_target="tpu_custom_call" | custom-call | flops 1 | bytes 1 | tf_op jit(solution)/shard_map/project_both/pallas_call | solution.py:668
  99.6 3.8 %project_near.1.refs_1_ = bf16[256,4096]{1,0:T(8,128)(2,1)} custom-call(bf16[512,2048]{1,0:T(8,128)(2,1)S(1)} %get-tuple-element.92.owns, bf16[512,2048]{1,0:T(8,128)(2,1)S(1)} %join.1.mates, bf16[2048,4096]{1,0:T(8,128)(2,1)} %w0_far.9, bf16[2048,4096]{1,0:T(8,128)(2,1)} %copy-done.1, bf16[256,512]{1,0:T(8,128)(2,1)S(1)} %collective-permute-done.19.arrived), custom_call_target="tpu_custom_call" | custom-call | flops 1 | bytes 1 | tf_op jit(solution)/shard_map/project_near/pallas_call | solution.py:692
  107.2 4.7 %collective-permute-done.13.refs_0_ = bf16[256,512]{1,0:T(8,128)(2,1)S(1)} collective-permute-done((bf16[256,512]{1,0:T(8,128)(2,1)S(1)}, bf16[256,512]{1,0:T(8,128)(2,1)S(1)}, u32[]{:S(2)}, u32[]{:S(2)}) %collective-permute-start.13) | collective-permute-done | bytes 262176 | tf_op jit(solution)/shard_map/ppermute | solution.py:735
  112.6 2.5 %collective-permute-done.12.refs_0_ = bf16[256,512]{1,0:T(8,128)(2,1)S(1)} collective-permute-done((bf16[256,512]{1,0:T(8,128)(2,1)S(1)}, bf16[256,512]{1,0:T(8,128)(2,1)S(1)}, u32[]{:S(2)}, u32[]{:S(2)}) %collective-permute-start.12) | collective-permute-done | bytes 262176 | tf_op jit(solution)/shard_map/ppermute | solution.py:735
  (50 shorter events, 23.2 us)
Async XLA Ops:
  0.9 8.5 %collective-permute-start = (bf16[16,2560]{1,0:T(8,128)(2,1)S(1)}, bf16[16,2560]{1,0:T(8,128)(2,1)S(1)}, u32[]{:S(2)}, u32[]{:S(2)}) collective-permute-start(bf16[16,2560]{1,0:T(8,128)(2,1)S(1)} %tail_rows.1), channel_id=1, source_target_pairs={{0,4},{4,8},{8,12},{12,16},{16,20},{20,24},{24,28},{28,0},{1,5},{5... | collective-permute-start | bytes 245768 | tf_op jit(solution)/shard_map/ppermute | solution.py:740
  4.0 3.9 %copy-start.2 = (bf16[1024,2,256]{2,1,0:T(2,128)(2,1)S(1)}, bf16[1024,2,256]{2,1,0:T(2,128)(2,1)}, u32[]{:S(2)}) copy-start(bf16[1024,2,256]{2,1,0:T(2,128)(2,1)} %bc.1) | copy-start | bytes 3145732
  14.8 41.1 %collective-permute-start.9 = (bf16[2048,4096]{1,0:T(8,128)(2,1)}, bf16[2048,4096]{1,0:T(8,128)(2,1)S(1)}, u32[]{:S(2)}, u32[]{:S(2)}) collective-permute-start(bf16[2048,4096]{1,0:T(8,128)(2,1)} %w0_far.9), channel_id=1, source_target_pairs={{0,1},{1,0},{2,3},{3,2},{4,5},{5,4},{6,7},{7,6},{8,9},{9,8},{10,11... | collective-permute-start | bytes 50331656 | tf_op jit(solution)/shard_map/ppermute | solution.py:735
  14.9 9.5 %collective-permute-start.1 = (bf16[144,1024]{1,0:T(8,128)(2,1)S(1)}, bf16[144,1024]{1,0:T(8,128)(2,1)S(1)}, u32[]{:S(2)}, u32[]{:S(2)}) collective-permute-start(bf16[144,1024]{1,0:T(8,128)(2,1)S(1)} %get-tuple-element.61), channel_id=1, source_target_pairs={{0,4},{4,0},{8,12},{12,8},{16,20},{20,16},{24,28},{28,24},{1,5},{5... | collective-permute-start | bytes 884744 | tf_op jit(solution)/shard_map/ppermute | solution.py:735
  25.2 9.3 %collective-permute-start.2 = (bf16[144,256]{1,0:T(8,128)(2,1)S(1)}, bf16[144,256]{1,0:T(8,128)(2,1)S(1)}, u32[]{:S(2)}, u32[]{:S(2)}) collective-permute-start(bf16[144,256]{1,0:T(8,128)(2,1)S(1)} %get-tuple-element.81), channel_id=1, source_target_pairs={{0,8},{4,12},{8,16},{12,20},{16,24},{20,28},{24,0},{28,4},{1,9},{5... | collective-permute-start | bytes 221192 | tf_op jit(solution)/shard_map/ppermute | solution.py:740
  26.8 7.8 %collective-permute-start.3 = (bf16[144,256]{1,0:T(8,128)(2,1)S(1)}, bf16[144,256]{1,0:T(8,128)(2,1)S(1)}, u32[]{:S(2)}, u32[]{:S(2)}) collective-permute-start(bf16[144,256]{1,0:T(8,128)(2,1)S(1)} %get-tuple-element.82), channel_id=1, source_target_pairs={{0,16},{4,20},{8,24},{12,28},{16,0},{20,4},{24,8},{28,12},{1,17},{... | collective-permute-start | bytes 221192 | tf_op jit(solution)/shard_map/ppermute | solution.py:740
  28.2 6.5 %collective-permute-start.4 = (bf16[144,256]{1,0:T(8,128)(2,1)S(1)}, bf16[144,256]{1,0:T(8,128)(2,1)S(1)}, u32[]{:S(2)}, u32[]{:S(2)}) collective-permute-start(bf16[144,256]{1,0:T(8,128)(2,1)S(1)} %get-tuple-element.83), channel_id=1, source_target_pairs={{0,24},{4,28},{8,0},{12,4},{16,8},{20,12},{24,16},{28,20},{1,25},{... | collective-permute-start | bytes 221192 | tf_op jit(solution)/shard_map/ppermute | solution.py:740
  35.3 8.3 %collective-permute-start.5 = (bf16[128,256]{1,0:T(8,128)(2,1)S(1)}, bf16[128,256]{1,0:T(8,128)(2,1)S(1)}, u32[]{:S(2)}, u32[]{:S(2)}) collective-permute-start(bf16[128,256]{1,0:T(8,128)(2,1)S(1)} %get-tuple-element.85), channel_id=1, source_target_pairs={{0,8},{4,12},{8,16},{12,20},{16,24},{20,28},{24,0},{28,4},{1,9},{5... | collective-permute-start | bytes 196616 | tf_op jit(solution)/shard_map/ppermute | solution.py:740
  37.4 6.6 %collective-permute-start.6 = (bf16[128,256]{1,0:T(8,128)(2,1)S(1)}, bf16[128,256]{1,0:T(8,128)(2,1)S(1)}, u32[]{:S(2)}, u32[]{:S(2)}) collective-permute-start(bf16[128,256]{1,0:T(8,128)(2,1)S(1)} %get-tuple-element.86), channel_id=1, source_target_pairs={{0,16},{4,20},{8,24},{12,28},{16,0},{20,4},{24,8},{28,12},{1,17},{... | collective-permute-start | bytes 196616 | tf_op jit(solution)/shard_map/ppermute | solution.py:740
  39.1 5.2 %collective-permute-start.7 = (bf16[128,256]{1,0:T(8,128)(2,1)S(1)}, bf16[128,256]{1,0:T(8,128)(2,1)S(1)}, u32[]{:S(2)}, u32[]{:S(2)}) collective-permute-start(bf16[128,256]{1,0:T(8,128)(2,1)S(1)} %get-tuple-element.87), channel_id=1, source_target_pairs={{0,24},{4,28},{8,0},{12,4},{16,8},{20,12},{24,16},{28,20},{1,25},{... | collective-permute-start | bytes 196616 | tf_op jit(solution)/shard_map/ppermute | solution.py:740
  45.1 4.7 %copy-start = (f32[2048]{0:T(1024)S(1)}, f32[2048]{0:T(1024)}, u32[]{:S(2)}) copy-start(f32[2048]{0:T(1024)} %param.18) | copy-start | bytes 24580
  45.1 8.0 %collective-permute-start.8 = (bf16[128,1024]{1,0:T(8,128)(2,1)S(1)}, bf16[128,1024]{1,0:T(8,128)(2,1)S(1)}, u32[]{:S(2)}, u32[]{:S(2)}) collective-permute-start(bf16[128,1024]{1,0:T(8,128)(2,1)S(1)} %get-tuple-element.88._), channel_id=1, source_target_pairs={{0,4},{4,0},{8,12},{12,8},{16,20},{20,16},{24,28},{28,24},{1,5},{5... | collective-permute-start | bytes 786440 | tf_op jit(solution)/shard_map/ppermute | solution.py:735
  55.3 9.1 %collective-permute-start.10 = (bf16[256,2048]{1,0:T(8,128)(2,1)S(1)}, bf16[256,2048]{1,0:T(8,128)(2,1)S(1)}, u32[]{:S(2)}, u32[]{:S(2)}) collective-permute-start(bf16[256,2048]{1,0:T(8,128)(2,1)S(1)} %get-tuple-element.90._), channel_id=1, source_target_pairs={{0,1},{1,0},{2,3},{3,2},{4,5},{5,4},{6,7},{7,6},{8,9},{9,8},{10,11... | collective-permute-start | bytes 3145736 | tf_op jit(solution)/shard_map/ppermute | solution.py:735
  55.4 11.9 %collective-permute-start.11 = (bf16[256,2048]{1,0:T(8,128)(2,1)S(1)}, bf16[256,2048]{1,0:T(8,128)(2,1)S(1)}, u32[]{:S(2)}, u32[]{:S(2)}) collective-permute-start(bf16[256,2048]{1,0:T(8,128)(2,1)S(1)} %get-tuple-element.93), channel_id=1, source_target_pairs={{0,1},{1,0},{2,3},{3,2},{4,5},{5,4},{6,7},{7,6},{8,9},{9,8},{10,11... | collective-permute-start | bytes 3145736 | tf_op jit(solution)/shard_map/ppermute | solution.py:735
  55.9 5.8 %copy-start.1 = (bf16[2048,4096]{1,0:T(8,128)(2,1)}, bf16[2048,4096]{1,0:T(8,128)(2,1)S(1)}, u32[]{:S(2)}) copy-start(bf16[2048,4096]{1,0:T(8,128)(2,1)S(1)} %collective-permute-done.9.refs_4_.w1_far) | copy-start | bytes 50331652
  65.7 31.3 %collective-permute-start.19 = (bf16[256,512]{1,0:T(8,128)(2,1)S(1)}, bf16[256,512]{1,0:T(8,128)(2,1)S(1)}, u32[]{:S(2)}, u32[]{:S(2)}) collective-permute-start(bf16[256,512]{1,0:T(8,128)(2,1)S(1)} %project_ahead.1._), channel_id=1, source_target_pairs={{0,2},{1,3},{2,0},{3,1},{4,6},{5,7},{6,4},{7,5},{8,10},{9,11},{10,... | collective-permute-start | bytes 786440 | tf_op jit(solution)/shard_map/ppermute | solution.py:735
  71.7 25.8 %collective-permute-start.18 = (bf16[256,512]{1,0:T(8,128)(2,1)S(1)}, bf16[256,512]{1,0:T(8,128)(2,1)S(1)}, u32[]{:S(2)}, u32[]{:S(2)}) collective-permute-start(bf16[256,512]{1,0:T(8,128)(2,1)S(1)} %get-tuple-element.106), channel_id=1, source_target_pairs={{0,2},{1,3},{2,0},{3,1},{4,6},{5,7},{6,4},{7,5},{8,10},{9,11},{10,... | collective-permute-start | bytes 786440 | tf_op jit(solution)/shard_map/ppermute | solution.py:735
  79.3 19.8 %collective-permute-start.16 = (bf16[256,512]{1,0:T(8,128)(2,1)S(1)}, bf16[256,512]{1,0:T(8,128)(2,1)S(1)}, u32[]{:S(2)}, u32[]{:S(2)}) collective-permute-start(bf16[256,512]{1,0:T(8,128)(2,1)S(1)} %get-tuple-element.103), channel_id=1, source_target_pairs={{0,2},{1,3},{2,0},{3,1},{4,6},{5,7},{6,4},{7,5},{8,10},{9,11},{10,... | collective-permute-start | bytes 786440 | tf_op jit(solution)/shard_map/ppermute | solution.py:735
  80.9 23.2 %collective-permute-start.17 = (bf16[256,512]{1,0:T(8,128)(2,1)S(1)}, bf16[256,512]{1,0:T(8,128)(2,1)S(1)}, u32[]{:S(2)}, u32[]{:S(2)}) collective-permute-start(bf16[256,512]{1,0:T(8,128)(2,1)S(1)} %get-tuple-element.104), channel_id=1, source_target_pairs={{0,2},{1,3},{2,0},{3,1},{4,6},{5,7},{6,4},{7,5},{8,10},{9,11},{10,... | collective-permute-start | bytes 786440 | tf_op jit(solution)/shard_map/ppermute | solution.py:735
  88.4 16.6 %collective-permute-start.14 = (bf16[256,512]{1,0:T(8,128)(2,1)S(1)}, bf16[256,512]{1,0:T(8,128)(2,1)S(1)}, u32[]{:S(2)}, u32[]{:S(2)}) collective-permute-start(bf16[256,512]{1,0:T(8,128)(2,1)S(1)} %get-tuple-element.100), channel_id=1, source_target_pairs={{0,2},{1,3},{2,0},{3,1},{4,6},{5,7},{6,4},{7,5},{8,10},{9,11},{10,... | collective-permute-start | bytes 786440 | tf_op jit(solution)/shard_map/ppermute | solution.py:735
  97.0 9.3 %collective-permute-start.15 = (bf16[256,512]{1,0:T(8,128)(2,1)S(1)}, bf16[256,512]{1,0:T(8,128)(2,1)S(1)}, u32[]{:S(2)}, u32[]{:S(2)}) collective-permute-start(bf16[256,512]{1,0:T(8,128)(2,1)S(1)} %get-tuple-element.101), channel_id=1, source_target_pairs={{0,2},{1,3},{2,0},{3,1},{4,6},{5,7},{6,4},{7,5},{8,10},{9,11},{10,... | collective-permute-start | bytes 786440 | tf_op jit(solution)/shard_map/ppermute | solution.py:735
  97.5 14.4 %collective-permute-start.13 = (bf16[256,512]{1,0:T(8,128)(2,1)S(1)}, bf16[256,512]{1,0:T(8,128)(2,1)S(1)}, u32[]{:S(2)}, u32[]{:S(2)}) collective-permute-start(bf16[256,512]{1,0:T(8,128)(2,1)S(1)} %get-tuple-element.98), channel_id=1, source_target_pairs={{0,2},{1,3},{2,0},{3,1},{4,6},{5,7},{6,4},{7,5},{8,10},{9,11},{10,... | collective-permute-start | bytes 786440 | tf_op jit(solution)/shard_map/ppermute | solution.py:735
  99.1 16.1 %collective-permute-start.12 = (bf16[256,512]{1,0:T(8,128)(2,1)S(1)}, bf16[256,512]{1,0:T(8,128)(2,1)S(1)}, u32[]{:S(2)}, u32[]{:S(2)}) collective-permute-start(bf16[256,512]{1,0:T(8,128)(2,1)S(1)} %get-tuple-element.97), channel_id=1, source_target_pairs={{0,2},{1,3},{2,0},{3,1},{4,6},{5,7},{6,4},{7,5},{8,10},{9,11},{10,... | collective-permute-start | bytes 786440 | tf_op jit(solution)/shard_map/ppermute | solution.py:735

commit v17 on v16

--- a/solution.py
+++ b/solution.py
@@ -66,12 +66,9 @@
     return [pltpu.make_async_copy(x_far.at[at, lanes], x.at[at], sems.at[k]) for k, at in enumerate(pieces)]
 
 
-def decay_kernel(info, ld_t, step_t, skip, x_far, *refs):
+def decay_kernel(info, ld_t, step_t, skip, *refs):
     cum, cum_s, log_s, f_dev, f_blk, rates = [refs[2 * k : 2 * k + 2] for k in range(6)]
-    ones, x, sem = refs[12:]
-    copies = group_copies(x_far, x, info[GROUP], sem)
-    for copy in copies:
-        copy.start()
+    ones = refs[12]
     heads, length = ld_t.shape
     blocks = length // TOK_B
     per = heads // 2
@@ -133,11 +130,9 @@
             cum_s[g][:, rows] = shifted[own, :]
             f_blk[g][:, rows] = fade[own, :]
         put(f_dev, rows, jnp.exp2(total - (cums[b] + before[b])) * s)
-    for copy in copies:
-        copy.wait()
-
-
-def decays(info, log_decay, step, skip, x, width):
+
+
+def decays(info, log_decay, step, skip, width):
     length, heads = log_decay.shape
     blocks = length // TOK_B
     per = heads // 2
@@ -148,19 +143,17 @@
     shapes = [shape for shape in (column, across, across, pair, across, rates) for _ in range(2)]
     shapes += [
         jax.ShapeDtypeStruct((2 * per, width), BF16),
-        pltpu.VMEM((length, width), BF16),
     ]
-    *refs, ones, x_near = pl.pallas_call(
+    *refs, ones = pl.pallas_call(
         decay_kernel,
-        in_specs=[SCALAR] + [FULL] * 3 + [FAR],
+        in_specs=[SCALAR] + [FULL] * 3,
         out_specs=[FULL] * len(shapes),
         out_shape=shapes,
-        scratch_shapes=[pltpu.SemaphoreType.DMA((4,))],
         compiler_params=params(16),
         cost_estimate=CHEAP,
         name="decays",
-    )(info, *far(log_decay.T, step.T, skip[None, :], x))
-    return [tuple(refs[2 * k : 2 * k + 2]) for k in range(6)], ones, x_near
+    )(info, *far(log_decay.T, step.T, skip[None, :]))
+    return [tuple(refs[2 * k : 2 * k + 2]) for k in range(6)], ones
 
 
 def tail_kernel(x, bc, out):
@@ -207,6 +200,7 @@
     next_far, refs = refs[0], refs[1:]
     x_out, bc_out, final = refs[:3]
     xf, state, down = refs[-3:]
+    x_far, x, own_sem = (x, refs[5], refs[6]) if order == 0 else (None, x, None)
     length, width = x_out.shape
     rows = TOK_A
     group = info[GROUP + order]
@@ -215,6 +209,8 @@
     first_bc = pl.multiple_of(group * 2 * N, 2 * N)
     if order == 0:
         copies = group_copies(next_far, taken, info[GROUP + 1], sem)
+        for copy in group_copies(x_far, x, group, own_sem):
+            copy.start()
     else:
         part = length // 4
         pieces = [pl.ds(k * part, part) for k in range(4)]
@@ -245,6 +241,9 @@
 
     def step(i, _):
         at = pl.ds(pl.multiple_of(i * rows, rows), rows)
+        if order == 0:
+            source = x_far.at[at, pl.ds(first_lane, width)]
+            here = pltpu.make_async_copy(source, x.at[at], own_sem.at[i])
         behind = pl.ds(pl.multiple_of(jnp.maximum(i * rows - LEAD, 0), LEAD), LEAD)
 
         def out(r):
@@ -261,6 +260,8 @@
             weights = [jnp.where(group == 0, wbc[k, 0:1, ds], wbc[k, 1:2, ds]) for k in range(KCONV)]
             conv(i, bc[at, src], dot(down[...], bc[at, src]), halo[:, halo_src], bc[behind, src], weights, emit_bc)
 
+        if order == 0:
+            here.wait()
         for lanes in range(0, width, SLAB):
             ds = slice(lanes, lanes + SLAB)
             src = pl.ds(pl.multiple_of(first_lane + lanes, SLAB), SLAB)
@@ -287,8 +288,9 @@
 
 
 def conv_states(order, info, x, bc, halo, wx, wbc, f_dev, ones, rates, ahead):
-    length, width = x.shape
+    length, width = bc.shape[0], ones.shape[1]
     column = lambda i, info: (0, info[GROUP + order])
+    own = [] if order else [pltpu.VMEM((length, width), BF16), pltpu.SemaphoreType.DMA((4,))]
     final = ((N + EXTRA, width), BF16) if order == 0 else ((N, width), F32)
     taken = (length, width) if order == 0 else ahead.shape
     return pl.pallas_call(
@@ -296,10 +298,11 @@
         grid_spec=pltpu.PrefetchScalarGridSpec(
             num_scalar_prefetch=1,
             grid=(1,),
-            in_specs=[FULL] * 3 + [pl.BlockSpec((KCONV, width), column)] + [FULL] * 4 + [FAR],
+            in_specs=[FULL if order else FAR] + [FULL] * 2 + [pl.BlockSpec((KCONV, width), column)] + [FULL] * 4 + [FAR],
             out_specs=[FULL] * 4,
             scratch_shapes=[
                 pltpu.SemaphoreType.DMA((4,)),
+                *own,
                 pltpu.VMEM((TOK_A, width), BF16),
                 pltpu.VMEM((N, width), F32),
                 pltpu.VMEM((TOK_A, TOK_A), BF16),
@@ -804,15 +807,13 @@
     (bc_far,) = far(bc_input)
     halo = rotate(tail_rows(x_far, bc_far), 1)
     bc = bc_input.reshape(length, -1)
-
-    (cum, cum_s, log_s, f_dev, f_blk, rates), ones, x_sent = decays(
-        info, log_decay, step_size, skip_gain, x_input, half
-    )
+    (weight_mate,) = far(swap(out_weight, "head", 1))
+
+    (cum, cum_s, log_s, f_dev, f_blk, rates), ones = decays(info, log_decay, step_size, skip_gain, half)
     taps = far(conv_weight_x, conv_weight_bc)
     shared = (bc, halo, *taps)
-    x0, bc0, send, x_kept = conv_states(0, info, x_sent, *shared, f_dev[0], ones, rates[0], x_far)
+    x0, bc0, send, x_kept = conv_states(0, info, x_far, *shared, f_dev[0], ones, rates[0], x_far)
     got = swap(send, "seq", 1)
-    (weight_mate,) = far(swap(lax.optimization_barrier((out_weight, send))[0], "head", 1))
     x1, bc1, keep, z_near = conv_states(1, info, x_kept, *shared, f_dev[1], ones, rates[1], z_far)
     rates_kept = rates[1]
 
@@ -873,10 +874,12 @@
     columns = out_weight.shape[1]
     chunk = columns // 8
     weights = (w_far, weight_mate)
-    (kept,) = norm_rows(1, (0, 2, 1, 3), info, count, held, bc1, held, gain, uvs[B_PARTS:])
+    kept, w0, w1 = norm_rows(
+        1, (0, 2, 1, 3), info, count, held, bc1, held, gain, uvs[B_PARTS:], weights=weights, columns=chunk
+    )
     shared = (bc0, other, gain, uvs[:B_PARTS], kept)
     far_mate, near_mate = norm_rows(0, (0, 2), info, count, kept, *shared, apart=True)
-    owns, w0, w1 = norm_rows(0, (1, 3), info, count, far_mate, *shared, 2 * count, False, weights, chunk)
+    (owns,) = norm_rows(0, (1, 3), info, count, far_mate, *shared, 2 * count)
     far_mate = swap(far_mate, "head", 1)
     sent = project_ahead(owns, far_mate, w0, w1)
     first = swap(sent, "head", 2)

time: 116 us -> 112 us (0.966)
  local copies, waits for them, and re-layouts: 6.07 us -> 0.33 us
  waiting for transfers between devices: 10.7 us -> 13 us
  starting transfers between devices: 23.5 us -> 22.2 us
    unnamed x7 -> x5, local copies, waits for them, and re-layouts: 5.99 us -> 0.24 us
    ppermute x7, starting transfers between devices: 13.1 us -> 10.9 us  [rotate(): lax.ppermute(block, 'seq', [(i, (i + distance) % size) for i in range(siz...]
    ppermute x7, waiting for transfers between devices: 2.17 us -> 4.36 us  [rotate(): lax.ppermute(block, 'seq', [(i, (i + distance) % size) for i in range(siz...]
    pallas_call x2, Pallas kernels: 10.7 us -> 12.3 us  [conv_states(): pl.pallas_call(functools.partial(conv_kernel, order), grid_spec=pltpu.Pre...]
    pallas_call x1, Pallas kernels: 3.93 us -> 2.43 us  [decays(): pl.pallas_call(decay_kernel, in_specs=[SCALAR] + [FULL] * 3, out_specs=[F...]
  transfers between devices with their start and end apart: 20 -> 20, of which waited for: 7 -> 6; matrix products, arithmetic and copies ran while one was open for 0% -> 0% of each run, Pallas kernels for 59% -> 65%
where the time goes in v17:
time: 112 us; the launch traced here: 111 us
  Pallas kernels  75.4 us (67%)
  starting transfers between devices  22.2 us (20%)
  waiting for transfers between devices  13 us (12%)
    pallas_call x4, Pallas kernels, project_both(): pl.pallas_call(functools.partial(both_kernel, first // TILE, cut), grid=(...  25.2 us
    pallas_call x4, Pallas kernels, scan_part(): pl.pallas_call(functools.partial(scan_kernel, order, part), in_specs=[SCA...  15.5 us
    pallas_call x2, Pallas kernels, conv_states(): pl.pallas_call(functools.partial(conv_kernel, order), grid_spec=pltpu.Pre...  12.3 us
    ppermute x13, starting transfers between devices, swap(): lax.ppermute(block, axis, [(i, i ^ bit) for i in range(lax.axis_size(axis...  11.3 us
    ppermute x7, starting transfers between devices, rotate(): lax.ppermute(block, 'seq', [(i, (i + distance) % size) for i in range(siz...  10.9 us
    ppermute x13, waiting for transfers between devices, swap(): lax.ppermute(block, axis, [(i, i ^ bit) for i in range(lax.axis_size(axis...  8.66 us
    pallas_call x3, Pallas kernels, norm_rows(): pl.pallas_call(functools.partial(norm_kernel, order, places, skip, len(we...  7.57 us
    ppermute x7, waiting for transfers between devices, rotate(): lax.ppermute(block, 'seq', [(i, (i + distance) % size) for i in range(siz...  4.36 us
  transfers between devices with their start and end apart: 20, of which 6 were waited for; matrix products, arithmetic and copies ran while one was open for 0% of the time, Pallas kernels for 65%

profile of v17, /device:TPU:0, one launch (start us, length us, event | category | flops | bytes accessed | tf_op | source)
XLA Modules:
  0.0 111.2 jit_solution(8151637849518788784)
XLA Ops:
  1.3 2.7 %collective-permute-start = (bf16[16,2560]{1,0:T(8,128)(2,1)S(1)}, bf16[16,2560]{1,0:T(8,128)(2,1)S(1)}, u32[]{:S(2)}, u32[]{:S(2)}) collective-permute-start(bf16[16,2560]{1,0:T(8,128)(2,1)S(1)} %tail_rows.1), channel_id=1, source_target_pairs={{0,4},{4,8},{8,12},{12,16},{16,20},{20,24},{24,28},{28,0},{1,5},{5... | collective-permute-start | bytes 245768 | tf_op jit(solution)/shard_map/ppermute | solution.py:743
  4.1 2.4 %decays.1 = (f32[1024,16]{1,0:T(8,128)S(1)}, f32[1024,16]{1,0:T(8,128)S(1)}, f32[16,1024]{1,0:T(8,128)S(1)}, f32[16,1024]{1,0:T(8,128)S(1)}, f32[16,1024]{1,0:T(...) custom-call(s32[9]{0:T(128)S(1)} %stack.36.info, ...), custom_call_target="tpu_custom_call" | custom-call | flops 1 | bytes 1 | tf_op jit(solution)/shard_map/decays/pallas_call | solution.py:147
  6.8 3.3 %collective-permute-done.halo = bf16[16,2560]{1,0:T(8,128)(2,1)S(1)} collective-permute-done((bf16[16,2560]{1,0:T(8,128)(2,1)S(1)}, bf16[16,2560]{1,0:T(8,128)(2,1)S(1)}, u32[]{:S(2)}, u32[]{:S(2)}) %collective-permute-start) | collective-permute-done | bytes 81952 | tf_op jit(solution)/shard_map/ppermute | solution.py:743
  10.1 6.8 %conv_states.2 = (bf16[1024,1024]{1,0:T(8,128)(2,1)S(1)}, bf16[1024,256]{1,0:T(8,128)(2,1)S(1)}, bf16[144,1024]{1,0:T(8,128)(2,1)S(1)}, bf16[1024,1024]{1,0:T(8,128)(2,1)S(1)}) custom-call(s32[9]{0:T(128)S(1)} %stack.36.info, bf16[1024,2048]{1,0:T(8,128)(2,1)} %refs_0_.2, bf16[1024,512]{1,0:T(8,128)(2,1)S(1)} %bitcast.14, ...), custom_call_target="tpu_custom_call" | custom-call | flops 1 | bytes 1 | tf_op jit(solution)/shard_map/conv_states/pallas_call | solution.py:296
  17.0 5.4 %conv_states.3 = (bf16[1024,1024]{1,0:T(8,128)(2,1)S(1)}, bf16[1024,256]{1,0:T(8,128)(2,1)S(1)}, f32[128,1024]{1,0:T(8,128)S(1)}, bf16[1024,2048]{1,0:T(8,128)(2,1)S(1)}) custom-call(s32[9]{0:T(128)S(1)} %stack.36.info, bf16[1024,1024]{1,0:T(8,128)(2,1)S(1)} %get-tuple-element.59.x, bf16[1024,512]{1,0:T(8,128)(2,1)S(1)} %bitcast.15, ...), custom_call_target="tpu_custom_call" | custom-call | flops 1 | bytes 1 | tf_op jit(solution)/shard_map/conv_states/pallas_call | solution.py:296
  22.4 3.9 %scan_part.4._.refs_0_ = bf16[1024,1024]{1,0:T(8,128)(2,1)S(1)} custom-call(s32[9]{0:T(128)S(1)} %stack.36.info, bf16[1024,1024]{1,0:T(8,128)(2,1)S(1)} %get-tuple-element.63.x, bf16[1024,2048]{1,0:T(8,128)(2,1)S(1)} %get-tuple-element.64.z, bf16[1024,256]{1,0:T(8,128)(2,1)S(1)} %get-tuple-element.57.bc, f32[1024,16]{1,0:T(8,128)S(1)} %get-tuple-element.65.cum, ...), custom_call_target="tpu_custom_call" | custom-call | flops 1 | bytes 1 | tf_op jit(solution)/shard_map/scan_part/pallas_call | solution.py:495
  27.6 2.6 %collective-permute-start.3 = (bf16[144,256]{1,0:T(8,128)(2,1)S(1)}, bf16[144,256]{1,0:T(8,128)(2,1)S(1)}, u32[]{:S(2)}, u32[]{:S(2)}) collective-permute-start(bf16[144,256]{1,0:T(8,128)(2,1)S(1)} %get-tuple-element.79), channel_id=1, source_target_pairs={{0,16},{4,20},{8,24},{12,28},{16,0},{20,4},{24,8},{28,12},{1,17},{... | collective-permute-start | bytes 221192 | tf_op jit(solution)/shard_map/ppermute | solution.py:743
  31.5 3.9 %scan_part.5.refs_4_.refs_1_ = bf16[1024,1024]{1,0:T(8,128)(2,1)S(1)} custom-call(s32[9]{0:T(128)S(1)} %stack.36.info, bf16[1024,1024]{1,0:T(8,128)(2,1)S(1)} %get-tuple-element.63.x, bf16[1024,2048]{1,0:T(8,128)(2,1)S(1)} %get-tuple-element.64.z, bf16[1024,256]{1,0:T(8,128)(2,1)S(1)} %get-tuple-element.57.bc, f32[1024,16]{1,0:T(8,128)S(1)} %get-tuple-element.65.cum, ...), custom_call_target="tpu_custom_call" | custom-call | flops 1 | bytes 1 | tf_op jit(solution)/shard_map/scan_part/pallas_call | solution.py:495
  38.3 1.5 %collective-permute-start.6 = (bf16[128,256]{1,0:T(8,128)(2,1)S(1)}, bf16[128,256]{1,0:T(8,128)(2,1)S(1)}, u32[]{:S(2)}, u32[]{:S(2)}) collective-permute-start(bf16[128,256]{1,0:T(8,128)(2,1)S(1)} %get-tuple-element.83), channel_id=1, source_target_pairs={{0,16},{4,20},{8,24},{12,28},{16,0},{20,4},{24,8},{28,12},{1,17},{... | collective-permute-start | bytes 196616 | tf_op jit(solution)/shard_map/ppermute | solution.py:743
  40.8 3.9 %scan_part.6._.refs_0_ = bf16[1024,1024]{1,0:T(8,128)(2,1)S(1)} custom-call(s32[9]{0:T(128)S(1)} %stack.36.info, bf16[1024,1024]{1,0:T(8,128)(2,1)S(1)} %get-tuple-element.71.x, bf16[1024,2048]{1,0:T(8,128)(2,1)S(1)} %get-tuple-element.64.z, bf16[1024,256]{1,0:T(8,128)(2,1)S(1)} %get-tuple-element.72.bc, f32[1024,16]{1,0:T(8,128)S(1)} %get-tuple-element.73.cum, ...), custom_call_target="tpu_custom_call" | custom-call | flops 1 | bytes 1 | tf_op jit(solution)/shard_map/scan_part/pallas_call | solution.py:495
  45.8 1.8 %collective-permute-start.8 = (bf16[128,1024]{1,0:T(8,128)(2,1)S(1)}, bf16[128,1024]{1,0:T(8,128)(2,1)S(1)}, u32[]{:S(2)}, u32[]{:S(2)}) collective-permute-start(bf16[128,1024]{1,0:T(8,128)(2,1)S(1)} %get-tuple-element.85._), channel_id=1, source_target_pairs={{0,4},{4,0},{8,12},{12,8},{16,20},{20,16},{24,28},{28,24},{1,5},{5... | collective-permute-start | bytes 786440 | tf_op jit(solution)/shard_map/ppermute | solution.py:738
  47.6 3.8 %scan_part.7.refs_1_ = bf16[1024,1024]{1,0:T(8,128)(2,1)S(1)} custom-call(s32[9]{0:T(128)S(1)} %stack.36.info, bf16[1024,1024]{1,0:T(8,128)(2,1)S(1)} %get-tuple-element.71.x, bf16[1024,2048]{1,0:T(8,128)(2,1)S(1)} %get-tuple-element.64.z, bf16[1024,256]{1,0:T(8,128)(2,1)S(1)} %get-tuple-element.72.bc, f32[1024,16]{1,0:T(8,128)S(1)} %get-tuple-element.73.cum, ...), custom_call_target="tpu_custom_call" | custom-call | flops 1 | bytes 1 | tf_op jit(solution)/shard_map/scan_part/pallas_call | solution.py:495
  51.5 3.4 %norm_rows.3 = (bf16[1024,1024]{1,0:T(8,128)(2,1)S(1)}, bf16[2048,512]{1,0:T(8,128)(2,1)S(1)}, bf16[2048,512]{1,0:T(8,128)(2,1)S(1)}) custom-call(s32[9]{0:T(128)S(1)} %stack.36.info, bf16[1024,256]{1,0:T(8,128)(2,1)S(1)} %get-tuple-element.72.bc, bf16[128,1024]{1,0:T(8,128)(2,1)S(1)} %get-tuple-element.86.state._, f32[1,2048]{1,0:T(1,128)S(1)} %bitcast.16, ...), custom_call_target="tpu_custom_call" | custom-call | flops 1 | bytes 1 | tf_op jit(solution)/shard_map/norm_rows/pallas_call | solution.py:566
  54.8 2.1 %norm_rows.4 = (bf16[256,2048]{1,0:T(8,128)(2,1)S(1)}, bf16[256,2048]{1,0:T(8,128)(2,1)S(1)}) custom-call(s32[9]{0:T(128)S(1)} %stack.36.info, bf16[1024,256]{1,0:T(8,128)(2,1)S(1)} %get-tuple-element.57.bc, bf16[128,1024]{1,0:T(8,128)(2,1)S(1)} %collective-permute-done.8.state, f32[1,2048]{1,0:T(1,128)S(1)} %bitcast.17, ...), custom_call_target="tpu_custom_call" | custom-call | flops 1 | bytes 1 | tf_op jit(solution)/shard_map/norm_rows/pallas_call | solution.py:566
  57.5 2.1 %norm_rows.5.owns = bf16[512,2048]{1,0:T(8,128)(2,1)S(1)} custom-call(s32[9]{0:T(128)S(1)} %stack.36.info, bf16[1024,256]{1,0:T(8,128)(2,1)S(1)} %get-tuple-element.57.bc, bf16[128,1024]{1,0:T(8,128)(2,1)S(1)} %collective-permute-done.8.state, f32[1,2048]{1,0:T(1,128)S(1)} %bitcast.18, bf16[256,2048]{1,0:T(8,128)(2,1)S(1)} %get-tuple-element.88._, ...), custom_call_target="tpu_custom_call" | custom-call | flops 1 | bytes 1 | tf_op jit(solution)/shard_map/norm_rows/pallas_call | solution.py:566
  62.6 4.3 %project_both.7 = (bf16[256,512]{1,0:T(8,128)(2,1)S(1)}, f32[256,512]{1,0:T(8,128)S(1)}) custom-call(bf16[512,2048]{1,0:T(8,128)(2,1)S(1)} %norm_rows.5.owns, bf16[512,2048]{1,0:T(8,128)(2,1)S(1)} %join.1.mates, bf16[2048,4096]{1,0:T(8,128)(2,1)} %w0_far.9, bf16[2048,4096]{1,0:T(8,128)(2,1)} %collective-permute-done.9.refs_3_.w1_far), custom_call_target="tpu_custom_call" | custom-call | flops 1 | bytes 1 | tf_op jit(solution)/shard_map/project_both/pallas_call | solution.py:671
  67.5 7.0 %project_both.6 = (bf16[256,512]{1,0:T(8,128)(2,1)S(1)}, bf16[256,512]{1,0:T(8,128)(2,1)S(1)}, f32[256,1024]{1,0:T(8,128)S(1)}) custom-call(bf16[512,2048]{1,0:T(8,128)(2,1)S(1)} %norm_rows.5.owns, bf16[512,2048]{1,0:T(8,128)(2,1)S(1)} %join.1.mates, bf16[2048,4096]{1,0:T(8,128)(2,1)} %w0_far.9, bf16[2048,4096]{1,0:T(8,128)(2,1)} %collective-permute-done.9.refs_3_.w1_far), custom_call_target="tpu_custom_call" | custom-call | flops 1 | bytes 1 | tf_op jit(solution)/shard_map/project_both/pallas_call | solution.py:671
  74.5 1.5 %collective-permute-start.16 = (bf16[256,512]{1,0:T(8,128)(2,1)S(1)}, bf16[256,512]{1,0:T(8,128)(2,1)S(1)}, u32[]{:S(2)}, u32[]{:S(2)}) collective-permute-start(bf16[256,512]{1,0:T(8,128)(2,1)S(1)} %get-tuple-element.99), channel_id=1, source_target_pairs={{0,2},{1,3},{2,0},{3,1},{4,6},{5,7},{6,4},{7,5},{8,10},{9,11},{10,... | collective-permute-start | bytes 786440 | tf_op jit(solution)/shard_map/ppermute | solution.py:738
  76.6 7.0 %project_both.5 = (bf16[256,512]{1,0:T(8,128)(2,1)S(1)}, bf16[256,512]{1,0:T(8,128)(2,1)S(1)}, f32[256,1024]{1,0:T(8,128)S(1)}) custom-call(bf16[512,2048]{1,0:T(8,128)(2,1)S(1)} %norm_rows.5.owns, bf16[512,2048]{1,0:T(8,128)(2,1)S(1)} %join.1.mates, bf16[2048,4096]{1,0:T(8,128)(2,1)} %w0_far.9, bf16[2048,4096]{1,0:T(8,128)(2,1)} %collective-permute-done.9.refs_3_.w1_far), custom_call_target="tpu_custom_call" | custom-call | flops 1 | bytes 1 | tf_op jit(solution)/shard_map/project_both/pallas_call | solution.py:671
  83.6 1.5 %collective-permute-start.14 = (bf16[256,512]{1,0:T(8,128)(2,1)S(1)}, bf16[256,512]{1,0:T(8,128)(2,1)S(1)}, u32[]{:S(2)}, u32[]{:S(2)}) collective-permute-start(bf16[256,512]{1,0:T(8,128)(2,1)S(1)} %get-tuple-element.96), channel_id=1, source_target_pairs={{0,2},{1,3},{2,0},{3,1},{4,6},{5,7},{6,4},{7,5},{8,10},{9,11},{10,... | collective-permute-start | bytes 786440 | tf_op jit(solution)/shard_map/ppermute | solution.py:738
  85.1 7.0 %project_both.4 = (bf16[256,512]{1,0:T(8,128)(2,1)S(1)}, bf16[256,512]{1,0:T(8,128)(2,1)S(1)}, f32[256,1024]{1,0:T(8,128)S(1)}) custom-call(bf16[512,2048]{1,0:T(8,128)(2,1)S(1)} %norm_rows.5.owns, bf16[512,2048]{1,0:T(8,128)(2,1)S(1)} %join.1.mates, bf16[2048,4096]{1,0:T(8,128)(2,1)} %w0_far.9, bf16[2048,4096]{1,0:T(8,128)(2,1)} %collective-permute-done.9.refs_3_.w1_far), custom_call_target="tpu_custom_call" | custom-call | flops 1 | bytes 1 | tf_op jit(solution)/shard_map/project_both/pallas_call | solution.py:671
  94.8 3.8 %project_near.1.refs_1_ = bf16[256,4096]{1,0:T(8,128)(2,1)} custom-call(bf16[512,2048]{1,0:T(8,128)(2,1)S(1)} %norm_rows.5.owns, bf16[512,2048]{1,0:T(8,128)(2,1)S(1)} %join.1.mates, bf16[2048,4096]{1,0:T(8,128)(2,1)} %w0_far.9, bf16[2048,4096]{1,0:T(8,128)(2,1)} %collective-permute-done.9.refs_3_.w1_far, bf16[256,512]{1,0:T(8,128)(2,1)S(1)} %collective-permute-done.19.arrived), custom_call_target="tpu_custom_call" | custom-call | flops 1 | bytes 1 | tf_op jit(solution)/shard_map/project_near/pallas_call | solution.py:695
  102.3 4.7 %collective-permute-done.13.refs_0_ = bf16[256,512]{1,0:T(8,128)(2,1)S(1)} collective-permute-done((bf16[256,512]{1,0:T(8,128)(2,1)S(1)}, bf16[256,512]{1,0:T(8,128)(2,1)S(1)}, u32[]{:S(2)}, u32[]{:S(2)}) %collective-permute-start.13) | collective-permute-done | bytes 262176 | tf_op jit(solution)/shard_map/ppermute | solution.py:738
  107.8 2.7 %collective-permute-done.12.refs_0_ = bf16[256,512]{1,0:T(8,128)(2,1)S(1)} collective-permute-done((bf16[256,512]{1,0:T(8,128)(2,1)S(1)}, bf16[256,512]{1,0:T(8,128)(2,1)S(1)}, u32[]{:S(2)}, u32[]{:S(2)}) %collective-permute-start.12) | collective-permute-done | bytes 262176 | tf_op jit(solution)/shard_map/ppermute | solution.py:738
  (48 shorter events, 21.8 us)
Async XLA Ops:
  0.0 6.5 %copy-start.1 = (bf16[1024,2,256]{2,1,0:T(2,128)(2,1)S(1)}, bf16[1024,2,256]{2,1,0:T(2,128)(2,1)}, u32[]{:S(2)}) copy-start(bf16[1024,2,256]{2,1,0:T(2,128)(2,1)} %bc.1) | copy-start | bytes 3145732
  0.0 51.4 %collective-permute-start.9 = (bf16[2048,4096]{1,0:T(8,128)(2,1)}, bf16[2048,4096]{1,0:T(8,128)(2,1)}, u32[]{:S(2)}, u32[]{:S(2)}) collective-permute-start(bf16[2048,4096]{1,0:T(8,128)(2,1)} %w0_far.9), channel_id=1, source_target_pairs={{0,1},{1,0},{2,3},{3,2},{4,5},{5,4},{6,7},{7,6},{8,9},{9,8},{10,11... | collective-permute-start | bytes 50331656 | tf_op jit(solution)/shard_map/ppermute | solution.py:738
  1.3 8.7 %collective-permute-start = (bf16[16,2560]{1,0:T(8,128)(2,1)S(1)}, bf16[16,2560]{1,0:T(8,128)(2,1)S(1)}, u32[]{:S(2)}, u32[]{:S(2)}) collective-permute-start(bf16[16,2560]{1,0:T(8,128)(2,1)S(1)} %tail_rows.1), channel_id=1, source_target_pairs={{0,4},{4,8},{8,12},{12,16},{16,20},{20,24},{24,28},{28,0},{1,5},{5... | collective-permute-start | bytes 245768 | tf_op jit(solution)/shard_map/ppermute | solution.py:743
  16.9 9.4 %collective-permute-start.1 = (bf16[144,1024]{1,0:T(8,128)(2,1)S(1)}, bf16[144,1024]{1,0:T(8,128)(2,1)S(1)}, u32[]{:S(2)}, u32[]{:S(2)}) collective-permute-start(bf16[144,1024]{1,0:T(8,128)(2,1)S(1)} %get-tuple-element.58), channel_id=1, source_target_pairs={{0,4},{4,0},{8,12},{12,8},{16,20},{20,16},{24,28},{28,24},{1,5},{5... | collective-permute-start | bytes 884744 | tf_op jit(solution)/shard_map/ppermute | solution.py:738
  27.2 8.2 %collective-permute-start.2 = (bf16[144,256]{1,0:T(8,128)(2,1)S(1)}, bf16[144,256]{1,0:T(8,128)(2,1)S(1)}, u32[]{:S(2)}, u32[]{:S(2)}) collective-permute-start(bf16[144,256]{1,0:T(8,128)(2,1)S(1)} %get-tuple-element.78), channel_id=1, source_target_pairs={{0,8},{4,12},{8,16},{12,20},{16,24},{20,28},{24,0},{28,4},{1,9},{5... | collective-permute-start | bytes 221192 | tf_op jit(solution)/shard_map/ppermute | solution.py:743
  27.6 8.6 %collective-permute-start.3 = (bf16[144,256]{1,0:T(8,128)(2,1)S(1)}, bf16[144,256]{1,0:T(8,128)(2,1)S(1)}, u32[]{:S(2)}, u32[]{:S(2)}) collective-permute-start(bf16[144,256]{1,0:T(8,128)(2,1)S(1)} %get-tuple-element.79), channel_id=1, source_target_pairs={{0,16},{4,20},{8,24},{12,28},{16,0},{20,4},{24,8},{28,12},{1,17},{... | collective-permute-start | bytes 221192 | tf_op jit(solution)/shard_map/ppermute | solution.py:743
  30.1 6.0 %collective-permute-start.4 = (bf16[144,256]{1,0:T(8,128)(2,1)S(1)}, bf16[144,256]{1,0:T(8,128)(2,1)S(1)}, u32[]{:S(2)}, u32[]{:S(2)}) collective-permute-start(bf16[144,256]{1,0:T(8,128)(2,1)S(1)} %get-tuple-element.80), channel_id=1, source_target_pairs={{0,24},{4,28},{8,0},{12,4},{16,8},{20,12},{24,16},{28,20},{1,25},{... | collective-permute-start | bytes 221192 | tf_op jit(solution)/shard_map/ppermute | solution.py:743
  36.8 7.8 %collective-permute-start.5 = (bf16[128,256]{1,0:T(8,128)(2,1)S(1)}, bf16[128,256]{1,0:T(8,128)(2,1)S(1)}, u32[]{:S(2)}, u32[]{:S(2)}) collective-permute-start(bf16[128,256]{1,0:T(8,128)(2,1)S(1)} %get-tuple-element.82), channel_id=1, source_target_pairs={{0,8},{4,12},{8,16},{12,20},{16,24},{20,28},{24,0},{28,4},{1,9},{5... | collective-permute-start | bytes 196616 | tf_op jit(solution)/shard_map/ppermute | solution.py:743
  38.3 6.6 %collective-permute-start.6 = (bf16[128,256]{1,0:T(8,128)(2,1)S(1)}, bf16[128,256]{1,0:T(8,128)(2,1)S(1)}, u32[]{:S(2)}, u32[]{:S(2)}) collective-permute-start(bf16[128,256]{1,0:T(8,128)(2,1)S(1)} %get-tuple-element.83), channel_id=1, source_target_pairs={{0,16},{4,20},{8,24},{12,28},{16,0},{20,4},{24,8},{28,12},{1,17},{... | collective-permute-start | bytes 196616 | tf_op jit(solution)/shard_map/ppermute | solution.py:743
  39.8 5.1 %collective-permute-start.7 = (bf16[128,256]{1,0:T(8,128)(2,1)S(1)}, bf16[128,256]{1,0:T(8,128)(2,1)S(1)}, u32[]{:S(2)}, u32[]{:S(2)}) collective-permute-start(bf16[128,256]{1,0:T(8,128)(2,1)S(1)} %get-tuple-element.84), channel_id=1, source_target_pairs={{0,24},{4,28},{8,0},{12,4},{16,8},{20,12},{24,16},{28,20},{1,25},{... | collective-permute-start | bytes 196616 | tf_op jit(solution)/shard_map/ppermute | solution.py:743
  45.8 5.7 %copy-start = (f32[2048]{0:T(1024)S(1)}, f32[2048]{0:T(1024)}, u32[]{:S(2)}) copy-start(f32[2048]{0:T(1024)} %param.18) | copy-start | bytes 24580
  45.8 9.1 %collective-permute-start.8 = (bf16[128,1024]{1,0:T(8,128)(2,1)S(1)}, bf16[128,1024]{1,0:T(8,128)(2,1)S(1)}, u32[]{:S(2)}, u32[]{:S(2)}) collective-permute-start(bf16[128,1024]{1,0:T(8,128)(2,1)S(1)} %get-tuple-element.85._), channel_id=1, source_target_pairs={{0,4},{4,0},{8,12},{12,8},{16,20},{20,16},{24,28},{28,24},{1,5},{5... | collective-permute-start | bytes 786440 | tf_op jit(solution)/shard_map/ppermute | solution.py:738
  56.9 2.7 %collective-permute-start.10 = (bf16[256,2048]{1,0:T(8,128)(2,1)S(1)}, bf16[256,2048]{1,0:T(8,128)(2,1)S(1)}, u32[]{:S(2)}, u32[]{:S(2)}) collective-permute-start(bf16[256,2048]{1,0:T(8,128)(2,1)S(1)} %get-tuple-element.88._), channel_id=1, source_target_pairs={{0,1},{1,0},{2,3},{3,2},{4,5},{5,4},{6,7},{7,6},{8,9},{9,8},{10,11... | collective-permute-start | bytes 3145736 | tf_op jit(solution)/shard_map/ppermute | solution.py:738
  57.0 5.4 %collective-permute-start.11 = (bf16[256,2048]{1,0:T(8,128)(2,1)S(1)}, bf16[256,2048]{1,0:T(8,128)(2,1)S(1)}, u32[]{:S(2)}, u32[]{:S(2)}) collective-permute-start(bf16[256,2048]{1,0:T(8,128)(2,1)S(1)} %get-tuple-element.89), channel_id=1, source_target_pairs={{0,1},{1,0},{2,3},{3,2},{4,5},{5,4},{6,7},{7,6},{8,9},{9,8},{10,11... | collective-permute-start | bytes 3145736 | tf_op jit(solution)/shard_map/ppermute | solution.py:738
  60.9 31.2 %collective-permute-start.19 = (bf16[256,512]{1,0:T(8,128)(2,1)S(1)}, bf16[256,512]{1,0:T(8,128)(2,1)S(1)}, u32[]{:S(2)}, u32[]{:S(2)}) collective-permute-start(bf16[256,512]{1,0:T(8,128)(2,1)S(1)} %project_ahead.1._), channel_id=1, source_target_pairs={{0,2},{1,3},{2,0},{3,1},{4,6},{5,7},{6,4},{7,5},{8,10},{9,11},{10,... | collective-permute-start | bytes 786440 | tf_op jit(solution)/shard_map/ppermute | solution.py:738
  66.9 25.9 %collective-permute-start.18 = (bf16[256,512]{1,0:T(8,128)(2,1)S(1)}, bf16[256,512]{1,0:T(8,128)(2,1)S(1)}, u32[]{:S(2)}, u32[]{:S(2)}) collective-permute-start(bf16[256,512]{1,0:T(8,128)(2,1)S(1)} %get-tuple-element.102), channel_id=1, source_target_pairs={{0,2},{1,3},{2,0},{3,1},{4,6},{5,7},{6,4},{7,5},{8,10},{9,11},{10,... | collective-permute-start | bytes 786440 | tf_op jit(solution)/shard_map/ppermute | solution.py:738
  74.5 19.7 %collective-permute-start.16 = (bf16[256,512]{1,0:T(8,128)(2,1)S(1)}, bf16[256,512]{1,0:T(8,128)(2,1)S(1)}, u32[]{:S(2)}, u32[]{:S(2)}) collective-permute-start(bf16[256,512]{1,0:T(8,128)(2,1)S(1)} %get-tuple-element.99), channel_id=1, source_target_pairs={{0,2},{1,3},{2,0},{3,1},{4,6},{5,7},{6,4},{7,5},{8,10},{9,11},{10,... | collective-permute-start | bytes 786440 | tf_op jit(solution)/shard_map/ppermute | solution.py:738
  76.0 23.3 %collective-permute-start.17 = (bf16[256,512]{1,0:T(8,128)(2,1)S(1)}, bf16[256,512]{1,0:T(8,128)(2,1)S(1)}, u32[]{:S(2)}, u32[]{:S(2)}) collective-permute-start(bf16[256,512]{1,0:T(8,128)(2,1)S(1)} %get-tuple-element.100), channel_id=1, source_target_pairs={{0,2},{1,3},{2,0},{3,1},{4,6},{5,7},{6,4},{7,5},{8,10},{9,11},{10,... | collective-permute-start | bytes 786440 | tf_op jit(solution)/shard_map/ppermute | solution.py:738
  83.6 16.6 %collective-permute-start.14 = (bf16[256,512]{1,0:T(8,128)(2,1)S(1)}, bf16[256,512]{1,0:T(8,128)(2,1)S(1)}, u32[]{:S(2)}, u32[]{:S(2)}) collective-permute-start(bf16[256,512]{1,0:T(8,128)(2,1)S(1)} %get-tuple-element.96), channel_id=1, source_target_pairs={{0,2},{1,3},{2,0},{3,1},{4,6},{5,7},{6,4},{7,5},{8,10},{9,11},{10,... | collective-permute-start | bytes 786440 | tf_op jit(solution)/shard_map/ppermute | solution.py:738
  92.1 9.3 %collective-permute-start.15 = (bf16[256,512]{1,0:T(8,128)(2,1)S(1)}, bf16[256,512]{1,0:T(8,128)(2,1)S(1)}, u32[]{:S(2)}, u32[]{:S(2)}) collective-permute-start(bf16[256,512]{1,0:T(8,128)(2,1)S(1)} %get-tuple-element.97), channel_id=1, source_target_pairs={{0,2},{1,3},{2,0},{3,1},{4,6},{5,7},{6,4},{7,5},{8,10},{9,11},{10,... | collective-permute-start | bytes 786440 | tf_op jit(solution)/shard_map/ppermute | solution.py:738
  92.8 14.3 %collective-permute-start.13 = (bf16[256,512]{1,0:T(8,128)(2,1)S(1)}, bf16[256,512]{1,0:T(8,128)(2,1)S(1)}, u32[]{:S(2)}, u32[]{:S(2)}) collective-permute-start(bf16[256,512]{1,0:T(8,128)(2,1)S(1)} %get-tuple-element.94), channel_id=1, source_target_pairs={{0,2},{1,3},{2,0},{3,1},{4,6},{5,7},{6,4},{7,5},{8,10},{9,11},{10,... | collective-permute-start | bytes 786440 | tf_op jit(solution)/shard_map/ppermute | solution.py:738
  94.2 16.3 %collective-permute-start.12 = (bf16[256,512]{1,0:T(8,128)(2,1)S(1)}, bf16[256,512]{1,0:T(8,128)(2,1)S(1)}, u32[]{:S(2)}, u32[]{:S(2)}) collective-permute-start(bf16[256,512]{1,0:T(8,128)(2,1)S(1)} %get-tuple-element.93), channel_id=1, source_target_pairs={{0,2},{1,3},{2,0},{3,1},{4,6},{5,7},{6,4},{7,5},{8,10},{9,11},{10,... | collective-permute-start | bytes 786440 | tf_op jit(solution)/shard_map/ppermute | solution.py:738

commit v18 on v17

--- a/solution.py
+++ b/solution.py
@@ -504,10 +504,8 @@
     )(info, x, z, bc, cum, cum_s, log_s, f_blk, rates, token)
 
 
-def norm_kernel(order, places, skip, fetched, info, bc, state, gain, _, *refs):
+def norm_kernel(order, places, fetched, info, bc, state, gain, _, *refs):
     uvs, refs = refs[:B_PARTS], refs[B_PARTS:]
-    if order == 0:
-        kept, refs = refs[0], refs[1:]
     weights, outs, tiles, sem = refs[:fetched], refs[fetched : -1 - fetched], refs[len(refs) - 1 - fetched : -1], refs[-1]
     copies = [
         pltpu.make_async_copy(weight.at[:, pl.ds(0, tile.shape[1])], tile, sem.at[k])
@@ -515,14 +513,12 @@
     ]
     for copy in copies:
         copy.start()
-    count = outs[0].shape[0] * len(outs) // len(places)
+    each = len(places) // len(outs)
+    count = outs[0].shape[0] // each
     per = state.shape[1]
     part = per // B_PARTS
 
-    def lanes(group, p=0, size=per):
-        return pl.ds(pl.multiple_of(info[GROUP + group] * per + p * part, part), size)
-
-    def rows(out, first, base, source):
+    def rows(out, first, base):
         to = pl.ds(pl.multiple_of(first, ROWS_C), ROWS_C)
         at = pl.ds(pl.multiple_of(base, ROWS_C), ROWS_C)
         c_mat = bc[at, N : 2 * N]
@@ -536,20 +532,13 @@
             pieces.append(gated)
         scale = lax.rsqrt(squares * (1.0 / per) + EPS)
         for p, gated in enumerate(pieces):
-            value = (gated * scale * gain[:, lanes(order, p, part)]).astype(BF16)
-            if order == 0:
-                out[to, lanes(0, p, part)] = value
-            else:
-                out[to, p * part : (p + 1) * part] = value
-        if order == 0:
-            out[to, lanes(1)] = kept[pl.ds(pl.multiple_of(source, ROWS_C), ROWS_C), :]
+            lanes = pl.ds(pl.multiple_of(info[GROUP + order] * per + p * part, part), part)
+            out[to, p * part : (p + 1) * part] = (gated * scale * gain[:, lanes]).astype(BF16)
 
     for k, place in enumerate(places):
 
         def step(j, _):
-            out, first = (outs[k], 0) if len(outs) > 1 else (outs[0], k * count)
-            source = skip + k * count + j * ROWS_C
-            rows(out, first + j * ROWS_C, info[ROWS + place] * count + j * ROWS_C, source)
+            rows(outs[k // each], (k % each) * count + j * ROWS_C, info[ROWS + place] * count + j * ROWS_C)
             return 0
 
         lax.fori_loop(0, count // ROWS_C, step, 0)
@@ -557,22 +546,19 @@
         copy.wait()
 
 
-def norm_rows(order, places, info, count, token, bc, state, gain, uvs, kept=None, skip=0, apart=False, weights=(), columns=0):
-    width = state.shape[1] if order else gain.shape[1]
+def norm_rows(order, places, arrays, info, count, token, bc, state, gain, uvs, weights=(), columns=0):
     tile = jax.ShapeDtypeStruct((gain.shape[1], columns), BF16)
-    arrays = len(places) if apart else 1
-    rows = jax.ShapeDtypeStruct((len(places) * count // arrays, width), BF16)
-    joined = [] if kept is None else [kept]
+    rows = jax.ShapeDtypeStruct((len(places) * count // arrays, state.shape[1]), BF16)
     return pl.pallas_call(
-        functools.partial(norm_kernel, order, places, skip, len(weights)),
-        in_specs=[SCALAR] + [FULL] * 3 + [ANY] + [FULL] * (len(uvs) + len(joined)) + [FAR] * len(weights),
+        functools.partial(norm_kernel, order, places, len(weights)),
+        in_specs=[SCALAR] + [FULL] * 3 + [ANY] + [FULL] * len(uvs) + [FAR] * len(weights),
         out_specs=[FULL] * (arrays + len(weights)),
         out_shape=[rows] * arrays + [tile] * len(weights),
         scratch_shapes=[pltpu.SemaphoreType.DMA((2,))],
         compiler_params=params(16),
         cost_estimate=CHEAP,
         name="norm_rows",
-    )(info, bc, state, gain, token, *uvs, *joined, *weights)
+    )(info, bc, state, gain, token, *uvs, *weights)
 
 
 def stream(base, w0_far, w1_far, w0, w1, sem):
@@ -612,20 +598,30 @@
     ]
 
 
-def ahead_kernel(owns, mate, w0, w1, out):
-    out[...] = (dot(owns[0 : out.shape[0], :], w0[...]) + dot(mate[...], w1[...])).astype(BF16)
-
-
-def project_ahead(owns, mate, w0, w1):
+def group_rows(info, order, depth):
+    return pl.ds(pl.multiple_of(info[GROUP + order] * (depth // 2), depth // 2), depth // 2)
+
+
+def ahead_kernel(info, own0, own1, mate0, mate1, w0, w1, out):
+    rows = slice(0, out.shape[0])
+    total = None
+    for order, (own, mate) in enumerate(((own0, mate0), (own1, mate1))):
+        at = group_rows(info, order, w0.shape[0])
+        term = dot(own[rows, :], w0[at, :]) + dot(mate[rows, :], w1[at, :])
+        total = term if total is None else total + term
+    out[...] = total.astype(BF16)
+
+
+def project_ahead(info, own0, own1, mate0, mate1, w0, w1):
     return pl.pallas_call(
         ahead_kernel,
-        in_specs=[FULL] * 4,
+        in_specs=[SCALAR] + [FULL] * 6,
         out_specs=FULL,
-        out_shape=jax.ShapeDtypeStruct((owns.shape[0] // 2, w0.shape[1]), BF16),
+        out_shape=jax.ShapeDtypeStruct((own0.shape[0] // 2, w0.shape[1]), BF16),
         compiler_params=params(16),
         cost_estimate=CHEAP,
         name="project_ahead",
-    )(owns, mate, w0, w1)
+    )(info, own0, own1, mate0, mate1, w0, w1)
 
 
 def join_kernel(first, second, _, out):
@@ -647,11 +643,15 @@
     )(first, second, token)
 
 
-def both_kernel(base, cut, owns, mates, w0_far, w1_far, *refs):
+def both_kernel(base, cut, info, own0, own1, mate0, mate1, w0_far, w1_far, *refs):
     fars, near, w0, w1, sem = refs[:-4], *refs[-4:]
     rows = near.shape[0]
     slot = stream(base, w0_far, w1_far, w0, w1, sem)
-    total = dot(owns[...], w0[slot]) + dot(mates[...], w1[slot])
+    total = None
+    for order, (own, mate) in enumerate(((own0, mate0), (own1, mate1))):
+        at = group_rows(info, order, w0.shape[1])
+        term = dot(own[...], w0[slot, at, :]) + dot(mate[...], w1[slot, at, :])
+        total = term if total is None else total + term
     near[...] = total[rows:]
     for k, far_out in enumerate(fars):
 
@@ -660,8 +660,8 @@
             far_out[...] = total[0:rows].astype(BF16)
 
 
-def project_both(owns, mates, w0, w1, first, count, chunk):
-    rows, depth = owns.shape[0] // 2, owns.shape[1]
+def project_both(info, own0, own1, mate0, mate1, w0, w1, first, count, chunk):
+    rows, depth = own0.shape[0] // 2, w0.shape[0]
     cut = chunk // TILE
     chunks = count // chunk
 
@@ -671,38 +671,41 @@
     *fars, near = pl.pallas_call(
         functools.partial(both_kernel, first // TILE, cut),
         grid=(count // TILE,),
-        in_specs=[FULL] * 2 + [FAR] * 2,
+        in_specs=[SCALAR] + [FULL] * 4 + [FAR] * 2,
         out_specs=[placed(k) for k in range(chunks)] + [pl.BlockSpec((rows, TILE), lambda j: (0, j))],
         out_shape=[jax.ShapeDtypeStruct((rows, chunk), BF16)] * chunks + [jax.ShapeDtypeStruct((rows, count), F32)],
         scratch_shapes=buffers(depth),
         compiler_params=params(24),
         cost_estimate=CHEAP,
         name="project_both",
-    )(owns, mates, w0, w1)
+    )(info, own0, own1, mate0, mate1, w0, w1)
     return fars, near
 
 
-def near_kernel(owns, mates, w0_far, w1_far, arrived, out, w0, w1, sem):
+def near_kernel(info, own0, own1, mate0, mate1, w0_far, w1_far, arrived, out, w0, w1, sem):
     slot = stream(0, w0_far, w1_far, w0, w1, sem)
-    rows = out.shape[0]
-    total = dot(owns[rows:, :], w0[slot]) + dot(mates[rows:, :], w1[slot])
-    out[...] = (total + arrived[...].astype(F32)).astype(BF16)
-
-
-def project_near(owns, mates, w0, w1, arrived):
-    rows, depth = owns.shape[0] // 2, owns.shape[1]
+    rows = slice(out.shape[0], 2 * out.shape[0])
+    total = arrived[...].astype(F32)
+    for order, (own, mate) in enumerate(((own0, mate0), (own1, mate1))):
+        at = group_rows(info, order, w0.shape[1])
+        total = total + dot(own[rows, :], w0[slot, at, :]) + dot(mate[rows, :], w1[slot, at, :])
+    out[...] = total.astype(out.dtype)
+
+
+def project_near(info, own0, own1, mate0, mate1, w0, w1, arrived):
+    rows, depth = own0.shape[0] // 2, w0.shape[0]
     placed = pl.BlockSpec((rows, TILE), lambda j: (0, j))
     return pl.pallas_call(
         near_kernel,
         grid=(arrived.shape[1] // TILE,),
-        in_specs=[FULL, FULL, FAR, FAR, placed],
+        in_specs=[SCALAR] + [FULL] * 4 + [FAR, FAR, placed],
         out_specs=placed,
         out_shape=jax.ShapeDtypeStruct((rows, w0.shape[1]), BF16),
         scratch_shapes=buffers(depth),
         compiler_params=params(20),
         cost_estimate=CHEAP,
         name="project_near",
-    )(owns, mates, w0, w1, arrived)
+    )(info, own0, own1, mate0, mate1, w0, w1, arrived)
 
 
 def add_kernel(near, *refs):
@@ -874,16 +877,17 @@
     columns = out_weight.shape[1]
     chunk = columns // 8
     weights = (w_far, weight_mate)
-    kept, w0, w1 = norm_rows(
-        1, (0, 2, 1, 3), info, count, held, bc1, held, gain, uvs[B_PARTS:], weights=weights, columns=chunk
-    )
-    shared = (bc0, other, gain, uvs[:B_PARTS], kept)
-    far_mate, near_mate = norm_rows(0, (0, 2), info, count, kept, *shared, apart=True)
-    (owns,) = norm_rows(0, (1, 3), info, count, far_mate, *shared, 2 * count)
+    kept = (info, count, held, bc1, held, gain, uvs[B_PARTS:])
+    kept_mates, kept_owns, w0, w1 = norm_rows(1, (0, 2, 1, 3), 2, *kept, weights, chunk)
+    kept_mates = swap(lax.optimization_barrier((kept_mates, other))[0], "head", 1)
+    sent_group = (bc0, other, gain, uvs[:B_PARTS])
+    far_mate, near_mate = norm_rows(0, (0, 2), 2, info, count, kept_owns, *sent_group)
+    (owns,) = norm_rows(0, (1, 3), 1, info, count, far_mate, *sent_group)
     far_mate = swap(far_mate, "head", 1)
-    sent = project_ahead(owns, far_mate, w0, w1)
+    sent = project_ahead(info, owns, kept_owns, far_mate, kept_mates, w0, w1)
     first = swap(sent, "head", 2)
-    operands = (owns, join(far_mate, swap(near_mate, "head", 1), sent), *weights)
+    mates = join(far_mate, swap(near_mate, "head", 1), sent)
+    operands = (info, owns, kept_owns, mates, kept_mates, *weights)
     calls = []
     for lo, hi in ((1, 2), (2, 4), (4, 6), (6, 8)):
         sent, near = project_both(*operands, lo * chunk, (hi - lo) * chunk, chunk)

time: 112 us -> 115 us (1.027)
  Pallas kernels: 75.4 us -> 78.9 us
    pallas_call x4, Pallas kernels: 25.2 us -> 27.8 us  [project_both(): pl.pallas_call(functools.partial(both_kernel, first // TILE, cut), grid=(...]
    ppermute x13 -> x14, waiting for transfers between devices: 8.66 us -> 8.29 us  [swap(): lax.ppermute(block, axis, [(i, i ^ bit) for i in range(lax.axis_size(axis...]
    ppermute x13 -> x14, starting transfers between devices: 11.3 us -> 11.5 us  [swap(): lax.ppermute(block, axis, [(i, i ^ bit) for i in range(lax.axis_size(axis...]
  transfers between devices with their start and end apart: 20 -> 21, of which waited for: 6 -> 6; matrix products, arithmetic and copies ran while one was open for 0% -> 0% of each run, Pallas kernels for 65% -> 68%
where the time goes in v18:
time: 115 us; the launch traced here: 114 us
  Pallas kernels  78.9 us (69%)
  starting transfers between devices  22.4 us (19%)
  waiting for transfers between devices  12.5 us (11%)
    pallas_call x4, Pallas kernels, project_both(): pl.pallas_call(functools.partial(both_kernel, first // TILE, cut), grid=(...  27.8 us
    pallas_call x4, Pallas kernels, scan_part(): pl.pallas_call(functools.partial(scan_kernel, order, part), in_specs=[SCA...  15.7 us
    pallas_call x2, Pallas kernels, conv_states(): pl.pallas_call(functools.partial(conv_kernel, order), grid_spec=pltpu.Pre...  12.3 us
    ppermute x14, starting transfers between devices, swap(): lax.ppermute(block, axis, [(i, i ^ bit) for i in range(lax.axis_size(axis...  11.5 us
    ppermute x7, starting transfers between devices, rotate(): lax.ppermute(block, 'seq', [(i, (i + distance) % size) for i in range(siz...  10.9 us
    ppermute x14, waiting for transfers between devices, swap(): lax.ppermute(block, axis, [(i, i ^ bit) for i in range(lax.axis_size(axis...  8.29 us
    pallas_call x3, Pallas kernels, norm_rows(): pl.pallas_call(functools.partial(norm_kernel, order, places, len(weights)...  7.24 us
    pallas_call x1, Pallas kernels, project_near(): pl.pallas_call(near_kernel, grid=(arrived.shape[1] // TILE,), in_specs=[S...  4.37 us
  transfers between devices with their start and end apart: 21, of which 6 were waited for; matrix products, arithmetic and copies ran while one was open for 0% of the time, Pallas kernels for 68%

profile of v18, /device:TPU:0, one launch (start us, length us, event | category | flops | bytes accessed | tf_op | source)
XLA Modules:
  0.0 114.4 jit_solution(13701750728707534259)
XLA Ops:
  1.3 2.7 %collective-permute-start = (bf16[16,2560]{1,0:T(8,128)(2,1)S(1)}, bf16[16,2560]{1,0:T(8,128)(2,1)S(1)}, u32[]{:S(2)}, u32[]{:S(2)}) collective-permute-start(bf16[16,2560]{1,0:T(8,128)(2,1)S(1)} %tail_rows.1), channel_id=1, source_target_pairs={{0,4},{4,8},{8,12},{12,16},{16,20},{20,24},{24,28},{28,0},{1,5},{5... | collective-permute-start | bytes 245768 | tf_op jit(solution)/shard_map/ppermute | solution.py:746
  4.1 2.4 %decays.1 = (f32[1024,16]{1,0:T(8,128)S(1)}, f32[1024,16]{1,0:T(8,128)S(1)}, f32[16,1024]{1,0:T(8,128)S(1)}, f32[16,1024]{1,0:T(8,128)S(1)}, f32[16,1024]{1,0:T(...) custom-call(s32[9]{0:T(128)S(1)} %stack.36.info, ...), custom_call_target="tpu_custom_call" | custom-call | flops 1 | bytes 1 | tf_op jit(solution)/shard_map/decays/pallas_call | solution.py:147
  6.8 3.3 %collective-permute-done.halo = bf16[16,2560]{1,0:T(8,128)(2,1)S(1)} collective-permute-done((bf16[16,2560]{1,0:T(8,128)(2,1)S(1)}, bf16[16,2560]{1,0:T(8,128)(2,1)S(1)}, u32[]{:S(2)}, u32[]{:S(2)}) %collective-permute-start) | collective-permute-done | bytes 81952 | tf_op jit(solution)/shard_map/ppermute | solution.py:746
  10.1 6.9 %conv_states.2 = (bf16[1024,1024]{1,0:T(8,128)(2,1)S(1)}, bf16[1024,256]{1,0:T(8,128)(2,1)S(1)}, bf16[144,1024]{1,0:T(8,128)(2,1)S(1)}, bf16[1024,1024]{1,0:T(8,128)(2,1)S(1)}) custom-call(s32[9]{0:T(128)S(1)} %stack.36.info, bf16[1024,2048]{1,0:T(8,128)(2,1)} %refs_0_.2, bf16[1024,512]{1,0:T(8,128)(2,1)S(1)} %bitcast.14, ...), custom_call_target="tpu_custom_call" | custom-call | flops 1 | bytes 1 | tf_op jit(solution)/shard_map/conv_states/pallas_call | solution.py:296
  17.0 5.5 %conv_states.3 = (bf16[1024,1024]{1,0:T(8,128)(2,1)S(1)}, bf16[1024,256]{1,0:T(8,128)(2,1)S(1)}, f32[128,1024]{1,0:T(8,128)S(1)}, bf16[1024,2048]{1,0:T(8,128)(2,1)S(1)}) custom-call(s32[9]{0:T(128)S(1)} %stack.36.info, bf16[1024,1024]{1,0:T(8,128)(2,1)S(1)} %get-tuple-element.61.x, bf16[1024,512]{1,0:T(8,128)(2,1)S(1)} %bitcast.15, ...), custom_call_target="tpu_custom_call" | custom-call | flops 1 | bytes 1 | tf_op jit(solution)/shard_map/conv_states/pallas_call | solution.py:296
  22.5 3.9 %scan_part.4._.refs_0_ = bf16[1024,1024]{1,0:T(8,128)(2,1)S(1)} custom-call(s32[9]{0:T(128)S(1)} %stack.36.info, bf16[1024,1024]{1,0:T(8,128)(2,1)S(1)} %get-tuple-element.65.x, bf16[1024,2048]{1,0:T(8,128)(2,1)S(1)} %get-tuple-element.66.z, bf16[1024,256]{1,0:T(8,128)(2,1)S(1)} %get-tuple-element.59.bc, f32[1024,16]{1,0:T(8,128)S(1)} %get-tuple-element.67.cum, ...), custom_call_target="tpu_custom_call" | custom-call | flops 1 | bytes 1 | tf_op jit(solution)/shard_map/scan_part/pallas_call | solution.py:495
  27.6 2.6 %collective-permute-start.3 = (bf16[144,256]{1,0:T(8,128)(2,1)S(1)}, bf16[144,256]{1,0:T(8,128)(2,1)S(1)}, u32[]{:S(2)}, u32[]{:S(2)}) collective-permute-start(bf16[144,256]{1,0:T(8,128)(2,1)S(1)} %get-tuple-element.81), channel_id=1, source_target_pairs={{0,16},{4,20},{8,24},{12,28},{16,0},{20,4},{24,8},{28,12},{1,17},{... | collective-permute-start | bytes 221192 | tf_op jit(solution)/shard_map/ppermute | solution.py:746
  31.6 3.9 %scan_part.5.refs_4_.refs_1_ = bf16[1024,1024]{1,0:T(8,128)(2,1)S(1)} custom-call(s32[9]{0:T(128)S(1)} %stack.36.info, bf16[1024,1024]{1,0:T(8,128)(2,1)S(1)} %get-tuple-element.65.x, bf16[1024,2048]{1,0:T(8,128)(2,1)S(1)} %get-tuple-element.66.z, bf16[1024,256]{1,0:T(8,128)(2,1)S(1)} %get-tuple-element.59.bc, f32[1024,16]{1,0:T(8,128)S(1)} %get-tuple-element.67.cum, ...), custom_call_target="tpu_custom_call" | custom-call | flops 1 | bytes 1 | tf_op jit(solution)/shard_map/scan_part/pallas_call | solution.py:495
  40.8 3.9 %scan_part.6._.refs_0_ = bf16[1024,1024]{1,0:T(8,128)(2,1)S(1)} custom-call(s32[9]{0:T(128)S(1)} %stack.36.info, bf16[1024,1024]{1,0:T(8,128)(2,1)S(1)} %get-tuple-element.73.x, bf16[1024,2048]{1,0:T(8,128)(2,1)S(1)} %get-tuple-element.66.z, bf16[1024,256]{1,0:T(8,128)(2,1)S(1)} %get-tuple-element.74.bc, f32[1024,16]{1,0:T(8,128)S(1)} %get-tuple-element.75.cum, ...), custom_call_target="tpu_custom_call" | custom-call | flops 1 | bytes 1 | tf_op jit(solution)/shard_map/scan_part/pallas_call | solution.py:495
  45.8 1.8 %collective-permute-start.8 = (bf16[128,1024]{1,0:T(8,128)(2,1)S(1)}, bf16[128,1024]{1,0:T(8,128)(2,1)S(1)}, u32[]{:S(2)}, u32[]{:S(2)}) collective-permute-start(bf16[128,1024]{1,0:T(8,128)(2,1)S(1)} %get-tuple-element.87._), channel_id=1, source_target_pairs={{0,4},{4,0},{8,12},{12,8},{16,20},{20,16},{24,28},{28,24},{1,5},{5... | collective-permute-start | bytes 786440 | tf_op jit(solution)/shard_map/ppermute | solution.py:741
  47.7 3.9 %scan_part.7.refs_1_ = bf16[1024,1024]{1,0:T(8,128)(2,1)S(1)} custom-call(s32[9]{0:T(128)S(1)} %stack.36.info, bf16[1024,1024]{1,0:T(8,128)(2,1)S(1)} %get-tuple-element.73.x, bf16[1024,2048]{1,0:T(8,128)(2,1)S(1)} %get-tuple-element.66.z, bf16[1024,256]{1,0:T(8,128)(2,1)S(1)} %get-tuple-element.74.bc, f32[1024,16]{1,0:T(8,128)S(1)} %get-tuple-element.75.cum, ...), custom_call_target="tpu_custom_call" | custom-call | flops 1 | bytes 1 | tf_op jit(solution)/shard_map/scan_part/pallas_call | solution.py:495
  51.6 3.4 %norm_rows.3 = (bf16[512,1024]{1,0:T(8,128)(2,1)S(1)}, bf16[512,1024]{1,0:T(8,128)(2,1)S(1)}, bf16[2048,512]{1,0:T(8,128)(2,1)S(1)}, bf16[2048,512]{1,0:T(8,128)(2,1)S(1)}) custom-call(s32[9]{0:T(128)S(1)} %stack.36.info, bf16[1024,256]{1,0:T(8,128)(2,1)S(1)} %get-tuple-element.74.bc, bf16[128,1024]{1,0:T(8,128)(2,1)S(1)} %get-tuple-element.88.state._, ...), custom_call_target="tpu_custom_call" | custom-call | flops 1 | bytes 1 | tf_op jit(solution)/shard_map/norm_rows/pallas_call | solution.py:552
  55.1 1.9 %norm_rows.4 = (bf16[256,1024]{1,0:T(8,128)(2,1)S(1)}, bf16[256,1024]{1,0:T(8,128)(2,1)S(1)}) custom-call(s32[9]{0:T(128)S(1)} %stack.36.info, bf16[1024,256]{1,0:T(8,128)(2,1)S(1)} %get-tuple-element.59.bc, bf16[128,1024]{1,0:T(8,128)(2,1)S(1)} %collective-permute-done.8.state, f32[1,2048]{1,0:T(1,128)S(1)} %bitcast.17, ...), custom_call_target="tpu_custom_call" | custom-call | flops 1 | bytes 1 | tf_op jit(solution)/shard_map/norm_rows/pallas_call | solution.py:552
  57.7 1.9 %norm_rows.5.own0 = bf16[512,1024]{1,0:T(8,128)(2,1)S(1)} custom-call(s32[9]{0:T(128)S(1)} %stack.36.info, bf16[1024,256]{1,0:T(8,128)(2,1)S(1)} %get-tuple-element.59.bc, bf16[128,1024]{1,0:T(8,128)(2,1)S(1)} %collective-permute-done.8.state, f32[1,2048]{1,0:T(1,128)S(1)} %bitcast.18, bf16[256,1024]{1,0:T(8,128)(2,1)S(1)} %get-tuple-element.90._, ...), custom_call_target="tpu_custom_call" | custom-call | flops 1 | bytes 1 | tf_op jit(solution)/shard_map/norm_rows/pallas_call | solution.py:552
  59.6 1.8 %project_ahead.1._ = bf16[256,512]{1,0:T(8,128)(2,1)S(1)} custom-call(s32[9]{0:T(128)S(1)} %stack.36.info, bf16[512,1024]{1,0:T(8,128)(2,1)S(1)} %norm_rows.5.own0, bf16[512,1024]{1,0:T(8,128)(2,1)S(1)} %get-tuple-element.89._.own1, bf16[256,1024]{1,0:T(8,128)(2,1)S(1)} %collective-permute-done.10.mate0.first, ...), custom_call_target="tpu_custom_call" | custom-call | flops 1 | bytes 1 | tf_op jit(solution)/shard_map/project_ahead/pallas_call | solution.py:616
  61.4 1.5 %collective-permute-start.20 = (bf16[256,512]{1,0:T(8,128)(2,1)S(1)}, bf16[256,512]{1,0:T(8,128)(2,1)S(1)}, u32[]{:S(2)}, u32[]{:S(2)}) collective-permute-start(bf16[256,512]{1,0:T(8,128)(2,1)S(1)} %project_ahead.1._), channel_id=1, source_target_pairs={{0,2},{1,3},{2,0},{3,1},{4,6},{5,7},{6,4},{7,5},{8,10},{9,11},{10,... | collective-permute-start | bytes 786440 | tf_op jit(solution)/shard_map/ppermute | solution.py:741
  63.1 4.9 %project_both.7 = (bf16[256,512]{1,0:T(8,128)(2,1)S(1)}, f32[256,512]{1,0:T(8,128)S(1)}) custom-call(s32[9]{0:T(128)S(1)} %stack.36.info, bf16[512,1024]{1,0:T(8,128)(2,1)S(1)} %norm_rows.5.own0, bf16[512,1024]{1,0:T(8,128)(2,1)S(1)} %get-tuple-element.89._.own1, bf16[512,1024]{1,0:T(8,128)(2,1)S(1)} %join.1.mate0, ...), custom_call_target="tpu_custom_call" | custom-call | flops 1 | bytes 1 | tf_op jit(solution)/shard_map/project_both/pallas_call | solution.py:671
  68.6 7.6 %project_both.6 = (bf16[256,512]{1,0:T(8,128)(2,1)S(1)}, bf16[256,512]{1,0:T(8,128)(2,1)S(1)}, f32[256,1024]{1,0:T(8,128)S(1)}) custom-call(s32[9]{0:T(128)S(1)} %stack.36.info, bf16[512,1024]{1,0:T(8,128)(2,1)S(1)} %norm_rows.5.own0, bf16[512,1024]{1,0:T(8,128)(2,1)S(1)} %get-tuple-element.89._.own1, bf16[512,1024]{1,0:T(8,128)(2,1)S(1)} %join.1.mate0, ...), custom_call_target="tpu_custom_call" | custom-call | flops 1 | bytes 1 | tf_op jit(solution)/shard_map/project_both/pallas_call | solution.py:671
  76.2 1.5 %collective-permute-start.17 = (bf16[256,512]{1,0:T(8,128)(2,1)S(1)}, bf16[256,512]{1,0:T(8,128)(2,1)S(1)}, u32[]{:S(2)}, u32[]{:S(2)}) collective-permute-start(bf16[256,512]{1,0:T(8,128)(2,1)S(1)} %get-tuple-element.103), channel_id=1, source_target_pairs={{0,2},{1,3},{2,0},{3,1},{4,6},{5,7},{6,4},{7,5},{8,10},{9,11},{10,... | collective-permute-start | bytes 786440 | tf_op jit(solution)/shard_map/ppermute | solution.py:741
  78.3 7.6 %project_both.5 = (bf16[256,512]{1,0:T(8,128)(2,1)S(1)}, bf16[256,512]{1,0:T(8,128)(2,1)S(1)}, f32[256,1024]{1,0:T(8,128)S(1)}) custom-call(s32[9]{0:T(128)S(1)} %stack.36.info, bf16[512,1024]{1,0:T(8,128)(2,1)S(1)} %norm_rows.5.own0, bf16[512,1024]{1,0:T(8,128)(2,1)S(1)} %get-tuple-element.89._.own1, bf16[512,1024]{1,0:T(8,128)(2,1)S(1)} %join.1.mate0, ...), custom_call_target="tpu_custom_call" | custom-call | flops 1 | bytes 1 | tf_op jit(solution)/shard_map/project_both/pallas_call | solution.py:671
  87.5 7.6 %project_both.4 = (bf16[256,512]{1,0:T(8,128)(2,1)S(1)}, bf16[256,512]{1,0:T(8,128)(2,1)S(1)}, f32[256,1024]{1,0:T(8,128)S(1)}) custom-call(s32[9]{0:T(128)S(1)} %stack.36.info, bf16[512,1024]{1,0:T(8,128)(2,1)S(1)} %norm_rows.5.own0, bf16[512,1024]{1,0:T(8,128)(2,1)S(1)} %get-tuple-element.89._.own1, bf16[512,1024]{1,0:T(8,128)(2,1)S(1)} %join.1.mate0, ...), custom_call_target="tpu_custom_call" | custom-call | flops 1 | bytes 1 | tf_op jit(solution)/shard_map/project_both/pallas_call | solution.py:671
  97.8 4.4 %project_near.1.refs_1_ = bf16[256,4096]{1,0:T(8,128)(2,1)} custom-call(s32[9]{0:T(128)S(1)} %stack.36.info, bf16[512,1024]{1,0:T(8,128)(2,1)S(1)} %norm_rows.5.own0, bf16[512,1024]{1,0:T(8,128)(2,1)S(1)} %get-tuple-element.89._.own1, bf16[512,1024]{1,0:T(8,128)(2,1)S(1)} %join.1.mate0, bf16[512,1024]{1,0:T(8,128)(2,1)S(1)} %collective-permute-done.12.mate1, ...), custom_call_target="tpu_custom_call" | custom-call | flops 1 | bytes 1 | tf_op jit(solution)/shard_map/project_near/pallas_call | solution.py:698
  105.3 4.7 %collective-permute-done.14.refs_0_ = bf16[256,512]{1,0:T(8,128)(2,1)S(1)} collective-permute-done((bf16[256,512]{1,0:T(8,128)(2,1)S(1)}, bf16[256,512]{1,0:T(8,128)(2,1)S(1)}, u32[]{:S(2)}, u32[]{:S(2)}) %collective-permute-start.14) | collective-permute-done | bytes 262176 | tf_op jit(solution)/shard_map/ppermute | solution.py:741
  110.8 2.9 %collective-permute-done.13.refs_0_ = bf16[256,512]{1,0:T(8,128)(2,1)S(1)} collective-permute-done((bf16[256,512]{1,0:T(8,128)(2,1)S(1)}, bf16[256,512]{1,0:T(8,128)(2,1)S(1)}, u32[]{:S(2)}, u32[]{:S(2)}) %collective-permute-start.13) | collective-permute-done | bytes 262176 | tf_op jit(solution)/shard_map/ppermute | solution.py:741
  (50 shorter events, 21.4 us)
Async XLA Ops:
  0.0 6.5 %copy-start.1 = (bf16[1024,2,256]{2,1,0:T(2,128)(2,1)S(1)}, bf16[1024,2,256]{2,1,0:T(2,128)(2,1)}, u32[]{:S(2)}) copy-start(bf16[1024,2,256]{2,1,0:T(2,128)(2,1)} %bc.1) | copy-start | bytes 3145732
  0.0 51.6 %collective-permute-start.9 = (bf16[2048,4096]{1,0:T(8,128)(2,1)}, bf16[2048,4096]{1,0:T(8,128)(2,1)}, u32[]{:S(2)}, u32[]{:S(2)}) collective-permute-start(bf16[2048,4096]{1,0:T(8,128)(2,1)} %w0_far.9), channel_id=1, source_target_pairs={{0,1},{1,0},{2,3},{3,2},{4,5},{5,4},{6,7},{7,6},{8,9},{9,8},{10,11... | collective-permute-start | bytes 50331656 | tf_op jit(solution)/shard_map/ppermute | solution.py:741
  1.3 8.7 %collective-permute-start = (bf16[16,2560]{1,0:T(8,128)(2,1)S(1)}, bf16[16,2560]{1,0:T(8,128)(2,1)S(1)}, u32[]{:S(2)}, u32[]{:S(2)}) collective-permute-start(bf16[16,2560]{1,0:T(8,128)(2,1)S(1)} %tail_rows.1), channel_id=1, source_target_pairs={{0,4},{4,8},{8,12},{12,16},{16,20},{20,24},{24,28},{28,0},{1,5},{5... | collective-permute-start | bytes 245768 | tf_op jit(solution)/shard_map/ppermute | solution.py:746
  16.9 9.5 %collective-permute-start.1 = (bf16[144,1024]{1,0:T(8,128)(2,1)S(1)}, bf16[144,1024]{1,0:T(8,128)(2,1)S(1)}, u32[]{:S(2)}, u32[]{:S(2)}) collective-permute-start(bf16[144,1024]{1,0:T(8,128)(2,1)S(1)} %get-tuple-element.60), channel_id=1, source_target_pairs={{0,4},{4,0},{8,12},{12,8},{16,20},{20,16},{24,28},{28,24},{1,5},{5... | collective-permute-start | bytes 884744 | tf_op jit(solution)/shard_map/ppermute | solution.py:741
  27.3 8.2 %collective-permute-start.2 = (bf16[144,256]{1,0:T(8,128)(2,1)S(1)}, bf16[144,256]{1,0:T(8,128)(2,1)S(1)}, u32[]{:S(2)}, u32[]{:S(2)}) collective-permute-start(bf16[144,256]{1,0:T(8,128)(2,1)S(1)} %get-tuple-element.80), channel_id=1, source_target_pairs={{0,8},{4,12},{8,16},{12,20},{16,24},{20,28},{24,0},{28,4},{1,9},{5... | collective-permute-start | bytes 221192 | tf_op jit(solution)/shard_map/ppermute | solution.py:746
  27.6 8.6 %collective-permute-start.3 = (bf16[144,256]{1,0:T(8,128)(2,1)S(1)}, bf16[144,256]{1,0:T(8,128)(2,1)S(1)}, u32[]{:S(2)}, u32[]{:S(2)}) collective-permute-start(bf16[144,256]{1,0:T(8,128)(2,1)S(1)} %get-tuple-element.81), channel_id=1, source_target_pairs={{0,16},{4,20},{8,24},{12,28},{16,0},{20,4},{24,8},{28,12},{1,17},{... | collective-permute-start | bytes 221192 | tf_op jit(solution)/shard_map/ppermute | solution.py:746
  30.2 6.0 %collective-permute-start.4 = (bf16[144,256]{1,0:T(8,128)(2,1)S(1)}, bf16[144,256]{1,0:T(8,128)(2,1)S(1)}, u32[]{:S(2)}, u32[]{:S(2)}) collective-permute-start(bf16[144,256]{1,0:T(8,128)(2,1)S(1)} %get-tuple-element.82), channel_id=1, source_target_pairs={{0,24},{4,28},{8,0},{12,4},{16,8},{20,12},{24,16},{28,20},{1,25},{... | collective-permute-start | bytes 221192 | tf_op jit(solution)/shard_map/ppermute | solution.py:746
  36.9 7.9 %collective-permute-start.5 = (bf16[128,256]{1,0:T(8,128)(2,1)S(1)}, bf16[128,256]{1,0:T(8,128)(2,1)S(1)}, u32[]{:S(2)}, u32[]{:S(2)}) collective-permute-start(bf16[128,256]{1,0:T(8,128)(2,1)S(1)} %get-tuple-element.84), channel_id=1, source_target_pairs={{0,8},{4,12},{8,16},{12,20},{16,24},{20,28},{24,0},{28,4},{1,9},{5... | collective-permute-start | bytes 196616 | tf_op jit(solution)/shard_map/ppermute | solution.py:746
  38.4 6.6 %collective-permute-start.6 = (bf16[128,256]{1,0:T(8,128)(2,1)S(1)}, bf16[128,256]{1,0:T(8,128)(2,1)S(1)}, u32[]{:S(2)}, u32[]{:S(2)}) collective-permute-start(bf16[128,256]{1,0:T(8,128)(2,1)S(1)} %get-tuple-element.85), channel_id=1, source_target_pairs={{0,16},{4,20},{8,24},{12,28},{16,0},{20,4},{24,8},{28,12},{1,17},{... | collective-permute-start | bytes 196616 | tf_op jit(solution)/shard_map/ppermute | solution.py:746
  39.9 5.1 %collective-permute-start.7 = (bf16[128,256]{1,0:T(8,128)(2,1)S(1)}, bf16[128,256]{1,0:T(8,128)(2,1)S(1)}, u32[]{:S(2)}, u32[]{:S(2)}) collective-permute-start(bf16[128,256]{1,0:T(8,128)(2,1)S(1)} %get-tuple-element.86), channel_id=1, source_target_pairs={{0,24},{4,28},{8,0},{12,4},{16,8},{20,12},{24,16},{28,20},{1,25},{... | collective-permute-start | bytes 196616 | tf_op jit(solution)/shard_map/ppermute | solution.py:746
  45.8 5.8 %copy-start = (f32[2048]{0:T(1024)S(1)}, f32[2048]{0:T(1024)}, u32[]{:S(2)}) copy-start(f32[2048]{0:T(1024)} %param.18) | copy-start | bytes 24580
  45.8 9.1 %collective-permute-start.8 = (bf16[128,1024]{1,0:T(8,128)(2,1)S(1)}, bf16[128,1024]{1,0:T(8,128)(2,1)S(1)}, u32[]{:S(2)}, u32[]{:S(2)}) collective-permute-start(bf16[128,1024]{1,0:T(8,128)(2,1)S(1)} %get-tuple-element.87._), channel_id=1, source_target_pairs={{0,4},{4,0},{8,12},{12,8},{16,20},{20,16},{24,28},{28,24},{1,5},{5... | collective-permute-start | bytes 786440 | tf_op jit(solution)/shard_map/ppermute | solution.py:741
  55.0 4.6 %collective-permute-start.12 = (bf16[512,1024]{1,0:T(8,128)(2,1)S(1)}, bf16[512,1024]{1,0:T(8,128)(2,1)S(1)}, u32[]{:S(2)}, u32[]{:S(2)}) collective-permute-start(bf16[512,1024]{1,0:T(8,128)(2,1)S(1)} %get-tuple-element.93), channel_id=1, source_target_pairs={{0,1},{1,0},{2,3},{3,2},{4,5},{5,4},{6,7},{7,6},{8,9},{9,8},{10,11... | collective-permute-start | bytes 3145736 | tf_op jit(solution)/shard_map/ppermute | solution.py:741
  57.0 2.6 %collective-permute-start.10 = (bf16[256,1024]{1,0:T(8,128)(2,1)S(1)}, bf16[256,1024]{1,0:T(8,128)(2,1)S(1)}, u32[]{:S(2)}, u32[]{:S(2)}) collective-permute-start(bf16[256,1024]{1,0:T(8,128)(2,1)S(1)} %get-tuple-element.90._), channel_id=1, source_target_pairs={{0,1},{1,0},{2,3},{3,2},{4,5},{5,4},{6,7},{7,6},{8,9},{9,8},{10,11... | collective-permute-start | bytes 1572872 | tf_op jit(solution)/shard_map/ppermute | solution.py:741
  57.6 5.4 %collective-permute-start.11 = (bf16[256,1024]{1,0:T(8,128)(2,1)S(1)}, bf16[256,1024]{1,0:T(8,128)(2,1)S(1)}, u32[]{:S(2)}, u32[]{:S(2)}) collective-permute-start(bf16[256,1024]{1,0:T(8,128)(2,1)S(1)} %get-tuple-element.91), channel_id=1, source_target_pairs={{0,1},{1,0},{2,3},{3,2},{4,5},{5,4},{6,7},{7,6},{8,9},{9,8},{10,11... | collective-permute-start | bytes 1572872 | tf_op jit(solution)/shard_map/ppermute | solution.py:741
  61.4 33.7 %collective-permute-start.20 = (bf16[256,512]{1,0:T(8,128)(2,1)S(1)}, bf16[256,512]{1,0:T(8,128)(2,1)S(1)}, u32[]{:S(2)}, u32[]{:S(2)}) collective-permute-start(bf16[256,512]{1,0:T(8,128)(2,1)S(1)} %project_ahead.1._), channel_id=1, source_target_pairs={{0,2},{1,3},{2,0},{3,1},{4,6},{5,7},{6,4},{7,5},{8,10},{9,11},{10,... | collective-permute-start | bytes 786440 | tf_op jit(solution)/shard_map/ppermute | solution.py:741
  67.9 27.8 %collective-permute-start.19 = (bf16[256,512]{1,0:T(8,128)(2,1)S(1)}, bf16[256,512]{1,0:T(8,128)(2,1)S(1)}, u32[]{:S(2)}, u32[]{:S(2)}) collective-permute-start(bf16[256,512]{1,0:T(8,128)(2,1)S(1)} %get-tuple-element.106), channel_id=1, source_target_pairs={{0,2},{1,3},{2,0},{3,1},{4,6},{5,7},{6,4},{7,5},{8,10},{9,11},{10,... | collective-permute-start | bytes 786440 | tf_op jit(solution)/shard_map/ppermute | solution.py:741
  76.2 21.0 %collective-permute-start.17 = (bf16[256,512]{1,0:T(8,128)(2,1)S(1)}, bf16[256,512]{1,0:T(8,128)(2,1)S(1)}, u32[]{:S(2)}, u32[]{:S(2)}) collective-permute-start(bf16[256,512]{1,0:T(8,128)(2,1)S(1)} %get-tuple-element.103), channel_id=1, source_target_pairs={{0,2},{1,3},{2,0},{3,1},{4,6},{5,7},{6,4},{7,5},{8,10},{9,11},{10,... | collective-permute-start | bytes 786440 | tf_op jit(solution)/shard_map/ppermute | solution.py:741
  77.7 25.2 %collective-permute-start.18 = (bf16[256,512]{1,0:T(8,128)(2,1)S(1)}, bf16[256,512]{1,0:T(8,128)(2,1)S(1)}, u32[]{:S(2)}, u32[]{:S(2)}) collective-permute-start(bf16[256,512]{1,0:T(8,128)(2,1)S(1)} %get-tuple-element.104), channel_id=1, source_target_pairs={{0,2},{1,3},{2,0},{3,1},{4,6},{5,7},{6,4},{7,5},{8,10},{9,11},{10,... | collective-permute-start | bytes 786440 | tf_op jit(solution)/shard_map/ppermute | solution.py:741
  85.9 17.9 %collective-permute-start.15 = (bf16[256,512]{1,0:T(8,128)(2,1)S(1)}, bf16[256,512]{1,0:T(8,128)(2,1)S(1)}, u32[]{:S(2)}, u32[]{:S(2)}) collective-permute-start(bf16[256,512]{1,0:T(8,128)(2,1)S(1)} %get-tuple-element.100), channel_id=1, source_target_pairs={{0,2},{1,3},{2,0},{3,1},{4,6},{5,7},{6,4},{7,5},{8,10},{9,11},{10,... | collective-permute-start | bytes 786440 | tf_op jit(solution)/shard_map/ppermute | solution.py:741
  95.1 9.3 %collective-permute-start.16 = (bf16[256,512]{1,0:T(8,128)(2,1)S(1)}, bf16[256,512]{1,0:T(8,128)(2,1)S(1)}, u32[]{:S(2)}, u32[]{:S(2)}) collective-permute-start(bf16[256,512]{1,0:T(8,128)(2,1)S(1)} %get-tuple-element.101), channel_id=1, source_target_pairs={{0,2},{1,3},{2,0},{3,1},{4,6},{5,7},{6,4},{7,5},{8,10},{9,11},{10,... | collective-permute-start | bytes 786440 | tf_op jit(solution)/shard_map/ppermute | solution.py:741
  95.7 14.3 %collective-permute-start.14 = (bf16[256,512]{1,0:T(8,128)(2,1)S(1)}, bf16[256,512]{1,0:T(8,128)(2,1)S(1)}, u32[]{:S(2)}, u32[]{:S(2)}) collective-permute-start(bf16[256,512]{1,0:T(8,128)(2,1)S(1)} %get-tuple-element.98), channel_id=1, source_target_pairs={{0,2},{1,3},{2,0},{3,1},{4,6},{5,7},{6,4},{7,5},{8,10},{9,11},{10,... | collective-permute-start | bytes 786440 | tf_op jit(solution)/shard_map/ppermute | solution.py:741
  97.2 16.5 %collective-permute-start.13 = (bf16[256,512]{1,0:T(8,128)(2,1)S(1)}, bf16[256,512]{1,0:T(8,128)(2,1)S(1)}, u32[]{:S(2)}, u32[]{:S(2)}) collective-permute-start(bf16[256,512]{1,0:T(8,128)(2,1)S(1)} %get-tuple-element.97), channel_id=1, source_target_pairs={{0,2},{1,3},{2,0},{3,1},{4,6},{5,7},{6,4},{7,5},{8,10},{9,11},{10,... | collective-permute-start | bytes 786440 | tf_op jit(solution)/shard_map/ppermute | solution.py:741

commit v19 on v16

--- a/solution.py
+++ b/solution.py
@@ -804,6 +804,7 @@
     (bc_far,) = far(bc_input)
     halo = rotate(tail_rows(x_far, bc_far), 1)
     bc = bc_input.reshape(length, -1)
+    (weight_mate,) = far(swap(out_weight, "head", 1))
 
     (cum, cum_s, log_s, f_dev, f_blk, rates), ones, x_sent = decays(
         info, log_decay, step_size, skip_gain, x_input, half
@@ -812,7 +813,6 @@
     shared = (bc, halo, *taps)
     x0, bc0, send, x_kept = conv_states(0, info, x_sent, *shared, f_dev[0], ones, rates[0], x_far)
     got = swap(send, "seq", 1)
-    (weight_mate,) = far(swap(lax.optimization_barrier((out_weight, send))[0], "head", 1))
     x1, bc1, keep, z_near = conv_states(1, info, x_kept, *shared, f_dev[1], ones, rates[1], z_far)
     rates_kept = rates[1]
 
@@ -873,10 +873,12 @@
     columns = out_weight.shape[1]
     chunk = columns // 8
     weights = (w_far, weight_mate)
-    (kept,) = norm_rows(1, (0, 2, 1, 3), info, count, held, bc1, held, gain, uvs[B_PARTS:])
+    kept, w0, w1 = norm_rows(
+        1, (0, 2, 1, 3), info, count, held, bc1, held, gain, uvs[B_PARTS:], weights=weights, columns=chunk
+    )
     shared = (bc0, other, gain, uvs[:B_PARTS], kept)
     far_mate, near_mate = norm_rows(0, (0, 2), info, count, kept, *shared, apart=True)
-    owns, w0, w1 = norm_rows(0, (1, 3), info, count, far_mate, *shared, 2 * count, False, weights, chunk)
+    (owns,) = norm_rows(0, (1, 3), info, count, far_mate, *shared, 2 * count)
     far_mate = swap(far_mate, "head", 1)
     sent = project_ahead(owns, far_mate, w0, w1)
     first = swap(sent, "head", 2)

time: 116 us -> 110 us (0.948)
  local copies, waits for them, and re-layouts: 6.07 us -> 0.33 us
    unnamed x7 -> x5, local copies, waits for them, and re-layouts: 5.99 us -> 0.24 us
  transfers between devices with their start and end apart: 20 -> 20, of which waited for: 7 -> 7; matrix products, arithmetic and copies ran while one was open for 0% -> 0% of each run, Pallas kernels for 59% -> 66%
where the time goes in v19:
time: 110 us
  Pallas kernels  75.6 us (69%)
  starting transfers between devices  22.5 us (20%)
  waiting for transfers between devices  11.2 us (10%)
    pallas_call x4, Pallas kernels, project_both(): pl.pallas_call(functools.partial(both_kernel, first // TILE, cut), grid=(...  25.2 us
    pallas_call x4, Pallas kernels, scan_part(): pl.pallas_call(functools.partial(scan_kernel, order, part), in_specs=[SCA...  15.5 us
    ppermute x7, starting transfers between devices, rotate(): lax.ppermute(block, 'seq', [(i, (i + distance) % size) for i in range(siz...  12.2 us
    pallas_call x2, Pallas kernels, conv_states(): pl.pallas_call(functools.partial(conv_kernel, order), grid_spec=pltpu.Pre...  10.9 us
    ppermute x13, starting transfers between devices, swap(): lax.ppermute(block, axis, [(i, i ^ bit) for i in range(lax.axis_size(axis...  10.4 us
    ppermute x13, waiting for transfers between devices, swap(): lax.ppermute(block, axis, [(i, i ^ bit) for i in range(lax.axis_size(axis...  8.63 us
    pallas_call x3, Pallas kernels, norm_rows(): pl.pallas_call(functools.partial(norm_kernel, order, places, skip, len(we...  7.55 us
    pallas_call x5, Pallas kernels, add_chunks(): pl.pallas_call(add_kernel, grid=(1,), in_specs=[pl.BlockSpec((rows, count...  4.06 us
  transfers between devices with their start and end apart: 20, of which 7 were waited for; matrix products, arithmetic and copies ran while one was open for 0% of the time, Pallas kernels for 66%

profile of v19, /device:TPU:0, one launch (start us, length us, event | category | flops | bytes accessed | tf_op | source)
XLA Modules:
  0.0 109.9 jit_solution(9733282093082611485)
XLA Ops:
  1.3 2.6 %collective-permute-start = (bf16[16,2560]{1,0:T(8,128)(2,1)S(1)}, bf16[16,2560]{1,0:T(8,128)(2,1)S(1)}, u32[]{:S(2)}, u32[]{:S(2)}) collective-permute-start(bf16[16,2560]{1,0:T(8,128)(2,1)S(1)} %tail_rows.1), channel_id=1, source_target_pairs={{0,4},{4,8},{8,12},{12,16},{16,20},{20,24},{24,28},{28,0},{1,5},{5... | collective-permute-start | bytes 245768 | tf_op jit(solution)/shard_map/ppermute | solution.py:740
  4.0 3.9 %decays.1 = (f32[1024,16]{1,0:T(8,128)S(1)}, f32[1024,16]{1,0:T(8,128)S(1)}, f32[16,1024]{1,0:T(8,128)S(1)}, f32[16,1024]{1,0:T(8,128)S(1)}, f32[16,1024]{1,0:T(...) custom-call(s32[9]{0:T(128)S(1)} %stack.36.info, ...), custom_call_target="tpu_custom_call" | custom-call | flops 1 | bytes 1 | tf_op jit(solution)/shard_map/decays/pallas_call | solution.py:153
  8.2 1.9 %collective-permute-done.halo = bf16[16,2560]{1,0:T(8,128)(2,1)S(1)} collective-permute-done((bf16[16,2560]{1,0:T(8,128)(2,1)S(1)}, bf16[16,2560]{1,0:T(8,128)(2,1)S(1)}, u32[]{:S(2)}, u32[]{:S(2)}) %collective-permute-start) | collective-permute-done | bytes 81952 | tf_op jit(solution)/shard_map/ppermute | solution.py:740
  10.1 5.5 %conv_states.2 = (bf16[1024,1024]{1,0:T(8,128)(2,1)S(1)}, bf16[1024,256]{1,0:T(8,128)(2,1)S(1)}, bf16[144,1024]{1,0:T(8,128)(2,1)S(1)}, bf16[1024,1024]{1,0:T(8,128)(2,1)S(1)}) custom-call(s32[9]{0:T(128)S(1)} %stack.36.info, bf16[1024,1024]{1,0:T(8,128)(2,1)S(1)} %get-tuple-element.55.x, bf16[1024,512]{1,0:T(8,128)(2,1)S(1)} %bitcast.14, ...), custom_call_target="tpu_custom_call" | custom-call | flops 1 | bytes 1 | tf_op jit(solution)/shard_map/conv_states/pallas_call | solution.py:294
  15.6 5.5 %conv_states.3 = (bf16[1024,1024]{1,0:T(8,128)(2,1)S(1)}, bf16[1024,256]{1,0:T(8,128)(2,1)S(1)}, f32[128,1024]{1,0:T(8,128)S(1)}, bf16[1024,2048]{1,0:T(8,128)(2,1)S(1)}) custom-call(s32[9]{0:T(128)S(1)} %stack.36.info, bf16[1024,1024]{1,0:T(8,128)(2,1)S(1)} %get-tuple-element.61.x, bf16[1024,512]{1,0:T(8,128)(2,1)S(1)} %bitcast.15, ...), custom_call_target="tpu_custom_call" | custom-call | flops 1 | bytes 1 | tf_op jit(solution)/shard_map/conv_states/pallas_call | solution.py:294
  21.1 3.9 %scan_part.4._.refs_0_ = bf16[1024,1024]{1,0:T(8,128)(2,1)S(1)} custom-call(s32[9]{0:T(128)S(1)} %stack.36.info, bf16[1024,1024]{1,0:T(8,128)(2,1)S(1)} %get-tuple-element.65.x, bf16[1024,2048]{1,0:T(8,128)(2,1)S(1)} %get-tuple-element.66.z, bf16[1024,256]{1,0:T(8,128)(2,1)S(1)} %get-tuple-element.59.bc, f32[1024,16]{1,0:T(8,128)S(1)} %get-tuple-element.67.cum, ...), custom_call_target="tpu_custom_call" | custom-call | flops 1 | bytes 1 | tf_op jit(solution)/shard_map/scan_part/pallas_call | solution.py:492
  27.2 1.6 %collective-permute-start.3 = (bf16[144,256]{1,0:T(8,128)(2,1)S(1)}, bf16[144,256]{1,0:T(8,128)(2,1)S(1)}, u32[]{:S(2)}, u32[]{:S(2)}) collective-permute-start(bf16[144,256]{1,0:T(8,128)(2,1)S(1)} %get-tuple-element.81), channel_id=1, source_target_pairs={{0,16},{4,20},{8,24},{12,28},{16,0},{20,4},{24,8},{28,12},{1,17},{... | collective-permute-start | bytes 221192 | tf_op jit(solution)/shard_map/ppermute | solution.py:740
  28.8 2.3 %collective-permute-start.4 = (bf16[144,256]{1,0:T(8,128)(2,1)S(1)}, bf16[144,256]{1,0:T(8,128)(2,1)S(1)}, u32[]{:S(2)}, u32[]{:S(2)}) collective-permute-start(bf16[144,256]{1,0:T(8,128)(2,1)S(1)} %get-tuple-element.82), channel_id=1, source_target_pairs={{0,24},{4,28},{8,0},{12,4},{16,8},{20,12},{24,16},{28,20},{1,25},{... | collective-permute-start | bytes 221192 | tf_op jit(solution)/shard_map/ppermute | solution.py:740
  31.1 3.9 %scan_part.5.refs_4_.refs_1_ = bf16[1024,1024]{1,0:T(8,128)(2,1)S(1)} custom-call(s32[9]{0:T(128)S(1)} %stack.36.info, bf16[1024,1024]{1,0:T(8,128)(2,1)S(1)} %get-tuple-element.65.x, bf16[1024,2048]{1,0:T(8,128)(2,1)S(1)} %get-tuple-element.66.z, bf16[1024,256]{1,0:T(8,128)(2,1)S(1)} %get-tuple-element.59.bc, f32[1024,16]{1,0:T(8,128)S(1)} %get-tuple-element.67.cum, ...), custom_call_target="tpu_custom_call" | custom-call | flops 1 | bytes 1 | tf_op jit(solution)/shard_map/scan_part/pallas_call | solution.py:492
  35.9 1.9 %collective-permute-start.5 = (bf16[128,256]{1,0:T(8,128)(2,1)S(1)}, bf16[128,256]{1,0:T(8,128)(2,1)S(1)}, u32[]{:S(2)}, u32[]{:S(2)}) collective-permute-start(bf16[128,256]{1,0:T(8,128)(2,1)S(1)} %get-tuple-element.84), channel_id=1, source_target_pairs={{0,8},{4,12},{8,16},{12,20},{16,24},{20,28},{24,0},{28,4},{1,9},{5... | collective-permute-start | bytes 196616 | tf_op jit(solution)/shard_map/ppermute | solution.py:740
  37.9 1.6 %collective-permute-start.6 = (bf16[128,256]{1,0:T(8,128)(2,1)S(1)}, bf16[128,256]{1,0:T(8,128)(2,1)S(1)}, u32[]{:S(2)}, u32[]{:S(2)}) collective-permute-start(bf16[128,256]{1,0:T(8,128)(2,1)S(1)} %get-tuple-element.85), channel_id=1, source_target_pairs={{0,16},{4,20},{8,24},{12,28},{16,0},{20,4},{24,8},{28,12},{1,17},{... | collective-permute-start | bytes 196616 | tf_op jit(solution)/shard_map/ppermute | solution.py:740
  40.3 3.8 %scan_part.6._.refs_0_ = bf16[1024,1024]{1,0:T(8,128)(2,1)S(1)} custom-call(s32[9]{0:T(128)S(1)} %stack.36.info, bf16[1024,1024]{1,0:T(8,128)(2,1)S(1)} %get-tuple-element.73.x, bf16[1024,2048]{1,0:T(8,128)(2,1)S(1)} %get-tuple-element.66.z, bf16[1024,256]{1,0:T(8,128)(2,1)S(1)} %get-tuple-element.74.bc, f32[1024,16]{1,0:T(8,128)S(1)} %get-tuple-element.75.cum, ...), custom_call_target="tpu_custom_call" | custom-call | flops 1 | bytes 1 | tf_op jit(solution)/shard_map/scan_part/pallas_call | solution.py:492
  46.3 3.8 %scan_part.7.refs_1_ = bf16[1024,1024]{1,0:T(8,128)(2,1)S(1)} custom-call(s32[9]{0:T(128)S(1)} %stack.36.info, bf16[1024,1024]{1,0:T(8,128)(2,1)S(1)} %get-tuple-element.73.x, bf16[1024,2048]{1,0:T(8,128)(2,1)S(1)} %get-tuple-element.66.z, bf16[1024,256]{1,0:T(8,128)(2,1)S(1)} %get-tuple-element.74.bc, f32[1024,16]{1,0:T(8,128)S(1)} %get-tuple-element.75.cum, ...), custom_call_target="tpu_custom_call" | custom-call | flops 1 | bytes 1 | tf_op jit(solution)/shard_map/scan_part/pallas_call | solution.py:492
  50.2 3.4 %norm_rows.3 = (bf16[1024,1024]{1,0:T(8,128)(2,1)S(1)}, bf16[2048,512]{1,0:T(8,128)(2,1)S(1)}, bf16[2048,512]{1,0:T(8,128)(2,1)S(1)}) custom-call(s32[9]{0:T(128)S(1)} %stack.36.info, bf16[1024,256]{1,0:T(8,128)(2,1)S(1)} %get-tuple-element.74.bc, bf16[128,1024]{1,0:T(8,128)(2,1)S(1)} %get-tuple-element.88.state._, f32[1,2048]{1,0:T(1,128)S(1)} %bitcast.16, ...), custom_call_target="tpu_custom_call" | custom-call | flops 1 | bytes 1 | tf_op jit(solution)/shard_map/norm_rows/pallas_call | solution.py:563
  53.6 2.1 %norm_rows.4 = (bf16[256,2048]{1,0:T(8,128)(2,1)S(1)}, bf16[256,2048]{1,0:T(8,128)(2,1)S(1)}) custom-call(s32[9]{0:T(128)S(1)} %stack.36.info, bf16[1024,256]{1,0:T(8,128)(2,1)S(1)} %get-tuple-element.59.bc, bf16[128,1024]{1,0:T(8,128)(2,1)S(1)} %collective-permute-done.8.state, f32[1,2048]{1,0:T(1,128)S(1)} %bitcast.17, ...), custom_call_target="tpu_custom_call" | custom-call | flops 1 | bytes 1 | tf_op jit(solution)/shard_map/norm_rows/pallas_call | solution.py:563
  56.3 2.1 %norm_rows.5.owns = bf16[512,2048]{1,0:T(8,128)(2,1)S(1)} custom-call(s32[9]{0:T(128)S(1)} %stack.36.info, bf16[1024,256]{1,0:T(8,128)(2,1)S(1)} %get-tuple-element.59.bc, bf16[128,1024]{1,0:T(8,128)(2,1)S(1)} %collective-permute-done.8.state, f32[1,2048]{1,0:T(1,128)S(1)} %bitcast.18, bf16[256,2048]{1,0:T(8,128)(2,1)S(1)} %get-tuple-element.90._, ...), custom_call_target="tpu_custom_call" | custom-call | flops 1 | bytes 1 | tf_op jit(solution)/shard_map/norm_rows/pallas_call | solution.py:563
  61.3 4.3 %project_both.7 = (bf16[256,512]{1,0:T(8,128)(2,1)S(1)}, f32[256,512]{1,0:T(8,128)S(1)}) custom-call(bf16[512,2048]{1,0:T(8,128)(2,1)S(1)} %norm_rows.5.owns, bf16[512,2048]{1,0:T(8,128)(2,1)S(1)} %join.1.mates, bf16[2048,4096]{1,0:T(8,128)(2,1)} %w0_far.9, bf16[2048,4096]{1,0:T(8,128)(2,1)} %collective-permute-done.9.refs_3_.w1_far), custom_call_target="tpu_custom_call" | custom-call | flops 1 | bytes 1 | tf_op jit(solution)/shard_map/project_both/pallas_call | solution.py:668
  66.3 7.0 %project_both.6 = (bf16[256,512]{1,0:T(8,128)(2,1)S(1)}, bf16[256,512]{1,0:T(8,128)(2,1)S(1)}, f32[256,1024]{1,0:T(8,128)S(1)}) custom-call(bf16[512,2048]{1,0:T(8,128)(2,1)S(1)} %norm_rows.5.owns, bf16[512,2048]{1,0:T(8,128)(2,1)S(1)} %join.1.mates, bf16[2048,4096]{1,0:T(8,128)(2,1)} %w0_far.9, bf16[2048,4096]{1,0:T(8,128)(2,1)} %collective-permute-done.9.refs_3_.w1_far), custom_call_target="tpu_custom_call" | custom-call | flops 1 | bytes 1 | tf_op jit(solution)/shard_map/project_both/pallas_call | solution.py:668
  73.2 1.5 %collective-permute-start.16 = (bf16[256,512]{1,0:T(8,128)(2,1)S(1)}, bf16[256,512]{1,0:T(8,128)(2,1)S(1)}, u32[]{:S(2)}, u32[]{:S(2)}) collective-permute-start(bf16[256,512]{1,0:T(8,128)(2,1)S(1)} %get-tuple-element.101), channel_id=1, source_target_pairs={{0,2},{1,3},{2,0},{3,1},{4,6},{5,7},{6,4},{7,5},{8,10},{9,11},{10,... | collective-permute-start | bytes 786440 | tf_op jit(solution)/shard_map/ppermute | solution.py:735
  75.3 7.0 %project_both.5 = (bf16[256,512]{1,0:T(8,128)(2,1)S(1)}, bf16[256,512]{1,0:T(8,128)(2,1)S(1)}, f32[256,1024]{1,0:T(8,128)S(1)}) custom-call(bf16[512,2048]{1,0:T(8,128)(2,1)S(1)} %norm_rows.5.owns, bf16[512,2048]{1,0:T(8,128)(2,1)S(1)} %join.1.mates, bf16[2048,4096]{1,0:T(8,128)(2,1)} %w0_far.9, bf16[2048,4096]{1,0:T(8,128)(2,1)} %collective-permute-done.9.refs_3_.w1_far), custom_call_target="tpu_custom_call" | custom-call | flops 1 | bytes 1 | tf_op jit(solution)/shard_map/project_both/pallas_call | solution.py:668
  83.8 7.0 %project_both.4 = (bf16[256,512]{1,0:T(8,128)(2,1)S(1)}, bf16[256,512]{1,0:T(8,128)(2,1)S(1)}, f32[256,1024]{1,0:T(8,128)S(1)}) custom-call(bf16[512,2048]{1,0:T(8,128)(2,1)S(1)} %norm_rows.5.owns, bf16[512,2048]{1,0:T(8,128)(2,1)S(1)} %join.1.mates, bf16[2048,4096]{1,0:T(8,128)(2,1)} %w0_far.9, bf16[2048,4096]{1,0:T(8,128)(2,1)} %collective-permute-done.9.refs_3_.w1_far), custom_call_target="tpu_custom_call" | custom-call | flops 1 | bytes 1 | tf_op jit(solution)/shard_map/project_both/pallas_call | solution.py:668
  93.5 3.8 %project_near.1.refs_1_ = bf16[256,4096]{1,0:T(8,128)(2,1)} custom-call(bf16[512,2048]{1,0:T(8,128)(2,1)S(1)} %norm_rows.5.owns, bf16[512,2048]{1,0:T(8,128)(2,1)S(1)} %join.1.mates, bf16[2048,4096]{1,0:T(8,128)(2,1)} %w0_far.9, bf16[2048,4096]{1,0:T(8,128)(2,1)} %collective-permute-done.9.refs_3_.w1_far, bf16[256,512]{1,0:T(8,128)(2,1)S(1)} %collective-permute-done.19.arrived), custom_call_target="tpu_custom_call" | custom-call | flops 1 | bytes 1 | tf_op jit(solution)/shard_map/project_near/pallas_call | solution.py:692
  101.0 4.7 %collective-permute-done.13.refs_0_ = bf16[256,512]{1,0:T(8,128)(2,1)S(1)} collective-permute-done((bf16[256,512]{1,0:T(8,128)(2,1)S(1)}, bf16[256,512]{1,0:T(8,128)(2,1)S(1)}, u32[]{:S(2)}, u32[]{:S(2)}) %collective-permute-start.13) | collective-permute-done | bytes 262176 | tf_op jit(solution)/shard_map/ppermute | solution.py:735
  106.5 2.7 %collective-permute-done.12.refs_0_ = bf16[256,512]{1,0:T(8,128)(2,1)S(1)} collective-permute-done((bf16[256,512]{1,0:T(8,128)(2,1)S(1)}, bf16[256,512]{1,0:T(8,128)(2,1)S(1)}, u32[]{:S(2)}, u32[]{:S(2)}) %collective-permute-start.12) | collective-permute-done | bytes 262176 | tf_op jit(solution)/shard_map/ppermute | solution.py:735
  (48 shorter events, 21.9 us)
Async XLA Ops:
  0.0 50.2 %collective-permute-start.9 = (bf16[2048,4096]{1,0:T(8,128)(2,1)}, bf16[2048,4096]{1,0:T(8,128)(2,1)}, u32[]{:S(2)}, u32[]{:S(2)}) collective-permute-start(bf16[2048,4096]{1,0:T(8,128)(2,1)} %w0_far.9), channel_id=1, source_target_pairs={{0,1},{1,0},{2,3},{3,2},{4,5},{5,4},{6,7},{7,6},{8,9},{9,8},{10,11... | collective-permute-start | bytes 50331656 | tf_op jit(solution)/shard_map/ppermute | solution.py:735
  1.3 8.7 %collective-permute-start = (bf16[16,2560]{1,0:T(8,128)(2,1)S(1)}, bf16[16,2560]{1,0:T(8,128)(2,1)S(1)}, u32[]{:S(2)}, u32[]{:S(2)}) collective-permute-start(bf16[16,2560]{1,0:T(8,128)(2,1)S(1)} %tail_rows.1), channel_id=1, source_target_pairs={{0,4},{4,8},{8,12},{12,16},{16,20},{20,24},{24,28},{28,0},{1,5},{5... | collective-permute-start | bytes 245768 | tf_op jit(solution)/shard_map/ppermute | solution.py:740
  4.0 3.9 %copy-start.1 = (bf16[1024,2,256]{2,1,0:T(2,128)(2,1)S(1)}, bf16[1024,2,256]{2,1,0:T(2,128)(2,1)}, u32[]{:S(2)}) copy-start(bf16[1024,2,256]{2,1,0:T(2,128)(2,1)} %bc.1) | copy-start | bytes 3145732
  15.5 9.5 %collective-permute-start.1 = (bf16[144,1024]{1,0:T(8,128)(2,1)S(1)}, bf16[144,1024]{1,0:T(8,128)(2,1)S(1)}, u32[]{:S(2)}, u32[]{:S(2)}) collective-permute-start(bf16[144,1024]{1,0:T(8,128)(2,1)S(1)} %get-tuple-element.60), channel_id=1, source_target_pairs={{0,4},{4,0},{8,12},{12,8},{16,20},{20,16},{24,28},{28,24},{1,5},{5... | collective-permute-start | bytes 884744 | tf_op jit(solution)/shard_map/ppermute | solution.py:735
  25.9 9.1 %collective-permute-start.2 = (bf16[144,256]{1,0:T(8,128)(2,1)S(1)}, bf16[144,256]{1,0:T(8,128)(2,1)S(1)}, u32[]{:S(2)}, u32[]{:S(2)}) collective-permute-start(bf16[144,256]{1,0:T(8,128)(2,1)S(1)} %get-tuple-element.80), channel_id=1, source_target_pairs={{0,8},{4,12},{8,16},{12,20},{16,24},{20,28},{24,0},{28,4},{1,9},{5... | collective-permute-start | bytes 221192 | tf_op jit(solution)/shard_map/ppermute | solution.py:740
  27.2 8.1 %collective-permute-start.3 = (bf16[144,256]{1,0:T(8,128)(2,1)S(1)}, bf16[144,256]{1,0:T(8,128)(2,1)S(1)}, u32[]{:S(2)}, u32[]{:S(2)}) collective-permute-start(bf16[144,256]{1,0:T(8,128)(2,1)S(1)} %get-tuple-element.81), channel_id=1, source_target_pairs={{0,16},{4,20},{8,24},{12,28},{16,0},{20,4},{24,8},{28,12},{1,17},{... | collective-permute-start | bytes 221192 | tf_op jit(solution)/shard_map/ppermute | solution.py:740
  28.8 6.5 %collective-permute-start.4 = (bf16[144,256]{1,0:T(8,128)(2,1)S(1)}, bf16[144,256]{1,0:T(8,128)(2,1)S(1)}, u32[]{:S(2)}, u32[]{:S(2)}) collective-permute-start(bf16[144,256]{1,0:T(8,128)(2,1)S(1)} %get-tuple-element.82), channel_id=1, source_target_pairs={{0,24},{4,28},{8,0},{12,4},{16,8},{20,12},{24,16},{28,20},{1,25},{... | collective-permute-start | bytes 221192 | tf_op jit(solution)/shard_map/ppermute | solution.py:740
  35.9 8.2 %collective-permute-start.5 = (bf16[128,256]{1,0:T(8,128)(2,1)S(1)}, bf16[128,256]{1,0:T(8,128)(2,1)S(1)}, u32[]{:S(2)}, u32[]{:S(2)}) collective-permute-start(bf16[128,256]{1,0:T(8,128)(2,1)S(1)} %get-tuple-element.84), channel_id=1, source_target_pairs={{0,8},{4,12},{8,16},{12,20},{16,24},{20,28},{24,0},{28,4},{1,9},{5... | collective-permute-start | bytes 196616 | tf_op jit(solution)/shard_map/ppermute | solution.py:740
  37.9 6.5 %collective-permute-start.6 = (bf16[128,256]{1,0:T(8,128)(2,1)S(1)}, bf16[128,256]{1,0:T(8,128)(2,1)S(1)}, u32[]{:S(2)}, u32[]{:S(2)}) collective-permute-start(bf16[128,256]{1,0:T(8,128)(2,1)S(1)} %get-tuple-element.85), channel_id=1, source_target_pairs={{0,16},{4,20},{8,24},{12,28},{16,0},{20,4},{24,8},{28,12},{1,17},{... | collective-permute-start | bytes 196616 | tf_op jit(solution)/shard_map/ppermute | solution.py:740
  39.4 5.2 %collective-permute-start.7 = (bf16[128,256]{1,0:T(8,128)(2,1)S(1)}, bf16[128,256]{1,0:T(8,128)(2,1)S(1)}, u32[]{:S(2)}, u32[]{:S(2)}) collective-permute-start(bf16[128,256]{1,0:T(8,128)(2,1)S(1)} %get-tuple-element.86), channel_id=1, source_target_pairs={{0,24},{4,28},{8,0},{12,4},{16,8},{20,12},{24,16},{28,20},{1,25},{... | collective-permute-start | bytes 196616 | tf_op jit(solution)/shard_map/ppermute | solution.py:740
  45.5 4.7 %copy-start = (f32[2048]{0:T(1024)S(1)}, f32[2048]{0:T(1024)}, u32[]{:S(2)}) copy-start(f32[2048]{0:T(1024)} %param.18) | copy-start | bytes 24580
  45.5 8.1 %collective-permute-start.8 = (bf16[128,1024]{1,0:T(8,128)(2,1)S(1)}, bf16[128,1024]{1,0:T(8,128)(2,1)S(1)}, u32[]{:S(2)}, u32[]{:S(2)}) collective-permute-start(bf16[128,1024]{1,0:T(8,128)(2,1)S(1)} %get-tuple-element.87._), channel_id=1, source_target_pairs={{0,4},{4,0},{8,12},{12,8},{16,20},{20,16},{24,28},{28,24},{1,5},{5... | collective-permute-start | bytes 786440 | tf_op jit(solution)/shard_map/ppermute | solution.py:735
  55.7 2.7 %collective-permute-start.10 = (bf16[256,2048]{1,0:T(8,128)(2,1)S(1)}, bf16[256,2048]{1,0:T(8,128)(2,1)S(1)}, u32[]{:S(2)}, u32[]{:S(2)}) collective-permute-start(bf16[256,2048]{1,0:T(8,128)(2,1)S(1)} %get-tuple-element.90._), channel_id=1, source_target_pairs={{0,1},{1,0},{2,3},{3,2},{4,5},{5,4},{6,7},{7,6},{8,9},{9,8},{10,11... | collective-permute-start | bytes 3145736 | tf_op jit(solution)/shard_map/ppermute | solution.py:735
  55.8 5.4 %collective-permute-start.11 = (bf16[256,2048]{1,0:T(8,128)(2,1)S(1)}, bf16[256,2048]{1,0:T(8,128)(2,1)S(1)}, u32[]{:S(2)}, u32[]{:S(2)}) collective-permute-start(bf16[256,2048]{1,0:T(8,128)(2,1)S(1)} %get-tuple-element.91), channel_id=1, source_target_pairs={{0,1},{1,0},{2,3},{3,2},{4,5},{5,4},{6,7},{7,6},{8,9},{9,8},{10,11... | collective-permute-start | bytes 3145736 | tf_op jit(solution)/shard_map/ppermute | solution.py:735
  59.7 31.2 %collective-permute-start.19 = (bf16[256,512]{1,0:T(8,128)(2,1)S(1)}, bf16[256,512]{1,0:T(8,128)(2,1)S(1)}, u32[]{:S(2)}, u32[]{:S(2)}) collective-permute-start(bf16[256,512]{1,0:T(8,128)(2,1)S(1)} %project_ahead.1._), channel_id=1, source_target_pairs={{0,2},{1,3},{2,0},{3,1},{4,6},{5,7},{6,4},{7,5},{8,10},{9,11},{10,... | collective-permute-start | bytes 786440 | tf_op jit(solution)/shard_map/ppermute | solution.py:735
  65.6 25.9 %collective-permute-start.18 = (bf16[256,512]{1,0:T(8,128)(2,1)S(1)}, bf16[256,512]{1,0:T(8,128)(2,1)S(1)}, u32[]{:S(2)}, u32[]{:S(2)}) collective-permute-start(bf16[256,512]{1,0:T(8,128)(2,1)S(1)} %get-tuple-element.104), channel_id=1, source_target_pairs={{0,2},{1,3},{2,0},{3,1},{4,6},{5,7},{6,4},{7,5},{8,10},{9,11},{10,... | collective-permute-start | bytes 786440 | tf_op jit(solution)/shard_map/ppermute | solution.py:735
  73.2 19.7 %collective-permute-start.16 = (bf16[256,512]{1,0:T(8,128)(2,1)S(1)}, bf16[256,512]{1,0:T(8,128)(2,1)S(1)}, u32[]{:S(2)}, u32[]{:S(2)}) collective-permute-start(bf16[256,512]{1,0:T(8,128)(2,1)S(1)} %get-tuple-element.101), channel_id=1, source_target_pairs={{0,2},{1,3},{2,0},{3,1},{4,6},{5,7},{6,4},{7,5},{8,10},{9,11},{10,... | collective-permute-start | bytes 786440 | tf_op jit(solution)/shard_map/ppermute | solution.py:735
  74.7 23.3 %collective-permute-start.17 = (bf16[256,512]{1,0:T(8,128)(2,1)S(1)}, bf16[256,512]{1,0:T(8,128)(2,1)S(1)}, u32[]{:S(2)}, u32[]{:S(2)}) collective-permute-start(bf16[256,512]{1,0:T(8,128)(2,1)S(1)} %get-tuple-element.102), channel_id=1, source_target_pairs={{0,2},{1,3},{2,0},{3,1},{4,6},{5,7},{6,4},{7,5},{8,10},{9,11},{10,... | collective-permute-start | bytes 786440 | tf_op jit(solution)/shard_map/ppermute | solution.py:735
  82.3 16.7 %collective-permute-start.14 = (bf16[256,512]{1,0:T(8,128)(2,1)S(1)}, bf16[256,512]{1,0:T(8,128)(2,1)S(1)}, u32[]{:S(2)}, u32[]{:S(2)}) collective-permute-start(bf16[256,512]{1,0:T(8,128)(2,1)S(1)} %get-tuple-element.98), channel_id=1, source_target_pairs={{0,2},{1,3},{2,0},{3,1},{4,6},{5,7},{6,4},{7,5},{8,10},{9,11},{10,... | collective-permute-start | bytes 786440 | tf_op jit(solution)/shard_map/ppermute | solution.py:735
  90.8 9.3 %collective-permute-start.15 = (bf16[256,512]{1,0:T(8,128)(2,1)S(1)}, bf16[256,512]{1,0:T(8,128)(2,1)S(1)}, u32[]{:S(2)}, u32[]{:S(2)}) collective-permute-start(bf16[256,512]{1,0:T(8,128)(2,1)S(1)} %get-tuple-element.99), channel_id=1, source_target_pairs={{0,2},{1,3},{2,0},{3,1},{4,6},{5,7},{6,4},{7,5},{8,10},{9,11},{10,... | collective-permute-start | bytes 786440 | tf_op jit(solution)/shard_map/ppermute | solution.py:735
  91.5 14.3 %collective-permute-start.13 = (bf16[256,512]{1,0:T(8,128)(2,1)S(1)}, bf16[256,512]{1,0:T(8,128)(2,1)S(1)}, u32[]{:S(2)}, u32[]{:S(2)}) collective-permute-start(bf16[256,512]{1,0:T(8,128)(2,1)S(1)} %get-tuple-element.96), channel_id=1, source_target_pairs={{0,2},{1,3},{2,0},{3,1},{4,6},{5,7},{6,4},{7,5},{8,10},{9,11},{10,... | collective-permute-start | bytes 786440 | tf_op jit(solution)/shard_map/ppermute | solution.py:735
  92.9 16.3 %collective-permute-start.12 = (bf16[256,512]{1,0:T(8,128)(2,1)S(1)}, bf16[256,512]{1,0:T(8,128)(2,1)S(1)}, u32[]{:S(2)}, u32[]{:S(2)}) collective-permute-start(bf16[256,512]{1,0:T(8,128)(2,1)S(1)} %get-tuple-element.95), channel_id=1, source_target_pairs={{0,2},{1,3},{2,0},{3,1},{4,6},{5,7},{6,4},{7,5},{8,10},{9,11},{10,... | collective-permute-start | bytes 786440 | tf_op jit(solution)/shard_map/ppermute | solution.py:735

commit v20 on v19

--- a/solution.py
+++ b/solution.py
@@ -19,7 +19,7 @@
 STEP_B = 256
 EXTRA = 16
 SLAB = 256
-ROWS_C = 128
+ROWS_C = 256
 TILE = 256
 SLOTS = 4
 LEAD = 16
@@ -447,7 +447,7 @@
         b_mat = bc[at, 0:N]
         c_mat = bc[at, N : 2 * N]
         b_across = b_mat.T
-        scores = jnp.where(keep, dot(c_mat, b_mat, ((1,), (1,))), 0.0)
+        scores = jnp.where(keep, dot(c_mat, b_mat, ((1,), (1,))), 0.0).astype(BF16)
         for s in range(width // SLAB):
             lanes = slice(s * SLAB, (s + 1) * SLAB)
             xb = x[at, part * width + s * SLAB : part * width + (s + 1) * SLAB]
@@ -465,7 +465,7 @@
                     own = slice(head, head + 1)
                     column = jnp.broadcast_to(cum[at, own], (TOK_B, TOK_B))
                     gap = jnp.minimum(column - cum_s[own, at], log_s[own, at])
-                    tables.append((scores * jnp.exp2(gap)).astype(BF16))
+                    tables.append(scores * jnp.exp2(gap).astype(BF16))
                     fades.append(b_across * f_blk[own, at].astype(BF16))
                     columns.append(column)
                 xp = xb[:, q * 2 * P_SIZE : (q + 1) * 2 * P_SIZE]

time: 110 us -> 110 us (level)
  transfers between devices with their start and end apart: 20 -> 20, of which waited for: 7 -> 8; matrix products, arithmetic and copies ran while one was open for 0% -> 0% of each run, Pallas kernels for 66% -> 66%
where the time goes in v20:
time: 110 us
  Pallas kernels  74.8 us (68%)
  starting transfers between devices  22.5 us (20%)
  waiting for transfers between devices  11.9 us (11%)
    pallas_call x4, Pallas kernels, project_both(): pl.pallas_call(functools.partial(both_kernel, first // TILE, cut), grid=(...  25.2 us
    pallas_call x4, Pallas kernels, scan_part(): pl.pallas_call(functools.partial(scan_kernel, order, part), in_specs=[SCA...  15.4 us
    ppermute x7, starting transfers between devices, rotate(): lax.ppermute(block, 'seq', [(i, (i + distance) % size) for i in range(siz...  12.2 us
    pallas_call x2, Pallas kernels, conv_states(): pl.pallas_call(functools.partial(conv_kernel, order), grid_spec=pltpu.Pre...  10.9 us
    ppermute x13, starting transfers between devices, swap(): lax.ppermute(block, axis, [(i, i ^ bit) for i in range(lax.axis_size(axis...  10.4 us
    ppermute x13, waiting for transfers between devices, swap(): lax.ppermute(block, axis, [(i, i ^ bit) for i in range(lax.axis_size(axis...  9.22 us
    pallas_call x3, Pallas kernels, norm_rows(): pl.pallas_call(functools.partial(norm_kernel, order, places, skip, len(we...  6.82 us
    pallas_call x5, Pallas kernels, add_chunks(): pl.pallas_call(add_kernel, grid=(1,), in_specs=[pl.BlockSpec((rows, count...  4.06 us
  transfers between devices with their start and end apart: 20, of which 8 were waited for; matrix products, arithmetic and copies ran while one was open for 0% of the time, Pallas kernels for 66%

profile of v20, /device:TPU:0, one launch (start us, length us, event | category | flops | bytes accessed | tf_op | source)
XLA Modules:
  0.0 109.7 jit_solution(3237254258063166233)
XLA Ops:
  1.3 2.6 %collective-permute-start = (bf16[16,2560]{1,0:T(8,128)(2,1)S(1)}, bf16[16,2560]{1,0:T(8,128)(2,1)S(1)}, u32[]{:S(2)}, u32[]{:S(2)}) collective-permute-start(bf16[16,2560]{1,0:T(8,128)(2,1)S(1)} %tail_rows.1), channel_id=1, source_target_pairs={{0,4},{4,8},{8,12},{12,16},{16,20},{20,24},{24,28},{28,0},{1,5},{5... | collective-permute-start | bytes 245768 | tf_op jit(solution)/shard_map/ppermute | solution.py:740
  4.0 3.9 %decays.1 = (f32[1024,16]{1,0:T(8,128)S(1)}, f32[1024,16]{1,0:T(8,128)S(1)}, f32[16,1024]{1,0:T(8,128)S(1)}, f32[16,1024]{1,0:T(8,128)S(1)}, f32[16,1024]{1,0:T(...) custom-call(s32[9]{0:T(128)S(1)} %stack.36.info, ...), custom_call_target="tpu_custom_call" | custom-call | flops 1 | bytes 1 | tf_op jit(solution)/shard_map/decays/pallas_call | solution.py:153
  8.2 1.9 %collective-permute-done.halo = bf16[16,2560]{1,0:T(8,128)(2,1)S(1)} collective-permute-done((bf16[16,2560]{1,0:T(8,128)(2,1)S(1)}, bf16[16,2560]{1,0:T(8,128)(2,1)S(1)}, u32[]{:S(2)}, u32[]{:S(2)}) %collective-permute-start) | collective-permute-done | bytes 81952 | tf_op jit(solution)/shard_map/ppermute | solution.py:740
  10.1 5.5 %conv_states.2 = (bf16[1024,1024]{1,0:T(8,128)(2,1)S(1)}, bf16[1024,256]{1,0:T(8,128)(2,1)S(1)}, bf16[144,1024]{1,0:T(8,128)(2,1)S(1)}, bf16[1024,1024]{1,0:T(8,128)(2,1)S(1)}) custom-call(s32[9]{0:T(128)S(1)} %stack.36.info, bf16[1024,1024]{1,0:T(8,128)(2,1)S(1)} %get-tuple-element.55.x, bf16[1024,512]{1,0:T(8,128)(2,1)S(1)} %bitcast.14, ...), custom_call_target="tpu_custom_call" | custom-call | flops 1 | bytes 1 | tf_op jit(solution)/shard_map/conv_states/pallas_call | solution.py:294
  15.6 5.5 %conv_states.3 = (bf16[1024,1024]{1,0:T(8,128)(2,1)S(1)}, bf16[1024,256]{1,0:T(8,128)(2,1)S(1)}, f32[128,1024]{1,0:T(8,128)S(1)}, bf16[1024,2048]{1,0:T(8,128)(2,1)S(1)}) custom-call(s32[9]{0:T(128)S(1)} %stack.36.info, bf16[1024,1024]{1,0:T(8,128)(2,1)S(1)} %get-tuple-element.61.x, bf16[1024,512]{1,0:T(8,128)(2,1)S(1)} %bitcast.15, ...), custom_call_target="tpu_custom_call" | custom-call | flops 1 | bytes 1 | tf_op jit(solution)/shard_map/conv_states/pallas_call | solution.py:294
  21.1 3.9 %scan_part.4._.refs_0_ = bf16[1024,1024]{1,0:T(8,128)(2,1)S(1)} custom-call(s32[9]{0:T(128)S(1)} %stack.36.info, bf16[1024,1024]{1,0:T(8,128)(2,1)S(1)} %get-tuple-element.65.x, bf16[1024,2048]{1,0:T(8,128)(2,1)S(1)} %get-tuple-element.66.z, bf16[1024,256]{1,0:T(8,128)(2,1)S(1)} %get-tuple-element.59.bc, f32[1024,16]{1,0:T(8,128)S(1)} %get-tuple-element.67.cum, ...), custom_call_target="tpu_custom_call" | custom-call | flops 1 | bytes 1 | tf_op jit(solution)/shard_map/scan_part/pallas_call | solution.py:492
  27.1 1.6 %collective-permute-start.3 = (bf16[144,256]{1,0:T(8,128)(2,1)S(1)}, bf16[144,256]{1,0:T(8,128)(2,1)S(1)}, u32[]{:S(2)}, u32[]{:S(2)}) collective-permute-start(bf16[144,256]{1,0:T(8,128)(2,1)S(1)} %get-tuple-element.81), channel_id=1, source_target_pairs={{0,16},{4,20},{8,24},{12,28},{16,0},{20,4},{24,8},{28,12},{1,17},{... | collective-permute-start | bytes 221192 | tf_op jit(solution)/shard_map/ppermute | solution.py:740
  28.8 2.3 %collective-permute-start.4 = (bf16[144,256]{1,0:T(8,128)(2,1)S(1)}, bf16[144,256]{1,0:T(8,128)(2,1)S(1)}, u32[]{:S(2)}, u32[]{:S(2)}) collective-permute-start(bf16[144,256]{1,0:T(8,128)(2,1)S(1)} %get-tuple-element.82), channel_id=1, source_target_pairs={{0,24},{4,28},{8,0},{12,4},{16,8},{20,12},{24,16},{28,20},{1,25},{... | collective-permute-start | bytes 221192 | tf_op jit(solution)/shard_map/ppermute | solution.py:740
  31.1 3.9 %scan_part.5.refs_4_.refs_1_ = bf16[1024,1024]{1,0:T(8,128)(2,1)S(1)} custom-call(s32[9]{0:T(128)S(1)} %stack.36.info, bf16[1024,1024]{1,0:T(8,128)(2,1)S(1)} %get-tuple-element.65.x, bf16[1024,2048]{1,0:T(8,128)(2,1)S(1)} %get-tuple-element.66.z, bf16[1024,256]{1,0:T(8,128)(2,1)S(1)} %get-tuple-element.59.bc, f32[1024,16]{1,0:T(8,128)S(1)} %get-tuple-element.67.cum, ...), custom_call_target="tpu_custom_call" | custom-call | flops 1 | bytes 1 | tf_op jit(solution)/shard_map/scan_part/pallas_call | solution.py:492
  35.9 1.9 %collective-permute-start.5 = (bf16[128,256]{1,0:T(8,128)(2,1)S(1)}, bf16[128,256]{1,0:T(8,128)(2,1)S(1)}, u32[]{:S(2)}, u32[]{:S(2)}) collective-permute-start(bf16[128,256]{1,0:T(8,128)(2,1)S(1)} %get-tuple-element.84), channel_id=1, source_target_pairs={{0,8},{4,12},{8,16},{12,20},{16,24},{20,28},{24,0},{28,4},{1,9},{5... | collective-permute-start | bytes 196616 | tf_op jit(solution)/shard_map/ppermute | solution.py:740
  37.8 1.6 %collective-permute-start.6 = (bf16[128,256]{1,0:T(8,128)(2,1)S(1)}, bf16[128,256]{1,0:T(8,128)(2,1)S(1)}, u32[]{:S(2)}, u32[]{:S(2)}) collective-permute-start(bf16[128,256]{1,0:T(8,128)(2,1)S(1)} %get-tuple-element.85), channel_id=1, source_target_pairs={{0,16},{4,20},{8,24},{12,28},{16,0},{20,4},{24,8},{28,12},{1,17},{... | collective-permute-start | bytes 196616 | tf_op jit(solution)/shard_map/ppermute | solution.py:740
  40.3 3.8 %scan_part.6._.refs_0_ = bf16[1024,1024]{1,0:T(8,128)(2,1)S(1)} custom-call(s32[9]{0:T(128)S(1)} %stack.36.info, bf16[1024,1024]{1,0:T(8,128)(2,1)S(1)} %get-tuple-element.73.x, bf16[1024,2048]{1,0:T(8,128)(2,1)S(1)} %get-tuple-element.66.z, bf16[1024,256]{1,0:T(8,128)(2,1)S(1)} %get-tuple-element.74.bc, f32[1024,16]{1,0:T(8,128)S(1)} %get-tuple-element.75.cum, ...), custom_call_target="tpu_custom_call" | custom-call | flops 1 | bytes 1 | tf_op jit(solution)/shard_map/scan_part/pallas_call | solution.py:492
  46.3 3.8 %scan_part.7.refs_1_ = bf16[1024,1024]{1,0:T(8,128)(2,1)S(1)} custom-call(s32[9]{0:T(128)S(1)} %stack.36.info, bf16[1024,1024]{1,0:T(8,128)(2,1)S(1)} %get-tuple-element.73.x, bf16[1024,2048]{1,0:T(8,128)(2,1)S(1)} %get-tuple-element.66.z, bf16[1024,256]{1,0:T(8,128)(2,1)S(1)} %get-tuple-element.74.bc, f32[1024,16]{1,0:T(8,128)S(1)} %get-tuple-element.75.cum, ...), custom_call_target="tpu_custom_call" | custom-call | flops 1 | bytes 1 | tf_op jit(solution)/shard_map/scan_part/pallas_call | solution.py:492
  50.1 3.8 %norm_rows.3 = (bf16[1024,1024]{1,0:T(8,128)(2,1)S(1)}, bf16[2048,512]{1,0:T(8,128)(2,1)S(1)}, bf16[2048,512]{1,0:T(8,128)(2,1)S(1)}) custom-call(s32[9]{0:T(128)S(1)} %stack.36.info, bf16[1024,256]{1,0:T(8,128)(2,1)S(1)} %get-tuple-element.74.bc, bf16[128,1024]{1,0:T(8,128)(2,1)S(1)} %get-tuple-element.88.state._, f32[1,2048]{1,0:T(1,128)S(1)} %bitcast.16, ...), custom_call_target="tpu_custom_call" | custom-call | flops 1 | bytes 1 | tf_op jit(solution)/shard_map/norm_rows/pallas_call | solution.py:563
  54.0 1.5 %norm_rows.4 = (bf16[256,2048]{1,0:T(8,128)(2,1)S(1)}, bf16[256,2048]{1,0:T(8,128)(2,1)S(1)}) custom-call(s32[9]{0:T(128)S(1)} %stack.36.info, bf16[1024,256]{1,0:T(8,128)(2,1)S(1)} %get-tuple-element.59.bc, bf16[128,1024]{1,0:T(8,128)(2,1)S(1)} %collective-permute-done.8.state, f32[1,2048]{1,0:T(1,128)S(1)} %bitcast.17, ...), custom_call_target="tpu_custom_call" | custom-call | flops 1 | bytes 1 | tf_op jit(solution)/shard_map/norm_rows/pallas_call | solution.py:563
  56.1 1.5 %norm_rows.5.owns = bf16[512,2048]{1,0:T(8,128)(2,1)S(1)} custom-call(s32[9]{0:T(128)S(1)} %stack.36.info, bf16[1024,256]{1,0:T(8,128)(2,1)S(1)} %get-tuple-element.59.bc, bf16[128,1024]{1,0:T(8,128)(2,1)S(1)} %collective-permute-done.8.state, f32[1,2048]{1,0:T(1,128)S(1)} %bitcast.18, bf16[256,2048]{1,0:T(8,128)(2,1)S(1)} %get-tuple-element.90._, ...), custom_call_target="tpu_custom_call" | custom-call | flops 1 | bytes 1 | tf_op jit(solution)/shard_map/norm_rows/pallas_call | solution.py:563
  59.5 1.5 %collective-permute-start.19 = (bf16[256,512]{1,0:T(8,128)(2,1)S(1)}, bf16[256,512]{1,0:T(8,128)(2,1)S(1)}, u32[]{:S(2)}, u32[]{:S(2)}) collective-permute-start(bf16[256,512]{1,0:T(8,128)(2,1)S(1)} %project_ahead.1._), channel_id=1, source_target_pairs={{0,2},{1,3},{2,0},{3,1},{4,6},{5,7},{6,4},{7,5},{8,10},{9,11},{10,... | collective-permute-start | bytes 786440 | tf_op jit(solution)/shard_map/ppermute | solution.py:735
  61.1 4.3 %project_both.7 = (bf16[256,512]{1,0:T(8,128)(2,1)S(1)}, f32[256,512]{1,0:T(8,128)S(1)}) custom-call(bf16[512,2048]{1,0:T(8,128)(2,1)S(1)} %norm_rows.5.owns, bf16[512,2048]{1,0:T(8,128)(2,1)S(1)} %join.1.mates, bf16[2048,4096]{1,0:T(8,128)(2,1)} %w0_far.9, bf16[2048,4096]{1,0:T(8,128)(2,1)} %collective-permute-done.9.refs_3_.w1_far), custom_call_target="tpu_custom_call" | custom-call | flops 1 | bytes 1 | tf_op jit(solution)/shard_map/project_both/pallas_call | solution.py:668
  66.1 7.0 %project_both.6 = (bf16[256,512]{1,0:T(8,128)(2,1)S(1)}, bf16[256,512]{1,0:T(8,128)(2,1)S(1)}, f32[256,1024]{1,0:T(8,128)S(1)}) custom-call(bf16[512,2048]{1,0:T(8,128)(2,1)S(1)} %norm_rows.5.owns, bf16[512,2048]{1,0:T(8,128)(2,1)S(1)} %join.1.mates, bf16[2048,4096]{1,0:T(8,128)(2,1)} %w0_far.9, bf16[2048,4096]{1,0:T(8,128)(2,1)} %collective-permute-done.9.refs_3_.w1_far), custom_call_target="tpu_custom_call" | custom-call | flops 1 | bytes 1 | tf_op jit(solution)/shard_map/project_both/pallas_call | solution.py:668
  75.1 7.0 %project_both.5 = (bf16[256,512]{1,0:T(8,128)(2,1)S(1)}, bf16[256,512]{1,0:T(8,128)(2,1)S(1)}, f32[256,1024]{1,0:T(8,128)S(1)}) custom-call(bf16[512,2048]{1,0:T(8,128)(2,1)S(1)} %norm_rows.5.owns, bf16[512,2048]{1,0:T(8,128)(2,1)S(1)} %join.1.mates, bf16[2048,4096]{1,0:T(8,128)(2,1)} %w0_far.9, bf16[2048,4096]{1,0:T(8,128)(2,1)} %collective-permute-done.9.refs_3_.w1_far), custom_call_target="tpu_custom_call" | custom-call | flops 1 | bytes 1 | tf_op jit(solution)/shard_map/project_both/pallas_call | solution.py:668
  83.6 7.0 %project_both.4 = (bf16[256,512]{1,0:T(8,128)(2,1)S(1)}, bf16[256,512]{1,0:T(8,128)(2,1)S(1)}, f32[256,1024]{1,0:T(8,128)S(1)}) custom-call(bf16[512,2048]{1,0:T(8,128)(2,1)S(1)} %norm_rows.5.owns, bf16[512,2048]{1,0:T(8,128)(2,1)S(1)} %join.1.mates, bf16[2048,4096]{1,0:T(8,128)(2,1)} %w0_far.9, bf16[2048,4096]{1,0:T(8,128)(2,1)} %collective-permute-done.9.refs_3_.w1_far), custom_call_target="tpu_custom_call" | custom-call | flops 1 | bytes 1 | tf_op jit(solution)/shard_map/project_both/pallas_call | solution.py:668
  93.3 3.8 %project_near.1.refs_1_ = bf16[256,4096]{1,0:T(8,128)(2,1)} custom-call(bf16[512,2048]{1,0:T(8,128)(2,1)S(1)} %norm_rows.5.owns, bf16[512,2048]{1,0:T(8,128)(2,1)S(1)} %join.1.mates, bf16[2048,4096]{1,0:T(8,128)(2,1)} %w0_far.9, bf16[2048,4096]{1,0:T(8,128)(2,1)} %collective-permute-done.9.refs_3_.w1_far, bf16[256,512]{1,0:T(8,128)(2,1)S(1)} %collective-permute-done.19.arrived), custom_call_target="tpu_custom_call" | custom-call | flops 1 | bytes 1 | tf_op jit(solution)/shard_map/project_near/pallas_call | solution.py:692
  100.8 4.7 %collective-permute-done.13.refs_0_ = bf16[256,512]{1,0:T(8,128)(2,1)S(1)} collective-permute-done((bf16[256,512]{1,0:T(8,128)(2,1)S(1)}, bf16[256,512]{1,0:T(8,128)(2,1)S(1)}, u32[]{:S(2)}, u32[]{:S(2)}) %collective-permute-start.13) | collective-permute-done | bytes 262176 | tf_op jit(solution)/shard_map/ppermute | solution.py:735
  106.3 2.7 %collective-permute-done.12.refs_0_ = bf16[256,512]{1,0:T(8,128)(2,1)S(1)} collective-permute-done((bf16[256,512]{1,0:T(8,128)(2,1)S(1)}, bf16[256,512]{1,0:T(8,128)(2,1)S(1)}, u32[]{:S(2)}, u32[]{:S(2)}) %collective-permute-start.12) | collective-permute-done | bytes 262176 | tf_op jit(solution)/shard_map/ppermute | solution.py:735
  (48 shorter events, 22.6 us)
Async XLA Ops:
  0.0 50.1 %collective-permute-start.9 = (bf16[2048,4096]{1,0:T(8,128)(2,1)}, bf16[2048,4096]{1,0:T(8,128)(2,1)}, u32[]{:S(2)}, u32[]{:S(2)}) collective-permute-start(bf16[2048,4096]{1,0:T(8,128)(2,1)} %w0_far.9), channel_id=1, source_target_pairs={{0,1},{1,0},{2,3},{3,2},{4,5},{5,4},{6,7},{7,6},{8,9},{9,8},{10,11... | collective-permute-start | bytes 50331656 | tf_op jit(solution)/shard_map/ppermute | solution.py:735
  1.3 8.7 %collective-permute-start = (bf16[16,2560]{1,0:T(8,128)(2,1)S(1)}, bf16[16,2560]{1,0:T(8,128)(2,1)S(1)}, u32[]{:S(2)}, u32[]{:S(2)}) collective-permute-start(bf16[16,2560]{1,0:T(8,128)(2,1)S(1)} %tail_rows.1), channel_id=1, source_target_pairs={{0,4},{4,8},{8,12},{12,16},{16,20},{20,24},{24,28},{28,0},{1,5},{5... | collective-permute-start | bytes 245768 | tf_op jit(solution)/shard_map/ppermute | solution.py:740
  4.0 3.9 %copy-start.1 = (bf16[1024,2,256]{2,1,0:T(2,128)(2,1)S(1)}, bf16[1024,2,256]{2,1,0:T(2,128)(2,1)}, u32[]{:S(2)}) copy-start(bf16[1024,2,256]{2,1,0:T(2,128)(2,1)} %bc.1) | copy-start | bytes 3145732
  15.5 9.5 %collective-permute-start.1 = (bf16[144,1024]{1,0:T(8,128)(2,1)S(1)}, bf16[144,1024]{1,0:T(8,128)(2,1)S(1)}, u32[]{:S(2)}, u32[]{:S(2)}) collective-permute-start(bf16[144,1024]{1,0:T(8,128)(2,1)S(1)} %get-tuple-element.60), channel_id=1, source_target_pairs={{0,4},{4,0},{8,12},{12,8},{16,20},{20,16},{24,28},{28,24},{1,5},{5... | collective-permute-start | bytes 884744 | tf_op jit(solution)/shard_map/ppermute | solution.py:735
  25.9 9.1 %collective-permute-start.2 = (bf16[144,256]{1,0:T(8,128)(2,1)S(1)}, bf16[144,256]{1,0:T(8,128)(2,1)S(1)}, u32[]{:S(2)}, u32[]{:S(2)}) collective-permute-start(bf16[144,256]{1,0:T(8,128)(2,1)S(1)} %get-tuple-element.80), channel_id=1, source_target_pairs={{0,8},{4,12},{8,16},{12,20},{16,24},{20,28},{24,0},{28,4},{1,9},{5... | collective-permute-start | bytes 221192 | tf_op jit(solution)/shard_map/ppermute | solution.py:740
  27.1 8.1 %collective-permute-start.3 = (bf16[144,256]{1,0:T(8,128)(2,1)S(1)}, bf16[144,256]{1,0:T(8,128)(2,1)S(1)}, u32[]{:S(2)}, u32[]{:S(2)}) collective-permute-start(bf16[144,256]{1,0:T(8,128)(2,1)S(1)} %get-tuple-element.81), channel_id=1, source_target_pairs={{0,16},{4,20},{8,24},{12,28},{16,0},{20,4},{24,8},{28,12},{1,17},{... | collective-permute-start | bytes 221192 | tf_op jit(solution)/shard_map/ppermute | solution.py:740
  28.8 6.5 %collective-permute-start.4 = (bf16[144,256]{1,0:T(8,128)(2,1)S(1)}, bf16[144,256]{1,0:T(8,128)(2,1)S(1)}, u32[]{:S(2)}, u32[]{:S(2)}) collective-permute-start(bf16[144,256]{1,0:T(8,128)(2,1)S(1)} %get-tuple-element.82), channel_id=1, source_target_pairs={{0,24},{4,28},{8,0},{12,4},{16,8},{20,12},{24,16},{28,20},{1,25},{... | collective-permute-start | bytes 221192 | tf_op jit(solution)/shard_map/ppermute | solution.py:740
  35.9 8.2 %collective-permute-start.5 = (bf16[128,256]{1,0:T(8,128)(2,1)S(1)}, bf16[128,256]{1,0:T(8,128)(2,1)S(1)}, u32[]{:S(2)}, u32[]{:S(2)}) collective-permute-start(bf16[128,256]{1,0:T(8,128)(2,1)S(1)} %get-tuple-element.84), channel_id=1, source_target_pairs={{0,8},{4,12},{8,16},{12,20},{16,24},{20,28},{24,0},{28,4},{1,9},{5... | collective-permute-start | bytes 196616 | tf_op jit(solution)/shard_map/ppermute | solution.py:740
  37.8 6.5 %collective-permute-start.6 = (bf16[128,256]{1,0:T(8,128)(2,1)S(1)}, bf16[128,256]{1,0:T(8,128)(2,1)S(1)}, u32[]{:S(2)}, u32[]{:S(2)}) collective-permute-start(bf16[128,256]{1,0:T(8,128)(2,1)S(1)} %get-tuple-element.85), channel_id=1, source_target_pairs={{0,16},{4,20},{8,24},{12,28},{16,0},{20,4},{24,8},{28,12},{1,17},{... | collective-permute-start | bytes 196616 | tf_op jit(solution)/shard_map/ppermute | solution.py:740
  39.4 5.2 %collective-permute-start.7 = (bf16[128,256]{1,0:T(8,128)(2,1)S(1)}, bf16[128,256]{1,0:T(8,128)(2,1)S(1)}, u32[]{:S(2)}, u32[]{:S(2)}) collective-permute-start(bf16[128,256]{1,0:T(8,128)(2,1)S(1)} %get-tuple-element.86), channel_id=1, source_target_pairs={{0,24},{4,28},{8,0},{12,4},{16,8},{20,12},{24,16},{28,20},{1,25},{... | collective-permute-start | bytes 196616 | tf_op jit(solution)/shard_map/ppermute | solution.py:740
  45.4 4.7 %copy-start = (f32[2048]{0:T(1024)S(1)}, f32[2048]{0:T(1024)}, u32[]{:S(2)}) copy-start(f32[2048]{0:T(1024)} %param.18) | copy-start | bytes 24580
  45.4 8.5 %collective-permute-start.8 = (bf16[128,1024]{1,0:T(8,128)(2,1)S(1)}, bf16[128,1024]{1,0:T(8,128)(2,1)S(1)}, u32[]{:S(2)}, u32[]{:S(2)}) collective-permute-start(bf16[128,1024]{1,0:T(8,128)(2,1)S(1)} %get-tuple-element.87._), channel_id=1, source_target_pairs={{0,4},{4,0},{8,12},{12,8},{16,20},{20,16},{24,28},{28,24},{1,5},{5... | collective-permute-start | bytes 786440 | tf_op jit(solution)/shard_map/ppermute | solution.py:735
  55.5 2.7 %collective-permute-start.10 = (bf16[256,2048]{1,0:T(8,128)(2,1)S(1)}, bf16[256,2048]{1,0:T(8,128)(2,1)S(1)}, u32[]{:S(2)}, u32[]{:S(2)}) collective-permute-start(bf16[256,2048]{1,0:T(8,128)(2,1)S(1)} %get-tuple-element.90._), channel_id=1, source_target_pairs={{0,1},{1,0},{2,3},{3,2},{4,5},{5,4},{6,7},{7,6},{8,9},{9,8},{10,11... | collective-permute-start | bytes 3145736 | tf_op jit(solution)/shard_map/ppermute | solution.py:735
  55.6 5.4 %collective-permute-start.11 = (bf16[256,2048]{1,0:T(8,128)(2,1)S(1)}, bf16[256,2048]{1,0:T(8,128)(2,1)S(1)}, u32[]{:S(2)}, u32[]{:S(2)}) collective-permute-start(bf16[256,2048]{1,0:T(8,128)(2,1)S(1)} %get-tuple-element.91), channel_id=1, source_target_pairs={{0,1},{1,0},{2,3},{3,2},{4,5},{5,4},{6,7},{7,6},{8,9},{9,8},{10,11... | collective-permute-start | bytes 3145736 | tf_op jit(solution)/shard_map/ppermute | solution.py:735
  59.5 31.2 %collective-permute-start.19 = (bf16[256,512]{1,0:T(8,128)(2,1)S(1)}, bf16[256,512]{1,0:T(8,128)(2,1)S(1)}, u32[]{:S(2)}, u32[]{:S(2)}) collective-permute-start(bf16[256,512]{1,0:T(8,128)(2,1)S(1)} %project_ahead.1._), channel_id=1, source_target_pairs={{0,2},{1,3},{2,0},{3,1},{4,6},{5,7},{6,4},{7,5},{8,10},{9,11},{10,... | collective-permute-start | bytes 786440 | tf_op jit(solution)/shard_map/ppermute | solution.py:735
  65.4 25.9 %collective-permute-start.18 = (bf16[256,512]{1,0:T(8,128)(2,1)S(1)}, bf16[256,512]{1,0:T(8,128)(2,1)S(1)}, u32[]{:S(2)}, u32[]{:S(2)}) collective-permute-start(bf16[256,512]{1,0:T(8,128)(2,1)S(1)} %get-tuple-element.104), channel_id=1, source_target_pairs={{0,2},{1,3},{2,0},{3,1},{4,6},{5,7},{6,4},{7,5},{8,10},{9,11},{10,... | collective-permute-start | bytes 786440 | tf_op jit(solution)/shard_map/ppermute | solution.py:735
  73.0 19.7 %collective-permute-start.16 = (bf16[256,512]{1,0:T(8,128)(2,1)S(1)}, bf16[256,512]{1,0:T(8,128)(2,1)S(1)}, u32[]{:S(2)}, u32[]{:S(2)}) collective-permute-start(bf16[256,512]{1,0:T(8,128)(2,1)S(1)} %get-tuple-element.101), channel_id=1, source_target_pairs={{0,2},{1,3},{2,0},{3,1},{4,6},{5,7},{6,4},{7,5},{8,10},{9,11},{10,... | collective-permute-start | bytes 786440 | tf_op jit(solution)/shard_map/ppermute | solution.py:735
  74.5 23.4 %collective-permute-start.17 = (bf16[256,512]{1,0:T(8,128)(2,1)S(1)}, bf16[256,512]{1,0:T(8,128)(2,1)S(1)}, u32[]{:S(2)}, u32[]{:S(2)}) collective-permute-start(bf16[256,512]{1,0:T(8,128)(2,1)S(1)} %get-tuple-element.102), channel_id=1, source_target_pairs={{0,2},{1,3},{2,0},{3,1},{4,6},{5,7},{6,4},{7,5},{8,10},{9,11},{10,... | collective-permute-start | bytes 786440 | tf_op jit(solution)/shard_map/ppermute | solution.py:735
  82.1 16.7 %collective-permute-start.14 = (bf16[256,512]{1,0:T(8,128)(2,1)S(1)}, bf16[256,512]{1,0:T(8,128)(2,1)S(1)}, u32[]{:S(2)}, u32[]{:S(2)}) collective-permute-start(bf16[256,512]{1,0:T(8,128)(2,1)S(1)} %get-tuple-element.98), channel_id=1, source_target_pairs={{0,2},{1,3},{2,0},{3,1},{4,6},{5,7},{6,4},{7,5},{8,10},{9,11},{10,... | collective-permute-start | bytes 786440 | tf_op jit(solution)/shard_map/ppermute | solution.py:735
  90.6 9.3 %collective-permute-start.15 = (bf16[256,512]{1,0:T(8,128)(2,1)S(1)}, bf16[256,512]{1,0:T(8,128)(2,1)S(1)}, u32[]{:S(2)}, u32[]{:S(2)}) collective-permute-start(bf16[256,512]{1,0:T(8,128)(2,1)S(1)} %get-tuple-element.99), channel_id=1, source_target_pairs={{0,2},{1,3},{2,0},{3,1},{4,6},{5,7},{6,4},{7,5},{8,10},{9,11},{10,... | collective-permute-start | bytes 786440 | tf_op jit(solution)/shard_map/ppermute | solution.py:735
  91.3 14.2 %collective-permute-start.13 = (bf16[256,512]{1,0:T(8,128)(2,1)S(1)}, bf16[256,512]{1,0:T(8,128)(2,1)S(1)}, u32[]{:S(2)}, u32[]{:S(2)}) collective-permute-start(bf16[256,512]{1,0:T(8,128)(2,1)S(1)} %get-tuple-element.96), channel_id=1, source_target_pairs={{0,2},{1,3},{2,0},{3,1},{4,6},{5,7},{6,4},{7,5},{8,10},{9,11},{10,... | collective-permute-start | bytes 786440 | tf_op jit(solution)/shard_map/ppermute | solution.py:735
  92.7 16.3 %collective-permute-start.12 = (bf16[256,512]{1,0:T(8,128)(2,1)S(1)}, bf16[256,512]{1,0:T(8,128)(2,1)S(1)}, u32[]{:S(2)}, u32[]{:S(2)}) collective-permute-start(bf16[256,512]{1,0:T(8,128)(2,1)S(1)} %get-tuple-element.95), channel_id=1, source_target_pairs={{0,2},{1,3},{2,0},{3,1},{4,6},{5,7},{6,4},{7,5},{8,10},{9,11},{10,... | collective-permute-start | bytes 786440 | tf_op jit(solution)/shard_map/ppermute | solution.py:735
